TPU v7x, 32 devices: a whole 2x2x4 slice. The times are simulated.
32 devices in a mesh: pert: 2 (over y), band: 16 (over z, x, core).
Axes of the slice: x: 2, y: 2, z: 4, core: 2. Of those that a mesh axis runs over, the one named last changes fastest.
Arguments:
- response: bfloat16 [1024, 12288], P('pert', 'band'), parts along dimension 0, may hold values from -6 to 6
- orbitals: bfloat16 [512, 12288], P(None, 'band'), may hold values from -6 to 6
- projectors: bfloat16 [2048, 12288], P(None, 'band'), may hold values from -6 to 6
- potential: float32 [12288], P('band'), may hold values from -1 to 1
- perturbing: float32 [24576], P(('pert', 'band')), parts along dimension 0, may hold values from -6 to 6
- energies: float32 [512], replicated, may hold values from -1 to -0.2
- window_start: int32 [512], replicated, may hold values from 0 to 31, as said below
- block_count: int32 [512], replicated, may hold values from 1 to 9, as said below
Outputs:
- updated_response: bfloat16 [1024, 12288], P('pert', 'band'), parts along dimension 0
- residual: bfloat16 [1024, 12288], P('pert', 'band'), parts along dimension 0
There are 2 independent parts, one for each index of `pert`. A program takes and returns all parts, laid end to end along the dimension named above; an argument that names none is the same for every part. Nothing has to cross between parts.
Inputs may be any that keep to these rules, and one draw needn't show every extreme that they name: `window_start`: band n lies in block n // 16. Each band's window contains its own block and starts at most 4 blocks below it. `block_count`: each band's window ends at most 4 blocks above its own block and never past block 31.
All inputs are finite; a program needn't handle non-finite values.
Results may differ from a plain program's by a relative error of at most 0.0041.
Values may be sent and summed in bfloat16 or wider, within the bound.
No kernel may reach another device: no remote copies, remote signals or barrier semaphores. Data moves between devices by JAX's collectives and lax.ppermute only.
A program may use at most 128 MiB of HBM per device.

v0:
```python
import math

import jax
import jax.numpy as jnp
from jax import lax
from jax.sharding import PartitionSpec as P

GY = 8
GZ = 16
NBLK = 32


COEFFS = (
    -5369.0 / 1800.0,
    12.0 / 7.0,
    -15.0 / 56.0,
    10.0 / 189.0,
    -1.0 / 112.0,
    2.0 / 1925.0,
    -1.0 / 16632.0,
)
KINETIC = 0.125
STEP_SIZE = 0.3
CONTRACT_CELLS = (((1,), (1,)), ((), ()))


def padded_2(cells, sides, width):
    for axis, dim in sides:
        count = lax.axis_size(axis)
        head = lax.slice_in_dim(cells, 0, width, axis=dim)
        tail = lax.slice_in_dim(cells, cells.shape[dim] - width, cells.shape[dim], axis=dim)
        cells = jnp.concatenate(
            [
                lax.ppermute(tail, axis, [(i, (i + 1) % count) for i in range(count)]),
                cells,
                lax.ppermute(head, axis, [((i + 1) % count, i) for i in range(count)]),
            ],
            axis=dim,
        )
    return cells


def slab_laplacian(padded, depth):
    centre = padded[:, 6 : 6 + depth]
    result = 3.0 * COEFFS[0] * centre
    for offset in range(1, 7):
        result = result + COEFFS[offset] * (
            padded[:, 6 + offset : 6 + offset + depth] + padded[:, 6 - offset : 6 - offset + depth]
        )
    for axis_number in (2, 3):
        for offset in range(1, 7):
            result = result + COEFFS[offset] * (
                jnp.roll(centre, offset, axis_number) + jnp.roll(centre, -offset, axis_number)
            )
    return result


def shards(
    response, orbitals, projectors, potential, perturbing, energies, window_start, block_count
):
    band_rows = response.shape[0]
    local_cells = response.shape[1]
    devices = lax.axis_size("band")
    cells = local_cells * devices
    plane = GY * GZ
    depth = local_cells // plane
    ace_scale = 1.0 / math.sqrt(cells * projectors.shape[0])
    window_scale = 1.0 / math.sqrt(cells * band_rows)
    padded = padded_2(response.reshape(band_rows, depth, plane), (("band", 1),), 6)
    padded_wide = padded.astype(jnp.float32).reshape(band_rows, depth + 12, GY, GZ)
    kinetic = -KINETIC * slab_laplacian(padded_wide, depth).reshape(band_rows, local_cells)
    response_wide = response.astype(jnp.float32)
    picked = response
    share = lax.psum_scatter(
        lax.dot_general(picked, projectors, CONTRACT_CELLS, preferred_element_type=jnp.float32),
        "band",
        scatter_dimension=0,
        tiled=True,
    )
    ace_intersection = lax.all_gather(
        (share * ace_scale).astype(jnp.bfloat16), "band", axis=0, tiled=True
    )
    ace_term = -jnp.dot(ace_intersection, projectors, preferred_element_type=jnp.float32)
    applied = (
        kinetic + potential[None, :] * response_wide + ace_term - energies[:, None] * response_wide
    )
    orbitals_wide = orbitals.astype(jnp.float32)
    unprojected = -(perturbing[None, :] * orbitals_wide) - applied
    unprojected_low = unprojected.astype(jnp.bfloat16)
    picked = unprojected_low
    window_share = lax.psum_scatter(
        lax.dot_general(picked, orbitals, CONTRACT_CELLS, preferred_element_type=jnp.float32),
        "band",
        scatter_dimension=0,
        tiled=True,
    )
    window_intersection = lax.all_gather(
        (window_share * window_scale).astype(jnp.bfloat16), "band", axis=0, tiled=True
    )
    block_ids = jnp.arange(band_rows, dtype=jnp.int32) // (band_rows // NBLK)
    lowest = window_start[:, None]
    highest = window_start[:, None] + block_count[:, None] - 1
    inside = (block_ids[None, :] >= lowest) & (block_ids[None, :] <= highest)
    window_intersection = jnp.where(
        inside, window_intersection, jnp.zeros_like(window_intersection)
    )
    residual_wide = unprojected - jnp.dot(
        window_intersection, orbitals, preferred_element_type=jnp.float32
    )
    updated_response = (response_wide + STEP_SIZE * residual_wide).astype(jnp.bfloat16)
    return (updated_response, residual_wide.astype(jnp.bfloat16))


def solution(mesh):
    in_specs = (
        P("pert", "band"),
        P(None, "band"),
        P(None, "band"),
        P("band"),
        P(("pert", "band")),
        P(),
        P(),
        P(),
    )
    out_specs = (P("pert", "band"), P("pert", "band"))
    return jax.shard_map(shards, mesh=mesh, in_specs=in_specs, out_specs=out_specs, check_vma=False)
```

profile of v0, /device:TPU:0, one launch (start us, length us, event | category | flops | bytes accessed | tf_op | source)
XLA Modules:
  0.0 228.2 jit_solution(8976337017419959127)
XLA Ops:
  7.2 0.0 copy-start
  7.2 0.0 reduce-scatter.3.cloned.1.call-start
  7.2 1.8 copy-done
  9.1 5.0 %fusion.69 = f32[512,2048]{1,0:T(8,128)} fusion(bf16[512,768]{1,0:T(8,128)(2,1)} %param.8, bf16[2048,768]{1,0:T(8,128)(2,1)S(1)} %copy-done), kind=kOutput, calls=%fused_computation.98 | convolution fusion | flops 1610612736 | bytes 8126464 | tf_op jit(solution)/shard_map/dot_general | solution.py:75
  14.0 0.0 reduce-scatter.3.cloned.1.call-update
  14.1 0.0 all-gather.2.cloned.1.call-start
  14.1 2.3 %copy.10 = bf16[512,768]{0,1:T(8,128)(2,1)} copy(bf16[512,768]{1,0:T(8,128)(2,1)} %param.8) | data formatting | bytes 1572864 | tf_op args[0]
  16.4 0.5 collective-permute-start
  16.9 5.0 %collective-permute-start.1 = (bf16[512,6,128]{0,2,1:T(8,128)(2,1)}, bf16[512,6,128]{0,2,1:T(8,128)(2,1)S(1)}, u32[]{:S(2)}, u32[]{:S(2)}) collective-permute-start(bf16[512,6,128]{0,2,1:T(8,128)(2,1)} %bitcast.13), channel_id=1, source_target_pairs={{1,0},{2,1},{3,2},{4,3},{5,4},{6,5},{7,6},{8,7},{9,8},{10,9},{11,1... | collective-permute-start | bytes 2359304 | tf_op jit(solution)/shard_map/ppermute | solution.py:36
  21.8 10.0 %collective-permute-done = bf16[512,6,128]{0,2,1:T(8,128)(2,1)S(1)} collective-permute-done((bf16[512,6,128]{0,2,1:T(8,128)(2,1)}, bf16[512,6,128]{0,2,1:T(8,128)(2,1)S(1)}, u32[]{:S(2)}, u32[]{:S(2)}) %collective-permute-start) | collective-permute-done | bytes 786464 | tf_op jit(solution)/shard_map/ppermute | solution.py:34
  31.8 0.0 collective-permute-done.1
  31.8 1.5 maximum_convert_fusion
  33.3 0.0 copy-start.1
  33.3 1.0 fusion.64
  34.4 1.3 fusion.49
  35.7 0.9 fusion.62
  36.6 1.1 fusion.58
  37.7 1.1 fusion.60
  38.8 1.2 fusion.51
  40.0 1.3 fusion.54
  41.4 1.4 fusion.56
  42.8 1.4 fusion.65
  44.1 1.6 fusion.52
  45.8 0.0 copy-done.1
  45.8 1.8 fusion.50
  47.5 42.0 %reduce-scatter.3.cloned.1.call-done = f32[32,2048]{1,0:T(8,128)} async-done(((f32[512,2048]{1,0:T(8,128)}), f32[32,2048]{1,0:T(8,128)}) %reduce-scatter.3.cloned.1.call-update) | async-done | bytes 262160 | tf_op jit(solution)/shard_map/reduce_scatter | solution.py:74
  89.5 1.6 multiply_convert_fusion
  91.1 0.0 all-gather.2.cloned.1.call-update
  91.2 0.0 reduce-scatter.5.cloned.1.call-start
  91.2 1.8 fusion.67
  93.0 0.0 copy-start.2
  93.0 3.9 %fusion.66 = (f32[512,6,7,16]{0,3,2,1:T(8,128)}, f32[512,6,7,16]{0,3,2,1:T(8,128)}) fusion(f32[512,18,8,16]{0,3,2,1:T(8,128)} %copy-done.1), kind=kLoop, calls=%fused_computation.95 | loop fusion | bytes 5505024 | tf_op jit(solution)/shard_map/jit(_roll_static)/slice | solution.py:53
  96.9 0.0 copy-done.2
  96.9 0.4 fusion.53
  97.3 1.5 fusion.55
  98.8 2.0 fusion.57
  100.8 2.0 fusion.59
  102.8 2.1 fusion.61
  104.8 2.0 fusion.63
  106.8 14.5 %fusion.19 = f32[512,6,8,16]{0,3,2,1:T(8,128)} fusion(f32[512,18,8,16]{0,3,2,1:T(8,128)S(1)} %copy-done.2, f32[512,6,7,16]{0,3,2,1:T(8,128)} %get-tuple-element.37, f32[512,6,1,16]{0,3,2,1:T(8,128)} %get-tuple-element.39, f32[512,6,1,16]{0,3,2,1:T(8,128)} %get-tuple-element.38, f32[512,6,7,16]{0,3,2,1:T(8,128)} %get-tuple-element.36, ...), kind=kLoop, calls=%fused_computation.24 | loop fusion | flops 28704768 | bytes 51904512 | tf_op jit(solution)/shard_map/mul | solution.py:71
  121.3 3.1 %copy.12 = f32[512,768]{1,0:T(8,128)} copy(f32[512,768]{0,1:T(8,128)} %bitcast.11) | data formatting | bytes 3145728 | tf_op jit(solution)/shard_map/mul | solution.py:71
  124.3 0.0 copy-start.7
  124.3 0.0 copy-start.8
  124.3 0.0 copy-start.9
  124.3 8.1 %all-gather.2.cloned.1.call-done = bf16[512,2048]{1,0:T(8,128)(2,1)} async-done(((bf16[32,2048]{1,0:T(8,128)(2,1)}), bf16[512,2048]{1,0:T(8,128)(2,1)}) %all-gather.2.cloned.1.call-update) | async-done | bytes 2097168 | tf_op jit(solution)/shard_map/all_gather | solution.py:80
  132.4 3.5 %fusion.70 = f32[512,768]{1,0:T(8,128)S(1)} fusion(bf16[512,2048]{1,0:T(8,128)(2,1)} %all-gather.2.cloned.1.call-done, bf16[2048,768]{1,0:T(8,128)(2,1)S(1)} %copy-done), kind=kOutput, calls=%fused_computation.99 | convolution fusion | flops 1610612736 | bytes 6815744 | tf_op jit(solution)/shard_map/dot_general | solution.py:83
  136.0 0.0 copy-start.6
  136.0 1.2 copy-done.6
  137.2 0.0 copy-done.7
  137.2 0.0 copy-done.8
  137.2 0.0 copy-done.9
  137.2 0.0 copy-done.3
  137.2 0.0 copy-done.4
  137.2 0.0 copy-done.5
  137.2 0.0 copy-start.10
  137.2 0.0 copy-start.11
  137.2 1.8 fusion.38
  139.0 0.0 reduce-scatter.5.cloned.1.call-update
  139.0 0.0 copy-done.10
  139.0 0.0 copy-done.11
  139.1 56.2 %reduce-scatter.5.cloned.1.call-done = f32[32,512]{1,0:T(8,128)} async-done(((f32[512,512]{1,0:T(8,128)}), f32[32,512]{1,0:T(8,128)}) %reduce-scatter.5.cloned.1.call-update) | async-done | bytes 65552 | tf_op jit(solution)/shard_map/reduce_scatter | solution.py:91
  195.3 0.8 multiply_convert_fusion.1
  196.2 20.9 %all_gather.7 = bf16[512,512]{1,0:T(8,128)(2,1)S(1)} all-gather(bf16[32,512]{1,0:T(8,128)(2,1)S(1)} %multiply_convert_fusion.1), channel_id=1, replica_groups=mesh['pert'=2,'band'=16] {'band'}, dimensions={0}, use_global_device_ids=true | all-gather | bytes 557056 | tf_op jit(solution)/shard_map/all_gather | solution.py:97
  217.0 4.7 %fusion.68 = (bf16[512,768]{1,0:T(8,128)(2,1)}, bf16[512,768]{1,0:T(8,128)(2,1)}) fusion(bf16[512,768]{1,0:T(8,128)(2,1)} %param.8, bf16[512,768]{1,0:T(8,128)(2,1)} %param.9, bf16[512,512]{1,0:T(8,128)(2,1)S(1)} %all_gather.7, s32[512]{0:T(512)S(1)} %get-tuple-element.42, s32[512]{0:T(512)S(1)} %get-tuple-element.43, s32[512]{0:T(512)S(1)} %copy-done.11, ...), kind=kOutput, calls=%fused_computation.97 | convolution fusion | flops 409993216 | bytes 6830080 | tf_op jit(solution)/shard_map/dot_general | solution.py:107
  (4 shorter events, 0.0 us)
Async XLA Ops:
  7.2 1.9 copy-start
  7.2 82.3 %reduce-scatter.3.cloned.1.call-start = ((), (), s32[]{:S(2)}) async-start(), calls=%async_computation.2 | async-start | bytes 4456448 | tf_op jit(solution)/shard_map/reduce_scatter | solution.py:74
  14.1 118.4 %all-gather.2.cloned.1.call-start = ((), (), s32[]{:S(2)}) async-start(), calls=%async_computation.3 | async-start | bytes 2228224 | tf_op jit(solution)/shard_map/all_gather | solution.py:80
  16.4 15.4 %collective-permute-start = (bf16[512,6,128]{0,2,1:T(8,128)(2,1)}, bf16[512,6,128]{0,2,1:T(8,128)(2,1)S(1)}, u32[]{:S(2)}, u32[]{:S(2)}) collective-permute-start(bf16[512,6,128]{0,2,1:T(8,128)(2,1)} %bitcast.12), channel_id=1, source_target_pairs={{0,1},{1,2},{2,3},{3,4},{4,5},{5,6},{6,7},{7,8},{8,9},{9,10},{10,1... | collective-permute-start | bytes 2359304 | tf_op jit(solution)/shard_map/ppermute | solution.py:34
  16.9 15.0 %collective-permute-start.1 = (bf16[512,6,128]{0,2,1:T(8,128)(2,1)}, bf16[512,6,128]{0,2,1:T(8,128)(2,1)S(1)}, u32[]{:S(2)}, u32[]{:S(2)}) collective-permute-start(bf16[512,6,128]{0,2,1:T(8,128)(2,1)} %bitcast.13), channel_id=1, source_target_pairs={{1,0},{2,1},{3,2},{4,3},{5,4},{6,5},{7,6},{8,7},{9,8},{10,9},{11,1... | collective-permute-start | bytes 2359304 | tf_op jit(solution)/shard_map/ppermute | solution.py:36
  33.3 12.4 %copy-start.1 = (f32[512,18,8,16]{0,3,2,1:T(8,128)}, f32[512,18,8,16]{0,3,2,1:T(8,128)S(1)}, u32[]{:S(2)}) copy-start(f32[512,18,8,16]{0,3,2,1:T(8,128)S(1)} %maximum_convert_fusion) | copy-start | bytes 14155780
  91.2 104.2 %reduce-scatter.5.cloned.1.call-start = ((), (), s32[]{:S(2)}) async-start(), calls=%async_computation.4 | async-start | bytes 1114112 | tf_op jit(solution)/shard_map/reduce_scatter | solution.py:91
  93.0 3.9 %copy-start.2 = (f32[512,18,8,16]{0,3,2,1:T(8,128)S(1)}, f32[512,18,8,16]{0,3,2,1:T(8,128)}, u32[]{:S(2)}) copy-start(f32[512,18,8,16]{0,3,2,1:T(8,128)} %copy-done.1) | copy-start | bytes 14155780
  124.3 12.8 %copy-start.7 = (f32[768]{0:T(1024)S(1)}, f32[768]{0:T(1024)}, u32[]{:S(2)}) copy-start(f32[768]{0:T(1024)} %param.11) | copy-start | bytes 9220
  124.3 12.8 %copy-start.8 = (f32[768]{0:T(1024)S(1)}, f32[768]{0:T(1024)}, u32[]{:S(2)}) copy-start(f32[768]{0:T(1024)} %param.12) | copy-start | bytes 9220
  124.3 12.8 %copy-start.9 = (f32[512]{0:T(512)S(1)}, f32[512]{0:T(512)}, u32[]{:S(2)}) copy-start(f32[512]{0:T(512)} %param.13) | copy-start | bytes 6148
  132.4 4.7 %copy-start.3 = (f32[512,768]{1,0:T(8,128)S(1)}, f32[512,768]{1,0:T(8,128)}, u32[]{:S(2)}) copy-start(f32[512,768]{1,0:T(8,128)} %copy.12) | copy-start | bytes 4718596
  132.4 4.8 %copy-start.4 = (bf16[512,768]{1,0:T(8,128)(2,1)S(1)}, bf16[512,768]{1,0:T(8,128)(2,1)}, u32[]{:S(2)}) copy-start(bf16[512,768]{1,0:T(8,128)(2,1)} %param.8) | copy-start | bytes 2359300
  132.4 4.8 %copy-start.5 = (bf16[512,768]{1,0:T(8,128)(2,1)S(1)}, bf16[512,768]{1,0:T(8,128)(2,1)}, u32[]{:S(2)}) copy-start(bf16[512,768]{1,0:T(8,128)(2,1)} %param.9) | copy-start | bytes 2359300
  136.0 1.2 copy-start.6
  137.2 1.8 copy-start.10
  137.2 1.8 copy-start.11
Sparse Core Ops, SparseCore 0:
  14.2 75.2 reduce-scatter.2
  91.9 40.4 all-gather.1
  139.2 56.1 reduce-scatter.4
where the time goes:
time: 229 us; the launch traced here: 228 us
  waiting for transfers between devices  116 us (51%)
  local copies, waits for them, and re-layouts  38.2 us (17%)
  blocking collectives  20.9 us (9%)
  other arithmetic  18.5 us (8%)
  matrix products  15 us (7%)
  between operations  13.9 us (6%)
  starting transfers between devices  5.54 us (2%)
    reduce_scatter x1, waiting for transfers between devices, shards(): lax.psum_scatter(lax.dot_general(picked, orbitals, CONTRACT_CELLS, prefer...  56.2 us
    reduce_scatter x1, waiting for transfers between devices, shards(): lax.psum_scatter(lax.dot_general(picked, projectors, CONTRACT_CELLS, pref...  42 us
    slice x14, local copies, waits for them, and re-layouts, slab_laplacian(): jnp.roll(centre, -offset, axis_number)  22.5 us
    all_gather x1, blocking collectives, shards(): lax.all_gather((window_share * window_scale).astype(jnp.bfloat16), 'band'...  20.9 us
    mul x1, other arithmetic, shards(): -KINETIC  14.5 us
    ppermute x1, waiting for transfers between devices, padded_2(): lax.ppermute(tail, axis, [(i, (i + 1) % count) for i in range(count)])  9.99 us
    all_gather x1, waiting for transfers between devices, shards(): lax.all_gather((share * ace_scale).astype(jnp.bfloat16), 'band', axis=0,...  8.09 us
    slice x5, local copies, waits for them, and re-layouts, slab_laplacian(): jnp.roll(centre, offset, axis_number)  7.27 us
  transfers between devices with their start and end apart: 5, of which 4 were waited for; matrix products, arithmetic and copies ran while one was open for 22% of the time, Pallas kernels for 0%

commit v1 on v0

v1 whole, which is shorter than its diff:
```python
import functools
import math

import jax
import jax.numpy as jnp
import ml_dtypes
import numpy as np
from jax import lax
from jax.experimental import pallas as pl
from jax.experimental.pallas import tpu as pltpu
from jax.sharding import PartitionSpec as P

GY = 8
GZ = 16
NBLK = 32
REACH = 4
GROUP_BLOCKS = 8
COEFFS = (
    -5369.0 / 1800.0,
    12.0 / 7.0,
    -15.0 / 56.0,
    10.0 / 189.0,
    -1.0 / 112.0,
    2.0 / 1925.0,
    -1.0 / 16632.0,
)
KINETIC = 0.125
STEP_SIZE = 0.3
CHUNKS = 2
VMEM_BYTES = 40 * 1024 * 1024
BF16 = jnp.bfloat16
F32 = jnp.float32
NT = (((1,), (1,)), ((), ()))


def levels_of(count):
    chips = count // 2
    across = 2 ** (int(math.log2(chips)) // 3)
    return (2, 1), (across, 2), (chips // across, 2 * across)


def position(level):
    size, stride = level
    return lax.rem(lax.div(lax.axis_index("band"), jnp.int32(stride)), jnp.int32(size))


def shifted(array, count, level, step):
    size, stride = level
    pairs = []
    for device in range(count):
        place = device // stride % size
        pairs.append((device, device + ((place + step) % size - place) * stride))
    return lax.ppermute(array, "band", pairs)


def plane_matrix():
    plane = GY * GZ
    matrix = 3.0 * COEFFS[0] * np.eye(plane)
    cells = np.arange(plane)
    y, z = cells // GZ, cells % GZ
    for offset in range(1, 7):
        for sign in (1, -1):
            np.add.at(matrix, ((y + sign * offset) % GY * GZ + z, cells), COEFFS[offset])
            np.add.at(matrix, (y * GZ + (z + sign * offset) % GZ, cells), COEFFS[offset])
    matrix = KINETIC * matrix
    high = matrix.astype(ml_dtypes.bfloat16)
    low = (matrix - high.astype(np.float64)).astype(ml_dtypes.bfloat16)
    return np.stack([high, low])


def whole():
    return pl.BlockSpec(memory_space=pltpu.VMEM)


def params():
    return pltpu.CompilerParams(vmem_limit_bytes=VMEM_BYTES)


def cost(flops, *arrays):
    moved = sum(math.prod(a.shape) * jnp.dtype(a.dtype).itemsize for a in arrays)
    return pl.CostEstimate(flops=int(flops), bytes_accessed=int(moved), transcendentals=0)


def local_call(body, outs, args, flops=0, scratch=()):
    return pl.pallas_call(
        body,
        out_shape=outs,
        in_specs=[whole() for _ in args],
        out_specs=jax.tree.map(lambda _: whole(), outs),
        scratch_shapes=scratch,
        compiler_params=params(),
        cost_estimate=cost(flops, *args, *jax.tree.leaves(outs)),
    )(*args)


def struct(shape, dtype):
    return jax.ShapeDtypeStruct(shape, dtype)


def partial_body(core, other, r_ref, p_ref, out_ref):
    half = out_ref.shape[0]
    c = position(core)
    row = pl.multiple_of((1 - c if other else c) * half, half)
    out_ref[...] = lax.dot_general(
        r_ref[pl.ds(row, half), :], p_ref[...], NT, preferred_element_type=F32
    ).astype(out_ref.dtype)


def partial_intersections(response, projectors, chunk, rows, core, other):
    cells = response.shape[1]
    count = projectors.shape[0]
    tile = min(512, count)
    out = struct((rows // 2, count), BF16 if other else F32)
    return pl.pallas_call(
        functools.partial(partial_body, core, other),
        grid=(count // tile,),
        out_shape=out,
        in_specs=[
            pl.BlockSpec((rows, cells), lambda i: (chunk, 0)),
            pl.BlockSpec((tile, cells), lambda i: (i, 0)),
        ],
        out_specs=pl.BlockSpec((rows // 2, tile), lambda i: (0, i)),
        compiler_params=params(),
        cost_estimate=cost(2 * rows // 2 * cells * count, projectors, out),
    )(response, projectors)


def split_body(received, level, along, *refs):
    keep_ref, taken, (own_ref, *sends) = refs[0], refs[1 : 1 + received], refs[1 + received :]
    size, _ = level
    me = position(level)
    width = own_ref.shape[along]
    for step, out in enumerate((own_ref, *sends)):
        at = pl.multiple_of(lax.rem(me + step, jnp.int32(size)) * width, width)
        part = (pl.ds(at, width), slice(None)) if along == 0 else (slice(None), pl.ds(at, width))
        total = keep_ref[part]
        for ref in taken:
            total = total + ref[part].astype(F32)
        out[...] = total.astype(out.dtype)


def split(keep, taken, level, along):
    size, _ = level
    shape = list(keep.shape)
    shape[along] //= size
    outs = [struct(shape, F32)] + [struct(shape, BF16)] * (size - 1)
    return local_call(
        functools.partial(split_body, len(taken), level, along), outs, [keep, *taken]
    )


def finish_body(scale, keep_ref, *refs):
    *taken, out_ref = refs
    total = keep_ref[...]
    for ref in taken:
        total = total + ref[...].astype(F32)
    out_ref[...] = (total * scale).astype(out_ref.dtype)


def finish(keep, taken, scale):
    return local_call(
        functools.partial(finish_body, scale), struct(keep.shape, BF16), [keep, *taken]
    )


def place_body(level, *refs):
    *parts, out_ref = refs
    size, _ = level
    me = position(level)
    width = parts[0].shape[1]
    for step, ref in enumerate(parts):
        at = pl.multiple_of(lax.rem(me - step + size, jnp.int32(size)) * width, width)
        out_ref[:, pl.ds(at, width)] = ref[...]


def place(parts, level):
    rows, width = parts[0].shape
    return local_call(
        functools.partial(place_body, level), struct((rows, width * level[0]), BF16), parts
    )


def local_body(depth, r_ref, l_ref, h_ref, o_ref, m_ref, pot_ref, v_ref, e_ref, out_ref):
    plane = GY * GZ
    reach = 6

    def plane_at(j):
        if j < 0:
            ref, k = l_ref, j + reach
        elif j < depth:
            ref, k = r_ref, j
        else:
            ref, k = h_ref, j - depth
        return ref[:, k * plane : (k + 1) * plane]

    for j in range(depth):
        cols = slice(j * plane, (j + 1) * plane)
        low = plane_at(j)
        centre = low.astype(F32)
        total = jnp.dot(low, m_ref[0], preferred_element_type=F32)
        total = total + jnp.dot(low, m_ref[1], preferred_element_type=F32)
        for offset in range(1, 7):
            pair = plane_at(j + offset).astype(F32) + plane_at(j - offset).astype(F32)
            total = total + (KINETIC * COEFFS[offset]) * pair
        total = total + (e_ref[...] - pot_ref[:, cols]) * centre
        out_ref[:, cols] = total - v_ref[:, cols] * o_ref[:, cols].astype(F32)


def local_part(response, low, high, orbitals, matrix, potential, perturbing, energies, chunk, rows):
    cells = response.shape[1]
    halo = low.shape[1]
    depth = cells // (GY * GZ)
    tile = 128
    per = rows // tile
    out = struct((rows, cells), F32)
    here = pl.BlockSpec((tile, cells), lambda i: (chunk * per + i, 0))
    side = pl.BlockSpec((tile, halo), lambda i: (i, 0))
    line = pl.BlockSpec((1, cells), lambda i: (0, 0))
    return pl.pallas_call(
        functools.partial(local_body, depth),
        grid=(per,),
        out_shape=out,
        in_specs=[
            here,
            side,
            side,
            here,
            pl.BlockSpec(matrix.shape, lambda i: (0, 0, 0)),
            line,
            line,
            pl.BlockSpec((tile, 1), lambda i: (chunk * per + i, 0)),
        ],
        out_specs=pl.BlockSpec((tile, cells), lambda i: (i, 0)),
        compiler_params=params(),
        cost_estimate=cost(2 * rows * cells * 300, low, high, low, low, out),
    )(response, low, high, orbitals, matrix, potential, perturbing, energies)


def first_orbital(group, group_rows, width, bands, blk):
    return max(0, min(group * group_rows - REACH * blk, bands - width))


def apply_body(chunk, core, across, group_rows, width, blk, *refs):
    size = across[0]
    blocks = refs[: 2 * size]
    p_ref, base_ref, o_ref, u_ref, send_ref, keep_ref, c_ref, s_ref = refs[2 * size :]
    rows, cells = u_ref.shape
    bands = o_ref.shape[0]
    c, x = position(core), position(across)
    share = blocks[0].shape[0]
    half = rows // 2
    for k, ref in enumerate(blocks):
        side, step = divmod(k, size)
        at = (c if side == 0 else 1 - c) * half
        at = at + lax.rem(x - step + size, jnp.int32(size)) * share
        c_ref[pl.ds(pl.multiple_of(at, share), share), :] = ref[...]
    tile = 256 if cells % 256 == 0 else 128
    for t in range(cells // tile):
        cols = slice(t * tile, (t + 1) * tile)
        u_ref[:, cols] = base_ref[:, cols] + jnp.dot(
            c_ref[...], p_ref[:, cols], preferred_element_type=F32
        )
    for g in range(rows // group_rows):
        start = first_orbital(chunk * (rows // group_rows) + g, group_rows, width, bands, blk)
        mine = slice(g * group_rows, (g + 1) * group_rows)
        s_ref[mine, :] = lax.dot_general(
            u_ref[mine, :].astype(BF16),
            o_ref[start : start + width, :],
            NT,
            preferred_element_type=F32,
        )
    send_ref[...] = s_ref[pl.ds(pl.multiple_of((1 - c) * half, half), half), :].astype(BF16)
    keep_ref[...] = s_ref[pl.ds(pl.multiple_of(c * half, half), half), :]


def sum_body(keep_ref, *refs):
    *taken, total_ref, low_ref = refs
    total = keep_ref[...]
    for ref in taken:
        total = total + ref[...].astype(F32)
    total_ref[...] = total
    low_ref[...] = total.astype(BF16)


def add_up(keep, taken):
    outs = [struct(keep.shape, F32), struct(keep.shape, BF16)]
    return local_call(sum_body, outs, [keep, *taken])


def project_body(chunk, core, group_rows, width, blk, *refs):
    own_ref, other_ref, o_ref, u_ref, r_ref, first_ref, many_ref = refs[:7]
    updated_ref, residual_ref, w_ref = refs[-3:]
    rows = u_ref.shape[0]
    bands = o_ref.shape[0]
    half = rows // 2
    c = position(core)
    w_ref[pl.ds(pl.multiple_of(c * half, half), half), :] = own_ref[...]
    w_ref[pl.ds(pl.multiple_of((1 - c) * half, half), half), :] = other_ref[...]
    for g in range(rows // group_rows):
        start = first_orbital(chunk * (rows // group_rows) + g, group_rows, width, bands, blk)
        mine = slice(g * group_rows, (g + 1) * group_rows)
        block = (lax.broadcasted_iota(jnp.int32, (group_rows, width), 1) + start) // blk
        lowest = first_ref[mine, :]
        inside = (block >= lowest) & (block < lowest + many_ref[mine, :])
        weights = jnp.where(inside, w_ref[mine, :].astype(F32), 0.0).astype(BF16)
        residual = u_ref[mine, :] - jnp.dot(
            weights, o_ref[start : start + width, :], preferred_element_type=F32
        )
        residual_ref[mine, :] = residual.astype(BF16)
        updated_ref[mine, :] = (r_ref[mine, :].astype(F32) + STEP_SIZE * residual).astype(BF16)


def project(own, other, orbitals, unprojected, response, first, many, before, chunk, core, sizes):
    rows, cells = unprojected.shape
    group_rows, width, blk = sizes
    out = struct(response.shape, BF16)
    here = pl.BlockSpec((rows, cells), lambda i: (chunk, 0))
    column = pl.BlockSpec((rows, 1), lambda i: (chunk, 0))

    def full(a):
        return pl.BlockSpec(a.shape, lambda i: (0, 0))

    args = [own, other, orbitals, unprojected, response, first, many, *before]
    specs = [full(own), full(other), full(orbitals), full(unprojected), here, column, column]
    specs += [pl.BlockSpec(memory_space=pl.ANY)] * len(before)
    return pl.pallas_call(
        functools.partial(project_body, chunk, core, group_rows, width, blk),
        grid=(1,),
        out_shape=[out, out],
        in_specs=specs,
        out_specs=[here, here],
        scratch_shapes=[pltpu.VMEM((rows, width), BF16)],
        input_output_aliases={7: 0, 8: 1} if before else {},
        compiler_params=params(),
        cost_estimate=cost(2 * rows * width * cells, orbitals, unprojected, unprojected),
    )(*args)


def shards(
    count, response, orbitals, projectors, potential, perturbing, energies, window_start, block_count
):
    bands, local_cells = response.shape
    cells = local_cells * count
    plane = GY * GZ
    halo = 6 * plane
    core, across, along = levels_of(count)
    ring = (count, 1)
    ace_scale = 1.0 / math.sqrt(cells * projectors.shape[0])
    window_scale = 1.0 / math.sqrt(cells * bands)
    blk = bands // NBLK
    group_rows = GROUP_BLOCKS * blk
    width = (GROUP_BLOCKS + 2 * REACH) * blk
    rows = bands // CHUNKS
    matrix = jnp.asarray(plane_matrix())
    potential, perturbing = potential[None, :], perturbing[None, :]
    energies, window_start, block_count = (
        a[:, None] for a in (energies, window_start, block_count)
    )

    sides = []
    keeps = []
    sent = []
    for chunk in range(CHUNKS):
        mine = slice(chunk * rows, (chunk + 1) * rows)
        sent.append(
            shifted(
                partial_intersections(response, projectors, chunk, rows, core, True), count, core, 1
            )
        )
        keeps.append(partial_intersections(response, projectors, chunk, rows, core, False))
        sides.append(
            (
                shifted(response[mine, local_cells - halo :], count, ring, 1),
                shifted(response[mine, :halo], count, ring, -1),
            )
        )

    outs = ()
    for chunk in range(CHUNKS):
        keep, *parts = split(keeps[chunk], [sent[chunk]], across, 0)
        taken = [shifted(part, count, across, k + 1) for k, part in enumerate(parts)]
        keep, *parts = split(keep, taken, along, 1)
        taken = [shifted(part, count, along, k + 1) for k, part in enumerate(parts)]
        share = finish(keep, taken, ace_scale)
        pieces = [share] + [shifted(share, count, along, k) for k in range(1, along[0])]
        own = place(pieces, along)
        blocks = [own] + [shifted(own, count, across, k) for k in range(1, across[0])]
        blocks += [shifted(block, count, core, 1) for block in blocks]
        low, high = sides[chunk]
        base = local_part(
            response, low, high, orbitals, matrix, potential, perturbing, energies, chunk, rows
        )
        unprojected, send, keep = local_call(
            functools.partial(apply_body, chunk, core, across, group_rows, width, blk),
            [
                struct((rows, local_cells), F32),
                struct((rows // 2, width), BF16),
                struct((rows // 2, width), F32),
            ],
            [*blocks, projectors, base, orbitals],
            flops=2 * rows * local_cells * (projectors.shape[0] + width),
            scratch=[
                pltpu.VMEM((rows, projectors.shape[0]), BF16),
                pltpu.VMEM((rows, width), F32),
            ],
        )
        total, low = add_up(keep, [shifted(send, count, core, 1)])
        total, low = add_up(total, [shifted(low, count, across, k) for k in range(1, across[0])])
        weights = finish(
            total, [shifted(low, count, along, k) for k in range(1, along[0])], window_scale
        )
        outs = project(
            weights,
            shifted(weights, count, core, 1),
            orbitals,
            unprojected,
            response,
            window_start,
            block_count,
            outs,
            chunk,
            core,
            (group_rows, width, blk),
        )
    return tuple(outs)


def solution(mesh):
    in_specs = (
        P("pert", "band"),
        P(None, "band"),
        P(None, "band"),
        P("band"),
        P(("pert", "band")),
        P(),
        P(),
        P(),
    )
    out_specs = (P("pert", "band"), P("pert", "band"))
    body = functools.partial(shards, mesh.shape["band"])
    return jax.shard_map(body, mesh=mesh, in_specs=in_specs, out_specs=out_specs, check_vma=False)
```

time: 229 us -> 115 us (0.50)
  waiting for transfers between devices: 116 us -> 43.4 us
  starting transfers between devices: 5.54 us -> 45.4 us
  local copies, waits for them, and re-layouts: 38.2 us -> 6.28 us
  blocking collectives: 20.9 us -> 0 us
  other arithmetic: 18.5 us -> 0 us
  Pallas kernels: 0 us -> 18 us
  matrix products: 15 us -> 0 us
  between operations: 13.9 us -> 1.05 us
    reduce_scatter x2 -> x0, waiting for transfers between devices: 98.2 us -> none  [the longest x1 56.2 us: shards(): lax.psum_scatter(lax.dot_general(picked, orbitals, CONTRACT_CELLS, prefer...]
    ppermute x2 -> x38, starting transfers between devices: 5.42 us -> 45.4 us  [shifted(): return lax.ppermute(array, 'band', pairs)]
    ppermute x2 -> x38, waiting for transfers between devices: 9.99 us -> 43.4 us  [shifted(): return lax.ppermute(array, 'band', pairs)]
    slice x19 -> x1, local copies, waits for them, and re-layouts: 29.8 us -> 0.8 us  [shards(): response[mine, local_cells - halo:]]
    all_gather x1 -> x0, blocking collectives: 20.9 us -> none  [shards(): lax.all_gather((window_share * window_scale).astype(jnp.bfloat16), 'band'...]
    pallas_call x0 -> x24, Pallas kernels: none -> 18 us  [the longest x4 6.62 us: partial_intersections(): pl.pallas_call(functools.partial(partial_body, core, other), grid=(count...]
    dot_general x4 -> x0, matrix products: 15 us -> none  [the longest x1 4.97 us: shards(): lax.dot_general(picked, projectors, CONTRACT_CELLS, preferred_element_typ...]
    mul x1 -> x0, other arithmetic: 14.5 us -> none  [shards(): -KINETIC]
  transfers between devices with their start and end apart: 5 -> 38, of which waited for: 4 -> 15; matrix products, arithmetic and copies ran while one was open for 22% -> 1% of each run, Pallas kernels for 0% -> 13%
where the time goes in v1:
time: 115 us; the launch traced here: 114 us
  starting transfers between devices  45.4 us (39%)
  waiting for transfers between devices  43.4 us (38%)
  Pallas kernels  18 us (16%)
  local copies, waits for them, and re-layouts  6.28 us (5%)
    ppermute x38, starting transfers between devices, shifted(): return lax.ppermute(array, 'band', pairs)  45.4 us
    ppermute x38, waiting for transfers between devices, shifted(): return lax.ppermute(array, 'band', pairs)  43.4 us
    pallas_call x4, Pallas kernels, partial_intersections(): pl.pallas_call(functools.partial(partial_body, core, other), grid=(count...  6.62 us
    pallas_call x16, Pallas kernels, local_call(): pl.pallas_call(body, out_shape=outs, in_specs=[whole() for _ in args], ou...  5.91 us
    unnamed x28, local copies, waits for them, and re-layouts  5.04 us
    pallas_call x2, Pallas kernels, local_part(): pl.pallas_call(functools.partial(local_body, depth), grid=(per,), out_sha...  3.1 us
    pallas_call x2, Pallas kernels, project(): pl.pallas_call(functools.partial(project_body, chunk, core, group_rows, w...  2.42 us
  transfers between devices with their start and end apart: 38, of which 15 were waited for; matrix products, arithmetic and copies ran while one was open for 1% of the time, Pallas kernels for 13%

profile of v1, /device:TPU:0, one launch (start us, length us, event | category | flops | bytes accessed | tf_op | source)
XLA Modules:
  0.0 114.2 jit_solution(12654068588538816622)
XLA Ops:
  0.6 1.9 %copy-done = bf16[2048,768]{1,0:T(8,128)(2,1)S(1)} copy-done((bf16[2048,768]{1,0:T(8,128)(2,1)S(1)}, bf16[2048,768]{1,0:T(8,128)(2,1)}, u32[]{:S(2)}) %copy-start) | copy-done | bytes 3145752
  2.5 1.1 copy-done.2
  3.7 1.7 %shard_map.105 = bf16[128,2048]{1,0:T(8,128)(2,1)S(1)} custom-call(bf16[512,768]{1,0:T(8,128)(2,1)S(1)} %copy-done.2, bf16[2048,768]{1,0:T(8,128)(2,1)S(1)} %copy-done), custom_call_target="tpu_custom_call" | custom-call | flops 402653184 | bytes 3670016 | tf_op jit(solution)/shard_map/pallas_call | solution.py:114
  5.3 0.5 collective-permute-start
  5.8 1.7 %shard_map.116 = bf16[128,2048]{1,0:T(8,128)(2,1)S(1)} custom-call(bf16[512,768]{1,0:T(8,128)(2,1)S(1)} %copy-done.2, bf16[2048,768]{1,0:T(8,128)(2,1)S(1)} %copy-done), custom_call_target="tpu_custom_call" | custom-call | flops 402653184 | bytes 3670016 | tf_op jit(solution)/shard_map/pallas_call | solution.py:114
  7.5 0.2 collective-permute-start.19
  7.6 1.6 %shard_map.104.refs_0_ = f32[128,2048]{1,0:T(8,128)S(1)} custom-call(bf16[512,768]{1,0:T(8,128)(2,1)S(1)} %copy-done.2, bf16[2048,768]{1,0:T(8,128)(2,1)S(1)} %copy-done), custom_call_target="tpu_custom_call" | custom-call | flops 402653184 | bytes 4194304 | tf_op jit(solution)/shard_map/pallas_call | solution.py:114
  9.3 1.7 %shard_map.115.refs_0_ = f32[128,2048]{1,0:T(8,128)S(1)} custom-call(bf16[512,768]{1,0:T(8,128)(2,1)S(1)} %copy-done.2, bf16[2048,768]{1,0:T(8,128)(2,1)S(1)} %copy-done), custom_call_target="tpu_custom_call" | custom-call | flops 402653184 | bytes 4194304 | tf_op jit(solution)/shard_map/pallas_call | solution.py:114
  11.0 0.1 shard_map.106
  11.1 3.0 %collective-permute-start.1 = (bf16[64,2048]{1,0:T(8,128)(2,1)S(1)}, bf16[64,2048]{1,0:T(8,128)(2,1)S(1)}, u32[]{:S(2)}, u32[]{:S(2)}) collective-permute-start(bf16[64,2048]{1,0:T(8,128)(2,1)S(1)} %get-tuple-element.31), channel_id=1, source_target_pairs={{0,2},{1,3},{2,0},{3,1},{4,6},{5,7},{6,4},{7,5},{8,10},{9,11},{10,... | collective-permute-start | bytes 786440 | tf_op jit(solution)/shard_map/ppermute | solution.py:53
  14.1 0.1 shard_map.117
  14.2 0.1 collective-permute-start.20
  14.3 0.8 fusion
  15.1 15.4 %collective-permute-done.20.refs_1_ = bf16[64,2048]{1,0:T(8,128)(2,1)S(1)} collective-permute-done((bf16[64,2048]{1,0:T(8,128)(2,1)S(1)}, bf16[64,2048]{1,0:T(8,128)(2,1)S(1)}, u32[]{:S(2)}, u32[]{:S(2)}) %collective-permute-start.20) | collective-permute-done | bytes 262176 | tf_op jit(solution)/shard_map/ppermute | solution.py:53
  30.5 1.8 %collective-permute-start.21 = (bf16[64,512]{1,0:T(8,128)(2,1)S(1)}, bf16[64,512]{1,0:T(8,128)(2,1)S(1)}, u32[]{:S(2)}, u32[]{:S(2)}) collective-permute-start(bf16[64,512]{1,0:T(8,128)(2,1)S(1)} %get-tuple-element.46), channel_id=1, source_target_pairs={{0,4},{1,5},{2,6},{3,7},{4,8},{5,9},{6,10},{7,11},{8,12},{9,13},{1... | collective-permute-start | bytes 196616 | tf_op jit(solution)/shard_map/ppermute | solution.py:53
  32.4 2.6 %collective-permute-start.22 = (bf16[64,512]{1,0:T(8,128)(2,1)S(1)}, bf16[64,512]{1,0:T(8,128)(2,1)S(1)}, u32[]{:S(2)}, u32[]{:S(2)}) collective-permute-start(bf16[64,512]{1,0:T(8,128)(2,1)S(1)} %get-tuple-element.47), channel_id=1, source_target_pairs={{0,8},{1,9},{2,10},{3,11},{4,12},{5,13},{6,14},{7,15},{8,0},{9,1},... | collective-permute-start | bytes 196616 | tf_op jit(solution)/shard_map/ppermute | solution.py:53
  35.0 1.4 %collective-permute-start.23 = (bf16[64,512]{1,0:T(8,128)(2,1)S(1)}, bf16[64,512]{1,0:T(8,128)(2,1)S(1)}, u32[]{:S(2)}, u32[]{:S(2)}) collective-permute-start(bf16[64,512]{1,0:T(8,128)(2,1)S(1)} %get-tuple-element.48), channel_id=1, source_target_pairs={{0,12},{1,13},{2,14},{3,15},{4,0},{5,1},{6,2},{7,3},{8,4},{9,5},{1... | collective-permute-start | bytes 196616 | tf_op jit(solution)/shard_map/ppermute | solution.py:53
  36.4 0.7 collective-permute-start.2
  37.1 0.3 collective-permute-done.21.refs_0_
  37.5 1.8 %collective-permute-start.3 = (bf16[64,512]{1,0:T(8,128)(2,1)S(1)}, bf16[64,512]{1,0:T(8,128)(2,1)S(1)}, u32[]{:S(2)}, u32[]{:S(2)}) collective-permute-start(bf16[64,512]{1,0:T(8,128)(2,1)S(1)} %get-tuple-element.34), channel_id=1, source_target_pairs={{0,8},{1,9},{2,10},{3,11},{4,12},{5,13},{6,14},{7,15},{8,0},{9,1},... | collective-permute-start | bytes 196616 | tf_op jit(solution)/shard_map/ppermute | solution.py:53
  39.3 1.7 %collective-permute-done.22.refs_1_ = bf16[64,512]{1,0:T(8,128)(2,1)S(1)} collective-permute-done((bf16[64,512]{1,0:T(8,128)(2,1)S(1)}, bf16[64,512]{1,0:T(8,128)(2,1)S(1)}, u32[]{:S(2)}, u32[]{:S(2)}) %collective-permute-start.22) | collective-permute-done | bytes 65568 | tf_op jit(solution)/shard_map/ppermute | solution.py:53
  41.0 3.5 %collective-permute-start.4 = (bf16[64,512]{1,0:T(8,128)(2,1)S(1)}, bf16[64,512]{1,0:T(8,128)(2,1)S(1)}, u32[]{:S(2)}, u32[]{:S(2)}) collective-permute-start(bf16[64,512]{1,0:T(8,128)(2,1)S(1)} %get-tuple-element.35), channel_id=1, source_target_pairs={{0,12},{1,13},{2,14},{3,15},{4,0},{5,1},{6,2},{7,3},{8,4},{9,5},{1... | collective-permute-start | bytes 196616 | tf_op jit(solution)/shard_map/ppermute | solution.py:53
  44.5 0.6 collective-permute-start.24
  45.1 0.7 collective-permute-done.3.refs_1_
  45.8 0.6 collective-permute-done.4.refs_2_
  46.4 4.2 %collective-permute-start.26 = (bf16[64,512]{1,0:T(8,128)(2,1)S(1)}, bf16[64,512]{1,0:T(8,128)(2,1)S(1)}, u32[]{:S(2)}, u32[]{:S(2)}) collective-permute-start(bf16[64,512]{1,0:T(8,128)(2,1)S(1)} %shard_map.119.refs_0_), channel_id=1, source_target_pairs={{0,12},{1,13},{2,14},{3,15},{4,0},{5,1},{6,2},{7,3},{8,4},{9,5},{1... | collective-permute-start | bytes 196616 | tf_op jit(solution)/shard_map/ppermute | solution.py:53
  50.6 0.8 collective-permute-done.24.refs_1_
  51.4 4.4 %collective-permute-done.25.refs_2_ = bf16[64,512]{1,0:T(8,128)(2,1)S(1)} collective-permute-done((bf16[64,512]{1,0:T(8,128)(2,1)S(1)}, bf16[64,512]{1,0:T(8,128)(2,1)S(1)}, u32[]{:S(2)}, u32[]{:S(2)}) %collective-permute-start.25) | collective-permute-done | bytes 65568 | tf_op jit(solution)/shard_map/ppermute | solution.py:53
  55.8 2.3 %collective-permute-start.6 = (bf16[64,512]{1,0:T(8,128)(2,1)S(1)}, bf16[64,512]{1,0:T(8,128)(2,1)S(1)}, u32[]{:S(2)}, u32[]{:S(2)}) collective-permute-start(bf16[64,512]{1,0:T(8,128)(2,1)S(1)} %shard_map.108.refs_0_), channel_id=1, source_target_pairs={{0,8},{1,9},{2,10},{3,11},{4,12},{5,13},{6,14},{7,15},{8,0},{9,1},... | collective-permute-start | bytes 196616 | tf_op jit(solution)/shard_map/ppermute | solution.py:53
  58.1 0.8 collective-permute-done.5.refs_1_
  58.9 2.1 %collective-permute-done.6.refs_2_ = bf16[64,512]{1,0:T(8,128)(2,1)S(1)} collective-permute-done((bf16[64,512]{1,0:T(8,128)(2,1)S(1)}, bf16[64,512]{1,0:T(8,128)(2,1)S(1)}, u32[]{:S(2)}, u32[]{:S(2)}) %collective-permute-start.6) | collective-permute-done | bytes 65568 | tf_op jit(solution)/shard_map/ppermute | solution.py:53
  61.0 4.6 %collective-permute-start.7 = (bf16[64,512]{1,0:T(8,128)(2,1)S(1)}, bf16[64,512]{1,0:T(8,128)(2,1)S(1)}, u32[]{:S(2)}, u32[]{:S(2)}) collective-permute-start(bf16[64,512]{1,0:T(8,128)(2,1)S(1)} %shard_map.108.refs_0_), channel_id=1, source_target_pairs={{0,12},{1,13},{2,14},{3,15},{4,0},{5,1},{6,2},{7,3},{8,4},{9,5},{1... | collective-permute-start | bytes 196616 | tf_op jit(solution)/shard_map/ppermute | solution.py:53
  65.6 1.9 %collective-permute-done.7.refs_3_ = bf16[64,512]{1,0:T(8,128)(2,1)S(1)} collective-permute-done((bf16[64,512]{1,0:T(8,128)(2,1)S(1)}, bf16[64,512]{1,0:T(8,128)(2,1)S(1)}, u32[]{:S(2)}, u32[]{:S(2)}) %collective-permute-start.7) | collective-permute-done | bytes 65568 | tf_op jit(solution)/shard_map/ppermute | solution.py:53
  67.6 2.6 %collective-permute-start.8 = (bf16[64,2048]{1,0:T(8,128)(2,1)S(1)}, bf16[64,2048]{1,0:T(8,128)(2,1)}, u32[]{:S(2)}, u32[]{:S(2)}) collective-permute-start(bf16[64,2048]{1,0:T(8,128)(2,1)S(1)} %shard_map.109.refs_0_), channel_id=1, source_target_pairs={{0,2},{1,3},{2,0},{3,1},{4,6},{5,7},{6,4},{7,5},{8,10},{9,11},{10,... | collective-permute-start | bytes 786440 | tf_op jit(solution)/shard_map/ppermute | solution.py:53
  70.2 2.0 %collective-permute-start.31 = (bf16[256,768]{1,0:T(8,128)(2,1)}, bf16[256,768]{1,0:T(8,128)(2,1)}, u32[]{:S(2)}, u32[]{:S(2)}) collective-permute-start(bf16[256,768]{1,0:T(8,128)(2,1)} %get-tuple-element.58), channel_id=1, source_target_pairs={{0,15},{1,0},{2,1},{3,2},{4,3},{5,4},{6,5},{7,6},{8,7},{9,8},{10,9... | collective-permute-start | bytes 1179656 | tf_op jit(solution)/shard_map/ppermute | solution.py:53
  72.1 0.9 collective-permute-start.29
  73.1 7.1 %collective-permute-done.8.refs_1_ = bf16[64,2048]{1,0:T(8,128)(2,1)} collective-permute-done((bf16[64,2048]{1,0:T(8,128)(2,1)S(1)}, bf16[64,2048]{1,0:T(8,128)(2,1)}, u32[]{:S(2)}, u32[]{:S(2)}) %collective-permute-start.8) | collective-permute-done | bytes 262176 | tf_op jit(solution)/shard_map/ppermute | solution.py:53
  80.3 0.1 copy.13.e_ref
  80.4 0.8 copy-done.7
  81.3 1.1 shard_map.110.refs_5_
  82.4 2.0 %shard_map.121.refs_5_ = f32[256,768]{1,0:T(8,128)S(1)} custom-call(bf16[512,768]{1,0:T(8,128)(2,1)S(1)} %copy-done.3, bf16[256,768]{1,0:T(8,128)(2,1)S(1)} %collective-permute-done.30.l_ref, bf16[256,768]{1,0:T(8,128)(2,1)} %collective-permute-done.31.h_ref, bf16[512,768]{1,0:T(8,128)(2,1)S(1)} %copy-done.4, bf16[2,128,128]{2,1,0:T(8,128)(2,1)S(1)} %copy-done.8, ...), custom_call_target="tpu_custom_call" | custom-call | flops 117964800 | bytes 2359296 | tf_op jit(solution)/shard_map/pallas_call | solution.py:219
  84.4 2.7 %shard_map.122 = (f32[256,768]{1,0:T(8,128)S(1)}, bf16[128,256]{1,0:T(8,128)(2,1)S(1)}, f32[128,256]{1,0:T(8,128)S(1)}) custom-call(bf16[64,2048]{1,0:T(8,128)(2,1)S(1)} %shard_map.120.refs_0_, bf16[64,2048]{1,0:T(8,128)(2,1)} %collective-permute-done.27.refs_1_, bf16[64,2048]{1,0:T(8,128)(2,1)} %collective-permute-done.28.refs_2_, ...), custom_call_target="tpu_custom_call" | custom-call | flops 905969664 | bytes 6750208 | tf_op jit(solution)/shard_map/pallas_call | solution.py:85
  87.2 0.6 collective-permute-start.32
  87.7 2.7 %shard_map.111 = (f32[256,768]{1,0:T(8,128)S(1)}, bf16[128,256]{1,0:T(8,128)(2,1)S(1)}, f32[128,256]{1,0:T(8,128)S(1)}) custom-call(bf16[64,2048]{1,0:T(8,128)(2,1)S(1)} %shard_map.109.refs_0_, bf16[64,2048]{1,0:T(8,128)(2,1)} %collective-permute-done.8.refs_1_, bf16[64,2048]{1,0:T(8,128)(2,1)} %collective-permute-done.9.refs_2_, ...), custom_call_target="tpu_custom_call" | custom-call | flops 905969664 | bytes 6750208 | tf_op jit(solution)/shard_map/pallas_call | solution.py:85
  90.4 0.3 collective-permute-start.13
  90.7 2.7 %collective-permute-start.33 = (bf16[128,256]{1,0:T(8,128)(2,1)S(1)}, bf16[128,256]{1,0:T(8,128)(2,1)S(1)}, u32[]{:S(2)}, u32[]{:S(2)}) collective-permute-start(bf16[128,256]{1,0:T(8,128)(2,1)S(1)} %get-tuple-element.52), channel_id=1, source_target_pairs={{0,2},{1,3},{2,0},{3,1},{4,6},{5,7},{6,4},{7,5},{8,10},{9,11},{10,... | collective-permute-start | bytes 196616 | tf_op jit(solution)/shard_map/ppermute | solution.py:53
  93.4 1.0 collective-permute-start.14
  94.4 1.5 %collective-permute-done.33.refs_0_ = bf16[128,256]{1,0:T(8,128)(2,1)S(1)} collective-permute-done((bf16[128,256]{1,0:T(8,128)(2,1)S(1)}, bf16[128,256]{1,0:T(8,128)(2,1)S(1)}, u32[]{:S(2)}, u32[]{:S(2)}) %collective-permute-start.33) | collective-permute-done | bytes 65568 | tf_op jit(solution)/shard_map/ppermute | solution.py:53
  95.9 0.9 collective-permute-start.34
  96.8 2.0 %collective-permute-start.35 = (bf16[128,256]{1,0:T(8,128)(2,1)S(1)}, bf16[128,256]{1,0:T(8,128)(2,1)S(1)}, u32[]{:S(2)}, u32[]{:S(2)}) collective-permute-start(bf16[128,256]{1,0:T(8,128)(2,1)S(1)} %get-tuple-element.54), channel_id=1, source_target_pairs={{0,8},{1,9},{2,10},{3,11},{4,12},{5,13},{6,14},{7,15},{8,0},{9,1},... | collective-permute-start | bytes 196616 | tf_op jit(solution)/shard_map/ppermute | solution.py:53
  98.8 1.0 collective-permute-start.36
  99.8 1.0 collective-permute-start.15
  100.9 1.1 collective-permute-start.16
  102.0 0.8 collective-permute-done.34.refs_0_
  102.8 2.0 %collective-permute-start.17 = (bf16[128,256]{1,0:T(8,128)(2,1)S(1)}, bf16[128,256]{1,0:T(8,128)(2,1)S(1)}, u32[]{:S(2)}, u32[]{:S(2)}) collective-permute-start(bf16[128,256]{1,0:T(8,128)(2,1)S(1)} %get-tuple-element.41), channel_id=1, source_target_pairs={{0,12},{1,13},{2,14},{3,15},{4,0},{5,1},{6,2},{7,3},{8,4},{9,5},{1... | collective-permute-start | bytes 196616 | tf_op jit(solution)/shard_map/ppermute | solution.py:53
  104.8 1.8 %collective-permute-done.35.refs_1_ = bf16[128,256]{1,0:T(8,128)(2,1)S(1)} collective-permute-done((bf16[128,256]{1,0:T(8,128)(2,1)S(1)}, bf16[128,256]{1,0:T(8,128)(2,1)S(1)}, u32[]{:S(2)}, u32[]{:S(2)}) %collective-permute-start.35) | collective-permute-done | bytes 65568 | tf_op jit(solution)/shard_map/ppermute | solution.py:53
  106.7 0.1 collective-permute-start.37
  106.8 3.4 %collective-permute-done.16.refs_1_ = bf16[128,256]{1,0:T(8,128)(2,1)S(1)} collective-permute-done((bf16[128,256]{1,0:T(8,128)(2,1)S(1)}, bf16[128,256]{1,0:T(8,128)(2,1)S(1)}, u32[]{:S(2)}, u32[]{:S(2)}) %collective-permute-start.16) | collective-permute-done | bytes 65568 | tf_op jit(solution)/shard_map/ppermute | solution.py:53
  110.2 0.1 collective-permute-start.18
  110.3 0.1 copy.17.refs_5_
  110.5 0.1 copy.18.refs_6_
  110.6 1.1 copy-done.6
  111.8 1.2 %shard_map.126 = (bf16[512,768]{1,0:T(8,128)(2,1)}, bf16[512,768]{1,0:T(8,128)(2,1)}) custom-call(bf16[128,256]{1,0:T(8,128)(2,1)S(1)} %shard_map.125.refs_0_, bf16[128,256]{1,0:T(8,128)(2,1)S(1)} %collective-permute-done.37.refs_1_, bf16[512,768]{1,0:T(8,128)(2,1)S(1)} %copy-done.4, f32[256,768]{1,0:T(8,128)S(1)} %copy-done.6, ...), custom_call_target="tpu_custom_call" | custom-call | flops 100663296 | bytes 2359296 | tf_op jit(solution)/shard_map/pallas_call | solution.py:326
  113.0 1.2 %shard_map.127 = (bf16[512,768]{1,0:T(8,128)(2,1)}, bf16[512,768]{1,0:T(8,128)(2,1)}) custom-call(bf16[128,256]{1,0:T(8,128)(2,1)S(1)} %shard_map.114.refs_0_, bf16[128,256]{1,0:T(8,128)(2,1)S(1)} %collective-permute-done.18.refs_1_, bf16[512,768]{1,0:T(8,128)(2,1)S(1)} %copy-done.4, ...), custom_call_target="tpu_custom_call", output_to_operand_aliasing={{0}: (7, {}), {1}: (8, {})} | custom-call | flops 100663296 | bytes 2359296 | tf_op jit(solution)/shard_map/pallas_call | solution.py:326
  (70 shorter events, 0.6 us)
Async XLA Ops:
  0.6 1.9 %copy-start = (bf16[2048,768]{1,0:T(8,128)(2,1)S(1)}, bf16[2048,768]{1,0:T(8,128)(2,1)}, u32[]{:S(2)}) copy-start(bf16[2048,768]{1,0:T(8,128)(2,1)} %refs_4_.5) | copy-start | bytes 9437188
  2.5 1.1 copy-start.2
  5.3 5.6 %collective-permute-start = (bf16[128,2048]{1,0:T(8,128)(2,1)S(1)}, bf16[128,2048]{1,0:T(8,128)(2,1)S(1)}, u32[]{:S(2)}, u32[]{:S(2)}) collective-permute-start(bf16[128,2048]{1,0:T(8,128)(2,1)S(1)} %shard_map.105), channel_id=1, source_target_pairs={{0,1},{1,0},{2,3},{3,2},{4,5},{5,4},{6,7},{7,6},{8,9},{9,8},{10,11... | collective-permute-start | bytes 1572872 | tf_op jit(solution)/shard_map/ppermute | solution.py:53
  7.5 6.6 %collective-permute-start.19 = (bf16[128,2048]{1,0:T(8,128)(2,1)S(1)}, bf16[128,2048]{1,0:T(8,128)(2,1)S(1)}, u32[]{:S(2)}, u32[]{:S(2)}) collective-permute-start(bf16[128,2048]{1,0:T(8,128)(2,1)S(1)} %shard_map.116), channel_id=1, source_target_pairs={{0,1},{1,0},{2,3},{3,2},{4,5},{5,4},{6,7},{7,6},{8,9},{9,8},{10,11... | collective-permute-start | bytes 1572872 | tf_op jit(solution)/shard_map/ppermute | solution.py:53
  9.3 5.0 %copy-start.3 = (bf16[512,768]{1,0:T(8,128)(2,1)S(1)}, bf16[512,768]{1,0:T(8,128)(2,1)}, u32[]{:S(2)}) copy-start(bf16[512,768]{1,0:T(8,128)(2,1)} %refs_4_.7) | copy-start | bytes 2359300
  11.1 69.1 %copy-start.9 = (f32[768]{0:T(1024)S(1)}, f32[768]{0:T(1024)}, u32[]{:S(2)}) copy-start(f32[768]{0:T(1024)} %param.12) | copy-start | bytes 9220
  11.1 69.1 %copy-start.10 = (f32[768]{0:T(1024)S(1)}, f32[768]{0:T(1024)}, u32[]{:S(2)}) copy-start(f32[768]{0:T(1024)} %param.13) | copy-start | bytes 9220
  11.1 69.2 %copy-start.11 = (f32[512]{0:T(512)S(1)}, f32[512]{0:T(512)}, u32[]{:S(2)}) copy-start(f32[512]{0:T(512)} %param.14) | copy-start | bytes 6148
  11.1 69.3 %copy-start.4 = (bf16[512,768]{1,0:T(8,128)(2,1)S(1)}, bf16[512,768]{1,0:T(8,128)(2,1)}, u32[]{:S(2)}) copy-start(bf16[512,768]{1,0:T(8,128)(2,1)} %refs_2_.3) | copy-start | bytes 2359300
  11.1 25.2 %collective-permute-start.1 = (bf16[64,2048]{1,0:T(8,128)(2,1)S(1)}, bf16[64,2048]{1,0:T(8,128)(2,1)S(1)}, u32[]{:S(2)}, u32[]{:S(2)}) collective-permute-start(bf16[64,2048]{1,0:T(8,128)(2,1)S(1)} %get-tuple-element.31), channel_id=1, source_target_pairs={{0,2},{1,3},{2,0},{3,1},{4,6},{5,7},{6,4},{7,5},{8,10},{9,11},{10,... | collective-permute-start | bytes 786440 | tf_op jit(solution)/shard_map/ppermute | solution.py:53
  14.2 16.3 %collective-permute-start.20 = (bf16[64,2048]{1,0:T(8,128)(2,1)S(1)}, bf16[64,2048]{1,0:T(8,128)(2,1)S(1)}, u32[]{:S(2)}, u32[]{:S(2)}) collective-permute-start(bf16[64,2048]{1,0:T(8,128)(2,1)S(1)} %get-tuple-element.44), channel_id=1, source_target_pairs={{0,2},{1,3},{2,0},{3,1},{4,6},{5,7},{6,4},{7,5},{8,10},{9,11},{10,... | collective-permute-start | bytes 786440 | tf_op jit(solution)/shard_map/ppermute | solution.py:53
  15.1 55.1 %collective-permute-start.11 = (bf16[256,768]{1,0:T(8,128)(2,1)S(1)}, bf16[256,768]{1,0:T(8,128)(2,1)S(1)}, u32[]{:S(2)}, u32[]{:S(2)}) collective-permute-start(bf16[256,768]{1,0:T(8,128)(2,1)S(1)} %get-tuple-element.59), channel_id=1, source_target_pairs={{0,1},{1,2},{2,3},{3,4},{4,5},{5,6},{6,7},{7,8},{8,9},{9,10},{10,1... | collective-permute-start | bytes 1179656 | tf_op jit(solution)/shard_map/ppermute | solution.py:53
  30.5 6.9 %collective-permute-start.21 = (bf16[64,512]{1,0:T(8,128)(2,1)S(1)}, bf16[64,512]{1,0:T(8,128)(2,1)S(1)}, u32[]{:S(2)}, u32[]{:S(2)}) collective-permute-start(bf16[64,512]{1,0:T(8,128)(2,1)S(1)} %get-tuple-element.46), channel_id=1, source_target_pairs={{0,4},{1,5},{2,6},{3,7},{4,8},{5,9},{6,10},{7,11},{8,12},{9,13},{1... | collective-permute-start | bytes 196616 | tf_op jit(solution)/shard_map/ppermute | solution.py:53
  32.4 8.6 %collective-permute-start.22 = (bf16[64,512]{1,0:T(8,128)(2,1)S(1)}, bf16[64,512]{1,0:T(8,128)(2,1)S(1)}, u32[]{:S(2)}, u32[]{:S(2)}) collective-permute-start(bf16[64,512]{1,0:T(8,128)(2,1)S(1)} %get-tuple-element.47), channel_id=1, source_target_pairs={{0,8},{1,9},{2,10},{3,11},{4,12},{5,13},{6,14},{7,15},{8,0},{9,1},... | collective-permute-start | bytes 196616 | tf_op jit(solution)/shard_map/ppermute | solution.py:53
  35.0 9.5 %collective-permute-start.23 = (bf16[64,512]{1,0:T(8,128)(2,1)S(1)}, bf16[64,512]{1,0:T(8,128)(2,1)S(1)}, u32[]{:S(2)}, u32[]{:S(2)}) collective-permute-start(bf16[64,512]{1,0:T(8,128)(2,1)S(1)} %get-tuple-element.48), channel_id=1, source_target_pairs={{0,12},{1,13},{2,14},{3,15},{4,0},{5,1},{6,2},{7,3},{8,4},{9,5},{1... | collective-permute-start | bytes 196616 | tf_op jit(solution)/shard_map/ppermute | solution.py:53
  36.4 8.7 %collective-permute-start.2 = (bf16[64,512]{1,0:T(8,128)(2,1)S(1)}, bf16[64,512]{1,0:T(8,128)(2,1)S(1)}, u32[]{:S(2)}, u32[]{:S(2)}) collective-permute-start(bf16[64,512]{1,0:T(8,128)(2,1)S(1)} %get-tuple-element.33), channel_id=1, source_target_pairs={{0,4},{1,5},{2,6},{3,7},{4,8},{5,9},{6,10},{7,11},{8,12},{9,13},{1... | collective-permute-start | bytes 196616 | tf_op jit(solution)/shard_map/ppermute | solution.py:53
  37.5 8.3 %collective-permute-start.3 = (bf16[64,512]{1,0:T(8,128)(2,1)S(1)}, bf16[64,512]{1,0:T(8,128)(2,1)S(1)}, u32[]{:S(2)}, u32[]{:S(2)}) collective-permute-start(bf16[64,512]{1,0:T(8,128)(2,1)S(1)} %get-tuple-element.34), channel_id=1, source_target_pairs={{0,8},{1,9},{2,10},{3,11},{4,12},{5,13},{6,14},{7,15},{8,0},{9,1},... | collective-permute-start | bytes 196616 | tf_op jit(solution)/shard_map/ppermute | solution.py:53
  41.0 5.4 %collective-permute-start.4 = (bf16[64,512]{1,0:T(8,128)(2,1)S(1)}, bf16[64,512]{1,0:T(8,128)(2,1)S(1)}, u32[]{:S(2)}, u32[]{:S(2)}) collective-permute-start(bf16[64,512]{1,0:T(8,128)(2,1)S(1)} %get-tuple-element.35), channel_id=1, source_target_pairs={{0,12},{1,13},{2,14},{3,15},{4,0},{5,1},{6,2},{7,3},{8,4},{9,5},{1... | collective-permute-start | bytes 196616 | tf_op jit(solution)/shard_map/ppermute | solution.py:53
  44.5 6.9 %collective-permute-start.24 = (bf16[64,512]{1,0:T(8,128)(2,1)S(1)}, bf16[64,512]{1,0:T(8,128)(2,1)S(1)}, u32[]{:S(2)}, u32[]{:S(2)}) collective-permute-start(bf16[64,512]{1,0:T(8,128)(2,1)S(1)} %shard_map.119.refs_0_), channel_id=1, source_target_pairs={{0,4},{1,5},{2,6},{3,7},{4,8},{5,9},{6,10},{7,11},{8,12},{9,13},{1... | collective-permute-start | bytes 196616 | tf_op jit(solution)/shard_map/ppermute | solution.py:53
  45.1 27.1 %collective-permute-start.12 = (bf16[256,768]{1,0:T(8,128)(2,1)S(1)}, bf16[256,768]{1,0:T(8,128)(2,1)S(1)}, u32[]{:S(2)}, u32[]{:S(2)}) collective-permute-start(bf16[256,768]{1,0:T(8,128)(2,1)S(1)} %get-tuple-element.59), channel_id=1, source_target_pairs={{0,15},{1,0},{2,1},{3,2},{4,3},{5,4},{6,5},{7,6},{8,7},{9,8},{10,9... | collective-permute-start | bytes 1179656 | tf_op jit(solution)/shard_map/ppermute | solution.py:53
  45.8 10.0 %collective-permute-start.25 = (bf16[64,512]{1,0:T(8,128)(2,1)S(1)}, bf16[64,512]{1,0:T(8,128)(2,1)S(1)}, u32[]{:S(2)}, u32[]{:S(2)}) collective-permute-start(bf16[64,512]{1,0:T(8,128)(2,1)S(1)} %shard_map.119.refs_0_), channel_id=1, source_target_pairs={{0,8},{1,9},{2,10},{3,11},{4,12},{5,13},{6,14},{7,15},{8,0},{9,1},... | collective-permute-start | bytes 196616 | tf_op jit(solution)/shard_map/ppermute | solution.py:53
  46.4 11.7 %collective-permute-start.26 = (bf16[64,512]{1,0:T(8,128)(2,1)S(1)}, bf16[64,512]{1,0:T(8,128)(2,1)S(1)}, u32[]{:S(2)}, u32[]{:S(2)}) collective-permute-start(bf16[64,512]{1,0:T(8,128)(2,1)S(1)} %shard_map.119.refs_0_), channel_id=1, source_target_pairs={{0,12},{1,13},{2,14},{3,15},{4,0},{5,1},{6,2},{7,3},{8,4},{9,5},{1... | collective-permute-start | bytes 196616 | tf_op jit(solution)/shard_map/ppermute | solution.py:53
  51.4 7.5 %collective-permute-start.5 = (bf16[64,512]{1,0:T(8,128)(2,1)S(1)}, bf16[64,512]{1,0:T(8,128)(2,1)S(1)}, u32[]{:S(2)}, u32[]{:S(2)}) collective-permute-start(bf16[64,512]{1,0:T(8,128)(2,1)S(1)} %shard_map.108.refs_0_), channel_id=1, source_target_pairs={{0,4},{1,5},{2,6},{3,7},{4,8},{5,9},{6,10},{7,11},{8,12},{9,13},{1... | collective-permute-start | bytes 196616 | tf_op jit(solution)/shard_map/ppermute | solution.py:53
  55.8 5.2 %collective-permute-start.6 = (bf16[64,512]{1,0:T(8,128)(2,1)S(1)}, bf16[64,512]{1,0:T(8,128)(2,1)S(1)}, u32[]{:S(2)}, u32[]{:S(2)}) collective-permute-start(bf16[64,512]{1,0:T(8,128)(2,1)S(1)} %shard_map.108.refs_0_), channel_id=1, source_target_pairs={{0,8},{1,9},{2,10},{3,11},{4,12},{5,13},{6,14},{7,15},{8,0},{9,1},... | collective-permute-start | bytes 196616 | tf_op jit(solution)/shard_map/ppermute | solution.py:53
  58.1 15.0 %collective-permute-start.30 = (bf16[256,768]{1,0:T(8,128)(2,1)}, bf16[256,768]{1,0:T(8,128)(2,1)S(1)}, u32[]{:S(2)}, u32[]{:S(2)}) collective-permute-start(bf16[256,768]{1,0:T(8,128)(2,1)} %get-tuple-element.58), channel_id=1, source_target_pairs={{0,1},{1,2},{2,3},{3,4},{4,5},{5,6},{6,7},{7,8},{8,9},{9,10},{10,1... | collective-permute-start | bytes 1179656 | tf_op jit(solution)/shard_map/ppermute | solution.py:53
  58.9 13.2 %collective-permute-start.27 = (bf16[64,2048]{1,0:T(8,128)(2,1)S(1)}, bf16[64,2048]{1,0:T(8,128)(2,1)}, u32[]{:S(2)}, u32[]{:S(2)}) collective-permute-start(bf16[64,2048]{1,0:T(8,128)(2,1)S(1)} %shard_map.120.refs_0_), channel_id=1, source_target_pairs={{0,2},{1,3},{2,0},{3,1},{4,6},{5,7},{6,4},{7,5},{8,10},{9,11},{10,... | collective-permute-start | bytes 786440 | tf_op jit(solution)/shard_map/ppermute | solution.py:53
  61.0 6.5 %collective-permute-start.7 = (bf16[64,512]{1,0:T(8,128)(2,1)S(1)}, bf16[64,512]{1,0:T(8,128)(2,1)S(1)}, u32[]{:S(2)}, u32[]{:S(2)}) collective-permute-start(bf16[64,512]{1,0:T(8,128)(2,1)S(1)} %shard_map.108.refs_0_), channel_id=1, source_target_pairs={{0,12},{1,13},{2,14},{3,15},{4,0},{5,1},{6,2},{7,3},{8,4},{9,5},{1... | collective-permute-start | bytes 196616 | tf_op jit(solution)/shard_map/ppermute | solution.py:53
  67.6 12.7 %collective-permute-start.8 = (bf16[64,2048]{1,0:T(8,128)(2,1)S(1)}, bf16[64,2048]{1,0:T(8,128)(2,1)}, u32[]{:S(2)}, u32[]{:S(2)}) collective-permute-start(bf16[64,2048]{1,0:T(8,128)(2,1)S(1)} %shard_map.109.refs_0_), channel_id=1, source_target_pairs={{0,2},{1,3},{2,0},{3,1},{4,6},{5,7},{6,4},{7,5},{8,10},{9,11},{10,... | collective-permute-start | bytes 786440 | tf_op jit(solution)/shard_map/ppermute | solution.py:53
  70.2 12.2 %collective-permute-start.31 = (bf16[256,768]{1,0:T(8,128)(2,1)}, bf16[256,768]{1,0:T(8,128)(2,1)}, u32[]{:S(2)}, u32[]{:S(2)}) collective-permute-start(bf16[256,768]{1,0:T(8,128)(2,1)} %get-tuple-element.58), channel_id=1, source_target_pairs={{0,15},{1,0},{2,1},{3,2},{4,3},{5,4},{6,5},{7,6},{8,7},{9,8},{10,9... | collective-permute-start | bytes 1179656 | tf_op jit(solution)/shard_map/ppermute | solution.py:53
  72.1 12.3 %collective-permute-start.28 = (bf16[64,2048]{1,0:T(8,128)(2,1)S(1)}, bf16[64,2048]{1,0:T(8,128)(2,1)}, u32[]{:S(2)}, u32[]{:S(2)}) collective-permute-start(bf16[64,2048]{1,0:T(8,128)(2,1)S(1)} %shard_map.120.refs_0_), channel_id=1, source_target_pairs={{0,1},{1,0},{2,3},{3,2},{4,5},{5,4},{6,7},{7,6},{8,9},{9,8},{10,11... | collective-permute-start | bytes 786440 | tf_op jit(solution)/shard_map/ppermute | solution.py:53
  72.1 12.3 %collective-permute-start.29 = (bf16[64,2048]{1,0:T(8,128)(2,1)}, bf16[64,2048]{1,0:T(8,128)(2,1)}, u32[]{:S(2)}, u32[]{:S(2)}) collective-permute-start(bf16[64,2048]{1,0:T(8,128)(2,1)} %collective-permute-done.27.refs_1_), channel_id=1, source_target_pairs={{0,1},{1,0},{2,3},{3,2},{4,5},{5,4},{6,7},{7,6},{8,9},{9,8},{10,11... | collective-permute-start | bytes 786440 | tf_op jit(solution)/shard_map/ppermute | solution.py:53
  73.1 14.6 %collective-permute-start.9 = (bf16[64,2048]{1,0:T(8,128)(2,1)S(1)}, bf16[64,2048]{1,0:T(8,128)(2,1)}, u32[]{:S(2)}, u32[]{:S(2)}) collective-permute-start(bf16[64,2048]{1,0:T(8,128)(2,1)S(1)} %shard_map.109.refs_0_), channel_id=1, source_target_pairs={{0,1},{1,0},{2,3},{3,2},{4,5},{5,4},{6,7},{7,6},{8,9},{9,8},{10,11... | collective-permute-start | bytes 786440 | tf_op jit(solution)/shard_map/ppermute | solution.py:53
  80.2 7.5 %collective-permute-start.10 = (bf16[64,2048]{1,0:T(8,128)(2,1)}, bf16[64,2048]{1,0:T(8,128)(2,1)}, u32[]{:S(2)}, u32[]{:S(2)}) collective-permute-start(bf16[64,2048]{1,0:T(8,128)(2,1)} %collective-permute-done.8.refs_1_), channel_id=1, source_target_pairs={{0,1},{1,0},{2,3},{3,2},{4,5},{5,4},{6,7},{7,6},{8,9},{9,8},{10,11... | collective-permute-start | bytes 786440 | tf_op jit(solution)/shard_map/ppermute | solution.py:53
  80.4 0.8 copy-start.7
  81.3 1.1 copy-start.8
  81.3 3.2 %copy-start.1 = (bf16[2048,768]{1,0:T(8,128)(2,1)S(1)}, bf16[2048,768]{1,0:T(8,128)(2,1)}, u32[]{:S(2)}) copy-start(bf16[2048,768]{1,0:T(8,128)(2,1)} %refs_4_.5) | copy-start | bytes 9437188
  87.1 8.8 %copy-start.5 = (f32[256,768]{1,0:T(8,128)}, f32[256,768]{1,0:T(8,128)S(1)}, u32[]{:S(2)}) copy-start(f32[256,768]{1,0:T(8,128)S(1)} %get-tuple-element.55.refs_3_) | copy-start | bytes 2359300
  87.1 23.2 %copy-start.12 = (s32[512]{0:T(512)S(1)}, s32[512]{0:T(512)}, u32[]{:S(2)}) copy-start(s32[512]{0:T(512)} %param.15) | copy-start | bytes 6148
  87.1 23.3 %copy-start.13 = (s32[512]{0:T(512)S(1)}, s32[512]{0:T(512)}, u32[]{:S(2)}) copy-start(s32[512]{0:T(512)} %param.16) | copy-start | bytes 6148
  87.2 3.5 %collective-permute-start.32 = (bf16[128,256]{1,0:T(8,128)(2,1)S(1)}, bf16[128,256]{1,0:T(8,128)(2,1)S(1)}, u32[]{:S(2)}, u32[]{:S(2)}) collective-permute-start(bf16[128,256]{1,0:T(8,128)(2,1)S(1)} %get-tuple-element.50), channel_id=1, source_target_pairs={{0,1},{1,0},{2,3},{3,2},{4,5},{5,4},{6,7},{7,6},{8,9},{9,8},{10,11... | collective-permute-start | bytes 196616 | tf_op jit(solution)/shard_map/ppermute | solution.py:53
  90.4 3.0 %collective-permute-start.13 = (bf16[128,256]{1,0:T(8,128)(2,1)S(1)}, bf16[128,256]{1,0:T(8,128)(2,1)S(1)}, u32[]{:S(2)}, u32[]{:S(2)}) collective-permute-start(bf16[128,256]{1,0:T(8,128)(2,1)S(1)} %get-tuple-element.37), channel_id=1, source_target_pairs={{0,1},{1,0},{2,3},{3,2},{4,5},{5,4},{6,7},{7,6},{8,9},{9,8},{10,11... | collective-permute-start | bytes 196616 | tf_op jit(solution)/shard_map/ppermute | solution.py:53
  90.7 5.2 %collective-permute-start.33 = (bf16[128,256]{1,0:T(8,128)(2,1)S(1)}, bf16[128,256]{1,0:T(8,128)(2,1)S(1)}, u32[]{:S(2)}, u32[]{:S(2)}) collective-permute-start(bf16[128,256]{1,0:T(8,128)(2,1)S(1)} %get-tuple-element.52), channel_id=1, source_target_pairs={{0,2},{1,3},{2,0},{3,1},{4,6},{5,7},{6,4},{7,5},{8,10},{9,11},{10,... | collective-permute-start | bytes 196616 | tf_op jit(solution)/shard_map/ppermute | solution.py:53
  93.4 6.4 %collective-permute-start.14 = (bf16[128,256]{1,0:T(8,128)(2,1)S(1)}, bf16[128,256]{1,0:T(8,128)(2,1)S(1)}, u32[]{:S(2)}, u32[]{:S(2)}) collective-permute-start(bf16[128,256]{1,0:T(8,128)(2,1)S(1)} %get-tuple-element.39), channel_id=1, source_target_pairs={{0,2},{1,3},{2,0},{3,1},{4,6},{5,7},{6,4},{7,5},{8,10},{9,11},{10,... | collective-permute-start | bytes 196616 | tf_op jit(solution)/shard_map/ppermute | solution.py:53
  95.9 6.9 %collective-permute-start.34 = (bf16[128,256]{1,0:T(8,128)(2,1)S(1)}, bf16[128,256]{1,0:T(8,128)(2,1)S(1)}, u32[]{:S(2)}, u32[]{:S(2)}) collective-permute-start(bf16[128,256]{1,0:T(8,128)(2,1)S(1)} %get-tuple-element.54), channel_id=1, source_target_pairs={{0,4},{1,5},{2,6},{3,7},{4,8},{5,9},{6,10},{7,11},{8,12},{9,13},{1... | collective-permute-start | bytes 196616 | tf_op jit(solution)/shard_map/ppermute | solution.py:53
  96.8 9.8 %collective-permute-start.35 = (bf16[128,256]{1,0:T(8,128)(2,1)S(1)}, bf16[128,256]{1,0:T(8,128)(2,1)S(1)}, u32[]{:S(2)}, u32[]{:S(2)}) collective-permute-start(bf16[128,256]{1,0:T(8,128)(2,1)S(1)} %get-tuple-element.54), channel_id=1, source_target_pairs={{0,8},{1,9},{2,10},{3,11},{4,12},{5,13},{6,14},{7,15},{8,0},{9,1},... | collective-permute-start | bytes 196616 | tf_op jit(solution)/shard_map/ppermute | solution.py:53
  98.8 7.9 %collective-permute-start.36 = (bf16[128,256]{1,0:T(8,128)(2,1)S(1)}, bf16[128,256]{1,0:T(8,128)(2,1)S(1)}, u32[]{:S(2)}, u32[]{:S(2)}) collective-permute-start(bf16[128,256]{1,0:T(8,128)(2,1)S(1)} %get-tuple-element.54), channel_id=1, source_target_pairs={{0,12},{1,13},{2,14},{3,15},{4,0},{5,1},{6,2},{7,3},{8,4},{9,5},{1... | collective-permute-start | bytes 196616 | tf_op jit(solution)/shard_map/ppermute | solution.py:53
  99.8 6.9 %collective-permute-start.15 = (bf16[128,256]{1,0:T(8,128)(2,1)S(1)}, bf16[128,256]{1,0:T(8,128)(2,1)S(1)}, u32[]{:S(2)}, u32[]{:S(2)}) collective-permute-start(bf16[128,256]{1,0:T(8,128)(2,1)S(1)} %get-tuple-element.41), channel_id=1, source_target_pairs={{0,4},{1,5},{2,6},{3,7},{4,8},{5,9},{6,10},{7,11},{8,12},{9,13},{1... | collective-permute-start | bytes 196616 | tf_op jit(solution)/shard_map/ppermute | solution.py:53
  100.9 9.3 %collective-permute-start.16 = (bf16[128,256]{1,0:T(8,128)(2,1)S(1)}, bf16[128,256]{1,0:T(8,128)(2,1)S(1)}, u32[]{:S(2)}, u32[]{:S(2)}) collective-permute-start(bf16[128,256]{1,0:T(8,128)(2,1)S(1)} %get-tuple-element.41), channel_id=1, source_target_pairs={{0,8},{1,9},{2,10},{3,11},{4,12},{5,13},{6,14},{7,15},{8,0},{9,1},... | collective-permute-start | bytes 196616 | tf_op jit(solution)/shard_map/ppermute | solution.py:53
  102.8 7.4 %collective-permute-start.17 = (bf16[128,256]{1,0:T(8,128)(2,1)S(1)}, bf16[128,256]{1,0:T(8,128)(2,1)S(1)}, u32[]{:S(2)}, u32[]{:S(2)}) collective-permute-start(bf16[128,256]{1,0:T(8,128)(2,1)S(1)} %get-tuple-element.41), channel_id=1, source_target_pairs={{0,12},{1,13},{2,14},{3,15},{4,0},{5,1},{6,2},{7,3},{8,4},{9,5},{1... | collective-permute-start | bytes 196616 | tf_op jit(solution)/shard_map/ppermute | solution.py:53
  106.7 4.0 %collective-permute-start.37 = (bf16[128,256]{1,0:T(8,128)(2,1)S(1)}, bf16[128,256]{1,0:T(8,128)(2,1)S(1)}, u32[]{:S(2)}, u32[]{:S(2)}) collective-permute-start(bf16[128,256]{1,0:T(8,128)(2,1)S(1)} %shard_map.125.refs_0_), channel_id=1, source_target_pairs={{0,1},{1,0},{2,3},{3,2},{4,5},{5,4},{6,7},{7,6},{8,9},{9,8},{10,11... | collective-permute-start | bytes 196616 | tf_op jit(solution)/shard_map/ppermute | solution.py:53
  110.2 2.8 %collective-permute-start.18 = (bf16[128,256]{1,0:T(8,128)(2,1)S(1)}, bf16[128,256]{1,0:T(8,128)(2,1)S(1)}, u32[]{:S(2)}, u32[]{:S(2)}) collective-permute-start(bf16[128,256]{1,0:T(8,128)(2,1)S(1)} %shard_map.114.refs_0_), channel_id=1, source_target_pairs={{0,1},{1,0},{2,3},{3,2},{4,5},{5,4},{6,7},{7,6},{8,9},{9,8},{10,11... | collective-permute-start | bytes 196616 | tf_op jit(solution)/shard_map/ppermute | solution.py:53
  110.6 1.1 copy-start.6

commit v2 on v1

v2 whole, which is shorter than its diff:
```python
import functools
import math

import jax
import jax.numpy as jnp
import ml_dtypes
import numpy as np
from jax import lax
from jax.experimental import pallas as pl
from jax.experimental.pallas import tpu as pltpu
from jax.sharding import PartitionSpec as P

GY = 8
GZ = 16
NBLK = 32
REACH = 4
GROUP_BLOCKS = 8
COEFFS = (
    -5369.0 / 1800.0,
    12.0 / 7.0,
    -15.0 / 56.0,
    10.0 / 189.0,
    -1.0 / 112.0,
    2.0 / 1925.0,
    -1.0 / 16632.0,
)
KINETIC = 0.125
STEP_SIZE = 0.3
VMEM_BYTES = 40 * 1024 * 1024
BF16 = jnp.bfloat16
F32 = jnp.float32
NT = (((1,), (1,)), ((), ()))


def levels_of(count):
    chips = count // 2
    across = 2 ** (int(math.log2(chips)) // 3)
    return (2, 1), (across, 2), (chips // across, 2 * across)


def position(level):
    size, stride = level
    return lax.rem(lax.div(lax.axis_index("band"), jnp.int32(stride)), jnp.int32(size))


def shifted(array, count, level, step):
    size, stride = level
    pairs = []
    for device in range(count):
        place = device // stride % size
        pairs.append((device, device + ((place + step) % size - place) * stride))
    return lax.ppermute(array, "band", pairs)


def plane_matrix():
    plane = GY * GZ
    matrix = 3.0 * COEFFS[0] * np.eye(plane)
    cells = np.arange(plane)
    y, z = cells // GZ, cells % GZ
    for offset in range(1, 7):
        for sign in (1, -1):
            np.add.at(matrix, ((y + sign * offset) % GY * GZ + z, cells), COEFFS[offset])
            np.add.at(matrix, (y * GZ + (z + sign * offset) % GZ, cells), COEFFS[offset])
    matrix = KINETIC * matrix
    high = matrix.astype(ml_dtypes.bfloat16)
    low = (matrix - high.astype(np.float64)).astype(ml_dtypes.bfloat16)
    return np.stack([high, low])


def whole():
    return pl.BlockSpec(memory_space=pltpu.VMEM)


def params():
    return pltpu.CompilerParams(vmem_limit_bytes=VMEM_BYTES)


def cost(flops, *arrays):
    moved = sum(math.prod(a.shape) * jnp.dtype(a.dtype).itemsize for a in arrays)
    return pl.CostEstimate(flops=int(flops), bytes_accessed=int(moved), transcendentals=0)


def local_call(body, outs, args, flops=0, scratch=()):
    return pl.pallas_call(
        body,
        out_shape=outs,
        in_specs=[whole() for _ in args],
        out_specs=jax.tree.map(lambda _: whole(), outs),
        scratch_shapes=scratch,
        compiler_params=params(),
        cost_estimate=cost(flops, *args, *jax.tree.leaves(outs)),
    )(*args)


def struct(shape, dtype):
    return jax.ShapeDtypeStruct(shape, dtype)


def partial_body(core, bands, parts, r_ref, p_ref, *outs):
    c = position(core)
    for (other, first, rows), out_ref in zip(parts, outs):
        row = pl.multiple_of((1 - c if other else c) * (bands // 2) + first, 16)
        out_ref[...] = lax.dot_general(
            r_ref[pl.ds(row, rows), :], p_ref[...], NT, preferred_element_type=F32
        ).astype(out_ref.dtype)


def partial_intersections(response, projectors, core, parts):
    bands, cells = response.shape
    count = projectors.shape[0]
    tile = min(512, count)
    outs = [struct((rows, count), BF16 if other else F32) for other, _, rows in parts]
    done = sum(rows for _, _, rows in parts)
    return pl.pallas_call(
        functools.partial(partial_body, core, bands, parts),
        grid=(count // tile,),
        out_shape=outs,
        in_specs=[
            pl.BlockSpec((bands, cells), lambda i: (0, 0)),
            pl.BlockSpec((tile, cells), lambda i: (i, 0)),
        ],
        out_specs=[pl.BlockSpec((rows, tile), lambda i: (0, i)) for _, _, rows in parts],
        compiler_params=params(),
        cost_estimate=cost(2 * done * cells * count, projectors, *outs),
    )(response, projectors)


def split_body(received, level, along, *refs):
    keep_ref, taken, (own_ref, *sends) = refs[0], refs[1 : 1 + received], refs[1 + received :]
    size, _ = level
    me = position(level)
    width = own_ref.shape[along]
    for step, out in enumerate((own_ref, *sends)):
        at = pl.multiple_of(lax.rem(me + step, jnp.int32(size)) * width, width)
        part = (pl.ds(at, width), slice(None)) if along == 0 else (slice(None), pl.ds(at, width))
        total = keep_ref[part]
        for ref in taken:
            total = total + ref[part].astype(F32)
        out[...] = total.astype(out.dtype)


def split(keep, taken, level, along):
    size, _ = level
    shape = list(keep.shape)
    shape[along] //= size
    outs = [struct(shape, F32)] + [struct(shape, BF16)] * (size - 1)
    return local_call(
        functools.partial(split_body, len(taken), level, along), outs, [keep, *taken]
    )


def finish_body(scale, keep_ref, *refs):
    *taken, out_ref = refs
    total = keep_ref[...]
    for ref in taken:
        total = total + ref[...].astype(F32)
    out_ref[...] = (total * scale).astype(out_ref.dtype)


def finish(keep, taken, scale):
    return local_call(
        functools.partial(finish_body, scale), struct(keep.shape, BF16), [keep, *taken]
    )


def place_body(level, along, *refs):
    *parts, out_ref = refs
    size, _ = level
    me = position(level)
    width = parts[0].shape[along]
    for step, ref in enumerate(parts):
        at = pl.multiple_of(lax.rem(me - step + size, jnp.int32(size)) * width, width)
        if along == 0:
            out_ref[pl.ds(at, width), :] = ref[...]
        else:
            out_ref[:, pl.ds(at, width)] = ref[...]


def place(parts, level, along):
    shape = list(parts[0].shape)
    shape[along] *= level[0]
    return local_call(functools.partial(place_body, level, along), struct(shape, BF16), parts)


def local_body(depth, r_ref, l_ref, h_ref, o_ref, m_ref, pot_ref, v_ref, e_ref, out_ref):
    plane = GY * GZ
    reach = 6

    def plane_at(j):
        if j < 0:
            ref, k = l_ref, j + reach
        elif j < depth:
            ref, k = r_ref, j
        else:
            ref, k = h_ref, j - depth
        return ref[:, k * plane : (k + 1) * plane]

    for j in range(depth):
        cols = slice(j * plane, (j + 1) * plane)
        low = plane_at(j)
        centre = low.astype(F32)
        total = jnp.dot(low, m_ref[0], preferred_element_type=F32)
        total = total + jnp.dot(low, m_ref[1], preferred_element_type=F32)
        for offset in range(1, 7):
            pair = plane_at(j + offset).astype(F32) + plane_at(j - offset).astype(F32)
            total = total + (KINETIC * COEFFS[offset]) * pair
        total = total + (e_ref[...] - pot_ref[:, cols]) * centre
        out_ref[:, cols] = total - v_ref[:, cols] * o_ref[:, cols].astype(F32)


def local_part(response, low, high, orbitals, matrix, potential, perturbing, energies):
    bands, cells = response.shape
    depth = cells // (GY * GZ)
    tile = 128
    out = struct((bands, cells), F32)
    here = pl.BlockSpec((tile, cells), lambda i: (i, 0))
    side = pl.BlockSpec((tile, low.shape[1]), lambda i: (i, 0))
    line = pl.BlockSpec((1, cells), lambda i: (0, 0))
    return pl.pallas_call(
        functools.partial(local_body, depth),
        grid=(bands // tile,),
        out_shape=out,
        in_specs=[
            here,
            side,
            side,
            here,
            pl.BlockSpec(matrix.shape, lambda i: (0, 0, 0)),
            line,
            line,
            pl.BlockSpec((tile, 1), lambda i: (i, 0)),
        ],
        out_specs=here,
        compiler_params=params(),
        cost_estimate=cost(2 * bands * cells * 300, low, high, low, low, out),
    )(response, low, high, orbitals, matrix, potential, perturbing, energies)


def first_orbital(group, group_rows, width, bands, blk):
    return max(0, min(group * group_rows - REACH * blk, bands - width))


def apply_body(core, across, rows_x, group_rows, width, blk, *refs):
    size = across[0]
    blocks = refs[: 2 * (size + 1)]
    p_ref, base_ref, o_ref, u_ref, send_ref, keep_ref, c_ref, s_ref = refs[2 * (size + 1) :]
    bands, cells = u_ref.shape
    c, x = position(core), position(across)
    half = bands // 2
    share = rows_x // size
    for k, ref in enumerate(blocks):
        side, step = divmod(k, size + 1)
        at = (c if side == 0 else 1 - c) * half
        if step < size:
            at = at + lax.rem(x - step + size, jnp.int32(size)) * share
        else:
            at = at + rows_x
        c_ref[pl.ds(pl.multiple_of(at, 16), ref.shape[0]), :] = ref[...]
    tile = 256 if cells % 256 == 0 else 128
    for t in range(cells // tile):
        cols = slice(t * tile, (t + 1) * tile)
        u_ref[:, cols] = base_ref[:, cols] + jnp.dot(
            c_ref[...], p_ref[:, cols], preferred_element_type=F32
        )
    for g in range(bands // group_rows):
        start = first_orbital(g, group_rows, width, bands, blk)
        mine = slice(g * group_rows, (g + 1) * group_rows)
        s_ref[mine, :] = lax.dot_general(
            u_ref[mine, :].astype(BF16),
            o_ref[start : start + width, :],
            NT,
            preferred_element_type=F32,
        )
    send_ref[...] = s_ref[pl.ds(pl.multiple_of((1 - c) * half, half), half), :].astype(BF16)
    keep_ref[...] = s_ref[pl.ds(pl.multiple_of(c * half, half), half), :]


def sum_body(keep_ref, *refs):
    *taken, total_ref, low_ref = refs
    total = keep_ref[...]
    for ref in taken:
        total = total + ref[...].astype(F32)
    total_ref[...] = total
    low_ref[...] = total.astype(BF16)


def add_up(keep, taken):
    outs = [struct(keep.shape, F32), struct(keep.shape, BF16)]
    return local_call(sum_body, outs, [keep, *taken])


def project_body(core, across, group_rows, width, blk, *refs):
    size = across[0]
    blocks = refs[: 2 * size]
    o_ref, u_ref, r_ref, first_ref, many_ref, updated_ref, residual_ref, w_ref = refs[2 * size :]
    bands = o_ref.shape[0]
    half = bands // 2
    c, x = position(core), position(across)
    for k, ref in enumerate(blocks):
        side, step = divmod(k, size)
        at = (c if side == 0 else 1 - c) * half
        at = at + lax.rem(x - step + size, jnp.int32(size)) * ref.shape[0]
        w_ref[pl.ds(pl.multiple_of(at, 16), ref.shape[0]), :] = ref[...]
    for g in range(bands // group_rows):
        start = first_orbital(g, group_rows, width, bands, blk)
        mine = slice(g * group_rows, (g + 1) * group_rows)
        block = (lax.broadcasted_iota(jnp.int32, (group_rows, width), 1) + start) // blk
        lowest = first_ref[mine, :]
        inside = (block >= lowest) & (block < lowest + many_ref[mine, :])
        weights = jnp.where(inside, w_ref[mine, :].astype(F32), 0.0).astype(BF16)
        residual = u_ref[mine, :] - jnp.dot(
            weights, o_ref[start : start + width, :], preferred_element_type=F32
        )
        residual_ref[mine, :] = residual.astype(BF16)
        updated_ref[mine, :] = (r_ref[mine, :].astype(F32) + STEP_SIZE * residual).astype(BF16)


def shards(
    count, response, orbitals, projectors, potential, perturbing, energies, window_start, block_count
):
    bands, local_cells = response.shape
    cells = local_cells * count
    projections = projectors.shape[0]
    halo = 6 * GY * GZ
    core, across, along = levels_of(count)
    ring = (count, 1)
    ace_scale = 1.0 / math.sqrt(cells * projections)
    window_scale = 1.0 / math.sqrt(cells * bands)
    blk = bands // NBLK
    group_rows = GROUP_BLOCKS * blk
    width = (GROUP_BLOCKS + 2 * REACH) * blk
    half = bands // 2
    rows_x = half // 2
    rows_z = half - rows_x
    matrix = jnp.asarray(plane_matrix())
    potential, perturbing = potential[None, :], perturbing[None, :]
    energies, window_start, block_count = (
        a[:, None] for a in (energies, window_start, block_count)
    )

    def to(array, level):
        return [shifted(array, count, level, k) for k in range(1, level[0])]

    def parts_to(parts, level):
        return [shifted(part, count, level, k + 1) for k, part in enumerate(parts)]

    low = shifted(response[:, local_cells - halo :], count, ring, 1)
    high = shifted(response[:, :halo], count, ring, -1)

    (sent_z,) = partial_intersections(response, projectors, core, [(True, rows_x, rows_z)])
    sent_z = shifted(sent_z, count, core, 1)
    (sent_x,) = partial_intersections(response, projectors, core, [(True, 0, rows_x)])
    sent_x = shifted(sent_x, count, core, 1)
    keep_z, keep_x = partial_intersections(
        response, projectors, core, [(False, rows_x, rows_z), (False, 0, rows_x)]
    )
    keep_z, *parts = split(keep_z, [sent_z], along, 1)
    taken_z = parts_to(parts, along)
    keep_x, *parts = split(keep_x, [sent_x], across, 0)
    taken_x = parts_to(parts, across)
    keep_x, *parts = split(keep_x, taken_x, along, 1)
    taken_x = parts_to(parts, along)
    keep_z, *parts = split(keep_z, taken_z, across, 0)
    taken_z = parts_to(parts, across)
    share_z = finish(keep_z, taken_z, ace_scale)
    share_x = finish(keep_x, taken_x, ace_scale)

    block_z = place([share_z, *to(share_z, across)], across, 0)
    block_x = place([share_x, *to(share_x, along)], along, 1)
    base = local_part(
        response, low, high, orbitals, matrix, potential, perturbing, energies
    )
    blocks_x = [block_x, *to(block_x, across)]
    block_z = place([block_z, *to(block_z, along)], along, 1)
    blocks = [*blocks_x, block_z]
    blocks += [shifted(block, count, core, 1) for block in blocks]

    unprojected, send, keep = local_call(
        functools.partial(apply_body, core, across, rows_x, group_rows, width, blk),
        [
            struct((bands, local_cells), F32),
            struct((half, width), BF16),
            struct((half, width), F32),
        ],
        [*blocks, projectors, base, orbitals],
        flops=2 * bands * local_cells * (projections + width),
        scratch=[pltpu.VMEM((bands, projections), BF16), pltpu.VMEM((bands, width), F32)],
    )
    keep, *parts = split(keep, to(send, core), across, 0)
    total, low = add_up(keep, parts_to(parts, across))
    weights = finish(total, to(low, along), window_scale)
    weights = [weights, *to(weights, across)]
    weights += [shifted(block, count, core, 1) for block in weights]
    out = struct((bands, local_cells), BF16)
    return local_call(
        functools.partial(project_body, core, across, group_rows, width, blk),
        (out, out),
        [*weights, orbitals, unprojected, response, window_start, block_count],
        flops=2 * bands * width * local_cells,
        scratch=[pltpu.VMEM((bands, width), BF16)],
    )


def solution(mesh):
    in_specs = (
        P("pert", "band"),
        P(None, "band"),
        P(None, "band"),
        P("band"),
        P(("pert", "band")),
        P(),
        P(),
        P(),
    )
    out_specs = (P("pert", "band"), P("pert", "band"))
    body = functools.partial(shards, mesh.shape["band"])
    return jax.shard_map(body, mesh=mesh, in_specs=in_specs, out_specs=out_specs, check_vma=False)
```

time: 115 us -> 111 us (0.965)
  starting transfers between devices: 45.4 us -> 30.3 us
  waiting for transfers between devices: 43.4 us -> 56.9 us
  Pallas kernels: 18 us -> 16.2 us
    ppermute x38 -> x31, starting transfers between devices: 45.4 us -> 30.3 us  [shifted(): return lax.ppermute(array, 'band', pairs)]
    ppermute x38 -> x31, waiting for transfers between devices: 43.4 us -> 56.9 us  [shifted(): return lax.ppermute(array, 'band', pairs)]
    pallas_call x8 -> x4, Pallas kernels: 12.1 us -> 9.67 us  [the longest x3 6.01 us: partial_intersections(): pl.pallas_call(functools.partial(partial_body, core, bands, parts), grid=...]
    unnamed x28 -> x26, local copies, waits for them, and re-layouts: 5.04 us -> 5.64 us
    pallas_call x16 -> x14, Pallas kernels: 5.91 us -> 6.5 us  [local_call(): pl.pallas_call(body, out_shape=outs, in_specs=[whole() for _ in args], ou...]
  transfers between devices with their start and end apart: 38 -> 31, of which waited for: 15 -> 16; matrix products, arithmetic and copies ran while one was open for 1% -> 0% of each run, Pallas kernels for 13% -> 8%
where the time goes in v2:
time: 111 us; the launch traced here: 110 us
  waiting for transfers between devices  56.9 us (51%)
  starting transfers between devices  30.3 us (27%)
  Pallas kernels  16.2 us (15%)
  local copies, waits for them, and re-layouts  6.09 us (5%)
    ppermute x31, waiting for transfers between devices, shifted(): return lax.ppermute(array, 'band', pairs)  56.9 us
    ppermute x31, starting transfers between devices, shifted(): return lax.ppermute(array, 'band', pairs)  30.3 us
    pallas_call x14, Pallas kernels, local_call(): pl.pallas_call(body, out_shape=outs, in_specs=[whole() for _ in args], ou...  6.5 us
    pallas_call x3, Pallas kernels, partial_intersections(): pl.pallas_call(functools.partial(partial_body, core, bands, parts), grid=...  6.01 us
    unnamed x26, local copies, waits for them, and re-layouts  5.64 us
    pallas_call x1, Pallas kernels, local_part(): pl.pallas_call(functools.partial(local_body, depth), grid=(bands // tile,...  3.66 us
  transfers between devices with their start and end apart: 31, of which 16 were waited for; matrix products, arithmetic and copies ran while one was open for 0% of the time, Pallas kernels for 8%

profile of v2, /device:TPU:0, one launch (start us, length us, event | category | flops | bytes accessed | tf_op | source)
XLA Modules:
  0.0 110.4 jit_solution(14008328760445074849)
XLA Ops:
  0.6 0.0 copy-start
  0.6 1.9 %copy-done = bf16[2048,768]{1,0:T(8,128)(2,1)S(1)} copy-done((bf16[2048,768]{1,0:T(8,128)(2,1)S(1)}, bf16[2048,768]{1,0:T(8,128)(2,1)}, u32[]{:S(2)}) %copy-start) | copy-done | bytes 3145752
  2.5 1.1 %copy-done.2 = bf16[512,768]{1,0:T(8,128)(2,1)S(1)} copy-done((bf16[512,768]{1,0:T(8,128)(2,1)S(1)}, bf16[512,768]{1,0:T(8,128)(2,1)}, u32[]{:S(2)}) %copy-start.2) | copy-done | bytes 786456
  3.7 1.7 %shard_map.110 = bf16[128,2048]{1,0:T(8,128)(2,1)S(1)} custom-call(bf16[512,768]{1,0:T(8,128)(2,1)S(1)} %copy-done.2, bf16[2048,768]{1,0:T(8,128)(2,1)S(1)} %copy-done), custom_call_target="tpu_custom_call" | custom-call | flops 402653184 | bytes 3670016 | tf_op jit(solution)/shard_map/pallas_call | solution.py:114
  5.3 0.5 collective-permute-start.9
  5.8 1.7 %shard_map.105 = bf16[128,2048]{1,0:T(8,128)(2,1)S(1)} custom-call(bf16[512,768]{1,0:T(8,128)(2,1)S(1)} %copy-done.2, bf16[2048,768]{1,0:T(8,128)(2,1)S(1)} %copy-done), custom_call_target="tpu_custom_call" | custom-call | flops 402653184 | bytes 3670016 | tf_op jit(solution)/shard_map/pallas_call | solution.py:114
  7.5 0.2 collective-permute-start
  7.6 2.7 %shard_map.104 = (f32[128,2048]{1,0:T(8,128)S(1)}, f32[128,2048]{1,0:T(8,128)S(1)}) custom-call(bf16[512,768]{1,0:T(8,128)(2,1)S(1)} %copy-done.2, bf16[2048,768]{1,0:T(8,128)(2,1)S(1)} %copy-done), custom_call_target="tpu_custom_call" | custom-call | flops 805306368 | bytes 5242880 | tf_op jit(solution)/shard_map/pallas_call | solution.py:114
  10.3 0.0 collective-permute-done.9.refs_1_
  10.3 0.1 shard_map.111
  10.5 0.0 copy-start.3
  10.5 3.0 %collective-permute-start.10 = (bf16[128,512]{1,0:T(8,128)(2,1)S(1)}, bf16[128,512]{1,0:T(8,128)(2,1)S(1)}, u32[]{:S(2)}, u32[]{:S(2)}) collective-permute-start(bf16[128,512]{1,0:T(8,128)(2,1)S(1)} %get-tuple-element.32), channel_id=1, source_target_pairs={{0,4},{1,5},{2,6},{3,7},{4,8},{5,9},{6,10},{7,11},{8,12},{9,13},{1... | collective-permute-start | bytes 393224 | tf_op jit(solution)/shard_map/ppermute | solution.py:52
  13.5 2.6 %collective-permute-start.11 = (bf16[128,512]{1,0:T(8,128)(2,1)S(1)}, bf16[128,512]{1,0:T(8,128)(2,1)S(1)}, u32[]{:S(2)}, u32[]{:S(2)}) collective-permute-start(bf16[128,512]{1,0:T(8,128)(2,1)S(1)} %get-tuple-element.33), channel_id=1, source_target_pairs={{0,8},{1,9},{2,10},{3,11},{4,12},{5,13},{6,14},{7,15},{8,0},{9,1},... | collective-permute-start | bytes 393224 | tf_op jit(solution)/shard_map/ppermute | solution.py:52
  16.1 1.4 %collective-permute-start.12 = (bf16[128,512]{1,0:T(8,128)(2,1)S(1)}, bf16[128,512]{1,0:T(8,128)(2,1)S(1)}, u32[]{:S(2)}, u32[]{:S(2)}) collective-permute-start(bf16[128,512]{1,0:T(8,128)(2,1)S(1)} %get-tuple-element.34), channel_id=1, source_target_pairs={{0,12},{1,13},{2,14},{3,15},{4,0},{5,1},{6,2},{7,3},{8,4},{9,5},{1... | collective-permute-start | bytes 393224 | tf_op jit(solution)/shard_map/ppermute | solution.py:52
  17.5 0.1 shard_map.106
  17.6 1.5 %collective-permute-start.1 = (bf16[64,2048]{1,0:T(8,128)(2,1)S(1)}, bf16[64,2048]{1,0:T(8,128)(2,1)S(1)}, u32[]{:S(2)}, u32[]{:S(2)}) collective-permute-start(bf16[64,2048]{1,0:T(8,128)(2,1)S(1)} %get-tuple-element.25), channel_id=1, source_target_pairs={{0,2},{1,3},{2,0},{3,1},{4,6},{5,7},{6,4},{7,5},{8,10},{9,11},{10,... | collective-permute-start | bytes 786440 | tf_op jit(solution)/shard_map/ppermute | solution.py:52
  19.1 0.8 collective-permute-done.10.refs_1_
  20.0 5.0 %collective-permute-done.11.refs_2_ = bf16[128,512]{1,0:T(8,128)(2,1)S(1)} collective-permute-done((bf16[128,512]{1,0:T(8,128)(2,1)S(1)}, bf16[128,512]{1,0:T(8,128)(2,1)S(1)}, u32[]{:S(2)}, u32[]{:S(2)}) %collective-permute-start.11) | collective-permute-done | bytes 131104 | tf_op jit(solution)/shard_map/ppermute | solution.py:52
  25.0 0.1 shard_map.112
  25.1 1.5 %collective-permute-start.13 = (bf16[64,512]{1,0:T(8,128)(2,1)S(1)}, bf16[64,512]{1,0:T(8,128)(2,1)S(1)}, u32[]{:S(2)}, u32[]{:S(2)}) collective-permute-start(bf16[64,512]{1,0:T(8,128)(2,1)S(1)} %get-tuple-element.36), channel_id=1, source_target_pairs={{0,2},{1,3},{2,0},{3,1},{4,6},{5,7},{6,4},{7,5},{8,10},{9,11},{10,... | collective-permute-start | bytes 196616 | tf_op jit(solution)/shard_map/ppermute | solution.py:52
  26.6 2.8 %collective-permute-done.13.refs_0_ = bf16[64,512]{1,0:T(8,128)(2,1)S(1)} collective-permute-done((bf16[64,512]{1,0:T(8,128)(2,1)S(1)}, bf16[64,512]{1,0:T(8,128)(2,1)S(1)}, u32[]{:S(2)}, u32[]{:S(2)}) %collective-permute-start.13) | collective-permute-done | bytes 65568 | tf_op jit(solution)/shard_map/ppermute | solution.py:52
  29.4 0.0 copy-start.10
  29.4 1.5 %collective-permute-start.14 = (bf16[64,512]{1,0:T(8,128)(2,1)S(1)}, bf16[64,512]{1,0:T(8,128)(2,1)S(1)}, u32[]{:S(2)}, u32[]{:S(2)}) collective-permute-start(bf16[64,512]{1,0:T(8,128)(2,1)S(1)} %shard_map.113.refs_0_), channel_id=1, source_target_pairs={{0,2},{1,3},{2,0},{3,1},{4,6},{5,7},{6,4},{7,5},{8,10},{9,11},{10,... | collective-permute-start | bytes 196616 | tf_op jit(solution)/shard_map/ppermute | solution.py:52
  31.0 4.4 %collective-permute-start.22 = (bf16[512,768]{1,0:T(8,128)(2,1)S(1)}, bf16[512,768]{1,0:T(8,128)(2,1)}, u32[]{:S(2)}, u32[]{:S(2)}) collective-permute-start(bf16[512,768]{1,0:T(8,128)(2,1)S(1)} %copy-done.3), channel_id=1, source_target_pairs={{0,15},{1,0},{2,1},{3,2},{4,3},{5,4},{6,5},{7,6},{8,7},{9,8},{10,9... | collective-permute-start | bytes 2359304 | tf_op jit(solution)/shard_map/ppermute | solution.py:52
  35.4 0.0 copy-start.7
  35.4 0.1 shard_map.107
  35.5 1.5 %collective-permute-start.2 = (bf16[64,512]{1,0:T(8,128)(2,1)S(1)}, bf16[64,512]{1,0:T(8,128)(2,1)S(1)}, u32[]{:S(2)}, u32[]{:S(2)}) collective-permute-start(bf16[64,512]{1,0:T(8,128)(2,1)S(1)} %get-tuple-element.27), channel_id=1, source_target_pairs={{0,4},{1,5},{2,6},{3,7},{4,8},{5,9},{6,10},{7,11},{8,12},{9,13},{1... | collective-permute-start | bytes 196616 | tf_op jit(solution)/shard_map/ppermute | solution.py:52
  37.0 1.7 %collective-permute-start.3 = (bf16[64,512]{1,0:T(8,128)(2,1)S(1)}, bf16[64,512]{1,0:T(8,128)(2,1)S(1)}, u32[]{:S(2)}, u32[]{:S(2)}) collective-permute-start(bf16[64,512]{1,0:T(8,128)(2,1)S(1)} %get-tuple-element.28), channel_id=1, source_target_pairs={{0,8},{1,9},{2,10},{3,11},{4,12},{5,13},{6,14},{7,15},{8,0},{9,1},... | collective-permute-start | bytes 196616 | tf_op jit(solution)/shard_map/ppermute | solution.py:52
  38.7 0.8 collective-permute-start.4
  39.5 15.0 %collective-permute-done.2.refs_0_ = bf16[64,512]{1,0:T(8,128)(2,1)S(1)} collective-permute-done((bf16[64,512]{1,0:T(8,128)(2,1)S(1)}, bf16[64,512]{1,0:T(8,128)(2,1)S(1)}, u32[]{:S(2)}, u32[]{:S(2)}) %collective-permute-start.2) | collective-permute-done | bytes 65568 | tf_op jit(solution)/shard_map/ppermute | solution.py:52
  54.4 2.2 %collective-permute-done.3.refs_1_ = bf16[64,512]{1,0:T(8,128)(2,1)S(1)} collective-permute-done((bf16[64,512]{1,0:T(8,128)(2,1)S(1)}, bf16[64,512]{1,0:T(8,128)(2,1)S(1)}, u32[]{:S(2)}, u32[]{:S(2)}) %collective-permute-start.3) | collective-permute-done | bytes 65568 | tf_op jit(solution)/shard_map/ppermute | solution.py:52
  56.7 1.7 %collective-permute-start.17 = (bf16[128,512]{1,0:T(8,128)(2,1)S(1)}, bf16[128,512]{1,0:T(8,128)(2,1)S(1)}, u32[]{:S(2)}, u32[]{:S(2)}) collective-permute-start(bf16[128,512]{1,0:T(8,128)(2,1)S(1)} %shard_map.114.refs_0_), channel_id=1, source_target_pairs={{0,12},{1,13},{2,14},{3,15},{4,0},{5,1},{6,2},{7,3},{8,4},{9,5},{1... | collective-permute-start | bytes 393224 | tf_op jit(solution)/shard_map/ppermute | solution.py:52
  58.4 3.1 %collective-permute-done.15.refs_1_ = bf16[128,512]{1,0:T(8,128)(2,1)S(1)} collective-permute-done((bf16[128,512]{1,0:T(8,128)(2,1)S(1)}, bf16[128,512]{1,0:T(8,128)(2,1)S(1)}, u32[]{:S(2)}, u32[]{:S(2)}) %collective-permute-start.15) | collective-permute-done | bytes 131104 | tf_op jit(solution)/shard_map/ppermute | solution.py:52
  61.4 4.0 %collective-permute-done.16.refs_2_ = bf16[128,512]{1,0:T(8,128)(2,1)S(1)} collective-permute-done((bf16[128,512]{1,0:T(8,128)(2,1)S(1)}, bf16[128,512]{1,0:T(8,128)(2,1)S(1)}, u32[]{:S(2)}, u32[]{:S(2)}) %collective-permute-start.16) | collective-permute-done | bytes 131104 | tf_op jit(solution)/shard_map/ppermute | solution.py:52
  65.4 2.3 %collective-permute-start.7 = (bf16[64,512]{1,0:T(8,128)(2,1)S(1)}, bf16[64,512]{1,0:T(8,128)(2,1)S(1)}, u32[]{:S(2)}, u32[]{:S(2)}) collective-permute-start(bf16[64,512]{1,0:T(8,128)(2,1)S(1)} %shard_map.108.refs_0_), channel_id=1, source_target_pairs={{0,12},{1,13},{2,14},{3,15},{4,0},{5,1},{6,2},{7,3},{8,4},{9,5},{1... | collective-permute-start | bytes 196616 | tf_op jit(solution)/shard_map/ppermute | solution.py:52
  67.8 0.1 collective-permute-start.20
  67.9 2.9 %collective-permute-done.6.refs_2_ = bf16[64,512]{1,0:T(8,128)(2,1)S(1)} collective-permute-done((bf16[64,512]{1,0:T(8,128)(2,1)S(1)}, bf16[64,512]{1,0:T(8,128)(2,1)S(1)}, u32[]{:S(2)}, u32[]{:S(2)}) %collective-permute-start.6) | collective-permute-done | bytes 65568 | tf_op jit(solution)/shard_map/ppermute | solution.py:52
  70.8 0.5 collective-permute-done.7.refs_3_
  71.3 0.1 collective-permute-start.8
  71.4 0.1 collective-permute-start.18
  71.5 6.4 %collective-permute-done.8.refs_1_ = bf16[64,2048]{1,0:T(8,128)(2,1)} collective-permute-done((bf16[64,2048]{1,0:T(8,128)(2,1)S(1)}, bf16[64,2048]{1,0:T(8,128)(2,1)}, u32[]{:S(2)}, u32[]{:S(2)}) %collective-permute-start.8) | collective-permute-done | bytes 262176 | tf_op jit(solution)/shard_map/ppermute | solution.py:52
  77.9 0.1 copy.11.e_ref
  78.1 0.0 copy-start.1
  78.1 3.7 %shard_map.116.refs_7_ = f32[512,768]{1,0:T(8,128)S(1)} custom-call(bf16[512,768]{1,0:T(8,128)(2,1)S(1)} %copy-done.3, bf16[512,768]{1,0:T(8,128)(2,1)S(1)} %collective-permute-done.21.l_ref, bf16[512,768]{1,0:T(8,128)(2,1)} %collective-permute-done.22.h_ref, bf16[512,768]{1,0:T(8,128)(2,1)S(1)} %copy-done.4, bf16[2,128,128]{2,1,0:T(8,128)(2,1)S(1)} %copy-done.7, ...), custom_call_target="tpu_custom_call" | custom-call | flops 235929600 | bytes 4718592 | tf_op jit(solution)/shard_map/pallas_call | solution.py:219
  81.8 0.0 copy-start.11
  81.8 0.0 copy-start.12
  81.8 4.3 %shard_map.117 = (f32[512,768]{1,0:T(8,128)S(1)}, bf16[256,256]{1,0:T(8,128)(2,1)S(1)}, f32[256,256]{1,0:T(8,128)S(1)}) custom-call(bf16[64,2048]{1,0:T(8,128)(2,1)S(1)} %shard_map.109.refs_0_, bf16[64,2048]{1,0:T(8,128)(2,1)} %collective-permute-done.8.refs_1_, bf16[128,2048]{1,0:T(8,128)(2,1)S(1)} %shard_map.115.refs_2_, ...), custom_call_target="tpu_custom_call" | custom-call | flops 1811939328 | bytes 9568256 | tf_op jit(solution)/shard_map/pallas_call | solution.py:84
  86.1 1.2 %copy-done.5 = f32[512,768]{1,0:T(8,128)} copy-done((f32[512,768]{1,0:T(8,128)}, f32[512,768]{1,0:T(8,128)S(1)}, u32[]{:S(2)}) %copy-start.5) | copy-done | bytes 1572888
  87.3 0.5 collective-permute-start.23
  87.8 1.0 collective-permute-done.23.refs_1_
  88.8 0.1 collective-permute-start.24
  88.9 4.3 %collective-permute-done.24.refs_0_ = bf16[128,256]{1,0:T(8,128)(2,1)S(1)} collective-permute-done((bf16[128,256]{1,0:T(8,128)(2,1)S(1)}, bf16[128,256]{1,0:T(8,128)(2,1)S(1)}, u32[]{:S(2)}, u32[]{:S(2)}) %collective-permute-start.24) | collective-permute-done | bytes 65568 | tf_op jit(solution)/shard_map/ppermute | solution.py:52
  93.3 1.4 %collective-permute-start.25 = (bf16[128,256]{1,0:T(8,128)(2,1)S(1)}, bf16[128,256]{1,0:T(8,128)(2,1)S(1)}, u32[]{:S(2)}, u32[]{:S(2)}) collective-permute-start(bf16[128,256]{1,0:T(8,128)(2,1)S(1)} %get-tuple-element.42), channel_id=1, source_target_pairs={{0,4},{1,5},{2,6},{3,7},{4,8},{5,9},{6,10},{7,11},{8,12},{9,13},{1... | collective-permute-start | bytes 196616 | tf_op jit(solution)/shard_map/ppermute | solution.py:52
  94.7 1.8 %collective-permute-start.26 = (bf16[128,256]{1,0:T(8,128)(2,1)S(1)}, bf16[128,256]{1,0:T(8,128)(2,1)S(1)}, u32[]{:S(2)}, u32[]{:S(2)}) collective-permute-start(bf16[128,256]{1,0:T(8,128)(2,1)S(1)} %get-tuple-element.42), channel_id=1, source_target_pairs={{0,8},{1,9},{2,10},{3,11},{4,12},{5,13},{6,14},{7,15},{8,0},{9,1},... | collective-permute-start | bytes 196616 | tf_op jit(solution)/shard_map/ppermute | solution.py:52
  96.5 1.1 %collective-permute-start.27 = (bf16[128,256]{1,0:T(8,128)(2,1)S(1)}, bf16[128,256]{1,0:T(8,128)(2,1)S(1)}, u32[]{:S(2)}, u32[]{:S(2)}) collective-permute-start(bf16[128,256]{1,0:T(8,128)(2,1)S(1)} %get-tuple-element.42), channel_id=1, source_target_pairs={{0,12},{1,13},{2,14},{3,15},{4,0},{5,1},{6,2},{7,3},{8,4},{9,5},{1... | collective-permute-start | bytes 196616 | tf_op jit(solution)/shard_map/ppermute | solution.py:52
  97.6 2.5 %collective-permute-done.25.refs_0_ = bf16[128,256]{1,0:T(8,128)(2,1)S(1)} collective-permute-done((bf16[128,256]{1,0:T(8,128)(2,1)S(1)}, bf16[128,256]{1,0:T(8,128)(2,1)S(1)}, u32[]{:S(2)}, u32[]{:S(2)}) %collective-permute-start.25) | collective-permute-done | bytes 65568 | tf_op jit(solution)/shard_map/ppermute | solution.py:52
  100.1 1.7 %collective-permute-done.26.refs_1_ = bf16[128,256]{1,0:T(8,128)(2,1)S(1)} collective-permute-done((bf16[128,256]{1,0:T(8,128)(2,1)S(1)}, bf16[128,256]{1,0:T(8,128)(2,1)S(1)}, u32[]{:S(2)}, u32[]{:S(2)}) %collective-permute-start.26) | collective-permute-done | bytes 65568 | tf_op jit(solution)/shard_map/ppermute | solution.py:52
  101.8 0.5 collective-permute-start.28
  102.3 3.8 %collective-permute-done.28.refs_1_ = bf16[128,256]{1,0:T(8,128)(2,1)S(1)} collective-permute-done((bf16[128,256]{1,0:T(8,128)(2,1)S(1)}, bf16[128,256]{1,0:T(8,128)(2,1)S(1)}, u32[]{:S(2)}, u32[]{:S(2)}) %collective-permute-start.28) | collective-permute-done | bytes 65568 | tf_op jit(solution)/shard_map/ppermute | solution.py:52
  106.1 0.1 copy.12.refs_7_
  106.3 0.1 copy.13.refs_8_
  106.4 0.9 collective-permute-done.30.refs_3_
  107.4 1.4 %copy-done.6 = f32[512,768]{1,0:T(8,128)S(1)} copy-done((f32[512,768]{1,0:T(8,128)S(1)}, f32[512,768]{1,0:T(8,128)}, u32[]{:S(2)}) %copy-start.6) | copy-done | bytes 1572888
  108.8 1.6 %shard_map.121 = (bf16[512,768]{1,0:T(8,128)(2,1)}, bf16[512,768]{1,0:T(8,128)(2,1)}) custom-call(bf16[128,256]{1,0:T(8,128)(2,1)S(1)} %shard_map.120.refs_0_, bf16[128,256]{1,0:T(8,128)(2,1)S(1)} %collective-permute-done.28.refs_1_, bf16[128,256]{1,0:T(8,128)(2,1)S(1)} %collective-permute-done.29.refs_2_, ...), custom_call_target="tpu_custom_call" | custom-call | flops 201326592 | bytes 4984832 | tf_op jit(solution)/shard_map/pallas_call | solution.py:84
  (47 shorter events, 0.3 us)
Async XLA Ops:
  0.6 1.9 %copy-start = (bf16[2048,768]{1,0:T(8,128)(2,1)S(1)}, bf16[2048,768]{1,0:T(8,128)(2,1)}, u32[]{:S(2)}) copy-start(bf16[2048,768]{1,0:T(8,128)(2,1)} %refs_6_.2) | copy-start | bytes 9437188
  2.5 1.1 %copy-start.2 = (bf16[512,768]{1,0:T(8,128)(2,1)S(1)}, bf16[512,768]{1,0:T(8,128)(2,1)}, u32[]{:S(2)}) copy-start(bf16[512,768]{1,0:T(8,128)(2,1)} %refs_6_.3) | copy-start | bytes 2359300
  5.3 5.0 %collective-permute-start.9 = (bf16[128,2048]{1,0:T(8,128)(2,1)S(1)}, bf16[128,2048]{1,0:T(8,128)(2,1)S(1)}, u32[]{:S(2)}, u32[]{:S(2)}) collective-permute-start(bf16[128,2048]{1,0:T(8,128)(2,1)S(1)} %shard_map.110), channel_id=1, source_target_pairs={{0,1},{1,0},{2,3},{3,2},{4,5},{5,4},{6,7},{7,6},{8,9},{9,8},{10,11... | collective-permute-start | bytes 1572872 | tf_op jit(solution)/shard_map/ppermute | solution.py:52
  7.5 10.0 %collective-permute-start = (bf16[128,2048]{1,0:T(8,128)(2,1)S(1)}, bf16[128,2048]{1,0:T(8,128)(2,1)S(1)}, u32[]{:S(2)}, u32[]{:S(2)}) collective-permute-start(bf16[128,2048]{1,0:T(8,128)(2,1)S(1)} %shard_map.105), channel_id=1, source_target_pairs={{0,1},{1,0},{2,3},{3,2},{4,5},{5,4},{6,7},{7,6},{8,9},{9,8},{10,11... | collective-permute-start | bytes 1572872 | tf_op jit(solution)/shard_map/ppermute | solution.py:52
  10.5 20.5 %copy-start.3 = (bf16[512,768]{1,0:T(8,128)(2,1)S(1)}, bf16[512,768]{1,0:T(8,128)(2,1)}, u32[]{:S(2)}) copy-start(bf16[512,768]{1,0:T(8,128)(2,1)} %refs_6_.3) | copy-start | bytes 2359300
  10.5 9.5 %collective-permute-start.10 = (bf16[128,512]{1,0:T(8,128)(2,1)S(1)}, bf16[128,512]{1,0:T(8,128)(2,1)S(1)}, u32[]{:S(2)}, u32[]{:S(2)}) collective-permute-start(bf16[128,512]{1,0:T(8,128)(2,1)S(1)} %get-tuple-element.32), channel_id=1, source_target_pairs={{0,4},{1,5},{2,6},{3,7},{4,8},{5,9},{6,10},{7,11},{8,12},{9,13},{1... | collective-permute-start | bytes 393224 | tf_op jit(solution)/shard_map/ppermute | solution.py:52
  13.5 11.5 %collective-permute-start.11 = (bf16[128,512]{1,0:T(8,128)(2,1)S(1)}, bf16[128,512]{1,0:T(8,128)(2,1)S(1)}, u32[]{:S(2)}, u32[]{:S(2)}) collective-permute-start(bf16[128,512]{1,0:T(8,128)(2,1)S(1)} %get-tuple-element.33), channel_id=1, source_target_pairs={{0,8},{1,9},{2,10},{3,11},{4,12},{5,13},{6,14},{7,15},{8,0},{9,1},... | collective-permute-start | bytes 393224 | tf_op jit(solution)/shard_map/ppermute | solution.py:52
  16.1 8.9 %collective-permute-start.12 = (bf16[128,512]{1,0:T(8,128)(2,1)S(1)}, bf16[128,512]{1,0:T(8,128)(2,1)S(1)}, u32[]{:S(2)}, u32[]{:S(2)}) collective-permute-start(bf16[128,512]{1,0:T(8,128)(2,1)S(1)} %get-tuple-element.34), channel_id=1, source_target_pairs={{0,12},{1,13},{2,14},{3,15},{4,0},{5,1},{6,2},{7,3},{8,4},{9,5},{1... | collective-permute-start | bytes 393224 | tf_op jit(solution)/shard_map/ppermute | solution.py:52
  17.6 17.8 %collective-permute-start.1 = (bf16[64,2048]{1,0:T(8,128)(2,1)S(1)}, bf16[64,2048]{1,0:T(8,128)(2,1)S(1)}, u32[]{:S(2)}, u32[]{:S(2)}) collective-permute-start(bf16[64,2048]{1,0:T(8,128)(2,1)S(1)} %get-tuple-element.25), channel_id=1, source_target_pairs={{0,2},{1,3},{2,0},{3,1},{4,6},{5,7},{6,4},{7,5},{8,10},{9,11},{10,... | collective-permute-start | bytes 786440 | tf_op jit(solution)/shard_map/ppermute | solution.py:52
  25.1 4.3 %collective-permute-start.13 = (bf16[64,512]{1,0:T(8,128)(2,1)S(1)}, bf16[64,512]{1,0:T(8,128)(2,1)S(1)}, u32[]{:S(2)}, u32[]{:S(2)}) collective-permute-start(bf16[64,512]{1,0:T(8,128)(2,1)S(1)} %get-tuple-element.36), channel_id=1, source_target_pairs={{0,2},{1,3},{2,0},{3,1},{4,6},{5,7},{6,4},{7,5},{8,10},{9,11},{10,... | collective-permute-start | bytes 196616 | tf_op jit(solution)/shard_map/ppermute | solution.py:52
  29.4 48.4 %copy-start.10 = (f32[512]{0:T(512)S(1)}, f32[512]{0:T(512)}, u32[]{:S(2)}) copy-start(f32[512]{0:T(512)} %param.14) | copy-start | bytes 6148
  29.4 9.3 %collective-permute-start.14 = (bf16[64,512]{1,0:T(8,128)(2,1)S(1)}, bf16[64,512]{1,0:T(8,128)(2,1)S(1)}, u32[]{:S(2)}, u32[]{:S(2)}) collective-permute-start(bf16[64,512]{1,0:T(8,128)(2,1)S(1)} %shard_map.113.refs_0_), channel_id=1, source_target_pairs={{0,2},{1,3},{2,0},{3,1},{4,6},{5,7},{6,4},{7,5},{8,10},{9,11},{10,... | collective-permute-start | bytes 196616 | tf_op jit(solution)/shard_map/ppermute | solution.py:52
  30.9 47.1 %collective-permute-start.21 = (bf16[512,768]{1,0:T(8,128)(2,1)S(1)}, bf16[512,768]{1,0:T(8,128)(2,1)S(1)}, u32[]{:S(2)}, u32[]{:S(2)}) collective-permute-start(bf16[512,768]{1,0:T(8,128)(2,1)S(1)} %copy-done.3), channel_id=1, source_target_pairs={{0,1},{1,2},{2,3},{3,4},{4,5},{5,6},{6,7},{7,8},{8,9},{9,10},{10,1... | collective-permute-start | bytes 2359304 | tf_op jit(solution)/shard_map/ppermute | solution.py:52
  31.0 47.1 %collective-permute-start.22 = (bf16[512,768]{1,0:T(8,128)(2,1)S(1)}, bf16[512,768]{1,0:T(8,128)(2,1)}, u32[]{:S(2)}, u32[]{:S(2)}) collective-permute-start(bf16[512,768]{1,0:T(8,128)(2,1)S(1)} %copy-done.3), channel_id=1, source_target_pairs={{0,15},{1,0},{2,1},{3,2},{4,3},{5,4},{6,5},{7,6},{8,7},{9,8},{10,9... | collective-permute-start | bytes 2359304 | tf_op jit(solution)/shard_map/ppermute | solution.py:52
  35.4 42.6 %copy-start.8 = (f32[768]{0:T(1024)S(1)}, f32[768]{0:T(1024)}, u32[]{:S(2)}) copy-start(f32[768]{0:T(1024)} %param.12) | copy-start | bytes 9220
  35.4 42.6 %copy-start.9 = (f32[768]{0:T(1024)S(1)}, f32[768]{0:T(1024)}, u32[]{:S(2)}) copy-start(f32[768]{0:T(1024)} %param.13) | copy-start | bytes 9220
  35.4 42.7 %copy-start.4 = (bf16[512,768]{1,0:T(8,128)(2,1)S(1)}, bf16[512,768]{1,0:T(8,128)(2,1)}, u32[]{:S(2)}) copy-start(bf16[512,768]{1,0:T(8,128)(2,1)} %refs_4_.1) | copy-start | bytes 2359300
  35.4 42.7 %copy-start.7 = (bf16[2,128,128]{2,1,0:T(8,128)(2,1)S(1)}, bf16[2,128,128]{2,1,0:T(8,128)(2,1)}, u32[]{:S(2)}) copy-start(bf16[2,128,128]{2,1,0:T(8,128)(2,1)} %constant.2.clone.m_ref) | copy-start | bytes 196612
  35.5 18.9 %collective-permute-start.2 = (bf16[64,512]{1,0:T(8,128)(2,1)S(1)}, bf16[64,512]{1,0:T(8,128)(2,1)S(1)}, u32[]{:S(2)}, u32[]{:S(2)}) collective-permute-start(bf16[64,512]{1,0:T(8,128)(2,1)S(1)} %get-tuple-element.27), channel_id=1, source_target_pairs={{0,4},{1,5},{2,6},{3,7},{4,8},{5,9},{6,10},{7,11},{8,12},{9,13},{1... | collective-permute-start | bytes 196616 | tf_op jit(solution)/shard_map/ppermute | solution.py:52
  37.0 19.6 %collective-permute-start.3 = (bf16[64,512]{1,0:T(8,128)(2,1)S(1)}, bf16[64,512]{1,0:T(8,128)(2,1)S(1)}, u32[]{:S(2)}, u32[]{:S(2)}) collective-permute-start(bf16[64,512]{1,0:T(8,128)(2,1)S(1)} %get-tuple-element.28), channel_id=1, source_target_pairs={{0,8},{1,9},{2,10},{3,11},{4,12},{5,13},{6,14},{7,15},{8,0},{9,1},... | collective-permute-start | bytes 196616 | tf_op jit(solution)/shard_map/ppermute | solution.py:52
  38.7 18.0 %collective-permute-start.4 = (bf16[64,512]{1,0:T(8,128)(2,1)S(1)}, bf16[64,512]{1,0:T(8,128)(2,1)S(1)}, u32[]{:S(2)}, u32[]{:S(2)}) collective-permute-start(bf16[64,512]{1,0:T(8,128)(2,1)S(1)} %get-tuple-element.29), channel_id=1, source_target_pairs={{0,12},{1,13},{2,14},{3,15},{4,0},{5,1},{6,2},{7,3},{8,4},{9,5},{1... | collective-permute-start | bytes 196616 | tf_op jit(solution)/shard_map/ppermute | solution.py:52
  54.4 7.0 %collective-permute-start.15 = (bf16[128,512]{1,0:T(8,128)(2,1)S(1)}, bf16[128,512]{1,0:T(8,128)(2,1)S(1)}, u32[]{:S(2)}, u32[]{:S(2)}) collective-permute-start(bf16[128,512]{1,0:T(8,128)(2,1)S(1)} %shard_map.114.refs_0_), channel_id=1, source_target_pairs={{0,4},{1,5},{2,6},{3,7},{4,8},{5,9},{6,10},{7,11},{8,12},{9,13},{1... | collective-permute-start | bytes 393224 | tf_op jit(solution)/shard_map/ppermute | solution.py:52
  56.7 8.8 %collective-permute-start.16 = (bf16[128,512]{1,0:T(8,128)(2,1)S(1)}, bf16[128,512]{1,0:T(8,128)(2,1)S(1)}, u32[]{:S(2)}, u32[]{:S(2)}) collective-permute-start(bf16[128,512]{1,0:T(8,128)(2,1)S(1)} %shard_map.114.refs_0_), channel_id=1, source_target_pairs={{0,8},{1,9},{2,10},{3,11},{4,12},{5,13},{6,14},{7,15},{8,0},{9,1},... | collective-permute-start | bytes 393224 | tf_op jit(solution)/shard_map/ppermute | solution.py:52
  56.7 8.8 %collective-permute-start.17 = (bf16[128,512]{1,0:T(8,128)(2,1)S(1)}, bf16[128,512]{1,0:T(8,128)(2,1)S(1)}, u32[]{:S(2)}, u32[]{:S(2)}) collective-permute-start(bf16[128,512]{1,0:T(8,128)(2,1)S(1)} %shard_map.114.refs_0_), channel_id=1, source_target_pairs={{0,12},{1,13},{2,14},{3,15},{4,0},{5,1},{6,2},{7,3},{8,4},{9,5},{1... | collective-permute-start | bytes 393224 | tf_op jit(solution)/shard_map/ppermute | solution.py:52
  61.4 6.4 %collective-permute-start.5 = (bf16[64,512]{1,0:T(8,128)(2,1)S(1)}, bf16[64,512]{1,0:T(8,128)(2,1)S(1)}, u32[]{:S(2)}, u32[]{:S(2)}) collective-permute-start(bf16[64,512]{1,0:T(8,128)(2,1)S(1)} %shard_map.108.refs_0_), channel_id=1, source_target_pairs={{0,4},{1,5},{2,6},{3,7},{4,8},{5,9},{6,10},{7,11},{8,12},{9,13},{1... | collective-permute-start | bytes 196616 | tf_op jit(solution)/shard_map/ppermute | solution.py:52
  65.4 5.4 %collective-permute-start.6 = (bf16[64,512]{1,0:T(8,128)(2,1)S(1)}, bf16[64,512]{1,0:T(8,128)(2,1)S(1)}, u32[]{:S(2)}, u32[]{:S(2)}) collective-permute-start(bf16[64,512]{1,0:T(8,128)(2,1)S(1)} %shard_map.108.refs_0_), channel_id=1, source_target_pairs={{0,8},{1,9},{2,10},{3,11},{4,12},{5,13},{6,14},{7,15},{8,0},{9,1},... | collective-permute-start | bytes 196616 | tf_op jit(solution)/shard_map/ppermute | solution.py:52
  65.4 5.8 %collective-permute-start.7 = (bf16[64,512]{1,0:T(8,128)(2,1)S(1)}, bf16[64,512]{1,0:T(8,128)(2,1)S(1)}, u32[]{:S(2)}, u32[]{:S(2)}) collective-permute-start(bf16[64,512]{1,0:T(8,128)(2,1)S(1)} %shard_map.108.refs_0_), channel_id=1, source_target_pairs={{0,12},{1,13},{2,14},{3,15},{4,0},{5,1},{6,2},{7,3},{8,4},{9,5},{1... | collective-permute-start | bytes 196616 | tf_op jit(solution)/shard_map/ppermute | solution.py:52
  67.8 14.0 %collective-permute-start.20 = (bf16[128,2048]{1,0:T(8,128)(2,1)S(1)}, bf16[128,2048]{1,0:T(8,128)(2,1)}, u32[]{:S(2)}, u32[]{:S(2)}) collective-permute-start(bf16[128,2048]{1,0:T(8,128)(2,1)S(1)} %shard_map.115.refs_2_), channel_id=1, source_target_pairs={{0,1},{1,0},{2,3},{3,2},{4,5},{5,4},{6,7},{7,6},{8,9},{9,8},{10,11... | collective-permute-start | bytes 1572872 | tf_op jit(solution)/shard_map/ppermute | solution.py:52
  71.3 6.5 %collective-permute-start.8 = (bf16[64,2048]{1,0:T(8,128)(2,1)S(1)}, bf16[64,2048]{1,0:T(8,128)(2,1)}, u32[]{:S(2)}, u32[]{:S(2)}) collective-permute-start(bf16[64,2048]{1,0:T(8,128)(2,1)S(1)} %shard_map.109.refs_0_), channel_id=1, source_target_pairs={{0,2},{1,3},{2,0},{3,1},{4,6},{5,7},{6,4},{7,5},{8,10},{9,11},{10,... | collective-permute-start | bytes 786440 | tf_op jit(solution)/shard_map/ppermute | solution.py:52
  71.4 10.4 %collective-permute-start.18 = (bf16[64,2048]{1,0:T(8,128)(2,1)S(1)}, bf16[64,2048]{1,0:T(8,128)(2,1)}, u32[]{:S(2)}, u32[]{:S(2)}) collective-permute-start(bf16[64,2048]{1,0:T(8,128)(2,1)S(1)} %shard_map.109.refs_0_), channel_id=1, source_target_pairs={{0,1},{1,0},{2,3},{3,2},{4,5},{5,4},{6,7},{7,6},{8,9},{9,8},{10,11... | collective-permute-start | bytes 786440 | tf_op jit(solution)/shard_map/ppermute | solution.py:52
  77.9 4.0 %collective-permute-start.19 = (bf16[64,2048]{1,0:T(8,128)(2,1)}, bf16[64,2048]{1,0:T(8,128)(2,1)}, u32[]{:S(2)}, u32[]{:S(2)}) collective-permute-start(bf16[64,2048]{1,0:T(8,128)(2,1)} %collective-permute-done.8.refs_1_), channel_id=1, source_target_pairs={{0,1},{1,0},{2,3},{3,2},{4,5},{5,4},{6,7},{7,6},{8,9},{9,8},{10,11... | collective-permute-start | bytes 786440 | tf_op jit(solution)/shard_map/ppermute | solution.py:52
  78.1 3.8 %copy-start.1 = (bf16[2048,768]{1,0:T(8,128)(2,1)S(1)}, bf16[2048,768]{1,0:T(8,128)(2,1)}, u32[]{:S(2)}) copy-start(bf16[2048,768]{1,0:T(8,128)(2,1)} %refs_6_.2) | copy-start | bytes 9437188
  81.8 24.3 %copy-start.11 = (s32[512]{0:T(512)S(1)}, s32[512]{0:T(512)}, u32[]{:S(2)}) copy-start(s32[512]{0:T(512)} %param.15) | copy-start | bytes 6148
  81.8 24.5 %copy-start.12 = (s32[512]{0:T(512)S(1)}, s32[512]{0:T(512)}, u32[]{:S(2)}) copy-start(s32[512]{0:T(512)} %param.16) | copy-start | bytes 6148
  86.1 1.2 %copy-start.5 = (f32[512,768]{1,0:T(8,128)}, f32[512,768]{1,0:T(8,128)S(1)}, u32[]{:S(2)}) copy-start(f32[512,768]{1,0:T(8,128)S(1)} %get-tuple-element.43.refs_5_) | copy-start | bytes 4718596
  87.3 1.5 %collective-permute-start.23 = (bf16[256,256]{1,0:T(8,128)(2,1)S(1)}, bf16[256,256]{1,0:T(8,128)(2,1)S(1)}, u32[]{:S(2)}, u32[]{:S(2)}) collective-permute-start(bf16[256,256]{1,0:T(8,128)(2,1)S(1)} %get-tuple-element.38), channel_id=1, source_target_pairs={{0,1},{1,0},{2,3},{3,2},{4,5},{5,4},{6,7},{7,6},{8,9},{9,8},{10,11... | collective-permute-start | bytes 393224 | tf_op jit(solution)/shard_map/ppermute | solution.py:52
  88.8 4.4 %collective-permute-start.24 = (bf16[128,256]{1,0:T(8,128)(2,1)S(1)}, bf16[128,256]{1,0:T(8,128)(2,1)S(1)}, u32[]{:S(2)}, u32[]{:S(2)}) collective-permute-start(bf16[128,256]{1,0:T(8,128)(2,1)S(1)} %get-tuple-element.40), channel_id=1, source_target_pairs={{0,2},{1,3},{2,0},{3,1},{4,6},{5,7},{6,4},{7,5},{8,10},{9,11},{10,... | collective-permute-start | bytes 196616 | tf_op jit(solution)/shard_map/ppermute | solution.py:52
  93.3 6.8 %collective-permute-start.25 = (bf16[128,256]{1,0:T(8,128)(2,1)S(1)}, bf16[128,256]{1,0:T(8,128)(2,1)S(1)}, u32[]{:S(2)}, u32[]{:S(2)}) collective-permute-start(bf16[128,256]{1,0:T(8,128)(2,1)S(1)} %get-tuple-element.42), channel_id=1, source_target_pairs={{0,4},{1,5},{2,6},{3,7},{4,8},{5,9},{6,10},{7,11},{8,12},{9,13},{1... | collective-permute-start | bytes 196616 | tf_op jit(solution)/shard_map/ppermute | solution.py:52
  94.7 7.1 %collective-permute-start.26 = (bf16[128,256]{1,0:T(8,128)(2,1)S(1)}, bf16[128,256]{1,0:T(8,128)(2,1)S(1)}, u32[]{:S(2)}, u32[]{:S(2)}) collective-permute-start(bf16[128,256]{1,0:T(8,128)(2,1)S(1)} %get-tuple-element.42), channel_id=1, source_target_pairs={{0,8},{1,9},{2,10},{3,11},{4,12},{5,13},{6,14},{7,15},{8,0},{9,1},... | collective-permute-start | bytes 196616 | tf_op jit(solution)/shard_map/ppermute | solution.py:52
  96.5 5.3 %collective-permute-start.27 = (bf16[128,256]{1,0:T(8,128)(2,1)S(1)}, bf16[128,256]{1,0:T(8,128)(2,1)S(1)}, u32[]{:S(2)}, u32[]{:S(2)}) collective-permute-start(bf16[128,256]{1,0:T(8,128)(2,1)S(1)} %get-tuple-element.42), channel_id=1, source_target_pairs={{0,12},{1,13},{2,14},{3,15},{4,0},{5,1},{6,2},{7,3},{8,4},{9,5},{1... | collective-permute-start | bytes 196616 | tf_op jit(solution)/shard_map/ppermute | solution.py:52
  101.8 4.3 %collective-permute-start.28 = (bf16[128,256]{1,0:T(8,128)(2,1)S(1)}, bf16[128,256]{1,0:T(8,128)(2,1)S(1)}, u32[]{:S(2)}, u32[]{:S(2)}) collective-permute-start(bf16[128,256]{1,0:T(8,128)(2,1)S(1)} %shard_map.120.refs_0_), channel_id=1, source_target_pairs={{0,2},{1,3},{2,0},{3,1},{4,6},{5,7},{6,4},{7,5},{8,10},{9,11},{10,... | collective-permute-start | bytes 196616 | tf_op jit(solution)/shard_map/ppermute | solution.py:52
  102.3 4.2 %collective-permute-start.29 = (bf16[128,256]{1,0:T(8,128)(2,1)S(1)}, bf16[128,256]{1,0:T(8,128)(2,1)S(1)}, u32[]{:S(2)}, u32[]{:S(2)}) collective-permute-start(bf16[128,256]{1,0:T(8,128)(2,1)S(1)} %shard_map.120.refs_0_), channel_id=1, source_target_pairs={{0,1},{1,0},{2,3},{3,2},{4,5},{5,4},{6,7},{7,6},{8,9},{9,8},{10,11... | collective-permute-start | bytes 196616 | tf_op jit(solution)/shard_map/ppermute | solution.py:52
  106.1 1.3 %collective-permute-start.30 = (bf16[128,256]{1,0:T(8,128)(2,1)S(1)}, bf16[128,256]{1,0:T(8,128)(2,1)S(1)}, u32[]{:S(2)}, u32[]{:S(2)}) collective-permute-start(bf16[128,256]{1,0:T(8,128)(2,1)S(1)} %collective-permute-done.28.refs_1_), channel_id=1, source_target_pairs={{0,1},{1,0},{2,3},{3,2},{4,5},{5,4},{6,7},{7,6},{8,9},{9,8},{10,11... | collective-permute-start | bytes 196616 | tf_op jit(solution)/shard_map/ppermute | solution.py:52
  107.4 1.4 %copy-start.6 = (f32[512,768]{1,0:T(8,128)S(1)}, f32[512,768]{1,0:T(8,128)}, u32[]{:S(2)}) copy-start(f32[512,768]{1,0:T(8,128)} %copy-done.5) | copy-start | bytes 4718596

commit v3 on v2

--- a/solution.py
+++ b/solution.py
@@ -125,61 +125,22 @@
     )(response, projectors)
 
 
-def split_body(received, level, along, *refs):
-    keep_ref, taken, (own_ref, *sends) = refs[0], refs[1 : 1 + received], refs[1 + received :]
-    size, _ = level
-    me = position(level)
-    width = own_ref.shape[along]
-    for step, out in enumerate((own_ref, *sends)):
-        at = pl.multiple_of(lax.rem(me + step, jnp.int32(size)) * width, width)
-        part = (pl.ds(at, width), slice(None)) if along == 0 else (slice(None), pl.ds(at, width))
-        total = keep_ref[part]
-        for ref in taken:
-            total = total + ref[part].astype(F32)
-        out[...] = total.astype(out.dtype)
-
-
-def split(keep, taken, level, along):
-    size, _ = level
-    shape = list(keep.shape)
-    shape[along] //= size
-    outs = [struct(shape, F32)] + [struct(shape, BF16)] * (size - 1)
-    return local_call(
-        functools.partial(split_body, len(taken), level, along), outs, [keep, *taken]
-    )
-
-
-def finish_body(scale, keep_ref, *refs):
-    *taken, out_ref = refs
-    total = keep_ref[...]
-    for ref in taken:
-        total = total + ref[...].astype(F32)
-    out_ref[...] = (total * scale).astype(out_ref.dtype)
-
-
-def finish(keep, taken, scale):
-    return local_call(
-        functools.partial(finish_body, scale), struct(keep.shape, BF16), [keep, *taken]
-    )
-
-
-def place_body(level, along, *refs):
-    *parts, out_ref = refs
-    size, _ = level
-    me = position(level)
-    width = parts[0].shape[along]
-    for step, ref in enumerate(parts):
-        at = pl.multiple_of(lax.rem(me - step + size, jnp.int32(size)) * width, width)
-        if along == 0:
-            out_ref[pl.ds(at, width), :] = ref[...]
-        else:
-            out_ref[:, pl.ds(at, width)] = ref[...]
-
-
-def place(parts, level, along):
-    shape = list(parts[0].shape)
-    shape[along] *= level[0]
-    return local_call(functools.partial(place_body, level, along), struct(shape, BF16), parts)
+def add_core_body(across, along, keep_ref, taken_ref, out_ref):
+    _, rows, width = out_ref.shape
+    for k in range(along[0]):
+        for i in range(across[0]):
+            part = (slice(i * rows, (i + 1) * rows), slice(k * width, (k + 1) * width))
+            total = keep_ref[part] + taken_ref[part].astype(F32)
+            out_ref[k * across[0] + i] = total.astype(BF16)
+
+
+def finish_body(scale, taken_ref, out_ref):
+    total = taken_ref[0].astype(F32)
+    for k in range(1, taken_ref.shape[0]):
+        total = total + taken_ref[k].astype(F32)
+    low = (total * scale).astype(BF16)
+    for k in range(out_ref.shape[0]):
+        out_ref[k] = low
 
 
 def local_body(depth, r_ref, l_ref, h_ref, o_ref, m_ref, pot_ref, v_ref, e_ref, out_ref):
@@ -240,22 +201,18 @@
     return max(0, min(group * group_rows - REACH * blk, bands - width))
 
 
-def apply_body(core, across, rows_x, group_rows, width, blk, *refs):
-    size = across[0]
-    blocks = refs[: 2 * (size + 1)]
-    p_ref, base_ref, o_ref, u_ref, send_ref, keep_ref, c_ref, s_ref = refs[2 * (size + 1) :]
+def apply_body(core, across, group_rows, width, blk, *refs):
+    own_ref, other_ref, p_ref, base_ref, o_ref, u_ref, s_out_ref, c_ref = refs
     bands, cells = u_ref.shape
-    c, x = position(core), position(across)
+    c = position(core)
     half = bands // 2
-    share = rows_x // size
-    for k, ref in enumerate(blocks):
-        side, step = divmod(k, size + 1)
-        at = (c if side == 0 else 1 - c) * half
-        if step < size:
-            at = at + lax.rem(x - step + size, jnp.int32(size)) * share
-        else:
-            at = at + rows_x
-        c_ref[pl.ds(pl.multiple_of(at, 16), ref.shape[0]), :] = ref[...]
+    _, rows, share = own_ref.shape
+    for side, ref in enumerate((own_ref, other_ref)):
+        first = (c if side == 0 else 1 - c) * half
+        for chip in range(ref.shape[0]):
+            k, i = divmod(chip, across[0])
+            at = pl.multiple_of(first + i * rows, 16)
+            c_ref[pl.ds(at, rows), k * share : (k + 1) * share] = ref[chip]
     tile = 256 if cells % 256 == 0 else 128
     for t in range(cells // tile):
         cols = slice(t * tile, (t + 1) * tile)
@@ -265,42 +222,17 @@
     for g in range(bands // group_rows):
         start = first_orbital(g, group_rows, width, bands, blk)
         mine = slice(g * group_rows, (g + 1) * group_rows)
-        s_ref[mine, :] = lax.dot_general(
+        s_out_ref[mine, :] = lax.dot_general(
             u_ref[mine, :].astype(BF16),
             o_ref[start : start + width, :],
             NT,
             preferred_element_type=F32,
-        )
-    send_ref[...] = s_ref[pl.ds(pl.multiple_of((1 - c) * half, half), half), :].astype(BF16)
-    keep_ref[...] = s_ref[pl.ds(pl.multiple_of(c * half, half), half), :]
-
-
-def sum_body(keep_ref, *refs):
-    *taken, total_ref, low_ref = refs
-    total = keep_ref[...]
-    for ref in taken:
-        total = total + ref[...].astype(F32)
-    total_ref[...] = total
-    low_ref[...] = total.astype(BF16)
-
-
-def add_up(keep, taken):
-    outs = [struct(keep.shape, F32), struct(keep.shape, BF16)]
-    return local_call(sum_body, outs, [keep, *taken])
-
-
-def project_body(core, across, group_rows, width, blk, *refs):
-    size = across[0]
-    blocks = refs[: 2 * size]
-    o_ref, u_ref, r_ref, first_ref, many_ref, updated_ref, residual_ref, w_ref = refs[2 * size :]
+        ).astype(BF16)
+
+
+def project_body(group_rows, width, blk, *refs):
+    w_ref, o_ref, u_ref, r_ref, first_ref, many_ref, updated_ref, residual_ref = refs
     bands = o_ref.shape[0]
-    half = bands // 2
-    c, x = position(core), position(across)
-    for k, ref in enumerate(blocks):
-        side, step = divmod(k, size)
-        at = (c if side == 0 else 1 - c) * half
-        at = at + lax.rem(x - step + size, jnp.int32(size)) * ref.shape[0]
-        w_ref[pl.ds(pl.multiple_of(at, 16), ref.shape[0]), :] = ref[...]
     for g in range(bands // group_rows):
         start = first_orbital(g, group_rows, width, bands, blk)
         mine = slice(g * group_rows, (g + 1) * group_rows)
@@ -323,6 +255,7 @@
     projections = projectors.shape[0]
     halo = 6 * GY * GZ
     core, across, along = levels_of(count)
+    chips = count // 2
     ring = (count, 1)
     ace_scale = 1.0 / math.sqrt(cells * projections)
     window_scale = 1.0 / math.sqrt(cells * bands)
@@ -330,74 +263,50 @@
     group_rows = GROUP_BLOCKS * blk
     width = (GROUP_BLOCKS + 2 * REACH) * blk
     half = bands // 2
-    rows_x = half // 2
-    rows_z = half - rows_x
+    same_core = [[2 * chip + side for chip in range(chips)] for side in range(2)]
     matrix = jnp.asarray(plane_matrix())
     potential, perturbing = potential[None, :], perturbing[None, :]
     energies, window_start, block_count = (
         a[:, None] for a in (energies, window_start, block_count)
     )
 
-    def to(array, level):
-        return [shifted(array, count, level, k) for k in range(1, level[0])]
-
-    def parts_to(parts, level):
-        return [shifted(part, count, level, k + 1) for k, part in enumerate(parts)]
-
     low = shifted(response[:, local_cells - halo :], count, ring, 1)
     high = shifted(response[:, :halo], count, ring, -1)
 
-    (sent_z,) = partial_intersections(response, projectors, core, [(True, rows_x, rows_z)])
-    sent_z = shifted(sent_z, count, core, 1)
-    (sent_x,) = partial_intersections(response, projectors, core, [(True, 0, rows_x)])
-    sent_x = shifted(sent_x, count, core, 1)
-    keep_z, keep_x = partial_intersections(
-        response, projectors, core, [(False, rows_x, rows_z), (False, 0, rows_x)]
-    )
-    keep_z, *parts = split(keep_z, [sent_z], along, 1)
-    taken_z = parts_to(parts, along)
-    keep_x, *parts = split(keep_x, [sent_x], across, 0)
-    taken_x = parts_to(parts, across)
-    keep_x, *parts = split(keep_x, taken_x, along, 1)
-    taken_x = parts_to(parts, along)
-    keep_z, *parts = split(keep_z, taken_z, across, 0)
-    taken_z = parts_to(parts, across)
-    share_z = finish(keep_z, taken_z, ace_scale)
-    share_x = finish(keep_x, taken_x, ace_scale)
-
-    block_z = place([share_z, *to(share_z, across)], across, 0)
-    block_x = place([share_x, *to(share_x, along)], along, 1)
+    (sent,) = partial_intersections(response, projectors, core, [(True, 0, half)])
+    sent = shifted(sent, count, core, 1)
+    (keep,) = partial_intersections(response, projectors, core, [(False, 0, half)])
+    shares = struct((chips, half // across[0], projections // along[0]), BF16)
+    parts = local_call(
+        functools.partial(add_core_body, across, along), shares, [keep, sent]
+    )
+    parts = lax.all_to_all(parts, "band", 0, 0, axis_index_groups=same_core)
+    low, high, parts = lax.optimization_barrier((low, high, parts))
     base = local_part(
         response, low, high, orbitals, matrix, potential, perturbing, energies
     )
-    blocks_x = [block_x, *to(block_x, across)]
-    block_z = place([block_z, *to(block_z, along)], along, 1)
-    blocks = [*blocks_x, block_z]
-    blocks += [shifted(block, count, core, 1) for block in blocks]
-
-    unprojected, send, keep = local_call(
-        functools.partial(apply_body, core, across, rows_x, group_rows, width, blk),
-        [
-            struct((bands, local_cells), F32),
-            struct((half, width), BF16),
-            struct((half, width), F32),
-        ],
-        [*blocks, projectors, base, orbitals],
+    parts, base = lax.optimization_barrier((parts, base))
+    parts = local_call(functools.partial(finish_body, ace_scale), shares, [parts])
+    own = lax.all_to_all(parts, "band", 0, 0, axis_index_groups=same_core)
+    other = shifted(own, count, core, 1)
+
+    unprojected, sums = local_call(
+        functools.partial(apply_body, core, across, group_rows, width, blk),
+        [struct((bands, local_cells), F32), struct((bands, width), BF16)],
+        [own, other, projectors, base, orbitals],
         flops=2 * bands * local_cells * (projections + width),
-        scratch=[pltpu.VMEM((bands, projections), BF16), pltpu.VMEM((bands, width), F32)],
-    )
-    keep, *parts = split(keep, to(send, core), across, 0)
-    total, low = add_up(keep, parts_to(parts, across))
-    weights = finish(total, to(low, along), window_scale)
-    weights = [weights, *to(weights, across)]
-    weights += [shifted(block, count, core, 1) for block in weights]
+        scratch=[pltpu.VMEM((bands, projections), BF16)],
+    )
+    shares = struct((count, bands // count, width), BF16)
+    sums = lax.all_to_all(sums.reshape(shares.shape), "band", 0, 0)
+    weights = local_call(functools.partial(finish_body, window_scale), shares, [sums])
+    weights = lax.all_to_all(weights, "band", 0, 0).reshape(bands, width)
     out = struct((bands, local_cells), BF16)
     return local_call(
-        functools.partial(project_body, core, across, group_rows, width, blk),
+        functools.partial(project_body, group_rows, width, blk),
         (out, out),
-        [*weights, orbitals, unprojected, response, window_start, block_count],
+        [weights, orbitals, unprojected, response, window_start, block_count],
         flops=2 * bands * width * local_cells,
-        scratch=[pltpu.VMEM((bands, width), BF16)],
     )
 
 

time: 111 us -> 121 us (1.090)
  blocking collectives: 0 us -> 46.1 us
  waiting for transfers between devices: 56.9 us -> 37.6 us
  starting transfers between devices: 30.3 us -> 15.9 us
  Pallas kernels: 16.2 us -> 12.8 us
  local copies, waits for them, and re-layouts: 6.09 us -> 7.82 us
    all_to_all x0 -> x2, blocking collectives: none -> 46.1 us  [the longest x1 32.5 us: shards(): own = lax.all_to_all(parts, 'band', 0, 0, axis_index_groups=same_core)]
    ppermute x31 -> x4, waiting for transfers between devices: 56.9 us -> 29.4 us  [shifted(): return lax.ppermute(array, 'band', pairs)]
    ppermute x31 -> x4, starting transfers between devices: 30.3 us -> 5.01 us  [shifted(): return lax.ppermute(array, 'band', pairs)]
    all_to_all x0 -> x2, starting transfers between devices: none -> 10.9 us  [the longest x1 7.32 us: shards(): parts = lax.all_to_all(parts, 'band', 0, 0, axis_index_groups=same_core)]
    all_to_all x0 -> x2, waiting for transfers between devices: none -> 8.28 us  [the longest x1 8.28 us: shards(): weights = lax.all_to_all(weights, 'band', 0, 0).reshape(bands, width)]
    pallas_call x3 -> x2, Pallas kernels: 6.01 us -> 3.45 us  [partial_intersections(): pl.pallas_call(functools.partial(partial_body, core, bands, parts), grid=...]
    broadcast_in_dim x3, local copies, waits for them, and re-layouts: 0.43 us -> 1.86 us  [shards(): a[:, None]]
    pallas_call x14 -> x5, Pallas kernels: 6.5 us -> 5.59 us  [local_call(): pl.pallas_call(body, out_shape=outs, in_specs=[whole() for _ in args], ou...]
  transfers between devices with their start and end apart: 31 -> 6, of which waited for: 16 -> 4; matrix products, arithmetic and copies ran while one was open for 0% -> 2% of each run, Pallas kernels for 8% -> 1%
where the time goes in v3:
time: 121 us
  blocking collectives  46.1 us (38%)
  waiting for transfers between devices  37.6 us (31%)
  starting transfers between devices  15.9 us (13%)
  Pallas kernels  12.8 us (11%)
  local copies, waits for them, and re-layouts  7.82 us (6%)
    all_to_all x1, blocking collectives, shards(): own = lax.all_to_all(parts, 'band', 0, 0, axis_index_groups=same_core)  32.5 us
    ppermute x4, waiting for transfers between devices, shifted(): return lax.ppermute(array, 'band', pairs)  29.4 us
    all_to_all x1, blocking collectives, shards(): sums = lax.all_to_all(sums.reshape(shares.shape), 'band', 0, 0)  13.6 us
    all_to_all x1, waiting for transfers between devices, shards(): weights = lax.all_to_all(weights, 'band', 0, 0).reshape(bands, width)  8.28 us
    all_to_all x1, starting transfers between devices, shards(): parts = lax.all_to_all(parts, 'band', 0, 0, axis_index_groups=same_core)  7.32 us
    unnamed x28, local copies, waits for them, and re-layouts  5.95 us
    pallas_call x5, Pallas kernels, local_call(): pl.pallas_call(body, out_shape=outs, in_specs=[whole() for _ in args], ou...  5.59 us
    ppermute x4, starting transfers between devices, shifted(): return lax.ppermute(array, 'band', pairs)  5.01 us
  transfers between devices with their start and end apart: 6, of which 4 were waited for; matrix products, arithmetic and copies ran while one was open for 2% of the time, Pallas kernels for 1%

profile of v3, /device:TPU:0, one launch (start us, length us, event | category | flops | bytes accessed | tf_op | source)
XLA Modules:
  0.0 121.0 jit_solution(2716730703679124592)
XLA Ops:
  0.6 0.0 copy-start
  0.6 1.9 %copy-done = bf16[2048,768]{1,0:T(8,128)(2,1)S(1)} copy-done((bf16[2048,768]{1,0:T(8,128)(2,1)S(1)}, bf16[2048,768]{1,0:T(8,128)(2,1)}, u32[]{:S(2)}) %copy-start) | copy-done | bytes 3145752
  2.5 0.0 copy-start.2
  2.5 1.1 copy-done.2
  3.7 1.7 %shard_map.105 = bf16[256,2048]{1,0:T(8,128)(2,1)S(1)} custom-call(bf16[512,768]{1,0:T(8,128)(2,1)S(1)} %copy-done.2, bf16[2048,768]{1,0:T(8,128)(2,1)S(1)} %copy-done), custom_call_target="tpu_custom_call" | custom-call | flops 805306368 | bytes 4194304 | tf_op jit(solution)/shard_map/pallas_call | solution.py:114
  5.3 0.5 collective-permute-start.2
  5.9 1.8 %shard_map.104.keep_ref = f32[256,2048]{1,0:T(8,128)S(1)} custom-call(bf16[512,768]{1,0:T(8,128)(2,1)S(1)} %copy-done.2, bf16[2048,768]{1,0:T(8,128)(2,1)S(1)} %copy-done), custom_call_target="tpu_custom_call" | custom-call | flops 805306368 | bytes 5242880 | tf_op jit(solution)/shard_map/pallas_call | solution.py:114
  7.6 0.5 collective-permute-done.2.taken_ref
  8.1 0.2 shard_map.106
  8.3 0.0 copy-start.5
  8.3 1.0 copy-done.5
  9.3 0.0 copy-start.3
  9.3 0.0 copy-start.11
  9.3 0.0 copy-start.9
  9.3 0.0 copy-start.10
  9.3 0.0 copy-start.4
  9.3 0.0 copy-start.8
  9.4 7.3 %all-to-all-start = ((bf16[8,128,512]{2,1,0:T(8,128)(2,1)}), bf16[8,128,512]{2,1,0:T(8,128)(2,1)S(1)}, u32[]{:S(2)}, u32[]{:S(2)}) async-start(bf16[8,128,512]{2,1,0:T(8,128)(2,1)} %copy-done.5), calls=%async_computation | async-start | bytes 2097152 | tf_op jit(solution)/shard_map/all_to_all | solution.py:283
  16.7 0.0 copy-done.3
  16.7 0.1 collective-permute-start
  16.7 4.4 %collective-permute-start.1 = (bf16[512,768]{1,0:T(8,128)(2,1)S(1)}, bf16[512,768]{1,0:T(8,128)(2,1)}, u32[]{:S(2)}, u32[]{:S(2)}) collective-permute-start(bf16[512,768]{1,0:T(8,128)(2,1)S(1)} %copy-done.3), channel_id=1, source_target_pairs={{0,15},{1,0},{2,1},{3,2},{4,3},{5,4},{6,5},{7,6},{8,7},{9,8},{10,9... | collective-permute-start | bytes 2359304 | tf_op jit(solution)/shard_map/ppermute | solution.py:52
  21.2 0.0 copy-done.11
  21.2 0.1 copy.11.e_ref
  21.3 0.0 copy-done.9
  21.4 0.0 copy-done.10
  21.4 26.2 %collective-permute-done.l_ref = bf16[512,768]{1,0:T(8,128)(2,1)} collective-permute-done((bf16[512,768]{1,0:T(8,128)(2,1)S(1)}, bf16[512,768]{1,0:T(8,128)(2,1)}, u32[]{:S(2)}, u32[]{:S(2)}) %collective-permute-start) | collective-permute-done | bytes 786464 | tf_op jit(solution)/shard_map/ppermute | solution.py:52
  47.6 0.0 collective-permute-done.1.h_ref
  47.6 0.0 all-to-all-done.taken_ref
  47.6 0.0 copy-done.4
  47.6 0.0 copy-done.8
  47.6 3.7 %shard_map.107.refs_3_ = f32[512,768]{1,0:T(8,128)S(1)} custom-call(bf16[512,768]{1,0:T(8,128)(2,1)S(1)} %copy-done.3, bf16[512,768]{1,0:T(8,128)(2,1)} %collective-permute-done.l_ref, bf16[512,768]{1,0:T(8,128)(2,1)} %collective-permute-done.1.h_ref, bf16[512,768]{1,0:T(8,128)(2,1)S(1)} %copy-done.4, bf16[2,128,128]{2,1,0:T(8,128)(2,1)S(1)} %copy-done.8, ...), custom_call_target="tpu_custom_call" | custom-call | flops 235929600 | bytes 4718592 | tf_op jit(solution)/shard_map/pallas_call | solution.py:180
  51.3 0.0 copy-start.1
  51.3 0.1 shard_map.108
  51.5 32.5 %all_to_all.20.refs_0_ = bf16[8,128,512]{2,1,0:T(8,128)(2,1)S(1)} all-to-all(bf16[8,128,512]{2,1,0:T(8,128)(2,1)S(1)} %shard_map.108), channel_id=1, replica_groups={{0,2,4,6,8,10,12,14},{1,3,5,7,9,11,13,15},{16,18,20,22,24,26,28,30},{17..., dimensions={0} | all-to-all | bytes 2097152 | tf_op jit(solution)/shard_map/all_to_all | solution.py:290
  84.0 0.0 copy-start.12
  84.0 0.0 copy-start.13
  84.0 0.0 collective-permute-start.3
  84.0 2.7 %collective-permute-done.3.refs_1_ = bf16[8,128,512]{2,1,0:T(8,128)(2,1)S(1)} collective-permute-done((bf16[8,128,512]{2,1,0:T(8,128)(2,1)S(1)}, bf16[8,128,512]{2,1,0:T(8,128)(2,1)S(1)}, u32[]{:S(2)}, u32[]{:S(2)}) %collective-permute-start.3) | collective-permute-done | bytes 1048608 | tf_op jit(solution)/shard_map/ppermute | solution.py:52
  86.7 0.0 copy-done.1
  86.7 2.9 %shard_map.109 = (f32[512,768]{1,0:T(8,128)S(1)}, bf16[512,256]{1,0:T(8,128)(2,1)S(1)}) custom-call(bf16[8,128,512]{2,1,0:T(8,128)(2,1)S(1)} %all_to_all.20.refs_0_, bf16[8,128,512]{2,1,0:T(8,128)(2,1)S(1)} %collective-permute-done.3.refs_1_, bf16[2048,768]{1,0:T(8,128)(2,1)S(1)} %copy-done.1, f32[512,768]{1,0:T(8,128)S(1)} %shard_map.107.refs_3_, ...), custom_call_target="tpu_custom_call" | custom-call | flops 1811939328 | bytes 9437184 | tf_op jit(solution)/shard_map/pallas_call | solution.py:84
  89.5 13.6 %all_to_all.21.taken_ref = bf16[16,32,256]{2,1,0:T(8,128)(2,1)S(1)} all-to-all(bf16[16,32,256]{2,1,0:T(8,128)(2,1)S(1)} %bitcast.6), channel_id=1, replica_groups=mesh['pert'=2,'band'=16] {'band'}, dimensions={0} | all-to-all | bytes 524288 | tf_op jit(solution)/shard_map/all_to_all | solution.py:301
  103.1 0.8 shard_map.110
  103.9 3.5 %all-to-all-start.3 = ((bf16[16,32,256]{2,1,0:T(8,128)(2,1)}), bf16[16,32,256]{2,1,0:T(8,128)(2,1)S(1)}, u32[]{:S(2)}, u32[]{:S(2)}) async-start(bf16[16,32,256]{2,1,0:T(8,128)(2,1)} %shard_map.110), calls=%async_computation.3 | async-start | bytes 524288 | tf_op jit(solution)/shard_map/all_to_all | solution.py:303
  107.4 0.0 copy-done.12
  107.4 0.9 copy.12.refs_4_
  108.3 0.0 copy-done.13
  108.3 0.9 copy.13.refs_5_
  109.2 8.3 %all-to-all-done.3 = bf16[16,32,256]{2,1,0:T(8,128)(2,1)S(1)} async-done(((bf16[16,32,256]{2,1,0:T(8,128)(2,1)}), bf16[16,32,256]{2,1,0:T(8,128)(2,1)S(1)}, u32[]{:S(2)}, u32[]{:S(2)}) %all-to-all-start.3) | async-done | bytes 262176 | tf_op jit(solution)/shard_map/all_to_all | solution.py:303
  117.4 0.0 copy-start.6
  117.4 0.9 copy-done.6
  118.4 0.0 copy-start.7
  118.4 0.9 copy-done.7
  119.3 1.6 %shard_map.111 = (bf16[512,768]{1,0:T(8,128)(2,1)}, bf16[512,768]{1,0:T(8,128)(2,1)}) custom-call(bf16[512,256]{1,0:T(8,128)(2,1)S(1)} %bitcast.5, bf16[512,768]{1,0:T(8,128)(2,1)S(1)} %copy-done.4, f32[512,768]{1,0:T(8,128)S(1)} %get-tuple-element.15.refs_2_, bf16[512,768]{1,0:T(8,128)(2,1)S(1)} %copy-done.3, s32[512,1]{1,0:T(8,128)S(1)} %copy-done.6, ...), custom_call_target="tpu_custom_call" | custom-call | flops 201326592 | bytes 4984832 | tf_op jit(solution)/shard_map/pallas_call | solution.py:84
  (2 shorter events, 0.0 us)
Async XLA Ops:
  0.6 1.9 %copy-start = (bf16[2048,768]{1,0:T(8,128)(2,1)S(1)}, bf16[2048,768]{1,0:T(8,128)(2,1)}, u32[]{:S(2)}) copy-start(bf16[2048,768]{1,0:T(8,128)(2,1)} %refs_2_.1) | copy-start | bytes 9437188
  2.5 1.1 copy-start.2
  5.3 2.8 %collective-permute-start.2 = (bf16[256,2048]{1,0:T(8,128)(2,1)S(1)}, bf16[256,2048]{1,0:T(8,128)(2,1)S(1)}, u32[]{:S(2)}, u32[]{:S(2)}) collective-permute-start(bf16[256,2048]{1,0:T(8,128)(2,1)S(1)} %shard_map.105), channel_id=1, source_target_pairs={{0,1},{1,0},{2,3},{3,2},{4,5},{5,4},{6,7},{7,6},{8,9},{9,8},{10,11... | collective-permute-start | bytes 3145736 | tf_op jit(solution)/shard_map/ppermute | solution.py:52
  8.3 1.0 copy-start.5
  9.3 7.4 %copy-start.3 = (bf16[512,768]{1,0:T(8,128)(2,1)S(1)}, bf16[512,768]{1,0:T(8,128)(2,1)}, u32[]{:S(2)}) copy-start(bf16[512,768]{1,0:T(8,128)(2,1)} %refs_3_.1) | copy-start | bytes 2359300
  9.3 11.9 %copy-start.11 = (f32[512]{0:T(512)S(1)}, f32[512]{0:T(512)}, u32[]{:S(2)}) copy-start(f32[512]{0:T(512)} %param.14) | copy-start | bytes 6148
  9.3 12.0 %copy-start.9 = (f32[768]{0:T(1024)S(1)}, f32[768]{0:T(1024)}, u32[]{:S(2)}) copy-start(f32[768]{0:T(1024)} %param.12) | copy-start | bytes 9220
  9.3 12.0 %copy-start.10 = (f32[768]{0:T(1024)S(1)}, f32[768]{0:T(1024)}, u32[]{:S(2)}) copy-start(f32[768]{0:T(1024)} %param.13) | copy-start | bytes 9220
  9.3 38.2 %copy-start.4 = (bf16[512,768]{1,0:T(8,128)(2,1)S(1)}, bf16[512,768]{1,0:T(8,128)(2,1)}, u32[]{:S(2)}) copy-start(bf16[512,768]{1,0:T(8,128)(2,1)} %refs_1_.1) | copy-start | bytes 2359300
  9.3 38.2 %copy-start.8 = (bf16[2,128,128]{2,1,0:T(8,128)(2,1)S(1)}, bf16[2,128,128]{2,1,0:T(8,128)(2,1)}, u32[]{:S(2)}) copy-start(bf16[2,128,128]{2,1,0:T(8,128)(2,1)} %constant.2.clone.m_ref) | copy-start | bytes 196612
  9.4 38.2 %all-to-all-start = ((bf16[8,128,512]{2,1,0:T(8,128)(2,1)}), bf16[8,128,512]{2,1,0:T(8,128)(2,1)S(1)}, u32[]{:S(2)}, u32[]{:S(2)}) async-start(bf16[8,128,512]{2,1,0:T(8,128)(2,1)} %copy-done.5), calls=%async_computation | async-start | bytes 2097152 | tf_op jit(solution)/shard_map/all_to_all | solution.py:283
  16.7 30.9 %collective-permute-start = (bf16[512,768]{1,0:T(8,128)(2,1)S(1)}, bf16[512,768]{1,0:T(8,128)(2,1)}, u32[]{:S(2)}, u32[]{:S(2)}) collective-permute-start(bf16[512,768]{1,0:T(8,128)(2,1)S(1)} %copy-done.3), channel_id=1, source_target_pairs={{0,1},{1,2},{2,3},{3,4},{4,5},{5,6},{6,7},{7,8},{8,9},{9,10},{10,1... | collective-permute-start | bytes 2359304 | tf_op jit(solution)/shard_map/ppermute | solution.py:52
  16.7 30.8 %collective-permute-start.1 = (bf16[512,768]{1,0:T(8,128)(2,1)S(1)}, bf16[512,768]{1,0:T(8,128)(2,1)}, u32[]{:S(2)}, u32[]{:S(2)}) collective-permute-start(bf16[512,768]{1,0:T(8,128)(2,1)S(1)} %copy-done.3), channel_id=1, source_target_pairs={{0,15},{1,0},{2,1},{3,2},{4,3},{5,4},{6,5},{7,6},{8,7},{9,8},{10,9... | collective-permute-start | bytes 2359304 | tf_op jit(solution)/shard_map/ppermute | solution.py:52
  51.3 35.3 %copy-start.1 = (bf16[2048,768]{1,0:T(8,128)(2,1)S(1)}, bf16[2048,768]{1,0:T(8,128)(2,1)}, u32[]{:S(2)}) copy-start(bf16[2048,768]{1,0:T(8,128)(2,1)} %refs_2_.1) | copy-start | bytes 9437188
  84.0 23.4 %copy-start.12 = (s32[512]{0:T(512)S(1)}, s32[512]{0:T(512)}, u32[]{:S(2)}) copy-start(s32[512]{0:T(512)} %param.15) | copy-start | bytes 6148
  84.0 24.3 %copy-start.13 = (s32[512]{0:T(512)S(1)}, s32[512]{0:T(512)}, u32[]{:S(2)}) copy-start(s32[512]{0:T(512)} %param.16) | copy-start | bytes 6148
  84.0 2.7 %collective-permute-start.3 = (bf16[8,128,512]{2,1,0:T(8,128)(2,1)S(1)}, bf16[8,128,512]{2,1,0:T(8,128)(2,1)S(1)}, u32[]{:S(2)}, u32[]{:S(2)}) collective-permute-start(bf16[8,128,512]{2,1,0:T(8,128)(2,1)S(1)} %all_to_all.20.refs_0_), channel_id=1, source_target_pairs={{0,1},{1,0},{2,3},{3,2},{4,5},{5,4},{6,7},{7,6},{8,9},{9,8},{10,11... | collective-permute-start | bytes 3145736 | tf_op jit(solution)/shard_map/ppermute | solution.py:52
  103.9 13.5 %all-to-all-start.3 = ((bf16[16,32,256]{2,1,0:T(8,128)(2,1)}), bf16[16,32,256]{2,1,0:T(8,128)(2,1)S(1)}, u32[]{:S(2)}, u32[]{:S(2)}) async-start(bf16[16,32,256]{2,1,0:T(8,128)(2,1)} %shard_map.110), calls=%async_computation.3 | async-start | bytes 524288 | tf_op jit(solution)/shard_map/all_to_all | solution.py:303
  117.4 1.0 copy-start.6
  118.4 0.9 copy-start.7

commit v4 on v2

--- a/solution.py
+++ b/solution.py
@@ -125,27 +125,33 @@
     )(response, projectors)
 
 
-def split_body(received, level, along, *refs):
+def split_body(received, level, along, first, *refs):
     keep_ref, taken, (own_ref, *sends) = refs[0], refs[1 : 1 + received], refs[1 + received :]
     size, _ = level
     me = position(level)
-    width = own_ref.shape[along]
+    rows, width = own_ref.shape
     for step, out in enumerate((own_ref, *sends)):
-        at = pl.multiple_of(lax.rem(me + step, jnp.int32(size)) * width, width)
-        part = (pl.ds(at, width), slice(None)) if along == 0 else (slice(None), pl.ds(at, width))
+        place = lax.rem(me + step, jnp.int32(size))
+        if along == 0:
+            at = pl.multiple_of(place * rows, 16)
+            part = (pl.ds(at, rows), slice(None))
+            theirs = (pl.ds(pl.multiple_of(at + first, 16), rows), slice(None))
+        else:
+            part = (slice(None), pl.ds(pl.multiple_of(place * width, width), width))
+            theirs = (slice(first, first + rows), part[1])
         total = keep_ref[part]
         for ref in taken:
-            total = total + ref[part].astype(F32)
+            total = total + ref[theirs].astype(F32)
         out[...] = total.astype(out.dtype)
 
 
-def split(keep, taken, level, along):
+def split(keep, taken, level, along, first=0):
     size, _ = level
     shape = list(keep.shape)
     shape[along] //= size
     outs = [struct(shape, F32)] + [struct(shape, BF16)] * (size - 1)
     return local_call(
-        functools.partial(split_body, len(taken), level, along), outs, [keep, *taken]
+        functools.partial(split_body, len(taken), level, along, first), outs, [keep, *taken]
     )
 
 
@@ -182,58 +188,88 @@
     return local_call(functools.partial(place_body, level, along), struct(shape, BF16), parts)
 
 
-def local_body(depth, r_ref, l_ref, h_ref, o_ref, m_ref, pot_ref, v_ref, e_ref, out_ref):
+def local_body(depth, sizes, *refs):
+    r_ref, l_ref, o_ref, m_ref, pot_ref, v_ref, e_ref, first_ref, many_ref, out_ref, mask_ref = refs
     plane = GY * GZ
     reach = 6
-
-    def plane_at(j):
-        if j < 0:
-            ref, k = l_ref, j + reach
-        elif j < depth:
-            ref, k = r_ref, j
-        else:
-            ref, k = h_ref, j - depth
-        return ref[:, k * plane : (k + 1) * plane]
-
     for j in range(depth):
         cols = slice(j * plane, (j + 1) * plane)
-        low = plane_at(j)
-        centre = low.astype(F32)
+        low = r_ref[:, cols]
         total = jnp.dot(low, m_ref[0], preferred_element_type=F32)
         total = total + jnp.dot(low, m_ref[1], preferred_element_type=F32)
         for offset in range(1, 7):
-            pair = plane_at(j + offset).astype(F32) + plane_at(j - offset).astype(F32)
+            pair = 0.0
+            for k in (j - offset, j + offset):
+                if 0 <= k < depth:
+                    pair = pair + r_ref[:, k * plane : (k + 1) * plane].astype(F32)
+                elif k < 0:
+                    k = k + reach
+                    pair = pair + l_ref[:, k * plane : (k + 1) * plane].astype(F32)
             total = total + (KINETIC * COEFFS[offset]) * pair
-        total = total + (e_ref[...] - pot_ref[:, cols]) * centre
+        total = total + (e_ref[...] - pot_ref[:, cols]) * low.astype(F32)
         out_ref[:, cols] = total - v_ref[:, cols] * o_ref[:, cols].astype(F32)
-
-
-def local_part(response, low, high, orbitals, matrix, potential, perturbing, energies):
+    group_rows, width, blk, bands = sizes
+    start = jnp.clip(pl.program_id(0) * group_rows - REACH * blk, 0, bands - width)
+    block = (lax.broadcasted_iota(jnp.int32, mask_ref.shape, 1) + start) // blk
+    lowest = first_ref[...]
+    inside = (block >= lowest) & (block < lowest + many_ref[...])
+    mask_ref[...] = jnp.where(inside, 1.0, 0.0).astype(BF16)
+
+
+def local_part(response, low, orbitals, matrix, lines, columns, group_rows, width, blk):
     bands, cells = response.shape
     depth = cells // (GY * GZ)
-    tile = 128
-    out = struct((bands, cells), F32)
-    here = pl.BlockSpec((tile, cells), lambda i: (i, 0))
-    side = pl.BlockSpec((tile, low.shape[1]), lambda i: (i, 0))
+    outs = [struct((bands, cells), F32), struct((bands, width), BF16)]
+    here = pl.BlockSpec((group_rows, cells), lambda i: (i, 0))
+    side = pl.BlockSpec((group_rows, low.shape[1]), lambda i: (i, 0))
     line = pl.BlockSpec((1, cells), lambda i: (0, 0))
+    column = pl.BlockSpec((group_rows, 1), lambda i: (i, 0))
     return pl.pallas_call(
-        functools.partial(local_body, depth),
-        grid=(bands // tile,),
-        out_shape=out,
+        functools.partial(local_body, depth, (group_rows, width, blk, bands)),
+        grid=(bands // group_rows,),
+        out_shape=outs,
         in_specs=[
             here,
-            side,
             side,
             here,
             pl.BlockSpec(matrix.shape, lambda i: (0, 0, 0)),
             line,
             line,
-            pl.BlockSpec((tile, 1), lambda i: (i, 0)),
+            column,
+            column,
+            column,
         ],
+        out_specs=[here, pl.BlockSpec((group_rows, width), lambda i: (i, 0))],
+        compiler_params=params(),
+        cost_estimate=cost(2 * bands * cells * 300, low, low, low, *outs),
+    )(response, low, orbitals, matrix, *lines, *columns)
+
+
+def next_body(depth, h_ref, base_ref, out_ref):
+    plane = GY * GZ
+    for j in range(depth):
+        cols = slice(j * plane, (j + 1) * plane)
+        total = base_ref[:, cols]
+        for k in range(depth, j + 7):
+            at = k - depth
+            far = h_ref[:, at * plane : (at + 1) * plane].astype(F32)
+            total = total + (KINETIC * COEFFS[k - j]) * far
+        out_ref[:, cols] = total
+
+
+def add_next(base, high, group_rows):
+    bands, cells = base.shape
+    out = struct(base.shape, F32)
+    here = pl.BlockSpec((group_rows, cells), lambda i: (i, 0))
+    return pl.pallas_call(
+        functools.partial(next_body, cells // (GY * GZ)),
+        grid=(bands // group_rows,),
+        out_shape=out,
+        in_specs=[pl.BlockSpec((group_rows, high.shape[1]), lambda i: (i, 0)), here],
         out_specs=here,
         compiler_params=params(),
-        cost_estimate=cost(2 * bands * cells * 300, low, high, low, low, out),
-    )(response, low, high, orbitals, matrix, potential, perturbing, energies)
+        cost_estimate=cost(bands * cells * 14, high, base, out),
+    )(high, base)
 
 
 def first_orbital(group, group_rows, width, bands, blk):
@@ -292,7 +328,7 @@
 def project_body(core, across, group_rows, width, blk, *refs):
     size = across[0]
     blocks = refs[: 2 * size]
-    o_ref, u_ref, r_ref, first_ref, many_ref, updated_ref, residual_ref, w_ref = refs[2 * size :]
+    o_ref, u_ref, r_ref, mask_ref, updated_ref, residual_ref, w_ref = refs[2 * size :]
     bands = o_ref.shape[0]
     half = bands // 2
     c, x = position(core), position(across)
@@ -304,9 +340,7 @@
     for g in range(bands // group_rows):
         start = first_orbital(g, group_rows, width, bands, blk)
         mine = slice(g * group_rows, (g + 1) * group_rows)
-        block = (lax.broadcasted_iota(jnp.int32, (group_rows, width), 1) + start) // blk
-        lowest = first_ref[mine, :]
-        inside = (block >= lowest) & (block < lowest + many_ref[mine, :])
+        inside = mask_ref[mine, :].astype(F32) > 0.5
         weights = jnp.where(inside, w_ref[mine, :].astype(F32), 0.0).astype(BF16)
         residual = u_ref[mine, :] - jnp.dot(
             weights, o_ref[start : start + width, :], preferred_element_type=F32
@@ -330,13 +364,12 @@
     group_rows = GROUP_BLOCKS * blk
     width = (GROUP_BLOCKS + 2 * REACH) * blk
     half = bands // 2
-    rows_x = half // 2
+    step = 16 * across[0]
+    rows_x = (2 * half // 3 + step // 2) // step * step
     rows_z = half - rows_x
     matrix = jnp.asarray(plane_matrix())
-    potential, perturbing = potential[None, :], perturbing[None, :]
-    energies, window_start, block_count = (
-        a[:, None] for a in (energies, window_start, block_count)
-    )
+    lines = (potential[None, :], perturbing[None, :])
+    columns = tuple(a[:, None] for a in (energies, window_start, block_count))
 
     def to(array, level):
         return [shifted(array, count, level, k) for k in range(1, level[0])]
@@ -345,36 +378,41 @@
         return [shifted(part, count, level, k + 1) for k, part in enumerate(parts)]
 
     low = shifted(response[:, local_cells - halo :], count, ring, 1)
-    high = shifted(response[:, :halo], count, ring, -1)
-
-    (sent_z,) = partial_intersections(response, projectors, core, [(True, rows_x, rows_z)])
-    sent_z = shifted(sent_z, count, core, 1)
-    (sent_x,) = partial_intersections(response, projectors, core, [(True, 0, rows_x)])
-    sent_x = shifted(sent_x, count, core, 1)
+
+    (sent,) = partial_intersections(response, projectors, core, [(True, 0, half)])
+    sent = shifted(sent, count, core, 1)
     keep_z, keep_x = partial_intersections(
         response, projectors, core, [(False, rows_x, rows_z), (False, 0, rows_x)]
     )
-    keep_z, *parts = split(keep_z, [sent_z], along, 1)
-    taken_z = parts_to(parts, along)
-    keep_x, *parts = split(keep_x, [sent_x], across, 0)
-    taken_x = parts_to(parts, across)
-    keep_x, *parts = split(keep_x, taken_x, along, 1)
-    taken_x = parts_to(parts, along)
-    keep_z, *parts = split(keep_z, taken_z, across, 0)
-    taken_z = parts_to(parts, across)
+    keep_z, *parts_z = split(keep_z, [sent], along, 1, rows_x)
+    keep_x, *parts_x = split(keep_x, [sent], across, 0, 0)
+    taken_z, taken_x = lax.optimization_barrier(
+        (parts_to(parts_z, along), parts_to(parts_x, across))
+    )
+    keep_x, *parts_x = split(keep_x, taken_x, along, 1)
+    keep_z, *parts_z = split(keep_z, taken_z, across, 0)
+    taken_x, taken_z = lax.optimization_barrier(
+        (parts_to(parts_x, along), parts_to(parts_z, across))
+    )
     share_z = finish(keep_z, taken_z, ace_scale)
     share_x = finish(keep_x, taken_x, ace_scale)
 
-    block_z = place([share_z, *to(share_z, across)], across, 0)
-    block_x = place([share_x, *to(share_x, along)], along, 1)
-    base = local_part(
-        response, low, high, orbitals, matrix, potential, perturbing, energies
-    )
+    head, low, _ = lax.optimization_barrier((response[:, :halo], low, share_z))
+    high = shifted(head, count, ring, -1)
+    base, mask = local_part(
+        response, low, orbitals, matrix, lines, columns, group_rows, width, blk
+    )
+    pieces_x, pieces_z, base = lax.optimization_barrier(
+        ([share_x, *to(share_x, along)], [share_z, *to(share_z, across)], base)
+    )
+    block_x = place(pieces_x, along, 1)
+    block_z = place(pieces_z, across, 0)
     blocks_x = [block_x, *to(block_x, across)]
     block_z = place([block_z, *to(block_z, along)], along, 1)
     blocks = [*blocks_x, block_z]
     blocks += [shifted(block, count, core, 1) for block in blocks]
 
+    base = add_next(base, high, group_rows)
     unprojected, send, keep = local_call(
         functools.partial(apply_body, core, across, rows_x, group_rows, width, blk),
         [
@@ -395,7 +433,7 @@
     return local_call(
         functools.partial(project_body, core, across, group_rows, width, blk),
         (out, out),
-        [*weights, orbitals, unprojected, response, window_start, block_count],
+        [*weights, orbitals, unprojected, response, mask],
         flops=2 * bands * width * local_cells,
         scratch=[pltpu.VMEM((bands, width), BF16)],
     )

time: 111 us -> 97.1 us (0.87)
  waiting for transfers between devices: 56.9 us -> 41.8 us
  local copies, waits for them, and re-layouts: 6.09 us -> 3.2 us
  starting transfers between devices: 30.3 us -> 33 us
  Pallas kernels: 16.2 us -> 17.7 us
    ppermute x31 -> x30, waiting for transfers between devices: 56.9 us -> 41.8 us  [shifted(): return lax.ppermute(array, 'band', pairs)]
    unnamed x26 -> x18, local copies, waits for them, and re-layouts: 5.64 us -> 2.76 us
    ppermute x31 -> x30, starting transfers between devices: 30.3 us -> 33 us  [shifted(): return lax.ppermute(array, 'band', pairs)]
    pallas_call x3 -> x2, Pallas kernels: 6.01 us -> 6.63 us  [partial_intersections(): pl.pallas_call(functools.partial(partial_body, core, bands, parts), grid=...]
    pallas_call x1 -> x2, Pallas kernels: 3.66 us -> 3.95 us  [the longest x1 3.4 us: local_part(): pl.pallas_call(functools.partial(local_body, depth, (group_rows, width, b...]
  transfers between devices with their start and end apart: 31 -> 30, of which waited for: 16 -> 18; matrix products, arithmetic and copies ran while one was open for 0% -> 0% of each run, Pallas kernels for 8% -> 9%
where the time goes in v4:
time: 97.1 us; the launch traced here: 96.7 us
  waiting for transfers between devices  41.8 us (43%)
  starting transfers between devices  33 us (34%)
  Pallas kernels  17.7 us (18%)
  local copies, waits for them, and re-layouts  3.2 us (3%)
    ppermute x30, waiting for transfers between devices, shifted(): return lax.ppermute(array, 'band', pairs)  41.8 us
    ppermute x30, starting transfers between devices, shifted(): return lax.ppermute(array, 'band', pairs)  33 us
    pallas_call x14, Pallas kernels, local_call(): pl.pallas_call(body, out_shape=outs, in_specs=[whole() for _ in args], ou...  7.1 us
    pallas_call x2, Pallas kernels, partial_intersections(): pl.pallas_call(functools.partial(partial_body, core, bands, parts), grid=...  6.63 us
    pallas_call x1, Pallas kernels, local_part(): pl.pallas_call(functools.partial(local_body, depth, (group_rows, width, b...  3.4 us
    unnamed x18, local copies, waits for them, and re-layouts  2.76 us
  transfers between devices with their start and end apart: 30, of which 18 were waited for; matrix products, arithmetic and copies ran while one was open for 0% of the time, Pallas kernels for 9%

profile of v4, /device:TPU:0, one launch (start us, length us, event | category | flops | bytes accessed | tf_op | source)
XLA Modules:
  0.0 96.7 jit_solution(6295764798375408624)
XLA Ops:
  0.6 1.9 %copy-done = bf16[2048,768]{1,0:T(8,128)(2,1)S(1)} copy-done((bf16[2048,768]{1,0:T(8,128)(2,1)S(1)}, bf16[2048,768]{1,0:T(8,128)(2,1)}, u32[]{:S(2)}) %copy-start) | copy-done | bytes 3145752
  2.5 2.8 %shard_map.105 = bf16[256,2048]{1,0:T(8,128)(2,1)S(1)} custom-call(bf16[512,768]{1,0:T(8,128)(2,1)} %refs_6_.3, bf16[2048,768]{1,0:T(8,128)(2,1)S(1)} %copy-done), custom_call_target="tpu_custom_call" | custom-call | flops 805306368 | bytes 4194304 | tf_op jit(solution)/shard_map/pallas_call | solution.py:114
  5.3 0.5 collective-permute-start
  5.9 0.1 collective-permute-start.13
  5.9 3.8 %shard_map.104 = (f32[96,2048]{1,0:T(8,128)S(1)}, f32[160,2048]{1,0:T(8,128)S(1)}) custom-call(bf16[512,768]{1,0:T(8,128)(2,1)} %refs_6_.3, bf16[2048,768]{1,0:T(8,128)(2,1)S(1)} %copy-done), custom_call_target="tpu_custom_call" | custom-call | flops 805306368 | bytes 5242880 | tf_op jit(solution)/shard_map/pallas_call | solution.py:114
  9.8 0.1 shard_map.106
  9.9 3.0 %collective-permute-start.4 = (bf16[80,2048]{1,0:T(8,128)(2,1)S(1)}, bf16[80,2048]{1,0:T(8,128)(2,1)S(1)}, u32[]{:S(2)}, u32[]{:S(2)}) collective-permute-start(bf16[80,2048]{1,0:T(8,128)(2,1)S(1)} %get-tuple-element.48), channel_id=1, source_target_pairs={{0,2},{1,3},{2,0},{3,1},{4,6},{5,7},{6,4},{7,5},{8,10},{9,11},{10,... | collective-permute-start | bytes 983048 | tf_op jit(solution)/shard_map/ppermute | solution.py:52
  12.9 0.1 shard_map.107
  13.0 0.0 copy-start.7
  13.0 0.0 copy-start.5
  13.0 0.0 copy-start.2
  13.1 1.6 %collective-permute-start.1 = (bf16[96,512]{1,0:T(8,128)(2,1)S(1)}, bf16[96,512]{1,0:T(8,128)(2,1)S(1)}, u32[]{:S(2)}, u32[]{:S(2)}) collective-permute-start(bf16[96,512]{1,0:T(8,128)(2,1)S(1)} %get-tuple-element.45), channel_id=1, source_target_pairs={{0,4},{1,5},{2,6},{3,7},{4,8},{5,9},{6,10},{7,11},{8,12},{9,13},{1... | collective-permute-start | bytes 294920 | tf_op jit(solution)/shard_map/ppermute | solution.py:52
  14.7 2.6 %collective-permute-start.2 = (bf16[96,512]{1,0:T(8,128)(2,1)S(1)}, bf16[96,512]{1,0:T(8,128)(2,1)S(1)}, u32[]{:S(2)}, u32[]{:S(2)}) collective-permute-start(bf16[96,512]{1,0:T(8,128)(2,1)S(1)} %get-tuple-element.46), channel_id=1, source_target_pairs={{0,8},{1,9},{2,10},{3,11},{4,12},{5,13},{6,14},{7,15},{8,0},{9,1},... | collective-permute-start | bytes 294920 | tf_op jit(solution)/shard_map/ppermute | solution.py:52
  17.3 1.3 %collective-permute-start.3 = (bf16[96,512]{1,0:T(8,128)(2,1)S(1)}, bf16[96,512]{1,0:T(8,128)(2,1)S(1)}, u32[]{:S(2)}, u32[]{:S(2)}) collective-permute-start(bf16[96,512]{1,0:T(8,128)(2,1)S(1)} %get-tuple-element.47), channel_id=1, source_target_pairs={{0,12},{1,13},{2,14},{3,15},{4,0},{5,1},{6,2},{7,3},{8,4},{9,5},{1... | collective-permute-start | bytes 294920 | tf_op jit(solution)/shard_map/ppermute | solution.py:52
  18.6 2.2 %collective-permute-done.1.refs_1_ = bf16[96,512]{1,0:T(8,128)(2,1)S(1)} collective-permute-done((bf16[96,512]{1,0:T(8,128)(2,1)S(1)}, bf16[96,512]{1,0:T(8,128)(2,1)S(1)}, u32[]{:S(2)}, u32[]{:S(2)}) %collective-permute-start.1) | collective-permute-done | bytes 98336 | tf_op jit(solution)/shard_map/ppermute | solution.py:52
  20.8 4.1 %collective-permute-done.2.refs_2_ = bf16[96,512]{1,0:T(8,128)(2,1)S(1)} collective-permute-done((bf16[96,512]{1,0:T(8,128)(2,1)S(1)}, bf16[96,512]{1,0:T(8,128)(2,1)S(1)}, u32[]{:S(2)}, u32[]{:S(2)}) %collective-permute-start.2) | collective-permute-done | bytes 98336 | tf_op jit(solution)/shard_map/ppermute | solution.py:52
  24.8 3.5 %collective-permute-done.4.refs_1_ = bf16[80,2048]{1,0:T(8,128)(2,1)S(1)} collective-permute-done((bf16[80,2048]{1,0:T(8,128)(2,1)S(1)}, bf16[80,2048]{1,0:T(8,128)(2,1)S(1)}, u32[]{:S(2)}, u32[]{:S(2)}) %collective-permute-start.4) | collective-permute-done | bytes 327712 | tf_op jit(solution)/shard_map/ppermute | solution.py:52
  28.3 0.1 shard_map.108
  28.4 0.1 collective-permute-start.5
  28.5 2.3 %collective-permute-start.6 = (bf16[80,512]{1,0:T(8,128)(2,1)S(1)}, bf16[80,512]{1,0:T(8,128)(2,1)S(1)}, u32[]{:S(2)}, u32[]{:S(2)}) collective-permute-start(bf16[80,512]{1,0:T(8,128)(2,1)S(1)} %get-tuple-element.52), channel_id=1, source_target_pairs={{0,8},{1,9},{2,10},{3,11},{4,12},{5,13},{6,14},{7,15},{8,0},{9,1},... | collective-permute-start | bytes 245768 | tf_op jit(solution)/shard_map/ppermute | solution.py:52
  30.7 1.5 %collective-permute-start.7 = (bf16[80,512]{1,0:T(8,128)(2,1)S(1)}, bf16[80,512]{1,0:T(8,128)(2,1)S(1)}, u32[]{:S(2)}, u32[]{:S(2)}) collective-permute-start(bf16[80,512]{1,0:T(8,128)(2,1)S(1)} %get-tuple-element.53), channel_id=1, source_target_pairs={{0,12},{1,13},{2,14},{3,15},{4,0},{5,1},{6,2},{7,3},{8,4},{9,5},{1... | collective-permute-start | bytes 245768 | tf_op jit(solution)/shard_map/ppermute | solution.py:52
  32.3 1.3 %collective-permute-start.8 = (bf16[48,512]{1,0:T(8,128)(2,1)S(1)}, bf16[48,512]{1,0:T(8,128)(2,1)S(1)}, u32[]{:S(2)}, u32[]{:S(2)}) collective-permute-start(bf16[48,512]{1,0:T(8,128)(2,1)S(1)} %get-tuple-element.58), channel_id=1, source_target_pairs={{0,2},{1,3},{2,0},{3,1},{4,6},{5,7},{6,4},{7,5},{8,10},{9,11},{10,... | collective-permute-start | bytes 147464 | tf_op jit(solution)/shard_map/ppermute | solution.py:52
  33.6 2.9 %collective-permute-done.8.refs_0_ = bf16[48,512]{1,0:T(8,128)(2,1)S(1)} collective-permute-done((bf16[48,512]{1,0:T(8,128)(2,1)S(1)}, bf16[48,512]{1,0:T(8,128)(2,1)S(1)}, u32[]{:S(2)}, u32[]{:S(2)}) %collective-permute-start.8) | collective-permute-done | bytes 49184 | tf_op jit(solution)/shard_map/ppermute | solution.py:52
  36.5 1.7 %collective-permute-done.6.refs_1_ = bf16[80,512]{1,0:T(8,128)(2,1)S(1)} collective-permute-done((bf16[80,512]{1,0:T(8,128)(2,1)S(1)}, bf16[80,512]{1,0:T(8,128)(2,1)S(1)}, u32[]{:S(2)}, u32[]{:S(2)}) %collective-permute-start.6) | collective-permute-done | bytes 81952 | tf_op jit(solution)/shard_map/ppermute | solution.py:52
  38.3 1.1 %collective-permute-start.21 = (bf16[512,768]{1,0:T(8,128)(2,1)}, bf16[512,768]{1,0:T(8,128)(2,1)S(1)}, u32[]{:S(2)}, u32[]{:S(2)}) collective-permute-start(bf16[512,768]{1,0:T(8,128)(2,1)} %refs_6_.3), channel_id=1, source_target_pairs={{0,15},{1,0},{2,1},{3,2},{4,3},{5,4},{6,5},{7,6},{8,7},{9,8},{10,9... | collective-permute-start | bytes 2359304 | tf_op jit(solution)/shard_map/ppermute | solution.py:52
  39.4 1.8 %collective-permute-start.10 = (bf16[80,512]{1,0:T(8,128)(2,1)S(1)}, bf16[80,512]{1,0:T(8,128)(2,1)S(1)}, u32[]{:S(2)}, u32[]{:S(2)}) collective-permute-start(bf16[80,512]{1,0:T(8,128)(2,1)S(1)} %shard_map.110.refs_0_), channel_id=1, source_target_pairs={{0,8},{1,9},{2,10},{3,11},{4,12},{5,13},{6,14},{7,15},{8,0},{9,1},... | collective-permute-start | bytes 245768 | tf_op jit(solution)/shard_map/ppermute | solution.py:52
  41.3 1.0 %collective-permute-start.11 = (bf16[80,512]{1,0:T(8,128)(2,1)S(1)}, bf16[80,512]{1,0:T(8,128)(2,1)S(1)}, u32[]{:S(2)}, u32[]{:S(2)}) collective-permute-start(bf16[80,512]{1,0:T(8,128)(2,1)S(1)} %shard_map.110.refs_0_), channel_id=1, source_target_pairs={{0,12},{1,13},{2,14},{3,15},{4,0},{5,1},{6,2},{7,3},{8,4},{9,5},{1... | collective-permute-start | bytes 245768 | tf_op jit(solution)/shard_map/ppermute | solution.py:52
  42.3 1.0 %collective-permute-start.9 = (bf16[80,512]{1,0:T(8,128)(2,1)S(1)}, bf16[80,512]{1,0:T(8,128)(2,1)S(1)}, u32[]{:S(2)}, u32[]{:S(2)}) collective-permute-start(bf16[80,512]{1,0:T(8,128)(2,1)S(1)} %shard_map.110.refs_0_), channel_id=1, source_target_pairs={{0,4},{1,5},{2,6},{3,7},{4,8},{5,9},{6,10},{7,11},{8,12},{9,13},{1... | collective-permute-start | bytes 245768 | tf_op jit(solution)/shard_map/ppermute | solution.py:52
  43.3 0.1 copy.11.refs_6_
  43.5 0.1 copy.12.refs_7_
  43.6 0.1 copy.13.refs_8_
  43.8 0.0 copy-start.3
  43.8 0.8 copy-done.3
  44.7 3.4 %shard_map.112 = (f32[512,768]{1,0:T(8,128)S(1)}, bf16[512,256]{1,0:T(8,128)(2,1)S(1)}) custom-call(bf16[512,768]{1,0:T(8,128)(2,1)} %refs_6_.3, bf16[512,768]{1,0:T(8,128)(2,1)S(1)} %collective-permute-done.13.refs_1_, bf16[512,768]{1,0:T(8,128)(2,1)S(1)} %copy-done.2, bf16[2,128,128]{2,1,0:T(8,128)(2,1)S(1)} %copy-done.3, ...), custom_call_target="tpu_custom_call" | custom-call | flops 235929600 | bytes 4194304 | tf_op jit(solution)/shard_map/pallas_call | solution.py:227
  48.1 1.7 %collective-permute-done.12.refs_1_ = bf16[48,512]{1,0:T(8,128)(2,1)} collective-permute-done((bf16[48,512]{1,0:T(8,128)(2,1)S(1)}, bf16[48,512]{1,0:T(8,128)(2,1)}, u32[]{:S(2)}, u32[]{:S(2)}) %collective-permute-start.12) | collective-permute-done | bytes 49184 | tf_op jit(solution)/shard_map/ppermute | solution.py:52
  49.8 7.2 %collective-permute-done.10.refs_2_ = bf16[80,512]{1,0:T(8,128)(2,1)S(1)} collective-permute-done((bf16[80,512]{1,0:T(8,128)(2,1)S(1)}, bf16[80,512]{1,0:T(8,128)(2,1)S(1)}, u32[]{:S(2)}, u32[]{:S(2)}) %collective-permute-start.10) | collective-permute-done | bytes 81952 | tf_op jit(solution)/shard_map/ppermute | solution.py:52
  57.0 0.1 collective-permute-start.14
  57.1 0.8 shard_map.114.refs_0_
  57.9 1.5 %collective-permute-start.15 = (bf16[96,512]{1,0:T(8,128)(2,1)S(1)}, bf16[96,512]{1,0:T(8,128)(2,1)S(1)}, u32[]{:S(2)}, u32[]{:S(2)}) collective-permute-start(bf16[96,512]{1,0:T(8,128)(2,1)S(1)} %shard_map.114.refs_0_), channel_id=1, source_target_pairs={{0,4},{1,5},{2,6},{3,7},{4,8},{5,9},{6,10},{7,11},{8,12},{9,13},{1... | collective-permute-start | bytes 294920 | tf_op jit(solution)/shard_map/ppermute | solution.py:52
  59.4 0.6 collective-permute-start.16
  60.1 2.4 %collective-permute-start.17 = (bf16[96,512]{1,0:T(8,128)(2,1)S(1)}, bf16[96,512]{1,0:T(8,128)(2,1)S(1)}, u32[]{:S(2)}, u32[]{:S(2)}) collective-permute-start(bf16[96,512]{1,0:T(8,128)(2,1)S(1)} %shard_map.114.refs_0_), channel_id=1, source_target_pairs={{0,12},{1,13},{2,14},{3,15},{4,0},{5,1},{6,2},{7,3},{8,4},{9,5},{1... | collective-permute-start | bytes 294920 | tf_op jit(solution)/shard_map/ppermute | solution.py:52
  62.5 3.0 %collective-permute-done.15.refs_1_ = bf16[96,512]{1,0:T(8,128)(2,1)S(1)} collective-permute-done((bf16[96,512]{1,0:T(8,128)(2,1)S(1)}, bf16[96,512]{1,0:T(8,128)(2,1)S(1)}, u32[]{:S(2)}, u32[]{:S(2)}) %collective-permute-start.15) | collective-permute-done | bytes 98336 | tf_op jit(solution)/shard_map/ppermute | solution.py:52
  65.5 2.3 %collective-permute-done.16.refs_2_ = bf16[96,512]{1,0:T(8,128)(2,1)S(1)} collective-permute-done((bf16[96,512]{1,0:T(8,128)(2,1)S(1)}, bf16[96,512]{1,0:T(8,128)(2,1)S(1)}, u32[]{:S(2)}, u32[]{:S(2)}) %collective-permute-start.16) | collective-permute-done | bytes 98336 | tf_op jit(solution)/shard_map/ppermute | solution.py:52
  67.8 0.1 collective-permute-start.20
  67.9 0.5 collective-permute-start.18
  68.4 0.1 collective-permute-start.19
  68.5 0.5 shard_map.116.refs_7_
  69.0 1.0 %collective-permute-done.18.refs_3_ = bf16[80,2048]{1,0:T(8,128)(2,1)S(1)} collective-permute-done((bf16[80,2048]{1,0:T(8,128)(2,1)S(1)}, bf16[80,2048]{1,0:T(8,128)(2,1)S(1)}, u32[]{:S(2)}, u32[]{:S(2)}) %collective-permute-start.18) | collective-permute-done | bytes 327712 | tf_op jit(solution)/shard_map/ppermute | solution.py:52
  70.1 0.5 collective-permute-done.19.refs_4_
  70.5 3.0 %shard_map.117 = (f32[512,768]{1,0:T(8,128)S(1)}, bf16[256,256]{1,0:T(8,128)(2,1)S(1)}, f32[256,256]{1,0:T(8,128)S(1)}) custom-call(bf16[80,2048]{1,0:T(8,128)(2,1)S(1)} %shard_map.113.refs_0_, bf16[80,2048]{1,0:T(8,128)(2,1)S(1)} %collective-permute-done.14.refs_1_, bf16[96,2048]{1,0:T(8,128)(2,1)S(1)} %shard_map.115.refs_2_, ...), custom_call_target="tpu_custom_call" | custom-call | flops 1811939328 | bytes 9568256 | tf_op jit(solution)/shard_map/pallas_call | solution.py:84
  73.5 0.2 collective-permute-start.22
  73.7 1.2 %collective-permute-done.22.refs_1_ = bf16[256,256]{1,0:T(8,128)(2,1)S(1)} collective-permute-done((bf16[256,256]{1,0:T(8,128)(2,1)S(1)}, bf16[256,256]{1,0:T(8,128)(2,1)S(1)}, u32[]{:S(2)}, u32[]{:S(2)}) %collective-permute-start.22) | collective-permute-done | bytes 131104 | tf_op jit(solution)/shard_map/ppermute | solution.py:52
  75.0 1.8 %collective-permute-start.23 = (bf16[128,256]{1,0:T(8,128)(2,1)S(1)}, bf16[128,256]{1,0:T(8,128)(2,1)S(1)}, u32[]{:S(2)}, u32[]{:S(2)}) collective-permute-start(bf16[128,256]{1,0:T(8,128)(2,1)S(1)} %get-tuple-element.77), channel_id=1, source_target_pairs={{0,2},{1,3},{2,0},{3,1},{4,6},{5,7},{6,4},{7,5},{8,10},{9,11},{10,... | collective-permute-start | bytes 196616 | tf_op jit(solution)/shard_map/ppermute | solution.py:52
  76.8 2.5 %collective-permute-done.23.refs_0_ = bf16[128,256]{1,0:T(8,128)(2,1)S(1)} collective-permute-done((bf16[128,256]{1,0:T(8,128)(2,1)S(1)}, bf16[128,256]{1,0:T(8,128)(2,1)S(1)}, u32[]{:S(2)}, u32[]{:S(2)}) %collective-permute-start.23) | collective-permute-done | bytes 65568 | tf_op jit(solution)/shard_map/ppermute | solution.py:52
  79.3 1.7 %collective-permute-start.24 = (bf16[128,256]{1,0:T(8,128)(2,1)S(1)}, bf16[128,256]{1,0:T(8,128)(2,1)S(1)}, u32[]{:S(2)}, u32[]{:S(2)}) collective-permute-start(bf16[128,256]{1,0:T(8,128)(2,1)S(1)} %get-tuple-element.79), channel_id=1, source_target_pairs={{0,4},{1,5},{2,6},{3,7},{4,8},{5,9},{6,10},{7,11},{8,12},{9,13},{1... | collective-permute-start | bytes 196616 | tf_op jit(solution)/shard_map/ppermute | solution.py:52
  81.0 2.7 %collective-permute-start.25 = (bf16[128,256]{1,0:T(8,128)(2,1)S(1)}, bf16[128,256]{1,0:T(8,128)(2,1)S(1)}, u32[]{:S(2)}, u32[]{:S(2)}) collective-permute-start(bf16[128,256]{1,0:T(8,128)(2,1)S(1)} %get-tuple-element.79), channel_id=1, source_target_pairs={{0,8},{1,9},{2,10},{3,11},{4,12},{5,13},{6,14},{7,15},{8,0},{9,1},... | collective-permute-start | bytes 196616 | tf_op jit(solution)/shard_map/ppermute | solution.py:52
  83.7 0.3 collective-permute-start.26
  84.0 1.9 %collective-permute-done.24.refs_0_ = bf16[128,256]{1,0:T(8,128)(2,1)S(1)} collective-permute-done((bf16[128,256]{1,0:T(8,128)(2,1)S(1)}, bf16[128,256]{1,0:T(8,128)(2,1)S(1)}, u32[]{:S(2)}, u32[]{:S(2)}) %collective-permute-start.24) | collective-permute-done | bytes 65568 | tf_op jit(solution)/shard_map/ppermute | solution.py:52
  85.9 2.1 %collective-permute-done.25.refs_1_ = bf16[128,256]{1,0:T(8,128)(2,1)S(1)} collective-permute-done((bf16[128,256]{1,0:T(8,128)(2,1)S(1)}, bf16[128,256]{1,0:T(8,128)(2,1)S(1)}, u32[]{:S(2)}, u32[]{:S(2)}) %collective-permute-start.25) | collective-permute-done | bytes 65568 | tf_op jit(solution)/shard_map/ppermute | solution.py:52
  88.0 0.3 collective-permute-done.26.refs_2_
  88.3 1.8 %collective-permute-start.27 = (bf16[128,256]{1,0:T(8,128)(2,1)S(1)}, bf16[128,256]{1,0:T(8,128)(2,1)S(1)}, u32[]{:S(2)}, u32[]{:S(2)}) collective-permute-start(bf16[128,256]{1,0:T(8,128)(2,1)S(1)} %shard_map.120.refs_0_), channel_id=1, source_target_pairs={{0,2},{1,3},{2,0},{3,1},{4,6},{5,7},{6,4},{7,5},{8,10},{9,11},{10,... | collective-permute-start | bytes 196616 | tf_op jit(solution)/shard_map/ppermute | solution.py:52
  90.1 2.5 %collective-permute-done.27.refs_1_ = bf16[128,256]{1,0:T(8,128)(2,1)S(1)} collective-permute-done((bf16[128,256]{1,0:T(8,128)(2,1)S(1)}, bf16[128,256]{1,0:T(8,128)(2,1)S(1)}, u32[]{:S(2)}, u32[]{:S(2)}) %collective-permute-start.27) | collective-permute-done | bytes 65568 | tf_op jit(solution)/shard_map/ppermute | solution.py:52
  92.7 1.2 %collective-permute-done.29.refs_3_ = bf16[128,256]{1,0:T(8,128)(2,1)S(1)} collective-permute-done((bf16[128,256]{1,0:T(8,128)(2,1)S(1)}, bf16[128,256]{1,0:T(8,128)(2,1)S(1)}, u32[]{:S(2)}, u32[]{:S(2)}) %collective-permute-start.29) | collective-permute-done | bytes 65568 | tf_op jit(solution)/shard_map/ppermute | solution.py:52
  93.9 2.7 %shard_map.121 = (bf16[512,768]{1,0:T(8,128)(2,1)}, bf16[512,768]{1,0:T(8,128)(2,1)}) custom-call(bf16[128,256]{1,0:T(8,128)(2,1)S(1)} %shard_map.120.refs_0_, bf16[128,256]{1,0:T(8,128)(2,1)S(1)} %collective-permute-done.27.refs_1_, bf16[128,256]{1,0:T(8,128)(2,1)S(1)} %collective-permute-done.28.refs_2_, ...), custom_call_target="tpu_custom_call" | custom-call | flops 201326592 | bytes 5242880 | tf_op jit(solution)/shard_map/pallas_call | solution.py:84
  (37 shorter events, 0.3 us)
Async XLA Ops:
  0.6 1.9 %copy-start = (bf16[2048,768]{1,0:T(8,128)(2,1)S(1)}, bf16[2048,768]{1,0:T(8,128)(2,1)}, u32[]{:S(2)}) copy-start(bf16[2048,768]{1,0:T(8,128)(2,1)} %refs_6_.2) | copy-start | bytes 9437188
  5.3 4.4 %collective-permute-start = (bf16[256,2048]{1,0:T(8,128)(2,1)S(1)}, bf16[256,2048]{1,0:T(8,128)(2,1)S(1)}, u32[]{:S(2)}, u32[]{:S(2)}) collective-permute-start(bf16[256,2048]{1,0:T(8,128)(2,1)S(1)} %shard_map.105), channel_id=1, source_target_pairs={{0,1},{1,0},{2,3},{3,2},{4,5},{5,4},{6,7},{7,6},{8,9},{9,8},{10,11... | collective-permute-start | bytes 3145736 | tf_op jit(solution)/shard_map/ppermute | solution.py:52
  5.9 32.4 %collective-permute-start.13 = (bf16[512,768]{1,0:T(8,128)(2,1)}, bf16[512,768]{1,0:T(8,128)(2,1)S(1)}, u32[]{:S(2)}, u32[]{:S(2)}) collective-permute-start(bf16[512,768]{1,0:T(8,128)(2,1)} %refs_6_.3), channel_id=1, source_target_pairs={{0,1},{1,2},{2,3},{3,4},{4,5},{5,6},{6,7},{7,8},{8,9},{9,10},{10,1... | collective-permute-start | bytes 2359304 | tf_op jit(solution)/shard_map/ppermute | solution.py:52
  9.9 18.4 %collective-permute-start.4 = (bf16[80,2048]{1,0:T(8,128)(2,1)S(1)}, bf16[80,2048]{1,0:T(8,128)(2,1)S(1)}, u32[]{:S(2)}, u32[]{:S(2)}) collective-permute-start(bf16[80,2048]{1,0:T(8,128)(2,1)S(1)} %get-tuple-element.48), channel_id=1, source_target_pairs={{0,2},{1,3},{2,0},{3,1},{4,6},{5,7},{6,4},{7,5},{8,10},{9,11},{10,... | collective-permute-start | bytes 983048 | tf_op jit(solution)/shard_map/ppermute | solution.py:52
  12.9 30.4 %copy-start.6 = (f32[512]{0:T(512)S(1)}, f32[512]{0:T(512)}, u32[]{:S(2)}) copy-start(f32[512]{0:T(512)} %param.14) | copy-start | bytes 6148
  13.0 30.5 %copy-start.7 = (s32[512]{0:T(512)S(1)}, s32[512]{0:T(512)}, u32[]{:S(2)}) copy-start(s32[512]{0:T(512)} %param.15) | copy-start | bytes 6148
  13.0 30.6 %copy-start.8 = (s32[512]{0:T(512)S(1)}, s32[512]{0:T(512)}, u32[]{:S(2)}) copy-start(s32[512]{0:T(512)} %param.16) | copy-start | bytes 6148
  13.0 30.8 %copy-start.4 = (f32[768]{0:T(1024)S(1)}, f32[768]{0:T(1024)}, u32[]{:S(2)}) copy-start(f32[768]{0:T(1024)} %param.12) | copy-start | bytes 9220
  13.0 30.8 %copy-start.5 = (f32[768]{0:T(1024)S(1)}, f32[768]{0:T(1024)}, u32[]{:S(2)}) copy-start(f32[768]{0:T(1024)} %param.13) | copy-start | bytes 9220
  13.0 30.8 %copy-start.2 = (bf16[512,768]{1,0:T(8,128)(2,1)S(1)}, bf16[512,768]{1,0:T(8,128)(2,1)}, u32[]{:S(2)}) copy-start(bf16[512,768]{1,0:T(8,128)(2,1)} %refs_4_.1) | copy-start | bytes 2359300
  13.1 7.7 %collective-permute-start.1 = (bf16[96,512]{1,0:T(8,128)(2,1)S(1)}, bf16[96,512]{1,0:T(8,128)(2,1)S(1)}, u32[]{:S(2)}, u32[]{:S(2)}) collective-permute-start(bf16[96,512]{1,0:T(8,128)(2,1)S(1)} %get-tuple-element.45), channel_id=1, source_target_pairs={{0,4},{1,5},{2,6},{3,7},{4,8},{5,9},{6,10},{7,11},{8,12},{9,13},{1... | collective-permute-start | bytes 294920 | tf_op jit(solution)/shard_map/ppermute | solution.py:52
  14.7 10.1 %collective-permute-start.2 = (bf16[96,512]{1,0:T(8,128)(2,1)S(1)}, bf16[96,512]{1,0:T(8,128)(2,1)S(1)}, u32[]{:S(2)}, u32[]{:S(2)}) collective-permute-start(bf16[96,512]{1,0:T(8,128)(2,1)S(1)} %get-tuple-element.46), channel_id=1, source_target_pairs={{0,8},{1,9},{2,10},{3,11},{4,12},{5,13},{6,14},{7,15},{8,0},{9,1},... | collective-permute-start | bytes 294920 | tf_op jit(solution)/shard_map/ppermute | solution.py:52
  17.3 7.6 %collective-permute-start.3 = (bf16[96,512]{1,0:T(8,128)(2,1)S(1)}, bf16[96,512]{1,0:T(8,128)(2,1)S(1)}, u32[]{:S(2)}, u32[]{:S(2)}) collective-permute-start(bf16[96,512]{1,0:T(8,128)(2,1)S(1)} %get-tuple-element.47), channel_id=1, source_target_pairs={{0,12},{1,13},{2,14},{3,15},{4,0},{5,1},{6,2},{7,3},{8,4},{9,5},{1... | collective-permute-start | bytes 294920 | tf_op jit(solution)/shard_map/ppermute | solution.py:52
  28.4 8.1 %collective-permute-start.5 = (bf16[80,512]{1,0:T(8,128)(2,1)S(1)}, bf16[80,512]{1,0:T(8,128)(2,1)S(1)}, u32[]{:S(2)}, u32[]{:S(2)}) collective-permute-start(bf16[80,512]{1,0:T(8,128)(2,1)S(1)} %get-tuple-element.51), channel_id=1, source_target_pairs={{0,4},{1,5},{2,6},{3,7},{4,8},{5,9},{6,10},{7,11},{8,12},{9,13},{1... | collective-permute-start | bytes 245768 | tf_op jit(solution)/shard_map/ppermute | solution.py:52
  28.5 9.8 %collective-permute-start.6 = (bf16[80,512]{1,0:T(8,128)(2,1)S(1)}, bf16[80,512]{1,0:T(8,128)(2,1)S(1)}, u32[]{:S(2)}, u32[]{:S(2)}) collective-permute-start(bf16[80,512]{1,0:T(8,128)(2,1)S(1)} %get-tuple-element.52), channel_id=1, source_target_pairs={{0,8},{1,9},{2,10},{3,11},{4,12},{5,13},{6,14},{7,15},{8,0},{9,1},... | collective-permute-start | bytes 245768 | tf_op jit(solution)/shard_map/ppermute | solution.py:52
  30.7 7.5 %collective-permute-start.7 = (bf16[80,512]{1,0:T(8,128)(2,1)S(1)}, bf16[80,512]{1,0:T(8,128)(2,1)S(1)}, u32[]{:S(2)}, u32[]{:S(2)}) collective-permute-start(bf16[80,512]{1,0:T(8,128)(2,1)S(1)} %get-tuple-element.53), channel_id=1, source_target_pairs={{0,12},{1,13},{2,14},{3,15},{4,0},{5,1},{6,2},{7,3},{8,4},{9,5},{1... | collective-permute-start | bytes 245768 | tf_op jit(solution)/shard_map/ppermute | solution.py:52
  32.3 4.2 %collective-permute-start.8 = (bf16[48,512]{1,0:T(8,128)(2,1)S(1)}, bf16[48,512]{1,0:T(8,128)(2,1)S(1)}, u32[]{:S(2)}, u32[]{:S(2)}) collective-permute-start(bf16[48,512]{1,0:T(8,128)(2,1)S(1)} %get-tuple-element.58), channel_id=1, source_target_pairs={{0,2},{1,3},{2,0},{3,1},{4,6},{5,7},{6,4},{7,5},{8,10},{9,11},{10,... | collective-permute-start | bytes 147464 | tf_op jit(solution)/shard_map/ppermute | solution.py:52
  38.3 30.2 %collective-permute-start.21 = (bf16[512,768]{1,0:T(8,128)(2,1)}, bf16[512,768]{1,0:T(8,128)(2,1)S(1)}, u32[]{:S(2)}, u32[]{:S(2)}) collective-permute-start(bf16[512,768]{1,0:T(8,128)(2,1)} %refs_6_.3), channel_id=1, source_target_pairs={{0,15},{1,0},{2,1},{3,2},{4,3},{5,4},{6,5},{7,6},{8,7},{9,8},{10,9... | collective-permute-start | bytes 2359304 | tf_op jit(solution)/shard_map/ppermute | solution.py:52
  39.4 17.6 %collective-permute-start.10 = (bf16[80,512]{1,0:T(8,128)(2,1)S(1)}, bf16[80,512]{1,0:T(8,128)(2,1)S(1)}, u32[]{:S(2)}, u32[]{:S(2)}) collective-permute-start(bf16[80,512]{1,0:T(8,128)(2,1)S(1)} %shard_map.110.refs_0_), channel_id=1, source_target_pairs={{0,8},{1,9},{2,10},{3,11},{4,12},{5,13},{6,14},{7,15},{8,0},{9,1},... | collective-permute-start | bytes 245768 | tf_op jit(solution)/shard_map/ppermute | solution.py:52
  41.3 15.7 %collective-permute-start.11 = (bf16[80,512]{1,0:T(8,128)(2,1)S(1)}, bf16[80,512]{1,0:T(8,128)(2,1)S(1)}, u32[]{:S(2)}, u32[]{:S(2)}) collective-permute-start(bf16[80,512]{1,0:T(8,128)(2,1)S(1)} %shard_map.110.refs_0_), channel_id=1, source_target_pairs={{0,12},{1,13},{2,14},{3,15},{4,0},{5,1},{6,2},{7,3},{8,4},{9,5},{1... | collective-permute-start | bytes 245768 | tf_op jit(solution)/shard_map/ppermute | solution.py:52
  42.3 14.7 %collective-permute-start.9 = (bf16[80,512]{1,0:T(8,128)(2,1)S(1)}, bf16[80,512]{1,0:T(8,128)(2,1)S(1)}, u32[]{:S(2)}, u32[]{:S(2)}) collective-permute-start(bf16[80,512]{1,0:T(8,128)(2,1)S(1)} %shard_map.110.refs_0_), channel_id=1, source_target_pairs={{0,4},{1,5},{2,6},{3,7},{4,8},{5,9},{6,10},{7,11},{8,12},{9,13},{1... | collective-permute-start | bytes 245768 | tf_op jit(solution)/shard_map/ppermute | solution.py:52
  43.3 6.5 %collective-permute-start.12 = (bf16[48,512]{1,0:T(8,128)(2,1)S(1)}, bf16[48,512]{1,0:T(8,128)(2,1)}, u32[]{:S(2)}, u32[]{:S(2)}) collective-permute-start(bf16[48,512]{1,0:T(8,128)(2,1)S(1)} %shard_map.111.refs_0_), channel_id=1, source_target_pairs={{0,2},{1,3},{2,0},{3,1},{4,6},{5,7},{6,4},{7,5},{8,10},{9,11},{10,... | collective-permute-start | bytes 147464 | tf_op jit(solution)/shard_map/ppermute | solution.py:52
  43.8 0.8 copy-start.3
  57.0 11.3 %collective-permute-start.14 = (bf16[80,2048]{1,0:T(8,128)(2,1)S(1)}, bf16[80,2048]{1,0:T(8,128)(2,1)S(1)}, u32[]{:S(2)}, u32[]{:S(2)}) collective-permute-start(bf16[80,2048]{1,0:T(8,128)(2,1)S(1)} %shard_map.113.refs_0_), channel_id=1, source_target_pairs={{0,2},{1,3},{2,0},{3,1},{4,6},{5,7},{6,4},{7,5},{8,10},{9,11},{10,... | collective-permute-start | bytes 983048 | tf_op jit(solution)/shard_map/ppermute | solution.py:52
  57.9 7.5 %collective-permute-start.15 = (bf16[96,512]{1,0:T(8,128)(2,1)S(1)}, bf16[96,512]{1,0:T(8,128)(2,1)S(1)}, u32[]{:S(2)}, u32[]{:S(2)}) collective-permute-start(bf16[96,512]{1,0:T(8,128)(2,1)S(1)} %shard_map.114.refs_0_), channel_id=1, source_target_pairs={{0,4},{1,5},{2,6},{3,7},{4,8},{5,9},{6,10},{7,11},{8,12},{9,13},{1... | collective-permute-start | bytes 294920 | tf_op jit(solution)/shard_map/ppermute | solution.py:52
  59.4 8.3 %collective-permute-start.16 = (bf16[96,512]{1,0:T(8,128)(2,1)S(1)}, bf16[96,512]{1,0:T(8,128)(2,1)S(1)}, u32[]{:S(2)}, u32[]{:S(2)}) collective-permute-start(bf16[96,512]{1,0:T(8,128)(2,1)S(1)} %shard_map.114.refs_0_), channel_id=1, source_target_pairs={{0,8},{1,9},{2,10},{3,11},{4,12},{5,13},{6,14},{7,15},{8,0},{9,1},... | collective-permute-start | bytes 294920 | tf_op jit(solution)/shard_map/ppermute | solution.py:52
  60.1 7.7 %collective-permute-start.17 = (bf16[96,512]{1,0:T(8,128)(2,1)S(1)}, bf16[96,512]{1,0:T(8,128)(2,1)S(1)}, u32[]{:S(2)}, u32[]{:S(2)}) collective-permute-start(bf16[96,512]{1,0:T(8,128)(2,1)S(1)} %shard_map.114.refs_0_), channel_id=1, source_target_pairs={{0,12},{1,13},{2,14},{3,15},{4,0},{5,1},{6,2},{7,3},{8,4},{9,5},{1... | collective-permute-start | bytes 294920 | tf_op jit(solution)/shard_map/ppermute | solution.py:52
  67.8 2.7 %copy-start.1 = (bf16[2048,768]{1,0:T(8,128)(2,1)S(1)}, bf16[2048,768]{1,0:T(8,128)(2,1)}, u32[]{:S(2)}) copy-start(bf16[2048,768]{1,0:T(8,128)(2,1)} %refs_6_.2) | copy-start | bytes 9437188
  67.8 2.3 %collective-permute-start.20 = (bf16[96,2048]{1,0:T(8,128)(2,1)S(1)}, bf16[96,2048]{1,0:T(8,128)(2,1)S(1)}, u32[]{:S(2)}, u32[]{:S(2)}) collective-permute-start(bf16[96,2048]{1,0:T(8,128)(2,1)S(1)} %shard_map.115.refs_2_), channel_id=1, source_target_pairs={{0,1},{1,0},{2,3},{3,2},{4,5},{5,4},{6,7},{7,6},{8,9},{9,8},{10,11... | collective-permute-start | bytes 1179656 | tf_op jit(solution)/shard_map/ppermute | solution.py:52
  67.9 2.2 %collective-permute-start.18 = (bf16[80,2048]{1,0:T(8,128)(2,1)S(1)}, bf16[80,2048]{1,0:T(8,128)(2,1)S(1)}, u32[]{:S(2)}, u32[]{:S(2)}) collective-permute-start(bf16[80,2048]{1,0:T(8,128)(2,1)S(1)} %shard_map.113.refs_0_), channel_id=1, source_target_pairs={{0,1},{1,0},{2,3},{3,2},{4,5},{5,4},{6,7},{7,6},{8,9},{9,8},{10,11... | collective-permute-start | bytes 983048 | tf_op jit(solution)/shard_map/ppermute | solution.py:52
  68.4 2.1 %collective-permute-start.19 = (bf16[80,2048]{1,0:T(8,128)(2,1)S(1)}, bf16[80,2048]{1,0:T(8,128)(2,1)S(1)}, u32[]{:S(2)}, u32[]{:S(2)}) collective-permute-start(bf16[80,2048]{1,0:T(8,128)(2,1)S(1)} %collective-permute-done.14.refs_1_), channel_id=1, source_target_pairs={{0,1},{1,0},{2,3},{3,2},{4,5},{5,4},{6,7},{7,6},{8,9},{9,8},{10,11... | collective-permute-start | bytes 983048 | tf_op jit(solution)/shard_map/ppermute | solution.py:52
  73.5 1.4 %collective-permute-start.22 = (bf16[256,256]{1,0:T(8,128)(2,1)S(1)}, bf16[256,256]{1,0:T(8,128)(2,1)S(1)}, u32[]{:S(2)}, u32[]{:S(2)}) collective-permute-start(bf16[256,256]{1,0:T(8,128)(2,1)S(1)} %get-tuple-element.75), channel_id=1, source_target_pairs={{0,1},{1,0},{2,3},{3,2},{4,5},{5,4},{6,7},{7,6},{8,9},{9,8},{10,11... | collective-permute-start | bytes 393224 | tf_op jit(solution)/shard_map/ppermute | solution.py:52
  75.0 4.3 %collective-permute-start.23 = (bf16[128,256]{1,0:T(8,128)(2,1)S(1)}, bf16[128,256]{1,0:T(8,128)(2,1)S(1)}, u32[]{:S(2)}, u32[]{:S(2)}) collective-permute-start(bf16[128,256]{1,0:T(8,128)(2,1)S(1)} %get-tuple-element.77), channel_id=1, source_target_pairs={{0,2},{1,3},{2,0},{3,1},{4,6},{5,7},{6,4},{7,5},{8,10},{9,11},{10,... | collective-permute-start | bytes 196616 | tf_op jit(solution)/shard_map/ppermute | solution.py:52
  79.3 6.5 %collective-permute-start.24 = (bf16[128,256]{1,0:T(8,128)(2,1)S(1)}, bf16[128,256]{1,0:T(8,128)(2,1)S(1)}, u32[]{:S(2)}, u32[]{:S(2)}) collective-permute-start(bf16[128,256]{1,0:T(8,128)(2,1)S(1)} %get-tuple-element.79), channel_id=1, source_target_pairs={{0,4},{1,5},{2,6},{3,7},{4,8},{5,9},{6,10},{7,11},{8,12},{9,13},{1... | collective-permute-start | bytes 196616 | tf_op jit(solution)/shard_map/ppermute | solution.py:52
  81.0 7.0 %collective-permute-start.25 = (bf16[128,256]{1,0:T(8,128)(2,1)S(1)}, bf16[128,256]{1,0:T(8,128)(2,1)S(1)}, u32[]{:S(2)}, u32[]{:S(2)}) collective-permute-start(bf16[128,256]{1,0:T(8,128)(2,1)S(1)} %get-tuple-element.79), channel_id=1, source_target_pairs={{0,8},{1,9},{2,10},{3,11},{4,12},{5,13},{6,14},{7,15},{8,0},{9,1},... | collective-permute-start | bytes 196616 | tf_op jit(solution)/shard_map/ppermute | solution.py:52
  83.7 4.6 %collective-permute-start.26 = (bf16[128,256]{1,0:T(8,128)(2,1)S(1)}, bf16[128,256]{1,0:T(8,128)(2,1)S(1)}, u32[]{:S(2)}, u32[]{:S(2)}) collective-permute-start(bf16[128,256]{1,0:T(8,128)(2,1)S(1)} %get-tuple-element.79), channel_id=1, source_target_pairs={{0,12},{1,13},{2,14},{3,15},{4,0},{5,1},{6,2},{7,3},{8,4},{9,5},{1... | collective-permute-start | bytes 196616 | tf_op jit(solution)/shard_map/ppermute | solution.py:52
  88.3 4.3 %collective-permute-start.27 = (bf16[128,256]{1,0:T(8,128)(2,1)S(1)}, bf16[128,256]{1,0:T(8,128)(2,1)S(1)}, u32[]{:S(2)}, u32[]{:S(2)}) collective-permute-start(bf16[128,256]{1,0:T(8,128)(2,1)S(1)} %shard_map.120.refs_0_), channel_id=1, source_target_pairs={{0,2},{1,3},{2,0},{3,1},{4,6},{5,7},{6,4},{7,5},{8,10},{9,11},{10,... | collective-permute-start | bytes 196616 | tf_op jit(solution)/shard_map/ppermute | solution.py:52
  90.1 2.5 %collective-permute-start.28 = (bf16[128,256]{1,0:T(8,128)(2,1)S(1)}, bf16[128,256]{1,0:T(8,128)(2,1)S(1)}, u32[]{:S(2)}, u32[]{:S(2)}) collective-permute-start(bf16[128,256]{1,0:T(8,128)(2,1)S(1)} %shard_map.120.refs_0_), channel_id=1, source_target_pairs={{0,1},{1,0},{2,3},{3,2},{4,5},{5,4},{6,7},{7,6},{8,9},{9,8},{10,11... | collective-permute-start | bytes 196616 | tf_op jit(solution)/shard_map/ppermute | solution.py:52
  92.7 1.3 %collective-permute-start.29 = (bf16[128,256]{1,0:T(8,128)(2,1)S(1)}, bf16[128,256]{1,0:T(8,128)(2,1)S(1)}, u32[]{:S(2)}, u32[]{:S(2)}) collective-permute-start(bf16[128,256]{1,0:T(8,128)(2,1)S(1)} %collective-permute-done.27.refs_1_), channel_id=1, source_target_pairs={{0,1},{1,0},{2,3},{3,2},{4,5},{5,4},{6,7},{7,6},{8,9},{9,8},{10,11... | collective-permute-start | bytes 196616 | tf_op jit(solution)/shard_map/ppermute | solution.py:52

commit v5 on v4

--- a/solution.py
+++ b/solution.py
@@ -96,32 +96,32 @@
     return jax.ShapeDtypeStruct(shape, dtype)
 
 
-def partial_body(core, bands, parts, r_ref, p_ref, *outs):
+def partial_body(core, other, r_ref, p_ref, out_ref):
+    rows = out_ref.shape[0]
     c = position(core)
-    for (other, first, rows), out_ref in zip(parts, outs):
-        row = pl.multiple_of((1 - c if other else c) * (bands // 2) + first, 16)
-        out_ref[...] = lax.dot_general(
-            r_ref[pl.ds(row, rows), :], p_ref[...], NT, preferred_element_type=F32
-        ).astype(out_ref.dtype)
-
-
-def partial_intersections(response, projectors, core, parts):
+    row = pl.multiple_of((1 - c if other else c) * rows, rows)
+    out_ref[...] = lax.dot_general(
+        r_ref[pl.ds(row, rows), :], p_ref[...], NT, preferred_element_type=F32
+    ).astype(out_ref.dtype)
+
+
+def partial_intersections(response, projectors, core, other):
     bands, cells = response.shape
     count = projectors.shape[0]
+    rows = bands // 2
     tile = min(512, count)
-    outs = [struct((rows, count), BF16 if other else F32) for other, _, rows in parts]
-    done = sum(rows for _, _, rows in parts)
+    out = struct((rows, count), BF16 if other else F32)
     return pl.pallas_call(
-        functools.partial(partial_body, core, bands, parts),
+        functools.partial(partial_body, core, other),
         grid=(count // tile,),
-        out_shape=outs,
+        out_shape=out,
         in_specs=[
             pl.BlockSpec((bands, cells), lambda i: (0, 0)),
             pl.BlockSpec((tile, cells), lambda i: (i, 0)),
         ],
-        out_specs=[pl.BlockSpec((rows, tile), lambda i: (0, i)) for _, _, rows in parts],
+        out_specs=pl.BlockSpec((rows, tile), lambda i: (0, i)),
         compiler_params=params(),
-        cost_estimate=cost(2 * done * cells * count, projectors, *outs),
+        cost_estimate=cost(2 * rows * cells * count, projectors, out),
     )(response, projectors)
 
 
@@ -131,23 +131,20 @@
     me = position(level)
     rows, width = own_ref.shape
     for step, out in enumerate((own_ref, *sends)):
-        place = lax.rem(me + step, jnp.int32(size))
+        at = lax.rem(me + step, jnp.int32(size))
         if along == 0:
-            at = pl.multiple_of(place * rows, 16)
-            part = (pl.ds(at, rows), slice(None))
-            theirs = (pl.ds(pl.multiple_of(at + first, 16), rows), slice(None))
+            part = (pl.ds(pl.multiple_of(at * rows + first, 16), rows), slice(None))
         else:
-            part = (slice(None), pl.ds(pl.multiple_of(place * width, width), width))
-            theirs = (slice(first, first + rows), part[1])
+            part = (slice(first, first + rows), pl.ds(pl.multiple_of(at * width, width), width))
         total = keep_ref[part]
         for ref in taken:
-            total = total + ref[theirs].astype(F32)
+            total = total + ref[part].astype(F32)
         out[...] = total.astype(out.dtype)
 
 
-def split(keep, taken, level, along, first=0):
+def split(keep, taken, level, along, rows=None, first=0):
     size, _ = level
-    shape = list(keep.shape)
+    shape = [rows or keep.shape[0], keep.shape[1]]
     shape[along] //= size
     outs = [struct(shape, F32)] + [struct(shape, BF16)] * (size - 1)
     return local_call(
@@ -189,22 +186,27 @@
 
 
 def local_body(depth, sizes, *refs):
-    r_ref, l_ref, o_ref, m_ref, pot_ref, v_ref, e_ref, first_ref, many_ref, out_ref, mask_ref = refs
+    r_ref, l_ref, h_ref, o_ref, m_ref, pot_ref, v_ref, e_ref = refs[:8]
+    first_ref, many_ref, out_ref, mask_ref = refs[8:]
     plane = GY * GZ
     reach = 6
+
+    def plane_at(j):
+        if j < 0:
+            ref, k = l_ref, j + reach
+        elif j < depth:
+            ref, k = r_ref, j
+        else:
+            ref, k = h_ref, j - depth
+        return ref[:, k * plane : (k + 1) * plane]
+
     for j in range(depth):
         cols = slice(j * plane, (j + 1) * plane)
-        low = r_ref[:, cols]
+        low = plane_at(j)
         total = jnp.dot(low, m_ref[0], preferred_element_type=F32)
         total = total + jnp.dot(low, m_ref[1], preferred_element_type=F32)
         for offset in range(1, 7):
-            pair = 0.0
-            for k in (j - offset, j + offset):
-                if 0 <= k < depth:
-                    pair = pair + r_ref[:, k * plane : (k + 1) * plane].astype(F32)
-                elif k < 0:
-                    k = k + reach
-                    pair = pair + l_ref[:, k * plane : (k + 1) * plane].astype(F32)
+            pair = plane_at(j + offset).astype(F32) + plane_at(j - offset).astype(F32)
             total = total + (KINETIC * COEFFS[offset]) * pair
         total = total + (e_ref[...] - pot_ref[:, cols]) * low.astype(F32)
         out_ref[:, cols] = total - v_ref[:, cols] * o_ref[:, cols].astype(F32)
@@ -216,7 +218,7 @@
     mask_ref[...] = jnp.where(inside, 1.0, 0.0).astype(BF16)
 
 
-def local_part(response, low, orbitals, matrix, lines, columns, group_rows, width, blk):
+def local_part(response, low, high, orbitals, matrix, lines, columns, group_rows, width, blk):
     bands, cells = response.shape
     depth = cells // (GY * GZ)
     outs = [struct((bands, cells), F32), struct((bands, width), BF16)]
@@ -231,6 +233,7 @@
         in_specs=[
             here,
             side,
+            side,
             here,
             pl.BlockSpec(matrix.shape, lambda i: (0, 0, 0)),
             line,
@@ -241,35 +244,8 @@
         ],
         out_specs=[here, pl.BlockSpec((group_rows, width), lambda i: (i, 0))],
         compiler_params=params(),
-        cost_estimate=cost(2 * bands * cells * 300, low, low, low, *outs),
-    )(response, low, orbitals, matrix, *lines, *columns)
-
-
-def next_body(depth, h_ref, base_ref, out_ref):
-    plane = GY * GZ
-    for j in range(depth):
-        cols = slice(j * plane, (j + 1) * plane)
-        total = base_ref[:, cols]
-        for k in range(depth, j + 7):
-            at = k - depth
-            far = h_ref[:, at * plane : (at + 1) * plane].astype(F32)
-            total = total + (KINETIC * COEFFS[k - j]) * far
-        out_ref[:, cols] = total
-
-
-def add_next(base, high, group_rows):
-    bands, cells = base.shape
-    out = struct(base.shape, F32)
-    here = pl.BlockSpec((group_rows, cells), lambda i: (i, 0))
-    return pl.pallas_call(
-        functools.partial(next_body, cells // (GY * GZ)),
-        grid=(bands // group_rows,),
-        out_shape=out,
-        in_specs=[pl.BlockSpec((group_rows, high.shape[1]), lambda i: (i, 0)), here],
-        out_specs=here,
-        compiler_params=params(),
-        cost_estimate=cost(bands * cells * 14, high, base, out),
-    )(high, base)
+        cost_estimate=cost(2 * bands * cells * 300, low, high, low, low, *outs),
+    )(response, low, high, orbitals, matrix, *lines, *columns)
 
 
 def first_orbital(group, group_rows, width, bands, blk):
@@ -325,28 +301,59 @@
     return local_call(sum_body, outs, [keep, *taken])
 
 
-def project_body(core, across, group_rows, width, blk, *refs):
+def project_body(core, across, width, blk, *refs):
     size = across[0]
     blocks = refs[: 2 * size]
     o_ref, u_ref, r_ref, mask_ref, updated_ref, residual_ref, w_ref = refs[2 * size :]
     bands = o_ref.shape[0]
     half = bands // 2
-    c, x = position(core), position(across)
-    for k, ref in enumerate(blocks):
-        side, step = divmod(k, size)
-        at = (c if side == 0 else 1 - c) * half
-        at = at + lax.rem(x - step + size, jnp.int32(size)) * ref.shape[0]
-        w_ref[pl.ds(pl.multiple_of(at, 16), ref.shape[0]), :] = ref[...]
-    for g in range(bands // group_rows):
-        start = first_orbital(g, group_rows, width, bands, blk)
-        mine = slice(g * group_rows, (g + 1) * group_rows)
-        inside = mask_ref[mine, :].astype(F32) > 0.5
-        weights = jnp.where(inside, w_ref[mine, :].astype(F32), 0.0).astype(BF16)
-        residual = u_ref[mine, :] - jnp.dot(
-            weights, o_ref[start : start + width, :], preferred_element_type=F32
-        )
-        residual_ref[mine, :] = residual.astype(BF16)
-        updated_ref[mine, :] = (r_ref[mine, :].astype(F32) + STEP_SIZE * residual).astype(BF16)
+    group_rows = u_ref.shape[0]
+    g = pl.program_id(0)
+
+    @pl.when(g == 0)
+    def _():
+        c, x = position(core), position(across)
+        for k, ref in enumerate(blocks):
+            side, step = divmod(k, size)
+            at = (c if side == 0 else 1 - c) * half
+            at = at + lax.rem(x - step + size, jnp.int32(size)) * ref.shape[0]
+            w_ref[pl.ds(pl.multiple_of(at, 16), ref.shape[0]), :] = ref[...]
+
+    start = jnp.clip(g * group_rows - REACH * blk, 0, bands - width)
+    window = o_ref[pl.ds(pl.multiple_of(start, blk), width), :]
+    mine = pl.ds(pl.multiple_of(g * group_rows, group_rows), group_rows)
+    inside = mask_ref[...].astype(F32) > 0.5
+    weights = jnp.where(inside, w_ref[mine, :].astype(F32), 0.0).astype(BF16)
+    residual = u_ref[...] - jnp.dot(weights, window, preferred_element_type=F32)
+    residual_ref[...] = residual.astype(BF16)
+    updated_ref[...] = (r_ref[...].astype(F32) + STEP_SIZE * residual).astype(BF16)
+
+
+def project(weights, orbitals, unprojected, response, mask, core, across, group_rows, blk):
+    bands, cells = response.shape
+    width = mask.shape[1]
+    out = struct((bands, cells), BF16)
+    here = pl.BlockSpec((group_rows, cells), lambda g: (g, 0))
+
+    def full(a):
+        return pl.BlockSpec(a.shape, lambda g: (0, 0))
+
+    return pl.pallas_call(
+        functools.partial(project_body, core, across, width, blk),
+        grid=(bands // group_rows,),
+        out_shape=(out, out),
+        in_specs=[
+            *[full(a) for a in weights],
+            full(orbitals),
+            here,
+            here,
+            pl.BlockSpec((group_rows, width), lambda g: (g, 0)),
+        ],
+        out_specs=(here, here),
+        scratch_shapes=[pltpu.VMEM((bands, width), BF16)],
+        compiler_params=params(),
+        cost_estimate=cost(2 * bands * width * cells, orbitals, unprojected, response, out, out),
+    )(*weights, orbitals, unprojected, response, mask)
 
 
 def shards(
@@ -364,8 +371,7 @@
     group_rows = GROUP_BLOCKS * blk
     width = (GROUP_BLOCKS + 2 * REACH) * blk
     half = bands // 2
-    step = 16 * across[0]
-    rows_x = (2 * half // 3 + step // 2) // step * step
+    rows_x = half // 2
     rows_z = half - rows_x
     matrix = jnp.asarray(plane_matrix())
     lines = (potential[None, :], perturbing[None, :])
@@ -378,32 +384,28 @@
         return [shifted(part, count, level, k + 1) for k, part in enumerate(parts)]
 
     low = shifted(response[:, local_cells - halo :], count, ring, 1)
-
-    (sent,) = partial_intersections(response, projectors, core, [(True, 0, half)])
-    sent = shifted(sent, count, core, 1)
-    keep_z, keep_x = partial_intersections(
-        response, projectors, core, [(False, rows_x, rows_z), (False, 0, rows_x)]
-    )
-    keep_z, *parts_z = split(keep_z, [sent], along, 1, rows_x)
-    keep_x, *parts_x = split(keep_x, [sent], across, 0, 0)
-    taken_z, taken_x = lax.optimization_barrier(
-        (parts_to(parts_z, along), parts_to(parts_x, across))
+    high = shifted(response[:, :halo], count, ring, -1)
+
+    sent = shifted(partial_intersections(response, projectors, core, True), count, core, 1)
+    keep = partial_intersections(response, projectors, core, False)
+    keep_z, *parts_z = split(keep, [sent], along, 1, rows_z, rows_x)
+    keep_x, *parts_x = split(keep, [sent], across, 0, rows_x, 0)
+    taken_z, taken_x, low, high = lax.optimization_barrier(
+        (parts_to(parts_z, along), parts_to(parts_x, across), low, high)
+    )
+    base, mask = local_part(
+        response, low, high, orbitals, matrix, lines, columns, group_rows, width, blk
     )
     keep_x, *parts_x = split(keep_x, taken_x, along, 1)
     keep_z, *parts_z = split(keep_z, taken_z, across, 0)
-    taken_x, taken_z = lax.optimization_barrier(
-        (parts_to(parts_x, along), parts_to(parts_z, across))
+    taken_x, taken_z, base = lax.optimization_barrier(
+        (parts_to(parts_x, along), parts_to(parts_z, across), base)
     )
     share_z = finish(keep_z, taken_z, ace_scale)
     share_x = finish(keep_x, taken_x, ace_scale)
 
-    head, low, _ = lax.optimization_barrier((response[:, :halo], low, share_z))
-    high = shifted(head, count, ring, -1)
-    base, mask = local_part(
-        response, low, orbitals, matrix, lines, columns, group_rows, width, blk
-    )
-    pieces_x, pieces_z, base = lax.optimization_barrier(
-        ([share_x, *to(share_x, along)], [share_z, *to(share_z, across)], base)
+    pieces_x, pieces_z = lax.optimization_barrier(
+        ([share_x, *to(share_x, along)], [share_z, *to(share_z, across)])
     )
     block_x = place(pieces_x, along, 1)
     block_z = place(pieces_z, across, 0)
@@ -412,7 +414,6 @@
     blocks = [*blocks_x, block_z]
     blocks += [shifted(block, count, core, 1) for block in blocks]
 
-    base = add_next(base, high, group_rows)
     unprojected, send, keep = local_call(
         functools.partial(apply_body, core, across, rows_x, group_rows, width, blk),
         [
@@ -429,13 +430,8 @@
     weights = finish(total, to(low, along), window_scale)
     weights = [weights, *to(weights, across)]
     weights += [shifted(block, count, core, 1) for block in weights]
-    out = struct((bands, local_cells), BF16)
-    return local_call(
-        functools.partial(project_body, core, across, group_rows, width, blk),
-        (out, out),
-        [*weights, orbitals, unprojected, response, mask],
-        flops=2 * bands * width * local_cells,
-        scratch=[pltpu.VMEM((bands, width), BF16)],
+    return project(
+        weights, orbitals, unprojected, response, mask, core, across, group_rows, blk
     )
 
 

time: 97.1 us -> 98.5 us (1.014)
  starting transfers between devices: 33 us -> 42.7 us
  waiting for transfers between devices: 41.8 us -> 35.5 us
  Pallas kernels: 17.7 us -> 13.7 us
  local copies, waits for them, and re-layouts: 3.2 us -> 5.32 us
    ppermute x30, starting transfers between devices: 33 us -> 42.7 us  [shifted(): return lax.ppermute(array, 'band', pairs)]
    ppermute x30, waiting for transfers between devices: 41.8 us -> 35.5 us  [shifted(): return lax.ppermute(array, 'band', pairs)]
    pallas_call x3, Pallas kernels: 7.18 us -> 5.68 us  [the longest x2 3.44 us: partial_intersections(): pl.pallas_call(functools.partial(partial_body, core, other), grid=(count...]
    unnamed x18 -> x24, local copies, waits for them, and re-layouts: 2.76 us -> 4.2 us
    pallas_call x14 -> x13, Pallas kernels: 7.1 us -> 5.72 us  [local_call(): pl.pallas_call(body, out_shape=outs, in_specs=[whole() for _ in args], ou...]
    pallas_call x1, Pallas kernels: 3.4 us -> 2.29 us  [local_part(): pl.pallas_call(functools.partial(local_body, depth, (group_rows, width, b...]
  transfers between devices with their start and end apart: 30 -> 30, of which waited for: 18 -> 17; matrix products, arithmetic and copies ran while one was open for 0% -> 1% of each run, Pallas kernels for 9% -> 6%
where the time goes in v5:
time: 98.5 us; the launch traced here: 98.2 us
  starting transfers between devices  42.7 us (43%)
  waiting for transfers between devices  35.5 us (36%)
  Pallas kernels  13.7 us (14%)
  local copies, waits for them, and re-layouts  5.32 us (5%)
    ppermute x30, starting transfers between devices, shifted(): return lax.ppermute(array, 'band', pairs)  42.7 us
    ppermute x30, waiting for transfers between devices, shifted(): return lax.ppermute(array, 'band', pairs)  35.5 us
    pallas_call x13, Pallas kernels, local_call(): pl.pallas_call(body, out_shape=outs, in_specs=[whole() for _ in args], ou...  5.72 us
    unnamed x24, local copies, waits for them, and re-layouts  4.2 us
    pallas_call x2, Pallas kernels, partial_intersections(): pl.pallas_call(functools.partial(partial_body, core, other), grid=(count...  3.44 us
    pallas_call x1, Pallas kernels, local_part(): pl.pallas_call(functools.partial(local_body, depth, (group_rows, width, b...  2.29 us
    pallas_call x1, Pallas kernels, project(): pl.pallas_call(functools.partial(project_body, core, across, width, blk),...  2.24 us
  transfers between devices with their start and end apart: 30, of which 17 were waited for; matrix products, arithmetic and copies ran while one was open for 1% of the time, Pallas kernels for 6%

profile of v5, /device:TPU:0, one launch (start us, length us, event | category | flops | bytes accessed | tf_op | source)
XLA Modules:
  0.0 98.2 jit_solution(6256403290213907018)
XLA Ops:
  0.6 0.0 copy-start
  0.6 1.9 %copy-done = bf16[2048,768]{1,0:T(8,128)(2,1)S(1)} copy-done((bf16[2048,768]{1,0:T(8,128)(2,1)S(1)}, bf16[2048,768]{1,0:T(8,128)(2,1)}, u32[]{:S(2)}) %copy-start) | copy-done | bytes 3145752
  2.5 1.1 %copy-done.2 = bf16[512,768]{1,0:T(8,128)(2,1)S(1)} copy-done((bf16[512,768]{1,0:T(8,128)(2,1)S(1)}, bf16[512,768]{1,0:T(8,128)(2,1)}, u32[]{:S(2)}) %copy-start.2) | copy-done | bytes 786456
  3.7 1.7 %shard_map.105 = bf16[256,2048]{1,0:T(8,128)(2,1)S(1)} custom-call(bf16[512,768]{1,0:T(8,128)(2,1)S(1)} %copy-done.2, bf16[2048,768]{1,0:T(8,128)(2,1)S(1)} %copy-done), custom_call_target="tpu_custom_call" | custom-call | flops 805306368 | bytes 4194304 | tf_op jit(solution)/shard_map/pallas_call | solution.py:114
  5.3 0.5 collective-permute-start
  5.9 0.1 collective-permute-start.5
  5.9 5.6 %collective-permute-start.6 = (bf16[512,768]{1,0:T(8,128)(2,1)S(1)}, bf16[512,768]{1,0:T(8,128)(2,1)S(1)}, u32[]{:S(2)}, u32[]{:S(2)}) collective-permute-start(bf16[512,768]{1,0:T(8,128)(2,1)S(1)} %copy-done.2), channel_id=1, source_target_pairs={{0,15},{1,0},{2,1},{3,2},{4,3},{5,4},{6,5},{7,6},{8,7},{9,8},{10,9... | collective-permute-start | bytes 2359304 | tf_op jit(solution)/shard_map/ppermute | solution.py:52
  11.5 1.8 %shard_map.104.refs_0_ = f32[256,2048]{1,0:T(8,128)S(1)} custom-call(bf16[512,768]{1,0:T(8,128)(2,1)S(1)} %copy-done.2, bf16[2048,768]{1,0:T(8,128)(2,1)S(1)} %copy-done), custom_call_target="tpu_custom_call" | custom-call | flops 805306368 | bytes 5242880 | tf_op jit(solution)/shard_map/pallas_call | solution.py:114
  13.3 0.1 shard_map.106
  13.4 0.0 copy-start.8
  13.4 0.0 copy-start.9
  13.5 0.0 copy-start.7
  13.5 0.1 collective-permute-start.4
  13.6 0.1 shard_map.107
  13.7 0.3 collective-permute-start.1
  13.9 2.6 %collective-permute-start.2 = (bf16[128,512]{1,0:T(8,128)(2,1)S(1)}, bf16[128,512]{1,0:T(8,128)(2,1)S(1)}, u32[]{:S(2)}, u32[]{:S(2)}) collective-permute-start(bf16[128,512]{1,0:T(8,128)(2,1)S(1)} %get-tuple-element.42), channel_id=1, source_target_pairs={{0,8},{1,9},{2,10},{3,11},{4,12},{5,13},{6,14},{7,15},{8,0},{9,1},... | collective-permute-start | bytes 393224 | tf_op jit(solution)/shard_map/ppermute | solution.py:52
  16.5 5.4 %collective-permute-done.5.refs_1_ = bf16[512,768]{1,0:T(8,128)(2,1)S(1)} collective-permute-done((bf16[512,768]{1,0:T(8,128)(2,1)S(1)}, bf16[512,768]{1,0:T(8,128)(2,1)S(1)}, u32[]{:S(2)}, u32[]{:S(2)}) %collective-permute-start.5) | collective-permute-done | bytes 786464 | tf_op jit(solution)/shard_map/ppermute | solution.py:52
  21.9 2.6 %collective-permute-start.3 = (bf16[128,512]{1,0:T(8,128)(2,1)S(1)}, bf16[128,512]{1,0:T(8,128)(2,1)S(1)}, u32[]{:S(2)}, u32[]{:S(2)}) collective-permute-start(bf16[128,512]{1,0:T(8,128)(2,1)S(1)} %get-tuple-element.43), channel_id=1, source_target_pairs={{0,12},{1,13},{2,14},{3,15},{4,0},{5,1},{6,2},{7,3},{8,4},{9,5},{1... | collective-permute-start | bytes 393224 | tf_op jit(solution)/shard_map/ppermute | solution.py:52
  24.5 3.0 %collective-permute-done.1.refs_1_ = bf16[128,512]{1,0:T(8,128)(2,1)S(1)} collective-permute-done((bf16[128,512]{1,0:T(8,128)(2,1)S(1)}, bf16[128,512]{1,0:T(8,128)(2,1)S(1)}, u32[]{:S(2)}, u32[]{:S(2)}) %collective-permute-start.1) | collective-permute-done | bytes 131104 | tf_op jit(solution)/shard_map/ppermute | solution.py:52
  27.5 3.0 %collective-permute-done.2.refs_2_ = bf16[128,512]{1,0:T(8,128)(2,1)S(1)} collective-permute-done((bf16[128,512]{1,0:T(8,128)(2,1)S(1)}, bf16[128,512]{1,0:T(8,128)(2,1)S(1)}, u32[]{:S(2)}, u32[]{:S(2)}) %collective-permute-start.2) | collective-permute-done | bytes 131104 | tf_op jit(solution)/shard_map/ppermute | solution.py:52
  30.6 3.6 %collective-permute-done.4.refs_1_ = bf16[64,2048]{1,0:T(8,128)(2,1)S(1)} collective-permute-done((bf16[64,2048]{1,0:T(8,128)(2,1)S(1)}, bf16[64,2048]{1,0:T(8,128)(2,1)S(1)}, u32[]{:S(2)}, u32[]{:S(2)}) %collective-permute-start.4) | collective-permute-done | bytes 262176 | tf_op jit(solution)/shard_map/ppermute | solution.py:52
  34.2 0.7 shard_map.109
  34.8 3.0 %collective-permute-start.10 = (bf16[64,512]{1,0:T(8,128)(2,1)}, bf16[64,512]{1,0:T(8,128)(2,1)S(1)}, u32[]{:S(2)}, u32[]{:S(2)}) collective-permute-start(bf16[64,512]{1,0:T(8,128)(2,1)} %get-tuple-element.54), channel_id=1, source_target_pairs={{0,2},{1,3},{2,0},{3,1},{4,6},{5,7},{6,4},{7,5},{8,10},{9,11},{10,... | collective-permute-start | bytes 196616 | tf_op jit(solution)/shard_map/ppermute | solution.py:52
  37.8 0.7 shard_map.108
  38.5 0.4 collective-permute-start.7
  39.0 4.4 %collective-permute-start.8 = (bf16[64,512]{1,0:T(8,128)(2,1)}, bf16[64,512]{1,0:T(8,128)(2,1)}, u32[]{:S(2)}, u32[]{:S(2)}) collective-permute-start(bf16[64,512]{1,0:T(8,128)(2,1)} %get-tuple-element.48), channel_id=1, source_target_pairs={{0,8},{1,9},{2,10},{3,11},{4,12},{5,13},{6,14},{7,15},{8,0},{9,1},... | collective-permute-start | bytes 196616 | tf_op jit(solution)/shard_map/ppermute | solution.py:52
  43.4 0.1 copy.11.refs_7_
  43.5 0.1 copy.12.refs_8_
  43.7 0.8 copy.13.refs_9_
  44.6 0.0 copy-start.6
  44.6 1.1 %copy-done.6 = bf16[512,768]{1,0:T(8,128)(2,1)S(1)} copy-done((bf16[512,768]{1,0:T(8,128)(2,1)S(1)}, bf16[512,768]{1,0:T(8,128)(2,1)}, u32[]{:S(2)}) %copy-start.6) | copy-done | bytes 786456
  45.7 2.3 %shard_map.110 = (f32[512,768]{1,0:T(8,128)S(1)}, bf16[512,256]{1,0:T(8,128)(2,1)S(1)}) custom-call(bf16[512,768]{1,0:T(8,128)(2,1)S(1)} %copy-done.3, bf16[512,768]{1,0:T(8,128)(2,1)S(1)} %collective-permute-done.5.refs_1_, bf16[512,768]{1,0:T(8,128)(2,1)S(1)} %copy-done.6, bf16[512,768]{1,0:T(8,128)(2,1)S(1)} %copy-done.4, ...), custom_call_target="tpu_custom_call" | custom-call | flops 235929600 | bytes 4980736 | tf_op jit(solution)/shard_map/pallas_call | solution.py:229
  48.1 0.1 collective-permute-start.14
  48.2 0.9 shard_map.111.refs_0_
  49.1 2.1 %collective-permute-start.11 = (bf16[64,512]{1,0:T(8,128)(2,1)S(1)}, bf16[64,512]{1,0:T(8,128)(2,1)S(1)}, u32[]{:S(2)}, u32[]{:S(2)}) collective-permute-start(bf16[64,512]{1,0:T(8,128)(2,1)S(1)} %shard_map.111.refs_0_), channel_id=1, source_target_pairs={{0,4},{1,5},{2,6},{3,7},{4,8},{5,9},{6,10},{7,11},{8,12},{9,13},{1... | collective-permute-start | bytes 196616 | tf_op jit(solution)/shard_map/ppermute | solution.py:52
  51.2 0.9 collective-permute-start.12
  52.1 1.5 %collective-permute-start.13 = (bf16[64,512]{1,0:T(8,128)(2,1)S(1)}, bf16[64,512]{1,0:T(8,128)(2,1)S(1)}, u32[]{:S(2)}, u32[]{:S(2)}) collective-permute-start(bf16[64,512]{1,0:T(8,128)(2,1)S(1)} %shard_map.111.refs_0_), channel_id=1, source_target_pairs={{0,12},{1,13},{2,14},{3,15},{4,0},{5,1},{6,2},{7,3},{8,4},{9,5},{1... | collective-permute-start | bytes 196616 | tf_op jit(solution)/shard_map/ppermute | solution.py:52
  53.6 1.6 %collective-permute-done.11.refs_1_ = bf16[64,512]{1,0:T(8,128)(2,1)S(1)} collective-permute-done((bf16[64,512]{1,0:T(8,128)(2,1)S(1)}, bf16[64,512]{1,0:T(8,128)(2,1)S(1)}, u32[]{:S(2)}, u32[]{:S(2)}) %collective-permute-start.11) | collective-permute-done | bytes 65568 | tf_op jit(solution)/shard_map/ppermute | solution.py:52
  55.2 1.5 %collective-permute-done.12.refs_2_ = bf16[64,512]{1,0:T(8,128)(2,1)S(1)} collective-permute-done((bf16[64,512]{1,0:T(8,128)(2,1)S(1)}, bf16[64,512]{1,0:T(8,128)(2,1)S(1)}, u32[]{:S(2)}, u32[]{:S(2)}) %collective-permute-start.12) | collective-permute-done | bytes 65568 | tf_op jit(solution)/shard_map/ppermute | solution.py:52
  56.7 0.3 collective-permute-done.13.refs_3_
  57.1 0.9 collective-permute-start.16
  58.0 3.1 %collective-permute-start.17 = (bf16[128,512]{1,0:T(8,128)(2,1)S(1)}, bf16[128,512]{1,0:T(8,128)(2,1)S(1)}, u32[]{:S(2)}, u32[]{:S(2)}) collective-permute-start(bf16[128,512]{1,0:T(8,128)(2,1)S(1)} %shard_map.114.refs_0_), channel_id=1, source_target_pairs={{0,8},{1,9},{2,10},{3,11},{4,12},{5,13},{6,14},{7,15},{8,0},{9,1},... | collective-permute-start | bytes 393224 | tf_op jit(solution)/shard_map/ppermute | solution.py:52
  61.0 0.8 collective-permute-start.18
  61.9 4.8 %collective-permute-start.15 = (bf16[64,2048]{1,0:T(8,128)(2,1)S(1)}, bf16[64,2048]{1,0:T(8,128)(2,1)S(1)}, u32[]{:S(2)}, u32[]{:S(2)}) collective-permute-start(bf16[64,2048]{1,0:T(8,128)(2,1)S(1)} %shard_map.113.refs_0_), channel_id=1, source_target_pairs={{0,2},{1,3},{2,0},{3,1},{4,6},{5,7},{6,4},{7,5},{8,10},{9,11},{10,... | collective-permute-start | bytes 786440 | tf_op jit(solution)/shard_map/ppermute | solution.py:52
  66.7 0.7 collective-permute-done.17.refs_2_
  67.5 0.1 collective-permute-start.21
  67.5 0.5 collective-permute-start.19
  68.0 3.0 %collective-permute-done.15.refs_1_ = bf16[64,2048]{1,0:T(8,128)(2,1)S(1)} collective-permute-done((bf16[64,2048]{1,0:T(8,128)(2,1)S(1)}, bf16[64,2048]{1,0:T(8,128)(2,1)S(1)}, u32[]{:S(2)}, u32[]{:S(2)}) %collective-permute-start.15) | collective-permute-done | bytes 262176 | tf_op jit(solution)/shard_map/ppermute | solution.py:52
  71.1 1.5 %collective-permute-done.20.refs_4_ = bf16[64,2048]{1,0:T(8,128)(2,1)S(1)} collective-permute-done((bf16[64,2048]{1,0:T(8,128)(2,1)S(1)}, bf16[64,2048]{1,0:T(8,128)(2,1)S(1)}, u32[]{:S(2)}, u32[]{:S(2)}) %collective-permute-start.20) | collective-permute-done | bytes 262176 | tf_op jit(solution)/shard_map/ppermute | solution.py:52
  72.6 3.0 %shard_map.116 = (f32[512,768]{1,0:T(8,128)S(1)}, bf16[256,256]{1,0:T(8,128)(2,1)S(1)}, f32[256,256]{1,0:T(8,128)S(1)}) custom-call(bf16[64,2048]{1,0:T(8,128)(2,1)S(1)} %shard_map.113.refs_0_, bf16[64,2048]{1,0:T(8,128)(2,1)S(1)} %collective-permute-done.15.refs_1_, bf16[128,2048]{1,0:T(8,128)(2,1)S(1)} %shard_map.115.refs_2_, ...), custom_call_target="tpu_custom_call" | custom-call | flops 1811939328 | bytes 9568256 | tf_op jit(solution)/shard_map/pallas_call | solution.py:84
  75.6 0.2 collective-permute-start.22
  75.8 1.2 %collective-permute-done.22.refs_1_ = bf16[256,256]{1,0:T(8,128)(2,1)S(1)} collective-permute-done((bf16[256,256]{1,0:T(8,128)(2,1)S(1)}, bf16[256,256]{1,0:T(8,128)(2,1)S(1)}, u32[]{:S(2)}, u32[]{:S(2)}) %collective-permute-start.22) | collective-permute-done | bytes 131104 | tf_op jit(solution)/shard_map/ppermute | solution.py:52
  77.1 2.1 %collective-permute-start.23 = (bf16[128,256]{1,0:T(8,128)(2,1)S(1)}, bf16[128,256]{1,0:T(8,128)(2,1)S(1)}, u32[]{:S(2)}, u32[]{:S(2)}) collective-permute-start(bf16[128,256]{1,0:T(8,128)(2,1)S(1)} %get-tuple-element.73), channel_id=1, source_target_pairs={{0,2},{1,3},{2,0},{3,1},{4,6},{5,7},{6,4},{7,5},{8,10},{9,11},{10,... | collective-permute-start | bytes 196616 | tf_op jit(solution)/shard_map/ppermute | solution.py:52
  79.2 2.4 %collective-permute-done.23.refs_0_ = bf16[128,256]{1,0:T(8,128)(2,1)S(1)} collective-permute-done((bf16[128,256]{1,0:T(8,128)(2,1)S(1)}, bf16[128,256]{1,0:T(8,128)(2,1)S(1)}, u32[]{:S(2)}, u32[]{:S(2)}) %collective-permute-start.23) | collective-permute-done | bytes 65568 | tf_op jit(solution)/shard_map/ppermute | solution.py:52
  81.6 2.0 %collective-permute-start.24 = (bf16[128,256]{1,0:T(8,128)(2,1)S(1)}, bf16[128,256]{1,0:T(8,128)(2,1)S(1)}, u32[]{:S(2)}, u32[]{:S(2)}) collective-permute-start(bf16[128,256]{1,0:T(8,128)(2,1)S(1)} %get-tuple-element.75), channel_id=1, source_target_pairs={{0,4},{1,5},{2,6},{3,7},{4,8},{5,9},{6,10},{7,11},{8,12},{9,13},{1... | collective-permute-start | bytes 196616 | tf_op jit(solution)/shard_map/ppermute | solution.py:52
  83.6 1.5 %collective-permute-start.25 = (bf16[128,256]{1,0:T(8,128)(2,1)S(1)}, bf16[128,256]{1,0:T(8,128)(2,1)S(1)}, u32[]{:S(2)}, u32[]{:S(2)}) collective-permute-start(bf16[128,256]{1,0:T(8,128)(2,1)S(1)} %get-tuple-element.75), channel_id=1, source_target_pairs={{0,8},{1,9},{2,10},{3,11},{4,12},{5,13},{6,14},{7,15},{8,0},{9,1},... | collective-permute-start | bytes 196616 | tf_op jit(solution)/shard_map/ppermute | solution.py:52
  85.2 0.9 collective-permute-start.26
  86.1 2.0 %collective-permute-done.24.refs_0_ = bf16[128,256]{1,0:T(8,128)(2,1)S(1)} collective-permute-done((bf16[128,256]{1,0:T(8,128)(2,1)S(1)}, bf16[128,256]{1,0:T(8,128)(2,1)S(1)}, u32[]{:S(2)}, u32[]{:S(2)}) %collective-permute-start.24) | collective-permute-done | bytes 65568 | tf_op jit(solution)/shard_map/ppermute | solution.py:52
  88.1 2.1 %collective-permute-done.25.refs_1_ = bf16[128,256]{1,0:T(8,128)(2,1)S(1)} collective-permute-done((bf16[128,256]{1,0:T(8,128)(2,1)S(1)}, bf16[128,256]{1,0:T(8,128)(2,1)S(1)}, u32[]{:S(2)}, u32[]{:S(2)}) %collective-permute-start.25) | collective-permute-done | bytes 65568 | tf_op jit(solution)/shard_map/ppermute | solution.py:52
  90.2 0.1 collective-permute-done.26.refs_2_
  90.4 1.6 %collective-permute-start.27 = (bf16[128,256]{1,0:T(8,128)(2,1)S(1)}, bf16[128,256]{1,0:T(8,128)(2,1)S(1)}, u32[]{:S(2)}, u32[]{:S(2)}) collective-permute-start(bf16[128,256]{1,0:T(8,128)(2,1)S(1)} %shard_map.119.refs_0_), channel_id=1, source_target_pairs={{0,2},{1,3},{2,0},{3,1},{4,6},{5,7},{6,4},{7,5},{8,10},{9,11},{10,... | collective-permute-start | bytes 196616 | tf_op jit(solution)/shard_map/ppermute | solution.py:52
  92.0 2.7 %collective-permute-done.27.refs_1_ = bf16[128,256]{1,0:T(8,128)(2,1)S(1)} collective-permute-done((bf16[128,256]{1,0:T(8,128)(2,1)S(1)}, bf16[128,256]{1,0:T(8,128)(2,1)S(1)}, u32[]{:S(2)}, u32[]{:S(2)}) %collective-permute-start.27) | collective-permute-done | bytes 65568 | tf_op jit(solution)/shard_map/ppermute | solution.py:52
  94.7 1.2 %collective-permute-done.29.refs_3_ = bf16[128,256]{1,0:T(8,128)(2,1)S(1)} collective-permute-done((bf16[128,256]{1,0:T(8,128)(2,1)S(1)}, bf16[128,256]{1,0:T(8,128)(2,1)S(1)}, u32[]{:S(2)}, u32[]{:S(2)}) %collective-permute-start.29) | collective-permute-done | bytes 65568 | tf_op jit(solution)/shard_map/ppermute | solution.py:52
  95.9 2.2 %shard_map.120 = (bf16[512,768]{1,0:T(8,128)(2,1)}, bf16[512,768]{1,0:T(8,128)(2,1)}) custom-call(bf16[128,256]{1,0:T(8,128)(2,1)S(1)} %shard_map.119.refs_0_, bf16[128,256]{1,0:T(8,128)(2,1)S(1)} %collective-permute-done.27.refs_1_, bf16[128,256]{1,0:T(8,128)(2,1)S(1)} %collective-permute-done.28.refs_2_, ...), custom_call_target="tpu_custom_call" | custom-call | flops 201326592 | bytes 4718592 | tf_op jit(solution)/shard_map/pallas_call | solution.py:341
  (42 shorter events, 0.3 us)
Async XLA Ops:
  0.6 1.9 %copy-start = (bf16[2048,768]{1,0:T(8,128)(2,1)S(1)}, bf16[2048,768]{1,0:T(8,128)(2,1)}, u32[]{:S(2)}) copy-start(bf16[2048,768]{1,0:T(8,128)(2,1)} %refs_6_.2) | copy-start | bytes 9437188
  2.5 1.1 %copy-start.2 = (bf16[512,768]{1,0:T(8,128)(2,1)S(1)}, bf16[512,768]{1,0:T(8,128)(2,1)}, u32[]{:S(2)}) copy-start(bf16[512,768]{1,0:T(8,128)(2,1)} %refs_6_.3) | copy-start | bytes 2359300
  5.3 7.9 %collective-permute-start = (bf16[256,2048]{1,0:T(8,128)(2,1)S(1)}, bf16[256,2048]{1,0:T(8,128)(2,1)S(1)}, u32[]{:S(2)}, u32[]{:S(2)}) collective-permute-start(bf16[256,2048]{1,0:T(8,128)(2,1)S(1)} %shard_map.105), channel_id=1, source_target_pairs={{0,1},{1,0},{2,3},{3,2},{4,5},{5,4},{6,7},{7,6},{8,9},{9,8},{10,11... | collective-permute-start | bytes 3145736 | tf_op jit(solution)/shard_map/ppermute | solution.py:52
  5.9 16.1 %collective-permute-start.5 = (bf16[512,768]{1,0:T(8,128)(2,1)S(1)}, bf16[512,768]{1,0:T(8,128)(2,1)S(1)}, u32[]{:S(2)}, u32[]{:S(2)}) collective-permute-start(bf16[512,768]{1,0:T(8,128)(2,1)S(1)} %copy-done.2), channel_id=1, source_target_pairs={{0,1},{1,2},{2,3},{3,4},{4,5},{5,6},{6,7},{7,8},{8,9},{9,10},{10,1... | collective-permute-start | bytes 2359304 | tf_op jit(solution)/shard_map/ppermute | solution.py:52
  5.9 18.6 %collective-permute-start.6 = (bf16[512,768]{1,0:T(8,128)(2,1)S(1)}, bf16[512,768]{1,0:T(8,128)(2,1)S(1)}, u32[]{:S(2)}, u32[]{:S(2)}) collective-permute-start(bf16[512,768]{1,0:T(8,128)(2,1)S(1)} %copy-done.2), channel_id=1, source_target_pairs={{0,15},{1,0},{2,1},{3,2},{4,3},{5,4},{6,5},{7,6},{8,7},{9,8},{10,9... | collective-permute-start | bytes 2359304 | tf_op jit(solution)/shard_map/ppermute | solution.py:52
  13.4 29.9 %copy-start.10 = (f32[512]{0:T(512)S(1)}, f32[512]{0:T(512)}, u32[]{:S(2)}) copy-start(f32[512]{0:T(512)} %param.14) | copy-start | bytes 6148
  13.4 30.1 %copy-start.11 = (s32[512]{0:T(512)S(1)}, s32[512]{0:T(512)}, u32[]{:S(2)}) copy-start(s32[512]{0:T(512)} %param.15) | copy-start | bytes 6148
  13.4 31.1 %copy-start.8 = (f32[768]{0:T(1024)S(1)}, f32[768]{0:T(1024)}, u32[]{:S(2)}) copy-start(f32[768]{0:T(1024)} %param.12) | copy-start | bytes 9220
  13.4 31.1 %copy-start.9 = (f32[768]{0:T(1024)S(1)}, f32[768]{0:T(1024)}, u32[]{:S(2)}) copy-start(f32[768]{0:T(1024)} %param.13) | copy-start | bytes 9220
  13.5 31.1 %copy-start.3 = (bf16[512,768]{1,0:T(8,128)(2,1)S(1)}, bf16[512,768]{1,0:T(8,128)(2,1)}, u32[]{:S(2)}) copy-start(bf16[512,768]{1,0:T(8,128)(2,1)} %refs_6_.3) | copy-start | bytes 2359300
  13.5 31.1 %copy-start.4 = (bf16[512,768]{1,0:T(8,128)(2,1)S(1)}, bf16[512,768]{1,0:T(8,128)(2,1)}, u32[]{:S(2)}) copy-start(bf16[512,768]{1,0:T(8,128)(2,1)} %refs_4_.2) | copy-start | bytes 2359300
  13.5 31.1 %copy-start.7 = (bf16[2,128,128]{2,1,0:T(8,128)(2,1)S(1)}, bf16[2,128,128]{2,1,0:T(8,128)(2,1)}, u32[]{:S(2)}) copy-start(bf16[2,128,128]{2,1,0:T(8,128)(2,1)} %constant.2.clone.refs_4_) | copy-start | bytes 196612
  13.5 20.7 %collective-permute-start.4 = (bf16[64,2048]{1,0:T(8,128)(2,1)S(1)}, bf16[64,2048]{1,0:T(8,128)(2,1)S(1)}, u32[]{:S(2)}, u32[]{:S(2)}) collective-permute-start(bf16[64,2048]{1,0:T(8,128)(2,1)S(1)} %get-tuple-element.44), channel_id=1, source_target_pairs={{0,2},{1,3},{2,0},{3,1},{4,6},{5,7},{6,4},{7,5},{8,10},{9,11},{10,... | collective-permute-start | bytes 786440 | tf_op jit(solution)/shard_map/ppermute | solution.py:52
  13.7 13.8 %collective-permute-start.1 = (bf16[128,512]{1,0:T(8,128)(2,1)S(1)}, bf16[128,512]{1,0:T(8,128)(2,1)S(1)}, u32[]{:S(2)}, u32[]{:S(2)}) collective-permute-start(bf16[128,512]{1,0:T(8,128)(2,1)S(1)} %get-tuple-element.41), channel_id=1, source_target_pairs={{0,4},{1,5},{2,6},{3,7},{4,8},{5,9},{6,10},{7,11},{8,12},{9,13},{1... | collective-permute-start | bytes 393224 | tf_op jit(solution)/shard_map/ppermute | solution.py:52
  13.9 16.6 %collective-permute-start.2 = (bf16[128,512]{1,0:T(8,128)(2,1)S(1)}, bf16[128,512]{1,0:T(8,128)(2,1)S(1)}, u32[]{:S(2)}, u32[]{:S(2)}) collective-permute-start(bf16[128,512]{1,0:T(8,128)(2,1)S(1)} %get-tuple-element.42), channel_id=1, source_target_pairs={{0,8},{1,9},{2,10},{3,11},{4,12},{5,13},{6,14},{7,15},{8,0},{9,1},... | collective-permute-start | bytes 393224 | tf_op jit(solution)/shard_map/ppermute | solution.py:52
  21.9 8.7 %collective-permute-start.3 = (bf16[128,512]{1,0:T(8,128)(2,1)S(1)}, bf16[128,512]{1,0:T(8,128)(2,1)S(1)}, u32[]{:S(2)}, u32[]{:S(2)}) collective-permute-start(bf16[128,512]{1,0:T(8,128)(2,1)S(1)} %get-tuple-element.43), channel_id=1, source_target_pairs={{0,12},{1,13},{2,14},{3,15},{4,0},{5,1},{6,2},{7,3},{8,4},{9,5},{1... | collective-permute-start | bytes 393224 | tf_op jit(solution)/shard_map/ppermute | solution.py:52
  24.5 18.8 %copy-start.5 = (bf16[512,768]{1,0:T(8,128)(2,1)}, bf16[512,768]{1,0:T(8,128)(2,1)S(1)}, u32[]{:S(2)}) copy-start(bf16[512,768]{1,0:T(8,128)(2,1)S(1)} %collective-permute-done.6.refs_2_) | copy-start | bytes 2359300
  34.8 13.2 %collective-permute-start.10 = (bf16[64,512]{1,0:T(8,128)(2,1)}, bf16[64,512]{1,0:T(8,128)(2,1)S(1)}, u32[]{:S(2)}, u32[]{:S(2)}) collective-permute-start(bf16[64,512]{1,0:T(8,128)(2,1)} %get-tuple-element.54), channel_id=1, source_target_pairs={{0,2},{1,3},{2,0},{3,1},{4,6},{5,7},{6,4},{7,5},{8,10},{9,11},{10,... | collective-permute-start | bytes 196616 | tf_op jit(solution)/shard_map/ppermute | solution.py:52
  38.5 9.5 %collective-permute-start.7 = (bf16[64,512]{1,0:T(8,128)(2,1)}, bf16[64,512]{1,0:T(8,128)(2,1)}, u32[]{:S(2)}, u32[]{:S(2)}) collective-permute-start(bf16[64,512]{1,0:T(8,128)(2,1)} %get-tuple-element.47), channel_id=1, source_target_pairs={{0,4},{1,5},{2,6},{3,7},{4,8},{5,9},{6,10},{7,11},{8,12},{9,13},{1... | collective-permute-start | bytes 196616 | tf_op jit(solution)/shard_map/ppermute | solution.py:52
  39.0 9.1 %collective-permute-start.8 = (bf16[64,512]{1,0:T(8,128)(2,1)}, bf16[64,512]{1,0:T(8,128)(2,1)}, u32[]{:S(2)}, u32[]{:S(2)}) collective-permute-start(bf16[64,512]{1,0:T(8,128)(2,1)} %get-tuple-element.48), channel_id=1, source_target_pairs={{0,8},{1,9},{2,10},{3,11},{4,12},{5,13},{6,14},{7,15},{8,0},{9,1},... | collective-permute-start | bytes 196616 | tf_op jit(solution)/shard_map/ppermute | solution.py:52
  43.3 4.7 %collective-permute-start.9 = (bf16[64,512]{1,0:T(8,128)(2,1)}, bf16[64,512]{1,0:T(8,128)(2,1)}, u32[]{:S(2)}, u32[]{:S(2)}) collective-permute-start(bf16[64,512]{1,0:T(8,128)(2,1)} %get-tuple-element.49), channel_id=1, source_target_pairs={{0,12},{1,13},{2,14},{3,15},{4,0},{5,1},{6,2},{7,3},{8,4},{9,5},{1... | collective-permute-start | bytes 196616 | tf_op jit(solution)/shard_map/ppermute | solution.py:52
  44.6 1.1 %copy-start.6 = (bf16[512,768]{1,0:T(8,128)(2,1)S(1)}, bf16[512,768]{1,0:T(8,128)(2,1)}, u32[]{:S(2)}) copy-start(bf16[512,768]{1,0:T(8,128)(2,1)} %copy-done.5) | copy-start | bytes 2359300
  45.7 26.9 %copy-start.1 = (bf16[2048,768]{1,0:T(8,128)(2,1)S(1)}, bf16[2048,768]{1,0:T(8,128)(2,1)}, u32[]{:S(2)}) copy-start(bf16[2048,768]{1,0:T(8,128)(2,1)} %refs_6_.2) | copy-start | bytes 9437188
  48.1 5.5 %collective-permute-start.14 = (bf16[64,512]{1,0:T(8,128)(2,1)S(1)}, bf16[64,512]{1,0:T(8,128)(2,1)S(1)}, u32[]{:S(2)}, u32[]{:S(2)}) collective-permute-start(bf16[64,512]{1,0:T(8,128)(2,1)S(1)} %shard_map.112.refs_0_), channel_id=1, source_target_pairs={{0,2},{1,3},{2,0},{3,1},{4,6},{5,7},{6,4},{7,5},{8,10},{9,11},{10,... | collective-permute-start | bytes 196616 | tf_op jit(solution)/shard_map/ppermute | solution.py:52
  49.1 6.1 %collective-permute-start.11 = (bf16[64,512]{1,0:T(8,128)(2,1)S(1)}, bf16[64,512]{1,0:T(8,128)(2,1)S(1)}, u32[]{:S(2)}, u32[]{:S(2)}) collective-permute-start(bf16[64,512]{1,0:T(8,128)(2,1)S(1)} %shard_map.111.refs_0_), channel_id=1, source_target_pairs={{0,4},{1,5},{2,6},{3,7},{4,8},{5,9},{6,10},{7,11},{8,12},{9,13},{1... | collective-permute-start | bytes 196616 | tf_op jit(solution)/shard_map/ppermute | solution.py:52
  51.2 5.6 %collective-permute-start.12 = (bf16[64,512]{1,0:T(8,128)(2,1)S(1)}, bf16[64,512]{1,0:T(8,128)(2,1)S(1)}, u32[]{:S(2)}, u32[]{:S(2)}) collective-permute-start(bf16[64,512]{1,0:T(8,128)(2,1)S(1)} %shard_map.111.refs_0_), channel_id=1, source_target_pairs={{0,8},{1,9},{2,10},{3,11},{4,12},{5,13},{6,14},{7,15},{8,0},{9,1},... | collective-permute-start | bytes 196616 | tf_op jit(solution)/shard_map/ppermute | solution.py:52
  52.1 5.0 %collective-permute-start.13 = (bf16[64,512]{1,0:T(8,128)(2,1)S(1)}, bf16[64,512]{1,0:T(8,128)(2,1)S(1)}, u32[]{:S(2)}, u32[]{:S(2)}) collective-permute-start(bf16[64,512]{1,0:T(8,128)(2,1)S(1)} %shard_map.111.refs_0_), channel_id=1, source_target_pairs={{0,12},{1,13},{2,14},{3,15},{4,0},{5,1},{6,2},{7,3},{8,4},{9,5},{1... | collective-permute-start | bytes 196616 | tf_op jit(solution)/shard_map/ppermute | solution.py:52
  57.1 9.6 %collective-permute-start.16 = (bf16[128,512]{1,0:T(8,128)(2,1)S(1)}, bf16[128,512]{1,0:T(8,128)(2,1)S(1)}, u32[]{:S(2)}, u32[]{:S(2)}) collective-permute-start(bf16[128,512]{1,0:T(8,128)(2,1)S(1)} %shard_map.114.refs_0_), channel_id=1, source_target_pairs={{0,4},{1,5},{2,6},{3,7},{4,8},{5,9},{6,10},{7,11},{8,12},{9,13},{1... | collective-permute-start | bytes 393224 | tf_op jit(solution)/shard_map/ppermute | solution.py:52
  58.0 9.4 %collective-permute-start.17 = (bf16[128,512]{1,0:T(8,128)(2,1)S(1)}, bf16[128,512]{1,0:T(8,128)(2,1)S(1)}, u32[]{:S(2)}, u32[]{:S(2)}) collective-permute-start(bf16[128,512]{1,0:T(8,128)(2,1)S(1)} %shard_map.114.refs_0_), channel_id=1, source_target_pairs={{0,8},{1,9},{2,10},{3,11},{4,12},{5,13},{6,14},{7,15},{8,0},{9,1},... | collective-permute-start | bytes 393224 | tf_op jit(solution)/shard_map/ppermute | solution.py:52
  61.0 6.4 %collective-permute-start.18 = (bf16[128,512]{1,0:T(8,128)(2,1)S(1)}, bf16[128,512]{1,0:T(8,128)(2,1)S(1)}, u32[]{:S(2)}, u32[]{:S(2)}) collective-permute-start(bf16[128,512]{1,0:T(8,128)(2,1)S(1)} %shard_map.114.refs_0_), channel_id=1, source_target_pairs={{0,12},{1,13},{2,14},{3,15},{4,0},{5,1},{6,2},{7,3},{8,4},{9,5},{1... | collective-permute-start | bytes 393224 | tf_op jit(solution)/shard_map/ppermute | solution.py:52
  61.9 9.2 %collective-permute-start.15 = (bf16[64,2048]{1,0:T(8,128)(2,1)S(1)}, bf16[64,2048]{1,0:T(8,128)(2,1)S(1)}, u32[]{:S(2)}, u32[]{:S(2)}) collective-permute-start(bf16[64,2048]{1,0:T(8,128)(2,1)S(1)} %shard_map.113.refs_0_), channel_id=1, source_target_pairs={{0,2},{1,3},{2,0},{3,1},{4,6},{5,7},{6,4},{7,5},{8,10},{9,11},{10,... | collective-permute-start | bytes 786440 | tf_op jit(solution)/shard_map/ppermute | solution.py:52
  67.5 5.1 %collective-permute-start.21 = (bf16[128,2048]{1,0:T(8,128)(2,1)S(1)}, bf16[128,2048]{1,0:T(8,128)(2,1)S(1)}, u32[]{:S(2)}, u32[]{:S(2)}) collective-permute-start(bf16[128,2048]{1,0:T(8,128)(2,1)S(1)} %shard_map.115.refs_2_), channel_id=1, source_target_pairs={{0,1},{1,0},{2,3},{3,2},{4,5},{5,4},{6,7},{7,6},{8,9},{9,8},{10,11... | collective-permute-start | bytes 1572872 | tf_op jit(solution)/shard_map/ppermute | solution.py:52
  67.5 3.5 %collective-permute-start.19 = (bf16[64,2048]{1,0:T(8,128)(2,1)S(1)}, bf16[64,2048]{1,0:T(8,128)(2,1)S(1)}, u32[]{:S(2)}, u32[]{:S(2)}) collective-permute-start(bf16[64,2048]{1,0:T(8,128)(2,1)S(1)} %shard_map.113.refs_0_), channel_id=1, source_target_pairs={{0,1},{1,0},{2,3},{3,2},{4,5},{5,4},{6,7},{7,6},{8,9},{9,8},{10,11... | collective-permute-start | bytes 786440 | tf_op jit(solution)/shard_map/ppermute | solution.py:52
  71.1 1.5 %collective-permute-start.20 = (bf16[64,2048]{1,0:T(8,128)(2,1)S(1)}, bf16[64,2048]{1,0:T(8,128)(2,1)S(1)}, u32[]{:S(2)}, u32[]{:S(2)}) collective-permute-start(bf16[64,2048]{1,0:T(8,128)(2,1)S(1)} %collective-permute-done.15.refs_1_), channel_id=1, source_target_pairs={{0,1},{1,0},{2,3},{3,2},{4,5},{5,4},{6,7},{7,6},{8,9},{9,8},{10,11... | collective-permute-start | bytes 786440 | tf_op jit(solution)/shard_map/ppermute | solution.py:52
  75.6 1.4 %collective-permute-start.22 = (bf16[256,256]{1,0:T(8,128)(2,1)S(1)}, bf16[256,256]{1,0:T(8,128)(2,1)S(1)}, u32[]{:S(2)}, u32[]{:S(2)}) collective-permute-start(bf16[256,256]{1,0:T(8,128)(2,1)S(1)} %get-tuple-element.71), channel_id=1, source_target_pairs={{0,1},{1,0},{2,3},{3,2},{4,5},{5,4},{6,7},{7,6},{8,9},{9,8},{10,11... | collective-permute-start | bytes 393224 | tf_op jit(solution)/shard_map/ppermute | solution.py:52
  77.1 4.5 %collective-permute-start.23 = (bf16[128,256]{1,0:T(8,128)(2,1)S(1)}, bf16[128,256]{1,0:T(8,128)(2,1)S(1)}, u32[]{:S(2)}, u32[]{:S(2)}) collective-permute-start(bf16[128,256]{1,0:T(8,128)(2,1)S(1)} %get-tuple-element.73), channel_id=1, source_target_pairs={{0,2},{1,3},{2,0},{3,1},{4,6},{5,7},{6,4},{7,5},{8,10},{9,11},{10,... | collective-permute-start | bytes 196616 | tf_op jit(solution)/shard_map/ppermute | solution.py:52
  81.6 6.5 %collective-permute-start.24 = (bf16[128,256]{1,0:T(8,128)(2,1)S(1)}, bf16[128,256]{1,0:T(8,128)(2,1)S(1)}, u32[]{:S(2)}, u32[]{:S(2)}) collective-permute-start(bf16[128,256]{1,0:T(8,128)(2,1)S(1)} %get-tuple-element.75), channel_id=1, source_target_pairs={{0,4},{1,5},{2,6},{3,7},{4,8},{5,9},{6,10},{7,11},{8,12},{9,13},{1... | collective-permute-start | bytes 196616 | tf_op jit(solution)/shard_map/ppermute | solution.py:52
  83.6 6.5 %collective-permute-start.25 = (bf16[128,256]{1,0:T(8,128)(2,1)S(1)}, bf16[128,256]{1,0:T(8,128)(2,1)S(1)}, u32[]{:S(2)}, u32[]{:S(2)}) collective-permute-start(bf16[128,256]{1,0:T(8,128)(2,1)S(1)} %get-tuple-element.75), channel_id=1, source_target_pairs={{0,8},{1,9},{2,10},{3,11},{4,12},{5,13},{6,14},{7,15},{8,0},{9,1},... | collective-permute-start | bytes 196616 | tf_op jit(solution)/shard_map/ppermute | solution.py:52
  85.2 5.1 %collective-permute-start.26 = (bf16[128,256]{1,0:T(8,128)(2,1)S(1)}, bf16[128,256]{1,0:T(8,128)(2,1)S(1)}, u32[]{:S(2)}, u32[]{:S(2)}) collective-permute-start(bf16[128,256]{1,0:T(8,128)(2,1)S(1)} %get-tuple-element.75), channel_id=1, source_target_pairs={{0,12},{1,13},{2,14},{3,15},{4,0},{5,1},{6,2},{7,3},{8,4},{9,5},{1... | collective-permute-start | bytes 196616 | tf_op jit(solution)/shard_map/ppermute | solution.py:52
  90.4 4.3 %collective-permute-start.27 = (bf16[128,256]{1,0:T(8,128)(2,1)S(1)}, bf16[128,256]{1,0:T(8,128)(2,1)S(1)}, u32[]{:S(2)}, u32[]{:S(2)}) collective-permute-start(bf16[128,256]{1,0:T(8,128)(2,1)S(1)} %shard_map.119.refs_0_), channel_id=1, source_target_pairs={{0,2},{1,3},{2,0},{3,1},{4,6},{5,7},{6,4},{7,5},{8,10},{9,11},{10,... | collective-permute-start | bytes 196616 | tf_op jit(solution)/shard_map/ppermute | solution.py:52
  92.0 2.7 %collective-permute-start.28 = (bf16[128,256]{1,0:T(8,128)(2,1)S(1)}, bf16[128,256]{1,0:T(8,128)(2,1)S(1)}, u32[]{:S(2)}, u32[]{:S(2)}) collective-permute-start(bf16[128,256]{1,0:T(8,128)(2,1)S(1)} %shard_map.119.refs_0_), channel_id=1, source_target_pairs={{0,1},{1,0},{2,3},{3,2},{4,5},{5,4},{6,7},{7,6},{8,9},{9,8},{10,11... | collective-permute-start | bytes 196616 | tf_op jit(solution)/shard_map/ppermute | solution.py:52
  94.7 1.3 %collective-permute-start.29 = (bf16[128,256]{1,0:T(8,128)(2,1)S(1)}, bf16[128,256]{1,0:T(8,128)(2,1)S(1)}, u32[]{:S(2)}, u32[]{:S(2)}) collective-permute-start(bf16[128,256]{1,0:T(8,128)(2,1)S(1)} %collective-permute-done.27.refs_1_), channel_id=1, source_target_pairs={{0,1},{1,0},{2,3},{3,2},{4,5},{5,4},{6,7},{7,6},{8,9},{9,8},{10,11... | collective-permute-start | bytes 196616 | tf_op jit(solution)/shard_map/ppermute | solution.py:52

commit v6 on v5

--- a/solution.py
+++ b/solution.py
@@ -26,7 +26,10 @@
 )
 KINETIC = 0.125
 STEP_SIZE = 0.3
-VMEM_BYTES = 40 * 1024 * 1024
+MIB = 1024 * 1024
+VMEM_BYTES = 40 * MIB
+REDUCE_SHARE = 0.25
+GATHER_SHARE = 0.5
 BF16 = jnp.bfloat16
 F32 = jnp.float32
 NT = (((1,), (1,)), ((), ()))
@@ -71,8 +74,8 @@
     return pl.BlockSpec(memory_space=pltpu.VMEM)
 
 
-def params():
-    return pltpu.CompilerParams(vmem_limit_bytes=VMEM_BYTES)
+def params(size=VMEM_BYTES):
+    return pltpu.CompilerParams(vmem_limit_bytes=size)
 
 
 def cost(flops, *arrays):
@@ -120,50 +123,97 @@
             pl.BlockSpec((tile, cells), lambda i: (i, 0)),
         ],
         out_specs=pl.BlockSpec((rows, tile), lambda i: (0, i)),
-        compiler_params=params(),
+        compiler_params=params((56 if other else 40) * MIB),
         cost_estimate=cost(2 * rows * cells * count, projectors, out),
     )(response, projectors)
 
 
-def split_body(received, level, along, first, *refs):
-    keep_ref, taken, (own_ref, *sends) = refs[0], refs[1 : 1 + received], refs[1 + received :]
-    size, _ = level
+def rows_at(place, size):
+    return pl.ds(pl.multiple_of(place * size, 16), size)
+
+
+def cols_at(place, size):
+    return pl.ds(pl.multiple_of(place * size, size), size)
+
+
+def total_of(keep_ref, taken, part):
+    total = keep_ref[part]
+    for ref in taken:
+        total = total + ref[part].astype(F32)
+    return total
+
+
+def first_x_body(level, block, keep_ref, taken_ref, *outs):
     me = position(level)
-    rows, width = own_ref.shape
-    for step, out in enumerate((own_ref, *sends)):
-        at = lax.rem(me + step, jnp.int32(size))
+    rows = outs[0].shape[0]
+    for step, out in enumerate(outs):
+        at = lax.rem(me + step, jnp.int32(level[0])) * block
+        part = (pl.ds(pl.multiple_of(at, 16), rows), slice(None))
+        out[...] = total_of(keep_ref, [taken_ref], part).astype(out.dtype)
+
+
+def first_z_body(level, block, first, keep_ref, taken_ref, *outs):
+    me = position(level)
+    rows = block - first
+    width = outs[0].shape[1]
+    for step, out in enumerate(outs):
+        cols = cols_at(lax.rem(me + step, jnp.int32(level[0])), width)
+        for i in range(out.shape[0] // rows):
+            part = (slice(i * block + first, (i + 1) * block), cols)
+            mine = slice(i * rows, (i + 1) * rows)
+            out[mine, :] = total_of(keep_ref, [taken_ref], part).astype(out.dtype)
+
+
+def split_body(received, level, along, *refs):
+    keep_ref, taken, outs = refs[0], refs[1 : 1 + received], refs[1 + received :]
+    me = position(level)
+    rows, width = outs[0].shape
+    for step, out in enumerate(outs):
+        at = lax.rem(me + step, jnp.int32(level[0]))
         if along == 0:
-            part = (pl.ds(pl.multiple_of(at * rows + first, 16), rows), slice(None))
+            part = (rows_at(at, rows), slice(None))
         else:
-            part = (slice(first, first + rows), pl.ds(pl.multiple_of(at * width, width), width))
-        total = keep_ref[part]
-        for ref in taken:
-            total = total + ref[part].astype(F32)
-        out[...] = total.astype(out.dtype)
-
-
-def split(keep, taken, level, along, rows=None, first=0):
-    size, _ = level
-    shape = [rows or keep.shape[0], keep.shape[1]]
-    shape[along] //= size
-    outs = [struct(shape, F32)] + [struct(shape, BF16)] * (size - 1)
+            part = (slice(None), cols_at(at, width))
+        out[...] = total_of(keep_ref, taken, part).astype(out.dtype)
+
+
+def shares_of(shape, count):
+    return [struct(shape, F32)] + [struct(shape, BF16)] * (count - 1)
+
+
+def split(keep, taken, level, along):
+    shape = list(keep.shape)
+    shape[along] //= level[0]
     return local_call(
-        functools.partial(split_body, len(taken), level, along, first), outs, [keep, *taken]
+        functools.partial(split_body, len(taken), level, along),
+        shares_of(shape, level[0]),
+        [keep, *taken],
     )
 
 
 def finish_body(scale, keep_ref, *refs):
     *taken, out_ref = refs
-    total = keep_ref[...]
-    for ref in taken:
-        total = total + ref[...].astype(F32)
-    out_ref[...] = (total * scale).astype(out_ref.dtype)
+    out_ref[...] = (total_of(keep_ref, taken, ...) * scale).astype(out_ref.dtype)
 
 
 def finish(keep, taken, scale):
     return local_call(
         functools.partial(finish_body, scale), struct(keep.shape, BF16), [keep, *taken]
     )
+
+
+def finish_both_body(scale, received, *refs):
+    outs = refs[-2:]
+    cut = outs[0].shape[0]
+    row = 0
+    for keep_ref, *taken in (refs[: 1 + received], refs[1 + received : -2]):
+        low = (total_of(keep_ref, taken, ...) * scale).astype(BF16)
+        end = row + keep_ref.shape[0]
+        for out, first, last in ((outs[0], 0, cut), (outs[1], cut, cut + outs[1].shape[0])):
+            top, bottom = max(row, first), min(end, last)
+            if top < bottom:
+                out[top - first : bottom - first, :] = low[top - row : bottom - row, :]
+        row = end
 
 
 def place_body(level, along, *refs):
@@ -252,22 +302,25 @@
     return max(0, min(group * group_rows - REACH * blk, bands - width))
 
 
-def apply_body(core, across, rows_x, group_rows, width, blk, *refs):
+def apply_body(core, across, block, group_rows, width, blk, *refs):
     size = across[0]
     blocks = refs[: 2 * (size + 1)]
     p_ref, base_ref, o_ref, u_ref, send_ref, keep_ref, c_ref, s_ref = refs[2 * (size + 1) :]
     bands, cells = u_ref.shape
     c, x = position(core), position(across)
     half = bands // 2
-    share = rows_x // size
+    first = blocks[0].shape[0]
     for k, ref in enumerate(blocks):
         side, step = divmod(k, size + 1)
         at = (c if side == 0 else 1 - c) * half
         if step < size:
-            at = at + lax.rem(x - step + size, jnp.int32(size)) * share
+            at = at + lax.rem(x - step + size, jnp.int32(size)) * block
+            c_ref[pl.ds(pl.multiple_of(at, 16), first), :] = ref[...]
         else:
-            at = at + rows_x
-        c_ref[pl.ds(pl.multiple_of(at, 16), ref.shape[0]), :] = ref[...]
+            rest = block - first
+            for i in range(size):
+                there = pl.ds(pl.multiple_of(at + i * block + first, 16), rest)
+                c_ref[there, :] = ref[i * rest : (i + 1) * rest, :]
     tile = 256 if cells % 256 == 0 else 128
     for t in range(cells // tile):
         cols = slice(t * tile, (t + 1) * tile)
@@ -371,8 +424,9 @@
     group_rows = GROUP_BLOCKS * blk
     width = (GROUP_BLOCKS + 2 * REACH) * blk
     half = bands // 2
-    rows_x = half // 2
-    rows_z = half - rows_x
+    block = half // across[0]
+    first = max(16, round(REDUCE_SHARE * block / 16) * 16)
+    gather_first = max(16, round(GATHER_SHARE * block / 16) * 16)
     matrix = jnp.asarray(plane_matrix())
     lines = (potential[None, :], perturbing[None, :])
     columns = tuple(a[:, None] for a in (energies, window_start, block_count))
@@ -388,34 +442,48 @@
 
     sent = shifted(partial_intersections(response, projectors, core, True), count, core, 1)
     keep = partial_intersections(response, projectors, core, False)
-    keep_z, *parts_z = split(keep, [sent], along, 1, rows_z, rows_x)
-    keep_x, *parts_x = split(keep, [sent], across, 0, rows_x, 0)
+    keep_z, *parts_z = local_call(
+        functools.partial(first_z_body, along, block, first),
+        shares_of((half - across[0] * first, projections // along[0]), along[0]),
+        [keep, sent],
+    )
+    keep_x, *parts_x = local_call(
+        functools.partial(first_x_body, across, block),
+        shares_of((first, projections), across[0]),
+        [keep, sent],
+    )
     taken_z, taken_x, low, high = lax.optimization_barrier(
         (parts_to(parts_z, along), parts_to(parts_x, across), low, high)
     )
+    keep_x, *parts_x = split(keep_x, taken_x, along, 1)
+    keep_z, *parts_z = split(keep_z, taken_z, across, 0)
+    taken_x, taken_z = lax.optimization_barrier(
+        (parts_to(parts_x, along), parts_to(parts_z, across))
+    )
+    share_x, share_z = local_call(
+        functools.partial(finish_both_body, ace_scale, len(taken_x)),
+        [
+            struct((gather_first, projections // along[0]), BF16),
+            struct((block - gather_first, projections // along[0]), BF16),
+        ],
+        [keep_x, *taken_x, keep_z, *taken_z],
+    )
+
+    pieces_x, pieces_z, low, high = lax.optimization_barrier(
+        ([share_x, *to(share_x, along)], [share_z, *to(share_z, across)], low, high)
+    )
     base, mask = local_part(
         response, low, high, orbitals, matrix, lines, columns, group_rows, width, blk
-    )
-    keep_x, *parts_x = split(keep_x, taken_x, along, 1)
-    keep_z, *parts_z = split(keep_z, taken_z, across, 0)
-    taken_x, taken_z, base = lax.optimization_barrier(
-        (parts_to(parts_x, along), parts_to(parts_z, across), base)
-    )
-    share_z = finish(keep_z, taken_z, ace_scale)
-    share_x = finish(keep_x, taken_x, ace_scale)
-
-    pieces_x, pieces_z = lax.optimization_barrier(
-        ([share_x, *to(share_x, along)], [share_z, *to(share_z, across)])
     )
     block_x = place(pieces_x, along, 1)
     block_z = place(pieces_z, across, 0)
     blocks_x = [block_x, *to(block_x, across)]
-    block_z = place([block_z, *to(block_z, along)], along, 1)
-    blocks = [*blocks_x, block_z]
-    blocks += [shifted(block, count, core, 1) for block in blocks]
+    pieces_z, base = lax.optimization_barrier(([block_z, *to(block_z, along)], base))
+    blocks = [*blocks_x, place(pieces_z, along, 1)]
+    blocks += [shifted(part, count, core, 1) for part in blocks]
 
     unprojected, send, keep = local_call(
-        functools.partial(apply_body, core, across, rows_x, group_rows, width, blk),
+        functools.partial(apply_body, core, across, block, group_rows, width, blk),
         [
             struct((bands, local_cells), F32),
             struct((half, width), BF16),
@@ -429,7 +497,7 @@
     total, low = add_up(keep, parts_to(parts, across))
     weights = finish(total, to(low, along), window_scale)
     weights = [weights, *to(weights, across)]
-    weights += [shifted(block, count, core, 1) for block in weights]
+    weights += [shifted(part, count, core, 1) for part in weights]
     return project(
         weights, orbitals, unprojected, response, mask, core, across, group_rows, blk
     )

time: 98.5 us -> 108 us (1.096)
  local copies, waits for them, and re-layouts: 5.32 us -> 14.1 us
  starting transfers between devices: 42.7 us -> 35.3 us
  waiting for transfers between devices: 35.5 us -> 40.8 us
  Pallas kernels: 13.7 us -> 15.9 us
    ppermute x30, starting transfers between devices: 42.7 us -> 35.3 us  [shifted(): return lax.ppermute(array, 'band', pairs)]
    unnamed x24 -> x50, local copies, waits for them, and re-layouts: 4.2 us -> 11.6 us
    ppermute x30, waiting for transfers between devices: 35.5 us -> 40.8 us  [shifted(): return lax.ppermute(array, 'band', pairs)]
    pallas_call x2, Pallas kernels: 3.44 us -> 6.83 us  [partial_intersections(): pl.pallas_call(functools.partial(partial_body, core, other), grid=(count...]
    broadcast_in_dim x3, local copies, waits for them, and re-layouts: 1.12 us -> 2.57 us  [shards(): columns = tuple((a[:, None] for a in (energies, window_start, block_count)))]
    pallas_call x13 -> x12, Pallas kernels: 5.72 us -> 4.56 us  [local_call(): pl.pallas_call(body, out_shape=outs, in_specs=[whole() for _ in args], ou...]
  transfers between devices with their start and end apart: 30 -> 30, of which waited for: 17 -> 19; matrix products, arithmetic and copies ran while one was open for 1% -> 2% of each run, Pallas kernels for 6% -> 5%
where the time goes in v6:
time: 108 us; the launch traced here: 107 us
  waiting for transfers between devices  40.8 us (38%)
  starting transfers between devices  35.3 us (33%)
  Pallas kernels  15.9 us (15%)
  local copies, waits for them, and re-layouts  14.1 us (13%)
    ppermute x30, waiting for transfers between devices, shifted(): return lax.ppermute(array, 'band', pairs)  40.8 us
    ppermute x30, starting transfers between devices, shifted(): return lax.ppermute(array, 'band', pairs)  35.3 us
    unnamed x50, local copies, waits for them, and re-layouts  11.6 us
    pallas_call x2, Pallas kernels, partial_intersections(): pl.pallas_call(functools.partial(partial_body, core, other), grid=(count...  6.83 us
    pallas_call x12, Pallas kernels, local_call(): pl.pallas_call(body, out_shape=outs, in_specs=[whole() for _ in args], ou...  4.56 us
    broadcast_in_dim x3, local copies, waits for them, and re-layouts, shards(): columns = tuple((a[:, None] for a in (energies, window_start, block_count)))  2.57 us
    pallas_call x1, Pallas kernels, local_part(): pl.pallas_call(functools.partial(local_body, depth, (group_rows, width, b...  2.28 us
    pallas_call x1, Pallas kernels, project(): pl.pallas_call(functools.partial(project_body, core, across, width, blk),...  2.28 us
  transfers between devices with their start and end apart: 30, of which 19 were waited for; matrix products, arithmetic and copies ran while one was open for 2% of the time, Pallas kernels for 5%

profile of v6, /device:TPU:0, one launch (start us, length us, event | category | flops | bytes accessed | tf_op | source)
XLA Modules:
  0.0 107.1 jit_solution(7701349597664737709)
XLA Ops:
  0.7 5.1 %shard_map.105 = bf16[256,2048]{1,0:T(8,128)(2,1)} custom-call(bf16[512,768]{1,0:T(8,128)(2,1)} %refs_6_.3, bf16[2048,768]{1,0:T(8,128)(2,1)} %refs_6_.2), custom_call_target="tpu_custom_call" | custom-call | flops 805306368 | bytes 4194304 | tf_op jit(solution)/shard_map/pallas_call | solution.py:117
  5.7 0.5 collective-permute-start
  6.2 5.6 %collective-permute-start.6 = (bf16[512,768]{1,0:T(8,128)(2,1)S(1)}, bf16[512,768]{1,0:T(8,128)(2,1)S(1)}, u32[]{:S(2)}, u32[]{:S(2)}) collective-permute-start(bf16[512,768]{1,0:T(8,128)(2,1)S(1)} %copy-done.1), channel_id=1, source_target_pairs={{0,15},{1,0},{2,1},{3,2},{4,3},{5,4},{6,5},{7,6},{8,7},{9,8},{10,9... | collective-permute-start | bytes 2359304 | tf_op jit(solution)/shard_map/ppermute | solution.py:55
  11.8 1.8 %shard_map.104.keep_ref = f32[256,2048]{1,0:T(8,128)S(1)} custom-call(bf16[512,768]{1,0:T(8,128)(2,1)S(1)} %copy-done.1, bf16[2048,768]{1,0:T(8,128)(2,1)S(1)} %copy-done), custom_call_target="tpu_custom_call" | custom-call | flops 805306368 | bytes 5242880 | tf_op jit(solution)/shard_map/pallas_call | solution.py:117
  13.6 0.2 shard_map.107
  13.9 2.2 %collective-permute-start.2 = (bf16[192,512]{1,0:T(8,128)(2,1)S(1)}, bf16[192,512]{1,0:T(8,128)(2,1)S(1)}, u32[]{:S(2)}, u32[]{:S(2)}) collective-permute-start(bf16[192,512]{1,0:T(8,128)(2,1)S(1)} %get-tuple-element.50), channel_id=1, source_target_pairs={{0,8},{1,9},{2,10},{3,11},{4,12},{5,13},{6,14},{7,15},{8,0},{9,1},... | collective-permute-start | bytes 589832 | tf_op jit(solution)/shard_map/ppermute | solution.py:55
  16.1 1.6 %collective-permute-start.3 = (bf16[192,512]{1,0:T(8,128)(2,1)S(1)}, bf16[192,512]{1,0:T(8,128)(2,1)S(1)}, u32[]{:S(2)}, u32[]{:S(2)}) collective-permute-start(bf16[192,512]{1,0:T(8,128)(2,1)S(1)} %get-tuple-element.51), channel_id=1, source_target_pairs={{0,12},{1,13},{2,14},{3,15},{4,0},{5,1},{6,2},{7,3},{8,4},{9,5},{1... | collective-permute-start | bytes 589832 | tf_op jit(solution)/shard_map/ppermute | solution.py:55
  17.7 8.1 %collective-permute-done.5.refs_1_ = bf16[512,768]{1,0:T(8,128)(2,1)S(1)} collective-permute-done((bf16[512,768]{1,0:T(8,128)(2,1)S(1)}, bf16[512,768]{1,0:T(8,128)(2,1)S(1)}, u32[]{:S(2)}, u32[]{:S(2)}) %collective-permute-start.5) | collective-permute-done | bytes 786464 | tf_op jit(solution)/shard_map/ppermute | solution.py:55
  25.8 0.9 copy-done.8
  26.7 0.6 collective-permute-done.6.refs_2_
  27.3 4.4 %collective-permute-done.4.refs_1_ = bf16[32,2048]{1,0:T(8,128)(2,1)S(1)} collective-permute-done((bf16[32,2048]{1,0:T(8,128)(2,1)S(1)}, bf16[32,2048]{1,0:T(8,128)(2,1)S(1)}, u32[]{:S(2)}, u32[]{:S(2)}) %collective-permute-start.4) | collective-permute-done | bytes 131104 | tf_op jit(solution)/shard_map/ppermute | solution.py:55
  31.7 0.3 collective-permute-done.1.refs_1_
  32.0 5.2 %collective-permute-done.2.refs_2_ = bf16[192,512]{1,0:T(8,128)(2,1)S(1)} collective-permute-done((bf16[192,512]{1,0:T(8,128)(2,1)S(1)}, bf16[192,512]{1,0:T(8,128)(2,1)S(1)}, u32[]{:S(2)}, u32[]{:S(2)}) %collective-permute-start.2) | collective-permute-done | bytes 196640 | tf_op jit(solution)/shard_map/ppermute | solution.py:55
  37.2 0.1 shard_map.109
  37.3 0.1 collective-permute-start.10
  37.4 2.7 %collective-permute-start.7 = (bf16[32,512]{1,0:T(8,128)(2,1)S(1)}, bf16[32,512]{1,0:T(8,128)(2,1)S(1)}, u32[]{:S(2)}, u32[]{:S(2)}) collective-permute-start(bf16[32,512]{1,0:T(8,128)(2,1)S(1)} %get-tuple-element.55), channel_id=1, source_target_pairs={{0,4},{1,5},{2,6},{3,7},{4,8},{5,9},{6,10},{7,11},{8,12},{9,13},{1... | collective-permute-start | bytes 98312 | tf_op jit(solution)/shard_map/ppermute | solution.py:55
  40.1 2.9 %collective-permute-start.8 = (bf16[32,512]{1,0:T(8,128)(2,1)S(1)}, bf16[32,512]{1,0:T(8,128)(2,1)S(1)}, u32[]{:S(2)}, u32[]{:S(2)}) collective-permute-start(bf16[32,512]{1,0:T(8,128)(2,1)S(1)} %get-tuple-element.56), channel_id=1, source_target_pairs={{0,8},{1,9},{2,10},{3,11},{4,12},{5,13},{6,14},{7,15},{8,0},{9,1},... | collective-permute-start | bytes 98312 | tf_op jit(solution)/shard_map/ppermute | solution.py:55
  43.1 1.7 %collective-permute-done.7.refs_1_ = bf16[32,512]{1,0:T(8,128)(2,1)S(1)} collective-permute-done((bf16[32,512]{1,0:T(8,128)(2,1)S(1)}, bf16[32,512]{1,0:T(8,128)(2,1)S(1)}, u32[]{:S(2)}, u32[]{:S(2)}) %collective-permute-start.7) | collective-permute-done | bytes 32800 | tf_op jit(solution)/shard_map/ppermute | solution.py:55
  44.7 0.6 collective-permute-done.8.refs_2_
  45.3 1.6 %collective-permute-done.9.refs_3_ = bf16[32,512]{1,0:T(8,128)(2,1)S(1)} collective-permute-done((bf16[32,512]{1,0:T(8,128)(2,1)S(1)}, bf16[32,512]{1,0:T(8,128)(2,1)S(1)}, u32[]{:S(2)}, u32[]{:S(2)}) %collective-permute-start.9) | collective-permute-done | bytes 32800 | tf_op jit(solution)/shard_map/ppermute | solution.py:55
  47.0 0.1 collective-permute-start.11
  47.2 2.6 %collective-permute-start.12 = (bf16[64,512]{1,0:T(8,128)(2,1)S(1)}, bf16[64,512]{1,0:T(8,128)(2,1)S(1)}, u32[]{:S(2)}, u32[]{:S(2)}) collective-permute-start(bf16[64,512]{1,0:T(8,128)(2,1)S(1)} %get-tuple-element.72.refs_0_), channel_id=1, source_target_pairs={{0,8},{1,9},{2,10},{3,11},{4,12},{5,13},{6,14},{7,15},{8,0},{9,1},... | collective-permute-start | bytes 196616 | tf_op jit(solution)/shard_map/ppermute | solution.py:55
  49.8 1.1 %collective-permute-start.13 = (bf16[64,512]{1,0:T(8,128)(2,1)S(1)}, bf16[64,512]{1,0:T(8,128)(2,1)S(1)}, u32[]{:S(2)}, u32[]{:S(2)}) collective-permute-start(bf16[64,512]{1,0:T(8,128)(2,1)S(1)} %get-tuple-element.72.refs_0_), channel_id=1, source_target_pairs={{0,12},{1,13},{2,14},{3,15},{4,0},{5,1},{6,2},{7,3},{8,4},{9,5},{1... | collective-permute-start | bytes 196616 | tf_op jit(solution)/shard_map/ppermute | solution.py:55
  50.9 2.0 %collective-permute-start.14 = (bf16[64,512]{1,0:T(8,128)(2,1)S(1)}, bf16[64,512]{1,0:T(8,128)(2,1)S(1)}, u32[]{:S(2)}, u32[]{:S(2)}) collective-permute-start(bf16[64,512]{1,0:T(8,128)(2,1)S(1)} %get-tuple-element.76.refs_0_), channel_id=1, source_target_pairs={{0,2},{1,3},{2,0},{3,1},{4,6},{5,7},{6,4},{7,5},{8,10},{9,11},{10,... | collective-permute-start | bytes 196616 | tf_op jit(solution)/shard_map/ppermute | solution.py:55
  52.9 0.2 collective-permute-done.11.refs_1_
  53.2 0.9 collective-permute-done.13.refs_3_
  54.1 1.1 %collective-permute-done.14.refs_1_ = bf16[64,512]{1,0:T(8,128)(2,1)S(1)} collective-permute-done((bf16[64,512]{1,0:T(8,128)(2,1)S(1)}, bf16[64,512]{1,0:T(8,128)(2,1)S(1)}, u32[]{:S(2)}, u32[]{:S(2)}) %collective-permute-start.14) | collective-permute-done | bytes 65568 | tf_op jit(solution)/shard_map/ppermute | solution.py:55
  55.2 1.1 collective-permute-start.16
  56.3 1.9 %collective-permute-start.17 = (bf16[128,512]{1,0:T(8,128)(2,1)S(1)}, bf16[128,512]{1,0:T(8,128)(2,1)}, u32[]{:S(2)}, u32[]{:S(2)}) collective-permute-start(bf16[128,512]{1,0:T(8,128)(2,1)S(1)} %shard_map.112.refs_0_), channel_id=1, source_target_pairs={{0,8},{1,9},{2,10},{3,11},{4,12},{5,13},{6,14},{7,15},{8,0},{9,1},... | collective-permute-start | bytes 393224 | tf_op jit(solution)/shard_map/ppermute | solution.py:55
  58.2 2.0 %collective-permute-start.18 = (bf16[128,512]{1,0:T(8,128)(2,1)S(1)}, bf16[128,512]{1,0:T(8,128)(2,1)}, u32[]{:S(2)}, u32[]{:S(2)}) collective-permute-start(bf16[128,512]{1,0:T(8,128)(2,1)S(1)} %shard_map.112.refs_0_), channel_id=1, source_target_pairs={{0,12},{1,13},{2,14},{3,15},{4,0},{5,1},{6,2},{7,3},{8,4},{9,5},{1... | collective-permute-start | bytes 393224 | tf_op jit(solution)/shard_map/ppermute | solution.py:55
  60.2 0.1 copy.11.refs_7_
  60.4 0.9 copy.12.refs_8_
  61.3 1.5 %copy.13.refs_9_ = s32[512,1]{1,0:T(8,128)} copy(s32[512,1]{0,1:T(1,128)} %bitcast.5) | data formatting | bytes 4096 | tf_op jit(solution)/shard_map/broadcast_in_dim | solution.py:432
  62.8 0.8 copy-done.14
  63.7 0.8 copy-done.16
  64.5 0.8 copy-done.18
  65.4 0.8 copy-done.20
  66.2 3.1 %collective-permute-start.15 = (bf16[64,2048]{1,0:T(8,128)(2,1)S(1)}, bf16[64,2048]{1,0:T(8,128)(2,1)S(1)}, u32[]{:S(2)}, u32[]{:S(2)}) collective-permute-start(bf16[64,2048]{1,0:T(8,128)(2,1)S(1)} %shard_map.111.refs_0_), channel_id=1, source_target_pairs={{0,2},{1,3},{2,0},{3,1},{4,6},{5,7},{6,4},{7,5},{8,10},{9,11},{10,... | collective-permute-start | bytes 786440 | tf_op jit(solution)/shard_map/ppermute | solution.py:55
  69.4 1.1 %copy-done.2 = bf16[512,768]{1,0:T(8,128)(2,1)S(1)} copy-done((bf16[512,768]{1,0:T(8,128)(2,1)S(1)}, bf16[512,768]{1,0:T(8,128)(2,1)}, u32[]{:S(2)}) %copy-start.2) | copy-done | bytes 786456
  70.5 1.1 %copy-done.4 = bf16[512,768]{1,0:T(8,128)(2,1)S(1)} copy-done((bf16[512,768]{1,0:T(8,128)(2,1)S(1)}, bf16[512,768]{1,0:T(8,128)(2,1)}, u32[]{:S(2)}) %copy-start.4) | copy-done | bytes 786456
  71.6 0.9 copy-done.6
  72.6 0.9 copy-done.7
  73.5 1.1 %copy-done.9 = bf16[512,768]{1,0:T(8,128)(2,1)S(1)} copy-done((bf16[512,768]{1,0:T(8,128)(2,1)S(1)}, bf16[512,768]{1,0:T(8,128)(2,1)}, u32[]{:S(2)}) %copy-start.9) | copy-done | bytes 786456
  74.7 1.1 %copy-done.11 = bf16[512,768]{1,0:T(8,128)(2,1)S(1)} copy-done((bf16[512,768]{1,0:T(8,128)(2,1)S(1)}, bf16[512,768]{1,0:T(8,128)(2,1)}, u32[]{:S(2)}) %copy-start.11) | copy-done | bytes 786456
  75.8 0.8 copy-done.12
  76.6 2.3 %shard_map.113 = (f32[512,768]{1,0:T(8,128)S(1)}, bf16[512,256]{1,0:T(8,128)(2,1)S(1)}) custom-call(bf16[512,768]{1,0:T(8,128)(2,1)S(1)} %copy-done.2, bf16[512,768]{1,0:T(8,128)(2,1)S(1)} %copy-done.9, bf16[512,768]{1,0:T(8,128)(2,1)S(1)} %copy-done.11, bf16[512,768]{1,0:T(8,128)(2,1)S(1)} %copy-done.4, bf16[2,128,128]{2,1,0:T(8,128)(2,1)S(1)} %copy-done.12, ...), custom_call_target="tpu_custom_call" | custom-call | flops 235929600 | bytes 4980736 | tf_op jit(solution)/shard_map/pallas_call | solution.py:279
  78.9 1.1 %shard_map.114.refs_2_ = bf16[128,2048]{1,0:T(8,128)(2,1)S(1)} custom-call(bf16[128,512]{1,0:T(8,128)(2,1)S(1)} %shard_map.112.refs_0_, bf16[128,512]{1,0:T(8,128)(2,1)} %collective-permute-done.16.refs_1_, bf16[128,512]{1,0:T(8,128)(2,1)} %collective-permute-done.17.refs_2_, bf16[128,512]{1,0:T(8,128)(2,1)} %collective-permute-done.18.refs_3_), custom_call_target="tpu_custom_call" | custom-call | bytes 1048576 | tf_op jit(solution)/shard_map/pallas_call | solution.py:87
  80.1 0.5 collective-permute-start.19
  80.6 0.1 collective-permute-start.20
  80.7 1.7 %collective-permute-done.19.refs_3_ = bf16[64,2048]{1,0:T(8,128)(2,1)S(1)} collective-permute-done((bf16[64,2048]{1,0:T(8,128)(2,1)S(1)}, bf16[64,2048]{1,0:T(8,128)(2,1)S(1)}, u32[]{:S(2)}, u32[]{:S(2)}) %collective-permute-start.19) | collective-permute-done | bytes 262176 | tf_op jit(solution)/shard_map/ppermute | solution.py:55
  82.4 0.4 collective-permute-done.20.refs_4_
  82.8 3.0 %shard_map.115 = (f32[512,768]{1,0:T(8,128)S(1)}, bf16[256,256]{1,0:T(8,128)(2,1)S(1)}, f32[256,256]{1,0:T(8,128)S(1)}) custom-call(bf16[64,2048]{1,0:T(8,128)(2,1)S(1)} %shard_map.111.refs_0_, bf16[64,2048]{1,0:T(8,128)(2,1)S(1)} %collective-permute-done.15.refs_1_, bf16[128,2048]{1,0:T(8,128)(2,1)S(1)} %shard_map.114.refs_2_, ...), custom_call_target="tpu_custom_call" | custom-call | flops 1811939328 | bytes 9568256 | tf_op jit(solution)/shard_map/pallas_call | solution.py:87
  85.8 0.2 collective-permute-start.22
  86.0 1.2 %collective-permute-done.22.refs_1_ = bf16[256,256]{1,0:T(8,128)(2,1)S(1)} collective-permute-done((bf16[256,256]{1,0:T(8,128)(2,1)S(1)}, bf16[256,256]{1,0:T(8,128)(2,1)S(1)}, u32[]{:S(2)}, u32[]{:S(2)}) %collective-permute-start.22) | collective-permute-done | bytes 131104 | tf_op jit(solution)/shard_map/ppermute | solution.py:55
  87.2 0.1 collective-permute-start.23
  87.3 4.2 %collective-permute-done.23.refs_0_ = bf16[128,256]{1,0:T(8,128)(2,1)S(1)} collective-permute-done((bf16[128,256]{1,0:T(8,128)(2,1)S(1)}, bf16[128,256]{1,0:T(8,128)(2,1)S(1)}, u32[]{:S(2)}, u32[]{:S(2)}) %collective-permute-start.23) | collective-permute-done | bytes 65568 | tf_op jit(solution)/shard_map/ppermute | solution.py:55
  91.6 2.5 %collective-permute-start.25 = (bf16[128,256]{1,0:T(8,128)(2,1)S(1)}, bf16[128,256]{1,0:T(8,128)(2,1)S(1)}, u32[]{:S(2)}, u32[]{:S(2)}) collective-permute-start(bf16[128,256]{1,0:T(8,128)(2,1)S(1)} %get-tuple-element.91), channel_id=1, source_target_pairs={{0,8},{1,9},{2,10},{3,11},{4,12},{5,13},{6,14},{7,15},{8,0},{9,1},... | collective-permute-start | bytes 196616 | tf_op jit(solution)/shard_map/ppermute | solution.py:55
  94.1 1.3 %collective-permute-start.26 = (bf16[128,256]{1,0:T(8,128)(2,1)S(1)}, bf16[128,256]{1,0:T(8,128)(2,1)S(1)}, u32[]{:S(2)}, u32[]{:S(2)}) collective-permute-start(bf16[128,256]{1,0:T(8,128)(2,1)S(1)} %get-tuple-element.91), channel_id=1, source_target_pairs={{0,12},{1,13},{2,14},{3,15},{4,0},{5,1},{6,2},{7,3},{8,4},{9,5},{1... | collective-permute-start | bytes 196616 | tf_op jit(solution)/shard_map/ppermute | solution.py:55
  95.4 2.5 %collective-permute-done.24.refs_0_ = bf16[128,256]{1,0:T(8,128)(2,1)S(1)} collective-permute-done((bf16[128,256]{1,0:T(8,128)(2,1)S(1)}, bf16[128,256]{1,0:T(8,128)(2,1)S(1)}, u32[]{:S(2)}, u32[]{:S(2)}) %collective-permute-start.24) | collective-permute-done | bytes 65568 | tf_op jit(solution)/shard_map/ppermute | solution.py:55
  97.9 1.2 %collective-permute-done.25.refs_1_ = bf16[128,256]{1,0:T(8,128)(2,1)S(1)} collective-permute-done((bf16[128,256]{1,0:T(8,128)(2,1)S(1)}, bf16[128,256]{1,0:T(8,128)(2,1)S(1)}, u32[]{:S(2)}, u32[]{:S(2)}) %collective-permute-start.25) | collective-permute-done | bytes 65568 | tf_op jit(solution)/shard_map/ppermute | solution.py:55
  99.2 0.8 collective-permute-start.27
  100.0 3.5 %collective-permute-done.27.refs_1_ = bf16[128,256]{1,0:T(8,128)(2,1)S(1)} collective-permute-done((bf16[128,256]{1,0:T(8,128)(2,1)S(1)}, bf16[128,256]{1,0:T(8,128)(2,1)S(1)}, u32[]{:S(2)}, u32[]{:S(2)}) %collective-permute-start.27) | collective-permute-done | bytes 65568 | tf_op jit(solution)/shard_map/ppermute | solution.py:55
  103.5 1.2 %collective-permute-done.29.refs_3_ = bf16[128,256]{1,0:T(8,128)(2,1)S(1)} collective-permute-done((bf16[128,256]{1,0:T(8,128)(2,1)S(1)}, bf16[128,256]{1,0:T(8,128)(2,1)S(1)}, u32[]{:S(2)}, u32[]{:S(2)}) %collective-permute-start.29) | collective-permute-done | bytes 65568 | tf_op jit(solution)/shard_map/ppermute | solution.py:55
  104.8 2.3 %shard_map.119 = (bf16[512,768]{1,0:T(8,128)(2,1)}, bf16[512,768]{1,0:T(8,128)(2,1)}) custom-call(bf16[128,256]{1,0:T(8,128)(2,1)S(1)} %shard_map.118.refs_0_, bf16[128,256]{1,0:T(8,128)(2,1)S(1)} %collective-permute-done.27.refs_1_, bf16[128,256]{1,0:T(8,128)(2,1)S(1)} %collective-permute-done.28.refs_2_, ...), custom_call_target="tpu_custom_call" | custom-call | flops 201326592 | bytes 4718592 | tf_op jit(solution)/shard_map/pallas_call | solution.py:394
  (67 shorter events, 0.6 us)
Async XLA Ops:
  0.6 11.2 %copy-start = (bf16[2048,768]{1,0:T(8,128)(2,1)S(1)}, bf16[2048,768]{1,0:T(8,128)(2,1)}, u32[]{:S(2)}) copy-start(bf16[2048,768]{1,0:T(8,128)(2,1)} %refs_6_.2) | copy-start | bytes 9437188
  0.6 5.5 %copy-start.1 = (bf16[512,768]{1,0:T(8,128)(2,1)S(1)}, bf16[512,768]{1,0:T(8,128)(2,1)}, u32[]{:S(2)}) copy-start(bf16[512,768]{1,0:T(8,128)(2,1)} %refs_6_.3) | copy-start | bytes 2359300
  5.7 7.9 %collective-permute-start = (bf16[256,2048]{1,0:T(8,128)(2,1)}, bf16[256,2048]{1,0:T(8,128)(2,1)S(1)}, u32[]{:S(2)}, u32[]{:S(2)}) collective-permute-start(bf16[256,2048]{1,0:T(8,128)(2,1)} %shard_map.105), channel_id=1, source_target_pairs={{0,1},{1,0},{2,3},{3,2},{4,5},{5,4},{6,7},{7,6},{8,9},{9,8},{10,11... | collective-permute-start | bytes 3145736 | tf_op jit(solution)/shard_map/ppermute | solution.py:55
  6.2 19.6 %collective-permute-start.5 = (bf16[512,768]{1,0:T(8,128)(2,1)S(1)}, bf16[512,768]{1,0:T(8,128)(2,1)S(1)}, u32[]{:S(2)}, u32[]{:S(2)}) collective-permute-start(bf16[512,768]{1,0:T(8,128)(2,1)S(1)} %copy-done.1), channel_id=1, source_target_pairs={{0,1},{1,2},{2,3},{3,4},{4,5},{5,6},{6,7},{7,8},{8,9},{9,10},{10,1... | collective-permute-start | bytes 2359304 | tf_op jit(solution)/shard_map/ppermute | solution.py:55
  6.2 21.1 %collective-permute-start.6 = (bf16[512,768]{1,0:T(8,128)(2,1)S(1)}, bf16[512,768]{1,0:T(8,128)(2,1)S(1)}, u32[]{:S(2)}, u32[]{:S(2)}) collective-permute-start(bf16[512,768]{1,0:T(8,128)(2,1)S(1)} %copy-done.1), channel_id=1, source_target_pairs={{0,15},{1,0},{2,1},{3,2},{4,3},{5,4},{6,5},{7,6},{8,7},{9,8},{10,9... | collective-permute-start | bytes 2359304 | tf_op jit(solution)/shard_map/ppermute | solution.py:55
  13.8 18.2 %collective-permute-start.1 = (bf16[192,512]{1,0:T(8,128)(2,1)S(1)}, bf16[192,512]{1,0:T(8,128)(2,1)S(1)}, u32[]{:S(2)}, u32[]{:S(2)}) collective-permute-start(bf16[192,512]{1,0:T(8,128)(2,1)S(1)} %get-tuple-element.49), channel_id=1, source_target_pairs={{0,4},{1,5},{2,6},{3,7},{4,8},{5,9},{6,10},{7,11},{8,12},{9,13},{1... | collective-permute-start | bytes 589832 | tf_op jit(solution)/shard_map/ppermute | solution.py:55
  13.9 23.4 %collective-permute-start.2 = (bf16[192,512]{1,0:T(8,128)(2,1)S(1)}, bf16[192,512]{1,0:T(8,128)(2,1)S(1)}, u32[]{:S(2)}, u32[]{:S(2)}) collective-permute-start(bf16[192,512]{1,0:T(8,128)(2,1)S(1)} %get-tuple-element.50), channel_id=1, source_target_pairs={{0,8},{1,9},{2,10},{3,11},{4,12},{5,13},{6,14},{7,15},{8,0},{9,1},... | collective-permute-start | bytes 589832 | tf_op jit(solution)/shard_map/ppermute | solution.py:55
  16.1 44.2 %copy-start.23 = (f32[512]{0:T(512)S(1)}, f32[512]{0:T(512)}, u32[]{:S(2)}) copy-start(f32[512]{0:T(512)} %param.14) | copy-start | bytes 6148
  16.1 44.3 %copy-start.24 = (s32[512]{0:T(512)S(1)}, s32[512]{0:T(512)}, u32[]{:S(2)}) copy-start(s32[512]{0:T(512)} %param.15) | copy-start | bytes 6148
  16.1 21.1 %collective-permute-start.3 = (bf16[192,512]{1,0:T(8,128)(2,1)S(1)}, bf16[192,512]{1,0:T(8,128)(2,1)S(1)}, u32[]{:S(2)}, u32[]{:S(2)}) collective-permute-start(bf16[192,512]{1,0:T(8,128)(2,1)S(1)} %get-tuple-element.51), channel_id=1, source_target_pairs={{0,12},{1,13},{2,14},{3,15},{4,0},{5,1},{6,2},{7,3},{8,4},{9,5},{1... | collective-permute-start | bytes 589832 | tf_op jit(solution)/shard_map/ppermute | solution.py:55
  17.7 45.1 %copy-start.21 = (f32[768]{0:T(1024)S(1)}, f32[768]{0:T(1024)}, u32[]{:S(2)}) copy-start(f32[768]{0:T(1024)} %param.12) | copy-start | bytes 9220
  17.7 45.1 %copy-start.22 = (f32[768]{0:T(1024)S(1)}, f32[768]{0:T(1024)}, u32[]{:S(2)}) copy-start(f32[768]{0:T(1024)} %param.13) | copy-start | bytes 9220
  25.8 0.9 copy-start.8
  26.7 5.0 %collective-permute-start.4 = (bf16[32,2048]{1,0:T(8,128)(2,1)S(1)}, bf16[32,2048]{1,0:T(8,128)(2,1)S(1)}, u32[]{:S(2)}, u32[]{:S(2)}) collective-permute-start(bf16[32,2048]{1,0:T(8,128)(2,1)S(1)} %get-tuple-element.52), channel_id=1, source_target_pairs={{0,2},{1,3},{2,0},{3,1},{4,6},{5,7},{6,4},{7,5},{8,10},{9,11},{10,... | collective-permute-start | bytes 393224 | tf_op jit(solution)/shard_map/ppermute | solution.py:55
  27.3 32.9 %copy-start.10 = (bf16[512,768]{1,0:T(8,128)(2,1)}, bf16[512,768]{1,0:T(8,128)(2,1)S(1)}, u32[]{:S(2)}) copy-start(bf16[512,768]{1,0:T(8,128)(2,1)S(1)} %collective-permute-done.6.refs_2_) | copy-start | bytes 2359300
  37.3 9.7 %collective-permute-start.10 = (bf16[96,512]{1,0:T(8,128)(2,1)S(1)}, bf16[96,512]{1,0:T(8,128)(2,1)S(1)}, u32[]{:S(2)}, u32[]{:S(2)}) collective-permute-start(bf16[96,512]{1,0:T(8,128)(2,1)S(1)} %get-tuple-element.62), channel_id=1, source_target_pairs={{0,2},{1,3},{2,0},{3,1},{4,6},{5,7},{6,4},{7,5},{8,10},{9,11},{10,... | collective-permute-start | bytes 294920 | tf_op jit(solution)/shard_map/ppermute | solution.py:55
  37.4 7.3 %collective-permute-start.7 = (bf16[32,512]{1,0:T(8,128)(2,1)S(1)}, bf16[32,512]{1,0:T(8,128)(2,1)S(1)}, u32[]{:S(2)}, u32[]{:S(2)}) collective-permute-start(bf16[32,512]{1,0:T(8,128)(2,1)S(1)} %get-tuple-element.55), channel_id=1, source_target_pairs={{0,4},{1,5},{2,6},{3,7},{4,8},{5,9},{6,10},{7,11},{8,12},{9,13},{1... | collective-permute-start | bytes 98312 | tf_op jit(solution)/shard_map/ppermute | solution.py:55
  40.1 5.2 %collective-permute-start.8 = (bf16[32,512]{1,0:T(8,128)(2,1)S(1)}, bf16[32,512]{1,0:T(8,128)(2,1)S(1)}, u32[]{:S(2)}, u32[]{:S(2)}) collective-permute-start(bf16[32,512]{1,0:T(8,128)(2,1)S(1)} %get-tuple-element.56), channel_id=1, source_target_pairs={{0,8},{1,9},{2,10},{3,11},{4,12},{5,13},{6,14},{7,15},{8,0},{9,1},... | collective-permute-start | bytes 98312 | tf_op jit(solution)/shard_map/ppermute | solution.py:55
  43.1 3.9 %collective-permute-start.9 = (bf16[32,512]{1,0:T(8,128)(2,1)S(1)}, bf16[32,512]{1,0:T(8,128)(2,1)S(1)}, u32[]{:S(2)}, u32[]{:S(2)}) collective-permute-start(bf16[32,512]{1,0:T(8,128)(2,1)S(1)} %get-tuple-element.57), channel_id=1, source_target_pairs={{0,12},{1,13},{2,14},{3,15},{4,0},{5,1},{6,2},{7,3},{8,4},{9,5},{1... | collective-permute-start | bytes 98312 | tf_op jit(solution)/shard_map/ppermute | solution.py:55
  47.0 13.2 %copy-start.13 = (bf16[64,512]{1,0:T(8,128)(2,1)}, bf16[64,512]{1,0:T(8,128)(2,1)S(1)}, u32[]{:S(2)}) copy-start(bf16[64,512]{1,0:T(8,128)(2,1)S(1)} %get-tuple-element.72.refs_0_) | copy-start | bytes 196612
  47.0 6.1 %collective-permute-start.11 = (bf16[64,512]{1,0:T(8,128)(2,1)S(1)}, bf16[64,512]{1,0:T(8,128)(2,1)S(1)}, u32[]{:S(2)}, u32[]{:S(2)}) collective-permute-start(bf16[64,512]{1,0:T(8,128)(2,1)S(1)} %get-tuple-element.72.refs_0_), channel_id=1, source_target_pairs={{0,4},{1,5},{2,6},{3,7},{4,8},{5,9},{6,10},{7,11},{8,12},{9,13},{1... | collective-permute-start | bytes 196616 | tf_op jit(solution)/shard_map/ppermute | solution.py:55
  47.2 6.0 %collective-permute-start.12 = (bf16[64,512]{1,0:T(8,128)(2,1)S(1)}, bf16[64,512]{1,0:T(8,128)(2,1)S(1)}, u32[]{:S(2)}, u32[]{:S(2)}) collective-permute-start(bf16[64,512]{1,0:T(8,128)(2,1)S(1)} %get-tuple-element.72.refs_0_), channel_id=1, source_target_pairs={{0,8},{1,9},{2,10},{3,11},{4,12},{5,13},{6,14},{7,15},{8,0},{9,1},... | collective-permute-start | bytes 196616 | tf_op jit(solution)/shard_map/ppermute | solution.py:55
  49.8 4.3 %collective-permute-start.13 = (bf16[64,512]{1,0:T(8,128)(2,1)S(1)}, bf16[64,512]{1,0:T(8,128)(2,1)S(1)}, u32[]{:S(2)}, u32[]{:S(2)}) collective-permute-start(bf16[64,512]{1,0:T(8,128)(2,1)S(1)} %get-tuple-element.72.refs_0_), channel_id=1, source_target_pairs={{0,12},{1,13},{2,14},{3,15},{4,0},{5,1},{6,2},{7,3},{8,4},{9,5},{1... | collective-permute-start | bytes 196616 | tf_op jit(solution)/shard_map/ppermute | solution.py:55
  50.9 4.3 %collective-permute-start.14 = (bf16[64,512]{1,0:T(8,128)(2,1)S(1)}, bf16[64,512]{1,0:T(8,128)(2,1)S(1)}, u32[]{:S(2)}, u32[]{:S(2)}) collective-permute-start(bf16[64,512]{1,0:T(8,128)(2,1)S(1)} %get-tuple-element.76.refs_0_), channel_id=1, source_target_pairs={{0,2},{1,3},{2,0},{3,1},{4,6},{5,7},{6,4},{7,5},{8,10},{9,11},{10,... | collective-permute-start | bytes 196616 | tf_op jit(solution)/shard_map/ppermute | solution.py:55
  53.1 7.1 %copy-start.15 = (bf16[64,512]{1,0:T(8,128)(2,1)}, bf16[64,512]{1,0:T(8,128)(2,1)S(1)}, u32[]{:S(2)}) copy-start(bf16[64,512]{1,0:T(8,128)(2,1)S(1)} %collective-permute-done.11.refs_1_) | copy-start | bytes 196612
  53.1 7.1 %copy-start.17 = (bf16[64,512]{1,0:T(8,128)(2,1)}, bf16[64,512]{1,0:T(8,128)(2,1)S(1)}, u32[]{:S(2)}) copy-start(bf16[64,512]{1,0:T(8,128)(2,1)S(1)} %collective-permute-done.12.refs_2_) | copy-start | bytes 196612
  54.1 6.1 %copy-start.19 = (bf16[64,512]{1,0:T(8,128)(2,1)}, bf16[64,512]{1,0:T(8,128)(2,1)S(1)}, u32[]{:S(2)}) copy-start(bf16[64,512]{1,0:T(8,128)(2,1)S(1)} %collective-permute-done.13.refs_3_) | copy-start | bytes 196612
  55.2 23.7 %collective-permute-start.16 = (bf16[128,512]{1,0:T(8,128)(2,1)S(1)}, bf16[128,512]{1,0:T(8,128)(2,1)}, u32[]{:S(2)}, u32[]{:S(2)}) collective-permute-start(bf16[128,512]{1,0:T(8,128)(2,1)S(1)} %shard_map.112.refs_0_), channel_id=1, source_target_pairs={{0,4},{1,5},{2,6},{3,7},{4,8},{5,9},{6,10},{7,11},{8,12},{9,13},{1... | collective-permute-start | bytes 393224 | tf_op jit(solution)/shard_map/ppermute | solution.py:55
  56.3 22.7 %collective-permute-start.17 = (bf16[128,512]{1,0:T(8,128)(2,1)S(1)}, bf16[128,512]{1,0:T(8,128)(2,1)}, u32[]{:S(2)}, u32[]{:S(2)}) collective-permute-start(bf16[128,512]{1,0:T(8,128)(2,1)S(1)} %shard_map.112.refs_0_), channel_id=1, source_target_pairs={{0,8},{1,9},{2,10},{3,11},{4,12},{5,13},{6,14},{7,15},{8,0},{9,1},... | collective-permute-start | bytes 393224 | tf_op jit(solution)/shard_map/ppermute | solution.py:55
  58.2 20.8 %collective-permute-start.18 = (bf16[128,512]{1,0:T(8,128)(2,1)S(1)}, bf16[128,512]{1,0:T(8,128)(2,1)}, u32[]{:S(2)}, u32[]{:S(2)}) collective-permute-start(bf16[128,512]{1,0:T(8,128)(2,1)S(1)} %shard_map.112.refs_0_), channel_id=1, source_target_pairs={{0,12},{1,13},{2,14},{3,15},{4,0},{5,1},{6,2},{7,3},{8,4},{9,5},{1... | collective-permute-start | bytes 393224 | tf_op jit(solution)/shard_map/ppermute | solution.py:55
  62.8 0.8 copy-start.14
  63.7 0.8 copy-start.16
  64.5 0.8 copy-start.18
  65.4 0.8 copy-start.20
  66.2 14.4 %collective-permute-start.15 = (bf16[64,2048]{1,0:T(8,128)(2,1)S(1)}, bf16[64,2048]{1,0:T(8,128)(2,1)S(1)}, u32[]{:S(2)}, u32[]{:S(2)}) collective-permute-start(bf16[64,2048]{1,0:T(8,128)(2,1)S(1)} %shard_map.111.refs_0_), channel_id=1, source_target_pairs={{0,2},{1,3},{2,0},{3,1},{4,6},{5,7},{6,4},{7,5},{8,10},{9,11},{10,... | collective-permute-start | bytes 786440 | tf_op jit(solution)/shard_map/ppermute | solution.py:55
  69.3 1.1 %copy-start.2 = (bf16[512,768]{1,0:T(8,128)(2,1)S(1)}, bf16[512,768]{1,0:T(8,128)(2,1)}, u32[]{:S(2)}) copy-start(bf16[512,768]{1,0:T(8,128)(2,1)} %refs_6_.3) | copy-start | bytes 2359300
  70.5 1.1 %copy-start.4 = (bf16[512,768]{1,0:T(8,128)(2,1)S(1)}, bf16[512,768]{1,0:T(8,128)(2,1)}, u32[]{:S(2)}) copy-start(bf16[512,768]{1,0:T(8,128)(2,1)} %refs_4_.2) | copy-start | bytes 2359300
  71.6 0.9 copy-start.6
  72.6 0.9 copy-start.7
  73.5 1.1 %copy-start.9 = (bf16[512,768]{1,0:T(8,128)(2,1)S(1)}, bf16[512,768]{1,0:T(8,128)(2,1)}, u32[]{:S(2)}) copy-start(bf16[512,768]{1,0:T(8,128)(2,1)} %copy-done.8) | copy-start | bytes 2359300
  74.7 1.1 %copy-start.11 = (bf16[512,768]{1,0:T(8,128)(2,1)S(1)}, bf16[512,768]{1,0:T(8,128)(2,1)}, u32[]{:S(2)}) copy-start(bf16[512,768]{1,0:T(8,128)(2,1)} %copy-done.10) | copy-start | bytes 2359300
  75.8 0.8 copy-start.12
  80.0 24.7 %copy-start.3 = (bf16[512,768]{1,0:T(8,128)(2,1)S(1)}, bf16[512,768]{1,0:T(8,128)(2,1)}, u32[]{:S(2)}) copy-start(bf16[512,768]{1,0:T(8,128)(2,1)} %refs_6_.3) | copy-start | bytes 2359300
  80.0 24.7 %copy-start.5 = (bf16[512,768]{1,0:T(8,128)(2,1)S(1)}, bf16[512,768]{1,0:T(8,128)(2,1)}, u32[]{:S(2)}) copy-start(bf16[512,768]{1,0:T(8,128)(2,1)} %refs_4_.2) | copy-start | bytes 2359300
  80.1 2.7 %collective-permute-start.21 = (bf16[128,2048]{1,0:T(8,128)(2,1)S(1)}, bf16[128,2048]{1,0:T(8,128)(2,1)S(1)}, u32[]{:S(2)}, u32[]{:S(2)}) collective-permute-start(bf16[128,2048]{1,0:T(8,128)(2,1)S(1)} %shard_map.114.refs_2_), channel_id=1, source_target_pairs={{0,1},{1,0},{2,3},{3,2},{4,5},{5,4},{6,7},{7,6},{8,9},{9,8},{10,11... | collective-permute-start | bytes 1572872 | tf_op jit(solution)/shard_map/ppermute | solution.py:55
  80.1 2.3 %collective-permute-start.19 = (bf16[64,2048]{1,0:T(8,128)(2,1)S(1)}, bf16[64,2048]{1,0:T(8,128)(2,1)S(1)}, u32[]{:S(2)}, u32[]{:S(2)}) collective-permute-start(bf16[64,2048]{1,0:T(8,128)(2,1)S(1)} %shard_map.111.refs_0_), channel_id=1, source_target_pairs={{0,1},{1,0},{2,3},{3,2},{4,5},{5,4},{6,7},{7,6},{8,9},{9,8},{10,11... | collective-permute-start | bytes 786440 | tf_op jit(solution)/shard_map/ppermute | solution.py:55
  80.6 2.1 %collective-permute-start.20 = (bf16[64,2048]{1,0:T(8,128)(2,1)S(1)}, bf16[64,2048]{1,0:T(8,128)(2,1)S(1)}, u32[]{:S(2)}, u32[]{:S(2)}) collective-permute-start(bf16[64,2048]{1,0:T(8,128)(2,1)S(1)} %collective-permute-done.15.refs_1_), channel_id=1, source_target_pairs={{0,1},{1,0},{2,3},{3,2},{4,5},{5,4},{6,7},{7,6},{8,9},{9,8},{10,11... | collective-permute-start | bytes 786440 | tf_op jit(solution)/shard_map/ppermute | solution.py:55
  85.8 1.4 %collective-permute-start.22 = (bf16[256,256]{1,0:T(8,128)(2,1)S(1)}, bf16[256,256]{1,0:T(8,128)(2,1)S(1)}, u32[]{:S(2)}, u32[]{:S(2)}) collective-permute-start(bf16[256,256]{1,0:T(8,128)(2,1)S(1)} %get-tuple-element.87), channel_id=1, source_target_pairs={{0,1},{1,0},{2,3},{3,2},{4,5},{5,4},{6,7},{7,6},{8,9},{9,8},{10,11... | collective-permute-start | bytes 393224 | tf_op jit(solution)/shard_map/ppermute | solution.py:55
  87.2 4.3 %collective-permute-start.23 = (bf16[128,256]{1,0:T(8,128)(2,1)S(1)}, bf16[128,256]{1,0:T(8,128)(2,1)S(1)}, u32[]{:S(2)}, u32[]{:S(2)}) collective-permute-start(bf16[128,256]{1,0:T(8,128)(2,1)S(1)} %get-tuple-element.89), channel_id=1, source_target_pairs={{0,2},{1,3},{2,0},{3,1},{4,6},{5,7},{6,4},{7,5},{8,10},{9,11},{10,... | collective-permute-start | bytes 196616 | tf_op jit(solution)/shard_map/ppermute | solution.py:55
  91.5 6.4 %collective-permute-start.24 = (bf16[128,256]{1,0:T(8,128)(2,1)S(1)}, bf16[128,256]{1,0:T(8,128)(2,1)S(1)}, u32[]{:S(2)}, u32[]{:S(2)}) collective-permute-start(bf16[128,256]{1,0:T(8,128)(2,1)S(1)} %get-tuple-element.91), channel_id=1, source_target_pairs={{0,4},{1,5},{2,6},{3,7},{4,8},{5,9},{6,10},{7,11},{8,12},{9,13},{1... | collective-permute-start | bytes 196616 | tf_op jit(solution)/shard_map/ppermute | solution.py:55
  91.6 7.5 %collective-permute-start.25 = (bf16[128,256]{1,0:T(8,128)(2,1)S(1)}, bf16[128,256]{1,0:T(8,128)(2,1)S(1)}, u32[]{:S(2)}, u32[]{:S(2)}) collective-permute-start(bf16[128,256]{1,0:T(8,128)(2,1)S(1)} %get-tuple-element.91), channel_id=1, source_target_pairs={{0,8},{1,9},{2,10},{3,11},{4,12},{5,13},{6,14},{7,15},{8,0},{9,1},... | collective-permute-start | bytes 196616 | tf_op jit(solution)/shard_map/ppermute | solution.py:55
  94.1 5.0 %collective-permute-start.26 = (bf16[128,256]{1,0:T(8,128)(2,1)S(1)}, bf16[128,256]{1,0:T(8,128)(2,1)S(1)}, u32[]{:S(2)}, u32[]{:S(2)}) collective-permute-start(bf16[128,256]{1,0:T(8,128)(2,1)S(1)} %get-tuple-element.91), channel_id=1, source_target_pairs={{0,12},{1,13},{2,14},{3,15},{4,0},{5,1},{6,2},{7,3},{8,4},{9,5},{1... | collective-permute-start | bytes 196616 | tf_op jit(solution)/shard_map/ppermute | solution.py:55
  99.2 4.3 %collective-permute-start.27 = (bf16[128,256]{1,0:T(8,128)(2,1)S(1)}, bf16[128,256]{1,0:T(8,128)(2,1)S(1)}, u32[]{:S(2)}, u32[]{:S(2)}) collective-permute-start(bf16[128,256]{1,0:T(8,128)(2,1)S(1)} %shard_map.118.refs_0_), channel_id=1, source_target_pairs={{0,2},{1,3},{2,0},{3,1},{4,6},{5,7},{6,4},{7,5},{8,10},{9,11},{10,... | collective-permute-start | bytes 196616 | tf_op jit(solution)/shard_map/ppermute | solution.py:55
  100.0 3.5 %collective-permute-start.28 = (bf16[128,256]{1,0:T(8,128)(2,1)S(1)}, bf16[128,256]{1,0:T(8,128)(2,1)S(1)}, u32[]{:S(2)}, u32[]{:S(2)}) collective-permute-start(bf16[128,256]{1,0:T(8,128)(2,1)S(1)} %shard_map.118.refs_0_), channel_id=1, source_target_pairs={{0,1},{1,0},{2,3},{3,2},{4,5},{5,4},{6,7},{7,6},{8,9},{9,8},{10,11... | collective-permute-start | bytes 196616 | tf_op jit(solution)/shard_map/ppermute | solution.py:55
  103.5 1.3 %collective-permute-start.29 = (bf16[128,256]{1,0:T(8,128)(2,1)S(1)}, bf16[128,256]{1,0:T(8,128)(2,1)S(1)}, u32[]{:S(2)}, u32[]{:S(2)}) collective-permute-start(bf16[128,256]{1,0:T(8,128)(2,1)S(1)} %collective-permute-done.27.refs_1_), channel_id=1, source_target_pairs={{0,1},{1,0},{2,3},{3,2},{4,5},{5,4},{6,7},{7,6},{8,9},{9,8},{10,11... | collective-permute-start | bytes 196616 | tf_op jit(solution)/shard_map/ppermute | solution.py:55

commit v7 on v6

--- a/solution.py
+++ b/solution.py
@@ -28,7 +28,7 @@
 STEP_SIZE = 0.3
 MIB = 1024 * 1024
 VMEM_BYTES = 40 * MIB
-REDUCE_SHARE = 0.25
+REDUCE_SHARE = 0.375
 GATHER_SHARE = 0.5
 BF16 = jnp.bfloat16
 F32 = jnp.float32
@@ -99,32 +99,38 @@
     return jax.ShapeDtypeStruct(shape, dtype)
 
 
-def partial_body(core, other, r_ref, p_ref, out_ref):
-    rows = out_ref.shape[0]
+def partial_body(core, other, block, r_ref, p_ref, x_ref, z_ref):
+    rows = x_ref.shape[0] + z_ref.shape[0]
+    size = rows // block
+    first, rest = x_ref.shape[0] // size, z_ref.shape[0] // size
     c = position(core)
     row = pl.multiple_of((1 - c if other else c) * rows, rows)
-    out_ref[...] = lax.dot_general(
+    part = lax.dot_general(
         r_ref[pl.ds(row, rows), :], p_ref[...], NT, preferred_element_type=F32
-    ).astype(out_ref.dtype)
-
-
-def partial_intersections(response, projectors, core, other):
+    ).astype(x_ref.dtype)
+    for i in range(size):
+        x_ref[i * first : (i + 1) * first, :] = part[i * block : i * block + first, :]
+        z_ref[i * rest : (i + 1) * rest, :] = part[i * block + first : (i + 1) * block, :]
+
+
+def partial_intersections(response, projectors, core, other, block, first):
     bands, cells = response.shape
     count = projectors.shape[0]
     rows = bands // 2
     tile = min(512, count)
-    out = struct((rows, count), BF16 if other else F32)
+    rows_x = rows // block * first
+    outs = [struct((n, count), BF16 if other else F32) for n in (rows_x, rows - rows_x)]
     return pl.pallas_call(
-        functools.partial(partial_body, core, other),
+        functools.partial(partial_body, core, other, block),
         grid=(count // tile,),
-        out_shape=out,
+        out_shape=outs,
         in_specs=[
             pl.BlockSpec((bands, cells), lambda i: (0, 0)),
             pl.BlockSpec((tile, cells), lambda i: (i, 0)),
         ],
-        out_specs=pl.BlockSpec((rows, tile), lambda i: (0, i)),
-        compiler_params=params((56 if other else 40) * MIB),
-        cost_estimate=cost(2 * rows * cells * count, projectors, out),
+        out_specs=[pl.BlockSpec((out.shape[0], tile), lambda i: (0, i)) for out in outs],
+        compiler_params=params(),
+        cost_estimate=cost(2 * rows * cells * count, projectors, *outs),
     )(response, projectors)
 
 
@@ -141,27 +147,6 @@
     for ref in taken:
         total = total + ref[part].astype(F32)
     return total
-
-
-def first_x_body(level, block, keep_ref, taken_ref, *outs):
-    me = position(level)
-    rows = outs[0].shape[0]
-    for step, out in enumerate(outs):
-        at = lax.rem(me + step, jnp.int32(level[0])) * block
-        part = (pl.ds(pl.multiple_of(at, 16), rows), slice(None))
-        out[...] = total_of(keep_ref, [taken_ref], part).astype(out.dtype)
-
-
-def first_z_body(level, block, first, keep_ref, taken_ref, *outs):
-    me = position(level)
-    rows = block - first
-    width = outs[0].shape[1]
-    for step, out in enumerate(outs):
-        cols = cols_at(lax.rem(me + step, jnp.int32(level[0])), width)
-        for i in range(out.shape[0] // rows):
-            part = (slice(i * block + first, (i + 1) * block), cols)
-            mine = slice(i * rows, (i + 1) * rows)
-            out[mine, :] = total_of(keep_ref, [taken_ref], part).astype(out.dtype)
 
 
 def split_body(received, level, along, *refs):
@@ -440,18 +425,12 @@
     low = shifted(response[:, local_cells - halo :], count, ring, 1)
     high = shifted(response[:, :halo], count, ring, -1)
 
-    sent = shifted(partial_intersections(response, projectors, core, True), count, core, 1)
-    keep = partial_intersections(response, projectors, core, False)
-    keep_z, *parts_z = local_call(
-        functools.partial(first_z_body, along, block, first),
-        shares_of((half - across[0] * first, projections // along[0]), along[0]),
-        [keep, sent],
-    )
-    keep_x, *parts_x = local_call(
-        functools.partial(first_x_body, across, block),
-        shares_of((first, projections), across[0]),
-        [keep, sent],
-    )
+    sent_x, sent_z = partial_intersections(response, projectors, core, True, block, first)
+    sent_z = shifted(sent_z, count, core, 1)
+    sent_x = shifted(sent_x, count, core, 1)
+    keep_x, keep_z = partial_intersections(response, projectors, core, False, block, first)
+    keep_z, *parts_z = split(keep_z, [sent_z], along, 1)
+    keep_x, *parts_x = split(keep_x, [sent_x], across, 0)
     taken_z, taken_x, low, high = lax.optimization_barrier(
         (parts_to(parts_z, along), parts_to(parts_x, across), low, high)
     )

time: 108 us -> 104 us (0.963)
  local copies, waits for them, and re-layouts: 14.1 us -> 6.74 us
  Pallas kernels: 15.9 us -> 17.7 us
    unnamed x50 -> x34, local copies, waits for them, and re-layouts: 11.6 us -> 6.29 us
    broadcast_in_dim x3, local copies, waits for them, and re-layouts: 2.57 us -> 0.43 us  [shards(): columns = tuple((a[:, None] for a in (energies, window_start, block_count)))]
    pallas_call x1, Pallas kernels: 2.28 us -> 3.85 us  [project(): pl.pallas_call(functools.partial(project_body, core, across, width, blk),...]
    pallas_call x1, Pallas kernels: 2.28 us -> 3.64 us  [local_part(): pl.pallas_call(functools.partial(local_body, depth, (group_rows, width, b...]
    pallas_call x2, Pallas kernels: 6.83 us -> 5.75 us  [partial_intersections(): pl.pallas_call(functools.partial(partial_body, core, other, block), grid=...]
    ppermute x30 -> x31, waiting for transfers between devices: 40.8 us -> 41.8 us  [shifted(): return lax.ppermute(array, 'band', pairs)]
    ppermute x30 -> x31, starting transfers between devices: 35.3 us -> 35.8 us  [shifted(): return lax.ppermute(array, 'band', pairs)]
  transfers between devices with their start and end apart: 30 -> 31, of which waited for: 19 -> 17; matrix products, arithmetic and copies ran while one was open for 2% -> 0% of each run, Pallas kernels for 5% -> 8%
where the time goes in v7:
time: 104 us; the launch traced here: 103 us
  waiting for transfers between devices  41.8 us (40%)
  starting transfers between devices  35.8 us (34%)
  Pallas kernels  17.7 us (17%)
  local copies, waits for them, and re-layouts  6.74 us (6%)
    ppermute x31, waiting for transfers between devices, shifted(): return lax.ppermute(array, 'band', pairs)  41.8 us
    ppermute x31, starting transfers between devices, shifted(): return lax.ppermute(array, 'band', pairs)  35.8 us
    unnamed x34, local copies, waits for them, and re-layouts  6.29 us
    pallas_call x2, Pallas kernels, partial_intersections(): pl.pallas_call(functools.partial(partial_body, core, other, block), grid=...  5.75 us
    pallas_call x12, Pallas kernels, local_call(): pl.pallas_call(body, out_shape=outs, in_specs=[whole() for _ in args], ou...  4.42 us
    pallas_call x1, Pallas kernels, project(): pl.pallas_call(functools.partial(project_body, core, across, width, blk),...  3.85 us
    pallas_call x1, Pallas kernels, local_part(): pl.pallas_call(functools.partial(local_body, depth, (group_rows, width, b...  3.64 us
  transfers between devices with their start and end apart: 31, of which 17 were waited for; matrix products, arithmetic and copies ran while one was open for 0% of the time, Pallas kernels for 8%

profile of v7, /device:TPU:0, one launch (start us, length us, event | category | flops | bytes accessed | tf_op | source)
XLA Modules:
  0.0 103.0 jit_solution(2160422250471604120)
XLA Ops:
  0.6 0.0 copy-start
  0.6 1.9 %copy-done = bf16[2048,768]{1,0:T(8,128)(2,1)S(1)} copy-done((bf16[2048,768]{1,0:T(8,128)(2,1)S(1)}, bf16[2048,768]{1,0:T(8,128)(2,1)}, u32[]{:S(2)}) %copy-start) | copy-done | bytes 3145752
  2.5 2.8 %shard_map.105 = (bf16[96,2048]{1,0:T(8,128)(2,1)S(1)}, bf16[160,2048]{1,0:T(8,128)(2,1)S(1)}) custom-call(bf16[512,768]{1,0:T(8,128)(2,1)} %refs_6_.3, bf16[2048,768]{1,0:T(8,128)(2,1)S(1)} %copy-done), custom_call_target="tpu_custom_call" | custom-call | flops 805306368 | bytes 4194304 | tf_op jit(solution)/shard_map/pallas_call | solution.py:123
  5.4 0.5 collective-permute-start.1
  5.9 0.1 collective-permute-start.6
  6.0 5.6 %collective-permute-start.7 = (bf16[512,768]{1,0:T(8,128)(2,1)}, bf16[512,768]{1,0:T(8,128)(2,1)S(1)}, u32[]{:S(2)}, u32[]{:S(2)}) collective-permute-start(bf16[512,768]{1,0:T(8,128)(2,1)} %refs_6_.3), channel_id=1, source_target_pairs={{0,15},{1,0},{2,1},{3,2},{4,3},{5,4},{6,5},{7,6},{8,7},{9,8},{10,9... | collective-permute-start | bytes 2359304 | tf_op jit(solution)/shard_map/ppermute | solution.py:55
  11.5 2.9 %shard_map.104 = (f32[96,2048]{1,0:T(8,128)S(1)}, f32[160,2048]{1,0:T(8,128)S(1)}) custom-call(bf16[512,768]{1,0:T(8,128)(2,1)} %refs_6_.3, bf16[2048,768]{1,0:T(8,128)(2,1)S(1)} %copy-done), custom_call_target="tpu_custom_call" | custom-call | flops 805306368 | bytes 5242880 | tf_op jit(solution)/shard_map/pallas_call | solution.py:123
  14.5 0.1 shard_map.106
  14.6 0.1 collective-permute-start.5
  14.6 0.1 shard_map.107
  14.8 0.0 copy-start.14
  14.9 0.2 collective-permute-start.2
  15.1 2.6 %collective-permute-start.3 = (bf16[160,512]{1,0:T(8,128)(2,1)S(1)}, bf16[160,512]{1,0:T(8,128)(2,1)S(1)}, u32[]{:S(2)}, u32[]{:S(2)}) collective-permute-start(bf16[160,512]{1,0:T(8,128)(2,1)S(1)} %get-tuple-element.58), channel_id=1, source_target_pairs={{0,8},{1,9},{2,10},{3,11},{4,12},{5,13},{6,14},{7,15},{8,0},{9,1},... | collective-permute-start | bytes 491528 | tf_op jit(solution)/shard_map/ppermute | solution.py:55
  17.7 15.3 %collective-permute-done.5.refs_1_ = bf16[48,2048]{1,0:T(8,128)(2,1)S(1)} collective-permute-done((bf16[48,2048]{1,0:T(8,128)(2,1)S(1)}, bf16[48,2048]{1,0:T(8,128)(2,1)S(1)}, u32[]{:S(2)}, u32[]{:S(2)}) %collective-permute-start.5) | collective-permute-done | bytes 196640 | tf_op jit(solution)/shard_map/ppermute | solution.py:55
  33.0 2.7 %collective-permute-start.4 = (bf16[160,512]{1,0:T(8,128)(2,1)S(1)}, bf16[160,512]{1,0:T(8,128)(2,1)S(1)}, u32[]{:S(2)}, u32[]{:S(2)}) collective-permute-start(bf16[160,512]{1,0:T(8,128)(2,1)S(1)} %get-tuple-element.59), channel_id=1, source_target_pairs={{0,12},{1,13},{2,14},{3,15},{4,0},{5,1},{6,2},{7,3},{8,4},{9,5},{1... | collective-permute-start | bytes 491528 | tf_op jit(solution)/shard_map/ppermute | solution.py:55
  35.7 2.8 %collective-permute-done.4.refs_3_ = bf16[160,512]{1,0:T(8,128)(2,1)S(1)} collective-permute-done((bf16[160,512]{1,0:T(8,128)(2,1)S(1)}, bf16[160,512]{1,0:T(8,128)(2,1)S(1)}, u32[]{:S(2)}, u32[]{:S(2)}) %collective-permute-start.4) | collective-permute-done | bytes 163872 | tf_op jit(solution)/shard_map/ppermute | solution.py:55
  38.6 0.1 shard_map.109
  38.6 1.3 %collective-permute-start.11 = (bf16[80,512]{1,0:T(8,128)(2,1)S(1)}, bf16[80,512]{1,0:T(8,128)(2,1)S(1)}, u32[]{:S(2)}, u32[]{:S(2)}) collective-permute-start(bf16[80,512]{1,0:T(8,128)(2,1)S(1)} %get-tuple-element.70), channel_id=1, source_target_pairs={{0,2},{1,3},{2,0},{3,1},{4,6},{5,7},{6,4},{7,5},{8,10},{9,11},{10,... | collective-permute-start | bytes 245768 | tf_op jit(solution)/shard_map/ppermute | solution.py:55
  39.9 4.3 %collective-permute-start.10 = (bf16[48,512]{1,0:T(8,128)(2,1)S(1)}, bf16[48,512]{1,0:T(8,128)(2,1)S(1)}, u32[]{:S(2)}, u32[]{:S(2)}) collective-permute-start(bf16[48,512]{1,0:T(8,128)(2,1)S(1)} %get-tuple-element.65), channel_id=1, source_target_pairs={{0,12},{1,13},{2,14},{3,15},{4,0},{5,1},{6,2},{7,3},{8,4},{9,5},{1... | collective-permute-start | bytes 147464 | tf_op jit(solution)/shard_map/ppermute | solution.py:55
  44.3 0.6 collective-permute-start.9
  44.9 1.3 %collective-permute-done.10.refs_3_ = bf16[48,512]{1,0:T(8,128)(2,1)S(1)} collective-permute-done((bf16[48,512]{1,0:T(8,128)(2,1)S(1)}, bf16[48,512]{1,0:T(8,128)(2,1)S(1)}, u32[]{:S(2)}, u32[]{:S(2)}) %collective-permute-start.10) | collective-permute-done | bytes 49184 | tf_op jit(solution)/shard_map/ppermute | solution.py:55
  46.2 3.9 %collective-permute-done.8.refs_1_ = bf16[48,512]{1,0:T(8,128)(2,1)S(1)} collective-permute-done((bf16[48,512]{1,0:T(8,128)(2,1)S(1)}, bf16[48,512]{1,0:T(8,128)(2,1)S(1)}, u32[]{:S(2)}, u32[]{:S(2)}) %collective-permute-start.8) | collective-permute-done | bytes 49184 | tf_op jit(solution)/shard_map/ppermute | solution.py:55
  50.2 0.6 collective-permute-done.9.refs_2_
  50.8 0.6 collective-permute-start.12
  51.4 2.6 %collective-permute-start.13 = (bf16[64,512]{1,0:T(8,128)(2,1)S(1)}, bf16[64,512]{1,0:T(8,128)(2,1)S(1)}, u32[]{:S(2)}, u32[]{:S(2)}) collective-permute-start(bf16[64,512]{1,0:T(8,128)(2,1)S(1)} %get-tuple-element.80.refs_0_), channel_id=1, source_target_pairs={{0,8},{1,9},{2,10},{3,11},{4,12},{5,13},{6,14},{7,15},{8,0},{9,1},... | collective-permute-start | bytes 196616 | tf_op jit(solution)/shard_map/ppermute | solution.py:55
  54.0 0.7 collective-permute-start.14
  54.7 0.5 collective-permute-start.15
  55.2 1.8 %collective-permute-done.12.refs_1_ = bf16[64,512]{1,0:T(8,128)(2,1)S(1)} collective-permute-done((bf16[64,512]{1,0:T(8,128)(2,1)S(1)}, bf16[64,512]{1,0:T(8,128)(2,1)S(1)}, u32[]{:S(2)}, u32[]{:S(2)}) %collective-permute-start.12) | collective-permute-done | bytes 65568 | tf_op jit(solution)/shard_map/ppermute | solution.py:55
  57.0 1.0 collective-permute-done.13.refs_2_
  58.0 0.4 collective-permute-done.14.refs_3_
  58.5 0.5 collective-permute-done.15.refs_1_
  59.0 1.4 %collective-permute-start.17 = (bf16[128,512]{1,0:T(8,128)(2,1)S(1)}, bf16[128,512]{1,0:T(8,128)(2,1)S(1)}, u32[]{:S(2)}, u32[]{:S(2)}) collective-permute-start(bf16[128,512]{1,0:T(8,128)(2,1)S(1)} %shard_map.112.refs_0_), channel_id=1, source_target_pairs={{0,4},{1,5},{2,6},{3,7},{4,8},{5,9},{6,10},{7,11},{8,12},{9,13},{1... | collective-permute-start | bytes 393224 | tf_op jit(solution)/shard_map/ppermute | solution.py:55
  60.4 1.9 %collective-permute-start.18 = (bf16[128,512]{1,0:T(8,128)(2,1)S(1)}, bf16[128,512]{1,0:T(8,128)(2,1)S(1)}, u32[]{:S(2)}, u32[]{:S(2)}) collective-permute-start(bf16[128,512]{1,0:T(8,128)(2,1)S(1)} %shard_map.112.refs_0_), channel_id=1, source_target_pairs={{0,8},{1,9},{2,10},{3,11},{4,12},{5,13},{6,14},{7,15},{8,0},{9,1},... | collective-permute-start | bytes 393224 | tf_op jit(solution)/shard_map/ppermute | solution.py:55
  62.3 1.7 %collective-permute-start.19 = (bf16[128,512]{1,0:T(8,128)(2,1)S(1)}, bf16[128,512]{1,0:T(8,128)(2,1)}, u32[]{:S(2)}, u32[]{:S(2)}) collective-permute-start(bf16[128,512]{1,0:T(8,128)(2,1)S(1)} %shard_map.112.refs_0_), channel_id=1, source_target_pairs={{0,12},{1,13},{2,14},{3,15},{4,0},{5,1},{6,2},{7,3},{8,4},{9,5},{1... | collective-permute-start | bytes 393224 | tf_op jit(solution)/shard_map/ppermute | solution.py:55
  64.0 0.1 copy.11.refs_7_
  64.2 0.1 copy.12.refs_8_
  64.3 0.1 copy.13.refs_9_
  64.5 0.8 copy-done.5
  65.4 0.8 copy-done.7
  66.2 0.8 copy-done.9
  67.0 0.8 copy-done.11
  67.9 0.3 collective-permute-start.16
  68.3 1.0 copy-done.3
  69.2 3.6 %shard_map.113 = (f32[512,768]{1,0:T(8,128)S(1)}, bf16[512,256]{1,0:T(8,128)(2,1)S(1)}) custom-call(bf16[512,768]{1,0:T(8,128)(2,1)} %refs_6_.3, bf16[512,768]{1,0:T(8,128)(2,1)S(1)} %collective-permute-done.6.refs_1_, bf16[512,768]{1,0:T(8,128)(2,1)S(1)} %collective-permute-done.7.refs_2_, bf16[512,768]{1,0:T(8,128)(2,1)S(1)} %copy-done.2, ...), custom_call_target="tpu_custom_call" | custom-call | flops 235929600 | bytes 4980736 | tf_op jit(solution)/shard_map/pallas_call | solution.py:264
  72.9 1.0 shard_map.114.refs_2_
  73.9 0.1 collective-permute-start.22
  74.0 0.5 collective-permute-start.20
  74.5 0.1 collective-permute-start.21
  74.5 1.7 %collective-permute-done.20.refs_3_ = bf16[64,2048]{1,0:T(8,128)(2,1)S(1)} collective-permute-done((bf16[64,2048]{1,0:T(8,128)(2,1)S(1)}, bf16[64,2048]{1,0:T(8,128)(2,1)S(1)}, u32[]{:S(2)}, u32[]{:S(2)}) %collective-permute-start.20) | collective-permute-done | bytes 262176 | tf_op jit(solution)/shard_map/ppermute | solution.py:55
  76.2 0.4 collective-permute-done.21.refs_4_
  76.6 3.0 %shard_map.115 = (f32[512,768]{1,0:T(8,128)S(1)}, bf16[256,256]{1,0:T(8,128)(2,1)S(1)}, f32[256,256]{1,0:T(8,128)S(1)}) custom-call(bf16[64,2048]{1,0:T(8,128)(2,1)S(1)} %shard_map.111.refs_0_, bf16[64,2048]{1,0:T(8,128)(2,1)S(1)} %collective-permute-done.16.refs_1_, bf16[128,2048]{1,0:T(8,128)(2,1)S(1)} %shard_map.114.refs_2_, ...), custom_call_target="tpu_custom_call" | custom-call | flops 1811939328 | bytes 9568256 | tf_op jit(solution)/shard_map/pallas_call | solution.py:87
  79.6 0.2 collective-permute-start.23
  79.8 1.2 %collective-permute-done.23.refs_1_ = bf16[256,256]{1,0:T(8,128)(2,1)S(1)} collective-permute-done((bf16[256,256]{1,0:T(8,128)(2,1)S(1)}, bf16[256,256]{1,0:T(8,128)(2,1)S(1)}, u32[]{:S(2)}, u32[]{:S(2)}) %collective-permute-start.23) | collective-permute-done | bytes 131104 | tf_op jit(solution)/shard_map/ppermute | solution.py:55
  81.0 1.7 %collective-permute-start.24 = (bf16[128,256]{1,0:T(8,128)(2,1)S(1)}, bf16[128,256]{1,0:T(8,128)(2,1)S(1)}, u32[]{:S(2)}, u32[]{:S(2)}) collective-permute-start(bf16[128,256]{1,0:T(8,128)(2,1)S(1)} %get-tuple-element.97), channel_id=1, source_target_pairs={{0,2},{1,3},{2,0},{3,1},{4,6},{5,7},{6,4},{7,5},{8,10},{9,11},{10,... | collective-permute-start | bytes 196616 | tf_op jit(solution)/shard_map/ppermute | solution.py:55
  82.7 2.6 %collective-permute-done.24.refs_0_ = bf16[128,256]{1,0:T(8,128)(2,1)S(1)} collective-permute-done((bf16[128,256]{1,0:T(8,128)(2,1)S(1)}, bf16[128,256]{1,0:T(8,128)(2,1)S(1)}, u32[]{:S(2)}, u32[]{:S(2)}) %collective-permute-start.24) | collective-permute-done | bytes 65568 | tf_op jit(solution)/shard_map/ppermute | solution.py:55
  85.4 1.0 collective-permute-start.25
  86.3 1.2 %collective-permute-start.26 = (bf16[128,256]{1,0:T(8,128)(2,1)S(1)}, bf16[128,256]{1,0:T(8,128)(2,1)S(1)}, u32[]{:S(2)}, u32[]{:S(2)}) collective-permute-start(bf16[128,256]{1,0:T(8,128)(2,1)S(1)} %get-tuple-element.99), channel_id=1, source_target_pairs={{0,8},{1,9},{2,10},{3,11},{4,12},{5,13},{6,14},{7,15},{8,0},{9,1},... | collective-permute-start | bytes 196616 | tf_op jit(solution)/shard_map/ppermute | solution.py:55
  87.6 2.1 %collective-permute-start.27 = (bf16[128,256]{1,0:T(8,128)(2,1)S(1)}, bf16[128,256]{1,0:T(8,128)(2,1)S(1)}, u32[]{:S(2)}, u32[]{:S(2)}) collective-permute-start(bf16[128,256]{1,0:T(8,128)(2,1)S(1)} %get-tuple-element.99), channel_id=1, source_target_pairs={{0,12},{1,13},{2,14},{3,15},{4,0},{5,1},{6,2},{7,3},{8,4},{9,5},{1... | collective-permute-start | bytes 196616 | tf_op jit(solution)/shard_map/ppermute | solution.py:55
  89.7 2.1 %collective-permute-done.25.refs_0_ = bf16[128,256]{1,0:T(8,128)(2,1)S(1)} collective-permute-done((bf16[128,256]{1,0:T(8,128)(2,1)S(1)}, bf16[128,256]{1,0:T(8,128)(2,1)S(1)}, u32[]{:S(2)}, u32[]{:S(2)}) %collective-permute-start.25) | collective-permute-done | bytes 65568 | tf_op jit(solution)/shard_map/ppermute | solution.py:55
  91.8 1.7 %collective-permute-done.26.refs_1_ = bf16[128,256]{1,0:T(8,128)(2,1)S(1)} collective-permute-done((bf16[128,256]{1,0:T(8,128)(2,1)S(1)}, bf16[128,256]{1,0:T(8,128)(2,1)S(1)}, u32[]{:S(2)}, u32[]{:S(2)}) %collective-permute-start.26) | collective-permute-done | bytes 65568 | tf_op jit(solution)/shard_map/ppermute | solution.py:55
  93.5 1.2 %collective-permute-start.28 = (bf16[128,256]{1,0:T(8,128)(2,1)S(1)}, bf16[128,256]{1,0:T(8,128)(2,1)S(1)}, u32[]{:S(2)}, u32[]{:S(2)}) collective-permute-start(bf16[128,256]{1,0:T(8,128)(2,1)S(1)} %shard_map.118.refs_0_), channel_id=1, source_target_pairs={{0,2},{1,3},{2,0},{3,1},{4,6},{5,7},{6,4},{7,5},{8,10},{9,11},{10,... | collective-permute-start | bytes 196616 | tf_op jit(solution)/shard_map/ppermute | solution.py:55
  94.7 3.1 %collective-permute-done.28.refs_1_ = bf16[128,256]{1,0:T(8,128)(2,1)S(1)} collective-permute-done((bf16[128,256]{1,0:T(8,128)(2,1)S(1)}, bf16[128,256]{1,0:T(8,128)(2,1)S(1)}, u32[]{:S(2)}, u32[]{:S(2)}) %collective-permute-start.28) | collective-permute-done | bytes 65568 | tf_op jit(solution)/shard_map/ppermute | solution.py:55
  97.8 1.2 %collective-permute-done.30.refs_3_ = bf16[128,256]{1,0:T(8,128)(2,1)S(1)} collective-permute-done((bf16[128,256]{1,0:T(8,128)(2,1)S(1)}, bf16[128,256]{1,0:T(8,128)(2,1)S(1)}, u32[]{:S(2)}, u32[]{:S(2)}) %collective-permute-start.30) | collective-permute-done | bytes 65568 | tf_op jit(solution)/shard_map/ppermute | solution.py:55
  99.1 3.9 %shard_map.119 = (bf16[512,768]{1,0:T(8,128)(2,1)}, bf16[512,768]{1,0:T(8,128)(2,1)}) custom-call(bf16[128,256]{1,0:T(8,128)(2,1)S(1)} %shard_map.118.refs_0_, bf16[128,256]{1,0:T(8,128)(2,1)S(1)} %collective-permute-done.28.refs_1_, bf16[128,256]{1,0:T(8,128)(2,1)S(1)} %collective-permute-done.29.refs_2_, ...), custom_call_target="tpu_custom_call" | custom-call | flops 201326592 | bytes 4718592 | tf_op jit(solution)/shard_map/pallas_call | solution.py:379
  (53 shorter events, 0.3 us)
Async XLA Ops:
  0.6 1.9 %copy-start = (bf16[2048,768]{1,0:T(8,128)(2,1)S(1)}, bf16[2048,768]{1,0:T(8,128)(2,1)}, u32[]{:S(2)}) copy-start(bf16[2048,768]{1,0:T(8,128)(2,1)} %refs_6_.2) | copy-start | bytes 9437188
  5.4 9.3 %collective-permute-start.1 = (bf16[160,2048]{1,0:T(8,128)(2,1)S(1)}, bf16[160,2048]{1,0:T(8,128)(2,1)S(1)}, u32[]{:S(2)}, u32[]{:S(2)}) collective-permute-start(bf16[160,2048]{1,0:T(8,128)(2,1)S(1)} %get-tuple-element.56), channel_id=1, source_target_pairs={{0,1},{1,0},{2,3},{3,2},{4,5},{5,4},{6,7},{7,6},{8,9},{9,8},{10,11... | collective-permute-start | bytes 1966088 | tf_op jit(solution)/shard_map/ppermute | solution.py:55
  5.9 29.8 %collective-permute-start.6 = (bf16[512,768]{1,0:T(8,128)(2,1)}, bf16[512,768]{1,0:T(8,128)(2,1)S(1)}, u32[]{:S(2)}, u32[]{:S(2)}) collective-permute-start(bf16[512,768]{1,0:T(8,128)(2,1)} %refs_6_.3), channel_id=1, source_target_pairs={{0,1},{1,2},{2,3},{3,4},{4,5},{5,6},{6,7},{7,8},{8,9},{9,10},{10,1... | collective-permute-start | bytes 2359304 | tf_op jit(solution)/shard_map/ppermute | solution.py:55
  6.0 29.8 %collective-permute-start.7 = (bf16[512,768]{1,0:T(8,128)(2,1)}, bf16[512,768]{1,0:T(8,128)(2,1)S(1)}, u32[]{:S(2)}, u32[]{:S(2)}) collective-permute-start(bf16[512,768]{1,0:T(8,128)(2,1)} %refs_6_.3), channel_id=1, source_target_pairs={{0,15},{1,0},{2,1},{3,2},{4,3},{5,4},{6,5},{7,6},{8,7},{9,8},{10,9... | collective-permute-start | bytes 2359304 | tf_op jit(solution)/shard_map/ppermute | solution.py:55
  11.5 2.9 %collective-permute-start = (bf16[96,2048]{1,0:T(8,128)(2,1)S(1)}, bf16[96,2048]{1,0:T(8,128)(2,1)S(1)}, u32[]{:S(2)}, u32[]{:S(2)}) collective-permute-start(bf16[96,2048]{1,0:T(8,128)(2,1)S(1)} %get-tuple-element.53), channel_id=1, source_target_pairs={{0,1},{1,0},{2,3},{3,2},{4,5},{5,4},{6,7},{7,6},{8,9},{9,8},{10,11... | collective-permute-start | bytes 1179656 | tf_op jit(solution)/shard_map/ppermute | solution.py:55
  14.6 18.4 %collective-permute-start.5 = (bf16[48,2048]{1,0:T(8,128)(2,1)S(1)}, bf16[48,2048]{1,0:T(8,128)(2,1)S(1)}, u32[]{:S(2)}, u32[]{:S(2)}) collective-permute-start(bf16[48,2048]{1,0:T(8,128)(2,1)S(1)} %get-tuple-element.60), channel_id=1, source_target_pairs={{0,2},{1,3},{2,0},{3,1},{4,6},{5,7},{6,4},{7,5},{8,10},{9,11},{10,... | collective-permute-start | bytes 589832 | tf_op jit(solution)/shard_map/ppermute | solution.py:55
  14.8 49.2 %copy-start.14 = (f32[512]{0:T(512)S(1)}, f32[512]{0:T(512)}, u32[]{:S(2)}) copy-start(f32[512]{0:T(512)} %param.14) | copy-start | bytes 6148
  14.8 49.4 %copy-start.15 = (s32[512]{0:T(512)S(1)}, s32[512]{0:T(512)}, u32[]{:S(2)}) copy-start(s32[512]{0:T(512)} %param.15) | copy-start | bytes 6148
  14.8 49.5 %copy-start.16 = (s32[512]{0:T(512)S(1)}, s32[512]{0:T(512)}, u32[]{:S(2)}) copy-start(s32[512]{0:T(512)} %param.16) | copy-start | bytes 6148
  14.8 49.7 %copy-start.12 = (f32[768]{0:T(1024)S(1)}, f32[768]{0:T(1024)}, u32[]{:S(2)}) copy-start(f32[768]{0:T(1024)} %param.12) | copy-start | bytes 9220
  14.8 49.7 %copy-start.13 = (f32[768]{0:T(1024)S(1)}, f32[768]{0:T(1024)}, u32[]{:S(2)}) copy-start(f32[768]{0:T(1024)} %param.13) | copy-start | bytes 9220
  14.9 20.9 %collective-permute-start.2 = (bf16[160,512]{1,0:T(8,128)(2,1)S(1)}, bf16[160,512]{1,0:T(8,128)(2,1)S(1)}, u32[]{:S(2)}, u32[]{:S(2)}) collective-permute-start(bf16[160,512]{1,0:T(8,128)(2,1)S(1)} %get-tuple-element.57), channel_id=1, source_target_pairs={{0,4},{1,5},{2,6},{3,7},{4,8},{5,9},{6,10},{7,11},{8,12},{9,13},{1... | collective-permute-start | bytes 491528 | tf_op jit(solution)/shard_map/ppermute | solution.py:55
  15.1 20.6 %collective-permute-start.3 = (bf16[160,512]{1,0:T(8,128)(2,1)S(1)}, bf16[160,512]{1,0:T(8,128)(2,1)S(1)}, u32[]{:S(2)}, u32[]{:S(2)}) collective-permute-start(bf16[160,512]{1,0:T(8,128)(2,1)S(1)} %get-tuple-element.58), channel_id=1, source_target_pairs={{0,8},{1,9},{2,10},{3,11},{4,12},{5,13},{6,14},{7,15},{8,0},{9,1},... | collective-permute-start | bytes 491528 | tf_op jit(solution)/shard_map/ppermute | solution.py:55
  33.0 5.6 %collective-permute-start.4 = (bf16[160,512]{1,0:T(8,128)(2,1)S(1)}, bf16[160,512]{1,0:T(8,128)(2,1)S(1)}, u32[]{:S(2)}, u32[]{:S(2)}) collective-permute-start(bf16[160,512]{1,0:T(8,128)(2,1)S(1)} %get-tuple-element.59), channel_id=1, source_target_pairs={{0,12},{1,13},{2,14},{3,15},{4,0},{5,1},{6,2},{7,3},{8,4},{9,5},{1... | collective-permute-start | bytes 491528 | tf_op jit(solution)/shard_map/ppermute | solution.py:55
  38.6 29.7 %copy-start.2 = (bf16[512,768]{1,0:T(8,128)(2,1)S(1)}, bf16[512,768]{1,0:T(8,128)(2,1)}, u32[]{:S(2)}) copy-start(bf16[512,768]{1,0:T(8,128)(2,1)} %refs_4_.2) | copy-start | bytes 2359300
  38.6 12.1 %collective-permute-start.11 = (bf16[80,512]{1,0:T(8,128)(2,1)S(1)}, bf16[80,512]{1,0:T(8,128)(2,1)S(1)}, u32[]{:S(2)}, u32[]{:S(2)}) collective-permute-start(bf16[80,512]{1,0:T(8,128)(2,1)S(1)} %get-tuple-element.70), channel_id=1, source_target_pairs={{0,2},{1,3},{2,0},{3,1},{4,6},{5,7},{6,4},{7,5},{8,10},{9,11},{10,... | collective-permute-start | bytes 245768 | tf_op jit(solution)/shard_map/ppermute | solution.py:55
  39.9 6.3 %collective-permute-start.10 = (bf16[48,512]{1,0:T(8,128)(2,1)S(1)}, bf16[48,512]{1,0:T(8,128)(2,1)S(1)}, u32[]{:S(2)}, u32[]{:S(2)}) collective-permute-start(bf16[48,512]{1,0:T(8,128)(2,1)S(1)} %get-tuple-element.65), channel_id=1, source_target_pairs={{0,12},{1,13},{2,14},{3,15},{4,0},{5,1},{6,2},{7,3},{8,4},{9,5},{1... | collective-permute-start | bytes 147464 | tf_op jit(solution)/shard_map/ppermute | solution.py:55
  44.3 5.9 %collective-permute-start.8 = (bf16[48,512]{1,0:T(8,128)(2,1)S(1)}, bf16[48,512]{1,0:T(8,128)(2,1)S(1)}, u32[]{:S(2)}, u32[]{:S(2)}) collective-permute-start(bf16[48,512]{1,0:T(8,128)(2,1)S(1)} %get-tuple-element.63), channel_id=1, source_target_pairs={{0,4},{1,5},{2,6},{3,7},{4,8},{5,9},{6,10},{7,11},{8,12},{9,13},{1... | collective-permute-start | bytes 147464 | tf_op jit(solution)/shard_map/ppermute | solution.py:55
  44.3 6.5 %collective-permute-start.9 = (bf16[48,512]{1,0:T(8,128)(2,1)S(1)}, bf16[48,512]{1,0:T(8,128)(2,1)S(1)}, u32[]{:S(2)}, u32[]{:S(2)}) collective-permute-start(bf16[48,512]{1,0:T(8,128)(2,1)S(1)} %get-tuple-element.64), channel_id=1, source_target_pairs={{0,8},{1,9},{2,10},{3,11},{4,12},{5,13},{6,14},{7,15},{8,0},{9,1},... | collective-permute-start | bytes 147464 | tf_op jit(solution)/shard_map/ppermute | solution.py:55
  50.8 13.2 %copy-start.4 = (bf16[64,512]{1,0:T(8,128)(2,1)}, bf16[64,512]{1,0:T(8,128)(2,1)S(1)}, u32[]{:S(2)}) copy-start(bf16[64,512]{1,0:T(8,128)(2,1)S(1)} %get-tuple-element.80.refs_0_) | copy-start | bytes 196612
  50.8 6.2 %collective-permute-start.12 = (bf16[64,512]{1,0:T(8,128)(2,1)S(1)}, bf16[64,512]{1,0:T(8,128)(2,1)S(1)}, u32[]{:S(2)}, u32[]{:S(2)}) collective-permute-start(bf16[64,512]{1,0:T(8,128)(2,1)S(1)} %get-tuple-element.80.refs_0_), channel_id=1, source_target_pairs={{0,4},{1,5},{2,6},{3,7},{4,8},{5,9},{6,10},{7,11},{8,12},{9,13},{1... | collective-permute-start | bytes 196616 | tf_op jit(solution)/shard_map/ppermute | solution.py:55
  51.4 6.7 %collective-permute-start.13 = (bf16[64,512]{1,0:T(8,128)(2,1)S(1)}, bf16[64,512]{1,0:T(8,128)(2,1)S(1)}, u32[]{:S(2)}, u32[]{:S(2)}) collective-permute-start(bf16[64,512]{1,0:T(8,128)(2,1)S(1)} %get-tuple-element.80.refs_0_), channel_id=1, source_target_pairs={{0,8},{1,9},{2,10},{3,11},{4,12},{5,13},{6,14},{7,15},{8,0},{9,1},... | collective-permute-start | bytes 196616 | tf_op jit(solution)/shard_map/ppermute | solution.py:55
  54.0 4.5 %collective-permute-start.14 = (bf16[64,512]{1,0:T(8,128)(2,1)S(1)}, bf16[64,512]{1,0:T(8,128)(2,1)S(1)}, u32[]{:S(2)}, u32[]{:S(2)}) collective-permute-start(bf16[64,512]{1,0:T(8,128)(2,1)S(1)} %get-tuple-element.80.refs_0_), channel_id=1, source_target_pairs={{0,12},{1,13},{2,14},{3,15},{4,0},{5,1},{6,2},{7,3},{8,4},{9,5},{1... | collective-permute-start | bytes 196616 | tf_op jit(solution)/shard_map/ppermute | solution.py:55
  54.7 4.3 %collective-permute-start.15 = (bf16[64,512]{1,0:T(8,128)(2,1)S(1)}, bf16[64,512]{1,0:T(8,128)(2,1)S(1)}, u32[]{:S(2)}, u32[]{:S(2)}) collective-permute-start(bf16[64,512]{1,0:T(8,128)(2,1)S(1)} %get-tuple-element.84.refs_0_), channel_id=1, source_target_pairs={{0,2},{1,3},{2,0},{3,1},{4,6},{5,7},{6,4},{7,5},{8,10},{9,11},{10,... | collective-permute-start | bytes 196616 | tf_op jit(solution)/shard_map/ppermute | solution.py:55
  57.0 7.0 %copy-start.6 = (bf16[64,512]{1,0:T(8,128)(2,1)}, bf16[64,512]{1,0:T(8,128)(2,1)S(1)}, u32[]{:S(2)}) copy-start(bf16[64,512]{1,0:T(8,128)(2,1)S(1)} %collective-permute-done.12.refs_1_) | copy-start | bytes 196612
  58.0 5.9 %copy-start.8 = (bf16[64,512]{1,0:T(8,128)(2,1)}, bf16[64,512]{1,0:T(8,128)(2,1)S(1)}, u32[]{:S(2)}) copy-start(bf16[64,512]{1,0:T(8,128)(2,1)S(1)} %collective-permute-done.13.refs_2_) | copy-start | bytes 196612
  58.5 5.5 %copy-start.10 = (bf16[64,512]{1,0:T(8,128)(2,1)}, bf16[64,512]{1,0:T(8,128)(2,1)S(1)}, u32[]{:S(2)}) copy-start(bf16[64,512]{1,0:T(8,128)(2,1)S(1)} %collective-permute-done.14.refs_3_) | copy-start | bytes 196612
  59.0 13.9 %collective-permute-start.17 = (bf16[128,512]{1,0:T(8,128)(2,1)S(1)}, bf16[128,512]{1,0:T(8,128)(2,1)S(1)}, u32[]{:S(2)}, u32[]{:S(2)}) collective-permute-start(bf16[128,512]{1,0:T(8,128)(2,1)S(1)} %shard_map.112.refs_0_), channel_id=1, source_target_pairs={{0,4},{1,5},{2,6},{3,7},{4,8},{5,9},{6,10},{7,11},{8,12},{9,13},{1... | collective-permute-start | bytes 393224 | tf_op jit(solution)/shard_map/ppermute | solution.py:55
  60.4 12.5 %collective-permute-start.18 = (bf16[128,512]{1,0:T(8,128)(2,1)S(1)}, bf16[128,512]{1,0:T(8,128)(2,1)S(1)}, u32[]{:S(2)}, u32[]{:S(2)}) collective-permute-start(bf16[128,512]{1,0:T(8,128)(2,1)S(1)} %shard_map.112.refs_0_), channel_id=1, source_target_pairs={{0,8},{1,9},{2,10},{3,11},{4,12},{5,13},{6,14},{7,15},{8,0},{9,1},... | collective-permute-start | bytes 393224 | tf_op jit(solution)/shard_map/ppermute | solution.py:55
  62.3 10.6 %collective-permute-start.19 = (bf16[128,512]{1,0:T(8,128)(2,1)S(1)}, bf16[128,512]{1,0:T(8,128)(2,1)}, u32[]{:S(2)}, u32[]{:S(2)}) collective-permute-start(bf16[128,512]{1,0:T(8,128)(2,1)S(1)} %shard_map.112.refs_0_), channel_id=1, source_target_pairs={{0,12},{1,13},{2,14},{3,15},{4,0},{5,1},{6,2},{7,3},{8,4},{9,5},{1... | collective-permute-start | bytes 393224 | tf_op jit(solution)/shard_map/ppermute | solution.py:55
  64.5 0.8 copy-start.5
  65.4 0.8 copy-start.7
  66.2 0.8 copy-start.9
  67.0 0.8 copy-start.11
  67.9 8.7 %copy-start.1 = (bf16[2048,768]{1,0:T(8,128)(2,1)S(1)}, bf16[2048,768]{1,0:T(8,128)(2,1)}, u32[]{:S(2)}) copy-start(bf16[2048,768]{1,0:T(8,128)(2,1)} %refs_6_.2) | copy-start | bytes 9437188
  67.9 6.5 %collective-permute-start.16 = (bf16[64,2048]{1,0:T(8,128)(2,1)S(1)}, bf16[64,2048]{1,0:T(8,128)(2,1)S(1)}, u32[]{:S(2)}, u32[]{:S(2)}) collective-permute-start(bf16[64,2048]{1,0:T(8,128)(2,1)S(1)} %shard_map.111.refs_0_), channel_id=1, source_target_pairs={{0,2},{1,3},{2,0},{3,1},{4,6},{5,7},{6,4},{7,5},{8,10},{9,11},{10,... | collective-permute-start | bytes 786440 | tf_op jit(solution)/shard_map/ppermute | solution.py:55
  68.2 1.0 copy-start.3
  73.9 2.7 %collective-permute-start.22 = (bf16[128,2048]{1,0:T(8,128)(2,1)S(1)}, bf16[128,2048]{1,0:T(8,128)(2,1)S(1)}, u32[]{:S(2)}, u32[]{:S(2)}) collective-permute-start(bf16[128,2048]{1,0:T(8,128)(2,1)S(1)} %shard_map.114.refs_2_), channel_id=1, source_target_pairs={{0,1},{1,0},{2,3},{3,2},{4,5},{5,4},{6,7},{7,6},{8,9},{9,8},{10,11... | collective-permute-start | bytes 1572872 | tf_op jit(solution)/shard_map/ppermute | solution.py:55
  74.0 2.3 %collective-permute-start.20 = (bf16[64,2048]{1,0:T(8,128)(2,1)S(1)}, bf16[64,2048]{1,0:T(8,128)(2,1)S(1)}, u32[]{:S(2)}, u32[]{:S(2)}) collective-permute-start(bf16[64,2048]{1,0:T(8,128)(2,1)S(1)} %shard_map.111.refs_0_), channel_id=1, source_target_pairs={{0,1},{1,0},{2,3},{3,2},{4,5},{5,4},{6,7},{7,6},{8,9},{9,8},{10,11... | collective-permute-start | bytes 786440 | tf_op jit(solution)/shard_map/ppermute | solution.py:55
  74.5 2.1 %collective-permute-start.21 = (bf16[64,2048]{1,0:T(8,128)(2,1)S(1)}, bf16[64,2048]{1,0:T(8,128)(2,1)S(1)}, u32[]{:S(2)}, u32[]{:S(2)}) collective-permute-start(bf16[64,2048]{1,0:T(8,128)(2,1)S(1)} %collective-permute-done.16.refs_1_), channel_id=1, source_target_pairs={{0,1},{1,0},{2,3},{3,2},{4,5},{5,4},{6,7},{7,6},{8,9},{9,8},{10,11... | collective-permute-start | bytes 786440 | tf_op jit(solution)/shard_map/ppermute | solution.py:55
  79.6 1.4 %collective-permute-start.23 = (bf16[256,256]{1,0:T(8,128)(2,1)S(1)}, bf16[256,256]{1,0:T(8,128)(2,1)S(1)}, u32[]{:S(2)}, u32[]{:S(2)}) collective-permute-start(bf16[256,256]{1,0:T(8,128)(2,1)S(1)} %get-tuple-element.95), channel_id=1, source_target_pairs={{0,1},{1,0},{2,3},{3,2},{4,5},{5,4},{6,7},{7,6},{8,9},{9,8},{10,11... | collective-permute-start | bytes 393224 | tf_op jit(solution)/shard_map/ppermute | solution.py:55
  81.0 4.3 %collective-permute-start.24 = (bf16[128,256]{1,0:T(8,128)(2,1)S(1)}, bf16[128,256]{1,0:T(8,128)(2,1)S(1)}, u32[]{:S(2)}, u32[]{:S(2)}) collective-permute-start(bf16[128,256]{1,0:T(8,128)(2,1)S(1)} %get-tuple-element.97), channel_id=1, source_target_pairs={{0,2},{1,3},{2,0},{3,1},{4,6},{5,7},{6,4},{7,5},{8,10},{9,11},{10,... | collective-permute-start | bytes 196616 | tf_op jit(solution)/shard_map/ppermute | solution.py:55
  85.4 6.4 %collective-permute-start.25 = (bf16[128,256]{1,0:T(8,128)(2,1)S(1)}, bf16[128,256]{1,0:T(8,128)(2,1)S(1)}, u32[]{:S(2)}, u32[]{:S(2)}) collective-permute-start(bf16[128,256]{1,0:T(8,128)(2,1)S(1)} %get-tuple-element.99), channel_id=1, source_target_pairs={{0,4},{1,5},{2,6},{3,7},{4,8},{5,9},{6,10},{7,11},{8,12},{9,13},{1... | collective-permute-start | bytes 196616 | tf_op jit(solution)/shard_map/ppermute | solution.py:55
  86.3 7.1 %collective-permute-start.26 = (bf16[128,256]{1,0:T(8,128)(2,1)S(1)}, bf16[128,256]{1,0:T(8,128)(2,1)S(1)}, u32[]{:S(2)}, u32[]{:S(2)}) collective-permute-start(bf16[128,256]{1,0:T(8,128)(2,1)S(1)} %get-tuple-element.99), channel_id=1, source_target_pairs={{0,8},{1,9},{2,10},{3,11},{4,12},{5,13},{6,14},{7,15},{8,0},{9,1},... | collective-permute-start | bytes 196616 | tf_op jit(solution)/shard_map/ppermute | solution.py:55
  87.6 5.9 %collective-permute-start.27 = (bf16[128,256]{1,0:T(8,128)(2,1)S(1)}, bf16[128,256]{1,0:T(8,128)(2,1)S(1)}, u32[]{:S(2)}, u32[]{:S(2)}) collective-permute-start(bf16[128,256]{1,0:T(8,128)(2,1)S(1)} %get-tuple-element.99), channel_id=1, source_target_pairs={{0,12},{1,13},{2,14},{3,15},{4,0},{5,1},{6,2},{7,3},{8,4},{9,5},{1... | collective-permute-start | bytes 196616 | tf_op jit(solution)/shard_map/ppermute | solution.py:55
  93.5 4.3 %collective-permute-start.28 = (bf16[128,256]{1,0:T(8,128)(2,1)S(1)}, bf16[128,256]{1,0:T(8,128)(2,1)S(1)}, u32[]{:S(2)}, u32[]{:S(2)}) collective-permute-start(bf16[128,256]{1,0:T(8,128)(2,1)S(1)} %shard_map.118.refs_0_), channel_id=1, source_target_pairs={{0,2},{1,3},{2,0},{3,1},{4,6},{5,7},{6,4},{7,5},{8,10},{9,11},{10,... | collective-permute-start | bytes 196616 | tf_op jit(solution)/shard_map/ppermute | solution.py:55
  94.7 3.1 %collective-permute-start.29 = (bf16[128,256]{1,0:T(8,128)(2,1)S(1)}, bf16[128,256]{1,0:T(8,128)(2,1)S(1)}, u32[]{:S(2)}, u32[]{:S(2)}) collective-permute-start(bf16[128,256]{1,0:T(8,128)(2,1)S(1)} %shard_map.118.refs_0_), channel_id=1, source_target_pairs={{0,1},{1,0},{2,3},{3,2},{4,5},{5,4},{6,7},{7,6},{8,9},{9,8},{10,11... | collective-permute-start | bytes 196616 | tf_op jit(solution)/shard_map/ppermute | solution.py:55
  97.8 1.3 %collective-permute-start.30 = (bf16[128,256]{1,0:T(8,128)(2,1)S(1)}, bf16[128,256]{1,0:T(8,128)(2,1)S(1)}, u32[]{:S(2)}, u32[]{:S(2)}) collective-permute-start(bf16[128,256]{1,0:T(8,128)(2,1)S(1)} %collective-permute-done.28.refs_1_), channel_id=1, source_target_pairs={{0,1},{1,0},{2,3},{3,2},{4,5},{5,4},{6,7},{7,6},{8,9},{9,8},{10,11... | collective-permute-start | bytes 196616 | tf_op jit(solution)/shard_map/ppermute | solution.py:55

commit v8 on v7

--- a/solution.py
+++ b/solution.py
@@ -28,7 +28,7 @@
 STEP_SIZE = 0.3
 MIB = 1024 * 1024
 VMEM_BYTES = 40 * MIB
-REDUCE_SHARE = 0.375
+REDUCE_SHARE = 0.5
 GATHER_SHARE = 0.5
 BF16 = jnp.bfloat16
 F32 = jnp.float32
@@ -46,12 +46,16 @@
     return lax.rem(lax.div(lax.axis_index("band"), jnp.int32(stride)), jnp.int32(size))
 
 
-def shifted(array, count, level, step):
+def neighbour(array, count, step):
+    return lax.ppermute(array, "band", [(i, (i + step) % count) for i in range(count)])
+
+
+def swapped(array, count, level, step):
     size, stride = level
     pairs = []
     for device in range(count):
         place = device // stride % size
-        pairs.append((device, device + ((place + step) % size - place) * stride))
+        pairs.append((device, device + ((place ^ step) - place) * stride))
     return lax.ppermute(array, "band", pairs)
 
 
@@ -154,7 +158,7 @@
     me = position(level)
     rows, width = outs[0].shape
     for step, out in enumerate(outs):
-        at = lax.rem(me + step, jnp.int32(level[0]))
+        at = me ^ step
         if along == 0:
             part = (rows_at(at, rows), slice(None))
         else:
@@ -203,11 +207,10 @@
 
 def place_body(level, along, *refs):
     *parts, out_ref = refs
-    size, _ = level
     me = position(level)
     width = parts[0].shape[along]
     for step, ref in enumerate(parts):
-        at = pl.multiple_of(lax.rem(me - step + size, jnp.int32(size)) * width, width)
+        at = pl.multiple_of((me ^ step) * width, width)
         if along == 0:
             out_ref[pl.ds(at, width), :] = ref[...]
         else:
@@ -245,9 +248,9 @@
             total = total + (KINETIC * COEFFS[offset]) * pair
         total = total + (e_ref[...] - pot_ref[:, cols]) * low.astype(F32)
         out_ref[:, cols] = total - v_ref[:, cols] * o_ref[:, cols].astype(F32)
-    group_rows, width, blk, bands = sizes
-    start = jnp.clip(pl.program_id(0) * group_rows - REACH * blk, 0, bands - width)
-    block = (lax.broadcasted_iota(jnp.int32, mask_ref.shape, 1) + start) // blk
+    group_rows, blk = sizes
+    block = lax.broadcasted_iota(jnp.int32, mask_ref.shape, 1) // blk
+    block = block + (pl.program_id(0) * (group_rows // blk) - REACH)
     lowest = first_ref[...]
     inside = (block >= lowest) & (block < lowest + many_ref[...])
     mask_ref[...] = jnp.where(inside, 1.0, 0.0).astype(BF16)
@@ -262,7 +265,7 @@
     line = pl.BlockSpec((1, cells), lambda i: (0, 0))
     column = pl.BlockSpec((group_rows, 1), lambda i: (i, 0))
     return pl.pallas_call(
-        functools.partial(local_body, depth, (group_rows, width, blk, bands)),
+        functools.partial(local_body, depth, (group_rows, blk)),
         grid=(bands // group_rows,),
         out_shape=outs,
         in_specs=[
@@ -283,53 +286,98 @@
     )(response, low, high, orbitals, matrix, *lines, *columns)
 
 
-def first_orbital(group, group_rows, width, bands, blk):
-    return max(0, min(group * group_rows - REACH * blk, bands - width))
-
-
-def apply_body(core, across, block, group_rows, width, blk, *refs):
+def pad_orbitals(o_ref, pad_ref, blk):
+    bands, cells = o_ref.shape
+    edge = REACH * blk
+    pad_ref[:edge, :] = jnp.zeros((edge, cells), pad_ref.dtype)
+    pad_ref[edge : edge + bands, :] = o_ref[...]
+    pad_ref[edge + bands :, :] = jnp.zeros((edge, cells), pad_ref.dtype)
+
+
+def subgroup(shape, blk):
+    return lax.broadcasted_iota(jnp.int32, shape, 1) // (2 * blk)
+
+
+def packed(sums, blk):
+    rows = sums.shape[0]
+    sub = 2 * blk
+    near, far = sums[:, :rows], sums[:, rows:]
+    column = subgroup((rows, rows), blk)
+    row = lax.broadcasted_iota(jnp.int32, (rows, rows), 0) // sub
+    main = jnp.where(column >= row, near, far)
+    rest = far[:sub, :]
+    for k in range(1, rows // sub):
+        rest = jnp.where(column[:sub, :] == k, far[k * sub : (k + 1) * sub, :], rest)
+    return main, rest
+
+
+def unpacked(main, rest, blk):
+    rows = main.shape[0]
+    sub = 2 * blk
+    column = subgroup((rows, rows), blk)
+    row = lax.broadcasted_iota(jnp.int32, (rows, rows), 0) // sub
+    near = jnp.where(column >= row, main, 0.0)
+    last = jnp.where(column == row, jnp.concatenate([rest] * (rows // sub), axis=0), 0.0)
+    return near, jnp.where(column < row, main, last)
+
+
+def apply_body(core, across, block, group_rows, blk, other, *refs):
     size = across[0]
-    blocks = refs[: 2 * (size + 1)]
-    p_ref, base_ref, o_ref, u_ref, send_ref, keep_ref, c_ref, s_ref = refs[2 * (size + 1) :]
-    bands, cells = u_ref.shape
+    blocks = refs[: size + 1]
+    p_ref, base_ref, o_ref, u_ref, s_ref, c_ref, pad_ref = refs[size + 1 :]
+    rows, cells = u_ref.shape
     c, x = position(core), position(across)
-    half = bands // 2
+    side = 1 - c if other else c
     first = blocks[0].shape[0]
-    for k, ref in enumerate(blocks):
-        side, step = divmod(k, size + 1)
-        at = (c if side == 0 else 1 - c) * half
-        if step < size:
-            at = at + lax.rem(x - step + size, jnp.int32(size)) * block
-            c_ref[pl.ds(pl.multiple_of(at, 16), first), :] = ref[...]
-        else:
-            rest = block - first
-            for i in range(size):
-                there = pl.ds(pl.multiple_of(at + i * block + first, 16), rest)
-                c_ref[there, :] = ref[i * rest : (i + 1) * rest, :]
+    for step, ref in enumerate(blocks[:size]):
+        at = (x ^ step) * block
+        c_ref[pl.ds(pl.multiple_of(at, 16), first), :] = ref[...]
+    rest = block - first
+    for i in range(size):
+        there = slice(i * block + first, (i + 1) * block)
+        c_ref[there, :] = blocks[size][i * rest : (i + 1) * rest, :]
+    mine = pl.ds(pl.multiple_of(side * rows, rows), rows)
     tile = 256 if cells % 256 == 0 else 128
     for t in range(cells // tile):
         cols = slice(t * tile, (t + 1) * tile)
-        u_ref[:, cols] = base_ref[:, cols] + jnp.dot(
+        u_ref[:, cols] = base_ref[mine, cols] + jnp.dot(
             c_ref[...], p_ref[:, cols], preferred_element_type=F32
         )
-    for g in range(bands // group_rows):
-        start = first_orbital(g, group_rows, width, bands, blk)
-        mine = slice(g * group_rows, (g + 1) * group_rows)
-        s_ref[mine, :] = lax.dot_general(
-            u_ref[mine, :].astype(BF16),
-            o_ref[start : start + width, :],
+    pad_orbitals(o_ref, pad_ref, blk)
+    height = group_rows + 2 * blk
+    for g in range(rows // group_rows):
+        start = pl.multiple_of(side * rows + g * group_rows, group_rows)
+        sums = lax.dot_general(
+            u_ref[g * group_rows : (g + 1) * group_rows, :].astype(BF16),
+            pad_ref[pl.ds(start, 2 * group_rows), :],
             NT,
             preferred_element_type=F32,
         )
-    send_ref[...] = s_ref[pl.ds(pl.multiple_of((1 - c) * half, half), half), :].astype(BF16)
-    keep_ref[...] = s_ref[pl.ds(pl.multiple_of(c * half, half), half), :]
+        main, rest_sums = packed(sums, blk)
+        s_ref[g * height : g * height + group_rows, :] = main.astype(s_ref.dtype)
+        s_ref[g * height + group_rows : (g + 1) * height, :] = rest_sums.astype(s_ref.dtype)
+
+
+def apply(blocks, projectors, base, orbitals, core, across, block, group_rows, blk, other):
+    bands, cells = base.shape
+    rows = bands // 2
+    count = projectors.shape[0]
+    height = rows // group_rows * (group_rows + 2 * blk)
+    return local_call(
+        functools.partial(apply_body, core, across, block, group_rows, blk, other),
+        [struct((rows, cells), F32), struct((height, group_rows), BF16 if other else F32)],
+        [*blocks, projectors, base, orbitals],
+        flops=2 * rows * cells * (count + 2 * group_rows),
+        scratch=[
+            pltpu.VMEM((rows, count), BF16),
+            pltpu.VMEM((bands + 2 * REACH * blk, cells), BF16),
+        ],
+    )
 
 
 def sum_body(keep_ref, *refs):
     *taken, total_ref, low_ref = refs
-    total = keep_ref[...]
-    for ref in taken:
-        total = total + ref[...].astype(F32)
+    total = total_of(keep_ref, taken, ...)
     total_ref[...] = total
     low_ref[...] = total.astype(BF16)
 
@@ -339,37 +387,46 @@
     return local_call(sum_body, outs, [keep, *taken])
 
 
-def project_body(core, across, width, blk, *refs):
-    size = across[0]
-    blocks = refs[: 2 * size]
-    o_ref, u_ref, r_ref, mask_ref, updated_ref, residual_ref, w_ref = refs[2 * size :]
-    bands = o_ref.shape[0]
-    half = bands // 2
-    group_rows = u_ref.shape[0]
+def project_body(core, blk, *refs):
+    w_own, w_other, u_own, u_other, o_ref, r_ref, mask_ref = refs[:7]
+    updated_ref, residual_ref, pad_ref, w_ref, u_ref = refs[7:]
+    rows = u_ref.shape[0]
+    height = w_ref.shape[0]
+    per = u_own.shape[0] // rows
     g = pl.program_id(0)
+    own = lax.div(g, jnp.int32(per)) == position(core)
+    local = lax.rem(g, jnp.int32(per))
+    w_rows = pl.ds(pl.multiple_of(local * height, 16), height)
+    u_rows = pl.ds(pl.multiple_of(local * rows, rows), rows)
 
     @pl.when(g == 0)
     def _():
-        c, x = position(core), position(across)
-        for k, ref in enumerate(blocks):
-            side, step = divmod(k, size)
-            at = (c if side == 0 else 1 - c) * half
-            at = at + lax.rem(x - step + size, jnp.int32(size)) * ref.shape[0]
-            w_ref[pl.ds(pl.multiple_of(at, 16), ref.shape[0]), :] = ref[...]
-
-    start = jnp.clip(g * group_rows - REACH * blk, 0, bands - width)
-    window = o_ref[pl.ds(pl.multiple_of(start, blk), width), :]
-    mine = pl.ds(pl.multiple_of(g * group_rows, group_rows), group_rows)
-    inside = mask_ref[...].astype(F32) > 0.5
-    weights = jnp.where(inside, w_ref[mine, :].astype(F32), 0.0).astype(BF16)
-    residual = u_ref[...] - jnp.dot(weights, window, preferred_element_type=F32)
+        pad_orbitals(o_ref, pad_ref, blk)
+
+    @pl.when(own)
+    def _():
+        w_ref[...] = w_own[w_rows, :]
+        u_ref[...] = u_own[u_rows, :]
+
+    @pl.when(jnp.logical_not(own))
+    def _():
+        w_ref[...] = w_other[w_rows, :]
+        u_ref[...] = u_other[u_rows, :]
+
+    main, rest = w_ref[:rows, :].astype(F32), w_ref[rows:, :].astype(F32)
+    start = pl.multiple_of(g * rows, rows)
+    residual = u_ref[...]
+    for k, part in enumerate(unpacked(main, rest, blk)):
+        inside = mask_ref[:, k * rows : (k + 1) * rows].astype(F32) > 0.5
+        weights = jnp.where(inside, part, 0.0).astype(BF16)
+        window = pad_ref[pl.ds(pl.multiple_of(start + k * rows, rows), rows), :]
+        residual = residual - jnp.dot(weights, window, preferred_element_type=F32)
     residual_ref[...] = residual.astype(BF16)
     updated_ref[...] = (r_ref[...].astype(F32) + STEP_SIZE * residual).astype(BF16)
 
 
-def project(weights, orbitals, unprojected, response, mask, core, across, group_rows, blk):
+def project(weights, unprojected, orbitals, response, mask, core, group_rows, blk):
     bands, cells = response.shape
-    width = mask.shape[1]
     out = struct((bands, cells), BF16)
     here = pl.BlockSpec((group_rows, cells), lambda g: (g, 0))
 
@@ -377,21 +434,25 @@
         return pl.BlockSpec(a.shape, lambda g: (0, 0))
 
     return pl.pallas_call(
-        functools.partial(project_body, core, across, width, blk),
+        functools.partial(project_body, core, blk),
         grid=(bands // group_rows,),
         out_shape=(out, out),
         in_specs=[
-            *[full(a) for a in weights],
-            full(orbitals),
+            *[full(a) for a in (*weights, *unprojected, orbitals)],
             here,
-            here,
-            pl.BlockSpec((group_rows, width), lambda g: (g, 0)),
+            pl.BlockSpec((group_rows, mask.shape[1]), lambda g: (g, 0)),
         ],
         out_specs=(here, here),
-        scratch_shapes=[pltpu.VMEM((bands, width), BF16)],
+        scratch_shapes=[
+            pltpu.VMEM((bands + 2 * REACH * blk, cells), BF16),
+            pltpu.VMEM((group_rows + 2 * blk, group_rows), BF16),
+            pltpu.VMEM((group_rows, cells), F32),
+        ],
         compiler_params=params(),
-        cost_estimate=cost(2 * bands * width * cells, orbitals, unprojected, response, out, out),
-    )(*weights, orbitals, unprojected, response, mask)
+        cost_estimate=cost(
+            4 * bands * group_rows * cells, orbitals, *unprojected, response, out, out
+        ),
+    )(*weights, *unprojected, orbitals, response, mask)
 
 
 def shards(
@@ -402,12 +463,11 @@
     projections = projectors.shape[0]
     halo = 6 * GY * GZ
     core, across, along = levels_of(count)
-    ring = (count, 1)
     ace_scale = 1.0 / math.sqrt(cells * projections)
     window_scale = 1.0 / math.sqrt(cells * bands)
     blk = bands // NBLK
     group_rows = GROUP_BLOCKS * blk
-    width = (GROUP_BLOCKS + 2 * REACH) * blk
+    width = 2 * group_rows
     half = bands // 2
     block = half // across[0]
     first = max(16, round(REDUCE_SHARE * block / 16) * 16)
@@ -417,23 +477,23 @@
     columns = tuple(a[:, None] for a in (energies, window_start, block_count))
 
     def to(array, level):
-        return [shifted(array, count, level, k) for k in range(1, level[0])]
+        return [swapped(array, count, level, k) for k in range(1, level[0])]
 
     def parts_to(parts, level):
-        return [shifted(part, count, level, k + 1) for k, part in enumerate(parts)]
-
-    low = shifted(response[:, local_cells - halo :], count, ring, 1)
-    high = shifted(response[:, :halo], count, ring, -1)
+        return [swapped(part, count, level, k + 1) for k, part in enumerate(parts)]
+
+    low = neighbour(response[:, local_cells - halo :], count, 1)
 
     sent_x, sent_z = partial_intersections(response, projectors, core, True, block, first)
-    sent_z = shifted(sent_z, count, core, 1)
-    sent_x = shifted(sent_x, count, core, 1)
+    sent_z = swapped(sent_z, count, core, 1)
+    sent_x = swapped(sent_x, count, core, 1)
     keep_x, keep_z = partial_intersections(response, projectors, core, False, block, first)
     keep_z, *parts_z = split(keep_z, [sent_z], along, 1)
     keep_x, *parts_x = split(keep_x, [sent_x], across, 0)
-    taken_z, taken_x, low, high = lax.optimization_barrier(
-        (parts_to(parts_z, along), parts_to(parts_x, across), low, high)
-    )
+    taken_z, taken_x, low, head = lax.optimization_barrier(
+        (parts_to(parts_z, along), parts_to(parts_x, across), low, response[:, :halo])
+    )
+    high = neighbour(head, count, -1)
     keep_x, *parts_x = split(keep_x, taken_x, along, 1)
     keep_z, *parts_z = split(keep_z, taken_z, across, 0)
     taken_x, taken_z = lax.optimization_barrier(
@@ -459,27 +519,17 @@
     blocks_x = [block_x, *to(block_x, across)]
     pieces_z, base = lax.optimization_barrier(([block_z, *to(block_z, along)], base))
     blocks = [*blocks_x, place(pieces_z, along, 1)]
-    blocks += [shifted(part, count, core, 1) for part in blocks]
-
-    unprojected, send, keep = local_call(
-        functools.partial(apply_body, core, across, block, group_rows, width, blk),
-        [
-            struct((bands, local_cells), F32),
-            struct((half, width), BF16),
-            struct((half, width), F32),
-        ],
-        [*blocks, projectors, base, orbitals],
-        flops=2 * bands * local_cells * (projections + width),
-        scratch=[pltpu.VMEM((bands, projections), BF16), pltpu.VMEM((bands, width), F32)],
-    )
-    keep, *parts = split(keep, to(send, core), across, 0)
-    total, low = add_up(keep, parts_to(parts, across))
-    weights = finish(total, to(low, along), window_scale)
-    weights = [weights, *to(weights, across)]
-    weights += [shifted(part, count, core, 1) for part in weights]
-    return project(
-        weights, orbitals, unprojected, response, mask, core, across, group_rows, blk
-    )
+    others = [swapped(part, count, core, 1) for part in blocks]
+    sizes = (core, across, block, group_rows, blk)
+    wide, keep = apply(blocks, projectors, base, orbitals, *sizes, False)
+    others, keep = lax.optimization_barrier((others, keep))
+    other_wide, part = apply(others, projectors, base, orbitals, *sizes, True)
+    unprojected = (wide, other_wide)
+    total, part = add_up(keep, to(part, core))
+    total, part = add_up(total, to(part, across))
+    own = finish(total, to(part, along), window_scale)
+    weights = (own, *to(own, core))
+    return project(weights, unprojected, orbitals, response, mask, core, group_rows, blk)
 
 
 def solution(mesh):

time: 104 us -> 108 us (1.038)
  local copies, waits for them, and re-layouts: 6.74 us -> 17.3 us
  waiting for transfers between devices: 41.8 us -> 35.9 us
  starting transfers between devices: 35.8 us -> 34.4 us
    unnamed x34 -> x46, local copies, waits for them, and re-layouts: 6.29 us -> 14.8 us
    ppermute x31 -> x29, waiting for transfers between devices: 41.8 us -> 35.9 us  [the longest x27 35.9 us: swapped(): return lax.ppermute(array, 'band', pairs)]
    broadcast_in_dim x3, local copies, waits for them, and re-layouts: 0.43 us -> 2.57 us  [shards(): columns = tuple((a[:, None] for a in (energies, window_start, block_count)))]
    ppermute x31 -> x29, starting transfers between devices: 35.8 us -> 34.4 us  [the longest x27 30.1 us: swapped(): return lax.ppermute(array, 'band', pairs)]
    pallas_call x12 -> x13, Pallas kernels: 4.42 us -> 4.77 us  [local_call(): pl.pallas_call(body, out_shape=outs, in_specs=[whole() for _ in args], ou...]
  transfers between devices with their start and end apart: 31 -> 29, of which waited for: 17 -> 15; matrix products, arithmetic and copies ran while one was open for 0% -> 2% of each run, Pallas kernels for 8% -> 9%
where the time goes in v8:
time: 108 us; the launch traced here: 107 us
  waiting for transfers between devices  35.9 us (33%)
  starting transfers between devices  34.4 us (32%)
  Pallas kernels  18.2 us (17%)
  local copies, waits for them, and re-layouts  17.3 us (16%)
    ppermute x27, waiting for transfers between devices, swapped(): return lax.ppermute(array, 'band', pairs)  35.9 us
    ppermute x27, starting transfers between devices, swapped(): return lax.ppermute(array, 'band', pairs)  30.1 us
    unnamed x46, local copies, waits for them, and re-layouts  14.8 us
    pallas_call x2, Pallas kernels, partial_intersections(): pl.pallas_call(functools.partial(partial_body, core, other, block), grid=...  5.69 us
    pallas_call x13, Pallas kernels, local_call(): pl.pallas_call(body, out_shape=outs, in_specs=[whole() for _ in args], ou...  4.77 us
    ppermute x2, starting transfers between devices, neighbour(): lax.ppermute(array, 'band', [(i, (i + step) % count) for i in range(count)])  4.29 us
    pallas_call x1, Pallas kernels, project(): pl.pallas_call(functools.partial(project_body, core, blk), grid=(bands //...  4.03 us
    pallas_call x1, Pallas kernels, local_part(): pl.pallas_call(functools.partial(local_body, depth, (group_rows, blk)), g...  3.71 us
  transfers between devices with their start and end apart: 29, of which 15 were waited for; matrix products, arithmetic and copies ran while one was open for 2% of the time, Pallas kernels for 9%

profile of v8, /device:TPU:0, one launch (start us, length us, event | category | flops | bytes accessed | tf_op | source)
XLA Modules:
  0.0 106.7 jit_solution(6708278506259951332)
XLA Ops:
  0.6 1.9 %copy-done = bf16[2048,768]{1,0:T(8,128)(2,1)S(1)} copy-done((bf16[2048,768]{1,0:T(8,128)(2,1)S(1)}, bf16[2048,768]{1,0:T(8,128)(2,1)}, u32[]{:S(2)}) %copy-start) | copy-done | bytes 3145752
  2.5 2.8 %shard_map.105 = (bf16[128,2048]{1,0:T(8,128)(2,1)S(1)}, bf16[128,2048]{1,0:T(8,128)(2,1)S(1)}) custom-call(bf16[512,768]{1,0:T(8,128)(2,1)} %refs_5_.5, bf16[2048,768]{1,0:T(8,128)(2,1)S(1)} %copy-done), custom_call_target="tpu_custom_call" | custom-call | flops 805306368 | bytes 4194304 | tf_op jit(solution)/shard_map/pallas_call | solution.py:127
  5.4 0.5 collective-permute-start
  5.9 2.6 %collective-permute-start.1 = (bf16[128,2048]{1,0:T(8,128)(2,1)S(1)}, bf16[128,2048]{1,0:T(8,128)(2,1)S(1)}, u32[]{:S(2)}, u32[]{:S(2)}) collective-permute-start(bf16[128,2048]{1,0:T(8,128)(2,1)S(1)} %get-tuple-element.61), channel_id=1, source_target_pairs={{0,1},{1,0},{2,3},{3,2},{4,5},{5,4},{6,7},{7,6},{8,9},{9,8},{10,11... | collective-permute-start | bytes 1572872 | tf_op jit(solution)/shard_map/ppermute | solution.py:59
  8.5 2.9 %shard_map.104 = (f32[128,2048]{1,0:T(8,128)S(1)}, f32[128,2048]{1,0:T(8,128)S(1)}) custom-call(bf16[512,768]{1,0:T(8,128)(2,1)} %refs_5_.5, bf16[2048,768]{1,0:T(8,128)(2,1)S(1)} %copy-done), custom_call_target="tpu_custom_call" | custom-call | flops 805306368 | bytes 5242880 | tf_op jit(solution)/shard_map/pallas_call | solution.py:127
  11.5 0.1 shard_map.106
  11.6 1.6 %collective-permute-start.5 = (bf16[64,2048]{1,0:T(8,128)(2,1)S(1)}, bf16[64,2048]{1,0:T(8,128)(2,1)S(1)}, u32[]{:S(2)}, u32[]{:S(2)}) collective-permute-start(bf16[64,2048]{1,0:T(8,128)(2,1)S(1)} %get-tuple-element.65), channel_id=1, source_target_pairs={{0,2},{1,3},{2,0},{3,1},{4,6},{5,7},{6,4},{7,5},{8,10},{9,11},{10,... | collective-permute-start | bytes 786440 | tf_op jit(solution)/shard_map/ppermute | solution.py:59
  13.2 0.1 shard_map.107
  13.3 1.6 %collective-permute-start.2 = (bf16[128,512]{1,0:T(8,128)(2,1)S(1)}, bf16[128,512]{1,0:T(8,128)(2,1)S(1)}, u32[]{:S(2)}, u32[]{:S(2)}) collective-permute-start(bf16[128,512]{1,0:T(8,128)(2,1)S(1)} %get-tuple-element.62), channel_id=1, source_target_pairs={{0,4},{1,5},{2,6},{3,7},{4,0},{5,1},{6,2},{7,3},{8,12},{9,13},{10,... | collective-permute-start | bytes 393224 | tf_op jit(solution)/shard_map/ppermute | solution.py:59
  15.0 1.4 %collective-permute-start.3 = (bf16[128,512]{1,0:T(8,128)(2,1)S(1)}, bf16[128,512]{1,0:T(8,128)(2,1)S(1)}, u32[]{:S(2)}, u32[]{:S(2)}) collective-permute-start(bf16[128,512]{1,0:T(8,128)(2,1)S(1)} %get-tuple-element.63), channel_id=1, source_target_pairs={{0,8},{1,9},{2,10},{3,11},{4,12},{5,13},{6,14},{7,15},{8,0},{9,1},... | collective-permute-start | bytes 393224 | tf_op jit(solution)/shard_map/ppermute | solution.py:59
  16.3 1.4 %collective-permute-start.4 = (bf16[128,512]{1,0:T(8,128)(2,1)S(1)}, bf16[128,512]{1,0:T(8,128)(2,1)S(1)}, u32[]{:S(2)}, u32[]{:S(2)}) collective-permute-start(bf16[128,512]{1,0:T(8,128)(2,1)S(1)} %get-tuple-element.64), channel_id=1, source_target_pairs={{0,12},{1,13},{2,14},{3,15},{4,8},{5,9},{6,10},{7,11},{8,4},{9,5},... | collective-permute-start | bytes 393224 | tf_op jit(solution)/shard_map/ppermute | solution.py:59
  17.8 2.3 %collective-permute-done.2.refs_1_ = bf16[128,512]{1,0:T(8,128)(2,1)S(1)} collective-permute-done((bf16[128,512]{1,0:T(8,128)(2,1)S(1)}, bf16[128,512]{1,0:T(8,128)(2,1)S(1)}, u32[]{:S(2)}, u32[]{:S(2)}) %collective-permute-start.2) | collective-permute-done | bytes 131104 | tf_op jit(solution)/shard_map/ppermute | solution.py:59
  20.1 7.7 %collective-permute-done.3.refs_2_ = bf16[128,512]{1,0:T(8,128)(2,1)S(1)} collective-permute-done((bf16[128,512]{1,0:T(8,128)(2,1)S(1)}, bf16[128,512]{1,0:T(8,128)(2,1)S(1)}, u32[]{:S(2)}, u32[]{:S(2)}) %collective-permute-start.3) | collective-permute-done | bytes 131104 | tf_op jit(solution)/shard_map/ppermute | solution.py:59
  27.8 4.2 %collective-permute-start.15 = (bf16[512,768]{1,0:T(8,128)(2,1)}, bf16[512,768]{1,0:T(8,128)(2,1)S(1)}, u32[]{:S(2)}, u32[]{:S(2)}) collective-permute-start(bf16[512,768]{1,0:T(8,128)(2,1)} %refs_5_.5), channel_id=1, source_target_pairs={{0,15},{1,0},{2,1},{3,2},{4,3},{5,4},{6,5},{7,6},{8,7},{9,8},{10,9... | collective-permute-start | bytes 2359304 | tf_op jit(solution)/shard_map/ppermute | solution.py:50
  32.3 1.9 %collective-permute-start.7 = (bf16[64,512]{1,0:T(8,128)(2,1)S(1)}, bf16[64,512]{1,0:T(8,128)(2,1)S(1)}, u32[]{:S(2)}, u32[]{:S(2)}) collective-permute-start(bf16[64,512]{1,0:T(8,128)(2,1)S(1)} %get-tuple-element.68), channel_id=1, source_target_pairs={{0,4},{1,5},{2,6},{3,7},{4,0},{5,1},{6,2},{7,3},{8,12},{9,13},{10,... | collective-permute-start | bytes 196616 | tf_op jit(solution)/shard_map/ppermute | solution.py:59
  34.2 1.0 collective-permute-start.8
  35.1 1.6 %collective-permute-start.9 = (bf16[64,512]{1,0:T(8,128)(2,1)S(1)}, bf16[64,512]{1,0:T(8,128)(2,1)S(1)}, u32[]{:S(2)}, u32[]{:S(2)}) collective-permute-start(bf16[64,512]{1,0:T(8,128)(2,1)S(1)} %get-tuple-element.70), channel_id=1, source_target_pairs={{0,12},{1,13},{2,14},{3,15},{4,8},{5,9},{6,10},{7,11},{8,4},{9,5},... | collective-permute-start | bytes 196616 | tf_op jit(solution)/shard_map/ppermute | solution.py:59
  36.7 5.3 %collective-permute-done.10.refs_5_ = bf16[64,512]{1,0:T(8,128)(2,1)S(1)} collective-permute-done((bf16[64,512]{1,0:T(8,128)(2,1)S(1)}, bf16[64,512]{1,0:T(8,128)(2,1)S(1)}, u32[]{:S(2)}, u32[]{:S(2)}) %collective-permute-start.10) | collective-permute-done | bytes 65568 | tf_op jit(solution)/shard_map/ppermute | solution.py:59
  42.0 2.6 %collective-permute-done.7.refs_1_ = bf16[64,512]{1,0:T(8,128)(2,1)S(1)} collective-permute-done((bf16[64,512]{1,0:T(8,128)(2,1)S(1)}, bf16[64,512]{1,0:T(8,128)(2,1)S(1)}, u32[]{:S(2)}, u32[]{:S(2)}) %collective-permute-start.7) | collective-permute-done | bytes 65568 | tf_op jit(solution)/shard_map/ppermute | solution.py:59
  44.6 4.9 %collective-permute-done.8.refs_2_ = bf16[64,512]{1,0:T(8,128)(2,1)S(1)} collective-permute-done((bf16[64,512]{1,0:T(8,128)(2,1)S(1)}, bf16[64,512]{1,0:T(8,128)(2,1)S(1)}, u32[]{:S(2)}, u32[]{:S(2)}) %collective-permute-start.8) | collective-permute-done | bytes 65568 | tf_op jit(solution)/shard_map/ppermute | solution.py:59
  49.6 1.3 %collective-permute-start.11 = (bf16[64,512]{1,0:T(8,128)(2,1)S(1)}, bf16[64,512]{1,0:T(8,128)(2,1)S(1)}, u32[]{:S(2)}, u32[]{:S(2)}) collective-permute-start(bf16[64,512]{1,0:T(8,128)(2,1)S(1)} %get-tuple-element.85.refs_0_), channel_id=1, source_target_pairs={{0,4},{1,5},{2,6},{3,7},{4,0},{5,1},{6,2},{7,3},{8,12},{9,13},{10,... | collective-permute-start | bytes 196616 | tf_op jit(solution)/shard_map/ppermute | solution.py:59
  50.9 0.8 collective-permute-start.12
  51.7 2.3 %collective-permute-start.13 = (bf16[64,512]{1,0:T(8,128)(2,1)S(1)}, bf16[64,512]{1,0:T(8,128)(2,1)S(1)}, u32[]{:S(2)}, u32[]{:S(2)}) collective-permute-start(bf16[64,512]{1,0:T(8,128)(2,1)S(1)} %get-tuple-element.85.refs_0_), channel_id=1, source_target_pairs={{0,12},{1,13},{2,14},{3,15},{4,8},{5,9},{6,10},{7,11},{8,4},{9,5},... | collective-permute-start | bytes 196616 | tf_op jit(solution)/shard_map/ppermute | solution.py:59
  54.0 0.6 copy-done.11
  54.7 0.6 copy-done.13
  55.3 1.5 %collective-permute-done.12.refs_2_ = bf16[64,512]{1,0:T(8,128)(2,1)S(1)} collective-permute-done((bf16[64,512]{1,0:T(8,128)(2,1)S(1)}, bf16[64,512]{1,0:T(8,128)(2,1)S(1)}, u32[]{:S(2)}, u32[]{:S(2)}) %collective-permute-start.12) | collective-permute-done | bytes 65568 | tf_op jit(solution)/shard_map/ppermute | solution.py:59
  56.7 0.6 copy-done.15
  57.4 0.5 collective-permute-done.13.refs_3_
  57.9 0.6 copy-done.17
  58.5 0.4 collective-permute-done.14.refs_1_
  58.9 0.9 copy-done.8
  59.8 0.5 collective-permute-start.19
  60.3 2.0 %collective-permute-start.20 = (bf16[128,512]{1,0:T(8,128)(2,1)S(1)}, bf16[128,512]{1,0:T(8,128)(2,1)}, u32[]{:S(2)}, u32[]{:S(2)}) collective-permute-start(bf16[128,512]{1,0:T(8,128)(2,1)S(1)} %shard_map.112.refs_0_), channel_id=1, source_target_pairs={{0,8},{1,9},{2,10},{3,11},{4,12},{5,13},{6,14},{7,15},{8,0},{9,1},... | collective-permute-start | bytes 393224 | tf_op jit(solution)/shard_map/ppermute | solution.py:59
  62.3 2.0 %collective-permute-start.21 = (bf16[128,512]{1,0:T(8,128)(2,1)S(1)}, bf16[128,512]{1,0:T(8,128)(2,1)}, u32[]{:S(2)}, u32[]{:S(2)}) collective-permute-start(bf16[128,512]{1,0:T(8,128)(2,1)S(1)} %shard_map.112.refs_0_), channel_id=1, source_target_pairs={{0,12},{1,13},{2,14},{3,15},{4,8},{5,9},{6,10},{7,11},{8,4},{9,5},... | collective-permute-start | bytes 393224 | tf_op jit(solution)/shard_map/ppermute | solution.py:59
  64.3 0.1 copy.11.refs_7_
  64.4 0.9 copy.12.refs_8_
  65.3 1.5 %copy.13.refs_9_ = s32[512,1]{1,0:T(8,128)} copy(s32[512,1]{0,1:T(1,128)} %bitcast.5) | data formatting | bytes 4096 | tf_op jit(solution)/shard_map/broadcast_in_dim | solution.py:477
  66.9 0.8 copy-done.12
  67.7 0.8 copy-done.14
  68.6 0.8 copy-done.16
  69.4 0.8 copy-done.18
  70.4 1.1 %copy-done.2 = bf16[512,768]{1,0:T(8,128)(2,1)S(1)} copy-done((bf16[512,768]{1,0:T(8,128)(2,1)S(1)}, bf16[512,768]{1,0:T(8,128)(2,1)}, u32[]{:S(2)}) %copy-start.2) | copy-done | bytes 786456
  71.5 0.9 copy-done.4
  72.4 0.9 copy-done.5
  73.4 1.1 %copy-done.7 = bf16[512,768]{1,0:T(8,128)(2,1)S(1)} copy-done((bf16[512,768]{1,0:T(8,128)(2,1)S(1)}, bf16[512,768]{1,0:T(8,128)(2,1)}, u32[]{:S(2)}) %copy-start.7) | copy-done | bytes 786456
  74.5 1.1 %copy-done.9 = bf16[512,768]{1,0:T(8,128)(2,1)S(1)} copy-done((bf16[512,768]{1,0:T(8,128)(2,1)S(1)}, bf16[512,768]{1,0:T(8,128)(2,1)}, u32[]{:S(2)}) %copy-start.9) | copy-done | bytes 786456
  75.7 0.8 copy-done.10
  76.5 3.7 %shard_map.113 = (f32[512,768]{1,0:T(8,128)S(1)}, bf16[512,256]{1,0:T(8,128)(2,1)S(1)}) custom-call(bf16[512,768]{1,0:T(8,128)(2,1)} %refs_5_.5, bf16[512,768]{1,0:T(8,128)(2,1)S(1)} %copy-done.7, bf16[512,768]{1,0:T(8,128)(2,1)S(1)} %copy-done.9, bf16[512,768]{1,0:T(8,128)(2,1)S(1)} %copy-done.2, bf16[2,128,128]{2,1,0:T(8,128)(2,1)S(1)} %copy-done.10, ...), custom_call_target="tpu_custom_call" | custom-call | flops 235929600 | bytes 4980736 | tf_op jit(solution)/shard_map/pallas_call | solution.py:267
  80.3 1.1 %shard_map.114.refs_2_ = bf16[128,2048]{1,0:T(8,128)(2,1)S(1)} custom-call(bf16[128,512]{1,0:T(8,128)(2,1)S(1)} %shard_map.112.refs_0_, bf16[128,512]{1,0:T(8,128)(2,1)} %collective-permute-done.19.refs_1_, bf16[128,512]{1,0:T(8,128)(2,1)} %collective-permute-done.20.refs_2_, bf16[128,512]{1,0:T(8,128)(2,1)} %collective-permute-done.21.refs_3_), custom_call_target="tpu_custom_call" | custom-call | bytes 1048576 | tf_op jit(solution)/shard_map/pallas_call | solution.py:91
  81.4 0.5 collective-permute-start.16
  82.0 1.6 %shard_map.115 = (f32[256,768]{1,0:T(8,128)S(1)}, f32[320,128]{1,0:T(8,128)S(1)}) custom-call(bf16[64,2048]{1,0:T(8,128)(2,1)S(1)} %shard_map.111.refs_0_, bf16[64,2048]{1,0:T(8,128)(2,1)S(1)} %collective-permute-done.17.refs_1_, bf16[128,2048]{1,0:T(8,128)(2,1)S(1)} %shard_map.114.refs_2_, bf16[2048,768]{1,0:T(8,128)(2,1)S(1)} %copy-done.1, ...), custom_call_target="tpu_custom_call" | custom-call | flops 905969664 | bytes 7503872 | tf_op jit(solution)/shard_map/pallas_call | solution.py:91
  83.6 0.1 collective-permute-done.16.refs_0_
  83.7 0.4 collective-permute-done.18.refs_1_
  84.1 1.6 %shard_map.116 = (f32[256,768]{1,0:T(8,128)S(1)}, bf16[320,128]{1,0:T(8,128)(2,1)S(1)}) custom-call(bf16[64,2048]{1,0:T(8,128)(2,1)S(1)} %collective-permute-done.16.refs_0_, bf16[64,2048]{1,0:T(8,128)(2,1)S(1)} %collective-permute-done.18.refs_1_, bf16[128,2048]{1,0:T(8,128)(2,1)S(1)} %collective-permute-done.22.refs_2_, bf16[2048,768]{1,0:T(8,128)(2,1)S(1)} %copy-done.1, ...), custom_call_target="tpu_custom_call" | custom-call | flops 905969664 | bytes 7421952 | tf_op jit(solution)/shard_map/pallas_call | solution.py:91
  85.7 0.2 collective-permute-start.23
  85.9 1.2 %collective-permute-done.23.refs_0_ = bf16[320,128]{1,0:T(8,128)(2,1)S(1)} collective-permute-done((bf16[320,128]{1,0:T(8,128)(2,1)S(1)}, bf16[320,128]{1,0:T(8,128)(2,1)S(1)}, u32[]{:S(2)}, u32[]{:S(2)}) %collective-permute-start.23) | collective-permute-done | bytes 81952 | tf_op jit(solution)/shard_map/ppermute | solution.py:59
  87.0 2.1 %collective-permute-start.24 = (bf16[320,128]{1,0:T(8,128)(2,1)S(1)}, bf16[320,128]{1,0:T(8,128)(2,1)S(1)}, u32[]{:S(2)}, u32[]{:S(2)}) collective-permute-start(bf16[320,128]{1,0:T(8,128)(2,1)S(1)} %get-tuple-element.106), channel_id=1, source_target_pairs={{0,2},{1,3},{2,0},{3,1},{4,6},{5,7},{6,4},{7,5},{8,10},{9,11},{10,... | collective-permute-start | bytes 245768 | tf_op jit(solution)/shard_map/ppermute | solution.py:59
  89.1 2.8 %collective-permute-done.24.refs_0_ = bf16[320,128]{1,0:T(8,128)(2,1)S(1)} collective-permute-done((bf16[320,128]{1,0:T(8,128)(2,1)S(1)}, bf16[320,128]{1,0:T(8,128)(2,1)S(1)}, u32[]{:S(2)}, u32[]{:S(2)}) %collective-permute-start.24) | collective-permute-done | bytes 81952 | tf_op jit(solution)/shard_map/ppermute | solution.py:59
  92.0 2.4 %collective-permute-start.26 = (bf16[320,128]{1,0:T(8,128)(2,1)S(1)}, bf16[320,128]{1,0:T(8,128)(2,1)S(1)}, u32[]{:S(2)}, u32[]{:S(2)}) collective-permute-start(bf16[320,128]{1,0:T(8,128)(2,1)S(1)} %get-tuple-element.108), channel_id=1, source_target_pairs={{0,8},{1,9},{2,10},{3,11},{4,12},{5,13},{6,14},{7,15},{8,0},{9,1},... | collective-permute-start | bytes 245768 | tf_op jit(solution)/shard_map/ppermute | solution.py:59
  94.4 2.0 %collective-permute-start.27 = (bf16[320,128]{1,0:T(8,128)(2,1)S(1)}, bf16[320,128]{1,0:T(8,128)(2,1)S(1)}, u32[]{:S(2)}, u32[]{:S(2)}) collective-permute-start(bf16[320,128]{1,0:T(8,128)(2,1)S(1)} %get-tuple-element.108), channel_id=1, source_target_pairs={{0,12},{1,13},{2,14},{3,15},{4,8},{5,9},{6,10},{7,11},{8,4},{9,5},... | collective-permute-start | bytes 245768 | tf_op jit(solution)/shard_map/ppermute | solution.py:59
  96.4 0.6 collective-permute-done.25.refs_0_
  96.9 4.4 %collective-permute-done.26.refs_1_ = bf16[320,128]{1,0:T(8,128)(2,1)S(1)} collective-permute-done((bf16[320,128]{1,0:T(8,128)(2,1)S(1)}, bf16[320,128]{1,0:T(8,128)(2,1)S(1)}, u32[]{:S(2)}, u32[]{:S(2)}) %collective-permute-start.26) | collective-permute-done | bytes 81952 | tf_op jit(solution)/shard_map/ppermute | solution.py:59
  101.4 1.3 %collective-permute-done.28.refs_1_ = bf16[320,128]{1,0:T(8,128)(2,1)S(1)} collective-permute-done((bf16[320,128]{1,0:T(8,128)(2,1)S(1)}, bf16[320,128]{1,0:T(8,128)(2,1)S(1)}, u32[]{:S(2)}, u32[]{:S(2)}) %collective-permute-start.28) | collective-permute-done | bytes 81952 | tf_op jit(solution)/shard_map/ppermute | solution.py:59
  102.7 4.0 %shard_map.120 = (bf16[512,768]{1,0:T(8,128)(2,1)}, bf16[512,768]{1,0:T(8,128)(2,1)}) custom-call(bf16[320,128]{1,0:T(8,128)(2,1)S(1)} %shard_map.119.refs_0_, bf16[320,128]{1,0:T(8,128)(2,1)S(1)} %collective-permute-done.28.refs_1_, f32[256,768]{1,0:T(8,128)S(1)} %get-tuple-element.109.refs_2_, f32[256,768]{1,0:T(8,128)S(1)} %get-tuple-element.110.refs_3_, ...), custom_call_target="tpu_custom_call" | custom-call | flops 201326592 | bytes 4718592 | tf_op jit(solution)/shard_map/pallas_call | solution.py:436
  (62 shorter events, 0.9 us)
Async XLA Ops:
  0.6 1.9 %copy-start = (bf16[2048,768]{1,0:T(8,128)(2,1)S(1)}, bf16[2048,768]{1,0:T(8,128)(2,1)}, u32[]{:S(2)}) copy-start(bf16[2048,768]{1,0:T(8,128)(2,1)} %refs_3_.5) | copy-start | bytes 9437188
  5.4 6.1 %collective-permute-start = (bf16[128,2048]{1,0:T(8,128)(2,1)S(1)}, bf16[128,2048]{1,0:T(8,128)(2,1)S(1)}, u32[]{:S(2)}, u32[]{:S(2)}) collective-permute-start(bf16[128,2048]{1,0:T(8,128)(2,1)S(1)} %get-tuple-element.58), channel_id=1, source_target_pairs={{0,1},{1,0},{2,3},{3,2},{4,5},{5,4},{6,7},{7,6},{8,9},{9,8},{10,11... | collective-permute-start | bytes 1572872 | tf_op jit(solution)/shard_map/ppermute | solution.py:59
  5.9 21.9 %collective-permute-start.6 = (bf16[512,768]{1,0:T(8,128)(2,1)}, bf16[512,768]{1,0:T(8,128)(2,1)S(1)}, u32[]{:S(2)}, u32[]{:S(2)}) collective-permute-start(bf16[512,768]{1,0:T(8,128)(2,1)} %refs_5_.5), channel_id=1, source_target_pairs={{0,1},{1,2},{2,3},{3,4},{4,5},{5,6},{6,7},{7,8},{8,9},{9,10},{10,1... | collective-permute-start | bytes 2359304 | tf_op jit(solution)/shard_map/ppermute | solution.py:50
  5.9 7.3 %collective-permute-start.1 = (bf16[128,2048]{1,0:T(8,128)(2,1)S(1)}, bf16[128,2048]{1,0:T(8,128)(2,1)S(1)}, u32[]{:S(2)}, u32[]{:S(2)}) collective-permute-start(bf16[128,2048]{1,0:T(8,128)(2,1)S(1)} %get-tuple-element.61), channel_id=1, source_target_pairs={{0,1},{1,0},{2,3},{3,2},{4,5},{5,4},{6,7},{7,6},{8,9},{9,8},{10,11... | collective-permute-start | bytes 1572872 | tf_op jit(solution)/shard_map/ppermute | solution.py:59
  11.4 52.9 %copy-start.21 = (f32[512]{0:T(512)S(1)}, f32[512]{0:T(512)}, u32[]{:S(2)}) copy-start(f32[512]{0:T(512)} %param.14) | copy-start | bytes 6148
  11.4 53.0 %copy-start.22 = (s32[512]{0:T(512)S(1)}, s32[512]{0:T(512)}, u32[]{:S(2)}) copy-start(s32[512]{0:T(512)} %param.15) | copy-start | bytes 6148
  11.4 55.4 %copy-start.19 = (f32[768]{0:T(1024)S(1)}, f32[768]{0:T(1024)}, u32[]{:S(2)}) copy-start(f32[768]{0:T(1024)} %param.12) | copy-start | bytes 9220
  11.5 55.4 %copy-start.20 = (f32[768]{0:T(1024)S(1)}, f32[768]{0:T(1024)}, u32[]{:S(2)}) copy-start(f32[768]{0:T(1024)} %param.13) | copy-start | bytes 9220
  11.6 16.2 %collective-permute-start.5 = (bf16[64,2048]{1,0:T(8,128)(2,1)S(1)}, bf16[64,2048]{1,0:T(8,128)(2,1)S(1)}, u32[]{:S(2)}, u32[]{:S(2)}) collective-permute-start(bf16[64,2048]{1,0:T(8,128)(2,1)S(1)} %get-tuple-element.65), channel_id=1, source_target_pairs={{0,2},{1,3},{2,0},{3,1},{4,6},{5,7},{6,4},{7,5},{8,10},{9,11},{10,... | collective-permute-start | bytes 786440 | tf_op jit(solution)/shard_map/ppermute | solution.py:59
  13.3 6.7 %collective-permute-start.2 = (bf16[128,512]{1,0:T(8,128)(2,1)S(1)}, bf16[128,512]{1,0:T(8,128)(2,1)S(1)}, u32[]{:S(2)}, u32[]{:S(2)}) collective-permute-start(bf16[128,512]{1,0:T(8,128)(2,1)S(1)} %get-tuple-element.62), channel_id=1, source_target_pairs={{0,4},{1,5},{2,6},{3,7},{4,0},{5,1},{6,2},{7,3},{8,12},{9,13},{10,... | collective-permute-start | bytes 393224 | tf_op jit(solution)/shard_map/ppermute | solution.py:59
  15.0 12.8 %collective-permute-start.3 = (bf16[128,512]{1,0:T(8,128)(2,1)S(1)}, bf16[128,512]{1,0:T(8,128)(2,1)S(1)}, u32[]{:S(2)}, u32[]{:S(2)}) collective-permute-start(bf16[128,512]{1,0:T(8,128)(2,1)S(1)} %get-tuple-element.63), channel_id=1, source_target_pairs={{0,8},{1,9},{2,10},{3,11},{4,12},{5,13},{6,14},{7,15},{8,0},{9,1},... | collective-permute-start | bytes 393224 | tf_op jit(solution)/shard_map/ppermute | solution.py:59
  16.3 11.5 %collective-permute-start.4 = (bf16[128,512]{1,0:T(8,128)(2,1)S(1)}, bf16[128,512]{1,0:T(8,128)(2,1)S(1)}, u32[]{:S(2)}, u32[]{:S(2)}) collective-permute-start(bf16[128,512]{1,0:T(8,128)(2,1)S(1)} %get-tuple-element.64), channel_id=1, source_target_pairs={{0,12},{1,13},{2,14},{3,15},{4,8},{5,9},{6,10},{7,11},{8,4},{9,5},... | collective-permute-start | bytes 393224 | tf_op jit(solution)/shard_map/ppermute | solution.py:59
  27.8 36.5 %copy-start.6 = (bf16[512,768]{1,0:T(8,128)(2,1)}, bf16[512,768]{1,0:T(8,128)(2,1)S(1)}, u32[]{:S(2)}) copy-start(bf16[512,768]{1,0:T(8,128)(2,1)S(1)} %collective-permute-done.6.refs_1_) | copy-start | bytes 2359300
  27.8 31.1 %collective-permute-start.15 = (bf16[512,768]{1,0:T(8,128)(2,1)}, bf16[512,768]{1,0:T(8,128)(2,1)S(1)}, u32[]{:S(2)}, u32[]{:S(2)}) collective-permute-start(bf16[512,768]{1,0:T(8,128)(2,1)} %refs_5_.5), channel_id=1, source_target_pairs={{0,15},{1,0},{2,1},{3,2},{4,3},{5,4},{6,5},{7,6},{8,7},{9,8},{10,9... | collective-permute-start | bytes 2359304 | tf_op jit(solution)/shard_map/ppermute | solution.py:50
  32.1 9.9 %collective-permute-start.10 = (bf16[64,512]{1,0:T(8,128)(2,1)S(1)}, bf16[64,512]{1,0:T(8,128)(2,1)S(1)}, u32[]{:S(2)}, u32[]{:S(2)}) collective-permute-start(bf16[64,512]{1,0:T(8,128)(2,1)S(1)} %get-tuple-element.75), channel_id=1, source_target_pairs={{0,2},{1,3},{2,0},{3,1},{4,6},{5,7},{6,4},{7,5},{8,10},{9,11},{10,... | collective-permute-start | bytes 196616 | tf_op jit(solution)/shard_map/ppermute | solution.py:59
  32.3 12.3 %collective-permute-start.7 = (bf16[64,512]{1,0:T(8,128)(2,1)S(1)}, bf16[64,512]{1,0:T(8,128)(2,1)S(1)}, u32[]{:S(2)}, u32[]{:S(2)}) collective-permute-start(bf16[64,512]{1,0:T(8,128)(2,1)S(1)} %get-tuple-element.68), channel_id=1, source_target_pairs={{0,4},{1,5},{2,6},{3,7},{4,0},{5,1},{6,2},{7,3},{8,12},{9,13},{10,... | collective-permute-start | bytes 196616 | tf_op jit(solution)/shard_map/ppermute | solution.py:59
  34.2 15.4 %collective-permute-start.8 = (bf16[64,512]{1,0:T(8,128)(2,1)S(1)}, bf16[64,512]{1,0:T(8,128)(2,1)S(1)}, u32[]{:S(2)}, u32[]{:S(2)}) collective-permute-start(bf16[64,512]{1,0:T(8,128)(2,1)S(1)} %get-tuple-element.69), channel_id=1, source_target_pairs={{0,8},{1,9},{2,10},{3,11},{4,12},{5,13},{6,14},{7,15},{8,0},{9,1},... | collective-permute-start | bytes 196616 | tf_op jit(solution)/shard_map/ppermute | solution.py:59
  35.1 14.4 %collective-permute-start.9 = (bf16[64,512]{1,0:T(8,128)(2,1)S(1)}, bf16[64,512]{1,0:T(8,128)(2,1)S(1)}, u32[]{:S(2)}, u32[]{:S(2)}) collective-permute-start(bf16[64,512]{1,0:T(8,128)(2,1)S(1)} %get-tuple-element.70), channel_id=1, source_target_pairs={{0,12},{1,13},{2,14},{3,15},{4,8},{5,9},{6,10},{7,11},{8,4},{9,5},... | collective-permute-start | bytes 196616 | tf_op jit(solution)/shard_map/ppermute | solution.py:59
  49.6 5.1 %collective-permute-start.11 = (bf16[64,512]{1,0:T(8,128)(2,1)S(1)}, bf16[64,512]{1,0:T(8,128)(2,1)S(1)}, u32[]{:S(2)}, u32[]{:S(2)}) collective-permute-start(bf16[64,512]{1,0:T(8,128)(2,1)S(1)} %get-tuple-element.85.refs_0_), channel_id=1, source_target_pairs={{0,4},{1,5},{2,6},{3,7},{4,0},{5,1},{6,2},{7,3},{8,12},{9,13},{10,... | collective-permute-start | bytes 196616 | tf_op jit(solution)/shard_map/ppermute | solution.py:59
  50.9 5.9 %collective-permute-start.12 = (bf16[64,512]{1,0:T(8,128)(2,1)S(1)}, bf16[64,512]{1,0:T(8,128)(2,1)S(1)}, u32[]{:S(2)}, u32[]{:S(2)}) collective-permute-start(bf16[64,512]{1,0:T(8,128)(2,1)S(1)} %get-tuple-element.85.refs_0_), channel_id=1, source_target_pairs={{0,8},{1,9},{2,10},{3,11},{4,12},{5,13},{6,14},{7,15},{8,0},{9,1},... | collective-permute-start | bytes 196616 | tf_op jit(solution)/shard_map/ppermute | solution.py:59
  51.7 6.2 %collective-permute-start.13 = (bf16[64,512]{1,0:T(8,128)(2,1)S(1)}, bf16[64,512]{1,0:T(8,128)(2,1)S(1)}, u32[]{:S(2)}, u32[]{:S(2)}) collective-permute-start(bf16[64,512]{1,0:T(8,128)(2,1)S(1)} %get-tuple-element.85.refs_0_), channel_id=1, source_target_pairs={{0,12},{1,13},{2,14},{3,15},{4,8},{5,9},{6,10},{7,11},{8,4},{9,5},... | collective-permute-start | bytes 196616 | tf_op jit(solution)/shard_map/ppermute | solution.py:59
  54.0 0.6 copy-start.11
  54.6 4.3 %collective-permute-start.14 = (bf16[64,512]{1,0:T(8,128)(2,1)S(1)}, bf16[64,512]{1,0:T(8,128)(2,1)S(1)}, u32[]{:S(2)}, u32[]{:S(2)}) collective-permute-start(bf16[64,512]{1,0:T(8,128)(2,1)S(1)} %get-tuple-element.89.refs_0_), channel_id=1, source_target_pairs={{0,2},{1,3},{2,0},{3,1},{4,6},{5,7},{6,4},{7,5},{8,10},{9,11},{10,... | collective-permute-start | bytes 196616 | tf_op jit(solution)/shard_map/ppermute | solution.py:59
  54.7 0.6 copy-start.13
  56.7 0.6 copy-start.15
  57.9 0.6 copy-start.17
  58.9 0.9 copy-start.8
  59.8 20.4 %collective-permute-start.19 = (bf16[128,512]{1,0:T(8,128)(2,1)S(1)}, bf16[128,512]{1,0:T(8,128)(2,1)}, u32[]{:S(2)}, u32[]{:S(2)}) collective-permute-start(bf16[128,512]{1,0:T(8,128)(2,1)S(1)} %shard_map.112.refs_0_), channel_id=1, source_target_pairs={{0,4},{1,5},{2,6},{3,7},{4,0},{5,1},{6,2},{7,3},{8,12},{9,13},{10,... | collective-permute-start | bytes 393224 | tf_op jit(solution)/shard_map/ppermute | solution.py:59
  60.3 19.9 %collective-permute-start.20 = (bf16[128,512]{1,0:T(8,128)(2,1)S(1)}, bf16[128,512]{1,0:T(8,128)(2,1)}, u32[]{:S(2)}, u32[]{:S(2)}) collective-permute-start(bf16[128,512]{1,0:T(8,128)(2,1)S(1)} %shard_map.112.refs_0_), channel_id=1, source_target_pairs={{0,8},{1,9},{2,10},{3,11},{4,12},{5,13},{6,14},{7,15},{8,0},{9,1},... | collective-permute-start | bytes 393224 | tf_op jit(solution)/shard_map/ppermute | solution.py:59
  62.3 17.9 %collective-permute-start.21 = (bf16[128,512]{1,0:T(8,128)(2,1)S(1)}, bf16[128,512]{1,0:T(8,128)(2,1)}, u32[]{:S(2)}, u32[]{:S(2)}) collective-permute-start(bf16[128,512]{1,0:T(8,128)(2,1)S(1)} %shard_map.112.refs_0_), channel_id=1, source_target_pairs={{0,12},{1,13},{2,14},{3,15},{4,8},{5,9},{6,10},{7,11},{8,4},{9,5},... | collective-permute-start | bytes 393224 | tf_op jit(solution)/shard_map/ppermute | solution.py:59
  64.3 17.7 %copy-start.1 = (bf16[2048,768]{1,0:T(8,128)(2,1)S(1)}, bf16[2048,768]{1,0:T(8,128)(2,1)}, u32[]{:S(2)}) copy-start(bf16[2048,768]{1,0:T(8,128)(2,1)} %refs_3_.5) | copy-start | bytes 9437188
  66.9 0.8 copy-start.12
  67.7 0.8 copy-start.14
  68.6 0.8 copy-start.16
  69.4 0.8 copy-start.18
  70.3 11.6 %collective-permute-start.17 = (bf16[64,2048]{1,0:T(8,128)(2,1)S(1)}, bf16[64,2048]{1,0:T(8,128)(2,1)S(1)}, u32[]{:S(2)}, u32[]{:S(2)}) collective-permute-start(bf16[64,2048]{1,0:T(8,128)(2,1)S(1)} %shard_map.111.refs_0_), channel_id=1, source_target_pairs={{0,2},{1,3},{2,0},{3,1},{4,6},{5,7},{6,4},{7,5},{8,10},{9,11},{10,... | collective-permute-start | bytes 786440 | tf_op jit(solution)/shard_map/ppermute | solution.py:59
  70.4 1.1 %copy-start.2 = (bf16[512,768]{1,0:T(8,128)(2,1)S(1)}, bf16[512,768]{1,0:T(8,128)(2,1)}, u32[]{:S(2)}) copy-start(bf16[512,768]{1,0:T(8,128)(2,1)} %refs_4_.2) | copy-start | bytes 2359300
  71.5 0.9 copy-start.4
  72.4 0.9 copy-start.5
  73.4 1.1 %copy-start.7 = (bf16[512,768]{1,0:T(8,128)(2,1)S(1)}, bf16[512,768]{1,0:T(8,128)(2,1)}, u32[]{:S(2)}) copy-start(bf16[512,768]{1,0:T(8,128)(2,1)} %copy-done.6) | copy-start | bytes 2359300
  74.5 1.1 %copy-start.9 = (bf16[512,768]{1,0:T(8,128)(2,1)S(1)}, bf16[512,768]{1,0:T(8,128)(2,1)}, u32[]{:S(2)}) copy-start(bf16[512,768]{1,0:T(8,128)(2,1)} %copy-done.8) | copy-start | bytes 2359300
  75.7 0.8 copy-start.10
  81.3 2.7 %collective-permute-start.22 = (bf16[128,2048]{1,0:T(8,128)(2,1)S(1)}, bf16[128,2048]{1,0:T(8,128)(2,1)S(1)}, u32[]{:S(2)}, u32[]{:S(2)}) collective-permute-start(bf16[128,2048]{1,0:T(8,128)(2,1)S(1)} %shard_map.114.refs_2_), channel_id=1, source_target_pairs={{0,1},{1,0},{2,3},{3,2},{4,5},{5,4},{6,7},{7,6},{8,9},{9,8},{10,11... | collective-permute-start | bytes 1572872 | tf_op jit(solution)/shard_map/ppermute | solution.py:59
  81.4 2.3 %collective-permute-start.16 = (bf16[64,2048]{1,0:T(8,128)(2,1)S(1)}, bf16[64,2048]{1,0:T(8,128)(2,1)S(1)}, u32[]{:S(2)}, u32[]{:S(2)}) collective-permute-start(bf16[64,2048]{1,0:T(8,128)(2,1)S(1)} %shard_map.111.refs_0_), channel_id=1, source_target_pairs={{0,1},{1,0},{2,3},{3,2},{4,5},{5,4},{6,7},{7,6},{8,9},{9,8},{10,11... | collective-permute-start | bytes 786440 | tf_op jit(solution)/shard_map/ppermute | solution.py:59
  81.9 2.1 %collective-permute-start.18 = (bf16[64,2048]{1,0:T(8,128)(2,1)S(1)}, bf16[64,2048]{1,0:T(8,128)(2,1)S(1)}, u32[]{:S(2)}, u32[]{:S(2)}) collective-permute-start(bf16[64,2048]{1,0:T(8,128)(2,1)S(1)} %collective-permute-done.17.refs_1_), channel_id=1, source_target_pairs={{0,1},{1,0},{2,3},{3,2},{4,5},{5,4},{6,7},{7,6},{8,9},{9,8},{10,11... | collective-permute-start | bytes 786440 | tf_op jit(solution)/shard_map/ppermute | solution.py:59
  84.1 18.6 %copy-start.3 = (bf16[512,768]{1,0:T(8,128)(2,1)S(1)}, bf16[512,768]{1,0:T(8,128)(2,1)}, u32[]{:S(2)}) copy-start(bf16[512,768]{1,0:T(8,128)(2,1)} %refs_4_.2) | copy-start | bytes 2359300
  85.7 1.3 %collective-permute-start.23 = (bf16[320,128]{1,0:T(8,128)(2,1)S(1)}, bf16[320,128]{1,0:T(8,128)(2,1)S(1)}, u32[]{:S(2)}, u32[]{:S(2)}) collective-permute-start(bf16[320,128]{1,0:T(8,128)(2,1)S(1)} %get-tuple-element.104), channel_id=1, source_target_pairs={{0,1},{1,0},{2,3},{3,2},{4,5},{5,4},{6,7},{7,6},{8,9},{9,8},{10,11... | collective-permute-start | bytes 245768 | tf_op jit(solution)/shard_map/ppermute | solution.py:59
  87.0 4.8 %collective-permute-start.24 = (bf16[320,128]{1,0:T(8,128)(2,1)S(1)}, bf16[320,128]{1,0:T(8,128)(2,1)S(1)}, u32[]{:S(2)}, u32[]{:S(2)}) collective-permute-start(bf16[320,128]{1,0:T(8,128)(2,1)S(1)} %get-tuple-element.106), channel_id=1, source_target_pairs={{0,2},{1,3},{2,0},{3,1},{4,6},{5,7},{6,4},{7,5},{8,10},{9,11},{10,... | collective-permute-start | bytes 245768 | tf_op jit(solution)/shard_map/ppermute | solution.py:59
  91.9 5.0 %collective-permute-start.25 = (bf16[320,128]{1,0:T(8,128)(2,1)S(1)}, bf16[320,128]{1,0:T(8,128)(2,1)S(1)}, u32[]{:S(2)}, u32[]{:S(2)}) collective-permute-start(bf16[320,128]{1,0:T(8,128)(2,1)S(1)} %get-tuple-element.108), channel_id=1, source_target_pairs={{0,4},{1,5},{2,6},{3,7},{4,0},{5,1},{6,2},{7,3},{8,12},{9,13},{10,... | collective-permute-start | bytes 245768 | tf_op jit(solution)/shard_map/ppermute | solution.py:59
  92.0 9.3 %collective-permute-start.26 = (bf16[320,128]{1,0:T(8,128)(2,1)S(1)}, bf16[320,128]{1,0:T(8,128)(2,1)S(1)}, u32[]{:S(2)}, u32[]{:S(2)}) collective-permute-start(bf16[320,128]{1,0:T(8,128)(2,1)S(1)} %get-tuple-element.108), channel_id=1, source_target_pairs={{0,8},{1,9},{2,10},{3,11},{4,12},{5,13},{6,14},{7,15},{8,0},{9,1},... | collective-permute-start | bytes 245768 | tf_op jit(solution)/shard_map/ppermute | solution.py:59
  94.4 6.9 %collective-permute-start.27 = (bf16[320,128]{1,0:T(8,128)(2,1)S(1)}, bf16[320,128]{1,0:T(8,128)(2,1)S(1)}, u32[]{:S(2)}, u32[]{:S(2)}) collective-permute-start(bf16[320,128]{1,0:T(8,128)(2,1)S(1)} %get-tuple-element.108), channel_id=1, source_target_pairs={{0,12},{1,13},{2,14},{3,15},{4,8},{5,9},{6,10},{7,11},{8,4},{9,5},... | collective-permute-start | bytes 245768 | tf_op jit(solution)/shard_map/ppermute | solution.py:59
  101.4 1.3 %collective-permute-start.28 = (bf16[320,128]{1,0:T(8,128)(2,1)S(1)}, bf16[320,128]{1,0:T(8,128)(2,1)S(1)}, u32[]{:S(2)}, u32[]{:S(2)}) collective-permute-start(bf16[320,128]{1,0:T(8,128)(2,1)S(1)} %shard_map.119.refs_0_), channel_id=1, source_target_pairs={{0,1},{1,0},{2,3},{3,2},{4,5},{5,4},{6,7},{7,6},{8,9},{9,8},{10,11... | collective-permute-start | bytes 245768 | tf_op jit(solution)/shard_map/ppermute | solution.py:59

commit v9 on v8

--- a/solution.py
+++ b/solution.py
@@ -27,7 +27,7 @@
 KINETIC = 0.125
 STEP_SIZE = 0.3
 MIB = 1024 * 1024
-VMEM_BYTES = 40 * MIB
+VMEM_BYTES = 24 * MIB
 REDUCE_SHARE = 0.5
 GATHER_SHARE = 0.5
 BF16 = jnp.bfloat16
@@ -103,39 +103,64 @@
     return jax.ShapeDtypeStruct(shape, dtype)
 
 
-def partial_body(core, other, block, r_ref, p_ref, x_ref, z_ref):
-    rows = x_ref.shape[0] + z_ref.shape[0]
-    size = rows // block
+def cut(part, block, x_ref, z_ref, cols):
+    size = part.shape[0] // block
     first, rest = x_ref.shape[0] // size, z_ref.shape[0] // size
+    part = part.astype(x_ref.dtype)
+    for i in range(size):
+        x_ref[i * first : (i + 1) * first, cols] = part[i * block : i * block + first, :]
+        z_ref[i * rest : (i + 1) * rest, cols] = part[i * block + first : (i + 1) * block, :]
+
+
+def first_body(core, block, tile, r_ref, p_ref, *refs):
+    sent_x, sent_z, keep_x, keep_z, r_held, p_held, r_sem, p_sem = refs
+    rows = r_held.shape[0] // 2
+    r_copy = pltpu.make_async_copy(r_ref, r_held, r_sem)
+    r_copy.start()
+    copies = []
+    for t in range(p_held.shape[0] // tile):
+        part = pl.ds(t * tile, tile)
+        copies.append(pltpu.make_async_copy(p_ref.at[part, :], p_held.at[part, :], p_sem.at[t]))
+        copies[-1].start()
     c = position(core)
-    row = pl.multiple_of((1 - c if other else c) * rows, rows)
-    part = lax.dot_general(
-        r_ref[pl.ds(row, rows), :], p_ref[...], NT, preferred_element_type=F32
-    ).astype(x_ref.dtype)
-    for i in range(size):
-        x_ref[i * first : (i + 1) * first, :] = part[i * block : i * block + first, :]
-        z_ref[i * rest : (i + 1) * rest, :] = part[i * block + first : (i + 1) * block, :]
-
-
-def partial_intersections(response, projectors, core, other, block, first):
+    r_copy.wait()
+    for t, copy in enumerate(copies):
+        copy.wait()
+        cols = slice(t * tile, (t + 1) * tile)
+        for side, x_ref, z_ref in ((1 - c, sent_x, sent_z), (c, keep_x, keep_z)):
+            part = lax.dot_general(
+                r_held[pl.ds(pl.multiple_of(side * rows, rows), rows), :],
+                p_held[cols, :],
+                NT,
+                preferred_element_type=F32,
+            )
+            cut(part, block, x_ref, z_ref, cols)
+
+
+def first_sums(response, projectors, core, block, first):
     bands, cells = response.shape
     count = projectors.shape[0]
     rows = bands // 2
     tile = min(512, count)
     rows_x = rows // block * first
-    outs = [struct((n, count), BF16 if other else F32) for n in (rows_x, rows - rows_x)]
+    outs = [struct((n, count), t) for t in (BF16, F32) for n in (rows_x, rows - rows_x)]
     return pl.pallas_call(
-        functools.partial(partial_body, core, other, block),
-        grid=(count // tile,),
+        functools.partial(first_body, core, block, tile),
         out_shape=outs,
-        in_specs=[
-            pl.BlockSpec((bands, cells), lambda i: (0, 0)),
-            pl.BlockSpec((tile, cells), lambda i: (i, 0)),
+        in_specs=[pl.BlockSpec(memory_space=pltpu.HBM)] * 2,
+        out_specs=[whole() for _ in outs],
+        scratch_shapes=[
+            pltpu.VMEM((bands, cells), response.dtype),
+            pltpu.VMEM((count, cells), projectors.dtype),
+            pltpu.SemaphoreType.DMA,
+            pltpu.SemaphoreType.DMA((count // tile,)),
         ],
-        out_specs=[pl.BlockSpec((out.shape[0], tile), lambda i: (0, i)) for out in outs],
         compiler_params=params(),
-        cost_estimate=cost(2 * rows * cells * count, projectors, *outs),
-    )(response, projectors)
+        cost_estimate=cost(2 * bands * cells * count, projectors, *outs),
+    )(
+        pltpu.with_memory_space_constraint(response, pltpu.HBM),
+        pltpu.with_memory_space_constraint(projectors, pltpu.HBM),
+    )
 
 
 def rows_at(place, size):
@@ -223,6 +248,10 @@
     return local_call(functools.partial(place_body, level, along), struct(shape, BF16), parts)
 
 
+def turned(row, width):
+    return jnp.transpose(jnp.broadcast_to(row, (width, row.shape[1])))
+
+
 def local_body(depth, sizes, *refs):
     r_ref, l_ref, h_ref, o_ref, m_ref, pot_ref, v_ref, e_ref = refs[:8]
     first_ref, many_ref, out_ref, mask_ref = refs[8:]
@@ -238,6 +267,8 @@
             ref, k = h_ref, j - depth
         return ref[:, k * plane : (k + 1) * plane]
 
+    group_rows, blk = sizes
+    energy = turned(e_ref[...], plane)
     for j in range(depth):
         cols = slice(j * plane, (j + 1) * plane)
         low = plane_at(j)
@@ -246,24 +277,24 @@
         for offset in range(1, 7):
             pair = plane_at(j + offset).astype(F32) + plane_at(j - offset).astype(F32)
             total = total + (KINETIC * COEFFS[offset]) * pair
-        total = total + (e_ref[...] - pot_ref[:, cols]) * low.astype(F32)
+        total = total + (energy - pot_ref[:, cols]) * low.astype(F32)
         out_ref[:, cols] = total - v_ref[:, cols] * o_ref[:, cols].astype(F32)
-    group_rows, blk = sizes
+    width = mask_ref.shape[1]
     block = lax.broadcasted_iota(jnp.int32, mask_ref.shape, 1) // blk
-    block = block + (pl.program_id(0) * (group_rows // blk) - REACH)
-    lowest = first_ref[...]
-    inside = (block >= lowest) & (block < lowest + many_ref[...])
+    block = (block + (pl.program_id(0) * (group_rows // blk) - REACH)).astype(F32)
+    lowest = turned(first_ref[...].astype(F32), width)
+    inside = (block >= lowest) & (block < lowest + turned(many_ref[...].astype(F32), width))
     mask_ref[...] = jnp.where(inside, 1.0, 0.0).astype(BF16)
 
 
-def local_part(response, low, high, orbitals, matrix, lines, columns, group_rows, width, blk):
+def local_part(response, low, high, orbitals, matrix, lines, bounds, group_rows, width, blk):
     bands, cells = response.shape
     depth = cells // (GY * GZ)
     outs = [struct((bands, cells), F32), struct((bands, width), BF16)]
     here = pl.BlockSpec((group_rows, cells), lambda i: (i, 0))
     side = pl.BlockSpec((group_rows, low.shape[1]), lambda i: (i, 0))
     line = pl.BlockSpec((1, cells), lambda i: (0, 0))
-    column = pl.BlockSpec((group_rows, 1), lambda i: (i, 0))
+    band = pl.BlockSpec((1, group_rows), lambda i: (0, i))
     return pl.pallas_call(
         functools.partial(local_body, depth, (group_rows, blk)),
         grid=(bands // group_rows,),
@@ -276,14 +307,14 @@
             pl.BlockSpec(matrix.shape, lambda i: (0, 0, 0)),
             line,
             line,
-            column,
-            column,
-            column,
+            band,
+            band,
+            band,
         ],
         out_specs=[here, pl.BlockSpec((group_rows, width), lambda i: (i, 0))],
         compiler_params=params(),
         cost_estimate=cost(2 * bands * cells * 300, low, high, low, low, *outs),
-    )(response, low, high, orbitals, matrix, *lines, *columns)
+    )(response, low, high, orbitals, matrix, *lines, *bounds)
 
 
 def pad_orbitals(o_ref, pad_ref, blk):
@@ -474,7 +505,7 @@
     gather_first = max(16, round(GATHER_SHARE * block / 16) * 16)
     matrix = jnp.asarray(plane_matrix())
     lines = (potential[None, :], perturbing[None, :])
-    columns = tuple(a[:, None] for a in (energies, window_start, block_count))
+    bounds = tuple(a[None, :] for a in (energies, window_start, block_count))
 
     def to(array, level):
         return [swapped(array, count, level, k) for k in range(1, level[0])]
@@ -484,17 +515,20 @@
 
     low = neighbour(response[:, local_cells - halo :], count, 1)
 
-    sent_x, sent_z = partial_intersections(response, projectors, core, True, block, first)
+    sent_x, sent_z, keep_x, keep_z = first_sums(response, projectors, core, block, first)
     sent_z = swapped(sent_z, count, core, 1)
     sent_x = swapped(sent_x, count, core, 1)
-    keep_x, keep_z = partial_intersections(response, projectors, core, False, block, first)
+    low, head = lax.optimization_barrier((low, response[:, :halo]))
+    high = neighbour(head, count, -1)
     keep_z, *parts_z = split(keep_z, [sent_z], along, 1)
     keep_x, *parts_x = split(keep_x, [sent_x], across, 0)
-    taken_z, taken_x, low, head = lax.optimization_barrier(
-        (parts_to(parts_z, along), parts_to(parts_x, across), low, response[:, :halo])
-    )
+    parts_x, low = lax.optimization_barrier((parts_x, low))
+    taken_z, taken_x, low, high = lax.optimization_barrier(
+        (parts_to(parts_z, along), parts_to(parts_x, across), low, high)
+    )
+    keep_x, *parts_x = split(keep_x, taken_x, along, 1)
+    low, head, _ = lax.optimization_barrier((low, response[:, :halo], keep_x))
     high = neighbour(head, count, -1)
-    keep_x, *parts_x = split(keep_x, taken_x, along, 1)
     keep_z, *parts_z = split(keep_z, taken_z, across, 0)
     taken_x, taken_z = lax.optimization_barrier(
         (parts_to(parts_x, along), parts_to(parts_z, across))
@@ -508,11 +542,11 @@
         [keep_x, *taken_x, keep_z, *taken_z],
     )
 
-    pieces_x, pieces_z, low, high = lax.optimization_barrier(
-        ([share_x, *to(share_x, along)], [share_z, *to(share_z, across)], low, high)
+    pieces_x, pieces_z, bounds = lax.optimization_barrier(
+        ([share_x, *to(share_x, along)], [share_z, *to(share_z, across)], bounds)
     )
     base, mask = local_part(
-        response, low, high, orbitals, matrix, lines, columns, group_rows, width, blk
+        response, low, high, orbitals, matrix, lines, bounds, group_rows, width, blk
     )
     block_x = place(pieces_x, along, 1)
     block_z = place(pieces_z, across, 0)

time: 108 us -> 94.1 us (0.87)
  local copies, waits for them, and re-layouts: 17.3 us -> 0.06 us
  waiting for transfers between devices: 35.9 us -> 52.8 us
  starting transfers between devices: 34.4 us -> 27.5 us
  Pallas kernels: 18.2 us -> 12.6 us
    unnamed x46 -> x18, local copies, waits for them, and re-layouts: 14.8 us -> 0.06 us
    ppermute x27, waiting for transfers between devices: 35.9 us -> 46.6 us  [swapped(): return lax.ppermute(array, 'band', pairs)]
    ppermute x2, waiting for transfers between devices: 0.01 us -> 6.18 us  [neighbour(): lax.ppermute(array, 'band', [(i, (i + step) % count) for i in range(count)])]
    ppermute x2, starting transfers between devices: 4.29 us -> 0.56 us  [neighbour(): lax.ppermute(array, 'band', [(i, (i + step) % count) for i in range(count)])]
    ppermute x27, starting transfers between devices: 30.1 us -> 27 us  [swapped(): return lax.ppermute(array, 'band', pairs)]
    broadcast_in_dim x3 -> x0, local copies, waits for them, and re-layouts: 2.57 us -> none  [shards(): columns = tuple((a[:, None] for a in (energies, window_start, block_count)))]
    pallas_call x1, Pallas kernels: 4.03 us -> 2.49 us  [project(): pl.pallas_call(functools.partial(project_body, core, blk), grid=(bands //...]
    pallas_call x1, Pallas kernels: 3.71 us -> 2.23 us  [local_part(): pl.pallas_call(functools.partial(local_body, depth, (group_rows, blk)), g...]
  transfers between devices with their start and end apart: 29 -> 29, of which waited for: 15 -> 17; matrix products, arithmetic and copies ran while one was open for 2% -> 0% of each run, Pallas kernels for 9% -> 9%
where the time goes in v9:
time: 94.1 us; the launch traced here: 93.9 us
  waiting for transfers between devices  52.8 us (56%)
  starting transfers between devices  27.5 us (29%)
  Pallas kernels  12.6 us (13%)
    ppermute x27, waiting for transfers between devices, swapped(): return lax.ppermute(array, 'band', pairs)  46.6 us
    ppermute x27, starting transfers between devices, swapped(): return lax.ppermute(array, 'band', pairs)  27 us
    ppermute x2, waiting for transfers between devices, neighbour(): lax.ppermute(array, 'band', [(i, (i + step) % count) for i in range(count)])  6.18 us
    pallas_call x1, Pallas kernels, first_sums(): pl.pallas_call(functools.partial(first_body, core, block, tile), out_shap...  4.31 us
    pallas_call x13, Pallas kernels, local_call(): pl.pallas_call(body, out_shape=outs, in_specs=[whole() for _ in args], ou...  3.59 us
    pallas_call x1, Pallas kernels, project(): pl.pallas_call(functools.partial(project_body, core, blk), grid=(bands //...  2.49 us
    pallas_call x1, Pallas kernels, local_part(): pl.pallas_call(functools.partial(local_body, depth, (group_rows, blk)), g...  2.23 us
  transfers between devices with their start and end apart: 29, of which 17 were waited for; matrix products, arithmetic and copies ran while one was open for 0% of the time, Pallas kernels for 9%

profile of v9, /device:TPU:0, one launch (start us, length us, event | category | flops | bytes accessed | tf_op | source)
XLA Modules:
  0.0 93.9 jit_solution(13300281150982658350)
XLA Ops:
  0.6 0.5 collective-permute-start.5
  1.1 4.3 %shard_map.104 = (bf16[128,2048]{1,0:T(8,128)(2,1)S(1)}, bf16[128,2048]{1,0:T(8,128)(2,1)S(1)}, f32[128,2048]{1,0:T(8,128)S(1)}, f32[128,2048]{1,0:T(8,128)S(1)}) custom-call(bf16[512,768]{1,0:T(8,128)(2,1)} %refs_5_.5, bf16[2048,768]{1,0:T(8,128)(2,1)} %refs_3_.5), custom_call_target="tpu_custom_call" | custom-call | flops 1610612736 | bytes 6291456 | tf_op jit(solution)/shard_map/pallas_call | solution.py:147
  5.4 0.0 copy-start.2
  5.5 0.0 copy-start.7
  5.5 0.0 copy-start.8
  5.5 0.0 copy-start
  5.5 0.0 copy-start.3
  5.5 0.0 copy-start.4
  5.5 0.0 copy-start.5
  5.5 0.0 copy-start.6
  5.5 2.7 %collective-permute-start = (bf16[128,2048]{1,0:T(8,128)(2,1)S(1)}, bf16[128,2048]{1,0:T(8,128)(2,1)S(1)}, u32[]{:S(2)}, u32[]{:S(2)}) collective-permute-start(bf16[128,2048]{1,0:T(8,128)(2,1)S(1)} %get-tuple-element.63), channel_id=1, source_target_pairs={{0,1},{1,0},{2,3},{3,2},{4,5},{5,4},{6,7},{7,6},{8,9},{9,8},{10,11... | collective-permute-start | bytes 1572872 | tf_op jit(solution)/shard_map/ppermute | solution.py:59
  8.2 0.1 collective-permute-start.1
  8.3 1.5 %collective-permute-done.refs_1_ = bf16[128,2048]{1,0:T(8,128)(2,1)S(1)} collective-permute-done((bf16[128,2048]{1,0:T(8,128)(2,1)S(1)}, bf16[128,2048]{1,0:T(8,128)(2,1)S(1)}, u32[]{:S(2)}, u32[]{:S(2)}) %collective-permute-start) | collective-permute-done | bytes 524320 | tf_op jit(solution)/shard_map/ppermute | solution.py:59
  9.8 0.1 shard_map.105
  9.8 6.2 %collective-permute-done.5.refs_1_ = bf16[512,768]{1,0:T(8,128)(2,1)S(1)} collective-permute-done((bf16[512,768]{1,0:T(8,128)(2,1)}, bf16[512,768]{1,0:T(8,128)(2,1)S(1)}, u32[]{:S(2)}, u32[]{:S(2)}) %collective-permute-start.5) | collective-permute-done | bytes 786464 | tf_op jit(solution)/shard_map/ppermute | solution.py:50
  16.0 0.1 shard_map.106
  16.1 0.9 collective-permute-start.2
  17.0 2.6 %collective-permute-start.3 = (bf16[128,512]{1,0:T(8,128)(2,1)S(1)}, bf16[128,512]{1,0:T(8,128)(2,1)S(1)}, u32[]{:S(2)}, u32[]{:S(2)}) collective-permute-start(bf16[128,512]{1,0:T(8,128)(2,1)S(1)} %get-tuple-element.68), channel_id=1, source_target_pairs={{0,8},{1,9},{2,10},{3,11},{4,12},{5,13},{6,14},{7,15},{8,0},{9,1},... | collective-permute-start | bytes 393224 | tf_op jit(solution)/shard_map/ppermute | solution.py:59
  19.6 1.0 %collective-permute-start.4 = (bf16[128,512]{1,0:T(8,128)(2,1)S(1)}, bf16[128,512]{1,0:T(8,128)(2,1)S(1)}, u32[]{:S(2)}, u32[]{:S(2)}) collective-permute-start(bf16[128,512]{1,0:T(8,128)(2,1)S(1)} %get-tuple-element.69), channel_id=1, source_target_pairs={{0,12},{1,13},{2,14},{3,15},{4,8},{5,9},{6,10},{7,11},{8,4},{9,5},... | collective-permute-start | bytes 393224 | tf_op jit(solution)/shard_map/ppermute | solution.py:59
  20.6 1.6 %collective-permute-done.2.refs_1_ = bf16[128,512]{1,0:T(8,128)(2,1)S(1)} collective-permute-done((bf16[128,512]{1,0:T(8,128)(2,1)S(1)}, bf16[128,512]{1,0:T(8,128)(2,1)S(1)}, u32[]{:S(2)}, u32[]{:S(2)}) %collective-permute-start.2) | collective-permute-done | bytes 131104 | tf_op jit(solution)/shard_map/ppermute | solution.py:59
  22.2 6.9 %collective-permute-done.3.refs_2_ = bf16[128,512]{1,0:T(8,128)(2,1)S(1)} collective-permute-done((bf16[128,512]{1,0:T(8,128)(2,1)S(1)}, bf16[128,512]{1,0:T(8,128)(2,1)S(1)}, u32[]{:S(2)}, u32[]{:S(2)}) %collective-permute-start.3) | collective-permute-done | bytes 131104 | tf_op jit(solution)/shard_map/ppermute | solution.py:59
  29.1 0.1 shard_map.107
  29.1 0.0 copy-start.1
  29.1 0.1 collective-permute-start.21
  29.2 0.1 shard_map.108
  29.3 0.5 collective-permute-start.10
  29.8 2.0 %collective-permute-start.7 = (bf16[64,512]{1,0:T(8,128)(2,1)S(1)}, bf16[64,512]{1,0:T(8,128)(2,1)S(1)}, u32[]{:S(2)}, u32[]{:S(2)}) collective-permute-start(bf16[64,512]{1,0:T(8,128)(2,1)S(1)} %get-tuple-element.76), channel_id=1, source_target_pairs={{0,4},{1,5},{2,6},{3,7},{4,0},{5,1},{6,2},{7,3},{8,12},{9,13},{10,... | collective-permute-start | bytes 196616 | tf_op jit(solution)/shard_map/ppermute | solution.py:59
  31.8 1.4 %collective-permute-start.8 = (bf16[64,512]{1,0:T(8,128)(2,1)S(1)}, bf16[64,512]{1,0:T(8,128)(2,1)S(1)}, u32[]{:S(2)}, u32[]{:S(2)}) collective-permute-start(bf16[64,512]{1,0:T(8,128)(2,1)S(1)} %get-tuple-element.77), channel_id=1, source_target_pairs={{0,8},{1,9},{2,10},{3,11},{4,12},{5,13},{6,14},{7,15},{8,0},{9,1},... | collective-permute-start | bytes 196616 | tf_op jit(solution)/shard_map/ppermute | solution.py:59
  33.2 1.5 %collective-permute-start.9 = (bf16[64,512]{1,0:T(8,128)(2,1)S(1)}, bf16[64,512]{1,0:T(8,128)(2,1)S(1)}, u32[]{:S(2)}, u32[]{:S(2)}) collective-permute-start(bf16[64,512]{1,0:T(8,128)(2,1)S(1)} %get-tuple-element.78), channel_id=1, source_target_pairs={{0,12},{1,13},{2,14},{3,15},{4,8},{5,9},{6,10},{7,11},{8,4},{9,5},... | collective-permute-start | bytes 196616 | tf_op jit(solution)/shard_map/ppermute | solution.py:59
  34.6 6.4 %collective-permute-done.10.refs_5_ = bf16[64,512]{1,0:T(8,128)(2,1)S(1)} collective-permute-done((bf16[64,512]{1,0:T(8,128)(2,1)S(1)}, bf16[64,512]{1,0:T(8,128)(2,1)S(1)}, u32[]{:S(2)}, u32[]{:S(2)}) %collective-permute-start.10) | collective-permute-done | bytes 65568 | tf_op jit(solution)/shard_map/ppermute | solution.py:59
  41.0 2.9 %collective-permute-done.7.refs_1_ = bf16[64,512]{1,0:T(8,128)(2,1)S(1)} collective-permute-done((bf16[64,512]{1,0:T(8,128)(2,1)S(1)}, bf16[64,512]{1,0:T(8,128)(2,1)S(1)}, u32[]{:S(2)}, u32[]{:S(2)}) %collective-permute-start.7) | collective-permute-done | bytes 65568 | tf_op jit(solution)/shard_map/ppermute | solution.py:59
  43.9 3.2 %collective-permute-done.8.refs_2_ = bf16[64,512]{1,0:T(8,128)(2,1)S(1)} collective-permute-done((bf16[64,512]{1,0:T(8,128)(2,1)S(1)}, bf16[64,512]{1,0:T(8,128)(2,1)S(1)}, u32[]{:S(2)}, u32[]{:S(2)}) %collective-permute-start.8) | collective-permute-done | bytes 65568 | tf_op jit(solution)/shard_map/ppermute | solution.py:59
  47.1 0.1 shard_map.109
  47.2 1.3 %collective-permute-start.11 = (bf16[64,512]{1,0:T(8,128)(2,1)S(1)}, bf16[64,512]{1,0:T(8,128)(2,1)S(1)}, u32[]{:S(2)}, u32[]{:S(2)}) collective-permute-start(bf16[64,512]{1,0:T(8,128)(2,1)S(1)} %get-tuple-element.91.refs_0_), channel_id=1, source_target_pairs={{0,4},{1,5},{2,6},{3,7},{4,0},{5,1},{6,2},{7,3},{8,12},{9,13},{10,... | collective-permute-start | bytes 196616 | tf_op jit(solution)/shard_map/ppermute | solution.py:59
  48.5 0.2 collective-permute-start.12
  48.7 3.0 %collective-permute-start.13 = (bf16[64,512]{1,0:T(8,128)(2,1)S(1)}, bf16[64,512]{1,0:T(8,128)(2,1)S(1)}, u32[]{:S(2)}, u32[]{:S(2)}) collective-permute-start(bf16[64,512]{1,0:T(8,128)(2,1)S(1)} %get-tuple-element.91.refs_0_), channel_id=1, source_target_pairs={{0,12},{1,13},{2,14},{3,15},{4,8},{5,9},{6,10},{7,11},{8,4},{9,5},... | collective-permute-start | bytes 196616 | tf_op jit(solution)/shard_map/ppermute | solution.py:59
  51.7 3.9 %collective-permute-done.12.refs_2_ = bf16[64,512]{1,0:T(8,128)(2,1)S(1)} collective-permute-done((bf16[64,512]{1,0:T(8,128)(2,1)S(1)}, bf16[64,512]{1,0:T(8,128)(2,1)S(1)}, u32[]{:S(2)}, u32[]{:S(2)}) %collective-permute-start.12) | collective-permute-done | bytes 65568 | tf_op jit(solution)/shard_map/ppermute | solution.py:59
  55.6 0.3 collective-permute-done.14.refs_1_
  55.9 1.0 %collective-permute-start.18 = (bf16[128,512]{1,0:T(8,128)(2,1)S(1)}, bf16[128,512]{1,0:T(8,128)(2,1)S(1)}, u32[]{:S(2)}, u32[]{:S(2)}) collective-permute-start(bf16[128,512]{1,0:T(8,128)(2,1)S(1)} %shard_map.111.refs_0_), channel_id=1, source_target_pairs={{0,4},{1,5},{2,6},{3,7},{4,0},{5,1},{6,2},{7,3},{8,12},{9,13},{10,... | collective-permute-start | bytes 393224 | tf_op jit(solution)/shard_map/ppermute | solution.py:59
  56.9 1.5 %collective-permute-start.19 = (bf16[128,512]{1,0:T(8,128)(2,1)S(1)}, bf16[128,512]{1,0:T(8,128)(2,1)S(1)}, u32[]{:S(2)}, u32[]{:S(2)}) collective-permute-start(bf16[128,512]{1,0:T(8,128)(2,1)S(1)} %shard_map.111.refs_0_), channel_id=1, source_target_pairs={{0,8},{1,9},{2,10},{3,11},{4,12},{5,13},{6,14},{7,15},{8,0},{9,1},... | collective-permute-start | bytes 393224 | tf_op jit(solution)/shard_map/ppermute | solution.py:59
  58.5 1.9 %collective-permute-start.20 = (bf16[128,512]{1,0:T(8,128)(2,1)S(1)}, bf16[128,512]{1,0:T(8,128)(2,1)S(1)}, u32[]{:S(2)}, u32[]{:S(2)}) collective-permute-start(bf16[128,512]{1,0:T(8,128)(2,1)S(1)} %shard_map.111.refs_0_), channel_id=1, source_target_pairs={{0,12},{1,13},{2,14},{3,15},{4,8},{5,9},{6,10},{7,11},{8,4},{9,5},... | collective-permute-start | bytes 393224 | tf_op jit(solution)/shard_map/ppermute | solution.py:59
  60.5 0.1 collective-permute-start.16
  60.6 2.2 %shard_map.112 = (f32[512,768]{1,0:T(8,128)S(1)}, bf16[512,256]{1,0:T(8,128)(2,1)S(1)}) custom-call(bf16[512,768]{1,0:T(8,128)(2,1)S(1)} %copy-done.2, bf16[512,768]{1,0:T(8,128)(2,1)S(1)} %collective-permute-done.5.refs_1_, bf16[512,768]{1,0:T(8,128)(2,1)S(1)} %collective-permute-done.21.refs_2_, bf16[512,768]{1,0:T(8,128)(2,1)S(1)} %copy-done, ...), custom_call_target="tpu_custom_call" | custom-call | flops 235929600 | bytes 4980736 | tf_op jit(solution)/shard_map/pallas_call | solution.py:298
  62.9 6.2 %collective-permute-done.19.refs_2_ = bf16[128,512]{1,0:T(8,128)(2,1)S(1)} collective-permute-done((bf16[128,512]{1,0:T(8,128)(2,1)S(1)}, bf16[128,512]{1,0:T(8,128)(2,1)S(1)}, u32[]{:S(2)}, u32[]{:S(2)}) %collective-permute-start.19) | collective-permute-done | bytes 131104 | tf_op jit(solution)/shard_map/ppermute | solution.py:59
  69.0 0.1 shard_map.113.refs_2_
  69.1 0.1 collective-permute-start.22
  69.2 0.5 collective-permute-start.15
  69.7 0.1 collective-permute-start.17
  69.8 1.5 %shard_map.114 = (f32[256,768]{1,0:T(8,128)S(1)}, f32[320,128]{1,0:T(8,128)S(1)}) custom-call(bf16[64,2048]{1,0:T(8,128)(2,1)S(1)} %shard_map.110.refs_0_, bf16[64,2048]{1,0:T(8,128)(2,1)S(1)} %collective-permute-done.16.refs_1_, bf16[128,2048]{1,0:T(8,128)(2,1)S(1)} %shard_map.113.refs_2_, bf16[2048,768]{1,0:T(8,128)(2,1)S(1)} %copy-done.1, ...), custom_call_target="tpu_custom_call" | custom-call | flops 905969664 | bytes 7503872 | tf_op jit(solution)/shard_map/pallas_call | solution.py:91
  71.3 0.2 collective-permute-done.15.refs_0_
  71.4 0.4 collective-permute-done.17.refs_1_
  71.8 1.5 %shard_map.115 = (f32[256,768]{1,0:T(8,128)S(1)}, bf16[320,128]{1,0:T(8,128)(2,1)S(1)}) custom-call(bf16[64,2048]{1,0:T(8,128)(2,1)S(1)} %collective-permute-done.15.refs_0_, bf16[64,2048]{1,0:T(8,128)(2,1)S(1)} %collective-permute-done.17.refs_1_, bf16[128,2048]{1,0:T(8,128)(2,1)S(1)} %collective-permute-done.22.refs_2_, bf16[2048,768]{1,0:T(8,128)(2,1)S(1)} %copy-done.1, ...), custom_call_target="tpu_custom_call" | custom-call | flops 905969664 | bytes 7421952 | tf_op jit(solution)/shard_map/pallas_call | solution.py:91
  73.4 0.2 collective-permute-start.23
  73.6 1.1 %collective-permute-done.23.refs_0_ = bf16[320,128]{1,0:T(8,128)(2,1)S(1)} collective-permute-done((bf16[320,128]{1,0:T(8,128)(2,1)S(1)}, bf16[320,128]{1,0:T(8,128)(2,1)S(1)}, u32[]{:S(2)}, u32[]{:S(2)}) %collective-permute-start.23) | collective-permute-done | bytes 81952 | tf_op jit(solution)/shard_map/ppermute | solution.py:59
  74.7 0.1 collective-permute-start.24
  74.8 4.5 %collective-permute-done.24.refs_0_ = bf16[320,128]{1,0:T(8,128)(2,1)S(1)} collective-permute-done((bf16[320,128]{1,0:T(8,128)(2,1)S(1)}, bf16[320,128]{1,0:T(8,128)(2,1)S(1)}, u32[]{:S(2)}, u32[]{:S(2)}) %collective-permute-start.24) | collective-permute-done | bytes 81952 | tf_op jit(solution)/shard_map/ppermute | solution.py:59
  79.3 2.0 %collective-permute-start.25 = (bf16[320,128]{1,0:T(8,128)(2,1)S(1)}, bf16[320,128]{1,0:T(8,128)(2,1)S(1)}, u32[]{:S(2)}, u32[]{:S(2)}) collective-permute-start(bf16[320,128]{1,0:T(8,128)(2,1)S(1)} %get-tuple-element.118), channel_id=1, source_target_pairs={{0,4},{1,5},{2,6},{3,7},{4,0},{5,1},{6,2},{7,3},{8,12},{9,13},{10,... | collective-permute-start | bytes 245768 | tf_op jit(solution)/shard_map/ppermute | solution.py:59
  81.3 1.1 %collective-permute-start.26 = (bf16[320,128]{1,0:T(8,128)(2,1)S(1)}, bf16[320,128]{1,0:T(8,128)(2,1)S(1)}, u32[]{:S(2)}, u32[]{:S(2)}) collective-permute-start(bf16[320,128]{1,0:T(8,128)(2,1)S(1)} %get-tuple-element.118), channel_id=1, source_target_pairs={{0,8},{1,9},{2,10},{3,11},{4,12},{5,13},{6,14},{7,15},{8,0},{9,1},... | collective-permute-start | bytes 245768 | tf_op jit(solution)/shard_map/ppermute | solution.py:59
  82.4 1.4 %collective-permute-start.27 = (bf16[320,128]{1,0:T(8,128)(2,1)S(1)}, bf16[320,128]{1,0:T(8,128)(2,1)S(1)}, u32[]{:S(2)}, u32[]{:S(2)}) collective-permute-start(bf16[320,128]{1,0:T(8,128)(2,1)S(1)} %get-tuple-element.118), channel_id=1, source_target_pairs={{0,12},{1,13},{2,14},{3,15},{4,8},{5,9},{6,10},{7,11},{8,4},{9,5},... | collective-permute-start | bytes 245768 | tf_op jit(solution)/shard_map/ppermute | solution.py:59
  83.8 0.3 collective-permute-done.25.refs_0_
  84.1 5.9 %collective-permute-done.26.refs_1_ = bf16[320,128]{1,0:T(8,128)(2,1)S(1)} collective-permute-done((bf16[320,128]{1,0:T(8,128)(2,1)S(1)}, bf16[320,128]{1,0:T(8,128)(2,1)S(1)}, u32[]{:S(2)}, u32[]{:S(2)}) %collective-permute-start.26) | collective-permute-done | bytes 81952 | tf_op jit(solution)/shard_map/ppermute | solution.py:59
  90.1 0.1 collective-permute-start.28
  90.2 1.3 %collective-permute-done.28.refs_1_ = bf16[320,128]{1,0:T(8,128)(2,1)S(1)} collective-permute-done((bf16[320,128]{1,0:T(8,128)(2,1)S(1)}, bf16[320,128]{1,0:T(8,128)(2,1)S(1)}, u32[]{:S(2)}, u32[]{:S(2)}) %collective-permute-start.28) | collective-permute-done | bytes 81952 | tf_op jit(solution)/shard_map/ppermute | solution.py:59
  91.4 2.5 %shard_map.119 = (bf16[512,768]{1,0:T(8,128)(2,1)}, bf16[512,768]{1,0:T(8,128)(2,1)}) custom-call(bf16[320,128]{1,0:T(8,128)(2,1)S(1)} %shard_map.118.refs_0_, bf16[320,128]{1,0:T(8,128)(2,1)S(1)} %collective-permute-done.28.refs_1_, f32[256,768]{1,0:T(8,128)S(1)} %get-tuple-element.119.refs_2_, f32[256,768]{1,0:T(8,128)S(1)} %get-tuple-element.120.refs_3_, ...), custom_call_target="tpu_custom_call" | custom-call | flops 201326592 | bytes 4718592 | tf_op jit(solution)/shard_map/pallas_call | solution.py:467
  (30 shorter events, 0.2 us)
Async XLA Ops:
  0.6 15.4 %collective-permute-start.5 = (bf16[512,768]{1,0:T(8,128)(2,1)}, bf16[512,768]{1,0:T(8,128)(2,1)S(1)}, u32[]{:S(2)}, u32[]{:S(2)}) collective-permute-start(bf16[512,768]{1,0:T(8,128)(2,1)} %refs_5_.5), channel_id=1, source_target_pairs={{0,1},{1,2},{2,3},{3,4},{4,5},{5,6},{6,7},{7,8},{8,9},{9,10},{10,1... | collective-permute-start | bytes 2359304 | tf_op jit(solution)/shard_map/ppermute | solution.py:50
  5.4 23.7 %copy-start.2 = (bf16[512,768]{1,0:T(8,128)(2,1)S(1)}, bf16[512,768]{1,0:T(8,128)(2,1)}, u32[]{:S(2)}) copy-start(bf16[512,768]{1,0:T(8,128)(2,1)} %refs_5_.5) | copy-start | bytes 2359300
  5.5 54.9 %copy-start.7 = (f32[768]{0:T(1024)S(1)}, f32[768]{0:T(1024)}, u32[]{:S(2)}) copy-start(f32[768]{0:T(1024)} %param.12) | copy-start | bytes 9220
  5.5 54.9 %copy-start.8 = (f32[768]{0:T(1024)S(1)}, f32[768]{0:T(1024)}, u32[]{:S(2)}) copy-start(f32[768]{0:T(1024)} %param.13) | copy-start | bytes 9220
  5.5 55.1 %copy-start = (bf16[512,768]{1,0:T(8,128)(2,1)S(1)}, bf16[512,768]{1,0:T(8,128)(2,1)}, u32[]{:S(2)}) copy-start(bf16[512,768]{1,0:T(8,128)(2,1)} %refs_4_.2) | copy-start | bytes 2359300
  5.5 55.1 %copy-start.3 = (bf16[2,128,128]{2,1,0:T(8,128)(2,1)S(1)}, bf16[2,128,128]{2,1,0:T(8,128)(2,1)}, u32[]{:S(2)}) copy-start(bf16[2,128,128]{2,1,0:T(8,128)(2,1)} %constant.2.clone.refs_4_) | copy-start | bytes 196612
  5.5 55.1 %copy-start.4 = (f32[512]{0:T(512)S(1)}, f32[512]{0:T(512)}, u32[]{:S(2)}) copy-start(f32[512]{0:T(512)} %param.14) | copy-start | bytes 6148
  5.5 55.1 %copy-start.5 = (s32[512]{0:T(512)S(1)}, s32[512]{0:T(512)}, u32[]{:S(2)}) copy-start(s32[512]{0:T(512)} %param.15) | copy-start | bytes 6148
  5.5 55.1 %copy-start.6 = (s32[512]{0:T(512)S(1)}, s32[512]{0:T(512)}, u32[]{:S(2)}) copy-start(s32[512]{0:T(512)} %param.16) | copy-start | bytes 6148
  5.5 4.2 %collective-permute-start = (bf16[128,2048]{1,0:T(8,128)(2,1)S(1)}, bf16[128,2048]{1,0:T(8,128)(2,1)S(1)}, u32[]{:S(2)}, u32[]{:S(2)}) collective-permute-start(bf16[128,2048]{1,0:T(8,128)(2,1)S(1)} %get-tuple-element.63), channel_id=1, source_target_pairs={{0,1},{1,0},{2,3},{3,2},{4,5},{5,4},{6,7},{7,6},{8,9},{9,8},{10,11... | collective-permute-start | bytes 1572872 | tf_op jit(solution)/shard_map/ppermute | solution.py:59
  8.2 7.8 %collective-permute-start.1 = (bf16[128,2048]{1,0:T(8,128)(2,1)S(1)}, bf16[128,2048]{1,0:T(8,128)(2,1)S(1)}, u32[]{:S(2)}, u32[]{:S(2)}) collective-permute-start(bf16[128,2048]{1,0:T(8,128)(2,1)S(1)} %get-tuple-element.66), channel_id=1, source_target_pairs={{0,1},{1,0},{2,3},{3,2},{4,5},{5,4},{6,7},{7,6},{8,9},{9,8},{10,11... | collective-permute-start | bytes 1572872 | tf_op jit(solution)/shard_map/ppermute | solution.py:59
  16.0 13.0 %collective-permute-start.6 = (bf16[64,2048]{1,0:T(8,128)(2,1)S(1)}, bf16[64,2048]{1,0:T(8,128)(2,1)S(1)}, u32[]{:S(2)}, u32[]{:S(2)}) collective-permute-start(bf16[64,2048]{1,0:T(8,128)(2,1)S(1)} %get-tuple-element.72), channel_id=1, source_target_pairs={{0,2},{1,3},{2,0},{3,1},{4,6},{5,7},{6,4},{7,5},{8,10},{9,11},{10,... | collective-permute-start | bytes 786440 | tf_op jit(solution)/shard_map/ppermute | solution.py:59
  16.1 6.0 %collective-permute-start.2 = (bf16[128,512]{1,0:T(8,128)(2,1)S(1)}, bf16[128,512]{1,0:T(8,128)(2,1)S(1)}, u32[]{:S(2)}, u32[]{:S(2)}) collective-permute-start(bf16[128,512]{1,0:T(8,128)(2,1)S(1)} %get-tuple-element.67), channel_id=1, source_target_pairs={{0,4},{1,5},{2,6},{3,7},{4,0},{5,1},{6,2},{7,3},{8,12},{9,13},{10,... | collective-permute-start | bytes 393224 | tf_op jit(solution)/shard_map/ppermute | solution.py:59
  17.0 12.1 %collective-permute-start.3 = (bf16[128,512]{1,0:T(8,128)(2,1)S(1)}, bf16[128,512]{1,0:T(8,128)(2,1)S(1)}, u32[]{:S(2)}, u32[]{:S(2)}) collective-permute-start(bf16[128,512]{1,0:T(8,128)(2,1)S(1)} %get-tuple-element.68), channel_id=1, source_target_pairs={{0,8},{1,9},{2,10},{3,11},{4,12},{5,13},{6,14},{7,15},{8,0},{9,1},... | collective-permute-start | bytes 393224 | tf_op jit(solution)/shard_map/ppermute | solution.py:59
  19.6 9.5 %collective-permute-start.4 = (bf16[128,512]{1,0:T(8,128)(2,1)S(1)}, bf16[128,512]{1,0:T(8,128)(2,1)S(1)}, u32[]{:S(2)}, u32[]{:S(2)}) collective-permute-start(bf16[128,512]{1,0:T(8,128)(2,1)S(1)} %get-tuple-element.69), channel_id=1, source_target_pairs={{0,12},{1,13},{2,14},{3,15},{4,8},{5,9},{6,10},{7,11},{8,4},{9,5},... | collective-permute-start | bytes 393224 | tf_op jit(solution)/shard_map/ppermute | solution.py:59
  29.1 40.6 %copy-start.1 = (bf16[2048,768]{1,0:T(8,128)(2,1)S(1)}, bf16[2048,768]{1,0:T(8,128)(2,1)}, u32[]{:S(2)}) copy-start(bf16[2048,768]{1,0:T(8,128)(2,1)} %refs_3_.5) | copy-start | bytes 9437188
  29.1 31.4 %collective-permute-start.21 = (bf16[512,768]{1,0:T(8,128)(2,1)S(1)}, bf16[512,768]{1,0:T(8,128)(2,1)S(1)}, u32[]{:S(2)}, u32[]{:S(2)}) collective-permute-start(bf16[512,768]{1,0:T(8,128)(2,1)S(1)} %copy-done.2), channel_id=1, source_target_pairs={{0,15},{1,0},{2,1},{3,2},{4,3},{5,4},{6,5},{7,6},{8,7},{9,8},{10,9... | collective-permute-start | bytes 2359304 | tf_op jit(solution)/shard_map/ppermute | solution.py:50
  29.3 11.8 %collective-permute-start.10 = (bf16[64,512]{1,0:T(8,128)(2,1)S(1)}, bf16[64,512]{1,0:T(8,128)(2,1)S(1)}, u32[]{:S(2)}, u32[]{:S(2)}) collective-permute-start(bf16[64,512]{1,0:T(8,128)(2,1)S(1)} %get-tuple-element.83), channel_id=1, source_target_pairs={{0,2},{1,3},{2,0},{3,1},{4,6},{5,7},{6,4},{7,5},{8,10},{9,11},{10,... | collective-permute-start | bytes 196616 | tf_op jit(solution)/shard_map/ppermute | solution.py:59
  29.8 14.1 %collective-permute-start.7 = (bf16[64,512]{1,0:T(8,128)(2,1)S(1)}, bf16[64,512]{1,0:T(8,128)(2,1)S(1)}, u32[]{:S(2)}, u32[]{:S(2)}) collective-permute-start(bf16[64,512]{1,0:T(8,128)(2,1)S(1)} %get-tuple-element.76), channel_id=1, source_target_pairs={{0,4},{1,5},{2,6},{3,7},{4,0},{5,1},{6,2},{7,3},{8,12},{9,13},{10,... | collective-permute-start | bytes 196616 | tf_op jit(solution)/shard_map/ppermute | solution.py:59
  31.8 15.3 %collective-permute-start.8 = (bf16[64,512]{1,0:T(8,128)(2,1)S(1)}, bf16[64,512]{1,0:T(8,128)(2,1)S(1)}, u32[]{:S(2)}, u32[]{:S(2)}) collective-permute-start(bf16[64,512]{1,0:T(8,128)(2,1)S(1)} %get-tuple-element.77), channel_id=1, source_target_pairs={{0,8},{1,9},{2,10},{3,11},{4,12},{5,13},{6,14},{7,15},{8,0},{9,1},... | collective-permute-start | bytes 196616 | tf_op jit(solution)/shard_map/ppermute | solution.py:59
  33.2 14.0 %collective-permute-start.9 = (bf16[64,512]{1,0:T(8,128)(2,1)S(1)}, bf16[64,512]{1,0:T(8,128)(2,1)S(1)}, u32[]{:S(2)}, u32[]{:S(2)}) collective-permute-start(bf16[64,512]{1,0:T(8,128)(2,1)S(1)} %get-tuple-element.78), channel_id=1, source_target_pairs={{0,12},{1,13},{2,14},{3,15},{4,8},{5,9},{6,10},{7,11},{8,4},{9,5},... | collective-permute-start | bytes 196616 | tf_op jit(solution)/shard_map/ppermute | solution.py:59
  47.2 4.5 %collective-permute-start.11 = (bf16[64,512]{1,0:T(8,128)(2,1)S(1)}, bf16[64,512]{1,0:T(8,128)(2,1)S(1)}, u32[]{:S(2)}, u32[]{:S(2)}) collective-permute-start(bf16[64,512]{1,0:T(8,128)(2,1)S(1)} %get-tuple-element.91.refs_0_), channel_id=1, source_target_pairs={{0,4},{1,5},{2,6},{3,7},{4,0},{5,1},{6,2},{7,3},{8,12},{9,13},{10,... | collective-permute-start | bytes 196616 | tf_op jit(solution)/shard_map/ppermute | solution.py:59
  48.5 7.1 %collective-permute-start.12 = (bf16[64,512]{1,0:T(8,128)(2,1)S(1)}, bf16[64,512]{1,0:T(8,128)(2,1)S(1)}, u32[]{:S(2)}, u32[]{:S(2)}) collective-permute-start(bf16[64,512]{1,0:T(8,128)(2,1)S(1)} %get-tuple-element.91.refs_0_), channel_id=1, source_target_pairs={{0,8},{1,9},{2,10},{3,11},{4,12},{5,13},{6,14},{7,15},{8,0},{9,1},... | collective-permute-start | bytes 196616 | tf_op jit(solution)/shard_map/ppermute | solution.py:59
  48.7 6.9 %collective-permute-start.13 = (bf16[64,512]{1,0:T(8,128)(2,1)S(1)}, bf16[64,512]{1,0:T(8,128)(2,1)S(1)}, u32[]{:S(2)}, u32[]{:S(2)}) collective-permute-start(bf16[64,512]{1,0:T(8,128)(2,1)S(1)} %get-tuple-element.91.refs_0_), channel_id=1, source_target_pairs={{0,12},{1,13},{2,14},{3,15},{4,8},{5,9},{6,10},{7,11},{8,4},{9,5},... | collective-permute-start | bytes 196616 | tf_op jit(solution)/shard_map/ppermute | solution.py:59
  51.7 4.3 %collective-permute-start.14 = (bf16[64,512]{1,0:T(8,128)(2,1)S(1)}, bf16[64,512]{1,0:T(8,128)(2,1)S(1)}, u32[]{:S(2)}, u32[]{:S(2)}) collective-permute-start(bf16[64,512]{1,0:T(8,128)(2,1)S(1)} %get-tuple-element.95.refs_0_), channel_id=1, source_target_pairs={{0,2},{1,3},{2,0},{3,1},{4,6},{5,7},{6,4},{7,5},{8,10},{9,11},{10,... | collective-permute-start | bytes 196616 | tf_op jit(solution)/shard_map/ppermute | solution.py:59
  55.9 6.9 %collective-permute-start.18 = (bf16[128,512]{1,0:T(8,128)(2,1)S(1)}, bf16[128,512]{1,0:T(8,128)(2,1)S(1)}, u32[]{:S(2)}, u32[]{:S(2)}) collective-permute-start(bf16[128,512]{1,0:T(8,128)(2,1)S(1)} %shard_map.111.refs_0_), channel_id=1, source_target_pairs={{0,4},{1,5},{2,6},{3,7},{4,0},{5,1},{6,2},{7,3},{8,12},{9,13},{10,... | collective-permute-start | bytes 393224 | tf_op jit(solution)/shard_map/ppermute | solution.py:59
  56.9 12.1 %collective-permute-start.19 = (bf16[128,512]{1,0:T(8,128)(2,1)S(1)}, bf16[128,512]{1,0:T(8,128)(2,1)S(1)}, u32[]{:S(2)}, u32[]{:S(2)}) collective-permute-start(bf16[128,512]{1,0:T(8,128)(2,1)S(1)} %shard_map.111.refs_0_), channel_id=1, source_target_pairs={{0,8},{1,9},{2,10},{3,11},{4,12},{5,13},{6,14},{7,15},{8,0},{9,1},... | collective-permute-start | bytes 393224 | tf_op jit(solution)/shard_map/ppermute | solution.py:59
  58.5 10.5 %collective-permute-start.20 = (bf16[128,512]{1,0:T(8,128)(2,1)S(1)}, bf16[128,512]{1,0:T(8,128)(2,1)S(1)}, u32[]{:S(2)}, u32[]{:S(2)}) collective-permute-start(bf16[128,512]{1,0:T(8,128)(2,1)S(1)} %shard_map.111.refs_0_), channel_id=1, source_target_pairs={{0,12},{1,13},{2,14},{3,15},{4,8},{5,9},{6,10},{7,11},{8,4},{9,5},... | collective-permute-start | bytes 393224 | tf_op jit(solution)/shard_map/ppermute | solution.py:59
  60.5 9.2 %collective-permute-start.16 = (bf16[64,2048]{1,0:T(8,128)(2,1)S(1)}, bf16[64,2048]{1,0:T(8,128)(2,1)S(1)}, u32[]{:S(2)}, u32[]{:S(2)}) collective-permute-start(bf16[64,2048]{1,0:T(8,128)(2,1)S(1)} %shard_map.110.refs_0_), channel_id=1, source_target_pairs={{0,2},{1,3},{2,0},{3,1},{4,6},{5,7},{6,4},{7,5},{8,10},{9,11},{10,... | collective-permute-start | bytes 786440 | tf_op jit(solution)/shard_map/ppermute | solution.py:59
  69.1 2.7 %collective-permute-start.22 = (bf16[128,2048]{1,0:T(8,128)(2,1)S(1)}, bf16[128,2048]{1,0:T(8,128)(2,1)S(1)}, u32[]{:S(2)}, u32[]{:S(2)}) collective-permute-start(bf16[128,2048]{1,0:T(8,128)(2,1)S(1)} %shard_map.113.refs_2_), channel_id=1, source_target_pairs={{0,1},{1,0},{2,3},{3,2},{4,5},{5,4},{6,7},{7,6},{8,9},{9,8},{10,11... | collective-permute-start | bytes 1572872 | tf_op jit(solution)/shard_map/ppermute | solution.py:59
  69.2 2.3 %collective-permute-start.15 = (bf16[64,2048]{1,0:T(8,128)(2,1)S(1)}, bf16[64,2048]{1,0:T(8,128)(2,1)S(1)}, u32[]{:S(2)}, u32[]{:S(2)}) collective-permute-start(bf16[64,2048]{1,0:T(8,128)(2,1)S(1)} %shard_map.110.refs_0_), channel_id=1, source_target_pairs={{0,1},{1,0},{2,3},{3,2},{4,5},{5,4},{6,7},{7,6},{8,9},{9,8},{10,11... | collective-permute-start | bytes 786440 | tf_op jit(solution)/shard_map/ppermute | solution.py:59
  69.7 2.1 %collective-permute-start.17 = (bf16[64,2048]{1,0:T(8,128)(2,1)S(1)}, bf16[64,2048]{1,0:T(8,128)(2,1)S(1)}, u32[]{:S(2)}, u32[]{:S(2)}) collective-permute-start(bf16[64,2048]{1,0:T(8,128)(2,1)S(1)} %collective-permute-done.16.refs_1_), channel_id=1, source_target_pairs={{0,1},{1,0},{2,3},{3,2},{4,5},{5,4},{6,7},{7,6},{8,9},{9,8},{10,11... | collective-permute-start | bytes 786440 | tf_op jit(solution)/shard_map/ppermute | solution.py:59
  73.4 1.3 %collective-permute-start.23 = (bf16[320,128]{1,0:T(8,128)(2,1)S(1)}, bf16[320,128]{1,0:T(8,128)(2,1)S(1)}, u32[]{:S(2)}, u32[]{:S(2)}) collective-permute-start(bf16[320,128]{1,0:T(8,128)(2,1)S(1)} %get-tuple-element.114), channel_id=1, source_target_pairs={{0,1},{1,0},{2,3},{3,2},{4,5},{5,4},{6,7},{7,6},{8,9},{9,8},{10,11... | collective-permute-start | bytes 245768 | tf_op jit(solution)/shard_map/ppermute | solution.py:59
  74.7 4.6 %collective-permute-start.24 = (bf16[320,128]{1,0:T(8,128)(2,1)S(1)}, bf16[320,128]{1,0:T(8,128)(2,1)S(1)}, u32[]{:S(2)}, u32[]{:S(2)}) collective-permute-start(bf16[320,128]{1,0:T(8,128)(2,1)S(1)} %get-tuple-element.116), channel_id=1, source_target_pairs={{0,2},{1,3},{2,0},{3,1},{4,6},{5,7},{6,4},{7,5},{8,10},{9,11},{10,... | collective-permute-start | bytes 245768 | tf_op jit(solution)/shard_map/ppermute | solution.py:59
  79.3 4.8 %collective-permute-start.25 = (bf16[320,128]{1,0:T(8,128)(2,1)S(1)}, bf16[320,128]{1,0:T(8,128)(2,1)S(1)}, u32[]{:S(2)}, u32[]{:S(2)}) collective-permute-start(bf16[320,128]{1,0:T(8,128)(2,1)S(1)} %get-tuple-element.118), channel_id=1, source_target_pairs={{0,4},{1,5},{2,6},{3,7},{4,0},{5,1},{6,2},{7,3},{8,12},{9,13},{10,... | collective-permute-start | bytes 245768 | tf_op jit(solution)/shard_map/ppermute | solution.py:59
  81.3 8.7 %collective-permute-start.26 = (bf16[320,128]{1,0:T(8,128)(2,1)S(1)}, bf16[320,128]{1,0:T(8,128)(2,1)S(1)}, u32[]{:S(2)}, u32[]{:S(2)}) collective-permute-start(bf16[320,128]{1,0:T(8,128)(2,1)S(1)} %get-tuple-element.118), channel_id=1, source_target_pairs={{0,8},{1,9},{2,10},{3,11},{4,12},{5,13},{6,14},{7,15},{8,0},{9,1},... | collective-permute-start | bytes 245768 | tf_op jit(solution)/shard_map/ppermute | solution.py:59
  82.4 7.6 %collective-permute-start.27 = (bf16[320,128]{1,0:T(8,128)(2,1)S(1)}, bf16[320,128]{1,0:T(8,128)(2,1)S(1)}, u32[]{:S(2)}, u32[]{:S(2)}) collective-permute-start(bf16[320,128]{1,0:T(8,128)(2,1)S(1)} %get-tuple-element.118), channel_id=1, source_target_pairs={{0,12},{1,13},{2,14},{3,15},{4,8},{5,9},{6,10},{7,11},{8,4},{9,5},... | collective-permute-start | bytes 245768 | tf_op jit(solution)/shard_map/ppermute | solution.py:59
  90.1 1.3 %collective-permute-start.28 = (bf16[320,128]{1,0:T(8,128)(2,1)S(1)}, bf16[320,128]{1,0:T(8,128)(2,1)S(1)}, u32[]{:S(2)}, u32[]{:S(2)}) collective-permute-start(bf16[320,128]{1,0:T(8,128)(2,1)S(1)} %shard_map.118.refs_0_), channel_id=1, source_target_pairs={{0,1},{1,0},{2,3},{3,2},{4,5},{5,4},{6,7},{7,6},{8,9},{9,8},{10,11... | collective-permute-start | bytes 245768 | tf_op jit(solution)/shard_map/ppermute | solution.py:59

commit v10 on v9

--- a/solution.py
+++ b/solution.py
@@ -514,21 +514,18 @@
         return [swapped(part, count, level, k + 1) for k, part in enumerate(parts)]
 
     low = neighbour(response[:, local_cells - halo :], count, 1)
+    high = neighbour(response[:, :halo], count, -1)
 
     sent_x, sent_z, keep_x, keep_z = first_sums(response, projectors, core, block, first)
     sent_z = swapped(sent_z, count, core, 1)
     sent_x = swapped(sent_x, count, core, 1)
-    low, head = lax.optimization_barrier((low, response[:, :halo]))
-    high = neighbour(head, count, -1)
     keep_z, *parts_z = split(keep_z, [sent_z], along, 1)
     keep_x, *parts_x = split(keep_x, [sent_x], across, 0)
-    parts_x, low = lax.optimization_barrier((parts_x, low))
+    parts_z[-1], low = lax.optimization_barrier((parts_z[-1], low))
     taken_z, taken_x, low, high = lax.optimization_barrier(
         (parts_to(parts_z, along), parts_to(parts_x, across), low, high)
     )
     keep_x, *parts_x = split(keep_x, taken_x, along, 1)
-    low, head, _ = lax.optimization_barrier((low, response[:, :halo], keep_x))
-    high = neighbour(head, count, -1)
     keep_z, *parts_z = split(keep_z, taken_z, across, 0)
     taken_x, taken_z = lax.optimization_barrier(
         (parts_to(parts_x, along), parts_to(parts_z, across))

time: 94.1 us -> 86.8 us (0.922)
  waiting for transfers between devices: 52.8 us -> 36.3 us
  starting transfers between devices: 27.5 us -> 36.7 us
    ppermute x27, waiting for transfers between devices: 46.6 us -> 36.1 us  [swapped(): return lax.ppermute(array, 'band', pairs)]
    ppermute x27, starting transfers between devices: 27 us -> 33 us  [swapped(): return lax.ppermute(array, 'band', pairs)]
    ppermute x2, waiting for transfers between devices: 6.18 us -> 0.27 us  [neighbour(): lax.ppermute(array, 'band', [(i, (i + step) % count) for i in range(count)])]
    ppermute x2, starting transfers between devices: 0.56 us -> 3.62 us  [neighbour(): lax.ppermute(array, 'band', [(i, (i + step) % count) for i in range(count)])]
  transfers between devices with their start and end apart: 29 -> 29, of which waited for: 17 -> 16; matrix products, arithmetic and copies ran while one was open for 0% -> 0% of each run, Pallas kernels for 9% -> 10%
where the time goes in v10:
time: 86.8 us; the launch traced here: 86.7 us
  starting transfers between devices  36.7 us (42%)
  waiting for transfers between devices  36.3 us (42%)
  Pallas kernels  12.7 us (15%)
  between operations  0.92 us (1%)
    ppermute x27, waiting for transfers between devices, swapped(): return lax.ppermute(array, 'band', pairs)  36.1 us
    ppermute x27, starting transfers between devices, swapped(): return lax.ppermute(array, 'band', pairs)  33 us
    pallas_call x1, Pallas kernels, first_sums(): pl.pallas_call(functools.partial(first_body, core, block, tile), out_shap...  4.34 us
    ppermute x2, starting transfers between devices, neighbour(): lax.ppermute(array, 'band', [(i, (i + step) % count) for i in range(count)])  3.62 us
    pallas_call x13, Pallas kernels, local_call(): pl.pallas_call(body, out_shape=outs, in_specs=[whole() for _ in args], ou...  3.61 us
    pallas_call x1, Pallas kernels, project(): pl.pallas_call(functools.partial(project_body, core, blk), grid=(bands //...  2.48 us
    pallas_call x1, Pallas kernels, local_part(): pl.pallas_call(functools.partial(local_body, depth, (group_rows, blk)), g...  2.23 us
  transfers between devices with their start and end apart: 29, of which 16 were waited for; matrix products, arithmetic and copies ran while one was open for 0% of the time, Pallas kernels for 10%

profile of v10, /device:TPU:0, one launch (start us, length us, event | category | flops | bytes accessed | tf_op | source)
XLA Modules:
  0.0 86.7 jit_solution(6456434232190087636)
XLA Ops:
  0.6 0.5 collective-permute-start.4
  1.1 4.3 %shard_map.104 = (bf16[128,2048]{1,0:T(8,128)(2,1)S(1)}, bf16[128,2048]{1,0:T(8,128)(2,1)S(1)}, f32[128,2048]{1,0:T(8,128)S(1)}, f32[128,2048]{1,0:T(8,128)S(1)}) custom-call(bf16[512,768]{1,0:T(8,128)(2,1)} %refs_5_.5, bf16[2048,768]{1,0:T(8,128)(2,1)} %refs_3_.5), custom_call_target="tpu_custom_call" | custom-call | flops 1610612736 | bytes 6291456 | tf_op jit(solution)/shard_map/pallas_call | solution.py:147
  5.5 0.0 copy-start.7
  5.5 0.0 copy-start.8
  5.5 0.0 copy-start
  5.5 0.0 copy-start.3
  5.5 0.0 copy-start.4
  5.5 0.0 copy-start.5
  5.6 0.0 copy-start.6
  5.6 2.6 %collective-permute-start = (bf16[128,2048]{1,0:T(8,128)(2,1)S(1)}, bf16[128,2048]{1,0:T(8,128)(2,1)S(1)}, u32[]{:S(2)}, u32[]{:S(2)}) collective-permute-start(bf16[128,2048]{1,0:T(8,128)(2,1)S(1)} %get-tuple-element.61), channel_id=1, source_target_pairs={{0,1},{1,0},{2,3},{3,2},{4,5},{5,4},{6,7},{7,6},{8,9},{9,8},{10,11... | collective-permute-start | bytes 1572872 | tf_op jit(solution)/shard_map/ppermute | solution.py:59
  8.2 3.1 %collective-permute-start.7 = (bf16[512,768]{1,0:T(8,128)(2,1)S(1)}, bf16[512,768]{1,0:T(8,128)(2,1)S(1)}, u32[]{:S(2)}, u32[]{:S(2)}) collective-permute-start(bf16[512,768]{1,0:T(8,128)(2,1)S(1)} %copy-done.2), channel_id=1, source_target_pairs={{0,15},{1,0},{2,1},{3,2},{4,3},{5,4},{6,5},{7,6},{8,7},{9,8},{10,9... | collective-permute-start | bytes 2359304 | tf_op jit(solution)/shard_map/ppermute | solution.py:50
  11.3 0.0 collective-permute-start.1
  11.3 0.0 collective-permute-done.refs_1_
  11.3 0.1 shard_map.105
  11.4 0.1 collective-permute-start.6
  11.5 1.7 %collective-permute-done.1.refs_1_ = bf16[128,2048]{1,0:T(8,128)(2,1)S(1)} collective-permute-done((bf16[128,2048]{1,0:T(8,128)(2,1)S(1)}, bf16[128,2048]{1,0:T(8,128)(2,1)S(1)}, u32[]{:S(2)}, u32[]{:S(2)}) %collective-permute-start.1) | collective-permute-done | bytes 524320 | tf_op jit(solution)/shard_map/ppermute | solution.py:59
  13.2 0.1 shard_map.106
  13.3 0.1 collective-permute-start.2
  13.4 2.4 %collective-permute-start.3 = (bf16[128,512]{1,0:T(8,128)(2,1)S(1)}, bf16[128,512]{1,0:T(8,128)(2,1)S(1)}, u32[]{:S(2)}, u32[]{:S(2)}) collective-permute-start(bf16[128,512]{1,0:T(8,128)(2,1)S(1)} %get-tuple-element.66), channel_id=1, source_target_pairs={{0,8},{1,9},{2,10},{3,11},{4,12},{5,13},{6,14},{7,15},{8,0},{9,1},... | collective-permute-start | bytes 393224 | tf_op jit(solution)/shard_map/ppermute | solution.py:59
  15.8 0.3 collective-permute-done.4.refs_1_
  16.1 2.3 %collective-permute-start.5 = (bf16[128,512]{1,0:T(8,128)(2,1)S(1)}, bf16[128,512]{1,0:T(8,128)(2,1)S(1)}, u32[]{:S(2)}, u32[]{:S(2)}) collective-permute-start(bf16[128,512]{1,0:T(8,128)(2,1)S(1)} %get-tuple-element.68), channel_id=1, source_target_pairs={{0,12},{1,13},{2,14},{3,15},{4,8},{5,9},{6,10},{7,11},{8,4},{9,5},... | collective-permute-start | bytes 393224 | tf_op jit(solution)/shard_map/ppermute | solution.py:59
  18.4 8.2 %collective-permute-done.2.refs_1_ = bf16[128,512]{1,0:T(8,128)(2,1)S(1)} collective-permute-done((bf16[128,512]{1,0:T(8,128)(2,1)S(1)}, bf16[128,512]{1,0:T(8,128)(2,1)S(1)}, u32[]{:S(2)}, u32[]{:S(2)}) %collective-permute-start.2) | collective-permute-done | bytes 131104 | tf_op jit(solution)/shard_map/ppermute | solution.py:59
  26.5 5.2 %collective-permute-done.3.refs_2_ = bf16[128,512]{1,0:T(8,128)(2,1)S(1)} collective-permute-done((bf16[128,512]{1,0:T(8,128)(2,1)S(1)}, bf16[128,512]{1,0:T(8,128)(2,1)S(1)}, u32[]{:S(2)}, u32[]{:S(2)}) %collective-permute-start.3) | collective-permute-done | bytes 131104 | tf_op jit(solution)/shard_map/ppermute | solution.py:59
  31.8 0.1 shard_map.108
  31.9 0.1 collective-permute-start.11
  31.9 0.0 copy-start.1
  31.9 0.1 shard_map.107
  32.0 2.8 %collective-permute-start.10 = (bf16[64,512]{1,0:T(8,128)(2,1)S(1)}, bf16[64,512]{1,0:T(8,128)(2,1)S(1)}, u32[]{:S(2)}, u32[]{:S(2)}) collective-permute-start(bf16[64,512]{1,0:T(8,128)(2,1)S(1)} %get-tuple-element.75), channel_id=1, source_target_pairs={{0,12},{1,13},{2,14},{3,15},{4,8},{5,9},{6,10},{7,11},{8,4},{9,5},... | collective-permute-start | bytes 196616 | tf_op jit(solution)/shard_map/ppermute | solution.py:59
  34.8 1.9 %collective-permute-start.8 = (bf16[64,512]{1,0:T(8,128)(2,1)S(1)}, bf16[64,512]{1,0:T(8,128)(2,1)S(1)}, u32[]{:S(2)}, u32[]{:S(2)}) collective-permute-start(bf16[64,512]{1,0:T(8,128)(2,1)S(1)} %get-tuple-element.73), channel_id=1, source_target_pairs={{0,4},{1,5},{2,6},{3,7},{4,0},{5,1},{6,2},{7,3},{8,12},{9,13},{10,... | collective-permute-start | bytes 196616 | tf_op jit(solution)/shard_map/ppermute | solution.py:59
  36.7 1.9 %collective-permute-done.10.refs_3_ = bf16[64,512]{1,0:T(8,128)(2,1)S(1)} collective-permute-done((bf16[64,512]{1,0:T(8,128)(2,1)S(1)}, bf16[64,512]{1,0:T(8,128)(2,1)S(1)}, u32[]{:S(2)}, u32[]{:S(2)}) %collective-permute-start.10) | collective-permute-done | bytes 65568 | tf_op jit(solution)/shard_map/ppermute | solution.py:59
  38.6 0.6 collective-permute-done.8.refs_1_
  39.2 3.0 %collective-permute-done.9.refs_2_ = bf16[64,512]{1,0:T(8,128)(2,1)S(1)} collective-permute-done((bf16[64,512]{1,0:T(8,128)(2,1)S(1)}, bf16[64,512]{1,0:T(8,128)(2,1)S(1)}, u32[]{:S(2)}, u32[]{:S(2)}) %collective-permute-start.9) | collective-permute-done | bytes 65568 | tf_op jit(solution)/shard_map/ppermute | solution.py:59
  42.2 0.1 shard_map.109
  42.2 0.1 collective-permute-start.12
  42.3 2.8 %collective-permute-start.13 = (bf16[64,512]{1,0:T(8,128)(2,1)S(1)}, bf16[64,512]{1,0:T(8,128)(2,1)S(1)}, u32[]{:S(2)}, u32[]{:S(2)}) collective-permute-start(bf16[64,512]{1,0:T(8,128)(2,1)S(1)} %get-tuple-element.88.refs_0_), channel_id=1, source_target_pairs={{0,8},{1,9},{2,10},{3,11},{4,12},{5,13},{6,14},{7,15},{8,0},{9,1},... | collective-permute-start | bytes 196616 | tf_op jit(solution)/shard_map/ppermute | solution.py:59
  45.1 1.5 %collective-permute-start.14 = (bf16[64,512]{1,0:T(8,128)(2,1)S(1)}, bf16[64,512]{1,0:T(8,128)(2,1)S(1)}, u32[]{:S(2)}, u32[]{:S(2)}) collective-permute-start(bf16[64,512]{1,0:T(8,128)(2,1)S(1)} %get-tuple-element.88.refs_0_), channel_id=1, source_target_pairs={{0,12},{1,13},{2,14},{3,15},{4,8},{5,9},{6,10},{7,11},{8,4},{9,5},... | collective-permute-start | bytes 196616 | tf_op jit(solution)/shard_map/ppermute | solution.py:59
  46.7 2.0 %collective-permute-start.15 = (bf16[64,512]{1,0:T(8,128)(2,1)S(1)}, bf16[64,512]{1,0:T(8,128)(2,1)S(1)}, u32[]{:S(2)}, u32[]{:S(2)}) collective-permute-start(bf16[64,512]{1,0:T(8,128)(2,1)S(1)} %get-tuple-element.92.refs_0_), channel_id=1, source_target_pairs={{0,2},{1,3},{2,0},{3,1},{4,6},{5,7},{6,4},{7,5},{8,10},{9,11},{10,... | collective-permute-start | bytes 196616 | tf_op jit(solution)/shard_map/ppermute | solution.py:59
  48.6 0.3 collective-permute-done.13.refs_2_
  48.9 2.6 %collective-permute-done.14.refs_3_ = bf16[64,512]{1,0:T(8,128)(2,1)S(1)} collective-permute-done((bf16[64,512]{1,0:T(8,128)(2,1)S(1)}, bf16[64,512]{1,0:T(8,128)(2,1)S(1)}, u32[]{:S(2)}, u32[]{:S(2)}) %collective-permute-start.14) | collective-permute-done | bytes 65568 | tf_op jit(solution)/shard_map/ppermute | solution.py:59
  51.6 0.1 collective-permute-start.19
  51.7 2.2 %collective-permute-start.20 = (bf16[128,512]{1,0:T(8,128)(2,1)S(1)}, bf16[128,512]{1,0:T(8,128)(2,1)S(1)}, u32[]{:S(2)}, u32[]{:S(2)}) collective-permute-start(bf16[128,512]{1,0:T(8,128)(2,1)S(1)} %shard_map.111.refs_0_), channel_id=1, source_target_pairs={{0,8},{1,9},{2,10},{3,11},{4,12},{5,13},{6,14},{7,15},{8,0},{9,1},... | collective-permute-start | bytes 393224 | tf_op jit(solution)/shard_map/ppermute | solution.py:59
  53.9 2.2 %collective-permute-start.21 = (bf16[128,512]{1,0:T(8,128)(2,1)S(1)}, bf16[128,512]{1,0:T(8,128)(2,1)S(1)}, u32[]{:S(2)}, u32[]{:S(2)}) collective-permute-start(bf16[128,512]{1,0:T(8,128)(2,1)S(1)} %shard_map.111.refs_0_), channel_id=1, source_target_pairs={{0,12},{1,13},{2,14},{3,15},{4,8},{5,9},{6,10},{7,11},{8,4},{9,5},... | collective-permute-start | bytes 393224 | tf_op jit(solution)/shard_map/ppermute | solution.py:59
  56.1 2.2 %collective-permute-start.17 = (bf16[64,2048]{1,0:T(8,128)(2,1)S(1)}, bf16[64,2048]{1,0:T(8,128)(2,1)S(1)}, u32[]{:S(2)}, u32[]{:S(2)}) collective-permute-start(bf16[64,2048]{1,0:T(8,128)(2,1)S(1)} %shard_map.110.refs_0_), channel_id=1, source_target_pairs={{0,2},{1,3},{2,0},{3,1},{4,6},{5,7},{6,4},{7,5},{8,10},{9,11},{10,... | collective-permute-start | bytes 786440 | tf_op jit(solution)/shard_map/ppermute | solution.py:59
  58.3 2.2 %shard_map.112 = (f32[512,768]{1,0:T(8,128)S(1)}, bf16[512,256]{1,0:T(8,128)(2,1)S(1)}) custom-call(bf16[512,768]{1,0:T(8,128)(2,1)S(1)} %copy-done.2, bf16[512,768]{1,0:T(8,128)(2,1)S(1)} %collective-permute-done.4.refs_1_, bf16[512,768]{1,0:T(8,128)(2,1)S(1)} %collective-permute-done.7.refs_2_, bf16[512,768]{1,0:T(8,128)(2,1)S(1)} %copy-done, ...), custom_call_target="tpu_custom_call" | custom-call | flops 235929600 | bytes 4980736 | tf_op jit(solution)/shard_map/pallas_call | solution.py:298
  60.6 0.8 collective-permute-done.20.refs_2_
  61.4 0.1 shard_map.113.refs_2_
  61.5 0.1 collective-permute-start.22
  61.5 0.5 collective-permute-start.16
  62.0 0.6 collective-permute-done.17.refs_1_
  62.7 1.5 %shard_map.114 = (f32[256,768]{1,0:T(8,128)S(1)}, f32[320,128]{1,0:T(8,128)S(1)}) custom-call(bf16[64,2048]{1,0:T(8,128)(2,1)S(1)} %shard_map.110.refs_0_, bf16[64,2048]{1,0:T(8,128)(2,1)S(1)} %collective-permute-done.17.refs_1_, bf16[128,2048]{1,0:T(8,128)(2,1)S(1)} %shard_map.113.refs_2_, bf16[2048,768]{1,0:T(8,128)(2,1)S(1)} %copy-done.1, ...), custom_call_target="tpu_custom_call" | custom-call | flops 905969664 | bytes 7503872 | tf_op jit(solution)/shard_map/pallas_call | solution.py:91
  64.2 0.0 collective-permute-done.18.refs_1_
  64.2 1.5 %shard_map.115 = (f32[256,768]{1,0:T(8,128)S(1)}, bf16[320,128]{1,0:T(8,128)(2,1)S(1)}) custom-call(bf16[64,2048]{1,0:T(8,128)(2,1)S(1)} %collective-permute-done.16.refs_0_, bf16[64,2048]{1,0:T(8,128)(2,1)S(1)} %collective-permute-done.18.refs_1_, bf16[128,2048]{1,0:T(8,128)(2,1)S(1)} %collective-permute-done.22.refs_2_, bf16[2048,768]{1,0:T(8,128)(2,1)S(1)} %copy-done.1, ...), custom_call_target="tpu_custom_call" | custom-call | flops 905969664 | bytes 7421952 | tf_op jit(solution)/shard_map/pallas_call | solution.py:91
  65.7 0.6 collective-permute-start.23
  66.3 0.9 %collective-permute-done.23.refs_0_ = bf16[320,128]{1,0:T(8,128)(2,1)S(1)} collective-permute-done((bf16[320,128]{1,0:T(8,128)(2,1)S(1)}, bf16[320,128]{1,0:T(8,128)(2,1)S(1)}, u32[]{:S(2)}, u32[]{:S(2)}) %collective-permute-start.23) | collective-permute-done | bytes 81952 | tf_op jit(solution)/shard_map/ppermute | solution.py:59
  67.3 2.1 %collective-permute-start.24 = (bf16[320,128]{1,0:T(8,128)(2,1)S(1)}, bf16[320,128]{1,0:T(8,128)(2,1)S(1)}, u32[]{:S(2)}, u32[]{:S(2)}) collective-permute-start(bf16[320,128]{1,0:T(8,128)(2,1)S(1)} %get-tuple-element.112), channel_id=1, source_target_pairs={{0,2},{1,3},{2,0},{3,1},{4,6},{5,7},{6,4},{7,5},{8,10},{9,11},{10,... | collective-permute-start | bytes 245768 | tf_op jit(solution)/shard_map/ppermute | solution.py:59
  69.4 3.0 %collective-permute-done.24.refs_0_ = bf16[320,128]{1,0:T(8,128)(2,1)S(1)} collective-permute-done((bf16[320,128]{1,0:T(8,128)(2,1)S(1)}, bf16[320,128]{1,0:T(8,128)(2,1)S(1)}, u32[]{:S(2)}, u32[]{:S(2)}) %collective-permute-start.24) | collective-permute-done | bytes 81952 | tf_op jit(solution)/shard_map/ppermute | solution.py:59
  72.3 1.6 %collective-permute-start.25 = (bf16[320,128]{1,0:T(8,128)(2,1)S(1)}, bf16[320,128]{1,0:T(8,128)(2,1)S(1)}, u32[]{:S(2)}, u32[]{:S(2)}) collective-permute-start(bf16[320,128]{1,0:T(8,128)(2,1)S(1)} %get-tuple-element.114), channel_id=1, source_target_pairs={{0,4},{1,5},{2,6},{3,7},{4,0},{5,1},{6,2},{7,3},{8,12},{9,13},{10,... | collective-permute-start | bytes 245768 | tf_op jit(solution)/shard_map/ppermute | solution.py:59
  73.9 0.5 collective-permute-start.26
  74.4 2.4 %collective-permute-start.27 = (bf16[320,128]{1,0:T(8,128)(2,1)S(1)}, bf16[320,128]{1,0:T(8,128)(2,1)S(1)}, u32[]{:S(2)}, u32[]{:S(2)}) collective-permute-start(bf16[320,128]{1,0:T(8,128)(2,1)S(1)} %get-tuple-element.114), channel_id=1, source_target_pairs={{0,12},{1,13},{2,14},{3,15},{4,8},{5,9},{6,10},{7,11},{8,4},{9,5},... | collective-permute-start | bytes 245768 | tf_op jit(solution)/shard_map/ppermute | solution.py:59
  76.8 0.4 collective-permute-done.25.refs_0_
  77.1 5.6 %collective-permute-done.26.refs_1_ = bf16[320,128]{1,0:T(8,128)(2,1)S(1)} collective-permute-done((bf16[320,128]{1,0:T(8,128)(2,1)S(1)}, bf16[320,128]{1,0:T(8,128)(2,1)S(1)}, u32[]{:S(2)}, u32[]{:S(2)}) %collective-permute-start.26) | collective-permute-done | bytes 81952 | tf_op jit(solution)/shard_map/ppermute | solution.py:59
  82.8 0.1 collective-permute-start.28
  82.9 1.3 %collective-permute-done.28.refs_1_ = bf16[320,128]{1,0:T(8,128)(2,1)S(1)} collective-permute-done((bf16[320,128]{1,0:T(8,128)(2,1)S(1)}, bf16[320,128]{1,0:T(8,128)(2,1)S(1)}, u32[]{:S(2)}, u32[]{:S(2)}) %collective-permute-start.28) | collective-permute-done | bytes 81952 | tf_op jit(solution)/shard_map/ppermute | solution.py:59
  84.2 2.5 %shard_map.119 = (bf16[512,768]{1,0:T(8,128)(2,1)}, bf16[512,768]{1,0:T(8,128)(2,1)}) custom-call(bf16[320,128]{1,0:T(8,128)(2,1)S(1)} %shard_map.118.refs_0_, bf16[320,128]{1,0:T(8,128)(2,1)S(1)} %collective-permute-done.28.refs_1_, f32[256,768]{1,0:T(8,128)S(1)} %get-tuple-element.115.refs_2_, f32[256,768]{1,0:T(8,128)S(1)} %get-tuple-element.116.refs_3_, ...), custom_call_target="tpu_custom_call" | custom-call | flops 201326592 | bytes 4718592 | tf_op jit(solution)/shard_map/pallas_call | solution.py:467
  (30 shorter events, 0.2 us)
Async XLA Ops:
  0.6 7.6 %copy-start.2 = (bf16[512,768]{1,0:T(8,128)(2,1)S(1)}, bf16[512,768]{1,0:T(8,128)(2,1)}, u32[]{:S(2)}) copy-start(bf16[512,768]{1,0:T(8,128)(2,1)} %refs_5_.5) | copy-start | bytes 2359300
  0.6 15.5 %collective-permute-start.4 = (bf16[512,768]{1,0:T(8,128)(2,1)}, bf16[512,768]{1,0:T(8,128)(2,1)S(1)}, u32[]{:S(2)}, u32[]{:S(2)}) collective-permute-start(bf16[512,768]{1,0:T(8,128)(2,1)} %refs_5_.5), channel_id=1, source_target_pairs={{0,1},{1,2},{2,3},{3,4},{4,5},{5,6},{6,7},{7,8},{8,9},{9,10},{10,1... | collective-permute-start | bytes 2359304 | tf_op jit(solution)/shard_map/ppermute | solution.py:50
  5.5 50.6 %copy-start.7 = (f32[768]{0:T(1024)S(1)}, f32[768]{0:T(1024)}, u32[]{:S(2)}) copy-start(f32[768]{0:T(1024)} %param.12) | copy-start | bytes 9220
  5.5 50.5 %copy-start.8 = (f32[768]{0:T(1024)S(1)}, f32[768]{0:T(1024)}, u32[]{:S(2)}) copy-start(f32[768]{0:T(1024)} %param.13) | copy-start | bytes 9220
  5.5 52.8 %copy-start = (bf16[512,768]{1,0:T(8,128)(2,1)S(1)}, bf16[512,768]{1,0:T(8,128)(2,1)}, u32[]{:S(2)}) copy-start(bf16[512,768]{1,0:T(8,128)(2,1)} %refs_4_.2) | copy-start | bytes 2359300
  5.5 52.8 %copy-start.3 = (bf16[2,128,128]{2,1,0:T(8,128)(2,1)S(1)}, bf16[2,128,128]{2,1,0:T(8,128)(2,1)}, u32[]{:S(2)}) copy-start(bf16[2,128,128]{2,1,0:T(8,128)(2,1)} %constant.2.clone.refs_4_) | copy-start | bytes 196612
  5.5 52.8 %copy-start.4 = (f32[512]{0:T(512)S(1)}, f32[512]{0:T(512)}, u32[]{:S(2)}) copy-start(f32[512]{0:T(512)} %param.14) | copy-start | bytes 6148
  5.5 52.8 %copy-start.5 = (s32[512]{0:T(512)S(1)}, s32[512]{0:T(512)}, u32[]{:S(2)}) copy-start(s32[512]{0:T(512)} %param.15) | copy-start | bytes 6148
  5.6 52.8 %copy-start.6 = (s32[512]{0:T(512)S(1)}, s32[512]{0:T(512)}, u32[]{:S(2)}) copy-start(s32[512]{0:T(512)} %param.16) | copy-start | bytes 6148
  5.6 5.8 %collective-permute-start = (bf16[128,2048]{1,0:T(8,128)(2,1)S(1)}, bf16[128,2048]{1,0:T(8,128)(2,1)S(1)}, u32[]{:S(2)}, u32[]{:S(2)}) collective-permute-start(bf16[128,2048]{1,0:T(8,128)(2,1)S(1)} %get-tuple-element.61), channel_id=1, source_target_pairs={{0,1},{1,0},{2,3},{3,2},{4,5},{5,4},{6,7},{7,6},{8,9},{9,8},{10,11... | collective-permute-start | bytes 1572872 | tf_op jit(solution)/shard_map/ppermute | solution.py:59
  8.2 23.5 %collective-permute-start.7 = (bf16[512,768]{1,0:T(8,128)(2,1)S(1)}, bf16[512,768]{1,0:T(8,128)(2,1)S(1)}, u32[]{:S(2)}, u32[]{:S(2)}) collective-permute-start(bf16[512,768]{1,0:T(8,128)(2,1)S(1)} %copy-done.2), channel_id=1, source_target_pairs={{0,15},{1,0},{2,1},{3,2},{4,3},{5,4},{6,5},{7,6},{8,7},{9,8},{10,9... | collective-permute-start | bytes 2359304 | tf_op jit(solution)/shard_map/ppermute | solution.py:50
  11.3 1.9 %collective-permute-start.1 = (bf16[128,2048]{1,0:T(8,128)(2,1)S(1)}, bf16[128,2048]{1,0:T(8,128)(2,1)S(1)}, u32[]{:S(2)}, u32[]{:S(2)}) collective-permute-start(bf16[128,2048]{1,0:T(8,128)(2,1)S(1)} %get-tuple-element.64), channel_id=1, source_target_pairs={{0,1},{1,0},{2,3},{3,2},{4,5},{5,4},{6,7},{7,6},{8,9},{9,8},{10,11... | collective-permute-start | bytes 1572872 | tf_op jit(solution)/shard_map/ppermute | solution.py:59
  11.4 20.3 %collective-permute-start.6 = (bf16[64,2048]{1,0:T(8,128)(2,1)S(1)}, bf16[64,2048]{1,0:T(8,128)(2,1)S(1)}, u32[]{:S(2)}, u32[]{:S(2)}) collective-permute-start(bf16[64,2048]{1,0:T(8,128)(2,1)S(1)} %get-tuple-element.69), channel_id=1, source_target_pairs={{0,2},{1,3},{2,0},{3,1},{4,6},{5,7},{6,4},{7,5},{8,10},{9,11},{10,... | collective-permute-start | bytes 786440 | tf_op jit(solution)/shard_map/ppermute | solution.py:59
  13.3 13.2 %collective-permute-start.2 = (bf16[128,512]{1,0:T(8,128)(2,1)S(1)}, bf16[128,512]{1,0:T(8,128)(2,1)S(1)}, u32[]{:S(2)}, u32[]{:S(2)}) collective-permute-start(bf16[128,512]{1,0:T(8,128)(2,1)S(1)} %get-tuple-element.65), channel_id=1, source_target_pairs={{0,4},{1,5},{2,6},{3,7},{4,0},{5,1},{6,2},{7,3},{8,12},{9,13},{10,... | collective-permute-start | bytes 393224 | tf_op jit(solution)/shard_map/ppermute | solution.py:59
  13.4 18.3 %collective-permute-start.3 = (bf16[128,512]{1,0:T(8,128)(2,1)S(1)}, bf16[128,512]{1,0:T(8,128)(2,1)S(1)}, u32[]{:S(2)}, u32[]{:S(2)}) collective-permute-start(bf16[128,512]{1,0:T(8,128)(2,1)S(1)} %get-tuple-element.66), channel_id=1, source_target_pairs={{0,8},{1,9},{2,10},{3,11},{4,12},{5,13},{6,14},{7,15},{8,0},{9,1},... | collective-permute-start | bytes 393224 | tf_op jit(solution)/shard_map/ppermute | solution.py:59
  16.1 15.7 %collective-permute-start.5 = (bf16[128,512]{1,0:T(8,128)(2,1)S(1)}, bf16[128,512]{1,0:T(8,128)(2,1)S(1)}, u32[]{:S(2)}, u32[]{:S(2)}) collective-permute-start(bf16[128,512]{1,0:T(8,128)(2,1)S(1)} %get-tuple-element.68), channel_id=1, source_target_pairs={{0,12},{1,13},{2,14},{3,15},{4,8},{5,9},{6,10},{7,11},{8,4},{9,5},... | collective-permute-start | bytes 393224 | tf_op jit(solution)/shard_map/ppermute | solution.py:59
  31.9 4.9 %collective-permute-start.11 = (bf16[64,512]{1,0:T(8,128)(2,1)S(1)}, bf16[64,512]{1,0:T(8,128)(2,1)S(1)}, u32[]{:S(2)}, u32[]{:S(2)}) collective-permute-start(bf16[64,512]{1,0:T(8,128)(2,1)S(1)} %get-tuple-element.80), channel_id=1, source_target_pairs={{0,2},{1,3},{2,0},{3,1},{4,6},{5,7},{6,4},{7,5},{8,10},{9,11},{10,... | collective-permute-start | bytes 196616 | tf_op jit(solution)/shard_map/ppermute | solution.py:59
  31.9 30.7 %copy-start.1 = (bf16[2048,768]{1,0:T(8,128)(2,1)S(1)}, bf16[2048,768]{1,0:T(8,128)(2,1)}, u32[]{:S(2)}) copy-start(bf16[2048,768]{1,0:T(8,128)(2,1)} %refs_3_.5) | copy-start | bytes 9437188
  32.0 6.6 %collective-permute-start.10 = (bf16[64,512]{1,0:T(8,128)(2,1)S(1)}, bf16[64,512]{1,0:T(8,128)(2,1)S(1)}, u32[]{:S(2)}, u32[]{:S(2)}) collective-permute-start(bf16[64,512]{1,0:T(8,128)(2,1)S(1)} %get-tuple-element.75), channel_id=1, source_target_pairs={{0,12},{1,13},{2,14},{3,15},{4,8},{5,9},{6,10},{7,11},{8,4},{9,5},... | collective-permute-start | bytes 196616 | tf_op jit(solution)/shard_map/ppermute | solution.py:59
  34.8 4.4 %collective-permute-start.8 = (bf16[64,512]{1,0:T(8,128)(2,1)S(1)}, bf16[64,512]{1,0:T(8,128)(2,1)S(1)}, u32[]{:S(2)}, u32[]{:S(2)}) collective-permute-start(bf16[64,512]{1,0:T(8,128)(2,1)S(1)} %get-tuple-element.73), channel_id=1, source_target_pairs={{0,4},{1,5},{2,6},{3,7},{4,0},{5,1},{6,2},{7,3},{8,12},{9,13},{10,... | collective-permute-start | bytes 196616 | tf_op jit(solution)/shard_map/ppermute | solution.py:59
  36.7 5.5 %collective-permute-start.9 = (bf16[64,512]{1,0:T(8,128)(2,1)S(1)}, bf16[64,512]{1,0:T(8,128)(2,1)S(1)}, u32[]{:S(2)}, u32[]{:S(2)}) collective-permute-start(bf16[64,512]{1,0:T(8,128)(2,1)S(1)} %get-tuple-element.74), channel_id=1, source_target_pairs={{0,8},{1,9},{2,10},{3,11},{4,12},{5,13},{6,14},{7,15},{8,0},{9,1},... | collective-permute-start | bytes 196616 | tf_op jit(solution)/shard_map/ppermute | solution.py:59
  42.2 6.4 %collective-permute-start.12 = (bf16[64,512]{1,0:T(8,128)(2,1)S(1)}, bf16[64,512]{1,0:T(8,128)(2,1)S(1)}, u32[]{:S(2)}, u32[]{:S(2)}) collective-permute-start(bf16[64,512]{1,0:T(8,128)(2,1)S(1)} %get-tuple-element.88.refs_0_), channel_id=1, source_target_pairs={{0,4},{1,5},{2,6},{3,7},{4,0},{5,1},{6,2},{7,3},{8,12},{9,13},{10,... | collective-permute-start | bytes 196616 | tf_op jit(solution)/shard_map/ppermute | solution.py:59
  42.3 6.6 %collective-permute-start.13 = (bf16[64,512]{1,0:T(8,128)(2,1)S(1)}, bf16[64,512]{1,0:T(8,128)(2,1)S(1)}, u32[]{:S(2)}, u32[]{:S(2)}) collective-permute-start(bf16[64,512]{1,0:T(8,128)(2,1)S(1)} %get-tuple-element.88.refs_0_), channel_id=1, source_target_pairs={{0,8},{1,9},{2,10},{3,11},{4,12},{5,13},{6,14},{7,15},{8,0},{9,1},... | collective-permute-start | bytes 196616 | tf_op jit(solution)/shard_map/ppermute | solution.py:59
  45.1 6.4 %collective-permute-start.14 = (bf16[64,512]{1,0:T(8,128)(2,1)S(1)}, bf16[64,512]{1,0:T(8,128)(2,1)S(1)}, u32[]{:S(2)}, u32[]{:S(2)}) collective-permute-start(bf16[64,512]{1,0:T(8,128)(2,1)S(1)} %get-tuple-element.88.refs_0_), channel_id=1, source_target_pairs={{0,12},{1,13},{2,14},{3,15},{4,8},{5,9},{6,10},{7,11},{8,4},{9,5},... | collective-permute-start | bytes 196616 | tf_op jit(solution)/shard_map/ppermute | solution.py:59
  46.7 4.9 %collective-permute-start.15 = (bf16[64,512]{1,0:T(8,128)(2,1)S(1)}, bf16[64,512]{1,0:T(8,128)(2,1)S(1)}, u32[]{:S(2)}, u32[]{:S(2)}) collective-permute-start(bf16[64,512]{1,0:T(8,128)(2,1)S(1)} %get-tuple-element.92.refs_0_), channel_id=1, source_target_pairs={{0,2},{1,3},{2,0},{3,1},{4,6},{5,7},{6,4},{7,5},{8,10},{9,11},{10,... | collective-permute-start | bytes 196616 | tf_op jit(solution)/shard_map/ppermute | solution.py:59
  51.6 9.0 %collective-permute-start.19 = (bf16[128,512]{1,0:T(8,128)(2,1)S(1)}, bf16[128,512]{1,0:T(8,128)(2,1)S(1)}, u32[]{:S(2)}, u32[]{:S(2)}) collective-permute-start(bf16[128,512]{1,0:T(8,128)(2,1)S(1)} %shard_map.111.refs_0_), channel_id=1, source_target_pairs={{0,4},{1,5},{2,6},{3,7},{4,0},{5,1},{6,2},{7,3},{8,12},{9,13},{10,... | collective-permute-start | bytes 393224 | tf_op jit(solution)/shard_map/ppermute | solution.py:59
  51.7 9.7 %collective-permute-start.20 = (bf16[128,512]{1,0:T(8,128)(2,1)S(1)}, bf16[128,512]{1,0:T(8,128)(2,1)S(1)}, u32[]{:S(2)}, u32[]{:S(2)}) collective-permute-start(bf16[128,512]{1,0:T(8,128)(2,1)S(1)} %shard_map.111.refs_0_), channel_id=1, source_target_pairs={{0,8},{1,9},{2,10},{3,11},{4,12},{5,13},{6,14},{7,15},{8,0},{9,1},... | collective-permute-start | bytes 393224 | tf_op jit(solution)/shard_map/ppermute | solution.py:59
  53.9 7.5 %collective-permute-start.21 = (bf16[128,512]{1,0:T(8,128)(2,1)S(1)}, bf16[128,512]{1,0:T(8,128)(2,1)S(1)}, u32[]{:S(2)}, u32[]{:S(2)}) collective-permute-start(bf16[128,512]{1,0:T(8,128)(2,1)S(1)} %shard_map.111.refs_0_), channel_id=1, source_target_pairs={{0,12},{1,13},{2,14},{3,15},{4,8},{5,9},{6,10},{7,11},{8,4},{9,5},... | collective-permute-start | bytes 393224 | tf_op jit(solution)/shard_map/ppermute | solution.py:59
  56.1 6.6 %collective-permute-start.17 = (bf16[64,2048]{1,0:T(8,128)(2,1)S(1)}, bf16[64,2048]{1,0:T(8,128)(2,1)S(1)}, u32[]{:S(2)}, u32[]{:S(2)}) collective-permute-start(bf16[64,2048]{1,0:T(8,128)(2,1)S(1)} %shard_map.110.refs_0_), channel_id=1, source_target_pairs={{0,2},{1,3},{2,0},{3,1},{4,6},{5,7},{6,4},{7,5},{8,10},{9,11},{10,... | collective-permute-start | bytes 786440 | tf_op jit(solution)/shard_map/ppermute | solution.py:59
  61.5 2.7 %collective-permute-start.22 = (bf16[128,2048]{1,0:T(8,128)(2,1)S(1)}, bf16[128,2048]{1,0:T(8,128)(2,1)S(1)}, u32[]{:S(2)}, u32[]{:S(2)}) collective-permute-start(bf16[128,2048]{1,0:T(8,128)(2,1)S(1)} %shard_map.113.refs_2_), channel_id=1, source_target_pairs={{0,1},{1,0},{2,3},{3,2},{4,5},{5,4},{6,7},{7,6},{8,9},{9,8},{10,11... | collective-permute-start | bytes 1572872 | tf_op jit(solution)/shard_map/ppermute | solution.py:59
  61.5 2.6 %collective-permute-start.16 = (bf16[64,2048]{1,0:T(8,128)(2,1)S(1)}, bf16[64,2048]{1,0:T(8,128)(2,1)S(1)}, u32[]{:S(2)}, u32[]{:S(2)}) collective-permute-start(bf16[64,2048]{1,0:T(8,128)(2,1)S(1)} %shard_map.110.refs_0_), channel_id=1, source_target_pairs={{0,1},{1,0},{2,3},{3,2},{4,5},{5,4},{6,7},{7,6},{8,9},{9,8},{10,11... | collective-permute-start | bytes 786440 | tf_op jit(solution)/shard_map/ppermute | solution.py:59
  62.7 1.5 %collective-permute-start.18 = (bf16[64,2048]{1,0:T(8,128)(2,1)S(1)}, bf16[64,2048]{1,0:T(8,128)(2,1)S(1)}, u32[]{:S(2)}, u32[]{:S(2)}) collective-permute-start(bf16[64,2048]{1,0:T(8,128)(2,1)S(1)} %collective-permute-done.17.refs_1_), channel_id=1, source_target_pairs={{0,1},{1,0},{2,3},{3,2},{4,5},{5,4},{6,7},{7,6},{8,9},{9,8},{10,11... | collective-permute-start | bytes 786440 | tf_op jit(solution)/shard_map/ppermute | solution.py:59
  65.7 1.5 %collective-permute-start.23 = (bf16[320,128]{1,0:T(8,128)(2,1)S(1)}, bf16[320,128]{1,0:T(8,128)(2,1)S(1)}, u32[]{:S(2)}, u32[]{:S(2)}) collective-permute-start(bf16[320,128]{1,0:T(8,128)(2,1)S(1)} %get-tuple-element.110), channel_id=1, source_target_pairs={{0,1},{1,0},{2,3},{3,2},{4,5},{5,4},{6,7},{7,6},{8,9},{9,8},{10,11... | collective-permute-start | bytes 245768 | tf_op jit(solution)/shard_map/ppermute | solution.py:59
  67.3 5.0 %collective-permute-start.24 = (bf16[320,128]{1,0:T(8,128)(2,1)S(1)}, bf16[320,128]{1,0:T(8,128)(2,1)S(1)}, u32[]{:S(2)}, u32[]{:S(2)}) collective-permute-start(bf16[320,128]{1,0:T(8,128)(2,1)S(1)} %get-tuple-element.112), channel_id=1, source_target_pairs={{0,2},{1,3},{2,0},{3,1},{4,6},{5,7},{6,4},{7,5},{8,10},{9,11},{10,... | collective-permute-start | bytes 245768 | tf_op jit(solution)/shard_map/ppermute | solution.py:59
  72.3 4.8 %collective-permute-start.25 = (bf16[320,128]{1,0:T(8,128)(2,1)S(1)}, bf16[320,128]{1,0:T(8,128)(2,1)S(1)}, u32[]{:S(2)}, u32[]{:S(2)}) collective-permute-start(bf16[320,128]{1,0:T(8,128)(2,1)S(1)} %get-tuple-element.114), channel_id=1, source_target_pairs={{0,4},{1,5},{2,6},{3,7},{4,0},{5,1},{6,2},{7,3},{8,12},{9,13},{10,... | collective-permute-start | bytes 245768 | tf_op jit(solution)/shard_map/ppermute | solution.py:59
  73.9 8.9 %collective-permute-start.26 = (bf16[320,128]{1,0:T(8,128)(2,1)S(1)}, bf16[320,128]{1,0:T(8,128)(2,1)S(1)}, u32[]{:S(2)}, u32[]{:S(2)}) collective-permute-start(bf16[320,128]{1,0:T(8,128)(2,1)S(1)} %get-tuple-element.114), channel_id=1, source_target_pairs={{0,8},{1,9},{2,10},{3,11},{4,12},{5,13},{6,14},{7,15},{8,0},{9,1},... | collective-permute-start | bytes 245768 | tf_op jit(solution)/shard_map/ppermute | solution.py:59
  74.4 8.4 %collective-permute-start.27 = (bf16[320,128]{1,0:T(8,128)(2,1)S(1)}, bf16[320,128]{1,0:T(8,128)(2,1)S(1)}, u32[]{:S(2)}, u32[]{:S(2)}) collective-permute-start(bf16[320,128]{1,0:T(8,128)(2,1)S(1)} %get-tuple-element.114), channel_id=1, source_target_pairs={{0,12},{1,13},{2,14},{3,15},{4,8},{5,9},{6,10},{7,11},{8,4},{9,5},... | collective-permute-start | bytes 245768 | tf_op jit(solution)/shard_map/ppermute | solution.py:59
  82.8 1.3 %collective-permute-start.28 = (bf16[320,128]{1,0:T(8,128)(2,1)S(1)}, bf16[320,128]{1,0:T(8,128)(2,1)S(1)}, u32[]{:S(2)}, u32[]{:S(2)}) collective-permute-start(bf16[320,128]{1,0:T(8,128)(2,1)S(1)} %shard_map.118.refs_0_), channel_id=1, source_target_pairs={{0,1},{1,0},{2,3},{3,2},{4,5},{5,4},{6,7},{7,6},{8,9},{9,8},{10,11... | collective-permute-start | bytes 245768 | tf_op jit(solution)/shard_map/ppermute | solution.py:59

commit v11 on v10

--- a/solution.py
+++ b/solution.py
@@ -28,8 +28,7 @@
 STEP_SIZE = 0.3
 MIB = 1024 * 1024
 VMEM_BYTES = 24 * MIB
-REDUCE_SHARE = 0.5
-GATHER_SHARE = 0.5
+FIRST_SHARE = 0.5
 BF16 = jnp.bfloat16
 F32 = jnp.float32
 NT = (((1,), (1,)), ((), ()))
@@ -214,20 +213,6 @@
     return local_call(
         functools.partial(finish_body, scale), struct(keep.shape, BF16), [keep, *taken]
     )
-
-
-def finish_both_body(scale, received, *refs):
-    outs = refs[-2:]
-    cut = outs[0].shape[0]
-    row = 0
-    for keep_ref, *taken in (refs[: 1 + received], refs[1 + received : -2]):
-        low = (total_of(keep_ref, taken, ...) * scale).astype(BF16)
-        end = row + keep_ref.shape[0]
-        for out, first, last in ((outs[0], 0, cut), (outs[1], cut, cut + outs[1].shape[0])):
-            top, bottom = max(row, first), min(end, last)
-            if top < bottom:
-                out[top - first : bottom - first, :] = low[top - row : bottom - row, :]
-        row = end
 
 
 def place_body(level, along, *refs):
@@ -501,8 +486,7 @@
     width = 2 * group_rows
     half = bands // 2
     block = half // across[0]
-    first = max(16, round(REDUCE_SHARE * block / 16) * 16)
-    gather_first = max(16, round(GATHER_SHARE * block / 16) * 16)
+    first = max(16, round(FIRST_SHARE * block / 16) * 16)
     matrix = jnp.asarray(plane_matrix())
     lines = (potential[None, :], perturbing[None, :])
     bounds = tuple(a[None, :] for a in (energies, window_start, block_count))
@@ -527,26 +511,15 @@
     )
     keep_x, *parts_x = split(keep_x, taken_x, along, 1)
     keep_z, *parts_z = split(keep_z, taken_z, across, 0)
-    taken_x, taken_z = lax.optimization_barrier(
-        (parts_to(parts_x, along), parts_to(parts_z, across))
-    )
-    share_x, share_z = local_call(
-        functools.partial(finish_both_body, ace_scale, len(taken_x)),
-        [
-            struct((gather_first, projections // along[0]), BF16),
-            struct((block - gather_first, projections // along[0]), BF16),
-        ],
-        [keep_x, *taken_x, keep_z, *taken_z],
-    )
-
-    pieces_x, pieces_z, bounds = lax.optimization_barrier(
-        ([share_x, *to(share_x, along)], [share_z, *to(share_z, across)], bounds)
-    )
+    share_z = finish(keep_z, parts_to(parts_z, across), ace_scale)
+    share_x = finish(keep_x, parts_to(parts_x, along), ace_scale)
+
+    block_z = place([share_z, *to(share_z, across)], across, 0)
+    pieces_x, bounds = lax.optimization_barrier(([share_x, *to(share_x, along)], bounds))
     base, mask = local_part(
         response, low, high, orbitals, matrix, lines, bounds, group_rows, width, blk
     )
     block_x = place(pieces_x, along, 1)
-    block_z = place(pieces_z, across, 0)
     blocks_x = [block_x, *to(block_x, across)]
     pieces_z, base = lax.optimization_barrier(([block_z, *to(block_z, along)], base))
     blocks = [*blocks_x, place(pieces_z, along, 1)]

time: 86.8 us -> 92.1 us (1.061)
  waiting for transfers between devices: 36.3 us -> 42.7 us
  starting transfers between devices: 36.7 us -> 35.6 us
    ppermute x27, waiting for transfers between devices: 36.1 us -> 42.4 us  [swapped(): return lax.ppermute(array, 'band', pairs)]
    ppermute x27, starting transfers between devices: 33 us -> 32 us  [swapped(): return lax.ppermute(array, 'band', pairs)]
    pallas_call x13 -> x14, Pallas kernels: 3.61 us -> 3.62 us  [local_call(): pl.pallas_call(body, out_shape=outs, in_specs=[whole() for _ in args], ou...]
  transfers between devices with their start and end apart: 29 -> 29, of which waited for: 16 -> 13; matrix products, arithmetic and copies ran while one was open for 0% -> 0% of each run, Pallas kernels for 10% -> 9%
where the time goes in v11:
time: 92.1 us; the launch traced here: 92 us
  waiting for transfers between devices  42.7 us (46%)
  starting transfers between devices  35.6 us (39%)
  Pallas kernels  12.7 us (14%)
  between operations  0.94 us (1%)
    ppermute x27, waiting for transfers between devices, swapped(): return lax.ppermute(array, 'band', pairs)  42.4 us
    ppermute x27, starting transfers between devices, swapped(): return lax.ppermute(array, 'band', pairs)  32 us
    pallas_call x1, Pallas kernels, first_sums(): pl.pallas_call(functools.partial(first_body, core, block, tile), out_shap...  4.34 us
    pallas_call x14, Pallas kernels, local_call(): pl.pallas_call(body, out_shape=outs, in_specs=[whole() for _ in args], ou...  3.62 us
    ppermute x2, starting transfers between devices, neighbour(): lax.ppermute(array, 'band', [(i, (i + step) % count) for i in range(count)])  3.62 us
    pallas_call x1, Pallas kernels, project(): pl.pallas_call(functools.partial(project_body, core, blk), grid=(bands //...  2.48 us
    pallas_call x1, Pallas kernels, local_part(): pl.pallas_call(functools.partial(local_body, depth, (group_rows, blk)), g...  2.23 us
  transfers between devices with their start and end apart: 29, of which 13 were waited for; matrix products, arithmetic and copies ran while one was open for 0% of the time, Pallas kernels for 9%

profile of v11, /device:TPU:0, one launch (start us, length us, event | category | flops | bytes accessed | tf_op | source)
XLA Modules:
  0.0 92.0 jit_solution(7106356911780940803)
XLA Ops:
  0.6 0.5 collective-permute-start.4
  1.1 4.3 %shard_map.104 = (bf16[128,2048]{1,0:T(8,128)(2,1)S(1)}, bf16[128,2048]{1,0:T(8,128)(2,1)S(1)}, f32[128,2048]{1,0:T(8,128)S(1)}, f32[128,2048]{1,0:T(8,128)S(1)}) custom-call(bf16[512,768]{1,0:T(8,128)(2,1)} %refs_5_.5, bf16[2048,768]{1,0:T(8,128)(2,1)} %refs_3_.5), custom_call_target="tpu_custom_call" | custom-call | flops 1610612736 | bytes 6291456 | tf_op jit(solution)/shard_map/pallas_call | solution.py:146
  5.5 0.0 copy-start.7
  5.5 0.0 copy-start.8
  5.5 0.0 copy-start
  5.5 0.0 copy-start.3
  5.5 0.0 copy-start.4
  5.5 0.0 copy-start.5
  5.6 0.0 copy-start.6
  5.6 2.6 %collective-permute-start = (bf16[128,2048]{1,0:T(8,128)(2,1)S(1)}, bf16[128,2048]{1,0:T(8,128)(2,1)S(1)}, u32[]{:S(2)}, u32[]{:S(2)}) collective-permute-start(bf16[128,2048]{1,0:T(8,128)(2,1)S(1)} %get-tuple-element.53), channel_id=1, source_target_pairs={{0,1},{1,0},{2,3},{3,2},{4,5},{5,4},{6,7},{7,6},{8,9},{9,8},{10,11... | collective-permute-start | bytes 1572872 | tf_op jit(solution)/shard_map/ppermute | solution.py:58
  8.2 3.1 %collective-permute-start.7 = (bf16[512,768]{1,0:T(8,128)(2,1)S(1)}, bf16[512,768]{1,0:T(8,128)(2,1)S(1)}, u32[]{:S(2)}, u32[]{:S(2)}) collective-permute-start(bf16[512,768]{1,0:T(8,128)(2,1)S(1)} %copy-done.2), channel_id=1, source_target_pairs={{0,15},{1,0},{2,1},{3,2},{4,3},{5,4},{6,5},{7,6},{8,7},{9,8},{10,9... | collective-permute-start | bytes 2359304 | tf_op jit(solution)/shard_map/ppermute | solution.py:49
  11.3 0.0 collective-permute-start.1
  11.3 0.0 collective-permute-done.refs_1_
  11.3 0.1 shard_map.105
  11.4 0.1 collective-permute-start.6
  11.5 1.7 %collective-permute-done.1.refs_1_ = bf16[128,2048]{1,0:T(8,128)(2,1)S(1)} collective-permute-done((bf16[128,2048]{1,0:T(8,128)(2,1)S(1)}, bf16[128,2048]{1,0:T(8,128)(2,1)S(1)}, u32[]{:S(2)}, u32[]{:S(2)}) %collective-permute-start.1) | collective-permute-done | bytes 524320 | tf_op jit(solution)/shard_map/ppermute | solution.py:58
  13.2 0.1 shard_map.106
  13.3 0.1 collective-permute-start.2
  13.4 2.4 %collective-permute-start.3 = (bf16[128,512]{1,0:T(8,128)(2,1)S(1)}, bf16[128,512]{1,0:T(8,128)(2,1)S(1)}, u32[]{:S(2)}, u32[]{:S(2)}) collective-permute-start(bf16[128,512]{1,0:T(8,128)(2,1)S(1)} %get-tuple-element.58), channel_id=1, source_target_pairs={{0,8},{1,9},{2,10},{3,11},{4,12},{5,13},{6,14},{7,15},{8,0},{9,1},... | collective-permute-start | bytes 393224 | tf_op jit(solution)/shard_map/ppermute | solution.py:58
  15.8 0.3 collective-permute-done.4.refs_1_
  16.1 2.3 %collective-permute-start.5 = (bf16[128,512]{1,0:T(8,128)(2,1)S(1)}, bf16[128,512]{1,0:T(8,128)(2,1)S(1)}, u32[]{:S(2)}, u32[]{:S(2)}) collective-permute-start(bf16[128,512]{1,0:T(8,128)(2,1)S(1)} %get-tuple-element.60), channel_id=1, source_target_pairs={{0,12},{1,13},{2,14},{3,15},{4,8},{5,9},{6,10},{7,11},{8,4},{9,5},... | collective-permute-start | bytes 393224 | tf_op jit(solution)/shard_map/ppermute | solution.py:58
  18.4 8.2 %collective-permute-done.2.refs_1_ = bf16[128,512]{1,0:T(8,128)(2,1)S(1)} collective-permute-done((bf16[128,512]{1,0:T(8,128)(2,1)S(1)}, bf16[128,512]{1,0:T(8,128)(2,1)S(1)}, u32[]{:S(2)}, u32[]{:S(2)}) %collective-permute-start.2) | collective-permute-done | bytes 131104 | tf_op jit(solution)/shard_map/ppermute | solution.py:58
  26.5 5.2 %collective-permute-done.3.refs_2_ = bf16[128,512]{1,0:T(8,128)(2,1)S(1)} collective-permute-done((bf16[128,512]{1,0:T(8,128)(2,1)S(1)}, bf16[128,512]{1,0:T(8,128)(2,1)S(1)}, u32[]{:S(2)}, u32[]{:S(2)}) %collective-permute-start.3) | collective-permute-done | bytes 131104 | tf_op jit(solution)/shard_map/ppermute | solution.py:58
  31.8 0.0 collective-permute-done.6.refs_1_
  31.8 0.0 collective-permute-done.7.refs_2_
  31.8 0.1 shard_map.110
  31.9 0.1 collective-permute-start.17
  31.9 0.0 copy-start.1
  31.9 0.1 shard_map.107
  32.0 2.8 %collective-permute-start.10 = (bf16[64,512]{1,0:T(8,128)(2,1)S(1)}, bf16[64,512]{1,0:T(8,128)(2,1)S(1)}, u32[]{:S(2)}, u32[]{:S(2)}) collective-permute-start(bf16[64,512]{1,0:T(8,128)(2,1)S(1)} %get-tuple-element.67), channel_id=1, source_target_pairs={{0,12},{1,13},{2,14},{3,15},{4,8},{5,9},{6,10},{7,11},{8,4},{9,5},... | collective-permute-start | bytes 196616 | tf_op jit(solution)/shard_map/ppermute | solution.py:58
  34.8 1.9 %collective-permute-start.8 = (bf16[64,512]{1,0:T(8,128)(2,1)S(1)}, bf16[64,512]{1,0:T(8,128)(2,1)S(1)}, u32[]{:S(2)}, u32[]{:S(2)}) collective-permute-start(bf16[64,512]{1,0:T(8,128)(2,1)S(1)} %get-tuple-element.65), channel_id=1, source_target_pairs={{0,4},{1,5},{2,6},{3,7},{4,0},{5,1},{6,2},{7,3},{8,12},{9,13},{10,... | collective-permute-start | bytes 196616 | tf_op jit(solution)/shard_map/ppermute | solution.py:58
  36.7 2.1 %collective-permute-start.18 = (bf16[64,512]{1,0:T(8,128)(2,1)S(1)}, bf16[64,512]{1,0:T(8,128)(2,1)S(1)}, u32[]{:S(2)}, u32[]{:S(2)}) collective-permute-start(bf16[64,512]{1,0:T(8,128)(2,1)S(1)} %shard_map.111.refs_0_), channel_id=1, source_target_pairs={{0,2},{1,3},{2,0},{3,1},{4,6},{5,7},{6,4},{7,5},{8,10},{9,11},{10,... | collective-permute-start | bytes 196616 | tf_op jit(solution)/shard_map/ppermute | solution.py:58
  38.8 0.4 collective-permute-done.8.refs_0_
  39.2 3.0 %collective-permute-done.9.refs_1_ = bf16[64,512]{1,0:T(8,128)(2,1)S(1)} collective-permute-done((bf16[64,512]{1,0:T(8,128)(2,1)S(1)}, bf16[64,512]{1,0:T(8,128)(2,1)S(1)}, u32[]{:S(2)}, u32[]{:S(2)}) %collective-permute-start.9) | collective-permute-done | bytes 65568 | tf_op jit(solution)/shard_map/ppermute | solution.py:58
  42.2 0.1 collective-permute-start.11
  42.3 2.1 %collective-permute-start.19 = (bf16[128,512]{1,0:T(8,128)(2,1)S(1)}, bf16[128,512]{1,0:T(8,128)(2,1)S(1)}, u32[]{:S(2)}, u32[]{:S(2)}) collective-permute-start(bf16[128,512]{1,0:T(8,128)(2,1)S(1)} %shard_map.112.refs_0_), channel_id=1, source_target_pairs={{0,4},{1,5},{2,6},{3,7},{4,0},{5,1},{6,2},{7,3},{8,12},{9,13},{10,... | collective-permute-start | bytes 393224 | tf_op jit(solution)/shard_map/ppermute | solution.py:58
  44.4 0.9 collective-permute-start.20
  45.3 1.5 %collective-permute-start.21 = (bf16[128,512]{1,0:T(8,128)(2,1)S(1)}, bf16[128,512]{1,0:T(8,128)(2,1)S(1)}, u32[]{:S(2)}, u32[]{:S(2)}) collective-permute-start(bf16[128,512]{1,0:T(8,128)(2,1)S(1)} %shard_map.112.refs_0_), channel_id=1, source_target_pairs={{0,12},{1,13},{2,14},{3,15},{4,8},{5,9},{6,10},{7,11},{8,4},{9,5},... | collective-permute-start | bytes 393224 | tf_op jit(solution)/shard_map/ppermute | solution.py:58
  46.8 1.9 %collective-permute-start.12 = (bf16[64,512]{1,0:T(8,128)(2,1)S(1)}, bf16[64,512]{1,0:T(8,128)(2,1)S(1)}, u32[]{:S(2)}, u32[]{:S(2)}) collective-permute-start(bf16[64,512]{1,0:T(8,128)(2,1)S(1)} %shard_map.108.refs_0_), channel_id=1, source_target_pairs={{0,8},{1,9},{2,10},{3,11},{4,12},{5,13},{6,14},{7,15},{8,0},{9,1},... | collective-permute-start | bytes 196616 | tf_op jit(solution)/shard_map/ppermute | solution.py:58
  48.7 1.5 %collective-permute-start.13 = (bf16[64,512]{1,0:T(8,128)(2,1)S(1)}, bf16[64,512]{1,0:T(8,128)(2,1)S(1)}, u32[]{:S(2)}, u32[]{:S(2)}) collective-permute-start(bf16[64,512]{1,0:T(8,128)(2,1)S(1)} %shard_map.108.refs_0_), channel_id=1, source_target_pairs={{0,12},{1,13},{2,14},{3,15},{4,8},{5,9},{6,10},{7,11},{8,4},{9,5},... | collective-permute-start | bytes 196616 | tf_op jit(solution)/shard_map/ppermute | solution.py:58
  50.3 11.2 %collective-permute-done.12.refs_2_ = bf16[64,512]{1,0:T(8,128)(2,1)S(1)} collective-permute-done((bf16[64,512]{1,0:T(8,128)(2,1)S(1)}, bf16[64,512]{1,0:T(8,128)(2,1)S(1)}, u32[]{:S(2)}, u32[]{:S(2)}) %collective-permute-start.12) | collective-permute-done | bytes 65568 | tf_op jit(solution)/shard_map/ppermute | solution.py:58
  61.5 0.0 collective-permute-done.13.refs_3_
  61.5 2.0 %collective-permute-start.15 = (bf16[64,2048]{1,0:T(8,128)(2,1)S(1)}, bf16[64,2048]{1,0:T(8,128)(2,1)S(1)}, u32[]{:S(2)}, u32[]{:S(2)}) collective-permute-start(bf16[64,2048]{1,0:T(8,128)(2,1)S(1)} %shard_map.109.refs_0_), channel_id=1, source_target_pairs={{0,2},{1,3},{2,0},{3,1},{4,6},{5,7},{6,4},{7,5},{8,10},{9,11},{10,... | collective-permute-start | bytes 786440 | tf_op jit(solution)/shard_map/ppermute | solution.py:58
  63.6 2.2 %shard_map.113 = (f32[512,768]{1,0:T(8,128)S(1)}, bf16[512,256]{1,0:T(8,128)(2,1)S(1)}) custom-call(bf16[512,768]{1,0:T(8,128)(2,1)S(1)} %copy-done.2, bf16[512,768]{1,0:T(8,128)(2,1)S(1)} %collective-permute-done.4.refs_1_, bf16[512,768]{1,0:T(8,128)(2,1)S(1)} %collective-permute-done.7.refs_2_, bf16[512,768]{1,0:T(8,128)(2,1)S(1)} %copy-done, ...), custom_call_target="tpu_custom_call" | custom-call | flops 235929600 | bytes 4980736 | tf_op jit(solution)/shard_map/pallas_call | solution.py:283
  65.8 0.0 collective-permute-done.21.refs_3_
  65.9 0.1 shard_map.114.refs_2_
  65.9 0.1 collective-permute-start.22
  66.0 0.5 collective-permute-start.14
  66.5 1.5 %collective-permute-done.15.refs_1_ = bf16[64,2048]{1,0:T(8,128)(2,1)S(1)} collective-permute-done((bf16[64,2048]{1,0:T(8,128)(2,1)S(1)}, bf16[64,2048]{1,0:T(8,128)(2,1)S(1)}, u32[]{:S(2)}, u32[]{:S(2)}) %collective-permute-start.15) | collective-permute-done | bytes 262176 | tf_op jit(solution)/shard_map/ppermute | solution.py:58
  68.0 1.5 %shard_map.115 = (f32[256,768]{1,0:T(8,128)S(1)}, f32[320,128]{1,0:T(8,128)S(1)}) custom-call(bf16[64,2048]{1,0:T(8,128)(2,1)S(1)} %shard_map.109.refs_0_, bf16[64,2048]{1,0:T(8,128)(2,1)S(1)} %collective-permute-done.15.refs_1_, bf16[128,2048]{1,0:T(8,128)(2,1)S(1)} %shard_map.114.refs_2_, bf16[2048,768]{1,0:T(8,128)(2,1)S(1)} %copy-done.1, ...), custom_call_target="tpu_custom_call" | custom-call | flops 905969664 | bytes 7503872 | tf_op jit(solution)/shard_map/pallas_call | solution.py:90
  69.5 0.0 collective-permute-done.16.refs_1_
  69.5 1.5 %shard_map.116 = (f32[256,768]{1,0:T(8,128)S(1)}, bf16[320,128]{1,0:T(8,128)(2,1)S(1)}) custom-call(bf16[64,2048]{1,0:T(8,128)(2,1)S(1)} %collective-permute-done.14.refs_0_, bf16[64,2048]{1,0:T(8,128)(2,1)S(1)} %collective-permute-done.16.refs_1_, bf16[128,2048]{1,0:T(8,128)(2,1)S(1)} %collective-permute-done.22.refs_2_, bf16[2048,768]{1,0:T(8,128)(2,1)S(1)} %copy-done.1, ...), custom_call_target="tpu_custom_call" | custom-call | flops 905969664 | bytes 7421952 | tf_op jit(solution)/shard_map/pallas_call | solution.py:90
  71.1 0.6 collective-permute-start.23
  71.6 0.9 %collective-permute-done.23.refs_0_ = bf16[320,128]{1,0:T(8,128)(2,1)S(1)} collective-permute-done((bf16[320,128]{1,0:T(8,128)(2,1)S(1)}, bf16[320,128]{1,0:T(8,128)(2,1)S(1)}, u32[]{:S(2)}, u32[]{:S(2)}) %collective-permute-start.23) | collective-permute-done | bytes 81952 | tf_op jit(solution)/shard_map/ppermute | solution.py:58
  72.6 2.0 %collective-permute-start.24 = (bf16[320,128]{1,0:T(8,128)(2,1)S(1)}, bf16[320,128]{1,0:T(8,128)(2,1)S(1)}, u32[]{:S(2)}, u32[]{:S(2)}) collective-permute-start(bf16[320,128]{1,0:T(8,128)(2,1)S(1)} %get-tuple-element.96), channel_id=1, source_target_pairs={{0,2},{1,3},{2,0},{3,1},{4,6},{5,7},{6,4},{7,5},{8,10},{9,11},{10,... | collective-permute-start | bytes 245768 | tf_op jit(solution)/shard_map/ppermute | solution.py:58
  74.6 3.0 %collective-permute-done.24.refs_0_ = bf16[320,128]{1,0:T(8,128)(2,1)S(1)} collective-permute-done((bf16[320,128]{1,0:T(8,128)(2,1)S(1)}, bf16[320,128]{1,0:T(8,128)(2,1)S(1)}, u32[]{:S(2)}, u32[]{:S(2)}) %collective-permute-start.24) | collective-permute-done | bytes 81952 | tf_op jit(solution)/shard_map/ppermute | solution.py:58
  77.6 1.3 %collective-permute-start.25 = (bf16[320,128]{1,0:T(8,128)(2,1)S(1)}, bf16[320,128]{1,0:T(8,128)(2,1)S(1)}, u32[]{:S(2)}, u32[]{:S(2)}) collective-permute-start(bf16[320,128]{1,0:T(8,128)(2,1)S(1)} %get-tuple-element.98), channel_id=1, source_target_pairs={{0,4},{1,5},{2,6},{3,7},{4,0},{5,1},{6,2},{7,3},{8,12},{9,13},{10,... | collective-permute-start | bytes 245768 | tf_op jit(solution)/shard_map/ppermute | solution.py:58
  78.9 1.7 %collective-permute-start.26 = (bf16[320,128]{1,0:T(8,128)(2,1)S(1)}, bf16[320,128]{1,0:T(8,128)(2,1)S(1)}, u32[]{:S(2)}, u32[]{:S(2)}) collective-permute-start(bf16[320,128]{1,0:T(8,128)(2,1)S(1)} %get-tuple-element.98), channel_id=1, source_target_pairs={{0,8},{1,9},{2,10},{3,11},{4,12},{5,13},{6,14},{7,15},{8,0},{9,1},... | collective-permute-start | bytes 245768 | tf_op jit(solution)/shard_map/ppermute | solution.py:58
  80.6 1.4 %collective-permute-start.27 = (bf16[320,128]{1,0:T(8,128)(2,1)S(1)}, bf16[320,128]{1,0:T(8,128)(2,1)S(1)}, u32[]{:S(2)}, u32[]{:S(2)}) collective-permute-start(bf16[320,128]{1,0:T(8,128)(2,1)S(1)} %get-tuple-element.98), channel_id=1, source_target_pairs={{0,12},{1,13},{2,14},{3,15},{4,8},{5,9},{6,10},{7,11},{8,4},{9,5},... | collective-permute-start | bytes 245768 | tf_op jit(solution)/shard_map/ppermute | solution.py:58
  82.0 0.9 %collective-permute-done.25.refs_0_ = bf16[320,128]{1,0:T(8,128)(2,1)S(1)} collective-permute-done((bf16[320,128]{1,0:T(8,128)(2,1)S(1)}, bf16[320,128]{1,0:T(8,128)(2,1)S(1)}, u32[]{:S(2)}, u32[]{:S(2)}) %collective-permute-start.25) | collective-permute-done | bytes 81952 | tf_op jit(solution)/shard_map/ppermute | solution.py:58
  83.0 5.1 %collective-permute-done.26.refs_1_ = bf16[320,128]{1,0:T(8,128)(2,1)S(1)} collective-permute-done((bf16[320,128]{1,0:T(8,128)(2,1)S(1)}, bf16[320,128]{1,0:T(8,128)(2,1)S(1)}, u32[]{:S(2)}, u32[]{:S(2)}) %collective-permute-start.26) | collective-permute-done | bytes 81952 | tf_op jit(solution)/shard_map/ppermute | solution.py:58
  88.1 0.1 collective-permute-start.28
  88.2 1.3 %collective-permute-done.28.refs_1_ = bf16[320,128]{1,0:T(8,128)(2,1)S(1)} collective-permute-done((bf16[320,128]{1,0:T(8,128)(2,1)S(1)}, bf16[320,128]{1,0:T(8,128)(2,1)S(1)}, u32[]{:S(2)}, u32[]{:S(2)}) %collective-permute-start.28) | collective-permute-done | bytes 81952 | tf_op jit(solution)/shard_map/ppermute | solution.py:58
  89.5 2.5 %shard_map.120 = (bf16[512,768]{1,0:T(8,128)(2,1)}, bf16[512,768]{1,0:T(8,128)(2,1)}) custom-call(bf16[320,128]{1,0:T(8,128)(2,1)S(1)} %shard_map.119.refs_0_, bf16[320,128]{1,0:T(8,128)(2,1)S(1)} %collective-permute-done.28.refs_1_, f32[256,768]{1,0:T(8,128)S(1)} %get-tuple-element.99.refs_2_, f32[256,768]{1,0:T(8,128)S(1)} %get-tuple-element.100.refs_3_, ...), custom_call_target="tpu_custom_call" | custom-call | flops 201326592 | bytes 4718592 | tf_op jit(solution)/shard_map/pallas_call | solution.py:452
  (31 shorter events, 0.3 us)
Async XLA Ops:
  0.6 7.6 %copy-start.2 = (bf16[512,768]{1,0:T(8,128)(2,1)S(1)}, bf16[512,768]{1,0:T(8,128)(2,1)}, u32[]{:S(2)}) copy-start(bf16[512,768]{1,0:T(8,128)(2,1)} %refs_5_.5) | copy-start | bytes 2359300
  0.6 15.5 %collective-permute-start.4 = (bf16[512,768]{1,0:T(8,128)(2,1)}, bf16[512,768]{1,0:T(8,128)(2,1)S(1)}, u32[]{:S(2)}, u32[]{:S(2)}) collective-permute-start(bf16[512,768]{1,0:T(8,128)(2,1)} %refs_5_.5), channel_id=1, source_target_pairs={{0,1},{1,2},{2,3},{3,4},{4,5},{5,6},{6,7},{7,8},{8,9},{9,10},{10,1... | collective-permute-start | bytes 2359304 | tf_op jit(solution)/shard_map/ppermute | solution.py:49
  5.5 44.7 %copy-start.7 = (f32[768]{0:T(1024)S(1)}, f32[768]{0:T(1024)}, u32[]{:S(2)}) copy-start(f32[768]{0:T(1024)} %param.12) | copy-start | bytes 9220
  5.5 44.7 %copy-start.8 = (f32[768]{0:T(1024)S(1)}, f32[768]{0:T(1024)}, u32[]{:S(2)}) copy-start(f32[768]{0:T(1024)} %param.13) | copy-start | bytes 9220
  5.5 58.0 %copy-start = (bf16[512,768]{1,0:T(8,128)(2,1)S(1)}, bf16[512,768]{1,0:T(8,128)(2,1)}, u32[]{:S(2)}) copy-start(bf16[512,768]{1,0:T(8,128)(2,1)} %refs_4_.2) | copy-start | bytes 2359300
  5.5 58.0 %copy-start.3 = (bf16[2,128,128]{2,1,0:T(8,128)(2,1)S(1)}, bf16[2,128,128]{2,1,0:T(8,128)(2,1)}, u32[]{:S(2)}) copy-start(bf16[2,128,128]{2,1,0:T(8,128)(2,1)} %constant.2.clone.refs_4_) | copy-start | bytes 196612
  5.5 58.0 %copy-start.4 = (f32[512]{0:T(512)S(1)}, f32[512]{0:T(512)}, u32[]{:S(2)}) copy-start(f32[512]{0:T(512)} %param.14) | copy-start | bytes 6148
  5.5 58.0 %copy-start.5 = (s32[512]{0:T(512)S(1)}, s32[512]{0:T(512)}, u32[]{:S(2)}) copy-start(s32[512]{0:T(512)} %param.15) | copy-start | bytes 6148
  5.6 58.0 %copy-start.6 = (s32[512]{0:T(512)S(1)}, s32[512]{0:T(512)}, u32[]{:S(2)}) copy-start(s32[512]{0:T(512)} %param.16) | copy-start | bytes 6148
  5.6 5.8 %collective-permute-start = (bf16[128,2048]{1,0:T(8,128)(2,1)S(1)}, bf16[128,2048]{1,0:T(8,128)(2,1)S(1)}, u32[]{:S(2)}, u32[]{:S(2)}) collective-permute-start(bf16[128,2048]{1,0:T(8,128)(2,1)S(1)} %get-tuple-element.53), channel_id=1, source_target_pairs={{0,1},{1,0},{2,3},{3,2},{4,5},{5,4},{6,7},{7,6},{8,9},{9,8},{10,11... | collective-permute-start | bytes 1572872 | tf_op jit(solution)/shard_map/ppermute | solution.py:58
  8.2 23.5 %collective-permute-start.7 = (bf16[512,768]{1,0:T(8,128)(2,1)S(1)}, bf16[512,768]{1,0:T(8,128)(2,1)S(1)}, u32[]{:S(2)}, u32[]{:S(2)}) collective-permute-start(bf16[512,768]{1,0:T(8,128)(2,1)S(1)} %copy-done.2), channel_id=1, source_target_pairs={{0,15},{1,0},{2,1},{3,2},{4,3},{5,4},{6,5},{7,6},{8,7},{9,8},{10,9... | collective-permute-start | bytes 2359304 | tf_op jit(solution)/shard_map/ppermute | solution.py:49
  11.3 1.9 %collective-permute-start.1 = (bf16[128,2048]{1,0:T(8,128)(2,1)S(1)}, bf16[128,2048]{1,0:T(8,128)(2,1)S(1)}, u32[]{:S(2)}, u32[]{:S(2)}) collective-permute-start(bf16[128,2048]{1,0:T(8,128)(2,1)S(1)} %get-tuple-element.56), channel_id=1, source_target_pairs={{0,1},{1,0},{2,3},{3,2},{4,5},{5,4},{6,7},{7,6},{8,9},{9,8},{10,11... | collective-permute-start | bytes 1572872 | tf_op jit(solution)/shard_map/ppermute | solution.py:58
  11.4 20.3 %collective-permute-start.6 = (bf16[64,2048]{1,0:T(8,128)(2,1)S(1)}, bf16[64,2048]{1,0:T(8,128)(2,1)S(1)}, u32[]{:S(2)}, u32[]{:S(2)}) collective-permute-start(bf16[64,2048]{1,0:T(8,128)(2,1)S(1)} %get-tuple-element.61), channel_id=1, source_target_pairs={{0,2},{1,3},{2,0},{3,1},{4,6},{5,7},{6,4},{7,5},{8,10},{9,11},{10,... | collective-permute-start | bytes 786440 | tf_op jit(solution)/shard_map/ppermute | solution.py:58
  13.3 13.2 %collective-permute-start.2 = (bf16[128,512]{1,0:T(8,128)(2,1)S(1)}, bf16[128,512]{1,0:T(8,128)(2,1)S(1)}, u32[]{:S(2)}, u32[]{:S(2)}) collective-permute-start(bf16[128,512]{1,0:T(8,128)(2,1)S(1)} %get-tuple-element.57), channel_id=1, source_target_pairs={{0,4},{1,5},{2,6},{3,7},{4,0},{5,1},{6,2},{7,3},{8,12},{9,13},{10,... | collective-permute-start | bytes 393224 | tf_op jit(solution)/shard_map/ppermute | solution.py:58
  13.4 18.3 %collective-permute-start.3 = (bf16[128,512]{1,0:T(8,128)(2,1)S(1)}, bf16[128,512]{1,0:T(8,128)(2,1)S(1)}, u32[]{:S(2)}, u32[]{:S(2)}) collective-permute-start(bf16[128,512]{1,0:T(8,128)(2,1)S(1)} %get-tuple-element.58), channel_id=1, source_target_pairs={{0,8},{1,9},{2,10},{3,11},{4,12},{5,13},{6,14},{7,15},{8,0},{9,1},... | collective-permute-start | bytes 393224 | tf_op jit(solution)/shard_map/ppermute | solution.py:58
  16.1 15.7 %collective-permute-start.5 = (bf16[128,512]{1,0:T(8,128)(2,1)S(1)}, bf16[128,512]{1,0:T(8,128)(2,1)S(1)}, u32[]{:S(2)}, u32[]{:S(2)}) collective-permute-start(bf16[128,512]{1,0:T(8,128)(2,1)S(1)} %get-tuple-element.60), channel_id=1, source_target_pairs={{0,12},{1,13},{2,14},{3,15},{4,8},{5,9},{6,10},{7,11},{8,4},{9,5},... | collective-permute-start | bytes 393224 | tf_op jit(solution)/shard_map/ppermute | solution.py:58
  31.9 4.9 %collective-permute-start.17 = (bf16[64,512]{1,0:T(8,128)(2,1)S(1)}, bf16[64,512]{1,0:T(8,128)(2,1)S(1)}, u32[]{:S(2)}, u32[]{:S(2)}) collective-permute-start(bf16[64,512]{1,0:T(8,128)(2,1)S(1)} %get-tuple-element.77), channel_id=1, source_target_pairs={{0,2},{1,3},{2,0},{3,1},{4,6},{5,7},{6,4},{7,5},{8,10},{9,11},{10,... | collective-permute-start | bytes 196616 | tf_op jit(solution)/shard_map/ppermute | solution.py:58
  31.9 36.0 %copy-start.1 = (bf16[2048,768]{1,0:T(8,128)(2,1)S(1)}, bf16[2048,768]{1,0:T(8,128)(2,1)}, u32[]{:S(2)}) copy-start(bf16[2048,768]{1,0:T(8,128)(2,1)} %refs_3_.5) | copy-start | bytes 9437188
  32.0 6.8 %collective-permute-start.10 = (bf16[64,512]{1,0:T(8,128)(2,1)S(1)}, bf16[64,512]{1,0:T(8,128)(2,1)S(1)}, u32[]{:S(2)}, u32[]{:S(2)}) collective-permute-start(bf16[64,512]{1,0:T(8,128)(2,1)S(1)} %get-tuple-element.67), channel_id=1, source_target_pairs={{0,12},{1,13},{2,14},{3,15},{4,8},{5,9},{6,10},{7,11},{8,4},{9,5},... | collective-permute-start | bytes 196616 | tf_op jit(solution)/shard_map/ppermute | solution.py:58
  34.8 4.4 %collective-permute-start.8 = (bf16[64,512]{1,0:T(8,128)(2,1)S(1)}, bf16[64,512]{1,0:T(8,128)(2,1)S(1)}, u32[]{:S(2)}, u32[]{:S(2)}) collective-permute-start(bf16[64,512]{1,0:T(8,128)(2,1)S(1)} %get-tuple-element.65), channel_id=1, source_target_pairs={{0,4},{1,5},{2,6},{3,7},{4,0},{5,1},{6,2},{7,3},{8,12},{9,13},{10,... | collective-permute-start | bytes 196616 | tf_op jit(solution)/shard_map/ppermute | solution.py:58
  36.7 5.5 %collective-permute-start.9 = (bf16[64,512]{1,0:T(8,128)(2,1)S(1)}, bf16[64,512]{1,0:T(8,128)(2,1)S(1)}, u32[]{:S(2)}, u32[]{:S(2)}) collective-permute-start(bf16[64,512]{1,0:T(8,128)(2,1)S(1)} %get-tuple-element.66), channel_id=1, source_target_pairs={{0,8},{1,9},{2,10},{3,11},{4,12},{5,13},{6,14},{7,15},{8,0},{9,1},... | collective-permute-start | bytes 196616 | tf_op jit(solution)/shard_map/ppermute | solution.py:58
  36.7 5.5 %collective-permute-start.18 = (bf16[64,512]{1,0:T(8,128)(2,1)S(1)}, bf16[64,512]{1,0:T(8,128)(2,1)S(1)}, u32[]{:S(2)}, u32[]{:S(2)}) collective-permute-start(bf16[64,512]{1,0:T(8,128)(2,1)S(1)} %shard_map.111.refs_0_), channel_id=1, source_target_pairs={{0,2},{1,3},{2,0},{3,1},{4,6},{5,7},{6,4},{7,5},{8,10},{9,11},{10,... | collective-permute-start | bytes 196616 | tf_op jit(solution)/shard_map/ppermute | solution.py:58
  42.2 6.5 %collective-permute-start.11 = (bf16[64,512]{1,0:T(8,128)(2,1)S(1)}, bf16[64,512]{1,0:T(8,128)(2,1)S(1)}, u32[]{:S(2)}, u32[]{:S(2)}) collective-permute-start(bf16[64,512]{1,0:T(8,128)(2,1)S(1)} %shard_map.108.refs_0_), channel_id=1, source_target_pairs={{0,4},{1,5},{2,6},{3,7},{4,0},{5,1},{6,2},{7,3},{8,12},{9,13},{10,... | collective-permute-start | bytes 196616 | tf_op jit(solution)/shard_map/ppermute | solution.py:58
  42.3 23.5 %collective-permute-start.19 = (bf16[128,512]{1,0:T(8,128)(2,1)S(1)}, bf16[128,512]{1,0:T(8,128)(2,1)S(1)}, u32[]{:S(2)}, u32[]{:S(2)}) collective-permute-start(bf16[128,512]{1,0:T(8,128)(2,1)S(1)} %shard_map.112.refs_0_), channel_id=1, source_target_pairs={{0,4},{1,5},{2,6},{3,7},{4,0},{5,1},{6,2},{7,3},{8,12},{9,13},{10,... | collective-permute-start | bytes 393224 | tf_op jit(solution)/shard_map/ppermute | solution.py:58
  44.4 21.5 %collective-permute-start.20 = (bf16[128,512]{1,0:T(8,128)(2,1)S(1)}, bf16[128,512]{1,0:T(8,128)(2,1)S(1)}, u32[]{:S(2)}, u32[]{:S(2)}) collective-permute-start(bf16[128,512]{1,0:T(8,128)(2,1)S(1)} %shard_map.112.refs_0_), channel_id=1, source_target_pairs={{0,8},{1,9},{2,10},{3,11},{4,12},{5,13},{6,14},{7,15},{8,0},{9,1},... | collective-permute-start | bytes 393224 | tf_op jit(solution)/shard_map/ppermute | solution.py:58
  45.3 20.6 %collective-permute-start.21 = (bf16[128,512]{1,0:T(8,128)(2,1)S(1)}, bf16[128,512]{1,0:T(8,128)(2,1)S(1)}, u32[]{:S(2)}, u32[]{:S(2)}) collective-permute-start(bf16[128,512]{1,0:T(8,128)(2,1)S(1)} %shard_map.112.refs_0_), channel_id=1, source_target_pairs={{0,12},{1,13},{2,14},{3,15},{4,8},{5,9},{6,10},{7,11},{8,4},{9,5},... | collective-permute-start | bytes 393224 | tf_op jit(solution)/shard_map/ppermute | solution.py:58
  46.8 14.7 %collective-permute-start.12 = (bf16[64,512]{1,0:T(8,128)(2,1)S(1)}, bf16[64,512]{1,0:T(8,128)(2,1)S(1)}, u32[]{:S(2)}, u32[]{:S(2)}) collective-permute-start(bf16[64,512]{1,0:T(8,128)(2,1)S(1)} %shard_map.108.refs_0_), channel_id=1, source_target_pairs={{0,8},{1,9},{2,10},{3,11},{4,12},{5,13},{6,14},{7,15},{8,0},{9,1},... | collective-permute-start | bytes 196616 | tf_op jit(solution)/shard_map/ppermute | solution.py:58
  48.7 12.8 %collective-permute-start.13 = (bf16[64,512]{1,0:T(8,128)(2,1)S(1)}, bf16[64,512]{1,0:T(8,128)(2,1)S(1)}, u32[]{:S(2)}, u32[]{:S(2)}) collective-permute-start(bf16[64,512]{1,0:T(8,128)(2,1)S(1)} %shard_map.108.refs_0_), channel_id=1, source_target_pairs={{0,12},{1,13},{2,14},{3,15},{4,8},{5,9},{6,10},{7,11},{8,4},{9,5},... | collective-permute-start | bytes 196616 | tf_op jit(solution)/shard_map/ppermute | solution.py:58
  61.5 6.4 %collective-permute-start.15 = (bf16[64,2048]{1,0:T(8,128)(2,1)S(1)}, bf16[64,2048]{1,0:T(8,128)(2,1)S(1)}, u32[]{:S(2)}, u32[]{:S(2)}) collective-permute-start(bf16[64,2048]{1,0:T(8,128)(2,1)S(1)} %shard_map.109.refs_0_), channel_id=1, source_target_pairs={{0,2},{1,3},{2,0},{3,1},{4,6},{5,7},{6,4},{7,5},{8,10},{9,11},{10,... | collective-permute-start | bytes 786440 | tf_op jit(solution)/shard_map/ppermute | solution.py:58
  65.9 3.6 %collective-permute-start.22 = (bf16[128,2048]{1,0:T(8,128)(2,1)S(1)}, bf16[128,2048]{1,0:T(8,128)(2,1)S(1)}, u32[]{:S(2)}, u32[]{:S(2)}) collective-permute-start(bf16[128,2048]{1,0:T(8,128)(2,1)S(1)} %shard_map.114.refs_2_), channel_id=1, source_target_pairs={{0,1},{1,0},{2,3},{3,2},{4,5},{5,4},{6,7},{7,6},{8,9},{9,8},{10,11... | collective-permute-start | bytes 1572872 | tf_op jit(solution)/shard_map/ppermute | solution.py:58
  66.0 3.5 %collective-permute-start.14 = (bf16[64,2048]{1,0:T(8,128)(2,1)S(1)}, bf16[64,2048]{1,0:T(8,128)(2,1)S(1)}, u32[]{:S(2)}, u32[]{:S(2)}) collective-permute-start(bf16[64,2048]{1,0:T(8,128)(2,1)S(1)} %shard_map.109.refs_0_), channel_id=1, source_target_pairs={{0,1},{1,0},{2,3},{3,2},{4,5},{5,4},{6,7},{7,6},{8,9},{9,8},{10,11... | collective-permute-start | bytes 786440 | tf_op jit(solution)/shard_map/ppermute | solution.py:58
  68.0 1.5 %collective-permute-start.16 = (bf16[64,2048]{1,0:T(8,128)(2,1)S(1)}, bf16[64,2048]{1,0:T(8,128)(2,1)S(1)}, u32[]{:S(2)}, u32[]{:S(2)}) collective-permute-start(bf16[64,2048]{1,0:T(8,128)(2,1)S(1)} %collective-permute-done.15.refs_1_), channel_id=1, source_target_pairs={{0,1},{1,0},{2,3},{3,2},{4,5},{5,4},{6,7},{7,6},{8,9},{9,8},{10,11... | collective-permute-start | bytes 786440 | tf_op jit(solution)/shard_map/ppermute | solution.py:58
  71.1 1.5 %collective-permute-start.23 = (bf16[320,128]{1,0:T(8,128)(2,1)S(1)}, bf16[320,128]{1,0:T(8,128)(2,1)S(1)}, u32[]{:S(2)}, u32[]{:S(2)}) collective-permute-start(bf16[320,128]{1,0:T(8,128)(2,1)S(1)} %get-tuple-element.94), channel_id=1, source_target_pairs={{0,1},{1,0},{2,3},{3,2},{4,5},{5,4},{6,7},{7,6},{8,9},{9,8},{10,11... | collective-permute-start | bytes 245768 | tf_op jit(solution)/shard_map/ppermute | solution.py:58
  72.6 5.0 %collective-permute-start.24 = (bf16[320,128]{1,0:T(8,128)(2,1)S(1)}, bf16[320,128]{1,0:T(8,128)(2,1)S(1)}, u32[]{:S(2)}, u32[]{:S(2)}) collective-permute-start(bf16[320,128]{1,0:T(8,128)(2,1)S(1)} %get-tuple-element.96), channel_id=1, source_target_pairs={{0,2},{1,3},{2,0},{3,1},{4,6},{5,7},{6,4},{7,5},{8,10},{9,11},{10,... | collective-permute-start | bytes 245768 | tf_op jit(solution)/shard_map/ppermute | solution.py:58
  77.6 5.4 %collective-permute-start.25 = (bf16[320,128]{1,0:T(8,128)(2,1)S(1)}, bf16[320,128]{1,0:T(8,128)(2,1)S(1)}, u32[]{:S(2)}, u32[]{:S(2)}) collective-permute-start(bf16[320,128]{1,0:T(8,128)(2,1)S(1)} %get-tuple-element.98), channel_id=1, source_target_pairs={{0,4},{1,5},{2,6},{3,7},{4,0},{5,1},{6,2},{7,3},{8,12},{9,13},{10,... | collective-permute-start | bytes 245768 | tf_op jit(solution)/shard_map/ppermute | solution.py:58
  78.9 9.2 %collective-permute-start.26 = (bf16[320,128]{1,0:T(8,128)(2,1)S(1)}, bf16[320,128]{1,0:T(8,128)(2,1)S(1)}, u32[]{:S(2)}, u32[]{:S(2)}) collective-permute-start(bf16[320,128]{1,0:T(8,128)(2,1)S(1)} %get-tuple-element.98), channel_id=1, source_target_pairs={{0,8},{1,9},{2,10},{3,11},{4,12},{5,13},{6,14},{7,15},{8,0},{9,1},... | collective-permute-start | bytes 245768 | tf_op jit(solution)/shard_map/ppermute | solution.py:58
  80.6 7.5 %collective-permute-start.27 = (bf16[320,128]{1,0:T(8,128)(2,1)S(1)}, bf16[320,128]{1,0:T(8,128)(2,1)S(1)}, u32[]{:S(2)}, u32[]{:S(2)}) collective-permute-start(bf16[320,128]{1,0:T(8,128)(2,1)S(1)} %get-tuple-element.98), channel_id=1, source_target_pairs={{0,12},{1,13},{2,14},{3,15},{4,8},{5,9},{6,10},{7,11},{8,4},{9,5},... | collective-permute-start | bytes 245768 | tf_op jit(solution)/shard_map/ppermute | solution.py:58
  88.1 1.3 %collective-permute-start.28 = (bf16[320,128]{1,0:T(8,128)(2,1)S(1)}, bf16[320,128]{1,0:T(8,128)(2,1)S(1)}, u32[]{:S(2)}, u32[]{:S(2)}) collective-permute-start(bf16[320,128]{1,0:T(8,128)(2,1)S(1)} %shard_map.119.refs_0_), channel_id=1, source_target_pairs={{0,1},{1,0},{2,3},{3,2},{4,5},{5,4},{6,7},{7,6},{8,9},{9,8},{10,11... | collective-permute-start | bytes 245768 | tf_op jit(solution)/shard_map/ppermute | solution.py:58

commit v12 on v10

--- a/solution.py
+++ b/solution.py
@@ -28,7 +28,7 @@
 STEP_SIZE = 0.3
 MIB = 1024 * 1024
 VMEM_BYTES = 24 * MIB
-REDUCE_SHARE = 0.5
+REDUCE_SHARE = 0.625
 GATHER_SHARE = 0.5
 BF16 = jnp.bfloat16
 F32 = jnp.float32
@@ -317,12 +317,21 @@
     )(response, low, high, orbitals, matrix, *lines, *bounds)
 
 
-def pad_orbitals(o_ref, pad_ref, blk):
+def pad_body(edge, o_ref, pad_ref):
     bands, cells = o_ref.shape
-    edge = REACH * blk
     pad_ref[:edge, :] = jnp.zeros((edge, cells), pad_ref.dtype)
     pad_ref[edge : edge + bands, :] = o_ref[...]
     pad_ref[edge + bands :, :] = jnp.zeros((edge, cells), pad_ref.dtype)
+
+
+def pad_orbitals(orbitals, blk):
+    bands, cells = orbitals.shape
+    edge = REACH * blk
+    return local_call(
+        functools.partial(pad_body, edge),
+        struct((bands + 2 * edge, cells), orbitals.dtype),
+        [orbitals],
+    )
 
 
 def subgroup(shape, blk):
@@ -355,7 +364,7 @@
 def apply_body(core, across, block, group_rows, blk, other, *refs):
     size = across[0]
     blocks = refs[: size + 1]
-    p_ref, base_ref, o_ref, u_ref, s_ref, c_ref, pad_ref = refs[size + 1 :]
+    p_ref, base_ref, pad_ref, u_ref, s_ref, c_ref = refs[size + 1 :]
     rows, cells = u_ref.shape
     c, x = position(core), position(across)
     side = 1 - c if other else c
@@ -374,7 +383,6 @@
         u_ref[:, cols] = base_ref[mine, cols] + jnp.dot(
             c_ref[...], p_ref[:, cols], preferred_element_type=F32
         )
-    pad_orbitals(o_ref, pad_ref, blk)
     height = group_rows + 2 * blk
     for g in range(rows // group_rows):
         start = pl.multiple_of(side * rows + g * group_rows, group_rows)
@@ -389,7 +397,7 @@
         s_ref[g * height + group_rows : (g + 1) * height, :] = rest_sums.astype(s_ref.dtype)
 
 
-def apply(blocks, projectors, base, orbitals, core, across, block, group_rows, blk, other):
+def apply(blocks, projectors, base, padded, core, across, block, group_rows, blk, other):
     bands, cells = base.shape
     rows = bands // 2
     count = projectors.shape[0]
@@ -397,12 +405,9 @@
     return local_call(
         functools.partial(apply_body, core, across, block, group_rows, blk, other),
         [struct((rows, cells), F32), struct((height, group_rows), BF16 if other else F32)],
-        [*blocks, projectors, base, orbitals],
+        [*blocks, projectors, base, padded],
         flops=2 * rows * cells * (count + 2 * group_rows),
-        scratch=[
-            pltpu.VMEM((rows, count), BF16),
-            pltpu.VMEM((bands + 2 * REACH * blk, cells), BF16),
-        ],
+        scratch=[pltpu.VMEM((rows, count), BF16)],
     )
 
 
@@ -419,8 +424,8 @@
 
 
 def project_body(core, blk, *refs):
-    w_own, w_other, u_own, u_other, o_ref, r_ref, mask_ref = refs[:7]
-    updated_ref, residual_ref, pad_ref, w_ref, u_ref = refs[7:]
+    w_own, w_other, u_own, u_other, pad_ref, r_ref, mask_ref = refs[:7]
+    updated_ref, residual_ref, w_ref, u_ref = refs[7:]
     rows = u_ref.shape[0]
     height = w_ref.shape[0]
     per = u_own.shape[0] // rows
@@ -429,10 +434,6 @@
     local = lax.rem(g, jnp.int32(per))
     w_rows = pl.ds(pl.multiple_of(local * height, 16), height)
     u_rows = pl.ds(pl.multiple_of(local * rows, rows), rows)
-
-    @pl.when(g == 0)
-    def _():
-        pad_orbitals(o_ref, pad_ref, blk)
 
     @pl.when(own)
     def _():
@@ -456,7 +457,7 @@
     updated_ref[...] = (r_ref[...].astype(F32) + STEP_SIZE * residual).astype(BF16)
 
 
-def project(weights, unprojected, orbitals, response, mask, core, group_rows, blk):
+def project(weights, unprojected, padded, response, mask, core, group_rows, blk):
     bands, cells = response.shape
     out = struct((bands, cells), BF16)
     here = pl.BlockSpec((group_rows, cells), lambda g: (g, 0))
@@ -469,21 +470,20 @@
         grid=(bands // group_rows,),
         out_shape=(out, out),
         in_specs=[
-            *[full(a) for a in (*weights, *unprojected, orbitals)],
+            *[full(a) for a in (*weights, *unprojected, padded)],
             here,
             pl.BlockSpec((group_rows, mask.shape[1]), lambda g: (g, 0)),
         ],
         out_specs=(here, here),
         scratch_shapes=[
-            pltpu.VMEM((bands + 2 * REACH * blk, cells), BF16),
             pltpu.VMEM((group_rows + 2 * blk, group_rows), BF16),
             pltpu.VMEM((group_rows, cells), F32),
         ],
         compiler_params=params(),
         cost_estimate=cost(
-            4 * bands * group_rows * cells, orbitals, *unprojected, response, out, out
+            4 * bands * group_rows * cells, padded, *unprojected, response, out, out
         ),
-    )(*weights, *unprojected, orbitals, response, mask)
+    )(*weights, *unprojected, padded, response, mask)
 
 
 def shards(
@@ -514,11 +514,12 @@
         return [swapped(part, count, level, k + 1) for k, part in enumerate(parts)]
 
     low = neighbour(response[:, local_cells - halo :], count, 1)
-    high = neighbour(response[:, :halo], count, -1)
 
     sent_x, sent_z, keep_x, keep_z = first_sums(response, projectors, core, block, first)
     sent_z = swapped(sent_z, count, core, 1)
     sent_x = swapped(sent_x, count, core, 1)
+    head, sent_z = lax.optimization_barrier((response[:, :halo], sent_z))
+    high = neighbour(head, count, -1)
     keep_z, *parts_z = split(keep_z, [sent_z], along, 1)
     keep_x, *parts_x = split(keep_x, [sent_x], across, 0)
     parts_z[-1], low = lax.optimization_barrier((parts_z[-1], low))
@@ -548,19 +549,21 @@
     block_x = place(pieces_x, along, 1)
     block_z = place(pieces_z, across, 0)
     blocks_x = [block_x, *to(block_x, across)]
-    pieces_z, base = lax.optimization_barrier(([block_z, *to(block_z, along)], base))
+    pieces_z, base, padded = lax.optimization_barrier(
+        ([block_z, *to(block_z, along)], base, pad_orbitals(orbitals, blk))
+    )
     blocks = [*blocks_x, place(pieces_z, along, 1)]
     others = [swapped(part, count, core, 1) for part in blocks]
     sizes = (core, across, block, group_rows, blk)
-    wide, keep = apply(blocks, projectors, base, orbitals, *sizes, False)
+    wide, keep = apply(blocks, projectors, base, padded, *sizes, False)
     others, keep = lax.optimization_barrier((others, keep))
-    other_wide, part = apply(others, projectors, base, orbitals, *sizes, True)
+    other_wide, part = apply(others, projectors, base, padded, *sizes, True)
     unprojected = (wide, other_wide)
     total, part = add_up(keep, to(part, core))
     total, part = add_up(total, to(part, across))
     own = finish(total, to(part, along), window_scale)
     weights = (own, *to(own, core))
-    return project(weights, unprojected, orbitals, response, mask, core, group_rows, blk)
+    return project(weights, unprojected, padded, response, mask, core, group_rows, blk)
 
 
 def solution(mesh):

time: 86.8 us -> 90.9 us (1.047)
  starting transfers between devices: 36.7 us -> 39.6 us
  waiting for transfers between devices: 36.3 us -> 37.4 us
    ppermute x2, waiting for transfers between devices: 0.27 us -> 7.93 us  [neighbour(): lax.ppermute(array, 'band', [(i, (i + step) % count) for i in range(count)])]
    ppermute x27, waiting for transfers between devices: 36.1 us -> 29.4 us  [swapped(): return lax.ppermute(array, 'band', pairs)]
    ppermute x2, starting transfers between devices: 3.62 us -> 6.07 us  [neighbour(): lax.ppermute(array, 'band', [(i, (i + step) % count) for i in range(count)])]
    pallas_call x13 -> x14, Pallas kernels: 3.61 us -> 3.7 us  [local_call(): pl.pallas_call(body, out_shape=outs, in_specs=[whole() for _ in args], ou...]
  transfers between devices with their start and end apart: 29 -> 29, of which waited for: 16 -> 15; matrix products, arithmetic and copies ran while one was open for 0% -> 0% of each run, Pallas kernels for 10% -> 5%
where the time goes in v12:
time: 90.9 us; the launch traced here: 90.7 us
  starting transfers between devices  39.6 us (44%)
  waiting for transfers between devices  37.4 us (41%)
  Pallas kernels  12.8 us (14%)
  between operations  0.91 us (1%)
    ppermute x27, starting transfers between devices, swapped(): return lax.ppermute(array, 'band', pairs)  33.5 us
    ppermute x27, waiting for transfers between devices, swapped(): return lax.ppermute(array, 'band', pairs)  29.4 us
    ppermute x2, waiting for transfers between devices, neighbour(): lax.ppermute(array, 'band', [(i, (i + step) % count) for i in range(count)])  7.93 us
    ppermute x2, starting transfers between devices, neighbour(): lax.ppermute(array, 'band', [(i, (i + step) % count) for i in range(count)])  6.07 us
    pallas_call x1, Pallas kernels, first_sums(): pl.pallas_call(functools.partial(first_body, core, block, tile), out_shap...  4.39 us
    pallas_call x14, Pallas kernels, local_call(): pl.pallas_call(body, out_shape=outs, in_specs=[whole() for _ in args], ou...  3.7 us
    pallas_call x1, Pallas kernels, project(): pl.pallas_call(functools.partial(project_body, core, blk), grid=(bands //...  2.43 us
    pallas_call x1, Pallas kernels, local_part(): pl.pallas_call(functools.partial(local_body, depth, (group_rows, blk)), g...  2.3 us
  transfers between devices with their start and end apart: 29, of which 15 were waited for; matrix products, arithmetic and copies ran while one was open for 0% of the time, Pallas kernels for 5%

profile of v12, /device:TPU:0, one launch (start us, length us, event | category | flops | bytes accessed | tf_op | source)
XLA Modules:
  0.0 90.7 jit_solution(267855685112800508)
XLA Ops:
  0.6 4.4 %shard_map.104 = (bf16[160,2048]{1,0:T(8,128)(2,1)S(1)}, bf16[96,2048]{1,0:T(8,128)(2,1)S(1)}, f32[160,2048]{1,0:T(8,128)S(1)}, f32[96,2048]{1,0:T(8,128)S(1)}) custom-call(bf16[512,768]{1,0:T(8,128)(2,1)} %refs_5_.1, bf16[2048,768]{1,0:T(8,128)(2,1)} %refs_3_.5), custom_call_target="tpu_custom_call" | custom-call | flops 1610612736 | bytes 6291456 | tf_op jit(solution)/shard_map/pallas_call | solution.py:147
  5.0 0.5 collective-permute-start.1
  5.6 0.1 collective-permute-start
  5.6 0.4 collective-permute-start.4
  6.1 0.8 collective-permute-done.1.refs_1_
  6.9 5.6 %collective-permute-start.7 = (bf16[512,768]{1,0:T(8,128)(2,1)S(1)}, bf16[512,768]{1,0:T(8,128)(2,1)S(1)}, u32[]{:S(2)}, u32[]{:S(2)}) collective-permute-start(bf16[512,768]{1,0:T(8,128)(2,1)S(1)} %copy-done.2), channel_id=1, source_target_pairs={{0,15},{1,0},{2,1},{3,2},{4,3},{5,4},{6,5},{7,6},{8,7},{9,8},{10,9... | collective-permute-start | bytes 2359304 | tf_op jit(solution)/shard_map/ppermute | solution.py:50
  12.5 0.1 shard_map.105
  12.7 0.1 collective-permute-start.6
  12.8 0.0 copy-start.7
  12.8 0.0 copy-start.8
  12.8 0.0 copy-start.1
  12.8 0.1 shard_map.106
  12.9 0.1 collective-permute-start.2
  13.0 2.2 %collective-permute-start.3 = (bf16[96,512]{1,0:T(8,128)(2,1)S(1)}, bf16[96,512]{1,0:T(8,128)(2,1)S(1)}, u32[]{:S(2)}, u32[]{:S(2)}) collective-permute-start(bf16[96,512]{1,0:T(8,128)(2,1)S(1)} %get-tuple-element.70), channel_id=1, source_target_pairs={{0,8},{1,9},{2,10},{3,11},{4,12},{5,13},{6,14},{7,15},{8,0},{9,1},... | collective-permute-start | bytes 294920 | tf_op jit(solution)/shard_map/ppermute | solution.py:59
  15.2 7.9 %collective-permute-done.4.refs_1_ = bf16[512,768]{1,0:T(8,128)(2,1)S(1)} collective-permute-done((bf16[512,768]{1,0:T(8,128)(2,1)S(1)}, bf16[512,768]{1,0:T(8,128)(2,1)S(1)}, u32[]{:S(2)}, u32[]{:S(2)}) %collective-permute-start.4) | collective-permute-done | bytes 786464 | tf_op jit(solution)/shard_map/ppermute | solution.py:50
  23.2 3.0 %collective-permute-start.5 = (bf16[96,512]{1,0:T(8,128)(2,1)S(1)}, bf16[96,512]{1,0:T(8,128)(2,1)S(1)}, u32[]{:S(2)}, u32[]{:S(2)}) collective-permute-start(bf16[96,512]{1,0:T(8,128)(2,1)S(1)} %get-tuple-element.72), channel_id=1, source_target_pairs={{0,12},{1,13},{2,14},{3,15},{4,8},{5,9},{6,10},{7,11},{8,4},{9,5},... | collective-permute-start | bytes 294920 | tf_op jit(solution)/shard_map/ppermute | solution.py:59
  26.2 0.0 collective-permute-done.2.refs_1_
  26.2 0.0 collective-permute-done.3.refs_2_
  26.2 3.4 %collective-permute-done.5.refs_3_ = bf16[96,512]{1,0:T(8,128)(2,1)S(1)} collective-permute-done((bf16[96,512]{1,0:T(8,128)(2,1)S(1)}, bf16[96,512]{1,0:T(8,128)(2,1)S(1)}, u32[]{:S(2)}, u32[]{:S(2)}) %collective-permute-start.5) | collective-permute-done | bytes 98336 | tf_op jit(solution)/shard_map/ppermute | solution.py:59
  29.6 6.1 %collective-permute-done.6.refs_1_ = bf16[80,2048]{1,0:T(8,128)(2,1)S(1)} collective-permute-done((bf16[80,2048]{1,0:T(8,128)(2,1)S(1)}, bf16[80,2048]{1,0:T(8,128)(2,1)S(1)}, u32[]{:S(2)}, u32[]{:S(2)}) %collective-permute-start.6) | collective-permute-done | bytes 327712 | tf_op jit(solution)/shard_map/ppermute | solution.py:59
  35.7 0.0 collective-permute-done.7.refs_2_
  35.7 0.1 shard_map.107
  35.8 2.8 %collective-permute-start.10 = (bf16[80,512]{1,0:T(8,128)(2,1)S(1)}, bf16[80,512]{1,0:T(8,128)(2,1)S(1)}, u32[]{:S(2)}, u32[]{:S(2)}) collective-permute-start(bf16[80,512]{1,0:T(8,128)(2,1)S(1)} %get-tuple-element.80), channel_id=1, source_target_pairs={{0,12},{1,13},{2,14},{3,15},{4,8},{5,9},{6,10},{7,11},{8,4},{9,5},... | collective-permute-start | bytes 245768 | tf_op jit(solution)/shard_map/ppermute | solution.py:59
  38.6 1.7 %collective-permute-start.9 = (bf16[80,512]{1,0:T(8,128)(2,1)S(1)}, bf16[80,512]{1,0:T(8,128)(2,1)S(1)}, u32[]{:S(2)}, u32[]{:S(2)}) collective-permute-start(bf16[80,512]{1,0:T(8,128)(2,1)S(1)} %get-tuple-element.79), channel_id=1, source_target_pairs={{0,8},{1,9},{2,10},{3,11},{4,12},{5,13},{6,14},{7,15},{8,0},{9,1},... | collective-permute-start | bytes 245768 | tf_op jit(solution)/shard_map/ppermute | solution.py:59
  40.3 0.0 copy-start.3
  40.3 0.0 copy-start.4
  40.3 0.0 copy-start.5
  40.3 0.0 copy-start.6
  40.3 2.8 %collective-permute-start.11 = (bf16[48,512]{1,0:T(8,128)(2,1)S(1)}, bf16[48,512]{1,0:T(8,128)(2,1)S(1)}, u32[]{:S(2)}, u32[]{:S(2)}) collective-permute-start(bf16[48,512]{1,0:T(8,128)(2,1)S(1)} %get-tuple-element.85), channel_id=1, source_target_pairs={{0,2},{1,3},{2,0},{3,1},{4,6},{5,7},{6,4},{7,5},{8,10},{9,11},{10,... | collective-permute-start | bytes 147464 | tf_op jit(solution)/shard_map/ppermute | solution.py:59
  43.1 2.1 %collective-permute-done.11.refs_5_ = bf16[48,512]{1,0:T(8,128)(2,1)S(1)} collective-permute-done((bf16[48,512]{1,0:T(8,128)(2,1)S(1)}, bf16[48,512]{1,0:T(8,128)(2,1)S(1)}, u32[]{:S(2)}, u32[]{:S(2)}) %collective-permute-start.11) | collective-permute-done | bytes 49184 | tf_op jit(solution)/shard_map/ppermute | solution.py:59
  45.2 0.5 collective-permute-done.9.refs_2_
  45.7 0.1 shard_map.109
  45.8 0.8 collective-permute-start.12
  46.5 2.9 %collective-permute-start.13 = (bf16[64,512]{1,0:T(8,128)(2,1)S(1)}, bf16[64,512]{1,0:T(8,128)(2,1)S(1)}, u32[]{:S(2)}, u32[]{:S(2)}) collective-permute-start(bf16[64,512]{1,0:T(8,128)(2,1)S(1)} %get-tuple-element.93.refs_0_), channel_id=1, source_target_pairs={{0,8},{1,9},{2,10},{3,11},{4,12},{5,13},{6,14},{7,15},{8,0},{9,1},... | collective-permute-start | bytes 196616 | tf_op jit(solution)/shard_map/ppermute | solution.py:59
  49.4 0.8 collective-permute-start.14
  50.2 2.2 %collective-permute-start.15 = (bf16[64,512]{1,0:T(8,128)(2,1)S(1)}, bf16[64,512]{1,0:T(8,128)(2,1)S(1)}, u32[]{:S(2)}, u32[]{:S(2)}) collective-permute-start(bf16[64,512]{1,0:T(8,128)(2,1)S(1)} %get-tuple-element.97.refs_0_), channel_id=1, source_target_pairs={{0,2},{1,3},{2,0},{3,1},{4,6},{5,7},{6,4},{7,5},{8,10},{9,11},{10,... | collective-permute-start | bytes 196616 | tf_op jit(solution)/shard_map/ppermute | solution.py:59
  52.4 0.7 collective-permute-done.13.refs_2_
  53.1 3.2 %collective-permute-done.14.refs_3_ = bf16[64,512]{1,0:T(8,128)(2,1)S(1)} collective-permute-done((bf16[64,512]{1,0:T(8,128)(2,1)S(1)}, bf16[64,512]{1,0:T(8,128)(2,1)S(1)}, u32[]{:S(2)}, u32[]{:S(2)}) %collective-permute-start.14) | collective-permute-done | bytes 65568 | tf_op jit(solution)/shard_map/ppermute | solution.py:59
  56.3 0.1 collective-permute-start.19
  56.4 1.8 %collective-permute-start.20 = (bf16[128,512]{1,0:T(8,128)(2,1)S(1)}, bf16[128,512]{1,0:T(8,128)(2,1)S(1)}, u32[]{:S(2)}, u32[]{:S(2)}) collective-permute-start(bf16[128,512]{1,0:T(8,128)(2,1)S(1)} %shard_map.111.refs_0_), channel_id=1, source_target_pairs={{0,8},{1,9},{2,10},{3,11},{4,12},{5,13},{6,14},{7,15},{8,0},{9,1},... | collective-permute-start | bytes 393224 | tf_op jit(solution)/shard_map/ppermute | solution.py:59
  58.2 2.6 %collective-permute-start.21 = (bf16[128,512]{1,0:T(8,128)(2,1)S(1)}, bf16[128,512]{1,0:T(8,128)(2,1)S(1)}, u32[]{:S(2)}, u32[]{:S(2)}) collective-permute-start(bf16[128,512]{1,0:T(8,128)(2,1)S(1)} %shard_map.111.refs_0_), channel_id=1, source_target_pairs={{0,12},{1,13},{2,14},{3,15},{4,8},{5,9},{6,10},{7,11},{8,4},{9,5},... | collective-permute-start | bytes 393224 | tf_op jit(solution)/shard_map/ppermute | solution.py:59
  60.8 0.1 shard_map.113.refs_5_.refs_4_
  60.9 0.0 copy-start
  60.9 1.8 %collective-permute-start.17 = (bf16[64,2048]{1,0:T(8,128)(2,1)S(1)}, bf16[64,2048]{1,0:T(8,128)(2,1)S(1)}, u32[]{:S(2)}, u32[]{:S(2)}) collective-permute-start(bf16[64,2048]{1,0:T(8,128)(2,1)S(1)} %shard_map.110.refs_0_), channel_id=1, source_target_pairs={{0,2},{1,3},{2,0},{3,1},{4,6},{5,7},{6,4},{7,5},{8,10},{9,11},{10,... | collective-permute-start | bytes 786440 | tf_op jit(solution)/shard_map/ppermute | solution.py:59
  62.7 2.3 %shard_map.112 = (f32[512,768]{1,0:T(8,128)S(1)}, bf16[512,256]{1,0:T(8,128)(2,1)S(1)}) custom-call(bf16[512,768]{1,0:T(8,128)(2,1)S(1)} %copy-done.2, bf16[512,768]{1,0:T(8,128)(2,1)S(1)} %collective-permute-done.4.refs_1_, bf16[512,768]{1,0:T(8,128)(2,1)S(1)} %collective-permute-done.7.refs_2_, bf16[512,768]{1,0:T(8,128)(2,1)S(1)} %copy-done.1, ...), custom_call_target="tpu_custom_call" | custom-call | flops 235929600 | bytes 4980736 | tf_op jit(solution)/shard_map/pallas_call | solution.py:298
  65.1 0.9 collective-permute-done.20.refs_2_
  65.9 0.1 shard_map.114.refs_2_
  66.0 0.1 collective-permute-start.22
  66.1 0.5 collective-permute-start.16
  66.6 0.8 collective-permute-done.17.refs_1_
  67.4 1.5 %shard_map.115 = (f32[256,768]{1,0:T(8,128)S(1)}, f32[320,128]{1,0:T(8,128)S(1)}) custom-call(bf16[64,2048]{1,0:T(8,128)(2,1)S(1)} %shard_map.110.refs_0_, bf16[64,2048]{1,0:T(8,128)(2,1)S(1)} %collective-permute-done.17.refs_1_, bf16[128,2048]{1,0:T(8,128)(2,1)S(1)} %shard_map.114.refs_2_, bf16[2048,768]{1,0:T(8,128)(2,1)S(1)} %copy-done, ...), custom_call_target="tpu_custom_call" | custom-call | flops 905969664 | bytes 7700480 | tf_op jit(solution)/shard_map/pallas_call | solution.py:91
  68.9 1.5 %shard_map.116 = (f32[256,768]{1,0:T(8,128)S(1)}, bf16[320,128]{1,0:T(8,128)(2,1)S(1)}) custom-call(bf16[64,2048]{1,0:T(8,128)(2,1)S(1)} %collective-permute-done.16.refs_0_, bf16[64,2048]{1,0:T(8,128)(2,1)S(1)} %collective-permute-done.18.refs_1_, bf16[128,2048]{1,0:T(8,128)(2,1)S(1)} %collective-permute-done.22.refs_2_, bf16[2048,768]{1,0:T(8,128)(2,1)S(1)} %copy-done, ...), custom_call_target="tpu_custom_call" | custom-call | flops 905969664 | bytes 7618560 | tf_op jit(solution)/shard_map/pallas_call | solution.py:91
  70.4 0.6 collective-permute-start.23
  71.0 0.9 %collective-permute-done.23.refs_0_ = bf16[320,128]{1,0:T(8,128)(2,1)S(1)} collective-permute-done((bf16[320,128]{1,0:T(8,128)(2,1)S(1)}, bf16[320,128]{1,0:T(8,128)(2,1)S(1)}, u32[]{:S(2)}, u32[]{:S(2)}) %collective-permute-start.23) | collective-permute-done | bytes 81952 | tf_op jit(solution)/shard_map/ppermute | solution.py:59
  72.0 1.8 %collective-permute-start.24 = (bf16[320,128]{1,0:T(8,128)(2,1)S(1)}, bf16[320,128]{1,0:T(8,128)(2,1)S(1)}, u32[]{:S(2)}, u32[]{:S(2)}) collective-permute-start(bf16[320,128]{1,0:T(8,128)(2,1)S(1)} %get-tuple-element.118), channel_id=1, source_target_pairs={{0,2},{1,3},{2,0},{3,1},{4,6},{5,7},{6,4},{7,5},{8,10},{9,11},{10,... | collective-permute-start | bytes 245768 | tf_op jit(solution)/shard_map/ppermute | solution.py:59
  73.8 3.0 %collective-permute-done.24.refs_0_ = bf16[320,128]{1,0:T(8,128)(2,1)S(1)} collective-permute-done((bf16[320,128]{1,0:T(8,128)(2,1)S(1)}, bf16[320,128]{1,0:T(8,128)(2,1)S(1)}, u32[]{:S(2)}, u32[]{:S(2)}) %collective-permute-start.24) | collective-permute-done | bytes 81952 | tf_op jit(solution)/shard_map/ppermute | solution.py:59
  76.8 1.5 %collective-permute-start.25 = (bf16[320,128]{1,0:T(8,128)(2,1)S(1)}, bf16[320,128]{1,0:T(8,128)(2,1)S(1)}, u32[]{:S(2)}, u32[]{:S(2)}) collective-permute-start(bf16[320,128]{1,0:T(8,128)(2,1)S(1)} %get-tuple-element.120), channel_id=1, source_target_pairs={{0,4},{1,5},{2,6},{3,7},{4,0},{5,1},{6,2},{7,3},{8,12},{9,13},{10,... | collective-permute-start | bytes 245768 | tf_op jit(solution)/shard_map/ppermute | solution.py:59
  78.2 0.7 collective-permute-start.26
  78.9 2.3 %collective-permute-start.27 = (bf16[320,128]{1,0:T(8,128)(2,1)S(1)}, bf16[320,128]{1,0:T(8,128)(2,1)S(1)}, u32[]{:S(2)}, u32[]{:S(2)}) collective-permute-start(bf16[320,128]{1,0:T(8,128)(2,1)S(1)} %get-tuple-element.120), channel_id=1, source_target_pairs={{0,12},{1,13},{2,14},{3,15},{4,8},{5,9},{6,10},{7,11},{8,4},{9,5},... | collective-permute-start | bytes 245768 | tf_op jit(solution)/shard_map/ppermute | solution.py:59
  81.2 0.6 collective-permute-done.25.refs_0_
  81.9 5.1 %collective-permute-done.26.refs_1_ = bf16[320,128]{1,0:T(8,128)(2,1)S(1)} collective-permute-done((bf16[320,128]{1,0:T(8,128)(2,1)S(1)}, bf16[320,128]{1,0:T(8,128)(2,1)S(1)}, u32[]{:S(2)}, u32[]{:S(2)}) %collective-permute-start.26) | collective-permute-done | bytes 81952 | tf_op jit(solution)/shard_map/ppermute | solution.py:59
  87.0 0.1 collective-permute-start.28
  87.1 1.3 %collective-permute-done.28.refs_1_ = bf16[320,128]{1,0:T(8,128)(2,1)S(1)} collective-permute-done((bf16[320,128]{1,0:T(8,128)(2,1)S(1)}, bf16[320,128]{1,0:T(8,128)(2,1)S(1)}, u32[]{:S(2)}, u32[]{:S(2)}) %collective-permute-start.28) | collective-permute-done | bytes 81952 | tf_op jit(solution)/shard_map/ppermute | solution.py:59
  88.3 2.4 %shard_map.120 = (bf16[512,768]{1,0:T(8,128)(2,1)}, bf16[512,768]{1,0:T(8,128)(2,1)}) custom-call(bf16[320,128]{1,0:T(8,128)(2,1)S(1)} %shard_map.119.refs_0_, bf16[320,128]{1,0:T(8,128)(2,1)S(1)} %collective-permute-done.28.refs_1_, f32[256,768]{1,0:T(8,128)S(1)} %get-tuple-element.121.refs_2_, f32[256,768]{1,0:T(8,128)S(1)} %get-tuple-element.122.refs_3_, ...), custom_call_target="tpu_custom_call" | custom-call | flops 201326592 | bytes 4915200 | tf_op jit(solution)/shard_map/pallas_call | solution.py:468
  (31 shorter events, 0.3 us)
Async XLA Ops:
  0.6 5.0 %copy-start.2 = (bf16[512,768]{1,0:T(8,128)(2,1)S(1)}, bf16[512,768]{1,0:T(8,128)(2,1)}, u32[]{:S(2)}) copy-start(bf16[512,768]{1,0:T(8,128)(2,1)} %refs_5_.1) | copy-start | bytes 2359300
  5.0 1.9 %collective-permute-start.1 = (bf16[96,2048]{1,0:T(8,128)(2,1)S(1)}, bf16[96,2048]{1,0:T(8,128)(2,1)S(1)}, u32[]{:S(2)}, u32[]{:S(2)}) collective-permute-start(bf16[96,2048]{1,0:T(8,128)(2,1)S(1)} %get-tuple-element.67), channel_id=1, source_target_pairs={{0,1},{1,0},{2,3},{3,2},{4,5},{5,4},{6,7},{7,6},{8,9},{9,8},{10,11... | collective-permute-start | bytes 1179656 | tf_op jit(solution)/shard_map/ppermute | solution.py:59
  5.6 7.0 %collective-permute-start = (bf16[160,2048]{1,0:T(8,128)(2,1)S(1)}, bf16[160,2048]{1,0:T(8,128)(2,1)S(1)}, u32[]{:S(2)}, u32[]{:S(2)}) collective-permute-start(bf16[160,2048]{1,0:T(8,128)(2,1)S(1)} %get-tuple-element.64), channel_id=1, source_target_pairs={{0,1},{1,0},{2,3},{3,2},{4,5},{5,4},{6,7},{7,6},{8,9},{9,8},{10,11... | collective-permute-start | bytes 1966088 | tf_op jit(solution)/shard_map/ppermute | solution.py:59
  5.6 17.5 %collective-permute-start.4 = (bf16[512,768]{1,0:T(8,128)(2,1)S(1)}, bf16[512,768]{1,0:T(8,128)(2,1)S(1)}, u32[]{:S(2)}, u32[]{:S(2)}) collective-permute-start(bf16[512,768]{1,0:T(8,128)(2,1)S(1)} %copy-done.2), channel_id=1, source_target_pairs={{0,1},{1,2},{2,3},{3,4},{4,5},{5,6},{6,7},{7,8},{8,9},{9,10},{10,1... | collective-permute-start | bytes 2359304 | tf_op jit(solution)/shard_map/ppermute | solution.py:50
  6.9 28.8 %collective-permute-start.7 = (bf16[512,768]{1,0:T(8,128)(2,1)S(1)}, bf16[512,768]{1,0:T(8,128)(2,1)S(1)}, u32[]{:S(2)}, u32[]{:S(2)}) collective-permute-start(bf16[512,768]{1,0:T(8,128)(2,1)S(1)} %copy-done.2), channel_id=1, source_target_pairs={{0,15},{1,0},{2,1},{3,2},{4,3},{5,4},{6,5},{7,6},{8,7},{9,8},{10,9... | collective-permute-start | bytes 2359304 | tf_op jit(solution)/shard_map/ppermute | solution.py:50
  12.7 23.0 %collective-permute-start.6 = (bf16[80,2048]{1,0:T(8,128)(2,1)S(1)}, bf16[80,2048]{1,0:T(8,128)(2,1)S(1)}, u32[]{:S(2)}, u32[]{:S(2)}) collective-permute-start(bf16[80,2048]{1,0:T(8,128)(2,1)S(1)} %get-tuple-element.73), channel_id=1, source_target_pairs={{0,2},{1,3},{2,0},{3,1},{4,6},{5,7},{6,4},{7,5},{8,10},{9,11},{10,... | collective-permute-start | bytes 983048 | tf_op jit(solution)/shard_map/ppermute | solution.py:59
  12.8 48.0 %copy-start.7 = (f32[768]{0:T(1024)S(1)}, f32[768]{0:T(1024)}, u32[]{:S(2)}) copy-start(f32[768]{0:T(1024)} %param.12) | copy-start | bytes 9220
  12.8 48.0 %copy-start.8 = (f32[768]{0:T(1024)S(1)}, f32[768]{0:T(1024)}, u32[]{:S(2)}) copy-start(f32[768]{0:T(1024)} %param.13) | copy-start | bytes 9220
  12.8 48.0 %copy-start.1 = (bf16[512,768]{1,0:T(8,128)(2,1)S(1)}, bf16[512,768]{1,0:T(8,128)(2,1)}, u32[]{:S(2)}) copy-start(bf16[512,768]{1,0:T(8,128)(2,1)} %o_ref.1) | copy-start | bytes 2359300
  12.9 13.3 %collective-permute-start.2 = (bf16[96,512]{1,0:T(8,128)(2,1)S(1)}, bf16[96,512]{1,0:T(8,128)(2,1)S(1)}, u32[]{:S(2)}, u32[]{:S(2)}) collective-permute-start(bf16[96,512]{1,0:T(8,128)(2,1)S(1)} %get-tuple-element.69), channel_id=1, source_target_pairs={{0,4},{1,5},{2,6},{3,7},{4,0},{5,1},{6,2},{7,3},{8,12},{9,13},{10,... | collective-permute-start | bytes 294920 | tf_op jit(solution)/shard_map/ppermute | solution.py:59
  13.0 13.2 %collective-permute-start.3 = (bf16[96,512]{1,0:T(8,128)(2,1)S(1)}, bf16[96,512]{1,0:T(8,128)(2,1)S(1)}, u32[]{:S(2)}, u32[]{:S(2)}) collective-permute-start(bf16[96,512]{1,0:T(8,128)(2,1)S(1)} %get-tuple-element.70), channel_id=1, source_target_pairs={{0,8},{1,9},{2,10},{3,11},{4,12},{5,13},{6,14},{7,15},{8,0},{9,1},... | collective-permute-start | bytes 294920 | tf_op jit(solution)/shard_map/ppermute | solution.py:59
  23.2 6.4 %collective-permute-start.5 = (bf16[96,512]{1,0:T(8,128)(2,1)S(1)}, bf16[96,512]{1,0:T(8,128)(2,1)S(1)}, u32[]{:S(2)}, u32[]{:S(2)}) collective-permute-start(bf16[96,512]{1,0:T(8,128)(2,1)S(1)} %get-tuple-element.72), channel_id=1, source_target_pairs={{0,12},{1,13},{2,14},{3,15},{4,8},{5,9},{6,10},{7,11},{8,4},{9,5},... | collective-permute-start | bytes 294920 | tf_op jit(solution)/shard_map/ppermute | solution.py:59
  35.8 9.4 %collective-permute-start.10 = (bf16[80,512]{1,0:T(8,128)(2,1)S(1)}, bf16[80,512]{1,0:T(8,128)(2,1)S(1)}, u32[]{:S(2)}, u32[]{:S(2)}) collective-permute-start(bf16[80,512]{1,0:T(8,128)(2,1)S(1)} %get-tuple-element.80), channel_id=1, source_target_pairs={{0,12},{1,13},{2,14},{3,15},{4,8},{5,9},{6,10},{7,11},{8,4},{9,5},... | collective-permute-start | bytes 245768 | tf_op jit(solution)/shard_map/ppermute | solution.py:59
  38.6 6.6 %collective-permute-start.8 = (bf16[80,512]{1,0:T(8,128)(2,1)S(1)}, bf16[80,512]{1,0:T(8,128)(2,1)S(1)}, u32[]{:S(2)}, u32[]{:S(2)}) collective-permute-start(bf16[80,512]{1,0:T(8,128)(2,1)S(1)} %get-tuple-element.78), channel_id=1, source_target_pairs={{0,4},{1,5},{2,6},{3,7},{4,0},{5,1},{6,2},{7,3},{8,12},{9,13},{10,... | collective-permute-start | bytes 245768 | tf_op jit(solution)/shard_map/ppermute | solution.py:59
  38.6 7.1 %collective-permute-start.9 = (bf16[80,512]{1,0:T(8,128)(2,1)S(1)}, bf16[80,512]{1,0:T(8,128)(2,1)S(1)}, u32[]{:S(2)}, u32[]{:S(2)}) collective-permute-start(bf16[80,512]{1,0:T(8,128)(2,1)S(1)} %get-tuple-element.79), channel_id=1, source_target_pairs={{0,8},{1,9},{2,10},{3,11},{4,12},{5,13},{6,14},{7,15},{8,0},{9,1},... | collective-permute-start | bytes 245768 | tf_op jit(solution)/shard_map/ppermute | solution.py:59
  40.3 22.4 %copy-start.3 = (bf16[2,128,128]{2,1,0:T(8,128)(2,1)S(1)}, bf16[2,128,128]{2,1,0:T(8,128)(2,1)}, u32[]{:S(2)}) copy-start(bf16[2,128,128]{2,1,0:T(8,128)(2,1)} %constant.2.clone.refs_4_) | copy-start | bytes 196612
  40.3 22.4 %copy-start.4 = (f32[512]{0:T(512)S(1)}, f32[512]{0:T(512)}, u32[]{:S(2)}) copy-start(f32[512]{0:T(512)} %param.14) | copy-start | bytes 6148
  40.3 22.4 %copy-start.5 = (s32[512]{0:T(512)S(1)}, s32[512]{0:T(512)}, u32[]{:S(2)}) copy-start(s32[512]{0:T(512)} %param.15) | copy-start | bytes 6148
  40.3 22.4 %copy-start.6 = (s32[512]{0:T(512)S(1)}, s32[512]{0:T(512)}, u32[]{:S(2)}) copy-start(s32[512]{0:T(512)} %param.16) | copy-start | bytes 6148
  40.3 4.8 %collective-permute-start.11 = (bf16[48,512]{1,0:T(8,128)(2,1)S(1)}, bf16[48,512]{1,0:T(8,128)(2,1)S(1)}, u32[]{:S(2)}, u32[]{:S(2)}) collective-permute-start(bf16[48,512]{1,0:T(8,128)(2,1)S(1)} %get-tuple-element.85), channel_id=1, source_target_pairs={{0,2},{1,3},{2,0},{3,1},{4,6},{5,7},{6,4},{7,5},{8,10},{9,11},{10,... | collective-permute-start | bytes 147464 | tf_op jit(solution)/shard_map/ppermute | solution.py:59
  45.8 6.6 %collective-permute-start.12 = (bf16[64,512]{1,0:T(8,128)(2,1)S(1)}, bf16[64,512]{1,0:T(8,128)(2,1)S(1)}, u32[]{:S(2)}, u32[]{:S(2)}) collective-permute-start(bf16[64,512]{1,0:T(8,128)(2,1)S(1)} %get-tuple-element.93.refs_0_), channel_id=1, source_target_pairs={{0,4},{1,5},{2,6},{3,7},{4,0},{5,1},{6,2},{7,3},{8,12},{9,13},{10,... | collective-permute-start | bytes 196616 | tf_op jit(solution)/shard_map/ppermute | solution.py:59
  46.5 6.6 %collective-permute-start.13 = (bf16[64,512]{1,0:T(8,128)(2,1)S(1)}, bf16[64,512]{1,0:T(8,128)(2,1)S(1)}, u32[]{:S(2)}, u32[]{:S(2)}) collective-permute-start(bf16[64,512]{1,0:T(8,128)(2,1)S(1)} %get-tuple-element.93.refs_0_), channel_id=1, source_target_pairs={{0,8},{1,9},{2,10},{3,11},{4,12},{5,13},{6,14},{7,15},{8,0},{9,1},... | collective-permute-start | bytes 196616 | tf_op jit(solution)/shard_map/ppermute | solution.py:59
  49.4 6.9 %collective-permute-start.14 = (bf16[64,512]{1,0:T(8,128)(2,1)S(1)}, bf16[64,512]{1,0:T(8,128)(2,1)S(1)}, u32[]{:S(2)}, u32[]{:S(2)}) collective-permute-start(bf16[64,512]{1,0:T(8,128)(2,1)S(1)} %get-tuple-element.93.refs_0_), channel_id=1, source_target_pairs={{0,12},{1,13},{2,14},{3,15},{4,8},{5,9},{6,10},{7,11},{8,4},{9,5},... | collective-permute-start | bytes 196616 | tf_op jit(solution)/shard_map/ppermute | solution.py:59
  50.2 6.1 %collective-permute-start.15 = (bf16[64,512]{1,0:T(8,128)(2,1)S(1)}, bf16[64,512]{1,0:T(8,128)(2,1)S(1)}, u32[]{:S(2)}, u32[]{:S(2)}) collective-permute-start(bf16[64,512]{1,0:T(8,128)(2,1)S(1)} %get-tuple-element.97.refs_0_), channel_id=1, source_target_pairs={{0,2},{1,3},{2,0},{3,1},{4,6},{5,7},{6,4},{7,5},{8,10},{9,11},{10,... | collective-permute-start | bytes 196616 | tf_op jit(solution)/shard_map/ppermute | solution.py:59
  56.3 8.7 %collective-permute-start.19 = (bf16[128,512]{1,0:T(8,128)(2,1)S(1)}, bf16[128,512]{1,0:T(8,128)(2,1)S(1)}, u32[]{:S(2)}, u32[]{:S(2)}) collective-permute-start(bf16[128,512]{1,0:T(8,128)(2,1)S(1)} %shard_map.111.refs_0_), channel_id=1, source_target_pairs={{0,4},{1,5},{2,6},{3,7},{4,0},{5,1},{6,2},{7,3},{8,12},{9,13},{10,... | collective-permute-start | bytes 393224 | tf_op jit(solution)/shard_map/ppermute | solution.py:59
  56.4 9.5 %collective-permute-start.20 = (bf16[128,512]{1,0:T(8,128)(2,1)S(1)}, bf16[128,512]{1,0:T(8,128)(2,1)S(1)}, u32[]{:S(2)}, u32[]{:S(2)}) collective-permute-start(bf16[128,512]{1,0:T(8,128)(2,1)S(1)} %shard_map.111.refs_0_), channel_id=1, source_target_pairs={{0,8},{1,9},{2,10},{3,11},{4,12},{5,13},{6,14},{7,15},{8,0},{9,1},... | collective-permute-start | bytes 393224 | tf_op jit(solution)/shard_map/ppermute | solution.py:59
  58.2 7.8 %collective-permute-start.21 = (bf16[128,512]{1,0:T(8,128)(2,1)S(1)}, bf16[128,512]{1,0:T(8,128)(2,1)S(1)}, u32[]{:S(2)}, u32[]{:S(2)}) collective-permute-start(bf16[128,512]{1,0:T(8,128)(2,1)S(1)} %shard_map.111.refs_0_), channel_id=1, source_target_pairs={{0,12},{1,13},{2,14},{3,15},{4,8},{5,9},{6,10},{7,11},{8,4},{9,5},... | collective-permute-start | bytes 393224 | tf_op jit(solution)/shard_map/ppermute | solution.py:59
  60.9 6.5 %copy-start = (bf16[2048,768]{1,0:T(8,128)(2,1)S(1)}, bf16[2048,768]{1,0:T(8,128)(2,1)}, u32[]{:S(2)}) copy-start(bf16[2048,768]{1,0:T(8,128)(2,1)} %refs_3_.5) | copy-start | bytes 9437188
  60.9 6.4 %collective-permute-start.17 = (bf16[64,2048]{1,0:T(8,128)(2,1)S(1)}, bf16[64,2048]{1,0:T(8,128)(2,1)S(1)}, u32[]{:S(2)}, u32[]{:S(2)}) collective-permute-start(bf16[64,2048]{1,0:T(8,128)(2,1)S(1)} %shard_map.110.refs_0_), channel_id=1, source_target_pairs={{0,2},{1,3},{2,0},{3,1},{4,6},{5,7},{6,4},{7,5},{8,10},{9,11},{10,... | collective-permute-start | bytes 786440 | tf_op jit(solution)/shard_map/ppermute | solution.py:59
  66.0 2.9 %collective-permute-start.22 = (bf16[128,2048]{1,0:T(8,128)(2,1)S(1)}, bf16[128,2048]{1,0:T(8,128)(2,1)S(1)}, u32[]{:S(2)}, u32[]{:S(2)}) collective-permute-start(bf16[128,2048]{1,0:T(8,128)(2,1)S(1)} %shard_map.114.refs_2_), channel_id=1, source_target_pairs={{0,1},{1,0},{2,3},{3,2},{4,5},{5,4},{6,7},{7,6},{8,9},{9,8},{10,11... | collective-permute-start | bytes 1572872 | tf_op jit(solution)/shard_map/ppermute | solution.py:59
  66.1 2.8 %collective-permute-start.16 = (bf16[64,2048]{1,0:T(8,128)(2,1)S(1)}, bf16[64,2048]{1,0:T(8,128)(2,1)S(1)}, u32[]{:S(2)}, u32[]{:S(2)}) collective-permute-start(bf16[64,2048]{1,0:T(8,128)(2,1)S(1)} %shard_map.110.refs_0_), channel_id=1, source_target_pairs={{0,1},{1,0},{2,3},{3,2},{4,5},{5,4},{6,7},{7,6},{8,9},{9,8},{10,11... | collective-permute-start | bytes 786440 | tf_op jit(solution)/shard_map/ppermute | solution.py:59
  67.4 1.5 %collective-permute-start.18 = (bf16[64,2048]{1,0:T(8,128)(2,1)S(1)}, bf16[64,2048]{1,0:T(8,128)(2,1)S(1)}, u32[]{:S(2)}, u32[]{:S(2)}) collective-permute-start(bf16[64,2048]{1,0:T(8,128)(2,1)S(1)} %collective-permute-done.17.refs_1_), channel_id=1, source_target_pairs={{0,1},{1,0},{2,3},{3,2},{4,5},{5,4},{6,7},{7,6},{8,9},{9,8},{10,11... | collective-permute-start | bytes 786440 | tf_op jit(solution)/shard_map/ppermute | solution.py:59
  70.4 1.5 %collective-permute-start.23 = (bf16[320,128]{1,0:T(8,128)(2,1)S(1)}, bf16[320,128]{1,0:T(8,128)(2,1)S(1)}, u32[]{:S(2)}, u32[]{:S(2)}) collective-permute-start(bf16[320,128]{1,0:T(8,128)(2,1)S(1)} %get-tuple-element.116), channel_id=1, source_target_pairs={{0,1},{1,0},{2,3},{3,2},{4,5},{5,4},{6,7},{7,6},{8,9},{9,8},{10,11... | collective-permute-start | bytes 245768 | tf_op jit(solution)/shard_map/ppermute | solution.py:59
  72.0 4.8 %collective-permute-start.24 = (bf16[320,128]{1,0:T(8,128)(2,1)S(1)}, bf16[320,128]{1,0:T(8,128)(2,1)S(1)}, u32[]{:S(2)}, u32[]{:S(2)}) collective-permute-start(bf16[320,128]{1,0:T(8,128)(2,1)S(1)} %get-tuple-element.118), channel_id=1, source_target_pairs={{0,2},{1,3},{2,0},{3,1},{4,6},{5,7},{6,4},{7,5},{8,10},{9,11},{10,... | collective-permute-start | bytes 245768 | tf_op jit(solution)/shard_map/ppermute | solution.py:59
  76.8 5.1 %collective-permute-start.25 = (bf16[320,128]{1,0:T(8,128)(2,1)S(1)}, bf16[320,128]{1,0:T(8,128)(2,1)S(1)}, u32[]{:S(2)}, u32[]{:S(2)}) collective-permute-start(bf16[320,128]{1,0:T(8,128)(2,1)S(1)} %get-tuple-element.120), channel_id=1, source_target_pairs={{0,4},{1,5},{2,6},{3,7},{4,0},{5,1},{6,2},{7,3},{8,12},{9,13},{10,... | collective-permute-start | bytes 245768 | tf_op jit(solution)/shard_map/ppermute | solution.py:59
  78.2 8.7 %collective-permute-start.26 = (bf16[320,128]{1,0:T(8,128)(2,1)S(1)}, bf16[320,128]{1,0:T(8,128)(2,1)S(1)}, u32[]{:S(2)}, u32[]{:S(2)}) collective-permute-start(bf16[320,128]{1,0:T(8,128)(2,1)S(1)} %get-tuple-element.120), channel_id=1, source_target_pairs={{0,8},{1,9},{2,10},{3,11},{4,12},{5,13},{6,14},{7,15},{8,0},{9,1},... | collective-permute-start | bytes 245768 | tf_op jit(solution)/shard_map/ppermute | solution.py:59
  78.9 8.0 %collective-permute-start.27 = (bf16[320,128]{1,0:T(8,128)(2,1)S(1)}, bf16[320,128]{1,0:T(8,128)(2,1)S(1)}, u32[]{:S(2)}, u32[]{:S(2)}) collective-permute-start(bf16[320,128]{1,0:T(8,128)(2,1)S(1)} %get-tuple-element.120), channel_id=1, source_target_pairs={{0,12},{1,13},{2,14},{3,15},{4,8},{5,9},{6,10},{7,11},{8,4},{9,5},... | collective-permute-start | bytes 245768 | tf_op jit(solution)/shard_map/ppermute | solution.py:59
  87.0 1.3 %collective-permute-start.28 = (bf16[320,128]{1,0:T(8,128)(2,1)S(1)}, bf16[320,128]{1,0:T(8,128)(2,1)S(1)}, u32[]{:S(2)}, u32[]{:S(2)}) collective-permute-start(bf16[320,128]{1,0:T(8,128)(2,1)S(1)} %shard_map.119.refs_0_), channel_id=1, source_target_pairs={{0,1},{1,0},{2,3},{3,2},{4,5},{5,4},{6,7},{7,6},{8,9},{9,8},{10,11... | collective-permute-start | bytes 245768 | tf_op jit(solution)/shard_map/ppermute | solution.py:59

commit v13 on v12

--- a/solution.py
+++ b/solution.py
@@ -28,7 +28,7 @@
 STEP_SIZE = 0.3
 MIB = 1024 * 1024
 VMEM_BYTES = 24 * MIB
-REDUCE_SHARE = 0.625
+REDUCE_SHARE = 0.5
 GATHER_SHARE = 0.5
 BF16 = jnp.bfloat16
 F32 = jnp.float32
@@ -514,13 +514,13 @@
         return [swapped(part, count, level, k + 1) for k, part in enumerate(parts)]
 
     low = neighbour(response[:, local_cells - halo :], count, 1)
+    high = neighbour(response[:, :halo], count, -1)
 
     sent_x, sent_z, keep_x, keep_z = first_sums(response, projectors, core, block, first)
     sent_z = swapped(sent_z, count, core, 1)
     sent_x = swapped(sent_x, count, core, 1)
-    head, sent_z = lax.optimization_barrier((response[:, :halo], sent_z))
-    high = neighbour(head, count, -1)
     keep_z, *parts_z = split(keep_z, [sent_z], along, 1)
+    sent_x, parts_z[0] = lax.optimization_barrier((sent_x, parts_z[0]))
     keep_x, *parts_x = split(keep_x, [sent_x], across, 0)
     parts_z[-1], low = lax.optimization_barrier((parts_z[-1], low))
     taken_z, taken_x, low, high = lax.optimization_barrier(

time: 90.9 us -> 86.9 us (0.956)
  starting transfers between devices: 39.6 us -> 37.4 us
  waiting for transfers between devices: 37.4 us -> 35.6 us
    ppermute x2, waiting for transfers between devices: 7.93 us -> 1.06 us  [neighbour(): lax.ppermute(array, 'band', [(i, (i + step) % count) for i in range(count)])]
    ppermute x27, waiting for transfers between devices: 29.4 us -> 34.5 us  [swapped(): return lax.ppermute(array, 'band', pairs)]
    ppermute x2, starting transfers between devices: 6.07 us -> 3.62 us  [neighbour(): lax.ppermute(array, 'band', [(i, (i + step) % count) for i in range(count)])]
  transfers between devices with their start and end apart: 29 -> 29, of which waited for: 15 -> 15; matrix products, arithmetic and copies ran while one was open for 0% -> 0% of each run, Pallas kernels for 5% -> 10%
where the time goes in v13:
time: 86.9 us; the launch traced here: 86.8 us
  starting transfers between devices  37.4 us (43%)
  waiting for transfers between devices  35.6 us (41%)
  Pallas kernels  12.8 us (15%)
  between operations  0.92 us (1%)
    ppermute x27, waiting for transfers between devices, swapped(): return lax.ppermute(array, 'band', pairs)  34.5 us
    ppermute x27, starting transfers between devices, swapped(): return lax.ppermute(array, 'band', pairs)  33.8 us
    pallas_call x1, Pallas kernels, first_sums(): pl.pallas_call(functools.partial(first_body, core, block, tile), out_shap...  4.34 us
    pallas_call x14, Pallas kernels, local_call(): pl.pallas_call(body, out_shape=outs, in_specs=[whole() for _ in args], ou...  3.73 us
    ppermute x2, starting transfers between devices, neighbour(): lax.ppermute(array, 'band', [(i, (i + step) % count) for i in range(count)])  3.62 us
    pallas_call x1, Pallas kernels, project(): pl.pallas_call(functools.partial(project_body, core, blk), grid=(bands //...  2.43 us
    pallas_call x1, Pallas kernels, local_part(): pl.pallas_call(functools.partial(local_body, depth, (group_rows, blk)), g...  2.3 us
  transfers between devices with their start and end apart: 29, of which 15 were waited for; matrix products, arithmetic and copies ran while one was open for 0% of the time, Pallas kernels for 10%

profile of v13, /device:TPU:0, one launch (start us, length us, event | category | flops | bytes accessed | tf_op | source)
XLA Modules:
  0.0 86.8 jit_solution(18238754605873579837)
XLA Ops:
  0.6 0.5 collective-permute-start.4
  1.1 4.3 %shard_map.104 = (bf16[128,2048]{1,0:T(8,128)(2,1)S(1)}, bf16[128,2048]{1,0:T(8,128)(2,1)S(1)}, f32[128,2048]{1,0:T(8,128)S(1)}, f32[128,2048]{1,0:T(8,128)S(1)}) custom-call(bf16[512,768]{1,0:T(8,128)(2,1)} %refs_5_.1, bf16[2048,768]{1,0:T(8,128)(2,1)} %refs_3_.5), custom_call_target="tpu_custom_call" | custom-call | flops 1610612736 | bytes 6291456 | tf_op jit(solution)/shard_map/pallas_call | solution.py:147
  5.5 0.0 copy-start.7
  5.5 0.0 copy-start.8
  5.5 0.0 copy-start.1
  5.5 2.6 %collective-permute-start.1 = (bf16[128,2048]{1,0:T(8,128)(2,1)S(1)}, bf16[128,2048]{1,0:T(8,128)(2,1)S(1)}, u32[]{:S(2)}, u32[]{:S(2)}) collective-permute-start(bf16[128,2048]{1,0:T(8,128)(2,1)S(1)} %get-tuple-element.66), channel_id=1, source_target_pairs={{0,1},{1,0},{2,3},{3,2},{4,5},{5,4},{6,7},{7,6},{8,9},{9,8},{10,11... | collective-permute-start | bytes 1572872 | tf_op jit(solution)/shard_map/ppermute | solution.py:59
  8.2 0.1 collective-permute-start
  8.2 3.1 %collective-permute-start.7 = (bf16[512,768]{1,0:T(8,128)(2,1)S(1)}, bf16[512,768]{1,0:T(8,128)(2,1)S(1)}, u32[]{:S(2)}, u32[]{:S(2)}) collective-permute-start(bf16[512,768]{1,0:T(8,128)(2,1)S(1)} %copy-done.2), channel_id=1, source_target_pairs={{0,15},{1,0},{2,1},{3,2},{4,3},{5,4},{6,5},{7,6},{8,7},{9,8},{10,9... | collective-permute-start | bytes 2359304 | tf_op jit(solution)/shard_map/ppermute | solution.py:50
  11.4 0.0 collective-permute-done.1.refs_1_
  11.4 0.1 shard_map.105
  11.5 0.0 copy-start.3
  11.5 0.0 copy-start.4
  11.5 0.0 copy-start.5
  11.5 0.0 copy-start.6
  11.5 0.1 shard_map.106
  11.7 0.5 collective-permute-start.6
  12.2 1.6 %collective-permute-start.2 = (bf16[128,512]{1,0:T(8,128)(2,1)S(1)}, bf16[128,512]{1,0:T(8,128)(2,1)S(1)}, u32[]{:S(2)}, u32[]{:S(2)}) collective-permute-start(bf16[128,512]{1,0:T(8,128)(2,1)S(1)} %get-tuple-element.70), channel_id=1, source_target_pairs={{0,4},{1,5},{2,6},{3,7},{4,0},{5,1},{6,2},{7,3},{8,12},{9,13},{10,... | collective-permute-start | bytes 393224 | tf_op jit(solution)/shard_map/ppermute | solution.py:59
  13.8 1.4 %collective-permute-start.3 = (bf16[128,512]{1,0:T(8,128)(2,1)S(1)}, bf16[128,512]{1,0:T(8,128)(2,1)S(1)}, u32[]{:S(2)}, u32[]{:S(2)}) collective-permute-start(bf16[128,512]{1,0:T(8,128)(2,1)S(1)} %get-tuple-element.71), channel_id=1, source_target_pairs={{0,8},{1,9},{2,10},{3,11},{4,12},{5,13},{6,14},{7,15},{8,0},{9,1},... | collective-permute-start | bytes 393224 | tf_op jit(solution)/shard_map/ppermute | solution.py:59
  15.1 1.1 %collective-permute-done.4.refs_1_ = bf16[512,768]{1,0:T(8,128)(2,1)S(1)} collective-permute-done((bf16[512,768]{1,0:T(8,128)(2,1)}, bf16[512,768]{1,0:T(8,128)(2,1)S(1)}, u32[]{:S(2)}, u32[]{:S(2)}) %collective-permute-start.4) | collective-permute-done | bytes 786464 | tf_op jit(solution)/shard_map/ppermute | solution.py:50
  16.2 2.2 %collective-permute-start.5 = (bf16[128,512]{1,0:T(8,128)(2,1)S(1)}, bf16[128,512]{1,0:T(8,128)(2,1)S(1)}, u32[]{:S(2)}, u32[]{:S(2)}) collective-permute-start(bf16[128,512]{1,0:T(8,128)(2,1)S(1)} %get-tuple-element.73), channel_id=1, source_target_pairs={{0,12},{1,13},{2,14},{3,15},{4,8},{5,9},{6,10},{7,11},{8,4},{9,5},... | collective-permute-start | bytes 393224 | tf_op jit(solution)/shard_map/ppermute | solution.py:59
  18.4 8.6 %collective-permute-done.2.refs_1_ = bf16[128,512]{1,0:T(8,128)(2,1)S(1)} collective-permute-done((bf16[128,512]{1,0:T(8,128)(2,1)S(1)}, bf16[128,512]{1,0:T(8,128)(2,1)S(1)}, u32[]{:S(2)}, u32[]{:S(2)}) %collective-permute-start.2) | collective-permute-done | bytes 131104 | tf_op jit(solution)/shard_map/ppermute | solution.py:59
  26.9 5.2 %collective-permute-done.3.refs_2_ = bf16[128,512]{1,0:T(8,128)(2,1)S(1)} collective-permute-done((bf16[128,512]{1,0:T(8,128)(2,1)S(1)}, bf16[128,512]{1,0:T(8,128)(2,1)S(1)}, u32[]{:S(2)}, u32[]{:S(2)}) %collective-permute-start.3) | collective-permute-done | bytes 131104 | tf_op jit(solution)/shard_map/ppermute | solution.py:59
  32.1 0.0 collective-permute-done.7.refs_2_
  32.2 0.1 shard_map.108
  32.2 0.1 collective-permute-start.11
  32.3 0.1 shard_map.107
  32.4 2.7 %collective-permute-start.10 = (bf16[64,512]{1,0:T(8,128)(2,1)S(1)}, bf16[64,512]{1,0:T(8,128)(2,1)S(1)}, u32[]{:S(2)}, u32[]{:S(2)}) collective-permute-start(bf16[64,512]{1,0:T(8,128)(2,1)S(1)} %get-tuple-element.80), channel_id=1, source_target_pairs={{0,12},{1,13},{2,14},{3,15},{4,8},{5,9},{6,10},{7,11},{8,4},{9,5},... | collective-permute-start | bytes 196616 | tf_op jit(solution)/shard_map/ppermute | solution.py:59
  35.1 1.8 %collective-permute-start.8 = (bf16[64,512]{1,0:T(8,128)(2,1)S(1)}, bf16[64,512]{1,0:T(8,128)(2,1)S(1)}, u32[]{:S(2)}, u32[]{:S(2)}) collective-permute-start(bf16[64,512]{1,0:T(8,128)(2,1)S(1)} %get-tuple-element.78), channel_id=1, source_target_pairs={{0,4},{1,5},{2,6},{3,7},{4,0},{5,1},{6,2},{7,3},{8,12},{9,13},{10,... | collective-permute-start | bytes 196616 | tf_op jit(solution)/shard_map/ppermute | solution.py:59
  37.0 2.1 %collective-permute-done.10.refs_3_ = bf16[64,512]{1,0:T(8,128)(2,1)S(1)} collective-permute-done((bf16[64,512]{1,0:T(8,128)(2,1)S(1)}, bf16[64,512]{1,0:T(8,128)(2,1)S(1)}, u32[]{:S(2)}, u32[]{:S(2)}) %collective-permute-start.10) | collective-permute-done | bytes 65568 | tf_op jit(solution)/shard_map/ppermute | solution.py:59
  39.0 0.5 collective-permute-done.8.refs_1_
  39.6 2.8 %collective-permute-done.9.refs_2_ = bf16[64,512]{1,0:T(8,128)(2,1)S(1)} collective-permute-done((bf16[64,512]{1,0:T(8,128)(2,1)S(1)}, bf16[64,512]{1,0:T(8,128)(2,1)S(1)}, u32[]{:S(2)}, u32[]{:S(2)}) %collective-permute-start.9) | collective-permute-done | bytes 65568 | tf_op jit(solution)/shard_map/ppermute | solution.py:59
  42.4 0.1 shard_map.109
  42.5 0.1 collective-permute-start.12
  42.6 2.8 %collective-permute-start.13 = (bf16[64,512]{1,0:T(8,128)(2,1)S(1)}, bf16[64,512]{1,0:T(8,128)(2,1)S(1)}, u32[]{:S(2)}, u32[]{:S(2)}) collective-permute-start(bf16[64,512]{1,0:T(8,128)(2,1)S(1)} %get-tuple-element.93.refs_0_), channel_id=1, source_target_pairs={{0,8},{1,9},{2,10},{3,11},{4,12},{5,13},{6,14},{7,15},{8,0},{9,1},... | collective-permute-start | bytes 196616 | tf_op jit(solution)/shard_map/ppermute | solution.py:59
  45.4 1.5 %collective-permute-start.14 = (bf16[64,512]{1,0:T(8,128)(2,1)S(1)}, bf16[64,512]{1,0:T(8,128)(2,1)S(1)}, u32[]{:S(2)}, u32[]{:S(2)}) collective-permute-start(bf16[64,512]{1,0:T(8,128)(2,1)S(1)} %get-tuple-element.93.refs_0_), channel_id=1, source_target_pairs={{0,12},{1,13},{2,14},{3,15},{4,8},{5,9},{6,10},{7,11},{8,4},{9,5},... | collective-permute-start | bytes 196616 | tf_op jit(solution)/shard_map/ppermute | solution.py:59
  47.0 2.0 %collective-permute-start.15 = (bf16[64,512]{1,0:T(8,128)(2,1)S(1)}, bf16[64,512]{1,0:T(8,128)(2,1)S(1)}, u32[]{:S(2)}, u32[]{:S(2)}) collective-permute-start(bf16[64,512]{1,0:T(8,128)(2,1)S(1)} %get-tuple-element.97.refs_0_), channel_id=1, source_target_pairs={{0,2},{1,3},{2,0},{3,1},{4,6},{5,7},{6,4},{7,5},{8,10},{9,11},{10,... | collective-permute-start | bytes 196616 | tf_op jit(solution)/shard_map/ppermute | solution.py:59
  49.0 0.3 collective-permute-done.13.refs_2_
  49.2 2.7 %collective-permute-done.14.refs_3_ = bf16[64,512]{1,0:T(8,128)(2,1)S(1)} collective-permute-done((bf16[64,512]{1,0:T(8,128)(2,1)S(1)}, bf16[64,512]{1,0:T(8,128)(2,1)S(1)}, u32[]{:S(2)}, u32[]{:S(2)}) %collective-permute-start.14) | collective-permute-done | bytes 65568 | tf_op jit(solution)/shard_map/ppermute | solution.py:59
  51.9 0.1 collective-permute-start.19
  52.0 2.1 %collective-permute-start.20 = (bf16[128,512]{1,0:T(8,128)(2,1)S(1)}, bf16[128,512]{1,0:T(8,128)(2,1)S(1)}, u32[]{:S(2)}, u32[]{:S(2)}) collective-permute-start(bf16[128,512]{1,0:T(8,128)(2,1)S(1)} %shard_map.111.refs_0_), channel_id=1, source_target_pairs={{0,8},{1,9},{2,10},{3,11},{4,12},{5,13},{6,14},{7,15},{8,0},{9,1},... | collective-permute-start | bytes 393224 | tf_op jit(solution)/shard_map/ppermute | solution.py:59
  54.1 2.2 %collective-permute-start.21 = (bf16[128,512]{1,0:T(8,128)(2,1)S(1)}, bf16[128,512]{1,0:T(8,128)(2,1)S(1)}, u32[]{:S(2)}, u32[]{:S(2)}) collective-permute-start(bf16[128,512]{1,0:T(8,128)(2,1)S(1)} %shard_map.111.refs_0_), channel_id=1, source_target_pairs={{0,12},{1,13},{2,14},{3,15},{4,8},{5,9},{6,10},{7,11},{8,4},{9,5},... | collective-permute-start | bytes 393224 | tf_op jit(solution)/shard_map/ppermute | solution.py:59
  56.4 0.0 copy-start
  56.4 0.1 shard_map.113.refs_5_.refs_4_
  56.5 2.2 %collective-permute-start.17 = (bf16[64,2048]{1,0:T(8,128)(2,1)S(1)}, bf16[64,2048]{1,0:T(8,128)(2,1)S(1)}, u32[]{:S(2)}, u32[]{:S(2)}) collective-permute-start(bf16[64,2048]{1,0:T(8,128)(2,1)S(1)} %shard_map.110.refs_0_), channel_id=1, source_target_pairs={{0,2},{1,3},{2,0},{3,1},{4,6},{5,7},{6,4},{7,5},{8,10},{9,11},{10,... | collective-permute-start | bytes 786440 | tf_op jit(solution)/shard_map/ppermute | solution.py:59
  58.7 2.3 %shard_map.112 = (f32[512,768]{1,0:T(8,128)S(1)}, bf16[512,256]{1,0:T(8,128)(2,1)S(1)}) custom-call(bf16[512,768]{1,0:T(8,128)(2,1)S(1)} %copy-done.2, bf16[512,768]{1,0:T(8,128)(2,1)S(1)} %collective-permute-done.4.refs_1_, bf16[512,768]{1,0:T(8,128)(2,1)S(1)} %collective-permute-done.7.refs_2_, bf16[512,768]{1,0:T(8,128)(2,1)S(1)} %copy-done.1, ...), custom_call_target="tpu_custom_call" | custom-call | flops 235929600 | bytes 4980736 | tf_op jit(solution)/shard_map/pallas_call | solution.py:298
  61.0 0.7 collective-permute-done.20.refs_2_
  61.7 0.1 shard_map.114.refs_2_
  61.8 0.1 collective-permute-start.22
  61.8 0.5 collective-permute-start.16
  62.3 0.7 collective-permute-done.17.refs_1_
  63.0 1.5 %shard_map.115 = (f32[256,768]{1,0:T(8,128)S(1)}, f32[320,128]{1,0:T(8,128)S(1)}) custom-call(bf16[64,2048]{1,0:T(8,128)(2,1)S(1)} %shard_map.110.refs_0_, bf16[64,2048]{1,0:T(8,128)(2,1)S(1)} %collective-permute-done.17.refs_1_, bf16[128,2048]{1,0:T(8,128)(2,1)S(1)} %shard_map.114.refs_2_, bf16[2048,768]{1,0:T(8,128)(2,1)S(1)} %copy-done, ...), custom_call_target="tpu_custom_call" | custom-call | flops 905969664 | bytes 7700480 | tf_op jit(solution)/shard_map/pallas_call | solution.py:91
  64.6 1.5 %shard_map.116 = (f32[256,768]{1,0:T(8,128)S(1)}, bf16[320,128]{1,0:T(8,128)(2,1)S(1)}) custom-call(bf16[64,2048]{1,0:T(8,128)(2,1)S(1)} %collective-permute-done.16.refs_0_, bf16[64,2048]{1,0:T(8,128)(2,1)S(1)} %collective-permute-done.18.refs_1_, bf16[128,2048]{1,0:T(8,128)(2,1)S(1)} %collective-permute-done.22.refs_2_, bf16[2048,768]{1,0:T(8,128)(2,1)S(1)} %copy-done, ...), custom_call_target="tpu_custom_call" | custom-call | flops 905969664 | bytes 7618560 | tf_op jit(solution)/shard_map/pallas_call | solution.py:91
  66.1 0.6 collective-permute-start.23
  66.7 0.9 %collective-permute-done.23.refs_0_ = bf16[320,128]{1,0:T(8,128)(2,1)S(1)} collective-permute-done((bf16[320,128]{1,0:T(8,128)(2,1)S(1)}, bf16[320,128]{1,0:T(8,128)(2,1)S(1)}, u32[]{:S(2)}, u32[]{:S(2)}) %collective-permute-start.23) | collective-permute-done | bytes 81952 | tf_op jit(solution)/shard_map/ppermute | solution.py:59
  67.6 2.1 %collective-permute-start.24 = (bf16[320,128]{1,0:T(8,128)(2,1)S(1)}, bf16[320,128]{1,0:T(8,128)(2,1)S(1)}, u32[]{:S(2)}, u32[]{:S(2)}) collective-permute-start(bf16[320,128]{1,0:T(8,128)(2,1)S(1)} %get-tuple-element.118), channel_id=1, source_target_pairs={{0,2},{1,3},{2,0},{3,1},{4,6},{5,7},{6,4},{7,5},{8,10},{9,11},{10,... | collective-permute-start | bytes 245768 | tf_op jit(solution)/shard_map/ppermute | solution.py:59
  69.7 3.0 %collective-permute-done.24.refs_0_ = bf16[320,128]{1,0:T(8,128)(2,1)S(1)} collective-permute-done((bf16[320,128]{1,0:T(8,128)(2,1)S(1)}, bf16[320,128]{1,0:T(8,128)(2,1)S(1)}, u32[]{:S(2)}, u32[]{:S(2)}) %collective-permute-start.24) | collective-permute-done | bytes 81952 | tf_op jit(solution)/shard_map/ppermute | solution.py:59
  72.7 1.4 %collective-permute-start.25 = (bf16[320,128]{1,0:T(8,128)(2,1)S(1)}, bf16[320,128]{1,0:T(8,128)(2,1)S(1)}, u32[]{:S(2)}, u32[]{:S(2)}) collective-permute-start(bf16[320,128]{1,0:T(8,128)(2,1)S(1)} %get-tuple-element.120), channel_id=1, source_target_pairs={{0,4},{1,5},{2,6},{3,7},{4,0},{5,1},{6,2},{7,3},{8,12},{9,13},{10,... | collective-permute-start | bytes 245768 | tf_op jit(solution)/shard_map/ppermute | solution.py:59
  74.1 0.6 collective-permute-start.26
  74.8 2.4 %collective-permute-start.27 = (bf16[320,128]{1,0:T(8,128)(2,1)S(1)}, bf16[320,128]{1,0:T(8,128)(2,1)S(1)}, u32[]{:S(2)}, u32[]{:S(2)}) collective-permute-start(bf16[320,128]{1,0:T(8,128)(2,1)S(1)} %get-tuple-element.120), channel_id=1, source_target_pairs={{0,12},{1,13},{2,14},{3,15},{4,8},{5,9},{6,10},{7,11},{8,4},{9,5},... | collective-permute-start | bytes 245768 | tf_op jit(solution)/shard_map/ppermute | solution.py:59
  77.2 0.7 collective-permute-done.25.refs_0_
  77.8 5.1 %collective-permute-done.26.refs_1_ = bf16[320,128]{1,0:T(8,128)(2,1)S(1)} collective-permute-done((bf16[320,128]{1,0:T(8,128)(2,1)S(1)}, bf16[320,128]{1,0:T(8,128)(2,1)S(1)}, u32[]{:S(2)}, u32[]{:S(2)}) %collective-permute-start.26) | collective-permute-done | bytes 81952 | tf_op jit(solution)/shard_map/ppermute | solution.py:59
  83.0 0.1 collective-permute-start.28
  83.1 1.3 %collective-permute-done.28.refs_1_ = bf16[320,128]{1,0:T(8,128)(2,1)S(1)} collective-permute-done((bf16[320,128]{1,0:T(8,128)(2,1)S(1)}, bf16[320,128]{1,0:T(8,128)(2,1)S(1)}, u32[]{:S(2)}, u32[]{:S(2)}) %collective-permute-start.28) | collective-permute-done | bytes 81952 | tf_op jit(solution)/shard_map/ppermute | solution.py:59
  84.3 2.4 %shard_map.120 = (bf16[512,768]{1,0:T(8,128)(2,1)}, bf16[512,768]{1,0:T(8,128)(2,1)}) custom-call(bf16[320,128]{1,0:T(8,128)(2,1)S(1)} %shard_map.119.refs_0_, bf16[320,128]{1,0:T(8,128)(2,1)S(1)} %collective-permute-done.28.refs_1_, f32[256,768]{1,0:T(8,128)S(1)} %get-tuple-element.121.refs_2_, f32[256,768]{1,0:T(8,128)S(1)} %get-tuple-element.122.refs_3_, ...), custom_call_target="tpu_custom_call" | custom-call | flops 201326592 | bytes 4915200 | tf_op jit(solution)/shard_map/pallas_call | solution.py:468
  (31 shorter events, 0.2 us)
Async XLA Ops:
  0.6 7.6 %copy-start.2 = (bf16[512,768]{1,0:T(8,128)(2,1)S(1)}, bf16[512,768]{1,0:T(8,128)(2,1)}, u32[]{:S(2)}) copy-start(bf16[512,768]{1,0:T(8,128)(2,1)} %refs_5_.1) | copy-start | bytes 2359300
  0.6 15.6 %collective-permute-start.4 = (bf16[512,768]{1,0:T(8,128)(2,1)}, bf16[512,768]{1,0:T(8,128)(2,1)S(1)}, u32[]{:S(2)}, u32[]{:S(2)}) collective-permute-start(bf16[512,768]{1,0:T(8,128)(2,1)} %refs_5_.1), channel_id=1, source_target_pairs={{0,1},{1,2},{2,3},{3,4},{4,5},{5,6},{6,7},{7,8},{8,9},{9,10},{10,1... | collective-permute-start | bytes 2359304 | tf_op jit(solution)/shard_map/ppermute | solution.py:50
  5.5 50.9 %copy-start.7 = (f32[768]{0:T(1024)S(1)}, f32[768]{0:T(1024)}, u32[]{:S(2)}) copy-start(f32[768]{0:T(1024)} %param.12) | copy-start | bytes 9220
  5.5 50.9 %copy-start.8 = (f32[768]{0:T(1024)S(1)}, f32[768]{0:T(1024)}, u32[]{:S(2)}) copy-start(f32[768]{0:T(1024)} %param.13) | copy-start | bytes 9220
  5.5 50.9 %copy-start.1 = (bf16[512,768]{1,0:T(8,128)(2,1)S(1)}, bf16[512,768]{1,0:T(8,128)(2,1)}, u32[]{:S(2)}) copy-start(bf16[512,768]{1,0:T(8,128)(2,1)} %o_ref.1) | copy-start | bytes 2359300
  5.5 5.8 %collective-permute-start.1 = (bf16[128,2048]{1,0:T(8,128)(2,1)S(1)}, bf16[128,2048]{1,0:T(8,128)(2,1)S(1)}, u32[]{:S(2)}, u32[]{:S(2)}) collective-permute-start(bf16[128,2048]{1,0:T(8,128)(2,1)S(1)} %get-tuple-element.66), channel_id=1, source_target_pairs={{0,1},{1,0},{2,3},{3,2},{4,5},{5,4},{6,7},{7,6},{8,9},{9,8},{10,11... | collective-permute-start | bytes 1572872 | tf_op jit(solution)/shard_map/ppermute | solution.py:59
  8.2 3.4 %collective-permute-start = (bf16[128,2048]{1,0:T(8,128)(2,1)S(1)}, bf16[128,2048]{1,0:T(8,128)(2,1)S(1)}, u32[]{:S(2)}, u32[]{:S(2)}) collective-permute-start(bf16[128,2048]{1,0:T(8,128)(2,1)S(1)} %get-tuple-element.64), channel_id=1, source_target_pairs={{0,1},{1,0},{2,3},{3,2},{4,5},{5,4},{6,7},{7,6},{8,9},{9,8},{10,11... | collective-permute-start | bytes 1572872 | tf_op jit(solution)/shard_map/ppermute | solution.py:59
  8.2 23.9 %collective-permute-start.7 = (bf16[512,768]{1,0:T(8,128)(2,1)S(1)}, bf16[512,768]{1,0:T(8,128)(2,1)S(1)}, u32[]{:S(2)}, u32[]{:S(2)}) collective-permute-start(bf16[512,768]{1,0:T(8,128)(2,1)S(1)} %copy-done.2), channel_id=1, source_target_pairs={{0,15},{1,0},{2,1},{3,2},{4,3},{5,4},{6,5},{7,6},{8,7},{9,8},{10,9... | collective-permute-start | bytes 2359304 | tf_op jit(solution)/shard_map/ppermute | solution.py:50
  11.5 47.2 %copy-start.3 = (bf16[2,128,128]{2,1,0:T(8,128)(2,1)S(1)}, bf16[2,128,128]{2,1,0:T(8,128)(2,1)}, u32[]{:S(2)}) copy-start(bf16[2,128,128]{2,1,0:T(8,128)(2,1)} %constant.2.clone.refs_4_) | copy-start | bytes 196612
  11.5 47.2 %copy-start.4 = (f32[512]{0:T(512)S(1)}, f32[512]{0:T(512)}, u32[]{:S(2)}) copy-start(f32[512]{0:T(512)} %param.14) | copy-start | bytes 6148
  11.5 47.2 %copy-start.5 = (s32[512]{0:T(512)S(1)}, s32[512]{0:T(512)}, u32[]{:S(2)}) copy-start(s32[512]{0:T(512)} %param.15) | copy-start | bytes 6148
  11.5 47.2 %copy-start.6 = (s32[512]{0:T(512)S(1)}, s32[512]{0:T(512)}, u32[]{:S(2)}) copy-start(s32[512]{0:T(512)} %param.16) | copy-start | bytes 6148
  11.7 20.5 %collective-permute-start.6 = (bf16[64,2048]{1,0:T(8,128)(2,1)S(1)}, bf16[64,2048]{1,0:T(8,128)(2,1)S(1)}, u32[]{:S(2)}, u32[]{:S(2)}) collective-permute-start(bf16[64,2048]{1,0:T(8,128)(2,1)S(1)} %get-tuple-element.74), channel_id=1, source_target_pairs={{0,2},{1,3},{2,0},{3,1},{4,6},{5,7},{6,4},{7,5},{8,10},{9,11},{10,... | collective-permute-start | bytes 786440 | tf_op jit(solution)/shard_map/ppermute | solution.py:59
  12.2 14.7 %collective-permute-start.2 = (bf16[128,512]{1,0:T(8,128)(2,1)S(1)}, bf16[128,512]{1,0:T(8,128)(2,1)S(1)}, u32[]{:S(2)}, u32[]{:S(2)}) collective-permute-start(bf16[128,512]{1,0:T(8,128)(2,1)S(1)} %get-tuple-element.70), channel_id=1, source_target_pairs={{0,4},{1,5},{2,6},{3,7},{4,0},{5,1},{6,2},{7,3},{8,12},{9,13},{10,... | collective-permute-start | bytes 393224 | tf_op jit(solution)/shard_map/ppermute | solution.py:59
  13.8 18.4 %collective-permute-start.3 = (bf16[128,512]{1,0:T(8,128)(2,1)S(1)}, bf16[128,512]{1,0:T(8,128)(2,1)S(1)}, u32[]{:S(2)}, u32[]{:S(2)}) collective-permute-start(bf16[128,512]{1,0:T(8,128)(2,1)S(1)} %get-tuple-element.71), channel_id=1, source_target_pairs={{0,8},{1,9},{2,10},{3,11},{4,12},{5,13},{6,14},{7,15},{8,0},{9,1},... | collective-permute-start | bytes 393224 | tf_op jit(solution)/shard_map/ppermute | solution.py:59
  16.2 16.0 %collective-permute-start.5 = (bf16[128,512]{1,0:T(8,128)(2,1)S(1)}, bf16[128,512]{1,0:T(8,128)(2,1)S(1)}, u32[]{:S(2)}, u32[]{:S(2)}) collective-permute-start(bf16[128,512]{1,0:T(8,128)(2,1)S(1)} %get-tuple-element.73), channel_id=1, source_target_pairs={{0,12},{1,13},{2,14},{3,15},{4,8},{5,9},{6,10},{7,11},{8,4},{9,5},... | collective-permute-start | bytes 393224 | tf_op jit(solution)/shard_map/ppermute | solution.py:59
  32.2 4.7 %collective-permute-start.11 = (bf16[64,512]{1,0:T(8,128)(2,1)S(1)}, bf16[64,512]{1,0:T(8,128)(2,1)S(1)}, u32[]{:S(2)}, u32[]{:S(2)}) collective-permute-start(bf16[64,512]{1,0:T(8,128)(2,1)S(1)} %get-tuple-element.85), channel_id=1, source_target_pairs={{0,2},{1,3},{2,0},{3,1},{4,6},{5,7},{6,4},{7,5},{8,10},{9,11},{10,... | collective-permute-start | bytes 196616 | tf_op jit(solution)/shard_map/ppermute | solution.py:59
  32.4 6.6 %collective-permute-start.10 = (bf16[64,512]{1,0:T(8,128)(2,1)S(1)}, bf16[64,512]{1,0:T(8,128)(2,1)S(1)}, u32[]{:S(2)}, u32[]{:S(2)}) collective-permute-start(bf16[64,512]{1,0:T(8,128)(2,1)S(1)} %get-tuple-element.80), channel_id=1, source_target_pairs={{0,12},{1,13},{2,14},{3,15},{4,8},{5,9},{6,10},{7,11},{8,4},{9,5},... | collective-permute-start | bytes 196616 | tf_op jit(solution)/shard_map/ppermute | solution.py:59
  35.1 4.5 %collective-permute-start.8 = (bf16[64,512]{1,0:T(8,128)(2,1)S(1)}, bf16[64,512]{1,0:T(8,128)(2,1)S(1)}, u32[]{:S(2)}, u32[]{:S(2)}) collective-permute-start(bf16[64,512]{1,0:T(8,128)(2,1)S(1)} %get-tuple-element.78), channel_id=1, source_target_pairs={{0,4},{1,5},{2,6},{3,7},{4,0},{5,1},{6,2},{7,3},{8,12},{9,13},{10,... | collective-permute-start | bytes 196616 | tf_op jit(solution)/shard_map/ppermute | solution.py:59
  37.0 5.5 %collective-permute-start.9 = (bf16[64,512]{1,0:T(8,128)(2,1)S(1)}, bf16[64,512]{1,0:T(8,128)(2,1)S(1)}, u32[]{:S(2)}, u32[]{:S(2)}) collective-permute-start(bf16[64,512]{1,0:T(8,128)(2,1)S(1)} %get-tuple-element.79), channel_id=1, source_target_pairs={{0,8},{1,9},{2,10},{3,11},{4,12},{5,13},{6,14},{7,15},{8,0},{9,1},... | collective-permute-start | bytes 196616 | tf_op jit(solution)/shard_map/ppermute | solution.py:59
  42.5 6.5 %collective-permute-start.12 = (bf16[64,512]{1,0:T(8,128)(2,1)S(1)}, bf16[64,512]{1,0:T(8,128)(2,1)S(1)}, u32[]{:S(2)}, u32[]{:S(2)}) collective-permute-start(bf16[64,512]{1,0:T(8,128)(2,1)S(1)} %get-tuple-element.93.refs_0_), channel_id=1, source_target_pairs={{0,4},{1,5},{2,6},{3,7},{4,0},{5,1},{6,2},{7,3},{8,12},{9,13},{10,... | collective-permute-start | bytes 196616 | tf_op jit(solution)/shard_map/ppermute | solution.py:59
  42.6 6.6 %collective-permute-start.13 = (bf16[64,512]{1,0:T(8,128)(2,1)S(1)}, bf16[64,512]{1,0:T(8,128)(2,1)S(1)}, u32[]{:S(2)}, u32[]{:S(2)}) collective-permute-start(bf16[64,512]{1,0:T(8,128)(2,1)S(1)} %get-tuple-element.93.refs_0_), channel_id=1, source_target_pairs={{0,8},{1,9},{2,10},{3,11},{4,12},{5,13},{6,14},{7,15},{8,0},{9,1},... | collective-permute-start | bytes 196616 | tf_op jit(solution)/shard_map/ppermute | solution.py:59
  45.4 6.5 %collective-permute-start.14 = (bf16[64,512]{1,0:T(8,128)(2,1)S(1)}, bf16[64,512]{1,0:T(8,128)(2,1)S(1)}, u32[]{:S(2)}, u32[]{:S(2)}) collective-permute-start(bf16[64,512]{1,0:T(8,128)(2,1)S(1)} %get-tuple-element.93.refs_0_), channel_id=1, source_target_pairs={{0,12},{1,13},{2,14},{3,15},{4,8},{5,9},{6,10},{7,11},{8,4},{9,5},... | collective-permute-start | bytes 196616 | tf_op jit(solution)/shard_map/ppermute | solution.py:59
  47.0 4.9 %collective-permute-start.15 = (bf16[64,512]{1,0:T(8,128)(2,1)S(1)}, bf16[64,512]{1,0:T(8,128)(2,1)S(1)}, u32[]{:S(2)}, u32[]{:S(2)}) collective-permute-start(bf16[64,512]{1,0:T(8,128)(2,1)S(1)} %get-tuple-element.97.refs_0_), channel_id=1, source_target_pairs={{0,2},{1,3},{2,0},{3,1},{4,6},{5,7},{6,4},{7,5},{8,10},{9,11},{10,... | collective-permute-start | bytes 196616 | tf_op jit(solution)/shard_map/ppermute | solution.py:59
  51.9 9.1 %collective-permute-start.19 = (bf16[128,512]{1,0:T(8,128)(2,1)S(1)}, bf16[128,512]{1,0:T(8,128)(2,1)S(1)}, u32[]{:S(2)}, u32[]{:S(2)}) collective-permute-start(bf16[128,512]{1,0:T(8,128)(2,1)S(1)} %shard_map.111.refs_0_), channel_id=1, source_target_pairs={{0,4},{1,5},{2,6},{3,7},{4,0},{5,1},{6,2},{7,3},{8,12},{9,13},{10,... | collective-permute-start | bytes 393224 | tf_op jit(solution)/shard_map/ppermute | solution.py:59
  52.0 9.7 %collective-permute-start.20 = (bf16[128,512]{1,0:T(8,128)(2,1)S(1)}, bf16[128,512]{1,0:T(8,128)(2,1)S(1)}, u32[]{:S(2)}, u32[]{:S(2)}) collective-permute-start(bf16[128,512]{1,0:T(8,128)(2,1)S(1)} %shard_map.111.refs_0_), channel_id=1, source_target_pairs={{0,8},{1,9},{2,10},{3,11},{4,12},{5,13},{6,14},{7,15},{8,0},{9,1},... | collective-permute-start | bytes 393224 | tf_op jit(solution)/shard_map/ppermute | solution.py:59
  54.1 7.6 %collective-permute-start.21 = (bf16[128,512]{1,0:T(8,128)(2,1)S(1)}, bf16[128,512]{1,0:T(8,128)(2,1)S(1)}, u32[]{:S(2)}, u32[]{:S(2)}) collective-permute-start(bf16[128,512]{1,0:T(8,128)(2,1)S(1)} %shard_map.111.refs_0_), channel_id=1, source_target_pairs={{0,12},{1,13},{2,14},{3,15},{4,8},{5,9},{6,10},{7,11},{8,4},{9,5},... | collective-permute-start | bytes 393224 | tf_op jit(solution)/shard_map/ppermute | solution.py:59
  56.4 6.6 %copy-start = (bf16[2048,768]{1,0:T(8,128)(2,1)S(1)}, bf16[2048,768]{1,0:T(8,128)(2,1)}, u32[]{:S(2)}) copy-start(bf16[2048,768]{1,0:T(8,128)(2,1)} %refs_3_.5) | copy-start | bytes 9437188
  56.5 6.5 %collective-permute-start.17 = (bf16[64,2048]{1,0:T(8,128)(2,1)S(1)}, bf16[64,2048]{1,0:T(8,128)(2,1)S(1)}, u32[]{:S(2)}, u32[]{:S(2)}) collective-permute-start(bf16[64,2048]{1,0:T(8,128)(2,1)S(1)} %shard_map.110.refs_0_), channel_id=1, source_target_pairs={{0,2},{1,3},{2,0},{3,1},{4,6},{5,7},{6,4},{7,5},{8,10},{9,11},{10,... | collective-permute-start | bytes 786440 | tf_op jit(solution)/shard_map/ppermute | solution.py:59
  61.8 2.8 %collective-permute-start.22 = (bf16[128,2048]{1,0:T(8,128)(2,1)S(1)}, bf16[128,2048]{1,0:T(8,128)(2,1)S(1)}, u32[]{:S(2)}, u32[]{:S(2)}) collective-permute-start(bf16[128,2048]{1,0:T(8,128)(2,1)S(1)} %shard_map.114.refs_2_), channel_id=1, source_target_pairs={{0,1},{1,0},{2,3},{3,2},{4,5},{5,4},{6,7},{7,6},{8,9},{9,8},{10,11... | collective-permute-start | bytes 1572872 | tf_op jit(solution)/shard_map/ppermute | solution.py:59
  61.8 2.7 %collective-permute-start.16 = (bf16[64,2048]{1,0:T(8,128)(2,1)S(1)}, bf16[64,2048]{1,0:T(8,128)(2,1)S(1)}, u32[]{:S(2)}, u32[]{:S(2)}) collective-permute-start(bf16[64,2048]{1,0:T(8,128)(2,1)S(1)} %shard_map.110.refs_0_), channel_id=1, source_target_pairs={{0,1},{1,0},{2,3},{3,2},{4,5},{5,4},{6,7},{7,6},{8,9},{9,8},{10,11... | collective-permute-start | bytes 786440 | tf_op jit(solution)/shard_map/ppermute | solution.py:59
  63.0 1.5 %collective-permute-start.18 = (bf16[64,2048]{1,0:T(8,128)(2,1)S(1)}, bf16[64,2048]{1,0:T(8,128)(2,1)S(1)}, u32[]{:S(2)}, u32[]{:S(2)}) collective-permute-start(bf16[64,2048]{1,0:T(8,128)(2,1)S(1)} %collective-permute-done.17.refs_1_), channel_id=1, source_target_pairs={{0,1},{1,0},{2,3},{3,2},{4,5},{5,4},{6,7},{7,6},{8,9},{9,8},{10,11... | collective-permute-start | bytes 786440 | tf_op jit(solution)/shard_map/ppermute | solution.py:59
  66.1 1.5 %collective-permute-start.23 = (bf16[320,128]{1,0:T(8,128)(2,1)S(1)}, bf16[320,128]{1,0:T(8,128)(2,1)S(1)}, u32[]{:S(2)}, u32[]{:S(2)}) collective-permute-start(bf16[320,128]{1,0:T(8,128)(2,1)S(1)} %get-tuple-element.116), channel_id=1, source_target_pairs={{0,1},{1,0},{2,3},{3,2},{4,5},{5,4},{6,7},{7,6},{8,9},{9,8},{10,11... | collective-permute-start | bytes 245768 | tf_op jit(solution)/shard_map/ppermute | solution.py:59
  67.6 5.0 %collective-permute-start.24 = (bf16[320,128]{1,0:T(8,128)(2,1)S(1)}, bf16[320,128]{1,0:T(8,128)(2,1)S(1)}, u32[]{:S(2)}, u32[]{:S(2)}) collective-permute-start(bf16[320,128]{1,0:T(8,128)(2,1)S(1)} %get-tuple-element.118), channel_id=1, source_target_pairs={{0,2},{1,3},{2,0},{3,1},{4,6},{5,7},{6,4},{7,5},{8,10},{9,11},{10,... | collective-permute-start | bytes 245768 | tf_op jit(solution)/shard_map/ppermute | solution.py:59
  72.7 5.1 %collective-permute-start.25 = (bf16[320,128]{1,0:T(8,128)(2,1)S(1)}, bf16[320,128]{1,0:T(8,128)(2,1)S(1)}, u32[]{:S(2)}, u32[]{:S(2)}) collective-permute-start(bf16[320,128]{1,0:T(8,128)(2,1)S(1)} %get-tuple-element.120), channel_id=1, source_target_pairs={{0,4},{1,5},{2,6},{3,7},{4,0},{5,1},{6,2},{7,3},{8,12},{9,13},{10,... | collective-permute-start | bytes 245768 | tf_op jit(solution)/shard_map/ppermute | solution.py:59
  74.1 8.8 %collective-permute-start.26 = (bf16[320,128]{1,0:T(8,128)(2,1)S(1)}, bf16[320,128]{1,0:T(8,128)(2,1)S(1)}, u32[]{:S(2)}, u32[]{:S(2)}) collective-permute-start(bf16[320,128]{1,0:T(8,128)(2,1)S(1)} %get-tuple-element.120), channel_id=1, source_target_pairs={{0,8},{1,9},{2,10},{3,11},{4,12},{5,13},{6,14},{7,15},{8,0},{9,1},... | collective-permute-start | bytes 245768 | tf_op jit(solution)/shard_map/ppermute | solution.py:59
  74.8 8.2 %collective-permute-start.27 = (bf16[320,128]{1,0:T(8,128)(2,1)S(1)}, bf16[320,128]{1,0:T(8,128)(2,1)S(1)}, u32[]{:S(2)}, u32[]{:S(2)}) collective-permute-start(bf16[320,128]{1,0:T(8,128)(2,1)S(1)} %get-tuple-element.120), channel_id=1, source_target_pairs={{0,12},{1,13},{2,14},{3,15},{4,8},{5,9},{6,10},{7,11},{8,4},{9,5},... | collective-permute-start | bytes 245768 | tf_op jit(solution)/shard_map/ppermute | solution.py:59
  83.0 1.3 %collective-permute-start.28 = (bf16[320,128]{1,0:T(8,128)(2,1)S(1)}, bf16[320,128]{1,0:T(8,128)(2,1)S(1)}, u32[]{:S(2)}, u32[]{:S(2)}) collective-permute-start(bf16[320,128]{1,0:T(8,128)(2,1)S(1)} %shard_map.119.refs_0_), channel_id=1, source_target_pairs={{0,1},{1,0},{2,3},{3,2},{4,5},{5,4},{6,7},{7,6},{8,9},{9,8},{10,11... | collective-permute-start | bytes 245768 | tf_op jit(solution)/shard_map/ppermute | solution.py:59

commit v14 on v13

--- a/solution.py
+++ b/solution.py
@@ -526,10 +526,14 @@
     taken_z, taken_x, low, high = lax.optimization_barrier(
         (parts_to(parts_z, along), parts_to(parts_x, across), low, high)
     )
+    base, mask = local_part(
+        response, low, high, orbitals, matrix, lines, bounds, group_rows, width, blk
+    )
+    padded = pad_orbitals(orbitals, blk)
     keep_x, *parts_x = split(keep_x, taken_x, along, 1)
     keep_z, *parts_z = split(keep_z, taken_z, across, 0)
-    taken_x, taken_z = lax.optimization_barrier(
-        (parts_to(parts_x, along), parts_to(parts_z, across))
+    taken_x, taken_z, base, padded = lax.optimization_barrier(
+        (parts_to(parts_x, along), parts_to(parts_z, across), base, padded)
     )
     share_x, share_z = local_call(
         functools.partial(finish_both_body, ace_scale, len(taken_x)),
@@ -540,18 +544,13 @@
         [keep_x, *taken_x, keep_z, *taken_z],
     )
 
-    pieces_x, pieces_z, bounds = lax.optimization_barrier(
-        ([share_x, *to(share_x, along)], [share_z, *to(share_z, across)], bounds)
-    )
-    base, mask = local_part(
-        response, low, high, orbitals, matrix, lines, bounds, group_rows, width, blk
+    pieces_x, pieces_z = lax.optimization_barrier(
+        ([share_x, *to(share_x, along)], [share_z, *to(share_z, across)])
     )
     block_x = place(pieces_x, along, 1)
     block_z = place(pieces_z, across, 0)
     blocks_x = [block_x, *to(block_x, across)]
-    pieces_z, base, padded = lax.optimization_barrier(
-        ([block_z, *to(block_z, along)], base, pad_orbitals(orbitals, blk))
-    )
+    pieces_z = [block_z, *to(block_z, along)]
     blocks = [*blocks_x, place(pieces_z, along, 1)]
     others = [swapped(part, count, core, 1) for part in blocks]
     sizes = (core, across, block, group_rows, blk)

time: 86.9 us -> 86.9 us (level)
  transfers between devices with their start and end apart: 29 -> 29, of which waited for: 15 -> 14; matrix products, arithmetic and copies ran while one was open for 0% -> 0% of each run, Pallas kernels for 10% -> 10%
where the time goes in v14:
time: 86.9 us; the launch traced here: 86.7 us
  starting transfers between devices  37.4 us (43%)
  waiting for transfers between devices  35.6 us (41%)
  Pallas kernels  12.8 us (15%)
  between operations  0.93 us (1%)
    ppermute x27, waiting for transfers between devices, swapped(): return lax.ppermute(array, 'band', pairs)  34.5 us
    ppermute x27, starting transfers between devices, swapped(): return lax.ppermute(array, 'band', pairs)  33.8 us
    pallas_call x1, Pallas kernels, first_sums(): pl.pallas_call(functools.partial(first_body, core, block, tile), out_shap...  4.34 us
    pallas_call x14, Pallas kernels, local_call(): pl.pallas_call(body, out_shape=outs, in_specs=[whole() for _ in args], ou...  3.74 us
    ppermute x2, starting transfers between devices, neighbour(): lax.ppermute(array, 'band', [(i, (i + step) % count) for i in range(count)])  3.62 us
    pallas_call x1, Pallas kernels, project(): pl.pallas_call(functools.partial(project_body, core, blk), grid=(bands //...  2.43 us
    pallas_call x1, Pallas kernels, local_part(): pl.pallas_call(functools.partial(local_body, depth, (group_rows, blk)), g...  2.3 us
  transfers between devices with their start and end apart: 29, of which 14 were waited for; matrix products, arithmetic and copies ran while one was open for 0% of the time, Pallas kernels for 10%

profile of v14, /device:TPU:0, one launch (start us, length us, event | category | flops | bytes accessed | tf_op | source)
XLA Modules:
  0.0 86.7 jit_solution(12274912790983145301)
XLA Ops:
  0.6 0.5 collective-permute-start.4
  1.1 4.3 %shard_map.104 = (bf16[128,2048]{1,0:T(8,128)(2,1)S(1)}, bf16[128,2048]{1,0:T(8,128)(2,1)S(1)}, f32[128,2048]{1,0:T(8,128)S(1)}, f32[128,2048]{1,0:T(8,128)S(1)}) custom-call(bf16[512,768]{1,0:T(8,128)(2,1)} %refs_5_.1, bf16[2048,768]{1,0:T(8,128)(2,1)} %refs_3_.5), custom_call_target="tpu_custom_call" | custom-call | flops 1610612736 | bytes 6291456 | tf_op jit(solution)/shard_map/pallas_call | solution.py:147
  5.5 0.0 copy-start.7
  5.5 0.0 copy-start.8
  5.5 0.0 copy-start.1
  5.5 2.6 %collective-permute-start.1 = (bf16[128,2048]{1,0:T(8,128)(2,1)S(1)}, bf16[128,2048]{1,0:T(8,128)(2,1)S(1)}, u32[]{:S(2)}, u32[]{:S(2)}) collective-permute-start(bf16[128,2048]{1,0:T(8,128)(2,1)S(1)} %get-tuple-element.59), channel_id=1, source_target_pairs={{0,1},{1,0},{2,3},{3,2},{4,5},{5,4},{6,7},{7,6},{8,9},{9,8},{10,11... | collective-permute-start | bytes 1572872 | tf_op jit(solution)/shard_map/ppermute | solution.py:59
  8.2 0.1 collective-permute-start
  8.2 3.1 %collective-permute-start.7 = (bf16[512,768]{1,0:T(8,128)(2,1)S(1)}, bf16[512,768]{1,0:T(8,128)(2,1)S(1)}, u32[]{:S(2)}, u32[]{:S(2)}) collective-permute-start(bf16[512,768]{1,0:T(8,128)(2,1)S(1)} %copy-done.2), channel_id=1, source_target_pairs={{0,15},{1,0},{2,1},{3,2},{4,3},{5,4},{6,5},{7,6},{8,7},{9,8},{10,9... | collective-permute-start | bytes 2359304 | tf_op jit(solution)/shard_map/ppermute | solution.py:50
  11.4 0.0 collective-permute-done.1.refs_1_
  11.4 0.0 copy-start.6
  11.4 0.1 shard_map.105
  11.5 0.0 collective-permute-done.refs_1_
  11.5 0.1 shard_map.106
  11.7 0.5 collective-permute-start.6
  12.2 1.6 %collective-permute-start.2 = (bf16[128,512]{1,0:T(8,128)(2,1)S(1)}, bf16[128,512]{1,0:T(8,128)(2,1)S(1)}, u32[]{:S(2)}, u32[]{:S(2)}) collective-permute-start(bf16[128,512]{1,0:T(8,128)(2,1)S(1)} %get-tuple-element.63), channel_id=1, source_target_pairs={{0,4},{1,5},{2,6},{3,7},{4,0},{5,1},{6,2},{7,3},{8,12},{9,13},{10,... | collective-permute-start | bytes 393224 | tf_op jit(solution)/shard_map/ppermute | solution.py:59
  13.8 1.4 %collective-permute-start.3 = (bf16[128,512]{1,0:T(8,128)(2,1)S(1)}, bf16[128,512]{1,0:T(8,128)(2,1)S(1)}, u32[]{:S(2)}, u32[]{:S(2)}) collective-permute-start(bf16[128,512]{1,0:T(8,128)(2,1)S(1)} %get-tuple-element.64), channel_id=1, source_target_pairs={{0,8},{1,9},{2,10},{3,11},{4,12},{5,13},{6,14},{7,15},{8,0},{9,1},... | collective-permute-start | bytes 393224 | tf_op jit(solution)/shard_map/ppermute | solution.py:59
  15.1 1.1 %collective-permute-done.4.refs_1_ = bf16[512,768]{1,0:T(8,128)(2,1)S(1)} collective-permute-done((bf16[512,768]{1,0:T(8,128)(2,1)}, bf16[512,768]{1,0:T(8,128)(2,1)S(1)}, u32[]{:S(2)}, u32[]{:S(2)}) %collective-permute-start.4) | collective-permute-done | bytes 786464 | tf_op jit(solution)/shard_map/ppermute | solution.py:50
  16.2 2.2 %collective-permute-start.5 = (bf16[128,512]{1,0:T(8,128)(2,1)S(1)}, bf16[128,512]{1,0:T(8,128)(2,1)S(1)}, u32[]{:S(2)}, u32[]{:S(2)}) collective-permute-start(bf16[128,512]{1,0:T(8,128)(2,1)S(1)} %get-tuple-element.66), channel_id=1, source_target_pairs={{0,12},{1,13},{2,14},{3,15},{4,8},{5,9},{6,10},{7,11},{8,4},{9,5},... | collective-permute-start | bytes 393224 | tf_op jit(solution)/shard_map/ppermute | solution.py:59
  18.4 8.6 %collective-permute-done.2.refs_1_ = bf16[128,512]{1,0:T(8,128)(2,1)S(1)} collective-permute-done((bf16[128,512]{1,0:T(8,128)(2,1)S(1)}, bf16[128,512]{1,0:T(8,128)(2,1)S(1)}, u32[]{:S(2)}, u32[]{:S(2)}) %collective-permute-start.2) | collective-permute-done | bytes 131104 | tf_op jit(solution)/shard_map/ppermute | solution.py:59
  26.9 5.2 %collective-permute-done.3.refs_2_ = bf16[128,512]{1,0:T(8,128)(2,1)S(1)} collective-permute-done((bf16[128,512]{1,0:T(8,128)(2,1)S(1)}, bf16[128,512]{1,0:T(8,128)(2,1)S(1)}, u32[]{:S(2)}, u32[]{:S(2)}) %collective-permute-start.3) | collective-permute-done | bytes 131104 | tf_op jit(solution)/shard_map/ppermute | solution.py:59
  32.2 0.1 shard_map.108
  32.2 0.1 collective-permute-start.11
  32.3 0.1 shard_map.107
  32.4 2.7 %collective-permute-start.10 = (bf16[64,512]{1,0:T(8,128)(2,1)S(1)}, bf16[64,512]{1,0:T(8,128)(2,1)S(1)}, u32[]{:S(2)}, u32[]{:S(2)}) collective-permute-start(bf16[64,512]{1,0:T(8,128)(2,1)S(1)} %get-tuple-element.73), channel_id=1, source_target_pairs={{0,12},{1,13},{2,14},{3,15},{4,8},{5,9},{6,10},{7,11},{8,4},{9,5},... | collective-permute-start | bytes 196616 | tf_op jit(solution)/shard_map/ppermute | solution.py:59
  35.1 1.8 %collective-permute-start.8 = (bf16[64,512]{1,0:T(8,128)(2,1)S(1)}, bf16[64,512]{1,0:T(8,128)(2,1)S(1)}, u32[]{:S(2)}, u32[]{:S(2)}) collective-permute-start(bf16[64,512]{1,0:T(8,128)(2,1)S(1)} %get-tuple-element.71), channel_id=1, source_target_pairs={{0,4},{1,5},{2,6},{3,7},{4,0},{5,1},{6,2},{7,3},{8,12},{9,13},{10,... | collective-permute-start | bytes 196616 | tf_op jit(solution)/shard_map/ppermute | solution.py:59
  37.0 0.0 collective-permute-start.9
  37.0 0.1 shard_map.110.refs_5_.refs_4_
  37.1 0.0 copy-start
  37.1 2.3 %shard_map.109 = (f32[512,768]{1,0:T(8,128)S(1)}, bf16[512,256]{1,0:T(8,128)(2,1)S(1)}) custom-call(bf16[512,768]{1,0:T(8,128)(2,1)S(1)} %copy-done.2, bf16[512,768]{1,0:T(8,128)(2,1)S(1)} %collective-permute-done.4.refs_1_, bf16[512,768]{1,0:T(8,128)(2,1)S(1)} %collective-permute-done.7.refs_2_, bf16[512,768]{1,0:T(8,128)(2,1)S(1)} %copy-done.1, ...), custom_call_target="tpu_custom_call" | custom-call | flops 235929600 | bytes 4980736 | tf_op jit(solution)/shard_map/pallas_call | solution.py:298
  39.4 0.0 collective-permute-done.11.refs_5_
  39.5 0.1 collective-permute-done.8.refs_1_
  39.6 2.8 %collective-permute-done.9.refs_2_ = bf16[64,512]{1,0:T(8,128)(2,1)S(1)} collective-permute-done((bf16[64,512]{1,0:T(8,128)(2,1)S(1)}, bf16[64,512]{1,0:T(8,128)(2,1)S(1)}, u32[]{:S(2)}, u32[]{:S(2)}) %collective-permute-start.9) | collective-permute-done | bytes 65568 | tf_op jit(solution)/shard_map/ppermute | solution.py:59
  42.4 0.1 shard_map.111
  42.5 0.1 collective-permute-start.12
  42.6 2.8 %collective-permute-start.13 = (bf16[64,512]{1,0:T(8,128)(2,1)S(1)}, bf16[64,512]{1,0:T(8,128)(2,1)S(1)}, u32[]{:S(2)}, u32[]{:S(2)}) collective-permute-start(bf16[64,512]{1,0:T(8,128)(2,1)S(1)} %get-tuple-element.89.refs_0_), channel_id=1, source_target_pairs={{0,8},{1,9},{2,10},{3,11},{4,12},{5,13},{6,14},{7,15},{8,0},{9,1},... | collective-permute-start | bytes 196616 | tf_op jit(solution)/shard_map/ppermute | solution.py:59
  45.4 1.5 %collective-permute-start.14 = (bf16[64,512]{1,0:T(8,128)(2,1)S(1)}, bf16[64,512]{1,0:T(8,128)(2,1)S(1)}, u32[]{:S(2)}, u32[]{:S(2)}) collective-permute-start(bf16[64,512]{1,0:T(8,128)(2,1)S(1)} %get-tuple-element.89.refs_0_), channel_id=1, source_target_pairs={{0,12},{1,13},{2,14},{3,15},{4,8},{5,9},{6,10},{7,11},{8,4},{9,5},... | collective-permute-start | bytes 196616 | tf_op jit(solution)/shard_map/ppermute | solution.py:59
  47.0 2.0 %collective-permute-start.15 = (bf16[64,512]{1,0:T(8,128)(2,1)S(1)}, bf16[64,512]{1,0:T(8,128)(2,1)S(1)}, u32[]{:S(2)}, u32[]{:S(2)}) collective-permute-start(bf16[64,512]{1,0:T(8,128)(2,1)S(1)} %get-tuple-element.93.refs_0_), channel_id=1, source_target_pairs={{0,2},{1,3},{2,0},{3,1},{4,6},{5,7},{6,4},{7,5},{8,10},{9,11},{10,... | collective-permute-start | bytes 196616 | tf_op jit(solution)/shard_map/ppermute | solution.py:59
  48.9 0.0 collective-permute-done.12.refs_1_
  49.0 0.3 collective-permute-done.13.refs_2_
  49.2 2.7 %collective-permute-done.14.refs_3_ = bf16[64,512]{1,0:T(8,128)(2,1)S(1)} collective-permute-done((bf16[64,512]{1,0:T(8,128)(2,1)S(1)}, bf16[64,512]{1,0:T(8,128)(2,1)S(1)}, u32[]{:S(2)}, u32[]{:S(2)}) %collective-permute-start.14) | collective-permute-done | bytes 65568 | tf_op jit(solution)/shard_map/ppermute | solution.py:59
  51.9 0.1 collective-permute-start.19
  52.0 2.1 %collective-permute-start.20 = (bf16[128,512]{1,0:T(8,128)(2,1)S(1)}, bf16[128,512]{1,0:T(8,128)(2,1)S(1)}, u32[]{:S(2)}, u32[]{:S(2)}) collective-permute-start(bf16[128,512]{1,0:T(8,128)(2,1)S(1)} %shard_map.113.refs_0_), channel_id=1, source_target_pairs={{0,8},{1,9},{2,10},{3,11},{4,12},{5,13},{6,14},{7,15},{8,0},{9,1},... | collective-permute-start | bytes 393224 | tf_op jit(solution)/shard_map/ppermute | solution.py:59
  54.1 2.2 %collective-permute-start.21 = (bf16[128,512]{1,0:T(8,128)(2,1)S(1)}, bf16[128,512]{1,0:T(8,128)(2,1)S(1)}, u32[]{:S(2)}, u32[]{:S(2)}) collective-permute-start(bf16[128,512]{1,0:T(8,128)(2,1)S(1)} %shard_map.113.refs_0_), channel_id=1, source_target_pairs={{0,12},{1,13},{2,14},{3,15},{4,8},{5,9},{6,10},{7,11},{8,4},{9,5},... | collective-permute-start | bytes 393224 | tf_op jit(solution)/shard_map/ppermute | solution.py:59
  56.4 2.2 %collective-permute-start.17 = (bf16[64,2048]{1,0:T(8,128)(2,1)S(1)}, bf16[64,2048]{1,0:T(8,128)(2,1)S(1)}, u32[]{:S(2)}, u32[]{:S(2)}) collective-permute-start(bf16[64,2048]{1,0:T(8,128)(2,1)S(1)} %shard_map.112.refs_0_), channel_id=1, source_target_pairs={{0,2},{1,3},{2,0},{3,1},{4,6},{5,7},{6,4},{7,5},{8,10},{9,11},{10,... | collective-permute-start | bytes 786440 | tf_op jit(solution)/shard_map/ppermute | solution.py:59
  58.6 3.1 %collective-permute-done.20.refs_2_ = bf16[128,512]{1,0:T(8,128)(2,1)S(1)} collective-permute-done((bf16[128,512]{1,0:T(8,128)(2,1)S(1)}, bf16[128,512]{1,0:T(8,128)(2,1)S(1)}, u32[]{:S(2)}, u32[]{:S(2)}) %collective-permute-start.20) | collective-permute-done | bytes 131104 | tf_op jit(solution)/shard_map/ppermute | solution.py:59
  61.7 0.1 shard_map.114.refs_2_
  61.8 0.1 collective-permute-start.22
  61.8 0.5 collective-permute-start.16
  62.3 0.6 collective-permute-done.17.refs_1_
  62.9 1.5 %shard_map.115 = (f32[256,768]{1,0:T(8,128)S(1)}, f32[320,128]{1,0:T(8,128)S(1)}) custom-call(bf16[64,2048]{1,0:T(8,128)(2,1)S(1)} %shard_map.112.refs_0_, bf16[64,2048]{1,0:T(8,128)(2,1)S(1)} %collective-permute-done.17.refs_1_, bf16[128,2048]{1,0:T(8,128)(2,1)S(1)} %shard_map.114.refs_2_, bf16[2048,768]{1,0:T(8,128)(2,1)S(1)} %copy-done, ...), custom_call_target="tpu_custom_call" | custom-call | flops 905969664 | bytes 7700480 | tf_op jit(solution)/shard_map/pallas_call | solution.py:91
  64.5 0.0 collective-permute-done.18.refs_1_
  64.5 1.5 %shard_map.116 = (f32[256,768]{1,0:T(8,128)S(1)}, bf16[320,128]{1,0:T(8,128)(2,1)S(1)}) custom-call(bf16[64,2048]{1,0:T(8,128)(2,1)S(1)} %collective-permute-done.16.refs_0_, bf16[64,2048]{1,0:T(8,128)(2,1)S(1)} %collective-permute-done.18.refs_1_, bf16[128,2048]{1,0:T(8,128)(2,1)S(1)} %collective-permute-done.22.refs_2_, bf16[2048,768]{1,0:T(8,128)(2,1)S(1)} %copy-done, ...), custom_call_target="tpu_custom_call" | custom-call | flops 905969664 | bytes 7618560 | tf_op jit(solution)/shard_map/pallas_call | solution.py:91
  66.0 0.6 collective-permute-start.23
  66.6 0.9 %collective-permute-done.23.refs_0_ = bf16[320,128]{1,0:T(8,128)(2,1)S(1)} collective-permute-done((bf16[320,128]{1,0:T(8,128)(2,1)S(1)}, bf16[320,128]{1,0:T(8,128)(2,1)S(1)}, u32[]{:S(2)}, u32[]{:S(2)}) %collective-permute-start.23) | collective-permute-done | bytes 81952 | tf_op jit(solution)/shard_map/ppermute | solution.py:59
  67.5 2.1 %collective-permute-start.24 = (bf16[320,128]{1,0:T(8,128)(2,1)S(1)}, bf16[320,128]{1,0:T(8,128)(2,1)S(1)}, u32[]{:S(2)}, u32[]{:S(2)}) collective-permute-start(bf16[320,128]{1,0:T(8,128)(2,1)S(1)} %get-tuple-element.104), channel_id=1, source_target_pairs={{0,2},{1,3},{2,0},{3,1},{4,6},{5,7},{6,4},{7,5},{8,10},{9,11},{10,... | collective-permute-start | bytes 245768 | tf_op jit(solution)/shard_map/ppermute | solution.py:59
  69.6 3.0 %collective-permute-done.24.refs_0_ = bf16[320,128]{1,0:T(8,128)(2,1)S(1)} collective-permute-done((bf16[320,128]{1,0:T(8,128)(2,1)S(1)}, bf16[320,128]{1,0:T(8,128)(2,1)S(1)}, u32[]{:S(2)}, u32[]{:S(2)}) %collective-permute-start.24) | collective-permute-done | bytes 81952 | tf_op jit(solution)/shard_map/ppermute | solution.py:59
  72.6 1.5 %collective-permute-start.25 = (bf16[320,128]{1,0:T(8,128)(2,1)S(1)}, bf16[320,128]{1,0:T(8,128)(2,1)S(1)}, u32[]{:S(2)}, u32[]{:S(2)}) collective-permute-start(bf16[320,128]{1,0:T(8,128)(2,1)S(1)} %get-tuple-element.106), channel_id=1, source_target_pairs={{0,4},{1,5},{2,6},{3,7},{4,0},{5,1},{6,2},{7,3},{8,12},{9,13},{10,... | collective-permute-start | bytes 245768 | tf_op jit(solution)/shard_map/ppermute | solution.py:59
  74.1 0.5 collective-permute-start.26
  74.6 2.4 %collective-permute-start.27 = (bf16[320,128]{1,0:T(8,128)(2,1)S(1)}, bf16[320,128]{1,0:T(8,128)(2,1)S(1)}, u32[]{:S(2)}, u32[]{:S(2)}) collective-permute-start(bf16[320,128]{1,0:T(8,128)(2,1)S(1)} %get-tuple-element.106), channel_id=1, source_target_pairs={{0,12},{1,13},{2,14},{3,15},{4,8},{5,9},{6,10},{7,11},{8,4},{9,5},... | collective-permute-start | bytes 245768 | tf_op jit(solution)/shard_map/ppermute | solution.py:59
  77.0 0.5 collective-permute-done.25.refs_0_
  77.5 5.4 %collective-permute-done.26.refs_1_ = bf16[320,128]{1,0:T(8,128)(2,1)S(1)} collective-permute-done((bf16[320,128]{1,0:T(8,128)(2,1)S(1)}, bf16[320,128]{1,0:T(8,128)(2,1)S(1)}, u32[]{:S(2)}, u32[]{:S(2)}) %collective-permute-start.26) | collective-permute-done | bytes 81952 | tf_op jit(solution)/shard_map/ppermute | solution.py:59
  83.0 0.1 collective-permute-start.28
  83.1 1.3 %collective-permute-done.28.refs_1_ = bf16[320,128]{1,0:T(8,128)(2,1)S(1)} collective-permute-done((bf16[320,128]{1,0:T(8,128)(2,1)S(1)}, bf16[320,128]{1,0:T(8,128)(2,1)S(1)}, u32[]{:S(2)}, u32[]{:S(2)}) %collective-permute-start.28) | collective-permute-done | bytes 81952 | tf_op jit(solution)/shard_map/ppermute | solution.py:59
  84.3 2.4 %shard_map.120 = (bf16[512,768]{1,0:T(8,128)(2,1)}, bf16[512,768]{1,0:T(8,128)(2,1)}) custom-call(bf16[320,128]{1,0:T(8,128)(2,1)S(1)} %shard_map.119.refs_0_, bf16[320,128]{1,0:T(8,128)(2,1)S(1)} %collective-permute-done.28.refs_1_, f32[256,768]{1,0:T(8,128)S(1)} %get-tuple-element.107.refs_2_, f32[256,768]{1,0:T(8,128)S(1)} %get-tuple-element.108.refs_3_, ...), custom_call_target="tpu_custom_call" | custom-call | flops 201326592 | bytes 4915200 | tf_op jit(solution)/shard_map/pallas_call | solution.py:468
  (31 shorter events, 0.2 us)
Async XLA Ops:
  0.6 7.6 %copy-start.2 = (bf16[512,768]{1,0:T(8,128)(2,1)S(1)}, bf16[512,768]{1,0:T(8,128)(2,1)}, u32[]{:S(2)}) copy-start(bf16[512,768]{1,0:T(8,128)(2,1)} %refs_5_.1) | copy-start | bytes 2359300
  0.6 15.6 %collective-permute-start.4 = (bf16[512,768]{1,0:T(8,128)(2,1)}, bf16[512,768]{1,0:T(8,128)(2,1)S(1)}, u32[]{:S(2)}, u32[]{:S(2)}) collective-permute-start(bf16[512,768]{1,0:T(8,128)(2,1)} %refs_5_.1), channel_id=1, source_target_pairs={{0,1},{1,2},{2,3},{3,4},{4,5},{5,6},{6,7},{7,8},{8,9},{9,10},{10,1... | collective-permute-start | bytes 2359304 | tf_op jit(solution)/shard_map/ppermute | solution.py:50
  5.5 31.5 %copy-start.7 = (f32[768]{0:T(1024)S(1)}, f32[768]{0:T(1024)}, u32[]{:S(2)}) copy-start(f32[768]{0:T(1024)} %param.12) | copy-start | bytes 9220
  5.5 31.5 %copy-start.8 = (f32[768]{0:T(1024)S(1)}, f32[768]{0:T(1024)}, u32[]{:S(2)}) copy-start(f32[768]{0:T(1024)} %param.13) | copy-start | bytes 9220
  5.5 31.5 %copy-start.1 = (bf16[512,768]{1,0:T(8,128)(2,1)S(1)}, bf16[512,768]{1,0:T(8,128)(2,1)}, u32[]{:S(2)}) copy-start(bf16[512,768]{1,0:T(8,128)(2,1)} %o_ref.1) | copy-start | bytes 2359300
  5.5 5.8 %collective-permute-start.1 = (bf16[128,2048]{1,0:T(8,128)(2,1)S(1)}, bf16[128,2048]{1,0:T(8,128)(2,1)S(1)}, u32[]{:S(2)}, u32[]{:S(2)}) collective-permute-start(bf16[128,2048]{1,0:T(8,128)(2,1)S(1)} %get-tuple-element.59), channel_id=1, source_target_pairs={{0,1},{1,0},{2,3},{3,2},{4,5},{5,4},{6,7},{7,6},{8,9},{9,8},{10,11... | collective-permute-start | bytes 1572872 | tf_op jit(solution)/shard_map/ppermute | solution.py:59
  8.2 3.4 %collective-permute-start = (bf16[128,2048]{1,0:T(8,128)(2,1)S(1)}, bf16[128,2048]{1,0:T(8,128)(2,1)S(1)}, u32[]{:S(2)}, u32[]{:S(2)}) collective-permute-start(bf16[128,2048]{1,0:T(8,128)(2,1)S(1)} %get-tuple-element.57), channel_id=1, source_target_pairs={{0,1},{1,0},{2,3},{3,2},{4,5},{5,4},{6,7},{7,6},{8,9},{9,8},{10,11... | collective-permute-start | bytes 1572872 | tf_op jit(solution)/shard_map/ppermute | solution.py:59
  8.2 23.9 %collective-permute-start.7 = (bf16[512,768]{1,0:T(8,128)(2,1)S(1)}, bf16[512,768]{1,0:T(8,128)(2,1)S(1)}, u32[]{:S(2)}, u32[]{:S(2)}) collective-permute-start(bf16[512,768]{1,0:T(8,128)(2,1)S(1)} %copy-done.2), channel_id=1, source_target_pairs={{0,15},{1,0},{2,1},{3,2},{4,3},{5,4},{6,5},{7,6},{8,7},{9,8},{10,9... | collective-permute-start | bytes 2359304 | tf_op jit(solution)/shard_map/ppermute | solution.py:50
  11.4 25.7 %copy-start.3 = (bf16[2,128,128]{2,1,0:T(8,128)(2,1)S(1)}, bf16[2,128,128]{2,1,0:T(8,128)(2,1)}, u32[]{:S(2)}) copy-start(bf16[2,128,128]{2,1,0:T(8,128)(2,1)} %constant.2.clone.refs_4_) | copy-start | bytes 196612
  11.4 25.7 %copy-start.4 = (f32[512]{0:T(512)S(1)}, f32[512]{0:T(512)}, u32[]{:S(2)}) copy-start(f32[512]{0:T(512)} %param.14) | copy-start | bytes 6148
  11.4 25.7 %copy-start.5 = (s32[512]{0:T(512)S(1)}, s32[512]{0:T(512)}, u32[]{:S(2)}) copy-start(s32[512]{0:T(512)} %param.15) | copy-start | bytes 6148
  11.4 25.7 %copy-start.6 = (s32[512]{0:T(512)S(1)}, s32[512]{0:T(512)}, u32[]{:S(2)}) copy-start(s32[512]{0:T(512)} %param.16) | copy-start | bytes 6148
  11.7 20.5 %collective-permute-start.6 = (bf16[64,2048]{1,0:T(8,128)(2,1)S(1)}, bf16[64,2048]{1,0:T(8,128)(2,1)S(1)}, u32[]{:S(2)}, u32[]{:S(2)}) collective-permute-start(bf16[64,2048]{1,0:T(8,128)(2,1)S(1)} %get-tuple-element.67), channel_id=1, source_target_pairs={{0,2},{1,3},{2,0},{3,1},{4,6},{5,7},{6,4},{7,5},{8,10},{9,11},{10,... | collective-permute-start | bytes 786440 | tf_op jit(solution)/shard_map/ppermute | solution.py:59
  12.2 14.7 %collective-permute-start.2 = (bf16[128,512]{1,0:T(8,128)(2,1)S(1)}, bf16[128,512]{1,0:T(8,128)(2,1)S(1)}, u32[]{:S(2)}, u32[]{:S(2)}) collective-permute-start(bf16[128,512]{1,0:T(8,128)(2,1)S(1)} %get-tuple-element.63), channel_id=1, source_target_pairs={{0,4},{1,5},{2,6},{3,7},{4,0},{5,1},{6,2},{7,3},{8,12},{9,13},{10,... | collective-permute-start | bytes 393224 | tf_op jit(solution)/shard_map/ppermute | solution.py:59
  13.8 18.4 %collective-permute-start.3 = (bf16[128,512]{1,0:T(8,128)(2,1)S(1)}, bf16[128,512]{1,0:T(8,128)(2,1)S(1)}, u32[]{:S(2)}, u32[]{:S(2)}) collective-permute-start(bf16[128,512]{1,0:T(8,128)(2,1)S(1)} %get-tuple-element.64), channel_id=1, source_target_pairs={{0,8},{1,9},{2,10},{3,11},{4,12},{5,13},{6,14},{7,15},{8,0},{9,1},... | collective-permute-start | bytes 393224 | tf_op jit(solution)/shard_map/ppermute | solution.py:59
  16.2 16.0 %collective-permute-start.5 = (bf16[128,512]{1,0:T(8,128)(2,1)S(1)}, bf16[128,512]{1,0:T(8,128)(2,1)S(1)}, u32[]{:S(2)}, u32[]{:S(2)}) collective-permute-start(bf16[128,512]{1,0:T(8,128)(2,1)S(1)} %get-tuple-element.66), channel_id=1, source_target_pairs={{0,12},{1,13},{2,14},{3,15},{4,8},{5,9},{6,10},{7,11},{8,4},{9,5},... | collective-permute-start | bytes 393224 | tf_op jit(solution)/shard_map/ppermute | solution.py:59
  32.2 7.2 %collective-permute-start.11 = (bf16[64,512]{1,0:T(8,128)(2,1)S(1)}, bf16[64,512]{1,0:T(8,128)(2,1)S(1)}, u32[]{:S(2)}, u32[]{:S(2)}) collective-permute-start(bf16[64,512]{1,0:T(8,128)(2,1)S(1)} %get-tuple-element.78), channel_id=1, source_target_pairs={{0,2},{1,3},{2,0},{3,1},{4,6},{5,7},{6,4},{7,5},{8,10},{9,11},{10,... | collective-permute-start | bytes 196616 | tf_op jit(solution)/shard_map/ppermute | solution.py:59
  32.4 7.1 %collective-permute-start.10 = (bf16[64,512]{1,0:T(8,128)(2,1)S(1)}, bf16[64,512]{1,0:T(8,128)(2,1)S(1)}, u32[]{:S(2)}, u32[]{:S(2)}) collective-permute-start(bf16[64,512]{1,0:T(8,128)(2,1)S(1)} %get-tuple-element.73), channel_id=1, source_target_pairs={{0,12},{1,13},{2,14},{3,15},{4,8},{5,9},{6,10},{7,11},{8,4},{9,5},... | collective-permute-start | bytes 196616 | tf_op jit(solution)/shard_map/ppermute | solution.py:59
  35.1 4.5 %collective-permute-start.8 = (bf16[64,512]{1,0:T(8,128)(2,1)S(1)}, bf16[64,512]{1,0:T(8,128)(2,1)S(1)}, u32[]{:S(2)}, u32[]{:S(2)}) collective-permute-start(bf16[64,512]{1,0:T(8,128)(2,1)S(1)} %get-tuple-element.71), channel_id=1, source_target_pairs={{0,4},{1,5},{2,6},{3,7},{4,0},{5,1},{6,2},{7,3},{8,12},{9,13},{10,... | collective-permute-start | bytes 196616 | tf_op jit(solution)/shard_map/ppermute | solution.py:59
  37.0 5.5 %collective-permute-start.9 = (bf16[64,512]{1,0:T(8,128)(2,1)S(1)}, bf16[64,512]{1,0:T(8,128)(2,1)S(1)}, u32[]{:S(2)}, u32[]{:S(2)}) collective-permute-start(bf16[64,512]{1,0:T(8,128)(2,1)S(1)} %get-tuple-element.72), channel_id=1, source_target_pairs={{0,8},{1,9},{2,10},{3,11},{4,12},{5,13},{6,14},{7,15},{8,0},{9,1},... | collective-permute-start | bytes 196616 | tf_op jit(solution)/shard_map/ppermute | solution.py:59
  37.1 25.8 %copy-start = (bf16[2048,768]{1,0:T(8,128)(2,1)S(1)}, bf16[2048,768]{1,0:T(8,128)(2,1)}, u32[]{:S(2)}) copy-start(bf16[2048,768]{1,0:T(8,128)(2,1)} %refs_3_.5) | copy-start | bytes 9437188
  42.5 6.5 %collective-permute-start.12 = (bf16[64,512]{1,0:T(8,128)(2,1)S(1)}, bf16[64,512]{1,0:T(8,128)(2,1)S(1)}, u32[]{:S(2)}, u32[]{:S(2)}) collective-permute-start(bf16[64,512]{1,0:T(8,128)(2,1)S(1)} %get-tuple-element.89.refs_0_), channel_id=1, source_target_pairs={{0,4},{1,5},{2,6},{3,7},{4,0},{5,1},{6,2},{7,3},{8,12},{9,13},{10,... | collective-permute-start | bytes 196616 | tf_op jit(solution)/shard_map/ppermute | solution.py:59
  42.6 6.6 %collective-permute-start.13 = (bf16[64,512]{1,0:T(8,128)(2,1)S(1)}, bf16[64,512]{1,0:T(8,128)(2,1)S(1)}, u32[]{:S(2)}, u32[]{:S(2)}) collective-permute-start(bf16[64,512]{1,0:T(8,128)(2,1)S(1)} %get-tuple-element.89.refs_0_), channel_id=1, source_target_pairs={{0,8},{1,9},{2,10},{3,11},{4,12},{5,13},{6,14},{7,15},{8,0},{9,1},... | collective-permute-start | bytes 196616 | tf_op jit(solution)/shard_map/ppermute | solution.py:59
  45.4 6.5 %collective-permute-start.14 = (bf16[64,512]{1,0:T(8,128)(2,1)S(1)}, bf16[64,512]{1,0:T(8,128)(2,1)S(1)}, u32[]{:S(2)}, u32[]{:S(2)}) collective-permute-start(bf16[64,512]{1,0:T(8,128)(2,1)S(1)} %get-tuple-element.89.refs_0_), channel_id=1, source_target_pairs={{0,12},{1,13},{2,14},{3,15},{4,8},{5,9},{6,10},{7,11},{8,4},{9,5},... | collective-permute-start | bytes 196616 | tf_op jit(solution)/shard_map/ppermute | solution.py:59
  47.0 4.9 %collective-permute-start.15 = (bf16[64,512]{1,0:T(8,128)(2,1)S(1)}, bf16[64,512]{1,0:T(8,128)(2,1)S(1)}, u32[]{:S(2)}, u32[]{:S(2)}) collective-permute-start(bf16[64,512]{1,0:T(8,128)(2,1)S(1)} %get-tuple-element.93.refs_0_), channel_id=1, source_target_pairs={{0,2},{1,3},{2,0},{3,1},{4,6},{5,7},{6,4},{7,5},{8,10},{9,11},{10,... | collective-permute-start | bytes 196616 | tf_op jit(solution)/shard_map/ppermute | solution.py:59
  51.9 6.6 %collective-permute-start.19 = (bf16[128,512]{1,0:T(8,128)(2,1)S(1)}, bf16[128,512]{1,0:T(8,128)(2,1)S(1)}, u32[]{:S(2)}, u32[]{:S(2)}) collective-permute-start(bf16[128,512]{1,0:T(8,128)(2,1)S(1)} %shard_map.113.refs_0_), channel_id=1, source_target_pairs={{0,4},{1,5},{2,6},{3,7},{4,0},{5,1},{6,2},{7,3},{8,12},{9,13},{10,... | collective-permute-start | bytes 393224 | tf_op jit(solution)/shard_map/ppermute | solution.py:59
  52.0 9.7 %collective-permute-start.20 = (bf16[128,512]{1,0:T(8,128)(2,1)S(1)}, bf16[128,512]{1,0:T(8,128)(2,1)S(1)}, u32[]{:S(2)}, u32[]{:S(2)}) collective-permute-start(bf16[128,512]{1,0:T(8,128)(2,1)S(1)} %shard_map.113.refs_0_), channel_id=1, source_target_pairs={{0,8},{1,9},{2,10},{3,11},{4,12},{5,13},{6,14},{7,15},{8,0},{9,1},... | collective-permute-start | bytes 393224 | tf_op jit(solution)/shard_map/ppermute | solution.py:59
  54.1 7.6 %collective-permute-start.21 = (bf16[128,512]{1,0:T(8,128)(2,1)S(1)}, bf16[128,512]{1,0:T(8,128)(2,1)S(1)}, u32[]{:S(2)}, u32[]{:S(2)}) collective-permute-start(bf16[128,512]{1,0:T(8,128)(2,1)S(1)} %shard_map.113.refs_0_), channel_id=1, source_target_pairs={{0,12},{1,13},{2,14},{3,15},{4,8},{5,9},{6,10},{7,11},{8,4},{9,5},... | collective-permute-start | bytes 393224 | tf_op jit(solution)/shard_map/ppermute | solution.py:59
  56.4 6.5 %collective-permute-start.17 = (bf16[64,2048]{1,0:T(8,128)(2,1)S(1)}, bf16[64,2048]{1,0:T(8,128)(2,1)S(1)}, u32[]{:S(2)}, u32[]{:S(2)}) collective-permute-start(bf16[64,2048]{1,0:T(8,128)(2,1)S(1)} %shard_map.112.refs_0_), channel_id=1, source_target_pairs={{0,2},{1,3},{2,0},{3,1},{4,6},{5,7},{6,4},{7,5},{8,10},{9,11},{10,... | collective-permute-start | bytes 786440 | tf_op jit(solution)/shard_map/ppermute | solution.py:59
  61.8 2.7 %collective-permute-start.22 = (bf16[128,2048]{1,0:T(8,128)(2,1)S(1)}, bf16[128,2048]{1,0:T(8,128)(2,1)S(1)}, u32[]{:S(2)}, u32[]{:S(2)}) collective-permute-start(bf16[128,2048]{1,0:T(8,128)(2,1)S(1)} %shard_map.114.refs_2_), channel_id=1, source_target_pairs={{0,1},{1,0},{2,3},{3,2},{4,5},{5,4},{6,7},{7,6},{8,9},{9,8},{10,11... | collective-permute-start | bytes 1572872 | tf_op jit(solution)/shard_map/ppermute | solution.py:59
  61.8 2.6 %collective-permute-start.16 = (bf16[64,2048]{1,0:T(8,128)(2,1)S(1)}, bf16[64,2048]{1,0:T(8,128)(2,1)S(1)}, u32[]{:S(2)}, u32[]{:S(2)}) collective-permute-start(bf16[64,2048]{1,0:T(8,128)(2,1)S(1)} %shard_map.112.refs_0_), channel_id=1, source_target_pairs={{0,1},{1,0},{2,3},{3,2},{4,5},{5,4},{6,7},{7,6},{8,9},{9,8},{10,11... | collective-permute-start | bytes 786440 | tf_op jit(solution)/shard_map/ppermute | solution.py:59
  62.9 1.6 %collective-permute-start.18 = (bf16[64,2048]{1,0:T(8,128)(2,1)S(1)}, bf16[64,2048]{1,0:T(8,128)(2,1)S(1)}, u32[]{:S(2)}, u32[]{:S(2)}) collective-permute-start(bf16[64,2048]{1,0:T(8,128)(2,1)S(1)} %collective-permute-done.17.refs_1_), channel_id=1, source_target_pairs={{0,1},{1,0},{2,3},{3,2},{4,5},{5,4},{6,7},{7,6},{8,9},{9,8},{10,11... | collective-permute-start | bytes 786440 | tf_op jit(solution)/shard_map/ppermute | solution.py:59
  66.0 1.5 %collective-permute-start.23 = (bf16[320,128]{1,0:T(8,128)(2,1)S(1)}, bf16[320,128]{1,0:T(8,128)(2,1)S(1)}, u32[]{:S(2)}, u32[]{:S(2)}) collective-permute-start(bf16[320,128]{1,0:T(8,128)(2,1)S(1)} %get-tuple-element.102), channel_id=1, source_target_pairs={{0,1},{1,0},{2,3},{3,2},{4,5},{5,4},{6,7},{7,6},{8,9},{9,8},{10,11... | collective-permute-start | bytes 245768 | tf_op jit(solution)/shard_map/ppermute | solution.py:59
  67.5 5.0 %collective-permute-start.24 = (bf16[320,128]{1,0:T(8,128)(2,1)S(1)}, bf16[320,128]{1,0:T(8,128)(2,1)S(1)}, u32[]{:S(2)}, u32[]{:S(2)}) collective-permute-start(bf16[320,128]{1,0:T(8,128)(2,1)S(1)} %get-tuple-element.104), channel_id=1, source_target_pairs={{0,2},{1,3},{2,0},{3,1},{4,6},{5,7},{6,4},{7,5},{8,10},{9,11},{10,... | collective-permute-start | bytes 245768 | tf_op jit(solution)/shard_map/ppermute | solution.py:59
  72.6 4.9 %collective-permute-start.25 = (bf16[320,128]{1,0:T(8,128)(2,1)S(1)}, bf16[320,128]{1,0:T(8,128)(2,1)S(1)}, u32[]{:S(2)}, u32[]{:S(2)}) collective-permute-start(bf16[320,128]{1,0:T(8,128)(2,1)S(1)} %get-tuple-element.106), channel_id=1, source_target_pairs={{0,4},{1,5},{2,6},{3,7},{4,0},{5,1},{6,2},{7,3},{8,12},{9,13},{10,... | collective-permute-start | bytes 245768 | tf_op jit(solution)/shard_map/ppermute | solution.py:59
  74.1 8.8 %collective-permute-start.26 = (bf16[320,128]{1,0:T(8,128)(2,1)S(1)}, bf16[320,128]{1,0:T(8,128)(2,1)S(1)}, u32[]{:S(2)}, u32[]{:S(2)}) collective-permute-start(bf16[320,128]{1,0:T(8,128)(2,1)S(1)} %get-tuple-element.106), channel_id=1, source_target_pairs={{0,8},{1,9},{2,10},{3,11},{4,12},{5,13},{6,14},{7,15},{8,0},{9,1},... | collective-permute-start | bytes 245768 | tf_op jit(solution)/shard_map/ppermute | solution.py:59
  74.6 8.3 %collective-permute-start.27 = (bf16[320,128]{1,0:T(8,128)(2,1)S(1)}, bf16[320,128]{1,0:T(8,128)(2,1)S(1)}, u32[]{:S(2)}, u32[]{:S(2)}) collective-permute-start(bf16[320,128]{1,0:T(8,128)(2,1)S(1)} %get-tuple-element.106), channel_id=1, source_target_pairs={{0,12},{1,13},{2,14},{3,15},{4,8},{5,9},{6,10},{7,11},{8,4},{9,5},... | collective-permute-start | bytes 245768 | tf_op jit(solution)/shard_map/ppermute | solution.py:59
  83.0 1.3 %collective-permute-start.28 = (bf16[320,128]{1,0:T(8,128)(2,1)S(1)}, bf16[320,128]{1,0:T(8,128)(2,1)S(1)}, u32[]{:S(2)}, u32[]{:S(2)}) collective-permute-start(bf16[320,128]{1,0:T(8,128)(2,1)S(1)} %shard_map.119.refs_0_), channel_id=1, source_target_pairs={{0,1},{1,0},{2,3},{3,2},{4,5},{5,4},{6,7},{7,6},{8,9},{9,8},{10,11... | collective-permute-start | bytes 245768 | tf_op jit(solution)/shard_map/ppermute | solution.py:59

commit v15 on v14

--- a/solution.py
+++ b/solution.py
@@ -163,6 +163,11 @@
     )
 
 
+def reversed_bits(place, level):
+    bits = int(math.log2(level[0]))
+    return sum(((place >> bit) & 1) << (bits - 1 - bit) for bit in range(bits))
+
+
 def rows_at(place, size):
     return pl.ds(pl.multiple_of(place * size, 16), size)
 
@@ -187,8 +192,23 @@
         if along == 0:
             part = (rows_at(at, rows), slice(None))
         else:
-            part = (slice(None), cols_at(at, width))
+            part = (slice(None), cols_at(reversed_bits(at, level), width))
         out[...] = total_of(keep_ref, taken, part).astype(out.dtype)
+
+
+def halve_body(level, bit, keep_ref, taken_ref, own_ref, send_ref):
+    mine = (position(level) >> bit) & 1
+    width = own_ref.shape[1]
+    for out, half in ((own_ref, mine), (send_ref, 1 - mine)):
+        part = (slice(None), cols_at(half, width))
+        out[...] = total_of(keep_ref, [taken_ref], part).astype(out.dtype)
+
+
+def halve(keep, taken, level, bit):
+    rows, width = keep.shape
+    return local_call(
+        functools.partial(halve_body, level, bit), shares_of((rows, width // 2), 2), [keep, taken]
+    )
 
 
 def shares_of(shape, count):
@@ -235,11 +255,11 @@
     me = position(level)
     width = parts[0].shape[along]
     for step, ref in enumerate(parts):
-        at = pl.multiple_of((me ^ step) * width, width)
+        at = me ^ step
         if along == 0:
-            out_ref[pl.ds(at, width), :] = ref[...]
+            out_ref[pl.ds(pl.multiple_of(at * width, width), width), :] = ref[...]
         else:
-            out_ref[:, pl.ds(at, width)] = ref[...]
+            out_ref[:, cols_at(reversed_bits(at, level), width)] = ref[...]
 
 
 def place(parts, level, along):
@@ -317,21 +337,28 @@
     )(response, low, high, orbitals, matrix, *lines, *bounds)
 
 
-def pad_body(edge, o_ref, pad_ref):
+def pad_body(core, edge, o_ref, pad_ref, sides_ref):
     bands, cells = o_ref.shape
     pad_ref[:edge, :] = jnp.zeros((edge, cells), pad_ref.dtype)
     pad_ref[edge : edge + bands, :] = o_ref[...]
     pad_ref[edge + bands :, :] = jnp.zeros((edge, cells), pad_ref.dtype)
-
-
-def pad_orbitals(orbitals, blk):
+    c = position(core)
+    sides_ref[0] = c
+    sides_ref[1] = 1 - c
+
+
+def pad_orbitals(orbitals, core, blk):
     bands, cells = orbitals.shape
     edge = REACH * blk
-    return local_call(
-        functools.partial(pad_body, edge),
-        struct((bands + 2 * edge, cells), orbitals.dtype),
-        [orbitals],
-    )
+    padded, sides = struct((bands + 2 * edge, cells), orbitals.dtype), struct((2,), jnp.int32)
+    return pl.pallas_call(
+        functools.partial(pad_body, core, edge),
+        out_shape=[padded, sides],
+        in_specs=[whole()],
+        out_specs=[whole(), pl.BlockSpec(memory_space=pltpu.SMEM)],
+        compiler_params=params(),
+        cost_estimate=cost(0, orbitals, padded),
+    )(orbitals)
 
 
 def subgroup(shape, blk):
@@ -423,30 +450,12 @@
     return local_call(sum_body, outs, [keep, *taken])
 
 
-def project_body(core, blk, *refs):
-    w_own, w_other, u_own, u_other, pad_ref, r_ref, mask_ref = refs[:7]
-    updated_ref, residual_ref, w_ref, u_ref = refs[7:]
+def project_body(core, blk, other, *refs):
+    w_ref, u_ref, pad_ref, r_ref, mask_ref = refs[:5]
+    updated_ref, residual_ref = refs[-2:]
     rows = u_ref.shape[0]
-    height = w_ref.shape[0]
-    per = u_own.shape[0] // rows
-    g = pl.program_id(0)
-    own = lax.div(g, jnp.int32(per)) == position(core)
-    local = lax.rem(g, jnp.int32(per))
-    w_rows = pl.ds(pl.multiple_of(local * height, 16), height)
-    u_rows = pl.ds(pl.multiple_of(local * rows, rows), rows)
-
-    @pl.when(own)
-    def _():
-        w_ref[...] = w_own[w_rows, :]
-        u_ref[...] = u_own[u_rows, :]
-
-    @pl.when(jnp.logical_not(own))
-    def _():
-        w_ref[...] = w_other[w_rows, :]
-        u_ref[...] = u_other[u_rows, :]
-
     main, rest = w_ref[:rows, :].astype(F32), w_ref[rows:, :].astype(F32)
-    start = pl.multiple_of(g * rows, rows)
+    start = pl.multiple_of(group_of(core, other) * rows, rows)
     residual = u_ref[...]
     for k, part in enumerate(unpacked(main, rest, blk)):
         inside = mask_ref[:, k * rows : (k + 1) * rows].astype(F32) > 0.5
@@ -457,33 +466,42 @@
     updated_ref[...] = (r_ref[...].astype(F32) + STEP_SIZE * residual).astype(BF16)
 
 
-def project(weights, unprojected, padded, response, mask, core, group_rows, blk):
+def group_of(core, other):
+    c = position(core)
+    return (1 - c if other else c) * pl.num_programs(0) + pl.program_id(0)
+
+
+def project(weights, unprojected, padded, response, mask, sides, core, group_rows, blk, other, before):
     bands, cells = response.shape
+    rows = unprojected.shape[0]
+    per = rows // group_rows
+    height = weights.shape[0] // per
     out = struct((bands, cells), BF16)
-    here = pl.BlockSpec((group_rows, cells), lambda g: (g, 0))
-
-    def full(a):
-        return pl.BlockSpec(a.shape, lambda g: (0, 0))
-
+
+    def there(g, sides):
+        return (sides[1 if other else 0] * per + g, 0)
+
+    here = pl.BlockSpec((group_rows, cells), there)
     return pl.pallas_call(
-        functools.partial(project_body, core, blk),
-        grid=(bands // group_rows,),
+        lambda sides_ref, *refs: project_body(core, blk, other, *refs),
+        grid_spec=pltpu.PrefetchScalarGridSpec(
+            num_scalar_prefetch=1,
+            grid=(per,),
+            in_specs=[
+                pl.BlockSpec((height, group_rows), lambda g, sides: (g, 0)),
+                pl.BlockSpec((group_rows, cells), lambda g, sides: (g, 0)),
+                pl.BlockSpec(padded.shape, lambda g, sides: (0, 0)),
+                here,
+                pl.BlockSpec((group_rows, mask.shape[1]), there),
+                *[pl.BlockSpec(memory_space=pl.ANY)] * len(before),
+            ],
+            out_specs=(here, here),
+        ),
         out_shape=(out, out),
-        in_specs=[
-            *[full(a) for a in (*weights, *unprojected, padded)],
-            here,
-            pl.BlockSpec((group_rows, mask.shape[1]), lambda g: (g, 0)),
-        ],
-        out_specs=(here, here),
-        scratch_shapes=[
-            pltpu.VMEM((group_rows + 2 * blk, group_rows), BF16),
-            pltpu.VMEM((group_rows, cells), F32),
-        ],
+        input_output_aliases={6: 0, 7: 1} if before else {},
         compiler_params=params(),
-        cost_estimate=cost(
-            4 * bands * group_rows * cells, padded, *unprojected, response, out, out
-        ),
-    )(*weights, *unprojected, padded, response, mask)
+        cost_estimate=cost(4 * rows * group_rows * cells, padded, unprojected, unprojected),
+    )(sides, weights, unprojected, padded, response, mask, *before)
 
 
 def shards(
@@ -519,17 +537,19 @@
     sent_x, sent_z, keep_x, keep_z = first_sums(response, projectors, core, block, first)
     sent_z = swapped(sent_z, count, core, 1)
     sent_x = swapped(sent_x, count, core, 1)
-    keep_z, *parts_z = split(keep_z, [sent_z], along, 1)
-    sent_x, parts_z[0] = lax.optimization_barrier((sent_x, parts_z[0]))
+    keep_z, part_z = halve(keep_z, sent_z, along, 0)
     keep_x, *parts_x = split(keep_x, [sent_x], across, 0)
-    parts_z[-1], low = lax.optimization_barrier((parts_z[-1], low))
+    parts_x, low = lax.optimization_barrier((parts_x, low))
+    for bit in range(1, int(math.log2(along[0]))):
+        keep_z, part_z = halve(keep_z, swapped(part_z, count, along, 1 << (bit - 1)), along, bit)
+    taken_z = [swapped(part_z, count, along, along[0] // 2)]
     taken_z, taken_x, low, high = lax.optimization_barrier(
-        (parts_to(parts_z, along), parts_to(parts_x, across), low, high)
+        (taken_z, parts_to(parts_x, across), low, high)
     )
     base, mask = local_part(
         response, low, high, orbitals, matrix, lines, bounds, group_rows, width, blk
     )
-    padded = pad_orbitals(orbitals, blk)
+    padded, sides = pad_orbitals(orbitals, core, blk)
     keep_x, *parts_x = split(keep_x, taken_x, along, 1)
     keep_z, *parts_z = split(keep_z, taken_z, across, 0)
     taken_x, taken_z, base, padded = lax.optimization_barrier(
@@ -557,12 +577,13 @@
     wide, keep = apply(blocks, projectors, base, padded, *sizes, False)
     others, keep = lax.optimization_barrier((others, keep))
     other_wide, part = apply(others, projectors, base, padded, *sizes, True)
-    unprojected = (wide, other_wide)
     total, part = add_up(keep, to(part, core))
     total, part = add_up(total, to(part, across))
     own = finish(total, to(part, along), window_scale)
-    weights = (own, *to(own, core))
-    return project(weights, unprojected, padded, response, mask, core, group_rows, blk)
+    (theirs,) = to(own, core)
+    sizes = (core, group_rows, blk)
+    outs = project(own, wide, padded, response, mask, sides, *sizes, False, ())
+    return project(theirs, other_wide, padded, response, mask, sides, *sizes, True, outs)
 
 
 def solution(mesh):

time: 86.9 us -> 89.1 us (1.025)
  waiting for transfers between devices: 35.6 us -> 39.4 us
  starting transfers between devices: 37.4 us -> 33.8 us
  Pallas kernels: 12.8 us -> 14.8 us
    ppermute x27 -> x26, starting transfers between devices: 33.8 us -> 30.1 us  [swapped(): return lax.ppermute(array, 'band', pairs)]
    ppermute x2, waiting for transfers between devices: 1.06 us -> 4.44 us  [neighbour(): lax.ppermute(array, 'band', [(i, (i + step) % count) for i in range(count)])]
    pallas_call x1 -> x3, Pallas kernels: 2.43 us -> 4.49 us  [the longest x2 3.83 us: project(): pl.pallas_call(lambda sides_ref, *refs: project_body(core, blk, other, *r...]
    ppermute x27 -> x26, waiting for transfers between devices: 34.5 us -> 34.9 us  [swapped(): return lax.ppermute(array, 'band', pairs)]
  transfers between devices with their start and end apart: 29 -> 28, of which waited for: 14 -> 16; matrix products, arithmetic and copies ran while one was open for 0% -> 0% of each run, Pallas kernels for 10% -> 13%
where the time goes in v15:
time: 89.1 us; the launch traced here: 88.9 us
  waiting for transfers between devices  39.4 us (44%)
  starting transfers between devices  33.8 us (38%)
  Pallas kernels  14.8 us (17%)
  between operations  0.94 us (1%)
    ppermute x26, waiting for transfers between devices, swapped(): return lax.ppermute(array, 'band', pairs)  34.9 us
    ppermute x26, starting transfers between devices, swapped(): return lax.ppermute(array, 'band', pairs)  30.1 us
    ppermute x2, waiting for transfers between devices, neighbour(): lax.ppermute(array, 'band', [(i, (i + step) % count) for i in range(count)])  4.44 us
    pallas_call x1, Pallas kernels, first_sums(): pl.pallas_call(functools.partial(first_body, core, block, tile), out_shap...  4.34 us
    pallas_call x2, Pallas kernels, project(): pl.pallas_call(lambda sides_ref, *refs: project_body(core, blk, other, *r...  3.83 us
    pallas_call x14, Pallas kernels, local_call(): pl.pallas_call(body, out_shape=outs, in_specs=[whole() for _ in args], ou...  3.65 us
    ppermute x2, starting transfers between devices, neighbour(): lax.ppermute(array, 'band', [(i, (i + step) % count) for i in range(count)])  3.62 us
    pallas_call x1, Pallas kernels, local_part(): pl.pallas_call(functools.partial(local_body, depth, (group_rows, blk)), g...  2.29 us
  transfers between devices with their start and end apart: 28, of which 16 were waited for; matrix products, arithmetic and copies ran while one was open for 0% of the time, Pallas kernels for 13%

profile of v15, /device:TPU:0, one launch (start us, length us, event | category | flops | bytes accessed | tf_op | source)
XLA Modules:
  0.0 88.9 jit_solution(5720428931530457653)
XLA Ops:
  0.6 0.5 collective-permute-start.4
  1.1 4.3 %shard_map.105 = (bf16[128,2048]{1,0:T(8,128)(2,1)S(1)}, bf16[128,2048]{1,0:T(8,128)(2,1)S(1)}, f32[128,2048]{1,0:T(8,128)S(1)}, f32[128,2048]{1,0:T(8,128)S(1)}) custom-call(bf16[512,768]{1,0:T(8,128)(2,1)} %refs_3_.9, bf16[2048,768]{1,0:T(8,128)(2,1)} %refs_3_.7), custom_call_target="tpu_custom_call" | custom-call | flops 1610612736 | bytes 6291456 | tf_op jit(solution)/shard_map/pallas_call | solution.py:147
  5.5 0.0 copy-start.7
  5.5 0.0 copy-start.8
  5.5 0.0 copy-start.2
  5.5 0.0 copy-start.3
  5.5 0.0 copy-start.4
  5.5 0.0 copy-start.5
  5.6 0.0 copy-start.6
  5.6 2.6 %collective-permute-start.1 = (bf16[128,2048]{1,0:T(8,128)(2,1)S(1)}, bf16[128,2048]{1,0:T(8,128)(2,1)S(1)}, u32[]{:S(2)}, u32[]{:S(2)}) collective-permute-start(bf16[128,2048]{1,0:T(8,128)(2,1)S(1)} %get-tuple-element.61), channel_id=1, source_target_pairs={{0,1},{1,0},{2,3},{3,2},{4,5},{5,4},{6,7},{7,6},{8,9},{9,8},{10,11... | collective-permute-start | bytes 1572872 | tf_op jit(solution)/shard_map/ppermute | solution.py:59
  8.2 0.1 collective-permute-start
  8.3 3.1 %collective-permute-start.6 = (bf16[512,768]{1,0:T(8,128)(2,1)S(1)}, bf16[512,768]{1,0:T(8,128)(2,1)S(1)}, u32[]{:S(2)}, u32[]{:S(2)}) collective-permute-start(bf16[512,768]{1,0:T(8,128)(2,1)S(1)} %copy-done.1), channel_id=1, source_target_pairs={{0,15},{1,0},{2,1},{3,2},{4,3},{5,4},{6,5},{7,6},{8,7},{9,8},{10,9... | collective-permute-start | bytes 2359304 | tf_op jit(solution)/shard_map/ppermute | solution.py:50
  11.4 0.1 shard_map.107
  11.5 0.1 collective-permute-start.2
  11.6 0.1 shard_map.106
  11.8 4.4 %collective-permute-done.4.refs_1_ = bf16[512,768]{1,0:T(8,128)(2,1)S(1)} collective-permute-done((bf16[512,768]{1,0:T(8,128)(2,1)}, bf16[512,768]{1,0:T(8,128)(2,1)S(1)}, u32[]{:S(2)}, u32[]{:S(2)}) %collective-permute-start.4) | collective-permute-done | bytes 786464 | tf_op jit(solution)/shard_map/ppermute | solution.py:50
  16.2 0.0 collective-permute-start.5
  16.2 10.7 %collective-permute-done.2.taken_ref = bf16[128,1024]{1,0:T(8,128)(2,1)S(1)} collective-permute-done((bf16[128,1024]{1,0:T(8,128)(2,1)S(1)}, bf16[128,1024]{1,0:T(8,128)(2,1)S(1)}, u32[]{:S(2)}, u32[]{:S(2)}) %collective-permute-start.2) | collective-permute-done | bytes 262176 | tf_op jit(solution)/shard_map/ppermute | solution.py:59
  26.9 0.1 shard_map.108
  27.0 2.7 %collective-permute-start.3 = (bf16[128,512]{1,0:T(8,128)(2,1)S(1)}, bf16[128,512]{1,0:T(8,128)(2,1)S(1)}, u32[]{:S(2)}, u32[]{:S(2)}) collective-permute-start(bf16[128,512]{1,0:T(8,128)(2,1)S(1)} %get-tuple-element.64), channel_id=1, source_target_pairs={{0,8},{1,9},{2,10},{3,11},{4,12},{5,13},{6,14},{7,15},{8,0},{9,1},... | collective-permute-start | bytes 393224 | tf_op jit(solution)/shard_map/ppermute | solution.py:59
  29.6 0.0 collective-permute-done.6.refs_2_
  29.6 5.9 %collective-permute-done.3.refs_1_ = bf16[128,512]{1,0:T(8,128)(2,1)S(1)} collective-permute-done((bf16[128,512]{1,0:T(8,128)(2,1)S(1)}, bf16[128,512]{1,0:T(8,128)(2,1)S(1)}, u32[]{:S(2)}, u32[]{:S(2)}) %collective-permute-start.3) | collective-permute-done | bytes 131104 | tf_op jit(solution)/shard_map/ppermute | solution.py:59
  35.5 0.1 collective-permute-start.10
  35.6 0.1 shard_map.109
  35.7 0.3 collective-permute-start.7
  36.0 3.4 %collective-permute-start.8 = (bf16[64,512]{1,0:T(8,128)(2,1)S(1)}, bf16[64,512]{1,0:T(8,128)(2,1)S(1)}, u32[]{:S(2)}, u32[]{:S(2)}) collective-permute-start(bf16[64,512]{1,0:T(8,128)(2,1)S(1)} %get-tuple-element.71), channel_id=1, source_target_pairs={{0,8},{1,9},{2,10},{3,11},{4,12},{5,13},{6,14},{7,15},{8,0},{9,1},... | collective-permute-start | bytes 196616 | tf_op jit(solution)/shard_map/ppermute | solution.py:59
  39.4 0.8 collective-permute-start.9
  40.2 0.0 copy-start
  40.2 0.7 shard_map.104
  40.9 2.3 %shard_map.111 = (f32[512,768]{1,0:T(8,128)S(1)}, bf16[512,256]{1,0:T(8,128)(2,1)S(1)}) custom-call(bf16[512,768]{1,0:T(8,128)(2,1)S(1)} %copy-done.1, bf16[512,768]{1,0:T(8,128)(2,1)S(1)} %collective-permute-done.4.refs_1_, bf16[512,768]{1,0:T(8,128)(2,1)S(1)} %collective-permute-done.6.refs_2_, bf16[512,768]{1,0:T(8,128)(2,1)S(1)} %copy-done.2, ...), custom_call_target="tpu_custom_call" | custom-call | flops 235929600 | bytes 4980736 | tf_op jit(solution)/shard_map/pallas_call | solution.py:318
  43.2 0.2 collective-permute-done.8.refs_2_
  43.4 2.0 %collective-permute-done.9.refs_3_ = bf16[64,512]{1,0:T(8,128)(2,1)S(1)} collective-permute-done((bf16[64,512]{1,0:T(8,128)(2,1)S(1)}, bf16[64,512]{1,0:T(8,128)(2,1)S(1)}, u32[]{:S(2)}, u32[]{:S(2)}) %collective-permute-start.9) | collective-permute-done | bytes 65568 | tf_op jit(solution)/shard_map/ppermute | solution.py:59
  45.4 0.1 shard_map.112
  45.5 0.1 collective-permute-start.11
  45.5 1.7 %collective-permute-start.12 = (bf16[64,512]{1,0:T(8,128)(2,1)S(1)}, bf16[64,512]{1,0:T(8,128)(2,1)S(1)}, u32[]{:S(2)}, u32[]{:S(2)}) collective-permute-start(bf16[64,512]{1,0:T(8,128)(2,1)S(1)} %get-tuple-element.87.refs_0_), channel_id=1, source_target_pairs={{0,8},{1,9},{2,10},{3,11},{4,12},{5,13},{6,14},{7,15},{8,0},{9,1},... | collective-permute-start | bytes 196616 | tf_op jit(solution)/shard_map/ppermute | solution.py:59
  47.3 2.7 %collective-permute-start.13 = (bf16[64,512]{1,0:T(8,128)(2,1)S(1)}, bf16[64,512]{1,0:T(8,128)(2,1)S(1)}, u32[]{:S(2)}, u32[]{:S(2)}) collective-permute-start(bf16[64,512]{1,0:T(8,128)(2,1)S(1)} %get-tuple-element.87.refs_0_), channel_id=1, source_target_pairs={{0,12},{1,13},{2,14},{3,15},{4,8},{5,9},{6,10},{7,11},{8,4},{9,5},... | collective-permute-start | bytes 196616 | tf_op jit(solution)/shard_map/ppermute | solution.py:59
  49.9 2.0 %collective-permute-start.14 = (bf16[64,512]{1,0:T(8,128)(2,1)S(1)}, bf16[64,512]{1,0:T(8,128)(2,1)S(1)}, u32[]{:S(2)}, u32[]{:S(2)}) collective-permute-start(bf16[64,512]{1,0:T(8,128)(2,1)S(1)} %get-tuple-element.91.refs_0_), channel_id=1, source_target_pairs={{0,2},{1,3},{2,0},{3,1},{4,6},{5,7},{6,4},{7,5},{8,10},{9,11},{10,... | collective-permute-start | bytes 196616 | tf_op jit(solution)/shard_map/ppermute | solution.py:59
  51.9 1.7 %collective-permute-done.13.refs_3_ = bf16[64,512]{1,0:T(8,128)(2,1)S(1)} collective-permute-done((bf16[64,512]{1,0:T(8,128)(2,1)S(1)}, bf16[64,512]{1,0:T(8,128)(2,1)S(1)}, u32[]{:S(2)}, u32[]{:S(2)}) %collective-permute-start.13) | collective-permute-done | bytes 65568 | tf_op jit(solution)/shard_map/ppermute | solution.py:59
  53.6 0.5 collective-permute-done.14.refs_1_
  54.2 0.1 collective-permute-start.18
  54.3 3.2 %collective-permute-start.19 = (bf16[128,512]{1,0:T(8,128)(2,1)S(1)}, bf16[128,512]{1,0:T(8,128)(2,1)S(1)}, u32[]{:S(2)}, u32[]{:S(2)}) collective-permute-start(bf16[128,512]{1,0:T(8,128)(2,1)S(1)} %shard_map.114.refs_0_), channel_id=1, source_target_pairs={{0,8},{1,9},{2,10},{3,11},{4,12},{5,13},{6,14},{7,15},{8,0},{9,1},... | collective-permute-start | bytes 393224 | tf_op jit(solution)/shard_map/ppermute | solution.py:59
  57.4 1.2 %collective-permute-start.20 = (bf16[128,512]{1,0:T(8,128)(2,1)S(1)}, bf16[128,512]{1,0:T(8,128)(2,1)S(1)}, u32[]{:S(2)}, u32[]{:S(2)}) collective-permute-start(bf16[128,512]{1,0:T(8,128)(2,1)S(1)} %shard_map.114.refs_0_), channel_id=1, source_target_pairs={{0,12},{1,13},{2,14},{3,15},{4,8},{5,9},{6,10},{7,11},{8,4},{9,5},... | collective-permute-start | bytes 393224 | tf_op jit(solution)/shard_map/ppermute | solution.py:59
  58.7 2.1 %collective-permute-start.16 = (bf16[64,2048]{1,0:T(8,128)(2,1)S(1)}, bf16[64,2048]{1,0:T(8,128)(2,1)S(1)}, u32[]{:S(2)}, u32[]{:S(2)}) collective-permute-start(bf16[64,2048]{1,0:T(8,128)(2,1)S(1)} %shard_map.113.refs_0_), channel_id=1, source_target_pairs={{0,2},{1,3},{2,0},{3,1},{4,6},{5,7},{6,4},{7,5},{8,10},{9,11},{10,... | collective-permute-start | bytes 786440 | tf_op jit(solution)/shard_map/ppermute | solution.py:59
  60.8 1.7 %collective-permute-done.19.refs_2_ = bf16[128,512]{1,0:T(8,128)(2,1)S(1)} collective-permute-done((bf16[128,512]{1,0:T(8,128)(2,1)S(1)}, bf16[128,512]{1,0:T(8,128)(2,1)S(1)}, u32[]{:S(2)}, u32[]{:S(2)}) %collective-permute-start.19) | collective-permute-done | bytes 131104 | tf_op jit(solution)/shard_map/ppermute | solution.py:59
  62.4 1.9 %collective-permute-done.20.refs_3_ = bf16[128,512]{1,0:T(8,128)(2,1)S(1)} collective-permute-done((bf16[128,512]{1,0:T(8,128)(2,1)S(1)}, bf16[128,512]{1,0:T(8,128)(2,1)S(1)}, u32[]{:S(2)}, u32[]{:S(2)}) %collective-permute-start.20) | collective-permute-done | bytes 131104 | tf_op jit(solution)/shard_map/ppermute | solution.py:59
  64.4 0.1 collective-permute-start.21
  64.5 0.5 collective-permute-start.15
  64.9 0.2 collective-permute-done.16.refs_1_
  65.1 1.5 %shard_map.116 = (f32[256,768]{1,0:T(8,128)S(1)}, f32[320,128]{1,0:T(8,128)S(1)}) custom-call(bf16[64,2048]{1,0:T(8,128)(2,1)S(1)} %shard_map.113.refs_0_, bf16[64,2048]{1,0:T(8,128)(2,1)S(1)} %collective-permute-done.16.refs_1_, bf16[128,2048]{1,0:T(8,128)(2,1)S(1)} %shard_map.115.refs_2_, bf16[2048,768]{1,0:T(8,128)(2,1)S(1)} %copy-done, ...), custom_call_target="tpu_custom_call" | custom-call | flops 905969664 | bytes 7700480 | tf_op jit(solution)/shard_map/pallas_call | solution.py:91
  66.7 0.1 collective-permute-done.15.refs_0_
  66.7 0.4 collective-permute-done.17.refs_1_
  67.1 1.5 %shard_map.117 = (f32[256,768]{1,0:T(8,128)S(1)}, bf16[320,128]{1,0:T(8,128)(2,1)S(1)}) custom-call(bf16[64,2048]{1,0:T(8,128)(2,1)S(1)} %collective-permute-done.15.refs_0_, bf16[64,2048]{1,0:T(8,128)(2,1)S(1)} %collective-permute-done.17.refs_1_, bf16[128,2048]{1,0:T(8,128)(2,1)S(1)} %collective-permute-done.21.refs_2_, bf16[2048,768]{1,0:T(8,128)(2,1)S(1)} %copy-done, ...), custom_call_target="tpu_custom_call" | custom-call | flops 905969664 | bytes 7618560 | tf_op jit(solution)/shard_map/pallas_call | solution.py:91
  68.6 0.2 collective-permute-start.22
  68.8 1.1 %collective-permute-done.22.refs_0_ = bf16[320,128]{1,0:T(8,128)(2,1)S(1)} collective-permute-done((bf16[320,128]{1,0:T(8,128)(2,1)S(1)}, bf16[320,128]{1,0:T(8,128)(2,1)S(1)}, u32[]{:S(2)}, u32[]{:S(2)}) %collective-permute-start.22) | collective-permute-done | bytes 81952 | tf_op jit(solution)/shard_map/ppermute | solution.py:59
  70.0 1.9 %collective-permute-start.23 = (bf16[320,128]{1,0:T(8,128)(2,1)S(1)}, bf16[320,128]{1,0:T(8,128)(2,1)S(1)}, u32[]{:S(2)}, u32[]{:S(2)}) collective-permute-start(bf16[320,128]{1,0:T(8,128)(2,1)S(1)} %get-tuple-element.102), channel_id=1, source_target_pairs={{0,2},{1,3},{2,0},{3,1},{4,6},{5,7},{6,4},{7,5},{8,10},{9,11},{10,... | collective-permute-start | bytes 245768 | tf_op jit(solution)/shard_map/ppermute | solution.py:59
  71.9 2.8 %collective-permute-done.23.refs_0_ = bf16[320,128]{1,0:T(8,128)(2,1)S(1)} collective-permute-done((bf16[320,128]{1,0:T(8,128)(2,1)S(1)}, bf16[320,128]{1,0:T(8,128)(2,1)S(1)}, u32[]{:S(2)}, u32[]{:S(2)}) %collective-permute-start.23) | collective-permute-done | bytes 81952 | tf_op jit(solution)/shard_map/ppermute | solution.py:59
  74.8 1.4 %collective-permute-start.24 = (bf16[320,128]{1,0:T(8,128)(2,1)S(1)}, bf16[320,128]{1,0:T(8,128)(2,1)S(1)}, u32[]{:S(2)}, u32[]{:S(2)}) collective-permute-start(bf16[320,128]{1,0:T(8,128)(2,1)S(1)} %get-tuple-element.104), channel_id=1, source_target_pairs={{0,4},{1,5},{2,6},{3,7},{4,0},{5,1},{6,2},{7,3},{8,12},{9,13},{10,... | collective-permute-start | bytes 245768 | tf_op jit(solution)/shard_map/ppermute | solution.py:59
  76.2 1.7 %collective-permute-start.25 = (bf16[320,128]{1,0:T(8,128)(2,1)S(1)}, bf16[320,128]{1,0:T(8,128)(2,1)S(1)}, u32[]{:S(2)}, u32[]{:S(2)}) collective-permute-start(bf16[320,128]{1,0:T(8,128)(2,1)S(1)} %get-tuple-element.104), channel_id=1, source_target_pairs={{0,8},{1,9},{2,10},{3,11},{4,12},{5,13},{6,14},{7,15},{8,0},{9,1},... | collective-permute-start | bytes 245768 | tf_op jit(solution)/shard_map/ppermute | solution.py:59
  77.9 1.3 %collective-permute-start.26 = (bf16[320,128]{1,0:T(8,128)(2,1)S(1)}, bf16[320,128]{1,0:T(8,128)(2,1)S(1)}, u32[]{:S(2)}, u32[]{:S(2)}) collective-permute-start(bf16[320,128]{1,0:T(8,128)(2,1)S(1)} %get-tuple-element.104), channel_id=1, source_target_pairs={{0,12},{1,13},{2,14},{3,15},{4,8},{5,9},{6,10},{7,11},{8,4},{9,5},... | collective-permute-start | bytes 245768 | tf_op jit(solution)/shard_map/ppermute | solution.py:59
  79.2 0.9 %collective-permute-done.24.refs_0_ = bf16[320,128]{1,0:T(8,128)(2,1)S(1)} collective-permute-done((bf16[320,128]{1,0:T(8,128)(2,1)S(1)}, bf16[320,128]{1,0:T(8,128)(2,1)S(1)}, u32[]{:S(2)}, u32[]{:S(2)}) %collective-permute-start.24) | collective-permute-done | bytes 81952 | tf_op jit(solution)/shard_map/ppermute | solution.py:59
  80.2 4.8 %collective-permute-done.25.refs_1_ = bf16[320,128]{1,0:T(8,128)(2,1)S(1)} collective-permute-done((bf16[320,128]{1,0:T(8,128)(2,1)S(1)}, bf16[320,128]{1,0:T(8,128)(2,1)S(1)}, u32[]{:S(2)}, u32[]{:S(2)}) %collective-permute-start.25) | collective-permute-done | bytes 81952 | tf_op jit(solution)/shard_map/ppermute | solution.py:59
  85.0 0.1 collective-permute-start.27
  85.1 1.9 %shard_map.121 = (bf16[512,768]{1,0:T(8,128)(2,1)}, bf16[512,768]{1,0:T(8,128)(2,1)}) custom-call(s32[2]{0:T(128)S(1)} %get-tuple-element.56.sides_ref, bf16[320,128]{1,0:T(8,128)(2,1)S(1)} %shard_map.120.refs_0_, f32[256,768]{1,0:T(8,128)S(1)} %get-tuple-element.107.refs_1_, bf16[640,768]{1,0:T(8,128)(2,1)S(1)} %get-tuple-element.94.refs_5_.refs_2_, ...), custom_call_target="tpu_custom_call" | custom-call | flops 100663296 | bytes 2555904 | tf_op jit(solution)/shard_map/pallas_call | solution.py:485
  87.0 1.9 %shard_map.122 = (bf16[512,768]{1,0:T(8,128)(2,1)}, bf16[512,768]{1,0:T(8,128)(2,1)}) custom-call(s32[2]{0:T(128)S(1)} %get-tuple-element.56.sides_ref, bf16[320,128]{1,0:T(8,128)(2,1)S(1)} %collective-permute-done.27.refs_0_, f32[256,768]{1,0:T(8,128)S(1)} %get-tuple-element.105.refs_1_, ...), custom_call_target="tpu_custom_call", output_to_operand_aliasing={{0}: (6, {}), {1}: (7, {})} | custom-call | flops 100663296 | bytes 2555904 | tf_op jit(solution)/shard_map/pallas_call | solution.py:485
  (31 shorter events, 0.3 us)
Async XLA Ops:
  0.6 7.7 %copy-start.1 = (bf16[512,768]{1,0:T(8,128)(2,1)S(1)}, bf16[512,768]{1,0:T(8,128)(2,1)}, u32[]{:S(2)}) copy-start(bf16[512,768]{1,0:T(8,128)(2,1)} %refs_3_.9) | copy-start | bytes 2359300
  0.6 15.6 %collective-permute-start.4 = (bf16[512,768]{1,0:T(8,128)(2,1)}, bf16[512,768]{1,0:T(8,128)(2,1)S(1)}, u32[]{:S(2)}, u32[]{:S(2)}) collective-permute-start(bf16[512,768]{1,0:T(8,128)(2,1)} %refs_3_.9), channel_id=1, source_target_pairs={{0,1},{1,2},{2,3},{3,4},{4,5},{5,6},{6,7},{7,8},{8,9},{9,10},{10,1... | collective-permute-start | bytes 2359304 | tf_op jit(solution)/shard_map/ppermute | solution.py:50
  5.5 34.7 %copy-start.7 = (f32[768]{0:T(1024)S(1)}, f32[768]{0:T(1024)}, u32[]{:S(2)}) copy-start(f32[768]{0:T(1024)} %param.12) | copy-start | bytes 9220
  5.5 34.7 %copy-start.8 = (f32[768]{0:T(1024)S(1)}, f32[768]{0:T(1024)}, u32[]{:S(2)}) copy-start(f32[768]{0:T(1024)} %param.13) | copy-start | bytes 9220
  5.5 34.7 %copy-start.2 = (bf16[512,768]{1,0:T(8,128)(2,1)S(1)}, bf16[512,768]{1,0:T(8,128)(2,1)}, u32[]{:S(2)}) copy-start(bf16[512,768]{1,0:T(8,128)(2,1)} %refs_3_.5) | copy-start | bytes 2359300
  5.5 35.3 %copy-start.3 = (bf16[2,128,128]{2,1,0:T(8,128)(2,1)S(1)}, bf16[2,128,128]{2,1,0:T(8,128)(2,1)}, u32[]{:S(2)}) copy-start(bf16[2,128,128]{2,1,0:T(8,128)(2,1)} %constant.2.clone.refs_4_) | copy-start | bytes 196612
  5.5 35.3 %copy-start.4 = (f32[512]{0:T(512)S(1)}, f32[512]{0:T(512)}, u32[]{:S(2)}) copy-start(f32[512]{0:T(512)} %param.14) | copy-start | bytes 6148
  5.5 35.3 %copy-start.5 = (s32[512]{0:T(512)S(1)}, s32[512]{0:T(512)}, u32[]{:S(2)}) copy-start(s32[512]{0:T(512)} %param.15) | copy-start | bytes 6148
  5.6 35.3 %copy-start.6 = (s32[512]{0:T(512)S(1)}, s32[512]{0:T(512)}, u32[]{:S(2)}) copy-start(s32[512]{0:T(512)} %param.16) | copy-start | bytes 6148
  5.6 5.8 %collective-permute-start.1 = (bf16[128,2048]{1,0:T(8,128)(2,1)S(1)}, bf16[128,2048]{1,0:T(8,128)(2,1)S(1)}, u32[]{:S(2)}, u32[]{:S(2)}) collective-permute-start(bf16[128,2048]{1,0:T(8,128)(2,1)S(1)} %get-tuple-element.61), channel_id=1, source_target_pairs={{0,1},{1,0},{2,3},{3,2},{4,5},{5,4},{6,7},{7,6},{8,9},{9,8},{10,11... | collective-permute-start | bytes 1572872 | tf_op jit(solution)/shard_map/ppermute | solution.py:59
  8.2 3.4 %collective-permute-start = (bf16[128,2048]{1,0:T(8,128)(2,1)S(1)}, bf16[128,2048]{1,0:T(8,128)(2,1)S(1)}, u32[]{:S(2)}, u32[]{:S(2)}) collective-permute-start(bf16[128,2048]{1,0:T(8,128)(2,1)S(1)} %get-tuple-element.58), channel_id=1, source_target_pairs={{0,1},{1,0},{2,3},{3,2},{4,5},{5,4},{6,7},{7,6},{8,9},{9,8},{10,11... | collective-permute-start | bytes 1572872 | tf_op jit(solution)/shard_map/ppermute | solution.py:59
  8.3 21.4 %collective-permute-start.6 = (bf16[512,768]{1,0:T(8,128)(2,1)S(1)}, bf16[512,768]{1,0:T(8,128)(2,1)S(1)}, u32[]{:S(2)}, u32[]{:S(2)}) collective-permute-start(bf16[512,768]{1,0:T(8,128)(2,1)S(1)} %copy-done.1), channel_id=1, source_target_pairs={{0,15},{1,0},{2,1},{3,2},{4,3},{5,4},{6,5},{7,6},{8,7},{9,8},{10,9... | collective-permute-start | bytes 2359304 | tf_op jit(solution)/shard_map/ppermute | solution.py:50
  11.5 15.4 %collective-permute-start.2 = (bf16[128,1024]{1,0:T(8,128)(2,1)S(1)}, bf16[128,1024]{1,0:T(8,128)(2,1)S(1)}, u32[]{:S(2)}, u32[]{:S(2)}) collective-permute-start(bf16[128,1024]{1,0:T(8,128)(2,1)S(1)} %get-tuple-element.63), channel_id=1, source_target_pairs={{0,4},{1,5},{2,6},{3,7},{4,0},{5,1},{6,2},{7,3},{8,12},{9,13},{10,... | collective-permute-start | bytes 786440 | tf_op jit(solution)/shard_map/ppermute | solution.py:59
  16.2 19.3 %collective-permute-start.5 = (bf16[64,2048]{1,0:T(8,128)(2,1)S(1)}, bf16[64,2048]{1,0:T(8,128)(2,1)S(1)}, u32[]{:S(2)}, u32[]{:S(2)}) collective-permute-start(bf16[64,2048]{1,0:T(8,128)(2,1)S(1)} %get-tuple-element.66), channel_id=1, source_target_pairs={{0,2},{1,3},{2,0},{3,1},{4,6},{5,7},{6,4},{7,5},{8,10},{9,11},{10,... | collective-permute-start | bytes 786440 | tf_op jit(solution)/shard_map/ppermute | solution.py:59
  27.0 8.5 %collective-permute-start.3 = (bf16[128,512]{1,0:T(8,128)(2,1)S(1)}, bf16[128,512]{1,0:T(8,128)(2,1)S(1)}, u32[]{:S(2)}, u32[]{:S(2)}) collective-permute-start(bf16[128,512]{1,0:T(8,128)(2,1)S(1)} %get-tuple-element.64), channel_id=1, source_target_pairs={{0,8},{1,9},{2,10},{3,11},{4,12},{5,13},{6,14},{7,15},{8,0},{9,1},... | collective-permute-start | bytes 393224 | tf_op jit(solution)/shard_map/ppermute | solution.py:59
  35.5 7.7 %collective-permute-start.10 = (bf16[64,512]{1,0:T(8,128)(2,1)S(1)}, bf16[64,512]{1,0:T(8,128)(2,1)S(1)}, u32[]{:S(2)}, u32[]{:S(2)}) collective-permute-start(bf16[64,512]{1,0:T(8,128)(2,1)S(1)} %get-tuple-element.75), channel_id=1, source_target_pairs={{0,2},{1,3},{2,0},{3,1},{4,6},{5,7},{6,4},{7,5},{8,10},{9,11},{10,... | collective-permute-start | bytes 196616 | tf_op jit(solution)/shard_map/ppermute | solution.py:59
  35.7 7.5 %collective-permute-start.7 = (bf16[64,512]{1,0:T(8,128)(2,1)S(1)}, bf16[64,512]{1,0:T(8,128)(2,1)S(1)}, u32[]{:S(2)}, u32[]{:S(2)}) collective-permute-start(bf16[64,512]{1,0:T(8,128)(2,1)S(1)} %get-tuple-element.70), channel_id=1, source_target_pairs={{0,4},{1,5},{2,6},{3,7},{4,0},{5,1},{6,2},{7,3},{8,12},{9,13},{10,... | collective-permute-start | bytes 196616 | tf_op jit(solution)/shard_map/ppermute | solution.py:59
  36.0 7.5 %collective-permute-start.8 = (bf16[64,512]{1,0:T(8,128)(2,1)S(1)}, bf16[64,512]{1,0:T(8,128)(2,1)S(1)}, u32[]{:S(2)}, u32[]{:S(2)}) collective-permute-start(bf16[64,512]{1,0:T(8,128)(2,1)S(1)} %get-tuple-element.71), channel_id=1, source_target_pairs={{0,8},{1,9},{2,10},{3,11},{4,12},{5,13},{6,14},{7,15},{8,0},{9,1},... | collective-permute-start | bytes 196616 | tf_op jit(solution)/shard_map/ppermute | solution.py:59
  39.4 6.1 %collective-permute-start.9 = (bf16[64,512]{1,0:T(8,128)(2,1)S(1)}, bf16[64,512]{1,0:T(8,128)(2,1)S(1)}, u32[]{:S(2)}, u32[]{:S(2)}) collective-permute-start(bf16[64,512]{1,0:T(8,128)(2,1)S(1)} %get-tuple-element.72), channel_id=1, source_target_pairs={{0,12},{1,13},{2,14},{3,15},{4,8},{5,9},{6,10},{7,11},{8,4},{9,5},... | collective-permute-start | bytes 196616 | tf_op jit(solution)/shard_map/ppermute | solution.py:59
  40.2 25.0 %copy-start = (bf16[2048,768]{1,0:T(8,128)(2,1)S(1)}, bf16[2048,768]{1,0:T(8,128)(2,1)}, u32[]{:S(2)}) copy-start(bf16[2048,768]{1,0:T(8,128)(2,1)} %refs_3_.7) | copy-start | bytes 9437188
  45.5 6.5 %collective-permute-start.11 = (bf16[64,512]{1,0:T(8,128)(2,1)S(1)}, bf16[64,512]{1,0:T(8,128)(2,1)S(1)}, u32[]{:S(2)}, u32[]{:S(2)}) collective-permute-start(bf16[64,512]{1,0:T(8,128)(2,1)S(1)} %get-tuple-element.87.refs_0_), channel_id=1, source_target_pairs={{0,4},{1,5},{2,6},{3,7},{4,0},{5,1},{6,2},{7,3},{8,12},{9,13},{10,... | collective-permute-start | bytes 196616 | tf_op jit(solution)/shard_map/ppermute | solution.py:59
  45.5 6.4 %collective-permute-start.12 = (bf16[64,512]{1,0:T(8,128)(2,1)S(1)}, bf16[64,512]{1,0:T(8,128)(2,1)S(1)}, u32[]{:S(2)}, u32[]{:S(2)}) collective-permute-start(bf16[64,512]{1,0:T(8,128)(2,1)S(1)} %get-tuple-element.87.refs_0_), channel_id=1, source_target_pairs={{0,8},{1,9},{2,10},{3,11},{4,12},{5,13},{6,14},{7,15},{8,0},{9,1},... | collective-permute-start | bytes 196616 | tf_op jit(solution)/shard_map/ppermute | solution.py:59
  47.3 6.4 %collective-permute-start.13 = (bf16[64,512]{1,0:T(8,128)(2,1)S(1)}, bf16[64,512]{1,0:T(8,128)(2,1)S(1)}, u32[]{:S(2)}, u32[]{:S(2)}) collective-permute-start(bf16[64,512]{1,0:T(8,128)(2,1)S(1)} %get-tuple-element.87.refs_0_), channel_id=1, source_target_pairs={{0,12},{1,13},{2,14},{3,15},{4,8},{5,9},{6,10},{7,11},{8,4},{9,5},... | collective-permute-start | bytes 196616 | tf_op jit(solution)/shard_map/ppermute | solution.py:59
  49.9 4.3 %collective-permute-start.14 = (bf16[64,512]{1,0:T(8,128)(2,1)S(1)}, bf16[64,512]{1,0:T(8,128)(2,1)S(1)}, u32[]{:S(2)}, u32[]{:S(2)}) collective-permute-start(bf16[64,512]{1,0:T(8,128)(2,1)S(1)} %get-tuple-element.91.refs_0_), channel_id=1, source_target_pairs={{0,2},{1,3},{2,0},{3,1},{4,6},{5,7},{6,4},{7,5},{8,10},{9,11},{10,... | collective-permute-start | bytes 196616 | tf_op jit(solution)/shard_map/ppermute | solution.py:59
  54.2 6.6 %collective-permute-start.18 = (bf16[128,512]{1,0:T(8,128)(2,1)S(1)}, bf16[128,512]{1,0:T(8,128)(2,1)S(1)}, u32[]{:S(2)}, u32[]{:S(2)}) collective-permute-start(bf16[128,512]{1,0:T(8,128)(2,1)S(1)} %shard_map.114.refs_0_), channel_id=1, source_target_pairs={{0,4},{1,5},{2,6},{3,7},{4,0},{5,1},{6,2},{7,3},{8,12},{9,13},{10,... | collective-permute-start | bytes 393224 | tf_op jit(solution)/shard_map/ppermute | solution.py:59
  54.3 8.1 %collective-permute-start.19 = (bf16[128,512]{1,0:T(8,128)(2,1)S(1)}, bf16[128,512]{1,0:T(8,128)(2,1)S(1)}, u32[]{:S(2)}, u32[]{:S(2)}) collective-permute-start(bf16[128,512]{1,0:T(8,128)(2,1)S(1)} %shard_map.114.refs_0_), channel_id=1, source_target_pairs={{0,8},{1,9},{2,10},{3,11},{4,12},{5,13},{6,14},{7,15},{8,0},{9,1},... | collective-permute-start | bytes 393224 | tf_op jit(solution)/shard_map/ppermute | solution.py:59
  57.4 6.9 %collective-permute-start.20 = (bf16[128,512]{1,0:T(8,128)(2,1)S(1)}, bf16[128,512]{1,0:T(8,128)(2,1)S(1)}, u32[]{:S(2)}, u32[]{:S(2)}) collective-permute-start(bf16[128,512]{1,0:T(8,128)(2,1)S(1)} %shard_map.114.refs_0_), channel_id=1, source_target_pairs={{0,12},{1,13},{2,14},{3,15},{4,8},{5,9},{6,10},{7,11},{8,4},{9,5},... | collective-permute-start | bytes 393224 | tf_op jit(solution)/shard_map/ppermute | solution.py:59
  58.7 6.4 %collective-permute-start.16 = (bf16[64,2048]{1,0:T(8,128)(2,1)S(1)}, bf16[64,2048]{1,0:T(8,128)(2,1)S(1)}, u32[]{:S(2)}, u32[]{:S(2)}) collective-permute-start(bf16[64,2048]{1,0:T(8,128)(2,1)S(1)} %shard_map.113.refs_0_), channel_id=1, source_target_pairs={{0,2},{1,3},{2,0},{3,1},{4,6},{5,7},{6,4},{7,5},{8,10},{9,11},{10,... | collective-permute-start | bytes 786440 | tf_op jit(solution)/shard_map/ppermute | solution.py:59
  64.4 2.7 %collective-permute-start.21 = (bf16[128,2048]{1,0:T(8,128)(2,1)S(1)}, bf16[128,2048]{1,0:T(8,128)(2,1)S(1)}, u32[]{:S(2)}, u32[]{:S(2)}) collective-permute-start(bf16[128,2048]{1,0:T(8,128)(2,1)S(1)} %shard_map.115.refs_2_), channel_id=1, source_target_pairs={{0,1},{1,0},{2,3},{3,2},{4,5},{5,4},{6,7},{7,6},{8,9},{9,8},{10,11... | collective-permute-start | bytes 1572872 | tf_op jit(solution)/shard_map/ppermute | solution.py:59
  64.5 2.3 %collective-permute-start.15 = (bf16[64,2048]{1,0:T(8,128)(2,1)S(1)}, bf16[64,2048]{1,0:T(8,128)(2,1)S(1)}, u32[]{:S(2)}, u32[]{:S(2)}) collective-permute-start(bf16[64,2048]{1,0:T(8,128)(2,1)S(1)} %shard_map.113.refs_0_), channel_id=1, source_target_pairs={{0,1},{1,0},{2,3},{3,2},{4,5},{5,4},{6,7},{7,6},{8,9},{9,8},{10,11... | collective-permute-start | bytes 786440 | tf_op jit(solution)/shard_map/ppermute | solution.py:59
  65.1 2.0 %collective-permute-start.17 = (bf16[64,2048]{1,0:T(8,128)(2,1)S(1)}, bf16[64,2048]{1,0:T(8,128)(2,1)S(1)}, u32[]{:S(2)}, u32[]{:S(2)}) collective-permute-start(bf16[64,2048]{1,0:T(8,128)(2,1)S(1)} %collective-permute-done.16.refs_1_), channel_id=1, source_target_pairs={{0,1},{1,0},{2,3},{3,2},{4,5},{5,4},{6,7},{7,6},{8,9},{9,8},{10,11... | collective-permute-start | bytes 786440 | tf_op jit(solution)/shard_map/ppermute | solution.py:59
  68.6 1.3 %collective-permute-start.22 = (bf16[320,128]{1,0:T(8,128)(2,1)S(1)}, bf16[320,128]{1,0:T(8,128)(2,1)S(1)}, u32[]{:S(2)}, u32[]{:S(2)}) collective-permute-start(bf16[320,128]{1,0:T(8,128)(2,1)S(1)} %get-tuple-element.100), channel_id=1, source_target_pairs={{0,1},{1,0},{2,3},{3,2},{4,5},{5,4},{6,7},{7,6},{8,9},{9,8},{10,11... | collective-permute-start | bytes 245768 | tf_op jit(solution)/shard_map/ppermute | solution.py:59
  70.0 4.8 %collective-permute-start.23 = (bf16[320,128]{1,0:T(8,128)(2,1)S(1)}, bf16[320,128]{1,0:T(8,128)(2,1)S(1)}, u32[]{:S(2)}, u32[]{:S(2)}) collective-permute-start(bf16[320,128]{1,0:T(8,128)(2,1)S(1)} %get-tuple-element.102), channel_id=1, source_target_pairs={{0,2},{1,3},{2,0},{3,1},{4,6},{5,7},{6,4},{7,5},{8,10},{9,11},{10,... | collective-permute-start | bytes 245768 | tf_op jit(solution)/shard_map/ppermute | solution.py:59
  74.8 5.4 %collective-permute-start.24 = (bf16[320,128]{1,0:T(8,128)(2,1)S(1)}, bf16[320,128]{1,0:T(8,128)(2,1)S(1)}, u32[]{:S(2)}, u32[]{:S(2)}) collective-permute-start(bf16[320,128]{1,0:T(8,128)(2,1)S(1)} %get-tuple-element.104), channel_id=1, source_target_pairs={{0,4},{1,5},{2,6},{3,7},{4,0},{5,1},{6,2},{7,3},{8,12},{9,13},{10,... | collective-permute-start | bytes 245768 | tf_op jit(solution)/shard_map/ppermute | solution.py:59
  76.2 8.7 %collective-permute-start.25 = (bf16[320,128]{1,0:T(8,128)(2,1)S(1)}, bf16[320,128]{1,0:T(8,128)(2,1)S(1)}, u32[]{:S(2)}, u32[]{:S(2)}) collective-permute-start(bf16[320,128]{1,0:T(8,128)(2,1)S(1)} %get-tuple-element.104), channel_id=1, source_target_pairs={{0,8},{1,9},{2,10},{3,11},{4,12},{5,13},{6,14},{7,15},{8,0},{9,1},... | collective-permute-start | bytes 245768 | tf_op jit(solution)/shard_map/ppermute | solution.py:59
  77.9 7.0 %collective-permute-start.26 = (bf16[320,128]{1,0:T(8,128)(2,1)S(1)}, bf16[320,128]{1,0:T(8,128)(2,1)S(1)}, u32[]{:S(2)}, u32[]{:S(2)}) collective-permute-start(bf16[320,128]{1,0:T(8,128)(2,1)S(1)} %get-tuple-element.104), channel_id=1, source_target_pairs={{0,12},{1,13},{2,14},{3,15},{4,8},{5,9},{6,10},{7,11},{8,4},{9,5},... | collective-permute-start | bytes 245768 | tf_op jit(solution)/shard_map/ppermute | solution.py:59
  85.0 2.0 %collective-permute-start.27 = (bf16[320,128]{1,0:T(8,128)(2,1)S(1)}, bf16[320,128]{1,0:T(8,128)(2,1)S(1)}, u32[]{:S(2)}, u32[]{:S(2)}) collective-permute-start(bf16[320,128]{1,0:T(8,128)(2,1)S(1)} %shard_map.120.refs_0_), channel_id=1, source_target_pairs={{0,1},{1,0},{2,3},{3,2},{4,5},{5,4},{6,7},{7,6},{8,9},{9,8},{10,11... | collective-permute-start | bytes 245768 | tf_op jit(solution)/shard_map/ppermute | solution.py:59

commit v16 on v14

--- a/solution.py
+++ b/solution.py
@@ -115,26 +115,26 @@
 def first_body(core, block, tile, r_ref, p_ref, *refs):
     sent_x, sent_z, keep_x, keep_z, r_held, p_held, r_sem, p_sem = refs
     rows = r_held.shape[0] // 2
-    r_copy = pltpu.make_async_copy(r_ref, r_held, r_sem)
-    r_copy.start()
+    c = position(core)
+    r_copies = []
+    for k, side in enumerate((1 - c, c)):
+        there = pl.ds(pl.multiple_of(side * rows, rows), rows)
+        here = pl.ds(k * rows, rows)
+        r_copies.append(pltpu.make_async_copy(r_ref.at[there, :], r_held.at[here, :], r_sem.at[k]))
+        r_copies[-1].start()
     copies = []
     for t in range(p_held.shape[0] // tile):
         part = pl.ds(t * tile, tile)
         copies.append(pltpu.make_async_copy(p_ref.at[part, :], p_held.at[part, :], p_sem.at[t]))
         copies[-1].start()
-    c = position(core)
-    r_copy.wait()
+    for copy in r_copies:
+        copy.wait()
     for t, copy in enumerate(copies):
         copy.wait()
         cols = slice(t * tile, (t + 1) * tile)
-        for side, x_ref, z_ref in ((1 - c, sent_x, sent_z), (c, keep_x, keep_z)):
-            part = lax.dot_general(
-                r_held[pl.ds(pl.multiple_of(side * rows, rows), rows), :],
-                p_held[cols, :],
-                NT,
-                preferred_element_type=F32,
-            )
-            cut(part, block, x_ref, z_ref, cols)
+        part = lax.dot_general(r_held[...], p_held[cols, :], NT, preferred_element_type=F32)
+        cut(part[:rows, :], block, sent_x, sent_z, cols)
+        cut(part[rows:, :], block, keep_x, keep_z, cols)
 
 
 def first_sums(response, projectors, core, block, first):
@@ -152,7 +152,7 @@
         scratch_shapes=[
             pltpu.VMEM((bands, cells), response.dtype),
             pltpu.VMEM((count, cells), projectors.dtype),
-            pltpu.SemaphoreType.DMA,
+            pltpu.SemaphoreType.DMA((2,)),
             pltpu.SemaphoreType.DMA((count // tile,)),
         ],
         compiler_params=params(),

time: 86.9 us -> 87.5 us (level)
  transfers between devices with their start and end apart: 29 -> 29, of which waited for: 14 -> 12; matrix products, arithmetic and copies ran while one was open for 0% -> 0% of each run, Pallas kernels for 10% -> 10%
where the time goes in v16:
time: 87.5 us; the launch traced here: 87.3 us
  starting transfers between devices  37.8 us (43%)
  waiting for transfers between devices  35.5 us (41%)
  Pallas kernels  13 us (15%)
  between operations  0.95 us (1%)
    ppermute x27, waiting for transfers between devices, swapped(): return lax.ppermute(array, 'band', pairs)  34.7 us
    ppermute x27, starting transfers between devices, swapped(): return lax.ppermute(array, 'band', pairs)  34.2 us
    pallas_call x1, Pallas kernels, first_sums(): pl.pallas_call(functools.partial(first_body, core, block, tile), out_shap...  4.53 us
    pallas_call x14, Pallas kernels, local_call(): pl.pallas_call(body, out_shape=outs, in_specs=[whole() for _ in args], ou...  3.74 us
    ppermute x2, starting transfers between devices, neighbour(): lax.ppermute(array, 'band', [(i, (i + step) % count) for i in range(count)])  3.62 us
    pallas_call x1, Pallas kernels, project(): pl.pallas_call(functools.partial(project_body, core, blk), grid=(bands //...  2.43 us
    pallas_call x1, Pallas kernels, local_part(): pl.pallas_call(functools.partial(local_body, depth, (group_rows, blk)), g...  2.3 us
  transfers between devices with their start and end apart: 29, of which 12 were waited for; matrix products, arithmetic and copies ran while one was open for 0% of the time, Pallas kernels for 10%

profile of v16, /device:TPU:0, one launch (start us, length us, event | category | flops | bytes accessed | tf_op | source)
XLA Modules:
  0.0 87.3 jit_solution(9005643704547217731)
XLA Ops:
  0.6 0.5 collective-permute-start.4
  1.1 4.5 %shard_map.104 = (bf16[128,2048]{1,0:T(8,128)(2,1)S(1)}, bf16[128,2048]{1,0:T(8,128)(2,1)S(1)}, f32[128,2048]{1,0:T(8,128)S(1)}, f32[128,2048]{1,0:T(8,128)S(1)}) custom-call(bf16[512,768]{1,0:T(8,128)(2,1)} %refs_5_.1, bf16[2048,768]{1,0:T(8,128)(2,1)} %refs_3_.5), custom_call_target="tpu_custom_call" | custom-call | flops 1610612736 | bytes 6291456 | tf_op jit(solution)/shard_map/pallas_call | solution.py:147
  5.7 0.0 copy-start.7
  5.7 0.0 copy-start.8
  5.7 0.0 copy-start.1
  5.7 2.7 %collective-permute-start.1 = (bf16[128,2048]{1,0:T(8,128)(2,1)S(1)}, bf16[128,2048]{1,0:T(8,128)(2,1)S(1)}, u32[]{:S(2)}, u32[]{:S(2)}) collective-permute-start(bf16[128,2048]{1,0:T(8,128)(2,1)S(1)} %get-tuple-element.59), channel_id=1, source_target_pairs={{0,1},{1,0},{2,3},{3,2},{4,5},{5,4},{6,7},{7,6},{8,9},{9,8},{10,11... | collective-permute-start | bytes 1572872 | tf_op jit(solution)/shard_map/ppermute | solution.py:59
  8.4 0.1 collective-permute-start
  8.5 3.1 %collective-permute-start.7 = (bf16[512,768]{1,0:T(8,128)(2,1)S(1)}, bf16[512,768]{1,0:T(8,128)(2,1)S(1)}, u32[]{:S(2)}, u32[]{:S(2)}) collective-permute-start(bf16[512,768]{1,0:T(8,128)(2,1)S(1)} %copy-done.2), channel_id=1, source_target_pairs={{0,15},{1,0},{2,1},{3,2},{4,3},{5,4},{6,5},{7,6},{8,7},{9,8},{10,9... | collective-permute-start | bytes 2359304 | tf_op jit(solution)/shard_map/ppermute | solution.py:50
  11.6 0.0 copy-start.6
  11.6 0.1 shard_map.105
  11.8 0.0 collective-permute-done.refs_1_
  11.8 0.1 shard_map.106
  11.9 0.5 collective-permute-start.6
  12.4 1.6 %collective-permute-start.2 = (bf16[128,512]{1,0:T(8,128)(2,1)S(1)}, bf16[128,512]{1,0:T(8,128)(2,1)S(1)}, u32[]{:S(2)}, u32[]{:S(2)}) collective-permute-start(bf16[128,512]{1,0:T(8,128)(2,1)S(1)} %get-tuple-element.63), channel_id=1, source_target_pairs={{0,4},{1,5},{2,6},{3,7},{4,0},{5,1},{6,2},{7,3},{8,12},{9,13},{10,... | collective-permute-start | bytes 393224 | tf_op jit(solution)/shard_map/ppermute | solution.py:59
  14.0 1.4 %collective-permute-start.3 = (bf16[128,512]{1,0:T(8,128)(2,1)S(1)}, bf16[128,512]{1,0:T(8,128)(2,1)S(1)}, u32[]{:S(2)}, u32[]{:S(2)}) collective-permute-start(bf16[128,512]{1,0:T(8,128)(2,1)S(1)} %get-tuple-element.64), channel_id=1, source_target_pairs={{0,8},{1,9},{2,10},{3,11},{4,12},{5,13},{6,14},{7,15},{8,0},{9,1},... | collective-permute-start | bytes 393224 | tf_op jit(solution)/shard_map/ppermute | solution.py:59
  15.4 0.8 collective-permute-done.4.refs_1_
  16.2 2.2 %collective-permute-start.5 = (bf16[128,512]{1,0:T(8,128)(2,1)S(1)}, bf16[128,512]{1,0:T(8,128)(2,1)S(1)}, u32[]{:S(2)}, u32[]{:S(2)}) collective-permute-start(bf16[128,512]{1,0:T(8,128)(2,1)S(1)} %get-tuple-element.66), channel_id=1, source_target_pairs={{0,12},{1,13},{2,14},{3,15},{4,8},{5,9},{6,10},{7,11},{8,4},{9,5},... | collective-permute-start | bytes 393224 | tf_op jit(solution)/shard_map/ppermute | solution.py:59
  18.4 8.8 %collective-permute-done.2.refs_1_ = bf16[128,512]{1,0:T(8,128)(2,1)S(1)} collective-permute-done((bf16[128,512]{1,0:T(8,128)(2,1)S(1)}, bf16[128,512]{1,0:T(8,128)(2,1)S(1)}, u32[]{:S(2)}, u32[]{:S(2)}) %collective-permute-start.2) | collective-permute-done | bytes 131104 | tf_op jit(solution)/shard_map/ppermute | solution.py:59
  27.1 5.2 %collective-permute-done.3.refs_2_ = bf16[128,512]{1,0:T(8,128)(2,1)S(1)} collective-permute-done((bf16[128,512]{1,0:T(8,128)(2,1)S(1)}, bf16[128,512]{1,0:T(8,128)(2,1)S(1)}, u32[]{:S(2)}, u32[]{:S(2)}) %collective-permute-start.3) | collective-permute-done | bytes 131104 | tf_op jit(solution)/shard_map/ppermute | solution.py:59
  32.4 0.0 collective-permute-done.6.refs_1_
  32.4 0.0 collective-permute-done.7.refs_2_
  32.4 0.0 collective-permute-done.5.refs_3_
  32.4 0.1 shard_map.108
  32.5 0.1 collective-permute-start.11
  32.6 0.1 shard_map.107
  32.6 2.7 %collective-permute-start.10 = (bf16[64,512]{1,0:T(8,128)(2,1)S(1)}, bf16[64,512]{1,0:T(8,128)(2,1)S(1)}, u32[]{:S(2)}, u32[]{:S(2)}) collective-permute-start(bf16[64,512]{1,0:T(8,128)(2,1)S(1)} %get-tuple-element.73), channel_id=1, source_target_pairs={{0,12},{1,13},{2,14},{3,15},{4,8},{5,9},{6,10},{7,11},{8,4},{9,5},... | collective-permute-start | bytes 196616 | tf_op jit(solution)/shard_map/ppermute | solution.py:59
  35.3 2.5 %collective-permute-start.8 = (bf16[64,512]{1,0:T(8,128)(2,1)S(1)}, bf16[64,512]{1,0:T(8,128)(2,1)S(1)}, u32[]{:S(2)}, u32[]{:S(2)}) collective-permute-start(bf16[64,512]{1,0:T(8,128)(2,1)S(1)} %get-tuple-element.71), channel_id=1, source_target_pairs={{0,4},{1,5},{2,6},{3,7},{4,0},{5,1},{6,2},{7,3},{8,12},{9,13},{10,... | collective-permute-start | bytes 196616 | tf_op jit(solution)/shard_map/ppermute | solution.py:59
  37.9 0.1 shard_map.110.refs_5_.refs_4_
  38.0 0.0 copy-start
  38.1 2.3 %shard_map.109 = (f32[512,768]{1,0:T(8,128)S(1)}, bf16[512,256]{1,0:T(8,128)(2,1)S(1)}) custom-call(bf16[512,768]{1,0:T(8,128)(2,1)S(1)} %copy-done.2, bf16[512,768]{1,0:T(8,128)(2,1)S(1)} %collective-permute-done.4.refs_1_, bf16[512,768]{1,0:T(8,128)(2,1)S(1)} %collective-permute-done.7.refs_2_, bf16[512,768]{1,0:T(8,128)(2,1)S(1)} %copy-done.1, ...), custom_call_target="tpu_custom_call" | custom-call | flops 235929600 | bytes 4980736 | tf_op jit(solution)/shard_map/pallas_call | solution.py:298
  40.4 0.0 collective-permute-done.11.refs_5_
  40.4 0.0 collective-permute-done.10.refs_3_
  40.4 2.8 %collective-permute-done.9.refs_2_ = bf16[64,512]{1,0:T(8,128)(2,1)S(1)} collective-permute-done((bf16[64,512]{1,0:T(8,128)(2,1)S(1)}, bf16[64,512]{1,0:T(8,128)(2,1)S(1)}, u32[]{:S(2)}, u32[]{:S(2)}) %collective-permute-start.9) | collective-permute-done | bytes 65568 | tf_op jit(solution)/shard_map/ppermute | solution.py:59
  43.2 0.1 shard_map.111
  43.2 0.1 collective-permute-start.12
  43.3 2.3 %collective-permute-start.13 = (bf16[64,512]{1,0:T(8,128)(2,1)S(1)}, bf16[64,512]{1,0:T(8,128)(2,1)S(1)}, u32[]{:S(2)}, u32[]{:S(2)}) collective-permute-start(bf16[64,512]{1,0:T(8,128)(2,1)S(1)} %get-tuple-element.89.refs_0_), channel_id=1, source_target_pairs={{0,8},{1,9},{2,10},{3,11},{4,12},{5,13},{6,14},{7,15},{8,0},{9,1},... | collective-permute-start | bytes 196616 | tf_op jit(solution)/shard_map/ppermute | solution.py:59
  45.6 2.1 %collective-permute-start.14 = (bf16[64,512]{1,0:T(8,128)(2,1)S(1)}, bf16[64,512]{1,0:T(8,128)(2,1)S(1)}, u32[]{:S(2)}, u32[]{:S(2)}) collective-permute-start(bf16[64,512]{1,0:T(8,128)(2,1)S(1)} %get-tuple-element.89.refs_0_), channel_id=1, source_target_pairs={{0,12},{1,13},{2,14},{3,15},{4,8},{5,9},{6,10},{7,11},{8,4},{9,5},... | collective-permute-start | bytes 196616 | tf_op jit(solution)/shard_map/ppermute | solution.py:59
  47.7 2.0 %collective-permute-start.15 = (bf16[64,512]{1,0:T(8,128)(2,1)S(1)}, bf16[64,512]{1,0:T(8,128)(2,1)S(1)}, u32[]{:S(2)}, u32[]{:S(2)}) collective-permute-start(bf16[64,512]{1,0:T(8,128)(2,1)S(1)} %get-tuple-element.93.refs_0_), channel_id=1, source_target_pairs={{0,2},{1,3},{2,0},{3,1},{4,6},{5,7},{6,4},{7,5},{8,10},{9,11},{10,... | collective-permute-start | bytes 196616 | tf_op jit(solution)/shard_map/ppermute | solution.py:59
  49.7 0.0 collective-permute-done.12.refs_1_
  49.7 0.0 collective-permute-done.13.refs_2_
  49.7 2.8 %collective-permute-done.14.refs_3_ = bf16[64,512]{1,0:T(8,128)(2,1)S(1)} collective-permute-done((bf16[64,512]{1,0:T(8,128)(2,1)S(1)}, bf16[64,512]{1,0:T(8,128)(2,1)S(1)}, u32[]{:S(2)}, u32[]{:S(2)}) %collective-permute-start.14) | collective-permute-done | bytes 65568 | tf_op jit(solution)/shard_map/ppermute | solution.py:59
  52.5 0.1 collective-permute-start.19
  52.6 2.4 %collective-permute-start.20 = (bf16[128,512]{1,0:T(8,128)(2,1)S(1)}, bf16[128,512]{1,0:T(8,128)(2,1)S(1)}, u32[]{:S(2)}, u32[]{:S(2)}) collective-permute-start(bf16[128,512]{1,0:T(8,128)(2,1)S(1)} %shard_map.113.refs_0_), channel_id=1, source_target_pairs={{0,8},{1,9},{2,10},{3,11},{4,12},{5,13},{6,14},{7,15},{8,0},{9,1},... | collective-permute-start | bytes 393224 | tf_op jit(solution)/shard_map/ppermute | solution.py:59
  55.1 1.9 %collective-permute-start.21 = (bf16[128,512]{1,0:T(8,128)(2,1)S(1)}, bf16[128,512]{1,0:T(8,128)(2,1)S(1)}, u32[]{:S(2)}, u32[]{:S(2)}) collective-permute-start(bf16[128,512]{1,0:T(8,128)(2,1)S(1)} %shard_map.113.refs_0_), channel_id=1, source_target_pairs={{0,12},{1,13},{2,14},{3,15},{4,8},{5,9},{6,10},{7,11},{8,4},{9,5},... | collective-permute-start | bytes 393224 | tf_op jit(solution)/shard_map/ppermute | solution.py:59
  57.0 2.0 %collective-permute-start.17 = (bf16[64,2048]{1,0:T(8,128)(2,1)S(1)}, bf16[64,2048]{1,0:T(8,128)(2,1)S(1)}, u32[]{:S(2)}, u32[]{:S(2)}) collective-permute-start(bf16[64,2048]{1,0:T(8,128)(2,1)S(1)} %shard_map.112.refs_0_), channel_id=1, source_target_pairs={{0,2},{1,3},{2,0},{3,1},{4,6},{5,7},{6,4},{7,5},{8,10},{9,11},{10,... | collective-permute-start | bytes 786440 | tf_op jit(solution)/shard_map/ppermute | solution.py:59
  59.0 3.1 %collective-permute-done.20.refs_2_ = bf16[128,512]{1,0:T(8,128)(2,1)S(1)} collective-permute-done((bf16[128,512]{1,0:T(8,128)(2,1)S(1)}, bf16[128,512]{1,0:T(8,128)(2,1)S(1)}, u32[]{:S(2)}, u32[]{:S(2)}) %collective-permute-start.20) | collective-permute-done | bytes 131104 | tf_op jit(solution)/shard_map/ppermute | solution.py:59
  62.1 0.1 shard_map.114.refs_2_
  62.2 0.1 collective-permute-start.22
  62.3 0.5 collective-permute-start.16
  62.8 0.7 collective-permute-done.17.refs_1_
  63.5 1.5 %shard_map.115 = (f32[256,768]{1,0:T(8,128)S(1)}, f32[320,128]{1,0:T(8,128)S(1)}) custom-call(bf16[64,2048]{1,0:T(8,128)(2,1)S(1)} %shard_map.112.refs_0_, bf16[64,2048]{1,0:T(8,128)(2,1)S(1)} %collective-permute-done.17.refs_1_, bf16[128,2048]{1,0:T(8,128)(2,1)S(1)} %shard_map.114.refs_2_, bf16[2048,768]{1,0:T(8,128)(2,1)S(1)} %copy-done, ...), custom_call_target="tpu_custom_call" | custom-call | flops 905969664 | bytes 7700480 | tf_op jit(solution)/shard_map/pallas_call | solution.py:91
  65.0 1.5 %shard_map.116 = (f32[256,768]{1,0:T(8,128)S(1)}, bf16[320,128]{1,0:T(8,128)(2,1)S(1)}) custom-call(bf16[64,2048]{1,0:T(8,128)(2,1)S(1)} %collective-permute-done.16.refs_0_, bf16[64,2048]{1,0:T(8,128)(2,1)S(1)} %collective-permute-done.18.refs_1_, bf16[128,2048]{1,0:T(8,128)(2,1)S(1)} %collective-permute-done.22.refs_2_, bf16[2048,768]{1,0:T(8,128)(2,1)S(1)} %copy-done, ...), custom_call_target="tpu_custom_call" | custom-call | flops 905969664 | bytes 7618560 | tf_op jit(solution)/shard_map/pallas_call | solution.py:91
  66.5 0.6 collective-permute-start.23
  67.1 0.9 %collective-permute-done.23.refs_0_ = bf16[320,128]{1,0:T(8,128)(2,1)S(1)} collective-permute-done((bf16[320,128]{1,0:T(8,128)(2,1)S(1)}, bf16[320,128]{1,0:T(8,128)(2,1)S(1)}, u32[]{:S(2)}, u32[]{:S(2)}) %collective-permute-start.23) | collective-permute-done | bytes 81952 | tf_op jit(solution)/shard_map/ppermute | solution.py:59
  68.0 2.0 %collective-permute-start.24 = (bf16[320,128]{1,0:T(8,128)(2,1)S(1)}, bf16[320,128]{1,0:T(8,128)(2,1)S(1)}, u32[]{:S(2)}, u32[]{:S(2)}) collective-permute-start(bf16[320,128]{1,0:T(8,128)(2,1)S(1)} %get-tuple-element.104), channel_id=1, source_target_pairs={{0,2},{1,3},{2,0},{3,1},{4,6},{5,7},{6,4},{7,5},{8,10},{9,11},{10,... | collective-permute-start | bytes 245768 | tf_op jit(solution)/shard_map/ppermute | solution.py:59
  70.0 3.0 %collective-permute-done.24.refs_0_ = bf16[320,128]{1,0:T(8,128)(2,1)S(1)} collective-permute-done((bf16[320,128]{1,0:T(8,128)(2,1)S(1)}, bf16[320,128]{1,0:T(8,128)(2,1)S(1)}, u32[]{:S(2)}, u32[]{:S(2)}) %collective-permute-start.24) | collective-permute-done | bytes 81952 | tf_op jit(solution)/shard_map/ppermute | solution.py:59
  73.0 1.6 %collective-permute-start.25 = (bf16[320,128]{1,0:T(8,128)(2,1)S(1)}, bf16[320,128]{1,0:T(8,128)(2,1)S(1)}, u32[]{:S(2)}, u32[]{:S(2)}) collective-permute-start(bf16[320,128]{1,0:T(8,128)(2,1)S(1)} %get-tuple-element.106), channel_id=1, source_target_pairs={{0,4},{1,5},{2,6},{3,7},{4,0},{5,1},{6,2},{7,3},{8,12},{9,13},{10,... | collective-permute-start | bytes 245768 | tf_op jit(solution)/shard_map/ppermute | solution.py:59
  74.6 1.0 %collective-permute-start.26 = (bf16[320,128]{1,0:T(8,128)(2,1)S(1)}, bf16[320,128]{1,0:T(8,128)(2,1)S(1)}, u32[]{:S(2)}, u32[]{:S(2)}) collective-permute-start(bf16[320,128]{1,0:T(8,128)(2,1)S(1)} %get-tuple-element.106), channel_id=1, source_target_pairs={{0,8},{1,9},{2,10},{3,11},{4,12},{5,13},{6,14},{7,15},{8,0},{9,1},... | collective-permute-start | bytes 245768 | tf_op jit(solution)/shard_map/ppermute | solution.py:59
  75.6 1.8 %collective-permute-start.27 = (bf16[320,128]{1,0:T(8,128)(2,1)S(1)}, bf16[320,128]{1,0:T(8,128)(2,1)S(1)}, u32[]{:S(2)}, u32[]{:S(2)}) collective-permute-start(bf16[320,128]{1,0:T(8,128)(2,1)S(1)} %get-tuple-element.106), channel_id=1, source_target_pairs={{0,12},{1,13},{2,14},{3,15},{4,8},{5,9},{6,10},{7,11},{8,4},{9,5},... | collective-permute-start | bytes 245768 | tf_op jit(solution)/shard_map/ppermute | solution.py:59
  77.4 0.3 collective-permute-done.25.refs_0_
  77.7 5.8 %collective-permute-done.26.refs_1_ = bf16[320,128]{1,0:T(8,128)(2,1)S(1)} collective-permute-done((bf16[320,128]{1,0:T(8,128)(2,1)S(1)}, bf16[320,128]{1,0:T(8,128)(2,1)S(1)}, u32[]{:S(2)}, u32[]{:S(2)}) %collective-permute-start.26) | collective-permute-done | bytes 81952 | tf_op jit(solution)/shard_map/ppermute | solution.py:59
  83.6 0.1 collective-permute-start.28
  83.6 1.3 %collective-permute-done.28.refs_1_ = bf16[320,128]{1,0:T(8,128)(2,1)S(1)} collective-permute-done((bf16[320,128]{1,0:T(8,128)(2,1)S(1)}, bf16[320,128]{1,0:T(8,128)(2,1)S(1)}, u32[]{:S(2)}, u32[]{:S(2)}) %collective-permute-start.28) | collective-permute-done | bytes 81952 | tf_op jit(solution)/shard_map/ppermute | solution.py:59
  84.9 2.4 %shard_map.120 = (bf16[512,768]{1,0:T(8,128)(2,1)}, bf16[512,768]{1,0:T(8,128)(2,1)}) custom-call(bf16[320,128]{1,0:T(8,128)(2,1)S(1)} %shard_map.119.refs_0_, bf16[320,128]{1,0:T(8,128)(2,1)S(1)} %collective-permute-done.28.refs_1_, f32[256,768]{1,0:T(8,128)S(1)} %get-tuple-element.107.refs_2_, f32[256,768]{1,0:T(8,128)S(1)} %get-tuple-element.108.refs_3_, ...), custom_call_target="tpu_custom_call" | custom-call | flops 201326592 | bytes 4915200 | tf_op jit(solution)/shard_map/pallas_call | solution.py:468
  (31 shorter events, 0.2 us)
Async XLA Ops:
  0.6 7.8 %copy-start.2 = (bf16[512,768]{1,0:T(8,128)(2,1)S(1)}, bf16[512,768]{1,0:T(8,128)(2,1)}, u32[]{:S(2)}) copy-start(bf16[512,768]{1,0:T(8,128)(2,1)} %refs_5_.1) | copy-start | bytes 2359300
  0.6 15.6 %collective-permute-start.4 = (bf16[512,768]{1,0:T(8,128)(2,1)}, bf16[512,768]{1,0:T(8,128)(2,1)S(1)}, u32[]{:S(2)}, u32[]{:S(2)}) collective-permute-start(bf16[512,768]{1,0:T(8,128)(2,1)} %refs_5_.1), channel_id=1, source_target_pairs={{0,1},{1,2},{2,3},{3,4},{4,5},{5,6},{6,7},{7,8},{8,9},{9,10},{10,1... | collective-permute-start | bytes 2359304 | tf_op jit(solution)/shard_map/ppermute | solution.py:50
  5.7 32.2 %copy-start.7 = (f32[768]{0:T(1024)S(1)}, f32[768]{0:T(1024)}, u32[]{:S(2)}) copy-start(f32[768]{0:T(1024)} %param.12) | copy-start | bytes 9220
  5.7 32.2 %copy-start.8 = (f32[768]{0:T(1024)S(1)}, f32[768]{0:T(1024)}, u32[]{:S(2)}) copy-start(f32[768]{0:T(1024)} %param.13) | copy-start | bytes 9220
  5.7 32.2 %copy-start.1 = (bf16[512,768]{1,0:T(8,128)(2,1)S(1)}, bf16[512,768]{1,0:T(8,128)(2,1)}, u32[]{:S(2)}) copy-start(bf16[512,768]{1,0:T(8,128)(2,1)} %o_ref.1) | copy-start | bytes 2359300
  5.7 5.9 %collective-permute-start.1 = (bf16[128,2048]{1,0:T(8,128)(2,1)S(1)}, bf16[128,2048]{1,0:T(8,128)(2,1)S(1)}, u32[]{:S(2)}, u32[]{:S(2)}) collective-permute-start(bf16[128,2048]{1,0:T(8,128)(2,1)S(1)} %get-tuple-element.59), channel_id=1, source_target_pairs={{0,1},{1,0},{2,3},{3,2},{4,5},{5,4},{6,7},{7,6},{8,9},{9,8},{10,11... | collective-permute-start | bytes 1572872 | tf_op jit(solution)/shard_map/ppermute | solution.py:59
  8.4 3.4 %collective-permute-start = (bf16[128,2048]{1,0:T(8,128)(2,1)S(1)}, bf16[128,2048]{1,0:T(8,128)(2,1)S(1)}, u32[]{:S(2)}, u32[]{:S(2)}) collective-permute-start(bf16[128,2048]{1,0:T(8,128)(2,1)S(1)} %get-tuple-element.57), channel_id=1, source_target_pairs={{0,1},{1,0},{2,3},{3,2},{4,5},{5,4},{6,7},{7,6},{8,9},{9,8},{10,11... | collective-permute-start | bytes 1572872 | tf_op jit(solution)/shard_map/ppermute | solution.py:59
  8.5 23.9 %collective-permute-start.7 = (bf16[512,768]{1,0:T(8,128)(2,1)S(1)}, bf16[512,768]{1,0:T(8,128)(2,1)S(1)}, u32[]{:S(2)}, u32[]{:S(2)}) collective-permute-start(bf16[512,768]{1,0:T(8,128)(2,1)S(1)} %copy-done.2), channel_id=1, source_target_pairs={{0,15},{1,0},{2,1},{3,2},{4,3},{5,4},{6,5},{7,6},{8,7},{9,8},{10,9... | collective-permute-start | bytes 2359304 | tf_op jit(solution)/shard_map/ppermute | solution.py:50
  11.6 26.4 %copy-start.3 = (bf16[2,128,128]{2,1,0:T(8,128)(2,1)S(1)}, bf16[2,128,128]{2,1,0:T(8,128)(2,1)}, u32[]{:S(2)}) copy-start(bf16[2,128,128]{2,1,0:T(8,128)(2,1)} %constant.2.clone.refs_4_) | copy-start | bytes 196612
  11.6 26.4 %copy-start.4 = (f32[512]{0:T(512)S(1)}, f32[512]{0:T(512)}, u32[]{:S(2)}) copy-start(f32[512]{0:T(512)} %param.14) | copy-start | bytes 6148
  11.6 26.4 %copy-start.5 = (s32[512]{0:T(512)S(1)}, s32[512]{0:T(512)}, u32[]{:S(2)}) copy-start(s32[512]{0:T(512)} %param.15) | copy-start | bytes 6148
  11.6 26.4 %copy-start.6 = (s32[512]{0:T(512)S(1)}, s32[512]{0:T(512)}, u32[]{:S(2)}) copy-start(s32[512]{0:T(512)} %param.16) | copy-start | bytes 6148
  11.9 20.5 %collective-permute-start.6 = (bf16[64,2048]{1,0:T(8,128)(2,1)S(1)}, bf16[64,2048]{1,0:T(8,128)(2,1)S(1)}, u32[]{:S(2)}, u32[]{:S(2)}) collective-permute-start(bf16[64,2048]{1,0:T(8,128)(2,1)S(1)} %get-tuple-element.67), channel_id=1, source_target_pairs={{0,2},{1,3},{2,0},{3,1},{4,6},{5,7},{6,4},{7,5},{8,10},{9,11},{10,... | collective-permute-start | bytes 786440 | tf_op jit(solution)/shard_map/ppermute | solution.py:59
  12.4 14.7 %collective-permute-start.2 = (bf16[128,512]{1,0:T(8,128)(2,1)S(1)}, bf16[128,512]{1,0:T(8,128)(2,1)S(1)}, u32[]{:S(2)}, u32[]{:S(2)}) collective-permute-start(bf16[128,512]{1,0:T(8,128)(2,1)S(1)} %get-tuple-element.63), channel_id=1, source_target_pairs={{0,4},{1,5},{2,6},{3,7},{4,0},{5,1},{6,2},{7,3},{8,12},{9,13},{10,... | collective-permute-start | bytes 393224 | tf_op jit(solution)/shard_map/ppermute | solution.py:59
  14.0 18.4 %collective-permute-start.3 = (bf16[128,512]{1,0:T(8,128)(2,1)S(1)}, bf16[128,512]{1,0:T(8,128)(2,1)S(1)}, u32[]{:S(2)}, u32[]{:S(2)}) collective-permute-start(bf16[128,512]{1,0:T(8,128)(2,1)S(1)} %get-tuple-element.64), channel_id=1, source_target_pairs={{0,8},{1,9},{2,10},{3,11},{4,12},{5,13},{6,14},{7,15},{8,0},{9,1},... | collective-permute-start | bytes 393224 | tf_op jit(solution)/shard_map/ppermute | solution.py:59
  16.2 16.2 %collective-permute-start.5 = (bf16[128,512]{1,0:T(8,128)(2,1)S(1)}, bf16[128,512]{1,0:T(8,128)(2,1)S(1)}, u32[]{:S(2)}, u32[]{:S(2)}) collective-permute-start(bf16[128,512]{1,0:T(8,128)(2,1)S(1)} %get-tuple-element.66), channel_id=1, source_target_pairs={{0,12},{1,13},{2,14},{3,15},{4,8},{5,9},{6,10},{7,11},{8,4},{9,5},... | collective-permute-start | bytes 393224 | tf_op jit(solution)/shard_map/ppermute | solution.py:59
  32.5 7.9 %collective-permute-start.11 = (bf16[64,512]{1,0:T(8,128)(2,1)S(1)}, bf16[64,512]{1,0:T(8,128)(2,1)S(1)}, u32[]{:S(2)}, u32[]{:S(2)}) collective-permute-start(bf16[64,512]{1,0:T(8,128)(2,1)S(1)} %get-tuple-element.78), channel_id=1, source_target_pairs={{0,2},{1,3},{2,0},{3,1},{4,6},{5,7},{6,4},{7,5},{8,10},{9,11},{10,... | collective-permute-start | bytes 196616 | tf_op jit(solution)/shard_map/ppermute | solution.py:59
  32.6 7.7 %collective-permute-start.10 = (bf16[64,512]{1,0:T(8,128)(2,1)S(1)}, bf16[64,512]{1,0:T(8,128)(2,1)S(1)}, u32[]{:S(2)}, u32[]{:S(2)}) collective-permute-start(bf16[64,512]{1,0:T(8,128)(2,1)S(1)} %get-tuple-element.73), channel_id=1, source_target_pairs={{0,12},{1,13},{2,14},{3,15},{4,8},{5,9},{6,10},{7,11},{8,4},{9,5},... | collective-permute-start | bytes 196616 | tf_op jit(solution)/shard_map/ppermute | solution.py:59
  35.3 5.0 %collective-permute-start.8 = (bf16[64,512]{1,0:T(8,128)(2,1)S(1)}, bf16[64,512]{1,0:T(8,128)(2,1)S(1)}, u32[]{:S(2)}, u32[]{:S(2)}) collective-permute-start(bf16[64,512]{1,0:T(8,128)(2,1)S(1)} %get-tuple-element.71), channel_id=1, source_target_pairs={{0,4},{1,5},{2,6},{3,7},{4,0},{5,1},{6,2},{7,3},{8,12},{9,13},{10,... | collective-permute-start | bytes 196616 | tf_op jit(solution)/shard_map/ppermute | solution.py:59
  37.9 5.3 %collective-permute-start.9 = (bf16[64,512]{1,0:T(8,128)(2,1)S(1)}, bf16[64,512]{1,0:T(8,128)(2,1)S(1)}, u32[]{:S(2)}, u32[]{:S(2)}) collective-permute-start(bf16[64,512]{1,0:T(8,128)(2,1)S(1)} %get-tuple-element.72), channel_id=1, source_target_pairs={{0,8},{1,9},{2,10},{3,11},{4,12},{5,13},{6,14},{7,15},{8,0},{9,1},... | collective-permute-start | bytes 196616 | tf_op jit(solution)/shard_map/ppermute | solution.py:59
  38.0 25.5 %copy-start = (bf16[2048,768]{1,0:T(8,128)(2,1)S(1)}, bf16[2048,768]{1,0:T(8,128)(2,1)}, u32[]{:S(2)}) copy-start(bf16[2048,768]{1,0:T(8,128)(2,1)} %refs_3_.5) | copy-start | bytes 9437188
  43.2 6.5 %collective-permute-start.12 = (bf16[64,512]{1,0:T(8,128)(2,1)S(1)}, bf16[64,512]{1,0:T(8,128)(2,1)S(1)}, u32[]{:S(2)}, u32[]{:S(2)}) collective-permute-start(bf16[64,512]{1,0:T(8,128)(2,1)S(1)} %get-tuple-element.89.refs_0_), channel_id=1, source_target_pairs={{0,4},{1,5},{2,6},{3,7},{4,0},{5,1},{6,2},{7,3},{8,12},{9,13},{10,... | collective-permute-start | bytes 196616 | tf_op jit(solution)/shard_map/ppermute | solution.py:59
  43.3 6.4 %collective-permute-start.13 = (bf16[64,512]{1,0:T(8,128)(2,1)S(1)}, bf16[64,512]{1,0:T(8,128)(2,1)S(1)}, u32[]{:S(2)}, u32[]{:S(2)}) collective-permute-start(bf16[64,512]{1,0:T(8,128)(2,1)S(1)} %get-tuple-element.89.refs_0_), channel_id=1, source_target_pairs={{0,8},{1,9},{2,10},{3,11},{4,12},{5,13},{6,14},{7,15},{8,0},{9,1},... | collective-permute-start | bytes 196616 | tf_op jit(solution)/shard_map/ppermute | solution.py:59
  45.6 6.9 %collective-permute-start.14 = (bf16[64,512]{1,0:T(8,128)(2,1)S(1)}, bf16[64,512]{1,0:T(8,128)(2,1)S(1)}, u32[]{:S(2)}, u32[]{:S(2)}) collective-permute-start(bf16[64,512]{1,0:T(8,128)(2,1)S(1)} %get-tuple-element.89.refs_0_), channel_id=1, source_target_pairs={{0,12},{1,13},{2,14},{3,15},{4,8},{5,9},{6,10},{7,11},{8,4},{9,5},... | collective-permute-start | bytes 196616 | tf_op jit(solution)/shard_map/ppermute | solution.py:59
  47.7 4.8 %collective-permute-start.15 = (bf16[64,512]{1,0:T(8,128)(2,1)S(1)}, bf16[64,512]{1,0:T(8,128)(2,1)S(1)}, u32[]{:S(2)}, u32[]{:S(2)}) collective-permute-start(bf16[64,512]{1,0:T(8,128)(2,1)S(1)} %get-tuple-element.93.refs_0_), channel_id=1, source_target_pairs={{0,2},{1,3},{2,0},{3,1},{4,6},{5,7},{6,4},{7,5},{8,10},{9,11},{10,... | collective-permute-start | bytes 196616 | tf_op jit(solution)/shard_map/ppermute | solution.py:59
  52.5 6.4 %collective-permute-start.19 = (bf16[128,512]{1,0:T(8,128)(2,1)S(1)}, bf16[128,512]{1,0:T(8,128)(2,1)S(1)}, u32[]{:S(2)}, u32[]{:S(2)}) collective-permute-start(bf16[128,512]{1,0:T(8,128)(2,1)S(1)} %shard_map.113.refs_0_), channel_id=1, source_target_pairs={{0,4},{1,5},{2,6},{3,7},{4,0},{5,1},{6,2},{7,3},{8,12},{9,13},{10,... | collective-permute-start | bytes 393224 | tf_op jit(solution)/shard_map/ppermute | solution.py:59
  52.6 9.5 %collective-permute-start.20 = (bf16[128,512]{1,0:T(8,128)(2,1)S(1)}, bf16[128,512]{1,0:T(8,128)(2,1)S(1)}, u32[]{:S(2)}, u32[]{:S(2)}) collective-permute-start(bf16[128,512]{1,0:T(8,128)(2,1)S(1)} %shard_map.113.refs_0_), channel_id=1, source_target_pairs={{0,8},{1,9},{2,10},{3,11},{4,12},{5,13},{6,14},{7,15},{8,0},{9,1},... | collective-permute-start | bytes 393224 | tf_op jit(solution)/shard_map/ppermute | solution.py:59
  55.1 7.1 %collective-permute-start.21 = (bf16[128,512]{1,0:T(8,128)(2,1)S(1)}, bf16[128,512]{1,0:T(8,128)(2,1)S(1)}, u32[]{:S(2)}, u32[]{:S(2)}) collective-permute-start(bf16[128,512]{1,0:T(8,128)(2,1)S(1)} %shard_map.113.refs_0_), channel_id=1, source_target_pairs={{0,12},{1,13},{2,14},{3,15},{4,8},{5,9},{6,10},{7,11},{8,4},{9,5},... | collective-permute-start | bytes 393224 | tf_op jit(solution)/shard_map/ppermute | solution.py:59
  57.0 6.4 %collective-permute-start.17 = (bf16[64,2048]{1,0:T(8,128)(2,1)S(1)}, bf16[64,2048]{1,0:T(8,128)(2,1)S(1)}, u32[]{:S(2)}, u32[]{:S(2)}) collective-permute-start(bf16[64,2048]{1,0:T(8,128)(2,1)S(1)} %shard_map.112.refs_0_), channel_id=1, source_target_pairs={{0,2},{1,3},{2,0},{3,1},{4,6},{5,7},{6,4},{7,5},{8,10},{9,11},{10,... | collective-permute-start | bytes 786440 | tf_op jit(solution)/shard_map/ppermute | solution.py:59
  62.2 2.8 %collective-permute-start.22 = (bf16[128,2048]{1,0:T(8,128)(2,1)S(1)}, bf16[128,2048]{1,0:T(8,128)(2,1)S(1)}, u32[]{:S(2)}, u32[]{:S(2)}) collective-permute-start(bf16[128,2048]{1,0:T(8,128)(2,1)S(1)} %shard_map.114.refs_2_), channel_id=1, source_target_pairs={{0,1},{1,0},{2,3},{3,2},{4,5},{5,4},{6,7},{7,6},{8,9},{9,8},{10,11... | collective-permute-start | bytes 1572872 | tf_op jit(solution)/shard_map/ppermute | solution.py:59
  62.3 2.7 %collective-permute-start.16 = (bf16[64,2048]{1,0:T(8,128)(2,1)S(1)}, bf16[64,2048]{1,0:T(8,128)(2,1)S(1)}, u32[]{:S(2)}, u32[]{:S(2)}) collective-permute-start(bf16[64,2048]{1,0:T(8,128)(2,1)S(1)} %shard_map.112.refs_0_), channel_id=1, source_target_pairs={{0,1},{1,0},{2,3},{3,2},{4,5},{5,4},{6,7},{7,6},{8,9},{9,8},{10,11... | collective-permute-start | bytes 786440 | tf_op jit(solution)/shard_map/ppermute | solution.py:59
  63.5 1.5 %collective-permute-start.18 = (bf16[64,2048]{1,0:T(8,128)(2,1)S(1)}, bf16[64,2048]{1,0:T(8,128)(2,1)S(1)}, u32[]{:S(2)}, u32[]{:S(2)}) collective-permute-start(bf16[64,2048]{1,0:T(8,128)(2,1)S(1)} %collective-permute-done.17.refs_1_), channel_id=1, source_target_pairs={{0,1},{1,0},{2,3},{3,2},{4,5},{5,4},{6,7},{7,6},{8,9},{9,8},{10,11... | collective-permute-start | bytes 786440 | tf_op jit(solution)/shard_map/ppermute | solution.py:59
  66.5 1.5 %collective-permute-start.23 = (bf16[320,128]{1,0:T(8,128)(2,1)S(1)}, bf16[320,128]{1,0:T(8,128)(2,1)S(1)}, u32[]{:S(2)}, u32[]{:S(2)}) collective-permute-start(bf16[320,128]{1,0:T(8,128)(2,1)S(1)} %get-tuple-element.102), channel_id=1, source_target_pairs={{0,1},{1,0},{2,3},{3,2},{4,5},{5,4},{6,7},{7,6},{8,9},{9,8},{10,11... | collective-permute-start | bytes 245768 | tf_op jit(solution)/shard_map/ppermute | solution.py:59
  68.0 4.9 %collective-permute-start.24 = (bf16[320,128]{1,0:T(8,128)(2,1)S(1)}, bf16[320,128]{1,0:T(8,128)(2,1)S(1)}, u32[]{:S(2)}, u32[]{:S(2)}) collective-permute-start(bf16[320,128]{1,0:T(8,128)(2,1)S(1)} %get-tuple-element.104), channel_id=1, source_target_pairs={{0,2},{1,3},{2,0},{3,1},{4,6},{5,7},{6,4},{7,5},{8,10},{9,11},{10,... | collective-permute-start | bytes 245768 | tf_op jit(solution)/shard_map/ppermute | solution.py:59
  73.0 4.7 %collective-permute-start.25 = (bf16[320,128]{1,0:T(8,128)(2,1)S(1)}, bf16[320,128]{1,0:T(8,128)(2,1)S(1)}, u32[]{:S(2)}, u32[]{:S(2)}) collective-permute-start(bf16[320,128]{1,0:T(8,128)(2,1)S(1)} %get-tuple-element.106), channel_id=1, source_target_pairs={{0,4},{1,5},{2,6},{3,7},{4,0},{5,1},{6,2},{7,3},{8,12},{9,13},{10,... | collective-permute-start | bytes 245768 | tf_op jit(solution)/shard_map/ppermute | solution.py:59
  74.6 8.9 %collective-permute-start.26 = (bf16[320,128]{1,0:T(8,128)(2,1)S(1)}, bf16[320,128]{1,0:T(8,128)(2,1)S(1)}, u32[]{:S(2)}, u32[]{:S(2)}) collective-permute-start(bf16[320,128]{1,0:T(8,128)(2,1)S(1)} %get-tuple-element.106), channel_id=1, source_target_pairs={{0,8},{1,9},{2,10},{3,11},{4,12},{5,13},{6,14},{7,15},{8,0},{9,1},... | collective-permute-start | bytes 245768 | tf_op jit(solution)/shard_map/ppermute | solution.py:59
  75.6 7.9 %collective-permute-start.27 = (bf16[320,128]{1,0:T(8,128)(2,1)S(1)}, bf16[320,128]{1,0:T(8,128)(2,1)S(1)}, u32[]{:S(2)}, u32[]{:S(2)}) collective-permute-start(bf16[320,128]{1,0:T(8,128)(2,1)S(1)} %get-tuple-element.106), channel_id=1, source_target_pairs={{0,12},{1,13},{2,14},{3,15},{4,8},{5,9},{6,10},{7,11},{8,4},{9,5},... | collective-permute-start | bytes 245768 | tf_op jit(solution)/shard_map/ppermute | solution.py:59
  83.6 1.3 %collective-permute-start.28 = (bf16[320,128]{1,0:T(8,128)(2,1)S(1)}, bf16[320,128]{1,0:T(8,128)(2,1)S(1)}, u32[]{:S(2)}, u32[]{:S(2)}) collective-permute-start(bf16[320,128]{1,0:T(8,128)(2,1)S(1)} %shard_map.119.refs_0_), channel_id=1, source_target_pairs={{0,1},{1,0},{2,3},{3,2},{4,5},{5,4},{6,7},{7,6},{8,9},{9,8},{10,11... | collective-permute-start | bytes 245768 | tf_op jit(solution)/shard_map/ppermute | solution.py:59

commit v17 on v13

--- a/solution.py
+++ b/solution.py
@@ -28,7 +28,7 @@
 STEP_SIZE = 0.3
 MIB = 1024 * 1024
 VMEM_BYTES = 24 * MIB
-REDUCE_SHARE = 0.5
+REDUCE_SHARE = 0.625
 GATHER_SHARE = 0.5
 BF16 = jnp.bfloat16
 F32 = jnp.float32
@@ -113,7 +113,8 @@
 
 
 def first_body(core, block, tile, r_ref, p_ref, *refs):
-    sent_x, sent_z, keep_x, keep_z, r_held, p_held, r_sem, p_sem = refs
+    sent_low, sent_high, keep_x, keep_z, r_held, p_held, r_sem, p_sem = refs
+    width = sent_low.shape[1]
     rows = r_held.shape[0] // 2
     r_copy = pltpu.make_async_copy(r_ref, r_held, r_sem)
     r_copy.start()
@@ -127,23 +128,28 @@
     for t, copy in enumerate(copies):
         copy.wait()
         cols = slice(t * tile, (t + 1) * tile)
-        for side, x_ref, z_ref in ((1 - c, sent_x, sent_z), (c, keep_x, keep_z)):
+        for side in (1 - c, c):
             part = lax.dot_general(
                 r_held[pl.ds(pl.multiple_of(side * rows, rows), rows), :],
                 p_held[cols, :],
                 NT,
                 preferred_element_type=F32,
             )
-            cut(part, block, x_ref, z_ref, cols)
+            if side is c:
+                cut(part, block, keep_x, keep_z, cols)
+            else:
+                ref, first = (sent_low, 0) if t * tile < width else (sent_high, width)
+                ref[:, t * tile - first : (t + 1) * tile - first] = part.astype(BF16)
 
 
 def first_sums(response, projectors, core, block, first):
     bands, cells = response.shape
     count = projectors.shape[0]
     rows = bands // 2
-    tile = min(512, count)
+    tile = min(512, count // 2)
     rows_x = rows // block * first
-    outs = [struct((n, count), t) for t in (BF16, F32) for n in (rows_x, rows - rows_x)]
+    outs = [struct((rows, count // 2), BF16)] * 2
+    outs += [struct((n, count), F32) for n in (rows_x, rows - rows_x)]
     return pl.pallas_call(
         functools.partial(first_body, core, block, tile),
         out_shape=outs,
@@ -176,6 +182,35 @@
     for ref in taken:
         total = total + ref[part].astype(F32)
     return total
+
+
+def first_x_body(level, block, keep_ref, low_ref, high_ref, *outs):
+    me = position(level)
+    rows = outs[0].shape[0]
+    half = low_ref.shape[1]
+    for step, out in enumerate(outs):
+        at = me ^ step
+        mine = rows_at(at, rows)
+        theirs = pl.ds(pl.multiple_of(at * block, 16), rows)
+        for k, ref in enumerate((low_ref, high_ref)):
+            cols = slice(k * half, (k + 1) * half)
+            out[:, cols] = (keep_ref[mine, cols] + ref[theirs, :].astype(F32)).astype(out.dtype)
+
+
+def first_z_body(level, block, first, keep_ref, low_ref, high_ref, *outs):
+    me = position(level)
+    rows = block - first
+    width = outs[0].shape[1]
+    per = low_ref.shape[1] // width
+    for step, out in enumerate(outs):
+        at = me ^ step
+        cols = cols_at(at, width)
+        near = cols_at(lax.rem(at, jnp.int32(per)), width)
+        for i in range(out.shape[0] // rows):
+            mine = slice(i * rows, (i + 1) * rows)
+            theirs = slice(i * block + first, (i + 1) * block)
+            taken = jnp.where(at < per, low_ref[theirs, near], high_ref[theirs, near])
+            out[mine, :] = (keep_ref[mine, cols] + taken.astype(F32)).astype(out.dtype)
 
 
 def split_body(received, level, along, *refs):
@@ -516,12 +551,19 @@
     low = neighbour(response[:, local_cells - halo :], count, 1)
     high = neighbour(response[:, :halo], count, -1)
 
-    sent_x, sent_z, keep_x, keep_z = first_sums(response, projectors, core, block, first)
-    sent_z = swapped(sent_z, count, core, 1)
-    sent_x = swapped(sent_x, count, core, 1)
-    keep_z, *parts_z = split(keep_z, [sent_z], along, 1)
-    sent_x, parts_z[0] = lax.optimization_barrier((sent_x, parts_z[0]))
-    keep_x, *parts_x = split(keep_x, [sent_x], across, 0)
+    *sent, keep_x, keep_z = first_sums(response, projectors, core, block, first)
+    sent = [swapped(part, count, core, 1) for part in sent]
+    keep_z, *parts_z = local_call(
+        functools.partial(first_z_body, along, block, first),
+        shares_of((keep_z.shape[0], projections // along[0]), along[0]),
+        [keep_z, *sent],
+    )
+    keep_x, parts_z[0] = lax.optimization_barrier((keep_x, parts_z[0]))
+    keep_x, *parts_x = local_call(
+        functools.partial(first_x_body, across, block),
+        shares_of((first, projections), across[0]),
+        [keep_x, *sent],
+    )
     parts_z[-1], low = lax.optimization_barrier((parts_z[-1], low))
     taken_z, taken_x, low, high = lax.optimization_barrier(
         (parts_to(parts_z, along), parts_to(parts_x, across), low, high)

time: 86.9 us -> 87 us (level)
  waiting for transfers between devices: 35.6 us -> 40.5 us
  starting transfers between devices: 37.4 us -> 32.6 us
    ppermute x27, waiting for transfers between devices: 34.5 us -> 39.6 us  [swapped(): return lax.ppermute(array, 'band', pairs)]
    ppermute x27, starting transfers between devices: 33.8 us -> 29 us  [swapped(): return lax.ppermute(array, 'band', pairs)]
  transfers between devices with their start and end apart: 29 -> 29, of which waited for: 15 -> 18; matrix products, arithmetic and copies ran while one was open for 0% -> 0% of each run, Pallas kernels for 10% -> 10%
where the time goes in v17:
time: 87 us; the launch traced here: 86.9 us
  waiting for transfers between devices  40.5 us (47%)
  starting transfers between devices  32.6 us (37%)
  Pallas kernels  12.8 us (15%)
  between operations  0.91 us (1%)
    ppermute x27, waiting for transfers between devices, swapped(): return lax.ppermute(array, 'band', pairs)  39.6 us
    ppermute x27, starting transfers between devices, swapped(): return lax.ppermute(array, 'band', pairs)  29 us
    pallas_call x1, Pallas kernels, first_sums(): pl.pallas_call(functools.partial(first_body, core, block, tile), out_shap...  4.34 us
    pallas_call x14, Pallas kernels, local_call(): pl.pallas_call(body, out_shape=outs, in_specs=[whole() for _ in args], ou...  3.73 us
    ppermute x2, starting transfers between devices, neighbour(): lax.ppermute(array, 'band', [(i, (i + step) % count) for i in range(count)])  3.62 us
    pallas_call x1, Pallas kernels, project(): pl.pallas_call(functools.partial(project_body, core, blk), grid=(bands //...  2.43 us
    pallas_call x1, Pallas kernels, local_part(): pl.pallas_call(functools.partial(local_body, depth, (group_rows, blk)), g...  2.3 us
  transfers between devices with their start and end apart: 29, of which 18 were waited for; matrix products, arithmetic and copies ran while one was open for 0% of the time, Pallas kernels for 10%

profile of v17, /device:TPU:0, one launch (start us, length us, event | category | flops | bytes accessed | tf_op | source)
XLA Modules:
  0.0 86.9 jit_solution(744507060755345686)
XLA Ops:
  0.6 0.5 collective-permute-start.4
  1.1 4.3 %shard_map.104 = (bf16[256,1024]{1,0:T(8,128)(2,1)S(1)}, bf16[256,1024]{1,0:T(8,128)(2,1)S(1)}, f32[160,2048]{1,0:T(8,128)S(1)}, f32[96,2048]{1,0:T(8,128)S(1)}) custom-call(bf16[512,768]{1,0:T(8,128)(2,1)} %refs_5_.1, bf16[2048,768]{1,0:T(8,128)(2,1)} %refs_3_.5), custom_call_target="tpu_custom_call" | custom-call | flops 1610612736 | bytes 6291456 | tf_op jit(solution)/shard_map/pallas_call | solution.py:153
  5.5 2.6 %collective-permute-start = (bf16[256,1024]{1,0:T(8,128)(2,1)S(1)}, bf16[256,1024]{1,0:T(8,128)(2,1)S(1)}, u32[]{:S(2)}, u32[]{:S(2)}) collective-permute-start(bf16[256,1024]{1,0:T(8,128)(2,1)S(1)} %get-tuple-element.65), channel_id=1, source_target_pairs={{0,1},{1,0},{2,3},{3,2},{4,5},{5,4},{6,7},{7,6},{8,9},{9,8},{10,11... | collective-permute-start | bytes 1572872 | tf_op jit(solution)/shard_map/ppermute | solution.py:59
  8.1 0.1 collective-permute-start.1
  8.2 3.1 %collective-permute-start.7 = (bf16[512,768]{1,0:T(8,128)(2,1)S(1)}, bf16[512,768]{1,0:T(8,128)(2,1)S(1)}, u32[]{:S(2)}, u32[]{:S(2)}) collective-permute-start(bf16[512,768]{1,0:T(8,128)(2,1)S(1)} %copy-done.2), channel_id=1, source_target_pairs={{0,15},{1,0},{2,1},{3,2},{4,3},{5,4},{6,5},{7,6},{8,7},{9,8},{10,9... | collective-permute-start | bytes 2359304 | tf_op jit(solution)/shard_map/ppermute | solution.py:50
  11.3 0.1 shard_map.105
  11.5 0.1 shard_map.106
  11.6 0.0 copy-start.7
  11.6 0.0 copy-start.8
  11.6 0.0 copy-start.1
  11.6 0.7 collective-permute-start.6
  12.4 1.6 %collective-permute-start.2 = (bf16[96,512]{1,0:T(8,128)(2,1)S(1)}, bf16[96,512]{1,0:T(8,128)(2,1)S(1)}, u32[]{:S(2)}, u32[]{:S(2)}) collective-permute-start(bf16[96,512]{1,0:T(8,128)(2,1)S(1)} %get-tuple-element.70), channel_id=1, source_target_pairs={{0,4},{1,5},{2,6},{3,7},{4,0},{5,1},{6,2},{7,3},{8,12},{9,13},{10,... | collective-permute-start | bytes 294920 | tf_op jit(solution)/shard_map/ppermute | solution.py:59
  13.9 1.4 %collective-permute-start.3 = (bf16[96,512]{1,0:T(8,128)(2,1)S(1)}, bf16[96,512]{1,0:T(8,128)(2,1)S(1)}, u32[]{:S(2)}, u32[]{:S(2)}) collective-permute-start(bf16[96,512]{1,0:T(8,128)(2,1)S(1)} %get-tuple-element.71), channel_id=1, source_target_pairs={{0,8},{1,9},{2,10},{3,11},{4,12},{5,13},{6,14},{7,15},{8,0},{9,1},... | collective-permute-start | bytes 294920 | tf_op jit(solution)/shard_map/ppermute | solution.py:59
  15.3 0.9 %collective-permute-done.4.refs_1_ = bf16[512,768]{1,0:T(8,128)(2,1)S(1)} collective-permute-done((bf16[512,768]{1,0:T(8,128)(2,1)}, bf16[512,768]{1,0:T(8,128)(2,1)S(1)}, u32[]{:S(2)}, u32[]{:S(2)}) %collective-permute-start.4) | collective-permute-done | bytes 786464 | tf_op jit(solution)/shard_map/ppermute | solution.py:50
  16.2 2.2 %collective-permute-start.5 = (bf16[96,512]{1,0:T(8,128)(2,1)S(1)}, bf16[96,512]{1,0:T(8,128)(2,1)S(1)}, u32[]{:S(2)}, u32[]{:S(2)}) collective-permute-start(bf16[96,512]{1,0:T(8,128)(2,1)S(1)} %get-tuple-element.73), channel_id=1, source_target_pairs={{0,12},{1,13},{2,14},{3,15},{4,8},{5,9},{6,10},{7,11},{8,4},{9,5},... | collective-permute-start | bytes 294920 | tf_op jit(solution)/shard_map/ppermute | solution.py:59
  18.4 7.1 %collective-permute-done.2.refs_1_ = bf16[96,512]{1,0:T(8,128)(2,1)S(1)} collective-permute-done((bf16[96,512]{1,0:T(8,128)(2,1)S(1)}, bf16[96,512]{1,0:T(8,128)(2,1)S(1)}, u32[]{:S(2)}, u32[]{:S(2)}) %collective-permute-start.2) | collective-permute-done | bytes 98336 | tf_op jit(solution)/shard_map/ppermute | solution.py:59
  25.5 2.1 %collective-permute-done.3.refs_2_ = bf16[96,512]{1,0:T(8,128)(2,1)S(1)} collective-permute-done((bf16[96,512]{1,0:T(8,128)(2,1)S(1)}, bf16[96,512]{1,0:T(8,128)(2,1)S(1)}, u32[]{:S(2)}, u32[]{:S(2)}) %collective-permute-start.3) | collective-permute-done | bytes 98336 | tf_op jit(solution)/shard_map/ppermute | solution.py:59
  27.6 3.9 %collective-permute-done.6.refs_1_ = bf16[80,2048]{1,0:T(8,128)(2,1)S(1)} collective-permute-done((bf16[80,2048]{1,0:T(8,128)(2,1)S(1)}, bf16[80,2048]{1,0:T(8,128)(2,1)S(1)}, u32[]{:S(2)}, u32[]{:S(2)}) %collective-permute-start.6) | collective-permute-done | bytes 327712 | tf_op jit(solution)/shard_map/ppermute | solution.py:59
  31.5 0.1 shard_map.107
  31.5 2.3 %collective-permute-start.10 = (bf16[80,512]{1,0:T(8,128)(2,1)S(1)}, bf16[80,512]{1,0:T(8,128)(2,1)S(1)}, u32[]{:S(2)}, u32[]{:S(2)}) collective-permute-start(bf16[80,512]{1,0:T(8,128)(2,1)S(1)} %get-tuple-element.80), channel_id=1, source_target_pairs={{0,12},{1,13},{2,14},{3,15},{4,8},{5,9},{6,10},{7,11},{8,4},{9,5},... | collective-permute-start | bytes 245768 | tf_op jit(solution)/shard_map/ppermute | solution.py:59
  33.9 0.1 collective-permute-start.8
  34.0 2.0 %collective-permute-start.9 = (bf16[80,512]{1,0:T(8,128)(2,1)S(1)}, bf16[80,512]{1,0:T(8,128)(2,1)S(1)}, u32[]{:S(2)}, u32[]{:S(2)}) collective-permute-start(bf16[80,512]{1,0:T(8,128)(2,1)S(1)} %get-tuple-element.79), channel_id=1, source_target_pairs={{0,8},{1,9},{2,10},{3,11},{4,12},{5,13},{6,14},{7,15},{8,0},{9,1},... | collective-permute-start | bytes 245768 | tf_op jit(solution)/shard_map/ppermute | solution.py:59
  36.0 0.0 copy-start.3
  36.1 0.0 copy-start.4
  36.1 0.0 copy-start.6
  36.1 0.1 collective-permute-start.11
  36.2 4.1 %collective-permute-done.11.refs_5_ = bf16[48,512]{1,0:T(8,128)(2,1)S(1)} collective-permute-done((bf16[48,512]{1,0:T(8,128)(2,1)S(1)}, bf16[48,512]{1,0:T(8,128)(2,1)S(1)}, u32[]{:S(2)}, u32[]{:S(2)}) %collective-permute-start.11) | collective-permute-done | bytes 49184 | tf_op jit(solution)/shard_map/ppermute | solution.py:59
  40.2 0.2 collective-permute-done.8.refs_1_
  40.5 0.4 collective-permute-done.9.refs_2_
  40.9 0.1 shard_map.109
  41.0 0.5 collective-permute-start.12
  41.5 2.7 %collective-permute-start.13 = (bf16[64,512]{1,0:T(8,128)(2,1)S(1)}, bf16[64,512]{1,0:T(8,128)(2,1)S(1)}, u32[]{:S(2)}, u32[]{:S(2)}) collective-permute-start(bf16[64,512]{1,0:T(8,128)(2,1)S(1)} %get-tuple-element.93.refs_0_), channel_id=1, source_target_pairs={{0,8},{1,9},{2,10},{3,11},{4,12},{5,13},{6,14},{7,15},{8,0},{9,1},... | collective-permute-start | bytes 196616 | tf_op jit(solution)/shard_map/ppermute | solution.py:59
  44.2 1.2 %collective-permute-start.14 = (bf16[64,512]{1,0:T(8,128)(2,1)S(1)}, bf16[64,512]{1,0:T(8,128)(2,1)S(1)}, u32[]{:S(2)}, u32[]{:S(2)}) collective-permute-start(bf16[64,512]{1,0:T(8,128)(2,1)S(1)} %get-tuple-element.93.refs_0_), channel_id=1, source_target_pairs={{0,12},{1,13},{2,14},{3,15},{4,8},{5,9},{6,10},{7,11},{8,4},{9,5},... | collective-permute-start | bytes 196616 | tf_op jit(solution)/shard_map/ppermute | solution.py:59
  45.4 0.4 collective-permute-start.15
  45.8 2.6 %collective-permute-done.13.refs_2_ = bf16[64,512]{1,0:T(8,128)(2,1)S(1)} collective-permute-done((bf16[64,512]{1,0:T(8,128)(2,1)S(1)}, bf16[64,512]{1,0:T(8,128)(2,1)S(1)}, u32[]{:S(2)}, u32[]{:S(2)}) %collective-permute-start.13) | collective-permute-done | bytes 65568 | tf_op jit(solution)/shard_map/ppermute | solution.py:59
  48.5 1.8 %collective-permute-done.14.refs_3_ = bf16[64,512]{1,0:T(8,128)(2,1)S(1)} collective-permute-done((bf16[64,512]{1,0:T(8,128)(2,1)S(1)}, bf16[64,512]{1,0:T(8,128)(2,1)S(1)}, u32[]{:S(2)}, u32[]{:S(2)}) %collective-permute-start.14) | collective-permute-done | bytes 65568 | tf_op jit(solution)/shard_map/ppermute | solution.py:59
  50.3 0.1 collective-permute-start.19
  50.3 2.6 %collective-permute-start.20 = (bf16[128,512]{1,0:T(8,128)(2,1)S(1)}, bf16[128,512]{1,0:T(8,128)(2,1)S(1)}, u32[]{:S(2)}, u32[]{:S(2)}) collective-permute-start(bf16[128,512]{1,0:T(8,128)(2,1)S(1)} %shard_map.111.refs_0_), channel_id=1, source_target_pairs={{0,8},{1,9},{2,10},{3,11},{4,12},{5,13},{6,14},{7,15},{8,0},{9,1},... | collective-permute-start | bytes 393224 | tf_op jit(solution)/shard_map/ppermute | solution.py:59
  52.9 1.8 %collective-permute-start.21 = (bf16[128,512]{1,0:T(8,128)(2,1)S(1)}, bf16[128,512]{1,0:T(8,128)(2,1)S(1)}, u32[]{:S(2)}, u32[]{:S(2)}) collective-permute-start(bf16[128,512]{1,0:T(8,128)(2,1)S(1)} %shard_map.111.refs_0_), channel_id=1, source_target_pairs={{0,12},{1,13},{2,14},{3,15},{4,8},{5,9},{6,10},{7,11},{8,4},{9,5},... | collective-permute-start | bytes 393224 | tf_op jit(solution)/shard_map/ppermute | solution.py:59
  54.8 0.1 shard_map.113.refs_5_.refs_4_
  54.9 0.1 collective-permute-start.17
  55.0 2.3 %shard_map.112 = (f32[512,768]{1,0:T(8,128)S(1)}, bf16[512,256]{1,0:T(8,128)(2,1)S(1)}) custom-call(bf16[512,768]{1,0:T(8,128)(2,1)S(1)} %copy-done.2, bf16[512,768]{1,0:T(8,128)(2,1)S(1)} %collective-permute-done.4.refs_1_, bf16[512,768]{1,0:T(8,128)(2,1)S(1)} %collective-permute-done.7.refs_2_, bf16[512,768]{1,0:T(8,128)(2,1)S(1)} %copy-done.1, ...), custom_call_target="tpu_custom_call" | custom-call | flops 235929600 | bytes 4980736 | tf_op jit(solution)/shard_map/pallas_call | solution.py:333
  57.3 0.2 collective-permute-done.19.refs_1_
  57.5 4.3 %collective-permute-done.20.refs_2_ = bf16[128,512]{1,0:T(8,128)(2,1)S(1)} collective-permute-done((bf16[128,512]{1,0:T(8,128)(2,1)S(1)}, bf16[128,512]{1,0:T(8,128)(2,1)S(1)}, u32[]{:S(2)}, u32[]{:S(2)}) %collective-permute-start.20) | collective-permute-done | bytes 131104 | tf_op jit(solution)/shard_map/ppermute | solution.py:59
  61.8 0.1 shard_map.114.refs_2_
  61.9 0.1 collective-permute-start.22
  61.9 0.5 collective-permute-start.16
  62.4 0.1 collective-permute-start.18
  62.5 1.5 %shard_map.115 = (f32[256,768]{1,0:T(8,128)S(1)}, f32[320,128]{1,0:T(8,128)S(1)}) custom-call(bf16[64,2048]{1,0:T(8,128)(2,1)S(1)} %shard_map.110.refs_0_, bf16[64,2048]{1,0:T(8,128)(2,1)S(1)} %collective-permute-done.17.refs_1_, bf16[128,2048]{1,0:T(8,128)(2,1)S(1)} %shard_map.114.refs_2_, bf16[2048,768]{1,0:T(8,128)(2,1)S(1)} %copy-done, ...), custom_call_target="tpu_custom_call" | custom-call | flops 905969664 | bytes 7700480 | tf_op jit(solution)/shard_map/pallas_call | solution.py:91
  64.0 0.2 collective-permute-done.16.refs_0_
  64.2 0.4 collective-permute-done.18.refs_1_
  64.6 1.5 %shard_map.116 = (f32[256,768]{1,0:T(8,128)S(1)}, bf16[320,128]{1,0:T(8,128)(2,1)S(1)}) custom-call(bf16[64,2048]{1,0:T(8,128)(2,1)S(1)} %collective-permute-done.16.refs_0_, bf16[64,2048]{1,0:T(8,128)(2,1)S(1)} %collective-permute-done.18.refs_1_, bf16[128,2048]{1,0:T(8,128)(2,1)S(1)} %collective-permute-done.22.refs_2_, bf16[2048,768]{1,0:T(8,128)(2,1)S(1)} %copy-done, ...), custom_call_target="tpu_custom_call" | custom-call | flops 905969664 | bytes 7618560 | tf_op jit(solution)/shard_map/pallas_call | solution.py:91
  66.1 0.2 collective-permute-start.23
  66.3 1.1 %collective-permute-done.23.refs_0_ = bf16[320,128]{1,0:T(8,128)(2,1)S(1)} collective-permute-done((bf16[320,128]{1,0:T(8,128)(2,1)S(1)}, bf16[320,128]{1,0:T(8,128)(2,1)S(1)}, u32[]{:S(2)}, u32[]{:S(2)}) %collective-permute-start.23) | collective-permute-done | bytes 81952 | tf_op jit(solution)/shard_map/ppermute | solution.py:59
  67.5 1.0 %collective-permute-start.24 = (bf16[320,128]{1,0:T(8,128)(2,1)S(1)}, bf16[320,128]{1,0:T(8,128)(2,1)S(1)}, u32[]{:S(2)}, u32[]{:S(2)}) collective-permute-start(bf16[320,128]{1,0:T(8,128)(2,1)S(1)} %get-tuple-element.118), channel_id=1, source_target_pairs={{0,2},{1,3},{2,0},{3,1},{4,6},{5,7},{6,4},{7,5},{8,10},{9,11},{10,... | collective-permute-start | bytes 245768 | tf_op jit(solution)/shard_map/ppermute | solution.py:59
  68.5 3.6 %collective-permute-done.24.refs_0_ = bf16[320,128]{1,0:T(8,128)(2,1)S(1)} collective-permute-done((bf16[320,128]{1,0:T(8,128)(2,1)S(1)}, bf16[320,128]{1,0:T(8,128)(2,1)S(1)}, u32[]{:S(2)}, u32[]{:S(2)}) %collective-permute-start.24) | collective-permute-done | bytes 81952 | tf_op jit(solution)/shard_map/ppermute | solution.py:59
  72.1 2.2 %collective-permute-start.25 = (bf16[320,128]{1,0:T(8,128)(2,1)S(1)}, bf16[320,128]{1,0:T(8,128)(2,1)S(1)}, u32[]{:S(2)}, u32[]{:S(2)}) collective-permute-start(bf16[320,128]{1,0:T(8,128)(2,1)S(1)} %get-tuple-element.120), channel_id=1, source_target_pairs={{0,4},{1,5},{2,6},{3,7},{4,0},{5,1},{6,2},{7,3},{8,12},{9,13},{10,... | collective-permute-start | bytes 245768 | tf_op jit(solution)/shard_map/ppermute | solution.py:59
  74.3 0.8 collective-permute-start.26
  75.1 1.6 %collective-permute-start.27 = (bf16[320,128]{1,0:T(8,128)(2,1)S(1)}, bf16[320,128]{1,0:T(8,128)(2,1)S(1)}, u32[]{:S(2)}, u32[]{:S(2)}) collective-permute-start(bf16[320,128]{1,0:T(8,128)(2,1)S(1)} %get-tuple-element.120), channel_id=1, source_target_pairs={{0,12},{1,13},{2,14},{3,15},{4,8},{5,9},{6,10},{7,11},{8,4},{9,5},... | collective-permute-start | bytes 245768 | tf_op jit(solution)/shard_map/ppermute | solution.py:59
  76.7 0.3 collective-permute-done.25.refs_0_
  77.0 6.0 %collective-permute-done.26.refs_1_ = bf16[320,128]{1,0:T(8,128)(2,1)S(1)} collective-permute-done((bf16[320,128]{1,0:T(8,128)(2,1)S(1)}, bf16[320,128]{1,0:T(8,128)(2,1)S(1)}, u32[]{:S(2)}, u32[]{:S(2)}) %collective-permute-start.26) | collective-permute-done | bytes 81952 | tf_op jit(solution)/shard_map/ppermute | solution.py:59
  83.1 0.1 collective-permute-start.28
  83.2 1.3 %collective-permute-done.28.refs_1_ = bf16[320,128]{1,0:T(8,128)(2,1)S(1)} collective-permute-done((bf16[320,128]{1,0:T(8,128)(2,1)S(1)}, bf16[320,128]{1,0:T(8,128)(2,1)S(1)}, u32[]{:S(2)}, u32[]{:S(2)}) %collective-permute-start.28) | collective-permute-done | bytes 81952 | tf_op jit(solution)/shard_map/ppermute | solution.py:59
  84.4 2.4 %shard_map.120 = (bf16[512,768]{1,0:T(8,128)(2,1)}, bf16[512,768]{1,0:T(8,128)(2,1)}) custom-call(bf16[320,128]{1,0:T(8,128)(2,1)S(1)} %shard_map.119.refs_0_, bf16[320,128]{1,0:T(8,128)(2,1)S(1)} %collective-permute-done.28.refs_1_, f32[256,768]{1,0:T(8,128)S(1)} %get-tuple-element.121.refs_2_, f32[256,768]{1,0:T(8,128)S(1)} %get-tuple-element.122.refs_3_, ...), custom_call_target="tpu_custom_call" | custom-call | flops 201326592 | bytes 4915200 | tf_op jit(solution)/shard_map/pallas_call | solution.py:503
  (31 shorter events, 0.3 us)
Async XLA Ops:
  0.6 7.6 %copy-start.2 = (bf16[512,768]{1,0:T(8,128)(2,1)S(1)}, bf16[512,768]{1,0:T(8,128)(2,1)}, u32[]{:S(2)}) copy-start(bf16[512,768]{1,0:T(8,128)(2,1)} %refs_5_.1) | copy-start | bytes 2359300
  0.6 15.6 %collective-permute-start.4 = (bf16[512,768]{1,0:T(8,128)(2,1)}, bf16[512,768]{1,0:T(8,128)(2,1)S(1)}, u32[]{:S(2)}, u32[]{:S(2)}) collective-permute-start(bf16[512,768]{1,0:T(8,128)(2,1)} %refs_5_.1), channel_id=1, source_target_pairs={{0,1},{1,2},{2,3},{3,4},{4,5},{5,6},{6,7},{7,8},{8,9},{9,10},{10,1... | collective-permute-start | bytes 2359304 | tf_op jit(solution)/shard_map/ppermute | solution.py:50
  5.5 5.8 %collective-permute-start = (bf16[256,1024]{1,0:T(8,128)(2,1)S(1)}, bf16[256,1024]{1,0:T(8,128)(2,1)S(1)}, u32[]{:S(2)}, u32[]{:S(2)}) collective-permute-start(bf16[256,1024]{1,0:T(8,128)(2,1)S(1)} %get-tuple-element.65), channel_id=1, source_target_pairs={{0,1},{1,0},{2,3},{3,2},{4,5},{5,4},{6,7},{7,6},{8,9},{9,8},{10,11... | collective-permute-start | bytes 1572872 | tf_op jit(solution)/shard_map/ppermute | solution.py:59
  8.1 3.2 %collective-permute-start.1 = (bf16[256,1024]{1,0:T(8,128)(2,1)S(1)}, bf16[256,1024]{1,0:T(8,128)(2,1)S(1)}, u32[]{:S(2)}, u32[]{:S(2)}) collective-permute-start(bf16[256,1024]{1,0:T(8,128)(2,1)S(1)} %get-tuple-element.66), channel_id=1, source_target_pairs={{0,1},{1,0},{2,3},{3,2},{4,5},{5,4},{6,7},{7,6},{8,9},{9,8},{10,11... | collective-permute-start | bytes 1572872 | tf_op jit(solution)/shard_map/ppermute | solution.py:59
  8.2 19.4 %collective-permute-start.7 = (bf16[512,768]{1,0:T(8,128)(2,1)S(1)}, bf16[512,768]{1,0:T(8,128)(2,1)S(1)}, u32[]{:S(2)}, u32[]{:S(2)}) collective-permute-start(bf16[512,768]{1,0:T(8,128)(2,1)S(1)} %copy-done.2), channel_id=1, source_target_pairs={{0,15},{1,0},{2,1},{3,2},{4,3},{5,4},{6,5},{7,6},{8,7},{9,8},{10,9... | collective-permute-start | bytes 2359304 | tf_op jit(solution)/shard_map/ppermute | solution.py:50
  11.6 43.1 %copy-start.7 = (f32[768]{0:T(1024)S(1)}, f32[768]{0:T(1024)}, u32[]{:S(2)}) copy-start(f32[768]{0:T(1024)} %param.12) | copy-start | bytes 9220
  11.6 43.1 %copy-start.8 = (f32[768]{0:T(1024)S(1)}, f32[768]{0:T(1024)}, u32[]{:S(2)}) copy-start(f32[768]{0:T(1024)} %param.13) | copy-start | bytes 9220
  11.6 43.1 %copy-start.1 = (bf16[512,768]{1,0:T(8,128)(2,1)S(1)}, bf16[512,768]{1,0:T(8,128)(2,1)}, u32[]{:S(2)}) copy-start(bf16[512,768]{1,0:T(8,128)(2,1)} %o_ref.1) | copy-start | bytes 2359300
  11.6 19.8 %collective-permute-start.6 = (bf16[80,2048]{1,0:T(8,128)(2,1)S(1)}, bf16[80,2048]{1,0:T(8,128)(2,1)S(1)}, u32[]{:S(2)}, u32[]{:S(2)}) collective-permute-start(bf16[80,2048]{1,0:T(8,128)(2,1)S(1)} %get-tuple-element.74), channel_id=1, source_target_pairs={{0,2},{1,3},{2,0},{3,1},{4,6},{5,7},{6,4},{7,5},{8,10},{9,11},{10,... | collective-permute-start | bytes 983048 | tf_op jit(solution)/shard_map/ppermute | solution.py:59
  12.4 13.1 %collective-permute-start.2 = (bf16[96,512]{1,0:T(8,128)(2,1)S(1)}, bf16[96,512]{1,0:T(8,128)(2,1)S(1)}, u32[]{:S(2)}, u32[]{:S(2)}) collective-permute-start(bf16[96,512]{1,0:T(8,128)(2,1)S(1)} %get-tuple-element.70), channel_id=1, source_target_pairs={{0,4},{1,5},{2,6},{3,7},{4,0},{5,1},{6,2},{7,3},{8,12},{9,13},{10,... | collective-permute-start | bytes 294920 | tf_op jit(solution)/shard_map/ppermute | solution.py:59
  13.9 13.6 %collective-permute-start.3 = (bf16[96,512]{1,0:T(8,128)(2,1)S(1)}, bf16[96,512]{1,0:T(8,128)(2,1)S(1)}, u32[]{:S(2)}, u32[]{:S(2)}) collective-permute-start(bf16[96,512]{1,0:T(8,128)(2,1)S(1)} %get-tuple-element.71), channel_id=1, source_target_pairs={{0,8},{1,9},{2,10},{3,11},{4,12},{5,13},{6,14},{7,15},{8,0},{9,1},... | collective-permute-start | bytes 294920 | tf_op jit(solution)/shard_map/ppermute | solution.py:59
  16.2 15.3 %collective-permute-start.5 = (bf16[96,512]{1,0:T(8,128)(2,1)S(1)}, bf16[96,512]{1,0:T(8,128)(2,1)S(1)}, u32[]{:S(2)}, u32[]{:S(2)}) collective-permute-start(bf16[96,512]{1,0:T(8,128)(2,1)S(1)} %get-tuple-element.73), channel_id=1, source_target_pairs={{0,12},{1,13},{2,14},{3,15},{4,8},{5,9},{6,10},{7,11},{8,4},{9,5},... | collective-permute-start | bytes 294920 | tf_op jit(solution)/shard_map/ppermute | solution.py:59
  31.5 8.7 %collective-permute-start.10 = (bf16[80,512]{1,0:T(8,128)(2,1)S(1)}, bf16[80,512]{1,0:T(8,128)(2,1)S(1)}, u32[]{:S(2)}, u32[]{:S(2)}) collective-permute-start(bf16[80,512]{1,0:T(8,128)(2,1)S(1)} %get-tuple-element.80), channel_id=1, source_target_pairs={{0,12},{1,13},{2,14},{3,15},{4,8},{5,9},{6,10},{7,11},{8,4},{9,5},... | collective-permute-start | bytes 245768 | tf_op jit(solution)/shard_map/ppermute | solution.py:59
  33.9 6.6 %collective-permute-start.8 = (bf16[80,512]{1,0:T(8,128)(2,1)S(1)}, bf16[80,512]{1,0:T(8,128)(2,1)S(1)}, u32[]{:S(2)}, u32[]{:S(2)}) collective-permute-start(bf16[80,512]{1,0:T(8,128)(2,1)S(1)} %get-tuple-element.78), channel_id=1, source_target_pairs={{0,4},{1,5},{2,6},{3,7},{4,0},{5,1},{6,2},{7,3},{8,12},{9,13},{10,... | collective-permute-start | bytes 245768 | tf_op jit(solution)/shard_map/ppermute | solution.py:59
  34.0 6.9 %collective-permute-start.9 = (bf16[80,512]{1,0:T(8,128)(2,1)S(1)}, bf16[80,512]{1,0:T(8,128)(2,1)S(1)}, u32[]{:S(2)}, u32[]{:S(2)}) collective-permute-start(bf16[80,512]{1,0:T(8,128)(2,1)S(1)} %get-tuple-element.79), channel_id=1, source_target_pairs={{0,8},{1,9},{2,10},{3,11},{4,12},{5,13},{6,14},{7,15},{8,0},{9,1},... | collective-permute-start | bytes 245768 | tf_op jit(solution)/shard_map/ppermute | solution.py:59
  36.0 18.9 %copy-start.3 = (bf16[2,128,128]{2,1,0:T(8,128)(2,1)S(1)}, bf16[2,128,128]{2,1,0:T(8,128)(2,1)}, u32[]{:S(2)}) copy-start(bf16[2,128,128]{2,1,0:T(8,128)(2,1)} %constant.2.clone.refs_4_) | copy-start | bytes 196612
  36.1 18.9 %copy-start.4 = (f32[512]{0:T(512)S(1)}, f32[512]{0:T(512)}, u32[]{:S(2)}) copy-start(f32[512]{0:T(512)} %param.14) | copy-start | bytes 6148
  36.1 18.9 %copy-start.5 = (s32[512]{0:T(512)S(1)}, s32[512]{0:T(512)}, u32[]{:S(2)}) copy-start(s32[512]{0:T(512)} %param.15) | copy-start | bytes 6148
  36.1 18.9 %copy-start.6 = (s32[512]{0:T(512)S(1)}, s32[512]{0:T(512)}, u32[]{:S(2)}) copy-start(s32[512]{0:T(512)} %param.16) | copy-start | bytes 6148
  36.1 4.2 %collective-permute-start.11 = (bf16[48,512]{1,0:T(8,128)(2,1)S(1)}, bf16[48,512]{1,0:T(8,128)(2,1)S(1)}, u32[]{:S(2)}, u32[]{:S(2)}) collective-permute-start(bf16[48,512]{1,0:T(8,128)(2,1)S(1)} %get-tuple-element.85), channel_id=1, source_target_pairs={{0,2},{1,3},{2,0},{3,1},{4,6},{5,7},{6,4},{7,5},{8,10},{9,11},{10,... | collective-permute-start | bytes 147464 | tf_op jit(solution)/shard_map/ppermute | solution.py:59
  41.0 4.9 %collective-permute-start.12 = (bf16[64,512]{1,0:T(8,128)(2,1)S(1)}, bf16[64,512]{1,0:T(8,128)(2,1)S(1)}, u32[]{:S(2)}, u32[]{:S(2)}) collective-permute-start(bf16[64,512]{1,0:T(8,128)(2,1)S(1)} %get-tuple-element.93.refs_0_), channel_id=1, source_target_pairs={{0,4},{1,5},{2,6},{3,7},{4,0},{5,1},{6,2},{7,3},{8,12},{9,13},{10,... | collective-permute-start | bytes 196616 | tf_op jit(solution)/shard_map/ppermute | solution.py:59
  41.5 7.0 %collective-permute-start.13 = (bf16[64,512]{1,0:T(8,128)(2,1)S(1)}, bf16[64,512]{1,0:T(8,128)(2,1)S(1)}, u32[]{:S(2)}, u32[]{:S(2)}) collective-permute-start(bf16[64,512]{1,0:T(8,128)(2,1)S(1)} %get-tuple-element.93.refs_0_), channel_id=1, source_target_pairs={{0,8},{1,9},{2,10},{3,11},{4,12},{5,13},{6,14},{7,15},{8,0},{9,1},... | collective-permute-start | bytes 196616 | tf_op jit(solution)/shard_map/ppermute | solution.py:59
  44.2 6.1 %collective-permute-start.14 = (bf16[64,512]{1,0:T(8,128)(2,1)S(1)}, bf16[64,512]{1,0:T(8,128)(2,1)S(1)}, u32[]{:S(2)}, u32[]{:S(2)}) collective-permute-start(bf16[64,512]{1,0:T(8,128)(2,1)S(1)} %get-tuple-element.93.refs_0_), channel_id=1, source_target_pairs={{0,12},{1,13},{2,14},{3,15},{4,8},{5,9},{6,10},{7,11},{8,4},{9,5},... | collective-permute-start | bytes 196616 | tf_op jit(solution)/shard_map/ppermute | solution.py:59
  45.4 4.8 %collective-permute-start.15 = (bf16[64,512]{1,0:T(8,128)(2,1)S(1)}, bf16[64,512]{1,0:T(8,128)(2,1)S(1)}, u32[]{:S(2)}, u32[]{:S(2)}) collective-permute-start(bf16[64,512]{1,0:T(8,128)(2,1)S(1)} %get-tuple-element.97.refs_0_), channel_id=1, source_target_pairs={{0,2},{1,3},{2,0},{3,1},{4,6},{5,7},{6,4},{7,5},{8,10},{9,11},{10,... | collective-permute-start | bytes 196616 | tf_op jit(solution)/shard_map/ppermute | solution.py:59
  50.3 7.2 %collective-permute-start.19 = (bf16[128,512]{1,0:T(8,128)(2,1)S(1)}, bf16[128,512]{1,0:T(8,128)(2,1)S(1)}, u32[]{:S(2)}, u32[]{:S(2)}) collective-permute-start(bf16[128,512]{1,0:T(8,128)(2,1)S(1)} %shard_map.111.refs_0_), channel_id=1, source_target_pairs={{0,4},{1,5},{2,6},{3,7},{4,0},{5,1},{6,2},{7,3},{8,12},{9,13},{10,... | collective-permute-start | bytes 393224 | tf_op jit(solution)/shard_map/ppermute | solution.py:59
  50.3 11.5 %collective-permute-start.20 = (bf16[128,512]{1,0:T(8,128)(2,1)S(1)}, bf16[128,512]{1,0:T(8,128)(2,1)S(1)}, u32[]{:S(2)}, u32[]{:S(2)}) collective-permute-start(bf16[128,512]{1,0:T(8,128)(2,1)S(1)} %shard_map.111.refs_0_), channel_id=1, source_target_pairs={{0,8},{1,9},{2,10},{3,11},{4,12},{5,13},{6,14},{7,15},{8,0},{9,1},... | collective-permute-start | bytes 393224 | tf_op jit(solution)/shard_map/ppermute | solution.py:59
  52.9 8.9 %collective-permute-start.21 = (bf16[128,512]{1,0:T(8,128)(2,1)S(1)}, bf16[128,512]{1,0:T(8,128)(2,1)S(1)}, u32[]{:S(2)}, u32[]{:S(2)}) collective-permute-start(bf16[128,512]{1,0:T(8,128)(2,1)S(1)} %shard_map.111.refs_0_), channel_id=1, source_target_pairs={{0,12},{1,13},{2,14},{3,15},{4,8},{5,9},{6,10},{7,11},{8,4},{9,5},... | collective-permute-start | bytes 393224 | tf_op jit(solution)/shard_map/ppermute | solution.py:59
  54.9 7.7 %copy-start = (bf16[2048,768]{1,0:T(8,128)(2,1)S(1)}, bf16[2048,768]{1,0:T(8,128)(2,1)}, u32[]{:S(2)}) copy-start(bf16[2048,768]{1,0:T(8,128)(2,1)} %refs_3_.5) | copy-start | bytes 9437188
  54.9 7.6 %collective-permute-start.17 = (bf16[64,2048]{1,0:T(8,128)(2,1)S(1)}, bf16[64,2048]{1,0:T(8,128)(2,1)S(1)}, u32[]{:S(2)}, u32[]{:S(2)}) collective-permute-start(bf16[64,2048]{1,0:T(8,128)(2,1)S(1)} %shard_map.110.refs_0_), channel_id=1, source_target_pairs={{0,2},{1,3},{2,0},{3,1},{4,6},{5,7},{6,4},{7,5},{8,10},{9,11},{10,... | collective-permute-start | bytes 786440 | tf_op jit(solution)/shard_map/ppermute | solution.py:59
  61.9 2.7 %collective-permute-start.22 = (bf16[128,2048]{1,0:T(8,128)(2,1)S(1)}, bf16[128,2048]{1,0:T(8,128)(2,1)S(1)}, u32[]{:S(2)}, u32[]{:S(2)}) collective-permute-start(bf16[128,2048]{1,0:T(8,128)(2,1)S(1)} %shard_map.114.refs_2_), channel_id=1, source_target_pairs={{0,1},{1,0},{2,3},{3,2},{4,5},{5,4},{6,7},{7,6},{8,9},{9,8},{10,11... | collective-permute-start | bytes 1572872 | tf_op jit(solution)/shard_map/ppermute | solution.py:59
  61.9 2.3 %collective-permute-start.16 = (bf16[64,2048]{1,0:T(8,128)(2,1)S(1)}, bf16[64,2048]{1,0:T(8,128)(2,1)S(1)}, u32[]{:S(2)}, u32[]{:S(2)}) collective-permute-start(bf16[64,2048]{1,0:T(8,128)(2,1)S(1)} %shard_map.110.refs_0_), channel_id=1, source_target_pairs={{0,1},{1,0},{2,3},{3,2},{4,5},{5,4},{6,7},{7,6},{8,9},{9,8},{10,11... | collective-permute-start | bytes 786440 | tf_op jit(solution)/shard_map/ppermute | solution.py:59
  62.4 2.1 %collective-permute-start.18 = (bf16[64,2048]{1,0:T(8,128)(2,1)S(1)}, bf16[64,2048]{1,0:T(8,128)(2,1)S(1)}, u32[]{:S(2)}, u32[]{:S(2)}) collective-permute-start(bf16[64,2048]{1,0:T(8,128)(2,1)S(1)} %collective-permute-done.17.refs_1_), channel_id=1, source_target_pairs={{0,1},{1,0},{2,3},{3,2},{4,5},{5,4},{6,7},{7,6},{8,9},{9,8},{10,11... | collective-permute-start | bytes 786440 | tf_op jit(solution)/shard_map/ppermute | solution.py:59
  66.1 1.3 %collective-permute-start.23 = (bf16[320,128]{1,0:T(8,128)(2,1)S(1)}, bf16[320,128]{1,0:T(8,128)(2,1)S(1)}, u32[]{:S(2)}, u32[]{:S(2)}) collective-permute-start(bf16[320,128]{1,0:T(8,128)(2,1)S(1)} %get-tuple-element.116), channel_id=1, source_target_pairs={{0,1},{1,0},{2,3},{3,2},{4,5},{5,4},{6,7},{7,6},{8,9},{9,8},{10,11... | collective-permute-start | bytes 245768 | tf_op jit(solution)/shard_map/ppermute | solution.py:59
  67.5 4.6 %collective-permute-start.24 = (bf16[320,128]{1,0:T(8,128)(2,1)S(1)}, bf16[320,128]{1,0:T(8,128)(2,1)S(1)}, u32[]{:S(2)}, u32[]{:S(2)}) collective-permute-start(bf16[320,128]{1,0:T(8,128)(2,1)S(1)} %get-tuple-element.118), channel_id=1, source_target_pairs={{0,2},{1,3},{2,0},{3,1},{4,6},{5,7},{6,4},{7,5},{8,10},{9,11},{10,... | collective-permute-start | bytes 245768 | tf_op jit(solution)/shard_map/ppermute | solution.py:59
  72.1 5.0 %collective-permute-start.25 = (bf16[320,128]{1,0:T(8,128)(2,1)S(1)}, bf16[320,128]{1,0:T(8,128)(2,1)S(1)}, u32[]{:S(2)}, u32[]{:S(2)}) collective-permute-start(bf16[320,128]{1,0:T(8,128)(2,1)S(1)} %get-tuple-element.120), channel_id=1, source_target_pairs={{0,4},{1,5},{2,6},{3,7},{4,0},{5,1},{6,2},{7,3},{8,12},{9,13},{10,... | collective-permute-start | bytes 245768 | tf_op jit(solution)/shard_map/ppermute | solution.py:59
  74.3 8.8 %collective-permute-start.26 = (bf16[320,128]{1,0:T(8,128)(2,1)S(1)}, bf16[320,128]{1,0:T(8,128)(2,1)S(1)}, u32[]{:S(2)}, u32[]{:S(2)}) collective-permute-start(bf16[320,128]{1,0:T(8,128)(2,1)S(1)} %get-tuple-element.120), channel_id=1, source_target_pairs={{0,8},{1,9},{2,10},{3,11},{4,12},{5,13},{6,14},{7,15},{8,0},{9,1},... | collective-permute-start | bytes 245768 | tf_op jit(solution)/shard_map/ppermute | solution.py:59
  75.1 8.0 %collective-permute-start.27 = (bf16[320,128]{1,0:T(8,128)(2,1)S(1)}, bf16[320,128]{1,0:T(8,128)(2,1)S(1)}, u32[]{:S(2)}, u32[]{:S(2)}) collective-permute-start(bf16[320,128]{1,0:T(8,128)(2,1)S(1)} %get-tuple-element.120), channel_id=1, source_target_pairs={{0,12},{1,13},{2,14},{3,15},{4,8},{5,9},{6,10},{7,11},{8,4},{9,5},... | collective-permute-start | bytes 245768 | tf_op jit(solution)/shard_map/ppermute | solution.py:59
  83.1 1.3 %collective-permute-start.28 = (bf16[320,128]{1,0:T(8,128)(2,1)S(1)}, bf16[320,128]{1,0:T(8,128)(2,1)S(1)}, u32[]{:S(2)}, u32[]{:S(2)}) collective-permute-start(bf16[320,128]{1,0:T(8,128)(2,1)S(1)} %shard_map.119.refs_0_), channel_id=1, source_target_pairs={{0,1},{1,0},{2,3},{3,2},{4,5},{5,4},{6,7},{7,6},{8,9},{9,8},{10,11... | collective-permute-start | bytes 245768 | tf_op jit(solution)/shard_map/ppermute | solution.py:59

commit v18 on v17

--- a/solution.py
+++ b/solution.py
@@ -458,67 +458,59 @@
     return local_call(sum_body, outs, [keep, *taken])
 
 
-def project_body(core, blk, *refs):
-    w_own, w_other, u_own, u_other, pad_ref, r_ref, mask_ref = refs[:7]
-    updated_ref, residual_ref, w_ref, u_ref = refs[7:]
-    rows = u_ref.shape[0]
-    height = w_ref.shape[0]
-    per = u_own.shape[0] // rows
-    g = pl.program_id(0)
-    own = lax.div(g, jnp.int32(per)) == position(core)
-    local = lax.rem(g, jnp.int32(per))
-    w_rows = pl.ds(pl.multiple_of(local * height, 16), height)
-    u_rows = pl.ds(pl.multiple_of(local * rows, rows), rows)
-
-    @pl.when(own)
-    def _():
-        w_ref[...] = w_own[w_rows, :]
-        u_ref[...] = u_own[u_rows, :]
-
-    @pl.when(jnp.logical_not(own))
-    def _():
-        w_ref[...] = w_other[w_rows, :]
-        u_ref[...] = u_other[u_rows, :]
-
-    main, rest = w_ref[:rows, :].astype(F32), w_ref[rows:, :].astype(F32)
-    start = pl.multiple_of(g * rows, rows)
-    residual = u_ref[...]
-    for k, part in enumerate(unpacked(main, rest, blk)):
-        inside = mask_ref[:, k * rows : (k + 1) * rows].astype(F32) > 0.5
-        weights = jnp.where(inside, part, 0.0).astype(BF16)
-        window = pad_ref[pl.ds(pl.multiple_of(start + k * rows, rows), rows), :]
-        residual = residual - jnp.dot(weights, window, preferred_element_type=F32)
-    residual_ref[...] = residual.astype(BF16)
-    updated_ref[...] = (r_ref[...].astype(F32) + STEP_SIZE * residual).astype(BF16)
-
-
-def project(weights, unprojected, padded, response, mask, core, group_rows, blk):
-    bands, cells = response.shape
-    out = struct((bands, cells), BF16)
-    here = pl.BlockSpec((group_rows, cells), lambda g: (g, 0))
-
-    def full(a):
-        return pl.BlockSpec(a.shape, lambda g: (0, 0))
-
+def project_body(core, blk, other, *refs):
+    w_ref, u_ref, pad_ref, r_ref, mask_ref = refs[:5]
+    outs, helds, sems = refs[-5:-3], refs[-3:-1], refs[-1]
+    rows = mask_ref.shape[1] // 2
+    per = u_ref.shape[0] // rows
+    height = w_ref.shape[0] // per
+    c = position(core)
+    copies = []
+    for g in range(per):
+        mine = slice(g * rows, (g + 1) * rows)
+        start = pl.multiple_of(((1 - c if other else c) * per + g) * rows, rows)
+        there = pl.ds(start, rows)
+        main = w_ref[g * height : g * height + rows, :].astype(F32)
+        rest = w_ref[g * height + rows : (g + 1) * height, :].astype(F32)
+        residual = u_ref[mine, :]
+        for k, part in enumerate(unpacked(main, rest, blk)):
+            inside = mask_ref[there, k * rows : (k + 1) * rows].astype(F32) > 0.5
+            weights = jnp.where(inside, part, 0.0).astype(BF16)
+            window = pad_ref[pl.ds(pl.multiple_of(start + k * rows, rows), rows), :]
+            residual = residual - jnp.dot(weights, window, preferred_element_type=F32)
+        updated = r_ref[there, :].astype(F32) + STEP_SIZE * residual
+        for k, value in enumerate((updated, residual)):
+            helds[k][mine, :] = value.astype(BF16)
+            copies.append(
+                pltpu.make_async_copy(
+                    helds[k].at[pl.ds(g * rows, rows), :], outs[k].at[there, :], sems.at[k, g]
+                )
+            )
+            copies[-1].start()
+    for copy in copies:
+        copy.wait()
+
+
+def project(weights, unprojected, padded, response, mask, core, blk, other, before):
+    rows, cells = unprojected.shape
+    per = rows // (mask.shape[1] // 2)
+    out = struct(response.shape, BF16)
+    args = [weights, unprojected, padded, response, mask]
+    anywhere = pl.BlockSpec(memory_space=pl.ANY)
     return pl.pallas_call(
-        functools.partial(project_body, core, blk),
-        grid=(bands // group_rows,),
+        functools.partial(project_body, core, blk, other),
         out_shape=(out, out),
-        in_specs=[
-            *[full(a) for a in (*weights, *unprojected, padded)],
-            here,
-            pl.BlockSpec((group_rows, mask.shape[1]), lambda g: (g, 0)),
+        in_specs=[whole() for _ in args] + [anywhere for _ in before],
+        out_specs=(anywhere, anywhere),
+        scratch_shapes=[
+            pltpu.VMEM((rows, cells), BF16),
+            pltpu.VMEM((rows, cells), BF16),
+            pltpu.SemaphoreType.DMA((2, per)),
         ],
-        out_specs=(here, here),
-        scratch_shapes=[
-            pltpu.VMEM((group_rows + 2 * blk, group_rows), BF16),
-            pltpu.VMEM((group_rows, cells), F32),
-        ],
+        input_output_aliases={5: 0, 6: 1} if before else {},
         compiler_params=params(),
-        cost_estimate=cost(
-            4 * bands * group_rows * cells, padded, *unprojected, response, out, out
-        ),
-    )(*weights, *unprojected, padded, response, mask)
+        cost_estimate=cost(2 * rows * mask.shape[1] * cells, padded, unprojected, unprojected),
+    )(*args, *before)
 
 
 def shards(
@@ -570,8 +562,12 @@
     )
     keep_x, *parts_x = split(keep_x, taken_x, along, 1)
     keep_z, *parts_z = split(keep_z, taken_z, across, 0)
-    taken_x, taken_z = lax.optimization_barrier(
-        (parts_to(parts_x, along), parts_to(parts_z, across))
+    base, mask = local_part(
+        response, low, high, orbitals, matrix, lines, bounds, group_rows, width, blk
+    )
+    padded = pad_orbitals(orbitals, blk)
+    taken_x, taken_z, base, padded = lax.optimization_barrier(
+        (parts_to(parts_x, along), parts_to(parts_z, across), base, padded)
     )
     share_x, share_z = local_call(
         functools.partial(finish_both_body, ace_scale, len(taken_x)),
@@ -582,30 +578,25 @@
         [keep_x, *taken_x, keep_z, *taken_z],
     )
 
-    pieces_x, pieces_z, bounds = lax.optimization_barrier(
-        ([share_x, *to(share_x, along)], [share_z, *to(share_z, across)], bounds)
-    )
-    base, mask = local_part(
-        response, low, high, orbitals, matrix, lines, bounds, group_rows, width, blk
+    pieces_x, pieces_z = lax.optimization_barrier(
+        ([share_x, *to(share_x, along)], [share_z, *to(share_z, across)])
     )
     block_x = place(pieces_x, along, 1)
     block_z = place(pieces_z, across, 0)
     blocks_x = [block_x, *to(block_x, across)]
-    pieces_z, base, padded = lax.optimization_barrier(
-        ([block_z, *to(block_z, along)], base, pad_orbitals(orbitals, blk))
-    )
+    pieces_z = [block_z, *to(block_z, along)]
     blocks = [*blocks_x, place(pieces_z, along, 1)]
     others = [swapped(part, count, core, 1) for part in blocks]
     sizes = (core, across, block, group_rows, blk)
     wide, keep = apply(blocks, projectors, base, padded, *sizes, False)
     others, keep = lax.optimization_barrier((others, keep))
     other_wide, part = apply(others, projectors, base, padded, *sizes, True)
-    unprojected = (wide, other_wide)
     total, part = add_up(keep, to(part, core))
     total, part = add_up(total, to(part, across))
     own = finish(total, to(part, along), window_scale)
-    weights = (own, *to(own, core))
-    return project(weights, unprojected, padded, response, mask, core, group_rows, blk)
+    (theirs,) = to(own, core)
+    outs = project(own, wide, padded, response, mask, core, blk, False, ())
+    return project(theirs, other_wide, padded, response, mask, core, blk, True, outs)
 
 
 def solution(mesh):

time: 87 us -> 85.8 us (0.986)
  waiting for transfers between devices: 40.5 us -> 39.3 us
    ppermute x27, waiting for transfers between devices: 39.6 us -> 38.4 us  [swapped(): return lax.ppermute(array, 'band', pairs)]
    pallas_call x1 -> x2, Pallas kernels: 2.43 us -> 2.4 us  [project(): pl.pallas_call(functools.partial(project_body, core, blk, other), out_sha...]
  transfers between devices with their start and end apart: 29 -> 29, of which waited for: 18 -> 18; matrix products, arithmetic and copies ran while one was open for 0% -> 0% of each run, Pallas kernels for 10% -> 11%
where the time goes in v18:
time: 85.8 us; the launch traced here: 85.7 us
  waiting for transfers between devices  39.3 us (46%)
  starting transfers between devices  32.7 us (38%)
  Pallas kernels  12.6 us (15%)
  between operations  0.92 us (1%)
    ppermute x27, waiting for transfers between devices, swapped(): return lax.ppermute(array, 'band', pairs)  38.4 us
    ppermute x27, starting transfers between devices, swapped(): return lax.ppermute(array, 'band', pairs)  29.1 us
    pallas_call x1, Pallas kernels, first_sums(): pl.pallas_call(functools.partial(first_body, core, block, tile), out_shap...  4.34 us
    pallas_call x14, Pallas kernels, local_call(): pl.pallas_call(body, out_shape=outs, in_specs=[whole() for _ in args], ou...  3.66 us
    ppermute x2, starting transfers between devices, neighbour(): lax.ppermute(array, 'band', [(i, (i + step) % count) for i in range(count)])  3.62 us
    pallas_call x2, Pallas kernels, project(): pl.pallas_call(functools.partial(project_body, core, blk, other), out_sha...  2.4 us
    pallas_call x1, Pallas kernels, local_part(): pl.pallas_call(functools.partial(local_body, depth, (group_rows, blk)), g...  2.24 us
  transfers between devices with their start and end apart: 29, of which 18 were waited for; matrix products, arithmetic and copies ran while one was open for 0% of the time, Pallas kernels for 11%

profile of v18, /device:TPU:0, one launch (start us, length us, event | category | flops | bytes accessed | tf_op | source)
XLA Modules:
  0.0 85.7 jit_solution(6973060579256500324)
XLA Ops:
  0.6 0.5 collective-permute-start.4
  1.1 4.3 %shard_map.104 = (bf16[256,1024]{1,0:T(8,128)(2,1)S(1)}, bf16[256,1024]{1,0:T(8,128)(2,1)S(1)}, f32[160,2048]{1,0:T(8,128)S(1)}, f32[96,2048]{1,0:T(8,128)S(1)}) custom-call(bf16[512,768]{1,0:T(8,128)(2,1)} %refs_3_.9, bf16[2048,768]{1,0:T(8,128)(2,1)} %refs_3_.7), custom_call_target="tpu_custom_call" | custom-call | flops 1610612736 | bytes 6291456 | tf_op jit(solution)/shard_map/pallas_call | solution.py:153
  5.5 2.6 %collective-permute-start = (bf16[256,1024]{1,0:T(8,128)(2,1)S(1)}, bf16[256,1024]{1,0:T(8,128)(2,1)S(1)}, u32[]{:S(2)}, u32[]{:S(2)}) collective-permute-start(bf16[256,1024]{1,0:T(8,128)(2,1)S(1)} %get-tuple-element.60), channel_id=1, source_target_pairs={{0,1},{1,0},{2,3},{3,2},{4,5},{5,4},{6,7},{7,6},{8,9},{9,8},{10,11... | collective-permute-start | bytes 1572872 | tf_op jit(solution)/shard_map/ppermute | solution.py:59
  8.1 0.1 collective-permute-start.1
  8.2 3.1 %collective-permute-start.7 = (bf16[512,768]{1,0:T(8,128)(2,1)S(1)}, bf16[512,768]{1,0:T(8,128)(2,1)S(1)}, u32[]{:S(2)}, u32[]{:S(2)}) collective-permute-start(bf16[512,768]{1,0:T(8,128)(2,1)S(1)} %copy-done.1), channel_id=1, source_target_pairs={{0,15},{1,0},{2,1},{3,2},{4,3},{5,4},{6,5},{7,6},{8,7},{9,8},{10,9... | collective-permute-start | bytes 2359304 | tf_op jit(solution)/shard_map/ppermute | solution.py:50
  11.3 0.1 shard_map.105
  11.4 0.0 copy-start.7
  11.5 0.0 copy-start.8
  11.5 0.0 copy-start.2
  11.5 0.1 shard_map.106
  11.6 0.7 collective-permute-start.6
  12.3 1.6 %collective-permute-start.2 = (bf16[96,512]{1,0:T(8,128)(2,1)S(1)}, bf16[96,512]{1,0:T(8,128)(2,1)S(1)}, u32[]{:S(2)}, u32[]{:S(2)}) collective-permute-start(bf16[96,512]{1,0:T(8,128)(2,1)S(1)} %get-tuple-element.65), channel_id=1, source_target_pairs={{0,4},{1,5},{2,6},{3,7},{4,0},{5,1},{6,2},{7,3},{8,12},{9,13},{10,... | collective-permute-start | bytes 294920 | tf_op jit(solution)/shard_map/ppermute | solution.py:59
  13.9 1.4 %collective-permute-start.3 = (bf16[96,512]{1,0:T(8,128)(2,1)S(1)}, bf16[96,512]{1,0:T(8,128)(2,1)S(1)}, u32[]{:S(2)}, u32[]{:S(2)}) collective-permute-start(bf16[96,512]{1,0:T(8,128)(2,1)S(1)} %get-tuple-element.66), channel_id=1, source_target_pairs={{0,8},{1,9},{2,10},{3,11},{4,12},{5,13},{6,14},{7,15},{8,0},{9,1},... | collective-permute-start | bytes 294920 | tf_op jit(solution)/shard_map/ppermute | solution.py:59
  15.3 0.9 %collective-permute-done.4.refs_1_ = bf16[512,768]{1,0:T(8,128)(2,1)S(1)} collective-permute-done((bf16[512,768]{1,0:T(8,128)(2,1)}, bf16[512,768]{1,0:T(8,128)(2,1)S(1)}, u32[]{:S(2)}, u32[]{:S(2)}) %collective-permute-start.4) | collective-permute-done | bytes 786464 | tf_op jit(solution)/shard_map/ppermute | solution.py:50
  16.2 2.2 %collective-permute-start.5 = (bf16[96,512]{1,0:T(8,128)(2,1)S(1)}, bf16[96,512]{1,0:T(8,128)(2,1)S(1)}, u32[]{:S(2)}, u32[]{:S(2)}) collective-permute-start(bf16[96,512]{1,0:T(8,128)(2,1)S(1)} %get-tuple-element.68), channel_id=1, source_target_pairs={{0,12},{1,13},{2,14},{3,15},{4,8},{5,9},{6,10},{7,11},{8,4},{9,5},... | collective-permute-start | bytes 294920 | tf_op jit(solution)/shard_map/ppermute | solution.py:59
  18.4 7.1 %collective-permute-done.2.refs_1_ = bf16[96,512]{1,0:T(8,128)(2,1)S(1)} collective-permute-done((bf16[96,512]{1,0:T(8,128)(2,1)S(1)}, bf16[96,512]{1,0:T(8,128)(2,1)S(1)}, u32[]{:S(2)}, u32[]{:S(2)}) %collective-permute-start.2) | collective-permute-done | bytes 98336 | tf_op jit(solution)/shard_map/ppermute | solution.py:59
  25.5 2.1 %collective-permute-done.3.refs_2_ = bf16[96,512]{1,0:T(8,128)(2,1)S(1)} collective-permute-done((bf16[96,512]{1,0:T(8,128)(2,1)S(1)}, bf16[96,512]{1,0:T(8,128)(2,1)S(1)}, u32[]{:S(2)}, u32[]{:S(2)}) %collective-permute-start.3) | collective-permute-done | bytes 98336 | tf_op jit(solution)/shard_map/ppermute | solution.py:59
  27.6 3.9 %collective-permute-done.6.refs_1_ = bf16[80,2048]{1,0:T(8,128)(2,1)S(1)} collective-permute-done((bf16[80,2048]{1,0:T(8,128)(2,1)S(1)}, bf16[80,2048]{1,0:T(8,128)(2,1)S(1)}, u32[]{:S(2)}, u32[]{:S(2)}) %collective-permute-start.6) | collective-permute-done | bytes 327712 | tf_op jit(solution)/shard_map/ppermute | solution.py:59
  31.5 0.0 copy-start.6
  31.5 0.1 shard_map.107
  31.6 2.3 %collective-permute-start.10 = (bf16[80,512]{1,0:T(8,128)(2,1)S(1)}, bf16[80,512]{1,0:T(8,128)(2,1)S(1)}, u32[]{:S(2)}, u32[]{:S(2)}) collective-permute-start(bf16[80,512]{1,0:T(8,128)(2,1)S(1)} %get-tuple-element.75), channel_id=1, source_target_pairs={{0,12},{1,13},{2,14},{3,15},{4,8},{5,9},{6,10},{7,11},{8,4},{9,5},... | collective-permute-start | bytes 245768 | tf_op jit(solution)/shard_map/ppermute | solution.py:59
  33.9 0.1 collective-permute-start.8
  34.0 2.0 %collective-permute-start.9 = (bf16[80,512]{1,0:T(8,128)(2,1)S(1)}, bf16[80,512]{1,0:T(8,128)(2,1)S(1)}, u32[]{:S(2)}, u32[]{:S(2)}) collective-permute-start(bf16[80,512]{1,0:T(8,128)(2,1)S(1)} %get-tuple-element.74), channel_id=1, source_target_pairs={{0,8},{1,9},{2,10},{3,11},{4,12},{5,13},{6,14},{7,15},{8,0},{9,1},... | collective-permute-start | bytes 245768 | tf_op jit(solution)/shard_map/ppermute | solution.py:59
  36.1 0.1 collective-permute-start.11
  36.2 0.1 shard_map.110.refs_5_.refs_2_
  36.3 0.0 copy-start
  36.3 2.2 %shard_map.109 = (f32[512,768]{1,0:T(8,128)S(1)}, bf16[512,256]{1,0:T(8,128)(2,1)S(1)}) custom-call(bf16[512,768]{1,0:T(8,128)(2,1)S(1)} %copy-done.1, bf16[512,768]{1,0:T(8,128)(2,1)S(1)} %collective-permute-done.4.refs_1_, bf16[512,768]{1,0:T(8,128)(2,1)S(1)} %collective-permute-done.7.refs_2_, bf16[512,768]{1,0:T(8,128)(2,1)S(1)} %copy-done.2, ...), custom_call_target="tpu_custom_call" | custom-call | flops 235929600 | bytes 4980736 | tf_op jit(solution)/shard_map/pallas_call | solution.py:333
  38.6 1.6 %collective-permute-done.11.refs_5_ = bf16[48,512]{1,0:T(8,128)(2,1)S(1)} collective-permute-done((bf16[48,512]{1,0:T(8,128)(2,1)S(1)}, bf16[48,512]{1,0:T(8,128)(2,1)S(1)}, u32[]{:S(2)}, u32[]{:S(2)}) %collective-permute-start.11) | collective-permute-done | bytes 49184 | tf_op jit(solution)/shard_map/ppermute | solution.py:59
  40.2 0.3 collective-permute-done.8.refs_1_
  40.5 0.4 collective-permute-done.9.refs_2_
  40.9 0.1 shard_map.111
  41.0 0.5 collective-permute-start.12
  41.5 2.7 %collective-permute-start.13 = (bf16[64,512]{1,0:T(8,128)(2,1)S(1)}, bf16[64,512]{1,0:T(8,128)(2,1)S(1)}, u32[]{:S(2)}, u32[]{:S(2)}) collective-permute-start(bf16[64,512]{1,0:T(8,128)(2,1)S(1)} %get-tuple-element.91.refs_0_), channel_id=1, source_target_pairs={{0,8},{1,9},{2,10},{3,11},{4,12},{5,13},{6,14},{7,15},{8,0},{9,1},... | collective-permute-start | bytes 196616 | tf_op jit(solution)/shard_map/ppermute | solution.py:59
  44.2 1.2 %collective-permute-start.14 = (bf16[64,512]{1,0:T(8,128)(2,1)S(1)}, bf16[64,512]{1,0:T(8,128)(2,1)S(1)}, u32[]{:S(2)}, u32[]{:S(2)}) collective-permute-start(bf16[64,512]{1,0:T(8,128)(2,1)S(1)} %get-tuple-element.91.refs_0_), channel_id=1, source_target_pairs={{0,12},{1,13},{2,14},{3,15},{4,8},{5,9},{6,10},{7,11},{8,4},{9,5},... | collective-permute-start | bytes 196616 | tf_op jit(solution)/shard_map/ppermute | solution.py:59
  45.4 0.4 collective-permute-start.15
  45.9 2.6 %collective-permute-done.13.refs_2_ = bf16[64,512]{1,0:T(8,128)(2,1)S(1)} collective-permute-done((bf16[64,512]{1,0:T(8,128)(2,1)S(1)}, bf16[64,512]{1,0:T(8,128)(2,1)S(1)}, u32[]{:S(2)}, u32[]{:S(2)}) %collective-permute-start.13) | collective-permute-done | bytes 65568 | tf_op jit(solution)/shard_map/ppermute | solution.py:59
  48.5 1.8 %collective-permute-done.14.refs_3_ = bf16[64,512]{1,0:T(8,128)(2,1)S(1)} collective-permute-done((bf16[64,512]{1,0:T(8,128)(2,1)S(1)}, bf16[64,512]{1,0:T(8,128)(2,1)S(1)}, u32[]{:S(2)}, u32[]{:S(2)}) %collective-permute-start.14) | collective-permute-done | bytes 65568 | tf_op jit(solution)/shard_map/ppermute | solution.py:59
  50.3 0.1 collective-permute-start.19
  50.4 2.6 %collective-permute-start.20 = (bf16[128,512]{1,0:T(8,128)(2,1)S(1)}, bf16[128,512]{1,0:T(8,128)(2,1)S(1)}, u32[]{:S(2)}, u32[]{:S(2)}) collective-permute-start(bf16[128,512]{1,0:T(8,128)(2,1)S(1)} %shard_map.113.refs_0_), channel_id=1, source_target_pairs={{0,8},{1,9},{2,10},{3,11},{4,12},{5,13},{6,14},{7,15},{8,0},{9,1},... | collective-permute-start | bytes 393224 | tf_op jit(solution)/shard_map/ppermute | solution.py:59
  52.9 1.8 %collective-permute-start.21 = (bf16[128,512]{1,0:T(8,128)(2,1)S(1)}, bf16[128,512]{1,0:T(8,128)(2,1)S(1)}, u32[]{:S(2)}, u32[]{:S(2)}) collective-permute-start(bf16[128,512]{1,0:T(8,128)(2,1)S(1)} %shard_map.113.refs_0_), channel_id=1, source_target_pairs={{0,12},{1,13},{2,14},{3,15},{4,8},{5,9},{6,10},{7,11},{8,4},{9,5},... | collective-permute-start | bytes 393224 | tf_op jit(solution)/shard_map/ppermute | solution.py:59
  54.8 0.1 collective-permute-start.17
  54.8 2.6 %collective-permute-done.19.refs_1_ = bf16[128,512]{1,0:T(8,128)(2,1)S(1)} collective-permute-done((bf16[128,512]{1,0:T(8,128)(2,1)S(1)}, bf16[128,512]{1,0:T(8,128)(2,1)S(1)}, u32[]{:S(2)}, u32[]{:S(2)}) %collective-permute-start.19) | collective-permute-done | bytes 131104 | tf_op jit(solution)/shard_map/ppermute | solution.py:59
  57.5 4.3 %collective-permute-done.20.refs_2_ = bf16[128,512]{1,0:T(8,128)(2,1)S(1)} collective-permute-done((bf16[128,512]{1,0:T(8,128)(2,1)S(1)}, bf16[128,512]{1,0:T(8,128)(2,1)S(1)}, u32[]{:S(2)}, u32[]{:S(2)}) %collective-permute-start.20) | collective-permute-done | bytes 131104 | tf_op jit(solution)/shard_map/ppermute | solution.py:59
  61.8 0.1 shard_map.114.refs_2_
  61.9 0.1 collective-permute-start.22
  62.0 0.5 collective-permute-start.16
  62.5 0.1 collective-permute-start.18
  62.5 1.5 %shard_map.115 = (f32[256,768]{1,0:T(8,128)S(1)}, f32[320,128]{1,0:T(8,128)S(1)}) custom-call(bf16[64,2048]{1,0:T(8,128)(2,1)S(1)} %shard_map.112.refs_0_, bf16[64,2048]{1,0:T(8,128)(2,1)S(1)} %collective-permute-done.17.refs_1_, bf16[128,2048]{1,0:T(8,128)(2,1)S(1)} %shard_map.114.refs_2_, bf16[2048,768]{1,0:T(8,128)(2,1)S(1)} %copy-done, ...), custom_call_target="tpu_custom_call" | custom-call | flops 905969664 | bytes 7700480 | tf_op jit(solution)/shard_map/pallas_call | solution.py:91
  64.0 0.2 collective-permute-done.16.refs_0_
  64.2 0.4 collective-permute-done.18.refs_1_
  64.6 1.5 %shard_map.116 = (f32[256,768]{1,0:T(8,128)S(1)}, bf16[320,128]{1,0:T(8,128)(2,1)S(1)}) custom-call(bf16[64,2048]{1,0:T(8,128)(2,1)S(1)} %collective-permute-done.16.refs_0_, bf16[64,2048]{1,0:T(8,128)(2,1)S(1)} %collective-permute-done.18.refs_1_, bf16[128,2048]{1,0:T(8,128)(2,1)S(1)} %collective-permute-done.22.refs_2_, bf16[2048,768]{1,0:T(8,128)(2,1)S(1)} %copy-done, ...), custom_call_target="tpu_custom_call" | custom-call | flops 905969664 | bytes 7618560 | tf_op jit(solution)/shard_map/pallas_call | solution.py:91
  66.1 0.2 collective-permute-start.23
  66.3 1.1 %collective-permute-done.23.refs_0_ = bf16[320,128]{1,0:T(8,128)(2,1)S(1)} collective-permute-done((bf16[320,128]{1,0:T(8,128)(2,1)S(1)}, bf16[320,128]{1,0:T(8,128)(2,1)S(1)}, u32[]{:S(2)}, u32[]{:S(2)}) %collective-permute-start.23) | collective-permute-done | bytes 81952 | tf_op jit(solution)/shard_map/ppermute | solution.py:59
  67.5 1.0 %collective-permute-start.24 = (bf16[320,128]{1,0:T(8,128)(2,1)S(1)}, bf16[320,128]{1,0:T(8,128)(2,1)S(1)}, u32[]{:S(2)}, u32[]{:S(2)}) collective-permute-start(bf16[320,128]{1,0:T(8,128)(2,1)S(1)} %get-tuple-element.106), channel_id=1, source_target_pairs={{0,2},{1,3},{2,0},{3,1},{4,6},{5,7},{6,4},{7,5},{8,10},{9,11},{10,... | collective-permute-start | bytes 245768 | tf_op jit(solution)/shard_map/ppermute | solution.py:59
  68.5 3.5 %collective-permute-done.24.refs_0_ = bf16[320,128]{1,0:T(8,128)(2,1)S(1)} collective-permute-done((bf16[320,128]{1,0:T(8,128)(2,1)S(1)}, bf16[320,128]{1,0:T(8,128)(2,1)S(1)}, u32[]{:S(2)}, u32[]{:S(2)}) %collective-permute-start.24) | collective-permute-done | bytes 81952 | tf_op jit(solution)/shard_map/ppermute | solution.py:59
  72.1 2.2 %collective-permute-start.25 = (bf16[320,128]{1,0:T(8,128)(2,1)S(1)}, bf16[320,128]{1,0:T(8,128)(2,1)S(1)}, u32[]{:S(2)}, u32[]{:S(2)}) collective-permute-start(bf16[320,128]{1,0:T(8,128)(2,1)S(1)} %get-tuple-element.108), channel_id=1, source_target_pairs={{0,4},{1,5},{2,6},{3,7},{4,0},{5,1},{6,2},{7,3},{8,12},{9,13},{10,... | collective-permute-start | bytes 245768 | tf_op jit(solution)/shard_map/ppermute | solution.py:59
  74.3 0.8 collective-permute-start.26
  75.1 1.7 %collective-permute-start.27 = (bf16[320,128]{1,0:T(8,128)(2,1)S(1)}, bf16[320,128]{1,0:T(8,128)(2,1)S(1)}, u32[]{:S(2)}, u32[]{:S(2)}) collective-permute-start(bf16[320,128]{1,0:T(8,128)(2,1)S(1)} %get-tuple-element.108), channel_id=1, source_target_pairs={{0,12},{1,13},{2,14},{3,15},{4,8},{5,9},{6,10},{7,11},{8,4},{9,5},... | collective-permute-start | bytes 245768 | tf_op jit(solution)/shard_map/ppermute | solution.py:59
  76.7 0.4 collective-permute-done.25.refs_0_
  77.1 6.0 %collective-permute-done.26.refs_1_ = bf16[320,128]{1,0:T(8,128)(2,1)S(1)} collective-permute-done((bf16[320,128]{1,0:T(8,128)(2,1)S(1)}, bf16[320,128]{1,0:T(8,128)(2,1)S(1)}, u32[]{:S(2)}, u32[]{:S(2)}) %collective-permute-start.26) | collective-permute-done | bytes 81952 | tf_op jit(solution)/shard_map/ppermute | solution.py:59
  83.1 0.1 collective-permute-start.28
  83.2 1.2 %shard_map.120 = (bf16[512,768]{1,0:T(8,128)(2,1)}, bf16[512,768]{1,0:T(8,128)(2,1)}) custom-call(bf16[320,128]{1,0:T(8,128)(2,1)S(1)} %shard_map.119.refs_0_, f32[256,768]{1,0:T(8,128)S(1)} %get-tuple-element.111.refs_1_, bf16[640,768]{1,0:T(8,128)(2,1)S(1)} %shard_map.110.refs_5_.refs_2_, bf16[512,768]{1,0:T(8,128)(2,1)S(1)} %copy-done.1, ...), custom_call_target="tpu_custom_call" | custom-call | flops 100663296 | bytes 2555904 | tf_op jit(solution)/shard_map/pallas_call | solution.py:500
  84.4 0.1 collective-permute-done.28.refs_0_
  84.5 1.2 %shard_map.121 = (bf16[512,768]{1,0:T(8,128)(2,1)}, bf16[512,768]{1,0:T(8,128)(2,1)}) custom-call(bf16[320,128]{1,0:T(8,128)(2,1)S(1)} %collective-permute-done.28.refs_0_, f32[256,768]{1,0:T(8,128)S(1)} %get-tuple-element.109.refs_1_, bf16[640,768]{1,0:T(8,128)(2,1)S(1)} %shard_map.110.refs_5_.refs_2_, ...), custom_call_target="tpu_custom_call", output_to_operand_aliasing={{0}: (5, {}), {1}: (6, {})} | custom-call | flops 100663296 | bytes 2555904 | tf_op jit(solution)/shard_map/pallas_call | solution.py:500
  (32 shorter events, 0.2 us)
Async XLA Ops:
  0.6 7.6 %copy-start.1 = (bf16[512,768]{1,0:T(8,128)(2,1)S(1)}, bf16[512,768]{1,0:T(8,128)(2,1)}, u32[]{:S(2)}) copy-start(bf16[512,768]{1,0:T(8,128)(2,1)} %refs_3_.9) | copy-start | bytes 2359300
  0.6 15.6 %collective-permute-start.4 = (bf16[512,768]{1,0:T(8,128)(2,1)}, bf16[512,768]{1,0:T(8,128)(2,1)S(1)}, u32[]{:S(2)}, u32[]{:S(2)}) collective-permute-start(bf16[512,768]{1,0:T(8,128)(2,1)} %refs_3_.9), channel_id=1, source_target_pairs={{0,1},{1,2},{2,3},{3,4},{4,5},{5,6},{6,7},{7,8},{8,9},{9,10},{10,1... | collective-permute-start | bytes 2359304 | tf_op jit(solution)/shard_map/ppermute | solution.py:50
  5.5 5.8 %collective-permute-start = (bf16[256,1024]{1,0:T(8,128)(2,1)S(1)}, bf16[256,1024]{1,0:T(8,128)(2,1)S(1)}, u32[]{:S(2)}, u32[]{:S(2)}) collective-permute-start(bf16[256,1024]{1,0:T(8,128)(2,1)S(1)} %get-tuple-element.60), channel_id=1, source_target_pairs={{0,1},{1,0},{2,3},{3,2},{4,5},{5,4},{6,7},{7,6},{8,9},{9,8},{10,11... | collective-permute-start | bytes 1572872 | tf_op jit(solution)/shard_map/ppermute | solution.py:59
  8.1 3.2 %collective-permute-start.1 = (bf16[256,1024]{1,0:T(8,128)(2,1)S(1)}, bf16[256,1024]{1,0:T(8,128)(2,1)S(1)}, u32[]{:S(2)}, u32[]{:S(2)}) collective-permute-start(bf16[256,1024]{1,0:T(8,128)(2,1)S(1)} %get-tuple-element.61), channel_id=1, source_target_pairs={{0,1},{1,0},{2,3},{3,2},{4,5},{5,4},{6,7},{7,6},{8,9},{9,8},{10,11... | collective-permute-start | bytes 1572872 | tf_op jit(solution)/shard_map/ppermute | solution.py:59
  8.2 19.4 %collective-permute-start.7 = (bf16[512,768]{1,0:T(8,128)(2,1)S(1)}, bf16[512,768]{1,0:T(8,128)(2,1)S(1)}, u32[]{:S(2)}, u32[]{:S(2)}) collective-permute-start(bf16[512,768]{1,0:T(8,128)(2,1)S(1)} %copy-done.1), channel_id=1, source_target_pairs={{0,15},{1,0},{2,1},{3,2},{4,3},{5,4},{6,5},{7,6},{8,7},{9,8},{10,9... | collective-permute-start | bytes 2359304 | tf_op jit(solution)/shard_map/ppermute | solution.py:50
  11.4 24.7 %copy-start.7 = (f32[768]{0:T(1024)S(1)}, f32[768]{0:T(1024)}, u32[]{:S(2)}) copy-start(f32[768]{0:T(1024)} %param.12) | copy-start | bytes 9220
  11.5 24.7 %copy-start.8 = (f32[768]{0:T(1024)S(1)}, f32[768]{0:T(1024)}, u32[]{:S(2)}) copy-start(f32[768]{0:T(1024)} %param.13) | copy-start | bytes 9220
  11.5 24.7 %copy-start.2 = (bf16[512,768]{1,0:T(8,128)(2,1)S(1)}, bf16[512,768]{1,0:T(8,128)(2,1)}, u32[]{:S(2)}) copy-start(bf16[512,768]{1,0:T(8,128)(2,1)} %o_ref.1) | copy-start | bytes 2359300
  11.6 19.8 %collective-permute-start.6 = (bf16[80,2048]{1,0:T(8,128)(2,1)S(1)}, bf16[80,2048]{1,0:T(8,128)(2,1)S(1)}, u32[]{:S(2)}, u32[]{:S(2)}) collective-permute-start(bf16[80,2048]{1,0:T(8,128)(2,1)S(1)} %get-tuple-element.69), channel_id=1, source_target_pairs={{0,2},{1,3},{2,0},{3,1},{4,6},{5,7},{6,4},{7,5},{8,10},{9,11},{10,... | collective-permute-start | bytes 983048 | tf_op jit(solution)/shard_map/ppermute | solution.py:59
  12.3 13.2 %collective-permute-start.2 = (bf16[96,512]{1,0:T(8,128)(2,1)S(1)}, bf16[96,512]{1,0:T(8,128)(2,1)S(1)}, u32[]{:S(2)}, u32[]{:S(2)}) collective-permute-start(bf16[96,512]{1,0:T(8,128)(2,1)S(1)} %get-tuple-element.65), channel_id=1, source_target_pairs={{0,4},{1,5},{2,6},{3,7},{4,0},{5,1},{6,2},{7,3},{8,12},{9,13},{10,... | collective-permute-start | bytes 294920 | tf_op jit(solution)/shard_map/ppermute | solution.py:59
  13.9 13.7 %collective-permute-start.3 = (bf16[96,512]{1,0:T(8,128)(2,1)S(1)}, bf16[96,512]{1,0:T(8,128)(2,1)S(1)}, u32[]{:S(2)}, u32[]{:S(2)}) collective-permute-start(bf16[96,512]{1,0:T(8,128)(2,1)S(1)} %get-tuple-element.66), channel_id=1, source_target_pairs={{0,8},{1,9},{2,10},{3,11},{4,12},{5,13},{6,14},{7,15},{8,0},{9,1},... | collective-permute-start | bytes 294920 | tf_op jit(solution)/shard_map/ppermute | solution.py:59
  16.2 15.3 %collective-permute-start.5 = (bf16[96,512]{1,0:T(8,128)(2,1)S(1)}, bf16[96,512]{1,0:T(8,128)(2,1)S(1)}, u32[]{:S(2)}, u32[]{:S(2)}) collective-permute-start(bf16[96,512]{1,0:T(8,128)(2,1)S(1)} %get-tuple-element.68), channel_id=1, source_target_pairs={{0,12},{1,13},{2,14},{3,15},{4,8},{5,9},{6,10},{7,11},{8,4},{9,5},... | collective-permute-start | bytes 294920 | tf_op jit(solution)/shard_map/ppermute | solution.py:59
  31.5 4.8 %copy-start.3 = (bf16[2,128,128]{2,1,0:T(8,128)(2,1)S(1)}, bf16[2,128,128]{2,1,0:T(8,128)(2,1)}, u32[]{:S(2)}) copy-start(bf16[2,128,128]{2,1,0:T(8,128)(2,1)} %constant.2.clone.refs_4_) | copy-start | bytes 196612
  31.5 4.8 %copy-start.4 = (f32[512]{0:T(512)S(1)}, f32[512]{0:T(512)}, u32[]{:S(2)}) copy-start(f32[512]{0:T(512)} %param.14) | copy-start | bytes 6148
  31.5 4.8 %copy-start.5 = (s32[512]{0:T(512)S(1)}, s32[512]{0:T(512)}, u32[]{:S(2)}) copy-start(s32[512]{0:T(512)} %param.15) | copy-start | bytes 6148
  31.5 4.8 %copy-start.6 = (s32[512]{0:T(512)S(1)}, s32[512]{0:T(512)}, u32[]{:S(2)}) copy-start(s32[512]{0:T(512)} %param.16) | copy-start | bytes 6148
  31.6 8.7 %collective-permute-start.10 = (bf16[80,512]{1,0:T(8,128)(2,1)S(1)}, bf16[80,512]{1,0:T(8,128)(2,1)S(1)}, u32[]{:S(2)}, u32[]{:S(2)}) collective-permute-start(bf16[80,512]{1,0:T(8,128)(2,1)S(1)} %get-tuple-element.75), channel_id=1, source_target_pairs={{0,12},{1,13},{2,14},{3,15},{4,8},{5,9},{6,10},{7,11},{8,4},{9,5},... | collective-permute-start | bytes 245768 | tf_op jit(solution)/shard_map/ppermute | solution.py:59
  33.9 6.6 %collective-permute-start.8 = (bf16[80,512]{1,0:T(8,128)(2,1)S(1)}, bf16[80,512]{1,0:T(8,128)(2,1)S(1)}, u32[]{:S(2)}, u32[]{:S(2)}) collective-permute-start(bf16[80,512]{1,0:T(8,128)(2,1)S(1)} %get-tuple-element.73), channel_id=1, source_target_pairs={{0,4},{1,5},{2,6},{3,7},{4,0},{5,1},{6,2},{7,3},{8,12},{9,13},{10,... | collective-permute-start | bytes 245768 | tf_op jit(solution)/shard_map/ppermute | solution.py:59
  34.0 6.9 %collective-permute-start.9 = (bf16[80,512]{1,0:T(8,128)(2,1)S(1)}, bf16[80,512]{1,0:T(8,128)(2,1)S(1)}, u32[]{:S(2)}, u32[]{:S(2)}) collective-permute-start(bf16[80,512]{1,0:T(8,128)(2,1)S(1)} %get-tuple-element.74), channel_id=1, source_target_pairs={{0,8},{1,9},{2,10},{3,11},{4,12},{5,13},{6,14},{7,15},{8,0},{9,1},... | collective-permute-start | bytes 245768 | tf_op jit(solution)/shard_map/ppermute | solution.py:59
  36.1 4.2 %collective-permute-start.11 = (bf16[48,512]{1,0:T(8,128)(2,1)S(1)}, bf16[48,512]{1,0:T(8,128)(2,1)S(1)}, u32[]{:S(2)}, u32[]{:S(2)}) collective-permute-start(bf16[48,512]{1,0:T(8,128)(2,1)S(1)} %get-tuple-element.80), channel_id=1, source_target_pairs={{0,2},{1,3},{2,0},{3,1},{4,6},{5,7},{6,4},{7,5},{8,10},{9,11},{10,... | collective-permute-start | bytes 147464 | tf_op jit(solution)/shard_map/ppermute | solution.py:59
  36.3 26.2 %copy-start = (bf16[2048,768]{1,0:T(8,128)(2,1)S(1)}, bf16[2048,768]{1,0:T(8,128)(2,1)}, u32[]{:S(2)}) copy-start(bf16[2048,768]{1,0:T(8,128)(2,1)} %refs_3_.7) | copy-start | bytes 9437188
  41.0 4.9 %collective-permute-start.12 = (bf16[64,512]{1,0:T(8,128)(2,1)S(1)}, bf16[64,512]{1,0:T(8,128)(2,1)S(1)}, u32[]{:S(2)}, u32[]{:S(2)}) collective-permute-start(bf16[64,512]{1,0:T(8,128)(2,1)S(1)} %get-tuple-element.91.refs_0_), channel_id=1, source_target_pairs={{0,4},{1,5},{2,6},{3,7},{4,0},{5,1},{6,2},{7,3},{8,12},{9,13},{10,... | collective-permute-start | bytes 196616 | tf_op jit(solution)/shard_map/ppermute | solution.py:59
  41.5 7.0 %collective-permute-start.13 = (bf16[64,512]{1,0:T(8,128)(2,1)S(1)}, bf16[64,512]{1,0:T(8,128)(2,1)S(1)}, u32[]{:S(2)}, u32[]{:S(2)}) collective-permute-start(bf16[64,512]{1,0:T(8,128)(2,1)S(1)} %get-tuple-element.91.refs_0_), channel_id=1, source_target_pairs={{0,8},{1,9},{2,10},{3,11},{4,12},{5,13},{6,14},{7,15},{8,0},{9,1},... | collective-permute-start | bytes 196616 | tf_op jit(solution)/shard_map/ppermute | solution.py:59
  44.2 6.1 %collective-permute-start.14 = (bf16[64,512]{1,0:T(8,128)(2,1)S(1)}, bf16[64,512]{1,0:T(8,128)(2,1)S(1)}, u32[]{:S(2)}, u32[]{:S(2)}) collective-permute-start(bf16[64,512]{1,0:T(8,128)(2,1)S(1)} %get-tuple-element.91.refs_0_), channel_id=1, source_target_pairs={{0,12},{1,13},{2,14},{3,15},{4,8},{5,9},{6,10},{7,11},{8,4},{9,5},... | collective-permute-start | bytes 196616 | tf_op jit(solution)/shard_map/ppermute | solution.py:59
  45.4 4.8 %collective-permute-start.15 = (bf16[64,512]{1,0:T(8,128)(2,1)S(1)}, bf16[64,512]{1,0:T(8,128)(2,1)S(1)}, u32[]{:S(2)}, u32[]{:S(2)}) collective-permute-start(bf16[64,512]{1,0:T(8,128)(2,1)S(1)} %get-tuple-element.95.refs_0_), channel_id=1, source_target_pairs={{0,2},{1,3},{2,0},{3,1},{4,6},{5,7},{6,4},{7,5},{8,10},{9,11},{10,... | collective-permute-start | bytes 196616 | tf_op jit(solution)/shard_map/ppermute | solution.py:59
  50.3 7.2 %collective-permute-start.19 = (bf16[128,512]{1,0:T(8,128)(2,1)S(1)}, bf16[128,512]{1,0:T(8,128)(2,1)S(1)}, u32[]{:S(2)}, u32[]{:S(2)}) collective-permute-start(bf16[128,512]{1,0:T(8,128)(2,1)S(1)} %shard_map.113.refs_0_), channel_id=1, source_target_pairs={{0,4},{1,5},{2,6},{3,7},{4,0},{5,1},{6,2},{7,3},{8,12},{9,13},{10,... | collective-permute-start | bytes 393224 | tf_op jit(solution)/shard_map/ppermute | solution.py:59
  50.4 11.5 %collective-permute-start.20 = (bf16[128,512]{1,0:T(8,128)(2,1)S(1)}, bf16[128,512]{1,0:T(8,128)(2,1)S(1)}, u32[]{:S(2)}, u32[]{:S(2)}) collective-permute-start(bf16[128,512]{1,0:T(8,128)(2,1)S(1)} %shard_map.113.refs_0_), channel_id=1, source_target_pairs={{0,8},{1,9},{2,10},{3,11},{4,12},{5,13},{6,14},{7,15},{8,0},{9,1},... | collective-permute-start | bytes 393224 | tf_op jit(solution)/shard_map/ppermute | solution.py:59
  52.9 8.9 %collective-permute-start.21 = (bf16[128,512]{1,0:T(8,128)(2,1)S(1)}, bf16[128,512]{1,0:T(8,128)(2,1)S(1)}, u32[]{:S(2)}, u32[]{:S(2)}) collective-permute-start(bf16[128,512]{1,0:T(8,128)(2,1)S(1)} %shard_map.113.refs_0_), channel_id=1, source_target_pairs={{0,12},{1,13},{2,14},{3,15},{4,8},{5,9},{6,10},{7,11},{8,4},{9,5},... | collective-permute-start | bytes 393224 | tf_op jit(solution)/shard_map/ppermute | solution.py:59
  54.8 7.7 %collective-permute-start.17 = (bf16[64,2048]{1,0:T(8,128)(2,1)S(1)}, bf16[64,2048]{1,0:T(8,128)(2,1)S(1)}, u32[]{:S(2)}, u32[]{:S(2)}) collective-permute-start(bf16[64,2048]{1,0:T(8,128)(2,1)S(1)} %shard_map.112.refs_0_), channel_id=1, source_target_pairs={{0,2},{1,3},{2,0},{3,1},{4,6},{5,7},{6,4},{7,5},{8,10},{9,11},{10,... | collective-permute-start | bytes 786440 | tf_op jit(solution)/shard_map/ppermute | solution.py:59
  61.9 2.7 %collective-permute-start.22 = (bf16[128,2048]{1,0:T(8,128)(2,1)S(1)}, bf16[128,2048]{1,0:T(8,128)(2,1)S(1)}, u32[]{:S(2)}, u32[]{:S(2)}) collective-permute-start(bf16[128,2048]{1,0:T(8,128)(2,1)S(1)} %shard_map.114.refs_2_), channel_id=1, source_target_pairs={{0,1},{1,0},{2,3},{3,2},{4,5},{5,4},{6,7},{7,6},{8,9},{9,8},{10,11... | collective-permute-start | bytes 1572872 | tf_op jit(solution)/shard_map/ppermute | solution.py:59
  62.0 2.3 %collective-permute-start.16 = (bf16[64,2048]{1,0:T(8,128)(2,1)S(1)}, bf16[64,2048]{1,0:T(8,128)(2,1)S(1)}, u32[]{:S(2)}, u32[]{:S(2)}) collective-permute-start(bf16[64,2048]{1,0:T(8,128)(2,1)S(1)} %shard_map.112.refs_0_), channel_id=1, source_target_pairs={{0,1},{1,0},{2,3},{3,2},{4,5},{5,4},{6,7},{7,6},{8,9},{9,8},{10,11... | collective-permute-start | bytes 786440 | tf_op jit(solution)/shard_map/ppermute | solution.py:59
  62.5 2.1 %collective-permute-start.18 = (bf16[64,2048]{1,0:T(8,128)(2,1)S(1)}, bf16[64,2048]{1,0:T(8,128)(2,1)S(1)}, u32[]{:S(2)}, u32[]{:S(2)}) collective-permute-start(bf16[64,2048]{1,0:T(8,128)(2,1)S(1)} %collective-permute-done.17.refs_1_), channel_id=1, source_target_pairs={{0,1},{1,0},{2,3},{3,2},{4,5},{5,4},{6,7},{7,6},{8,9},{9,8},{10,11... | collective-permute-start | bytes 786440 | tf_op jit(solution)/shard_map/ppermute | solution.py:59
  66.1 1.3 %collective-permute-start.23 = (bf16[320,128]{1,0:T(8,128)(2,1)S(1)}, bf16[320,128]{1,0:T(8,128)(2,1)S(1)}, u32[]{:S(2)}, u32[]{:S(2)}) collective-permute-start(bf16[320,128]{1,0:T(8,128)(2,1)S(1)} %get-tuple-element.104), channel_id=1, source_target_pairs={{0,1},{1,0},{2,3},{3,2},{4,5},{5,4},{6,7},{7,6},{8,9},{9,8},{10,11... | collective-permute-start | bytes 245768 | tf_op jit(solution)/shard_map/ppermute | solution.py:59
  67.5 4.6 %collective-permute-start.24 = (bf16[320,128]{1,0:T(8,128)(2,1)S(1)}, bf16[320,128]{1,0:T(8,128)(2,1)S(1)}, u32[]{:S(2)}, u32[]{:S(2)}) collective-permute-start(bf16[320,128]{1,0:T(8,128)(2,1)S(1)} %get-tuple-element.106), channel_id=1, source_target_pairs={{0,2},{1,3},{2,0},{3,1},{4,6},{5,7},{6,4},{7,5},{8,10},{9,11},{10,... | collective-permute-start | bytes 245768 | tf_op jit(solution)/shard_map/ppermute | solution.py:59
  72.1 5.0 %collective-permute-start.25 = (bf16[320,128]{1,0:T(8,128)(2,1)S(1)}, bf16[320,128]{1,0:T(8,128)(2,1)S(1)}, u32[]{:S(2)}, u32[]{:S(2)}) collective-permute-start(bf16[320,128]{1,0:T(8,128)(2,1)S(1)} %get-tuple-element.108), channel_id=1, source_target_pairs={{0,4},{1,5},{2,6},{3,7},{4,0},{5,1},{6,2},{7,3},{8,12},{9,13},{10,... | collective-permute-start | bytes 245768 | tf_op jit(solution)/shard_map/ppermute | solution.py:59
  74.3 8.8 %collective-permute-start.26 = (bf16[320,128]{1,0:T(8,128)(2,1)S(1)}, bf16[320,128]{1,0:T(8,128)(2,1)S(1)}, u32[]{:S(2)}, u32[]{:S(2)}) collective-permute-start(bf16[320,128]{1,0:T(8,128)(2,1)S(1)} %get-tuple-element.108), channel_id=1, source_target_pairs={{0,8},{1,9},{2,10},{3,11},{4,12},{5,13},{6,14},{7,15},{8,0},{9,1},... | collective-permute-start | bytes 245768 | tf_op jit(solution)/shard_map/ppermute | solution.py:59
  75.1 8.0 %collective-permute-start.27 = (bf16[320,128]{1,0:T(8,128)(2,1)S(1)}, bf16[320,128]{1,0:T(8,128)(2,1)S(1)}, u32[]{:S(2)}, u32[]{:S(2)}) collective-permute-start(bf16[320,128]{1,0:T(8,128)(2,1)S(1)} %get-tuple-element.108), channel_id=1, source_target_pairs={{0,12},{1,13},{2,14},{3,15},{4,8},{5,9},{6,10},{7,11},{8,4},{9,5},... | collective-permute-start | bytes 245768 | tf_op jit(solution)/shard_map/ppermute | solution.py:59
  83.1 1.3 %collective-permute-start.28 = (bf16[320,128]{1,0:T(8,128)(2,1)S(1)}, bf16[320,128]{1,0:T(8,128)(2,1)S(1)}, u32[]{:S(2)}, u32[]{:S(2)}) collective-permute-start(bf16[320,128]{1,0:T(8,128)(2,1)S(1)} %shard_map.119.refs_0_), channel_id=1, source_target_pairs={{0,1},{1,0},{2,3},{3,2},{4,5},{5,4},{6,7},{7,6},{8,9},{9,8},{10,11... | collective-permute-start | bytes 245768 | tf_op jit(solution)/shard_map/ppermute | solution.py:59

commit v19 on v18

--- a/solution.py
+++ b/solution.py
@@ -29,7 +29,7 @@
 MIB = 1024 * 1024
 VMEM_BYTES = 24 * MIB
 REDUCE_SHARE = 0.625
-GATHER_SHARE = 0.5
+GATHER_SHARE = 0.625
 BF16 = jnp.bfloat16
 F32 = jnp.float32
 NT = (((1,), (1,)), ((), ()))
@@ -270,11 +270,11 @@
     me = position(level)
     width = parts[0].shape[along]
     for step, ref in enumerate(parts):
-        at = pl.multiple_of((me ^ step) * width, width)
+        at = (me ^ step) * width
         if along == 0:
-            out_ref[pl.ds(at, width), :] = ref[...]
+            out_ref[pl.ds(pl.multiple_of(at, 16), width), :] = ref[...]
         else:
-            out_ref[:, pl.ds(at, width)] = ref[...]
+            out_ref[:, pl.ds(pl.multiple_of(at, 128), width)] = ref[...]
 
 
 def place(parts, level, along):

time: 85.8 us -> 85.6 us (level)
  no operation moved by 1% of the time
where the time goes in v19:
time: 85.6 us; the launch traced here: 85.4 us
  waiting for transfers between devices  39.4 us (46%)
  starting transfers between devices  32.5 us (38%)
  Pallas kernels  12.6 us (15%)
  between operations  0.9 us (1%)
    ppermute x27, waiting for transfers between devices, swapped(): return lax.ppermute(array, 'band', pairs)  38.4 us
    ppermute x27, starting transfers between devices, swapped(): return lax.ppermute(array, 'band', pairs)  28.8 us
    pallas_call x1, Pallas kernels, first_sums(): pl.pallas_call(functools.partial(first_body, core, block, tile), out_shap...  4.34 us
    pallas_call x14, Pallas kernels, local_call(): pl.pallas_call(body, out_shape=outs, in_specs=[whole() for _ in args], ou...  3.66 us
    ppermute x2, starting transfers between devices, neighbour(): lax.ppermute(array, 'band', [(i, (i + step) % count) for i in range(count)])  3.62 us
    pallas_call x2, Pallas kernels, project(): pl.pallas_call(functools.partial(project_body, core, blk, other), out_sha...  2.4 us
    pallas_call x1, Pallas kernels, local_part(): pl.pallas_call(functools.partial(local_body, depth, (group_rows, blk)), g...  2.24 us
  transfers between devices with their start and end apart: 29, of which 18 were waited for; matrix products, arithmetic and copies ran while one was open for 0% of the time, Pallas kernels for 11%

profile of v19, /device:TPU:0, one launch (start us, length us, event | category | flops | bytes accessed | tf_op | source)
XLA Modules:
  0.0 85.4 jit_solution(10205849646754096156)
XLA Ops:
  0.6 0.5 collective-permute-start.4
  1.1 4.3 %shard_map.104 = (bf16[256,1024]{1,0:T(8,128)(2,1)S(1)}, bf16[256,1024]{1,0:T(8,128)(2,1)S(1)}, f32[160,2048]{1,0:T(8,128)S(1)}, f32[96,2048]{1,0:T(8,128)S(1)}) custom-call(bf16[512,768]{1,0:T(8,128)(2,1)} %refs_3_.9, bf16[2048,768]{1,0:T(8,128)(2,1)} %refs_3_.7), custom_call_target="tpu_custom_call" | custom-call | flops 1610612736 | bytes 6291456 | tf_op jit(solution)/shard_map/pallas_call | solution.py:153
  5.5 2.6 %collective-permute-start = (bf16[256,1024]{1,0:T(8,128)(2,1)S(1)}, bf16[256,1024]{1,0:T(8,128)(2,1)S(1)}, u32[]{:S(2)}, u32[]{:S(2)}) collective-permute-start(bf16[256,1024]{1,0:T(8,128)(2,1)S(1)} %get-tuple-element.60), channel_id=1, source_target_pairs={{0,1},{1,0},{2,3},{3,2},{4,5},{5,4},{6,7},{7,6},{8,9},{9,8},{10,11... | collective-permute-start | bytes 1572872 | tf_op jit(solution)/shard_map/ppermute | solution.py:59
  8.1 0.1 collective-permute-start.1
  8.2 3.1 %collective-permute-start.7 = (bf16[512,768]{1,0:T(8,128)(2,1)S(1)}, bf16[512,768]{1,0:T(8,128)(2,1)S(1)}, u32[]{:S(2)}, u32[]{:S(2)}) collective-permute-start(bf16[512,768]{1,0:T(8,128)(2,1)S(1)} %copy-done.1), channel_id=1, source_target_pairs={{0,15},{1,0},{2,1},{3,2},{4,3},{5,4},{6,5},{7,6},{8,7},{9,8},{10,9... | collective-permute-start | bytes 2359304 | tf_op jit(solution)/shard_map/ppermute | solution.py:50
  11.3 0.1 shard_map.105
  11.4 0.0 copy-start.7
  11.5 0.0 copy-start.8
  11.5 0.0 copy-start.2
  11.5 0.1 shard_map.106
  11.6 0.7 collective-permute-start.6
  12.3 1.6 %collective-permute-start.2 = (bf16[96,512]{1,0:T(8,128)(2,1)S(1)}, bf16[96,512]{1,0:T(8,128)(2,1)S(1)}, u32[]{:S(2)}, u32[]{:S(2)}) collective-permute-start(bf16[96,512]{1,0:T(8,128)(2,1)S(1)} %get-tuple-element.65), channel_id=1, source_target_pairs={{0,4},{1,5},{2,6},{3,7},{4,0},{5,1},{6,2},{7,3},{8,12},{9,13},{10,... | collective-permute-start | bytes 294920 | tf_op jit(solution)/shard_map/ppermute | solution.py:59
  13.9 1.4 %collective-permute-start.3 = (bf16[96,512]{1,0:T(8,128)(2,1)S(1)}, bf16[96,512]{1,0:T(8,128)(2,1)S(1)}, u32[]{:S(2)}, u32[]{:S(2)}) collective-permute-start(bf16[96,512]{1,0:T(8,128)(2,1)S(1)} %get-tuple-element.66), channel_id=1, source_target_pairs={{0,8},{1,9},{2,10},{3,11},{4,12},{5,13},{6,14},{7,15},{8,0},{9,1},... | collective-permute-start | bytes 294920 | tf_op jit(solution)/shard_map/ppermute | solution.py:59
  15.3 0.9 %collective-permute-done.4.refs_1_ = bf16[512,768]{1,0:T(8,128)(2,1)S(1)} collective-permute-done((bf16[512,768]{1,0:T(8,128)(2,1)}, bf16[512,768]{1,0:T(8,128)(2,1)S(1)}, u32[]{:S(2)}, u32[]{:S(2)}) %collective-permute-start.4) | collective-permute-done | bytes 786464 | tf_op jit(solution)/shard_map/ppermute | solution.py:50
  16.2 2.2 %collective-permute-start.5 = (bf16[96,512]{1,0:T(8,128)(2,1)S(1)}, bf16[96,512]{1,0:T(8,128)(2,1)S(1)}, u32[]{:S(2)}, u32[]{:S(2)}) collective-permute-start(bf16[96,512]{1,0:T(8,128)(2,1)S(1)} %get-tuple-element.68), channel_id=1, source_target_pairs={{0,12},{1,13},{2,14},{3,15},{4,8},{5,9},{6,10},{7,11},{8,4},{9,5},... | collective-permute-start | bytes 294920 | tf_op jit(solution)/shard_map/ppermute | solution.py:59
  18.4 7.1 %collective-permute-done.2.refs_1_ = bf16[96,512]{1,0:T(8,128)(2,1)S(1)} collective-permute-done((bf16[96,512]{1,0:T(8,128)(2,1)S(1)}, bf16[96,512]{1,0:T(8,128)(2,1)S(1)}, u32[]{:S(2)}, u32[]{:S(2)}) %collective-permute-start.2) | collective-permute-done | bytes 98336 | tf_op jit(solution)/shard_map/ppermute | solution.py:59
  25.5 2.1 %collective-permute-done.3.refs_2_ = bf16[96,512]{1,0:T(8,128)(2,1)S(1)} collective-permute-done((bf16[96,512]{1,0:T(8,128)(2,1)S(1)}, bf16[96,512]{1,0:T(8,128)(2,1)S(1)}, u32[]{:S(2)}, u32[]{:S(2)}) %collective-permute-start.3) | collective-permute-done | bytes 98336 | tf_op jit(solution)/shard_map/ppermute | solution.py:59
  27.6 3.9 %collective-permute-done.6.refs_1_ = bf16[80,2048]{1,0:T(8,128)(2,1)S(1)} collective-permute-done((bf16[80,2048]{1,0:T(8,128)(2,1)S(1)}, bf16[80,2048]{1,0:T(8,128)(2,1)S(1)}, u32[]{:S(2)}, u32[]{:S(2)}) %collective-permute-start.6) | collective-permute-done | bytes 327712 | tf_op jit(solution)/shard_map/ppermute | solution.py:59
  31.5 0.0 copy-start.6
  31.5 0.1 shard_map.107
  31.6 2.3 %collective-permute-start.10 = (bf16[80,512]{1,0:T(8,128)(2,1)S(1)}, bf16[80,512]{1,0:T(8,128)(2,1)S(1)}, u32[]{:S(2)}, u32[]{:S(2)}) collective-permute-start(bf16[80,512]{1,0:T(8,128)(2,1)S(1)} %get-tuple-element.75), channel_id=1, source_target_pairs={{0,12},{1,13},{2,14},{3,15},{4,8},{5,9},{6,10},{7,11},{8,4},{9,5},... | collective-permute-start | bytes 245768 | tf_op jit(solution)/shard_map/ppermute | solution.py:59
  33.9 0.1 collective-permute-start.8
  34.0 2.0 %collective-permute-start.9 = (bf16[80,512]{1,0:T(8,128)(2,1)S(1)}, bf16[80,512]{1,0:T(8,128)(2,1)S(1)}, u32[]{:S(2)}, u32[]{:S(2)}) collective-permute-start(bf16[80,512]{1,0:T(8,128)(2,1)S(1)} %get-tuple-element.74), channel_id=1, source_target_pairs={{0,8},{1,9},{2,10},{3,11},{4,12},{5,13},{6,14},{7,15},{8,0},{9,1},... | collective-permute-start | bytes 245768 | tf_op jit(solution)/shard_map/ppermute | solution.py:59
  36.1 0.1 collective-permute-start.11
  36.2 0.1 shard_map.110.refs_5_.refs_2_
  36.3 0.0 copy-start
  36.3 2.2 %shard_map.109 = (f32[512,768]{1,0:T(8,128)S(1)}, bf16[512,256]{1,0:T(8,128)(2,1)S(1)}) custom-call(bf16[512,768]{1,0:T(8,128)(2,1)S(1)} %copy-done.1, bf16[512,768]{1,0:T(8,128)(2,1)S(1)} %collective-permute-done.4.refs_1_, bf16[512,768]{1,0:T(8,128)(2,1)S(1)} %collective-permute-done.7.refs_2_, bf16[512,768]{1,0:T(8,128)(2,1)S(1)} %copy-done.2, ...), custom_call_target="tpu_custom_call" | custom-call | flops 235929600 | bytes 4980736 | tf_op jit(solution)/shard_map/pallas_call | solution.py:333
  38.6 1.6 %collective-permute-done.11.refs_5_ = bf16[48,512]{1,0:T(8,128)(2,1)S(1)} collective-permute-done((bf16[48,512]{1,0:T(8,128)(2,1)S(1)}, bf16[48,512]{1,0:T(8,128)(2,1)S(1)}, u32[]{:S(2)}, u32[]{:S(2)}) %collective-permute-start.11) | collective-permute-done | bytes 49184 | tf_op jit(solution)/shard_map/ppermute | solution.py:59
  40.2 0.3 collective-permute-done.8.refs_1_
  40.5 0.4 collective-permute-done.9.refs_2_
  40.9 0.1 shard_map.111
  41.0 0.5 collective-permute-start.12
  41.5 2.7 %collective-permute-start.13 = (bf16[80,512]{1,0:T(8,128)(2,1)S(1)}, bf16[80,512]{1,0:T(8,128)(2,1)S(1)}, u32[]{:S(2)}, u32[]{:S(2)}) collective-permute-start(bf16[80,512]{1,0:T(8,128)(2,1)S(1)} %get-tuple-element.91.refs_0_), channel_id=1, source_target_pairs={{0,8},{1,9},{2,10},{3,11},{4,12},{5,13},{6,14},{7,15},{8,0},{9,1},... | collective-permute-start | bytes 245768 | tf_op jit(solution)/shard_map/ppermute | solution.py:59
  44.2 1.2 %collective-permute-start.14 = (bf16[80,512]{1,0:T(8,128)(2,1)S(1)}, bf16[80,512]{1,0:T(8,128)(2,1)S(1)}, u32[]{:S(2)}, u32[]{:S(2)}) collective-permute-start(bf16[80,512]{1,0:T(8,128)(2,1)S(1)} %get-tuple-element.91.refs_0_), channel_id=1, source_target_pairs={{0,12},{1,13},{2,14},{3,15},{4,8},{5,9},{6,10},{7,11},{8,4},{9,5},... | collective-permute-start | bytes 245768 | tf_op jit(solution)/shard_map/ppermute | solution.py:59
  45.4 0.4 collective-permute-start.15
  45.9 3.6 %collective-permute-done.15.refs_1_ = bf16[48,512]{1,0:T(8,128)(2,1)S(1)} collective-permute-done((bf16[48,512]{1,0:T(8,128)(2,1)S(1)}, bf16[48,512]{1,0:T(8,128)(2,1)S(1)}, u32[]{:S(2)}, u32[]{:S(2)}) %collective-permute-start.15) | collective-permute-done | bytes 49184 | tf_op jit(solution)/shard_map/ppermute | solution.py:59
  49.5 0.0 collective-permute-done.13.refs_2_
  49.5 1.0 %collective-permute-done.14.refs_3_ = bf16[80,512]{1,0:T(8,128)(2,1)S(1)} collective-permute-done((bf16[80,512]{1,0:T(8,128)(2,1)S(1)}, bf16[80,512]{1,0:T(8,128)(2,1)S(1)}, u32[]{:S(2)}, u32[]{:S(2)}) %collective-permute-start.14) | collective-permute-done | bytes 81952 | tf_op jit(solution)/shard_map/ppermute | solution.py:59
  50.6 0.5 collective-permute-start.17
  51.1 1.5 %collective-permute-start.19 = (bf16[96,512]{1,0:T(8,128)(2,1)S(1)}, bf16[96,512]{1,0:T(8,128)(2,1)S(1)}, u32[]{:S(2)}, u32[]{:S(2)}) collective-permute-start(bf16[96,512]{1,0:T(8,128)(2,1)S(1)} %shard_map.113.refs_0_), channel_id=1, source_target_pairs={{0,4},{1,5},{2,6},{3,7},{4,0},{5,1},{6,2},{7,3},{8,12},{9,13},{10,... | collective-permute-start | bytes 294920 | tf_op jit(solution)/shard_map/ppermute | solution.py:59
  52.6 1.6 %collective-permute-start.20 = (bf16[96,512]{1,0:T(8,128)(2,1)S(1)}, bf16[96,512]{1,0:T(8,128)(2,1)S(1)}, u32[]{:S(2)}, u32[]{:S(2)}) collective-permute-start(bf16[96,512]{1,0:T(8,128)(2,1)S(1)} %shard_map.113.refs_0_), channel_id=1, source_target_pairs={{0,8},{1,9},{2,10},{3,11},{4,12},{5,13},{6,14},{7,15},{8,0},{9,1},... | collective-permute-start | bytes 294920 | tf_op jit(solution)/shard_map/ppermute | solution.py:59
  54.2 1.3 %collective-permute-start.21 = (bf16[96,512]{1,0:T(8,128)(2,1)S(1)}, bf16[96,512]{1,0:T(8,128)(2,1)S(1)}, u32[]{:S(2)}, u32[]{:S(2)}) collective-permute-start(bf16[96,512]{1,0:T(8,128)(2,1)S(1)} %shard_map.113.refs_0_), channel_id=1, source_target_pairs={{0,12},{1,13},{2,14},{3,15},{4,8},{5,9},{6,10},{7,11},{8,4},{9,5},... | collective-permute-start | bytes 294920 | tf_op jit(solution)/shard_map/ppermute | solution.py:59
  55.5 1.3 %collective-permute-done.19.refs_1_ = bf16[96,512]{1,0:T(8,128)(2,1)S(1)} collective-permute-done((bf16[96,512]{1,0:T(8,128)(2,1)S(1)}, bf16[96,512]{1,0:T(8,128)(2,1)S(1)}, u32[]{:S(2)}, u32[]{:S(2)}) %collective-permute-start.19) | collective-permute-done | bytes 98336 | tf_op jit(solution)/shard_map/ppermute | solution.py:59
  56.8 5.4 %collective-permute-done.20.refs_2_ = bf16[96,512]{1,0:T(8,128)(2,1)S(1)} collective-permute-done((bf16[96,512]{1,0:T(8,128)(2,1)S(1)}, bf16[96,512]{1,0:T(8,128)(2,1)S(1)}, u32[]{:S(2)}, u32[]{:S(2)}) %collective-permute-start.20) | collective-permute-done | bytes 98336 | tf_op jit(solution)/shard_map/ppermute | solution.py:59
  62.3 0.1 collective-permute-start.22
  62.3 0.5 collective-permute-start.16
  62.8 0.1 collective-permute-start.18
  62.9 1.5 %shard_map.115 = (f32[256,768]{1,0:T(8,128)S(1)}, f32[320,128]{1,0:T(8,128)S(1)}) custom-call(bf16[80,2048]{1,0:T(8,128)(2,1)S(1)} %shard_map.112.refs_0_, bf16[80,2048]{1,0:T(8,128)(2,1)S(1)} %collective-permute-done.17.refs_1_, bf16[96,2048]{1,0:T(8,128)(2,1)S(1)} %shard_map.114.refs_2_, bf16[2048,768]{1,0:T(8,128)(2,1)S(1)} %copy-done, ...), custom_call_target="tpu_custom_call" | custom-call | flops 905969664 | bytes 7700480 | tf_op jit(solution)/shard_map/pallas_call | solution.py:91
  64.4 0.1 collective-permute-done.16.refs_0_
  64.5 0.5 collective-permute-done.18.refs_1_
  65.0 1.5 %shard_map.116 = (f32[256,768]{1,0:T(8,128)S(1)}, bf16[320,128]{1,0:T(8,128)(2,1)S(1)}) custom-call(bf16[80,2048]{1,0:T(8,128)(2,1)S(1)} %collective-permute-done.16.refs_0_, bf16[80,2048]{1,0:T(8,128)(2,1)S(1)} %collective-permute-done.18.refs_1_, bf16[96,2048]{1,0:T(8,128)(2,1)S(1)} %collective-permute-done.22.refs_2_, bf16[2048,768]{1,0:T(8,128)(2,1)S(1)} %copy-done, ...), custom_call_target="tpu_custom_call" | custom-call | flops 905969664 | bytes 7618560 | tf_op jit(solution)/shard_map/pallas_call | solution.py:91
  66.5 0.2 collective-permute-start.23
  66.7 1.1 %collective-permute-done.23.refs_0_ = bf16[320,128]{1,0:T(8,128)(2,1)S(1)} collective-permute-done((bf16[320,128]{1,0:T(8,128)(2,1)S(1)}, bf16[320,128]{1,0:T(8,128)(2,1)S(1)}, u32[]{:S(2)}, u32[]{:S(2)}) %collective-permute-start.23) | collective-permute-done | bytes 81952 | tf_op jit(solution)/shard_map/ppermute | solution.py:59
  67.9 0.6 collective-permute-start.24
  68.4 4.0 %collective-permute-done.24.refs_0_ = bf16[320,128]{1,0:T(8,128)(2,1)S(1)} collective-permute-done((bf16[320,128]{1,0:T(8,128)(2,1)S(1)}, bf16[320,128]{1,0:T(8,128)(2,1)S(1)}, u32[]{:S(2)}, u32[]{:S(2)}) %collective-permute-start.24) | collective-permute-done | bytes 81952 | tf_op jit(solution)/shard_map/ppermute | solution.py:59
  72.5 1.7 %collective-permute-start.25 = (bf16[320,128]{1,0:T(8,128)(2,1)S(1)}, bf16[320,128]{1,0:T(8,128)(2,1)S(1)}, u32[]{:S(2)}, u32[]{:S(2)}) collective-permute-start(bf16[320,128]{1,0:T(8,128)(2,1)S(1)} %get-tuple-element.108), channel_id=1, source_target_pairs={{0,4},{1,5},{2,6},{3,7},{4,0},{5,1},{6,2},{7,3},{8,12},{9,13},{10,... | collective-permute-start | bytes 245768 | tf_op jit(solution)/shard_map/ppermute | solution.py:59
  74.1 1.3 %collective-permute-start.26 = (bf16[320,128]{1,0:T(8,128)(2,1)S(1)}, bf16[320,128]{1,0:T(8,128)(2,1)S(1)}, u32[]{:S(2)}, u32[]{:S(2)}) collective-permute-start(bf16[320,128]{1,0:T(8,128)(2,1)S(1)} %get-tuple-element.108), channel_id=1, source_target_pairs={{0,8},{1,9},{2,10},{3,11},{4,12},{5,13},{6,14},{7,15},{8,0},{9,1},... | collective-permute-start | bytes 245768 | tf_op jit(solution)/shard_map/ppermute | solution.py:59
  75.4 1.5 %collective-permute-start.27 = (bf16[320,128]{1,0:T(8,128)(2,1)S(1)}, bf16[320,128]{1,0:T(8,128)(2,1)S(1)}, u32[]{:S(2)}, u32[]{:S(2)}) collective-permute-start(bf16[320,128]{1,0:T(8,128)(2,1)S(1)} %get-tuple-element.108), channel_id=1, source_target_pairs={{0,12},{1,13},{2,14},{3,15},{4,8},{5,9},{6,10},{7,11},{8,4},{9,5},... | collective-permute-start | bytes 245768 | tf_op jit(solution)/shard_map/ppermute | solution.py:59
  76.9 0.8 collective-permute-done.25.refs_0_
  77.7 5.1 %collective-permute-done.26.refs_1_ = bf16[320,128]{1,0:T(8,128)(2,1)S(1)} collective-permute-done((bf16[320,128]{1,0:T(8,128)(2,1)S(1)}, bf16[320,128]{1,0:T(8,128)(2,1)S(1)}, u32[]{:S(2)}, u32[]{:S(2)}) %collective-permute-start.26) | collective-permute-done | bytes 81952 | tf_op jit(solution)/shard_map/ppermute | solution.py:59
  82.9 0.1 collective-permute-start.28
  82.9 1.2 %shard_map.120 = (bf16[512,768]{1,0:T(8,128)(2,1)}, bf16[512,768]{1,0:T(8,128)(2,1)}) custom-call(bf16[320,128]{1,0:T(8,128)(2,1)S(1)} %shard_map.119.refs_0_, f32[256,768]{1,0:T(8,128)S(1)} %get-tuple-element.111.refs_1_, bf16[640,768]{1,0:T(8,128)(2,1)S(1)} %shard_map.110.refs_5_.refs_2_, bf16[512,768]{1,0:T(8,128)(2,1)S(1)} %copy-done.1, ...), custom_call_target="tpu_custom_call" | custom-call | flops 100663296 | bytes 2555904 | tf_op jit(solution)/shard_map/pallas_call | solution.py:500
  84.2 0.1 collective-permute-done.28.refs_0_
  84.2 1.2 %shard_map.121 = (bf16[512,768]{1,0:T(8,128)(2,1)}, bf16[512,768]{1,0:T(8,128)(2,1)}) custom-call(bf16[320,128]{1,0:T(8,128)(2,1)S(1)} %collective-permute-done.28.refs_0_, f32[256,768]{1,0:T(8,128)S(1)} %get-tuple-element.109.refs_1_, bf16[640,768]{1,0:T(8,128)(2,1)S(1)} %shard_map.110.refs_5_.refs_2_, ...), custom_call_target="tpu_custom_call", output_to_operand_aliasing={{0}: (5, {}), {1}: (6, {})} | custom-call | flops 100663296 | bytes 2555904 | tf_op jit(solution)/shard_map/pallas_call | solution.py:500
  (32 shorter events, 0.3 us)
Async XLA Ops:
  0.6 7.6 %copy-start.1 = (bf16[512,768]{1,0:T(8,128)(2,1)S(1)}, bf16[512,768]{1,0:T(8,128)(2,1)}, u32[]{:S(2)}) copy-start(bf16[512,768]{1,0:T(8,128)(2,1)} %refs_3_.9) | copy-start | bytes 2359300
  0.6 15.6 %collective-permute-start.4 = (bf16[512,768]{1,0:T(8,128)(2,1)}, bf16[512,768]{1,0:T(8,128)(2,1)S(1)}, u32[]{:S(2)}, u32[]{:S(2)}) collective-permute-start(bf16[512,768]{1,0:T(8,128)(2,1)} %refs_3_.9), channel_id=1, source_target_pairs={{0,1},{1,2},{2,3},{3,4},{4,5},{5,6},{6,7},{7,8},{8,9},{9,10},{10,1... | collective-permute-start | bytes 2359304 | tf_op jit(solution)/shard_map/ppermute | solution.py:50
  5.5 5.8 %collective-permute-start = (bf16[256,1024]{1,0:T(8,128)(2,1)S(1)}, bf16[256,1024]{1,0:T(8,128)(2,1)S(1)}, u32[]{:S(2)}, u32[]{:S(2)}) collective-permute-start(bf16[256,1024]{1,0:T(8,128)(2,1)S(1)} %get-tuple-element.60), channel_id=1, source_target_pairs={{0,1},{1,0},{2,3},{3,2},{4,5},{5,4},{6,7},{7,6},{8,9},{9,8},{10,11... | collective-permute-start | bytes 1572872 | tf_op jit(solution)/shard_map/ppermute | solution.py:59
  8.1 3.2 %collective-permute-start.1 = (bf16[256,1024]{1,0:T(8,128)(2,1)S(1)}, bf16[256,1024]{1,0:T(8,128)(2,1)S(1)}, u32[]{:S(2)}, u32[]{:S(2)}) collective-permute-start(bf16[256,1024]{1,0:T(8,128)(2,1)S(1)} %get-tuple-element.61), channel_id=1, source_target_pairs={{0,1},{1,0},{2,3},{3,2},{4,5},{5,4},{6,7},{7,6},{8,9},{9,8},{10,11... | collective-permute-start | bytes 1572872 | tf_op jit(solution)/shard_map/ppermute | solution.py:59
  8.2 19.4 %collective-permute-start.7 = (bf16[512,768]{1,0:T(8,128)(2,1)S(1)}, bf16[512,768]{1,0:T(8,128)(2,1)S(1)}, u32[]{:S(2)}, u32[]{:S(2)}) collective-permute-start(bf16[512,768]{1,0:T(8,128)(2,1)S(1)} %copy-done.1), channel_id=1, source_target_pairs={{0,15},{1,0},{2,1},{3,2},{4,3},{5,4},{6,5},{7,6},{8,7},{9,8},{10,9... | collective-permute-start | bytes 2359304 | tf_op jit(solution)/shard_map/ppermute | solution.py:50
  11.4 24.7 %copy-start.7 = (f32[768]{0:T(1024)S(1)}, f32[768]{0:T(1024)}, u32[]{:S(2)}) copy-start(f32[768]{0:T(1024)} %param.12) | copy-start | bytes 9220
  11.5 24.7 %copy-start.8 = (f32[768]{0:T(1024)S(1)}, f32[768]{0:T(1024)}, u32[]{:S(2)}) copy-start(f32[768]{0:T(1024)} %param.13) | copy-start | bytes 9220
  11.5 24.7 %copy-start.2 = (bf16[512,768]{1,0:T(8,128)(2,1)S(1)}, bf16[512,768]{1,0:T(8,128)(2,1)}, u32[]{:S(2)}) copy-start(bf16[512,768]{1,0:T(8,128)(2,1)} %o_ref.1) | copy-start | bytes 2359300
  11.6 19.8 %collective-permute-start.6 = (bf16[80,2048]{1,0:T(8,128)(2,1)S(1)}, bf16[80,2048]{1,0:T(8,128)(2,1)S(1)}, u32[]{:S(2)}, u32[]{:S(2)}) collective-permute-start(bf16[80,2048]{1,0:T(8,128)(2,1)S(1)} %get-tuple-element.69), channel_id=1, source_target_pairs={{0,2},{1,3},{2,0},{3,1},{4,6},{5,7},{6,4},{7,5},{8,10},{9,11},{10,... | collective-permute-start | bytes 983048 | tf_op jit(solution)/shard_map/ppermute | solution.py:59
  12.3 13.2 %collective-permute-start.2 = (bf16[96,512]{1,0:T(8,128)(2,1)S(1)}, bf16[96,512]{1,0:T(8,128)(2,1)S(1)}, u32[]{:S(2)}, u32[]{:S(2)}) collective-permute-start(bf16[96,512]{1,0:T(8,128)(2,1)S(1)} %get-tuple-element.65), channel_id=1, source_target_pairs={{0,4},{1,5},{2,6},{3,7},{4,0},{5,1},{6,2},{7,3},{8,12},{9,13},{10,... | collective-permute-start | bytes 294920 | tf_op jit(solution)/shard_map/ppermute | solution.py:59
  13.9 13.7 %collective-permute-start.3 = (bf16[96,512]{1,0:T(8,128)(2,1)S(1)}, bf16[96,512]{1,0:T(8,128)(2,1)S(1)}, u32[]{:S(2)}, u32[]{:S(2)}) collective-permute-start(bf16[96,512]{1,0:T(8,128)(2,1)S(1)} %get-tuple-element.66), channel_id=1, source_target_pairs={{0,8},{1,9},{2,10},{3,11},{4,12},{5,13},{6,14},{7,15},{8,0},{9,1},... | collective-permute-start | bytes 294920 | tf_op jit(solution)/shard_map/ppermute | solution.py:59
  16.2 15.3 %collective-permute-start.5 = (bf16[96,512]{1,0:T(8,128)(2,1)S(1)}, bf16[96,512]{1,0:T(8,128)(2,1)S(1)}, u32[]{:S(2)}, u32[]{:S(2)}) collective-permute-start(bf16[96,512]{1,0:T(8,128)(2,1)S(1)} %get-tuple-element.68), channel_id=1, source_target_pairs={{0,12},{1,13},{2,14},{3,15},{4,8},{5,9},{6,10},{7,11},{8,4},{9,5},... | collective-permute-start | bytes 294920 | tf_op jit(solution)/shard_map/ppermute | solution.py:59
  31.5 4.8 %copy-start.3 = (bf16[2,128,128]{2,1,0:T(8,128)(2,1)S(1)}, bf16[2,128,128]{2,1,0:T(8,128)(2,1)}, u32[]{:S(2)}) copy-start(bf16[2,128,128]{2,1,0:T(8,128)(2,1)} %constant.2.clone.refs_4_) | copy-start | bytes 196612
  31.5 4.8 %copy-start.4 = (f32[512]{0:T(512)S(1)}, f32[512]{0:T(512)}, u32[]{:S(2)}) copy-start(f32[512]{0:T(512)} %param.14) | copy-start | bytes 6148
  31.5 4.8 %copy-start.5 = (s32[512]{0:T(512)S(1)}, s32[512]{0:T(512)}, u32[]{:S(2)}) copy-start(s32[512]{0:T(512)} %param.15) | copy-start | bytes 6148
  31.5 4.8 %copy-start.6 = (s32[512]{0:T(512)S(1)}, s32[512]{0:T(512)}, u32[]{:S(2)}) copy-start(s32[512]{0:T(512)} %param.16) | copy-start | bytes 6148
  31.6 8.7 %collective-permute-start.10 = (bf16[80,512]{1,0:T(8,128)(2,1)S(1)}, bf16[80,512]{1,0:T(8,128)(2,1)S(1)}, u32[]{:S(2)}, u32[]{:S(2)}) collective-permute-start(bf16[80,512]{1,0:T(8,128)(2,1)S(1)} %get-tuple-element.75), channel_id=1, source_target_pairs={{0,12},{1,13},{2,14},{3,15},{4,8},{5,9},{6,10},{7,11},{8,4},{9,5},... | collective-permute-start | bytes 245768 | tf_op jit(solution)/shard_map/ppermute | solution.py:59
  33.9 6.6 %collective-permute-start.8 = (bf16[80,512]{1,0:T(8,128)(2,1)S(1)}, bf16[80,512]{1,0:T(8,128)(2,1)S(1)}, u32[]{:S(2)}, u32[]{:S(2)}) collective-permute-start(bf16[80,512]{1,0:T(8,128)(2,1)S(1)} %get-tuple-element.73), channel_id=1, source_target_pairs={{0,4},{1,5},{2,6},{3,7},{4,0},{5,1},{6,2},{7,3},{8,12},{9,13},{10,... | collective-permute-start | bytes 245768 | tf_op jit(solution)/shard_map/ppermute | solution.py:59
  34.0 6.9 %collective-permute-start.9 = (bf16[80,512]{1,0:T(8,128)(2,1)S(1)}, bf16[80,512]{1,0:T(8,128)(2,1)S(1)}, u32[]{:S(2)}, u32[]{:S(2)}) collective-permute-start(bf16[80,512]{1,0:T(8,128)(2,1)S(1)} %get-tuple-element.74), channel_id=1, source_target_pairs={{0,8},{1,9},{2,10},{3,11},{4,12},{5,13},{6,14},{7,15},{8,0},{9,1},... | collective-permute-start | bytes 245768 | tf_op jit(solution)/shard_map/ppermute | solution.py:59
  36.1 4.2 %collective-permute-start.11 = (bf16[48,512]{1,0:T(8,128)(2,1)S(1)}, bf16[48,512]{1,0:T(8,128)(2,1)S(1)}, u32[]{:S(2)}, u32[]{:S(2)}) collective-permute-start(bf16[48,512]{1,0:T(8,128)(2,1)S(1)} %get-tuple-element.80), channel_id=1, source_target_pairs={{0,2},{1,3},{2,0},{3,1},{4,6},{5,7},{6,4},{7,5},{8,10},{9,11},{10,... | collective-permute-start | bytes 147464 | tf_op jit(solution)/shard_map/ppermute | solution.py:59
  36.3 26.6 %copy-start = (bf16[2048,768]{1,0:T(8,128)(2,1)S(1)}, bf16[2048,768]{1,0:T(8,128)(2,1)}, u32[]{:S(2)}) copy-start(bf16[2048,768]{1,0:T(8,128)(2,1)} %refs_3_.7) | copy-start | bytes 9437188
  41.0 8.5 %collective-permute-start.12 = (bf16[80,512]{1,0:T(8,128)(2,1)S(1)}, bf16[80,512]{1,0:T(8,128)(2,1)S(1)}, u32[]{:S(2)}, u32[]{:S(2)}) collective-permute-start(bf16[80,512]{1,0:T(8,128)(2,1)S(1)} %get-tuple-element.91.refs_0_), channel_id=1, source_target_pairs={{0,4},{1,5},{2,6},{3,7},{4,0},{5,1},{6,2},{7,3},{8,12},{9,13},{10,... | collective-permute-start | bytes 245768 | tf_op jit(solution)/shard_map/ppermute | solution.py:59
  41.5 8.0 %collective-permute-start.13 = (bf16[80,512]{1,0:T(8,128)(2,1)S(1)}, bf16[80,512]{1,0:T(8,128)(2,1)S(1)}, u32[]{:S(2)}, u32[]{:S(2)}) collective-permute-start(bf16[80,512]{1,0:T(8,128)(2,1)S(1)} %get-tuple-element.91.refs_0_), channel_id=1, source_target_pairs={{0,8},{1,9},{2,10},{3,11},{4,12},{5,13},{6,14},{7,15},{8,0},{9,1},... | collective-permute-start | bytes 245768 | tf_op jit(solution)/shard_map/ppermute | solution.py:59
  44.2 6.3 %collective-permute-start.14 = (bf16[80,512]{1,0:T(8,128)(2,1)S(1)}, bf16[80,512]{1,0:T(8,128)(2,1)S(1)}, u32[]{:S(2)}, u32[]{:S(2)}) collective-permute-start(bf16[80,512]{1,0:T(8,128)(2,1)S(1)} %get-tuple-element.91.refs_0_), channel_id=1, source_target_pairs={{0,12},{1,13},{2,14},{3,15},{4,8},{5,9},{6,10},{7,11},{8,4},{9,5},... | collective-permute-start | bytes 245768 | tf_op jit(solution)/shard_map/ppermute | solution.py:59
  45.4 4.1 %collective-permute-start.15 = (bf16[48,512]{1,0:T(8,128)(2,1)S(1)}, bf16[48,512]{1,0:T(8,128)(2,1)S(1)}, u32[]{:S(2)}, u32[]{:S(2)}) collective-permute-start(bf16[48,512]{1,0:T(8,128)(2,1)S(1)} %get-tuple-element.95.refs_0_), channel_id=1, source_target_pairs={{0,2},{1,3},{2,0},{3,1},{4,6},{5,7},{6,4},{7,5},{8,10},{9,11},{10,... | collective-permute-start | bytes 147464 | tf_op jit(solution)/shard_map/ppermute | solution.py:59
  50.6 12.3 %collective-permute-start.17 = (bf16[80,2048]{1,0:T(8,128)(2,1)S(1)}, bf16[80,2048]{1,0:T(8,128)(2,1)S(1)}, u32[]{:S(2)}, u32[]{:S(2)}) collective-permute-start(bf16[80,2048]{1,0:T(8,128)(2,1)S(1)} %shard_map.112.refs_0_), channel_id=1, source_target_pairs={{0,2},{1,3},{2,0},{3,1},{4,6},{5,7},{6,4},{7,5},{8,10},{9,11},{10,... | collective-permute-start | bytes 983048 | tf_op jit(solution)/shard_map/ppermute | solution.py:59
  51.1 5.7 %collective-permute-start.19 = (bf16[96,512]{1,0:T(8,128)(2,1)S(1)}, bf16[96,512]{1,0:T(8,128)(2,1)S(1)}, u32[]{:S(2)}, u32[]{:S(2)}) collective-permute-start(bf16[96,512]{1,0:T(8,128)(2,1)S(1)} %shard_map.113.refs_0_), channel_id=1, source_target_pairs={{0,4},{1,5},{2,6},{3,7},{4,0},{5,1},{6,2},{7,3},{8,12},{9,13},{10,... | collective-permute-start | bytes 294920 | tf_op jit(solution)/shard_map/ppermute | solution.py:59
  52.6 9.6 %collective-permute-start.20 = (bf16[96,512]{1,0:T(8,128)(2,1)S(1)}, bf16[96,512]{1,0:T(8,128)(2,1)S(1)}, u32[]{:S(2)}, u32[]{:S(2)}) collective-permute-start(bf16[96,512]{1,0:T(8,128)(2,1)S(1)} %shard_map.113.refs_0_), channel_id=1, source_target_pairs={{0,8},{1,9},{2,10},{3,11},{4,12},{5,13},{6,14},{7,15},{8,0},{9,1},... | collective-permute-start | bytes 294920 | tf_op jit(solution)/shard_map/ppermute | solution.py:59
  54.2 8.0 %collective-permute-start.21 = (bf16[96,512]{1,0:T(8,128)(2,1)S(1)}, bf16[96,512]{1,0:T(8,128)(2,1)S(1)}, u32[]{:S(2)}, u32[]{:S(2)}) collective-permute-start(bf16[96,512]{1,0:T(8,128)(2,1)S(1)} %shard_map.113.refs_0_), channel_id=1, source_target_pairs={{0,12},{1,13},{2,14},{3,15},{4,8},{5,9},{6,10},{7,11},{8,4},{9,5},... | collective-permute-start | bytes 294920 | tf_op jit(solution)/shard_map/ppermute | solution.py:59
  62.3 2.3 %collective-permute-start.22 = (bf16[96,2048]{1,0:T(8,128)(2,1)S(1)}, bf16[96,2048]{1,0:T(8,128)(2,1)S(1)}, u32[]{:S(2)}, u32[]{:S(2)}) collective-permute-start(bf16[96,2048]{1,0:T(8,128)(2,1)S(1)} %shard_map.114.refs_2_), channel_id=1, source_target_pairs={{0,1},{1,0},{2,3},{3,2},{4,5},{5,4},{6,7},{7,6},{8,9},{9,8},{10,11... | collective-permute-start | bytes 1179656 | tf_op jit(solution)/shard_map/ppermute | solution.py:59
  62.3 2.2 %collective-permute-start.16 = (bf16[80,2048]{1,0:T(8,128)(2,1)S(1)}, bf16[80,2048]{1,0:T(8,128)(2,1)S(1)}, u32[]{:S(2)}, u32[]{:S(2)}) collective-permute-start(bf16[80,2048]{1,0:T(8,128)(2,1)S(1)} %shard_map.112.refs_0_), channel_id=1, source_target_pairs={{0,1},{1,0},{2,3},{3,2},{4,5},{5,4},{6,7},{7,6},{8,9},{9,8},{10,11... | collective-permute-start | bytes 983048 | tf_op jit(solution)/shard_map/ppermute | solution.py:59
  62.8 2.1 %collective-permute-start.18 = (bf16[80,2048]{1,0:T(8,128)(2,1)S(1)}, bf16[80,2048]{1,0:T(8,128)(2,1)S(1)}, u32[]{:S(2)}, u32[]{:S(2)}) collective-permute-start(bf16[80,2048]{1,0:T(8,128)(2,1)S(1)} %collective-permute-done.17.refs_1_), channel_id=1, source_target_pairs={{0,1},{1,0},{2,3},{3,2},{4,5},{5,4},{6,7},{7,6},{8,9},{9,8},{10,11... | collective-permute-start | bytes 983048 | tf_op jit(solution)/shard_map/ppermute | solution.py:59
  66.5 1.3 %collective-permute-start.23 = (bf16[320,128]{1,0:T(8,128)(2,1)S(1)}, bf16[320,128]{1,0:T(8,128)(2,1)S(1)}, u32[]{:S(2)}, u32[]{:S(2)}) collective-permute-start(bf16[320,128]{1,0:T(8,128)(2,1)S(1)} %get-tuple-element.104), channel_id=1, source_target_pairs={{0,1},{1,0},{2,3},{3,2},{4,5},{5,4},{6,7},{7,6},{8,9},{9,8},{10,11... | collective-permute-start | bytes 245768 | tf_op jit(solution)/shard_map/ppermute | solution.py:59
  67.9 4.6 %collective-permute-start.24 = (bf16[320,128]{1,0:T(8,128)(2,1)S(1)}, bf16[320,128]{1,0:T(8,128)(2,1)S(1)}, u32[]{:S(2)}, u32[]{:S(2)}) collective-permute-start(bf16[320,128]{1,0:T(8,128)(2,1)S(1)} %get-tuple-element.106), channel_id=1, source_target_pairs={{0,2},{1,3},{2,0},{3,1},{4,6},{5,7},{6,4},{7,5},{8,10},{9,11},{10,... | collective-permute-start | bytes 245768 | tf_op jit(solution)/shard_map/ppermute | solution.py:59
  72.5 5.3 %collective-permute-start.25 = (bf16[320,128]{1,0:T(8,128)(2,1)S(1)}, bf16[320,128]{1,0:T(8,128)(2,1)S(1)}, u32[]{:S(2)}, u32[]{:S(2)}) collective-permute-start(bf16[320,128]{1,0:T(8,128)(2,1)S(1)} %get-tuple-element.108), channel_id=1, source_target_pairs={{0,4},{1,5},{2,6},{3,7},{4,0},{5,1},{6,2},{7,3},{8,12},{9,13},{10,... | collective-permute-start | bytes 245768 | tf_op jit(solution)/shard_map/ppermute | solution.py:59
  74.1 8.7 %collective-permute-start.26 = (bf16[320,128]{1,0:T(8,128)(2,1)S(1)}, bf16[320,128]{1,0:T(8,128)(2,1)S(1)}, u32[]{:S(2)}, u32[]{:S(2)}) collective-permute-start(bf16[320,128]{1,0:T(8,128)(2,1)S(1)} %get-tuple-element.108), channel_id=1, source_target_pairs={{0,8},{1,9},{2,10},{3,11},{4,12},{5,13},{6,14},{7,15},{8,0},{9,1},... | collective-permute-start | bytes 245768 | tf_op jit(solution)/shard_map/ppermute | solution.py:59
  75.4 7.4 %collective-permute-start.27 = (bf16[320,128]{1,0:T(8,128)(2,1)S(1)}, bf16[320,128]{1,0:T(8,128)(2,1)S(1)}, u32[]{:S(2)}, u32[]{:S(2)}) collective-permute-start(bf16[320,128]{1,0:T(8,128)(2,1)S(1)} %get-tuple-element.108), channel_id=1, source_target_pairs={{0,12},{1,13},{2,14},{3,15},{4,8},{5,9},{6,10},{7,11},{8,4},{9,5},... | collective-permute-start | bytes 245768 | tf_op jit(solution)/shard_map/ppermute | solution.py:59
  82.9 1.3 %collective-permute-start.28 = (bf16[320,128]{1,0:T(8,128)(2,1)S(1)}, bf16[320,128]{1,0:T(8,128)(2,1)S(1)}, u32[]{:S(2)}, u32[]{:S(2)}) collective-permute-start(bf16[320,128]{1,0:T(8,128)(2,1)S(1)} %shard_map.119.refs_0_), channel_id=1, source_target_pairs={{0,1},{1,0},{2,3},{3,2},{4,5},{5,4},{6,7},{7,6},{8,9},{9,8},{10,11... | collective-permute-start | bytes 245768 | tf_op jit(solution)/shard_map/ppermute | solution.py:59

commit v20 on v19

--- a/solution.py
+++ b/solution.py
@@ -270,7 +270,7 @@
     me = position(level)
     width = parts[0].shape[along]
     for step, ref in enumerate(parts):
-        at = (me ^ step) * width
+        at = (me ^ (level[0] - step) % level[0]) * width
         if along == 0:
             out_ref[pl.ds(pl.multiple_of(at, 16), width), :] = ref[...]
         else:
@@ -405,7 +405,7 @@
     side = 1 - c if other else c
     first = blocks[0].shape[0]
     for step, ref in enumerate(blocks[:size]):
-        at = (x ^ step) * block
+        at = (x ^ (size - step) % size) * block
         c_ref[pl.ds(pl.multiple_of(at, 16), first), :] = ref[...]
     rest = block - first
     for i in range(size):
@@ -535,10 +535,11 @@
     bounds = tuple(a[None, :] for a in (energies, window_start, block_count))
 
     def to(array, level):
-        return [swapped(array, count, level, k) for k in range(1, level[0])]
+        return [swapped(array, count, level, k) for k in reversed(range(1, level[0]))]
 
     def parts_to(parts, level):
-        return [swapped(part, count, level, k + 1) for k, part in enumerate(parts)]
+        order = reversed(list(enumerate(parts)))
+        return [swapped(part, count, level, k + 1) for k, part in order]
 
     low = neighbour(response[:, local_cells - halo :], count, 1)
     high = neighbour(response[:, :halo], count, -1)
@@ -556,7 +557,7 @@
         shares_of((first, projections), across[0]),
         [keep_x, *sent],
     )
-    parts_z[-1], low = lax.optimization_barrier((parts_z[-1], low))
+    parts_z[0], low = lax.optimization_barrier((parts_z[0], low))
     taken_z, taken_x, low, high = lax.optimization_barrier(
         (parts_to(parts_z, along), parts_to(parts_x, across), low, high)
     )

time: 85.6 us -> 85.2 us (level)
  starting transfers between devices: 32.5 us -> 31.5 us
    ppermute x27, starting transfers between devices: 28.8 us -> 27.9 us  [swapped(): return lax.ppermute(array, 'band', pairs)]
  transfers between devices with their start and end apart: 29 -> 29, of which waited for: 18 -> 17; matrix products, arithmetic and copies ran while one was open for 0% -> 0% of each run, Pallas kernels for 11% -> 11%
where the time goes in v20:
time: 85.2 us; the launch traced here: 85.1 us
  waiting for transfers between devices  39.9 us (47%)
  starting transfers between devices  31.5 us (37%)
  Pallas kernels  12.6 us (15%)
  between operations  0.9 us (1%)
    ppermute x27, waiting for transfers between devices, swapped(): return lax.ppermute(array, 'band', pairs)  39.2 us
    ppermute x27, starting transfers between devices, swapped(): return lax.ppermute(array, 'band', pairs)  27.9 us
    pallas_call x1, Pallas kernels, first_sums(): pl.pallas_call(functools.partial(first_body, core, block, tile), out_shap...  4.34 us
    pallas_call x14, Pallas kernels, local_call(): pl.pallas_call(body, out_shape=outs, in_specs=[whole() for _ in args], ou...  3.66 us
    ppermute x2, starting transfers between devices, neighbour(): lax.ppermute(array, 'band', [(i, (i + step) % count) for i in range(count)])  3.62 us
    pallas_call x2, Pallas kernels, project(): pl.pallas_call(functools.partial(project_body, core, blk, other), out_sha...  2.4 us
    pallas_call x1, Pallas kernels, local_part(): pl.pallas_call(functools.partial(local_body, depth, (group_rows, blk)), g...  2.24 us
  transfers between devices with their start and end apart: 29, of which 17 were waited for; matrix products, arithmetic and copies ran while one was open for 0% of the time, Pallas kernels for 11%

profile of v20, /device:TPU:0, one launch (start us, length us, event | category | flops | bytes accessed | tf_op | source)
XLA Modules:
  0.0 85.1 jit_solution(2819642344892293755)
XLA Ops:
  0.6 0.5 collective-permute-start.4
  1.1 4.3 %shard_map.104 = (bf16[256,1024]{1,0:T(8,128)(2,1)S(1)}, bf16[256,1024]{1,0:T(8,128)(2,1)S(1)}, f32[160,2048]{1,0:T(8,128)S(1)}, f32[96,2048]{1,0:T(8,128)S(1)}) custom-call(bf16[512,768]{1,0:T(8,128)(2,1)} %refs_3_.9, bf16[2048,768]{1,0:T(8,128)(2,1)} %refs_3_.7), custom_call_target="tpu_custom_call" | custom-call | flops 1610612736 | bytes 6291456 | tf_op jit(solution)/shard_map/pallas_call | solution.py:153
  5.5 2.6 %collective-permute-start = (bf16[256,1024]{1,0:T(8,128)(2,1)S(1)}, bf16[256,1024]{1,0:T(8,128)(2,1)S(1)}, u32[]{:S(2)}, u32[]{:S(2)}) collective-permute-start(bf16[256,1024]{1,0:T(8,128)(2,1)S(1)} %get-tuple-element.60), channel_id=1, source_target_pairs={{0,1},{1,0},{2,3},{3,2},{4,5},{5,4},{6,7},{7,6},{8,9},{9,8},{10,11... | collective-permute-start | bytes 1572872 | tf_op jit(solution)/shard_map/ppermute | solution.py:59
  8.1 0.1 collective-permute-start.1
  8.2 3.1 %collective-permute-start.7 = (bf16[512,768]{1,0:T(8,128)(2,1)S(1)}, bf16[512,768]{1,0:T(8,128)(2,1)S(1)}, u32[]{:S(2)}, u32[]{:S(2)}) collective-permute-start(bf16[512,768]{1,0:T(8,128)(2,1)S(1)} %copy-done.1), channel_id=1, source_target_pairs={{0,15},{1,0},{2,1},{3,2},{4,3},{5,4},{6,5},{7,6},{8,7},{9,8},{10,9... | collective-permute-start | bytes 2359304 | tf_op jit(solution)/shard_map/ppermute | solution.py:50
  11.3 0.0 collective-permute-done.1.high_ref
  11.3 0.1 shard_map.105
  11.4 0.0 copy-start.7
  11.5 0.0 copy-start.8
  11.5 0.0 copy-start.2
  11.5 0.1 shard_map.106
  11.6 0.7 collective-permute-start.6
  12.3 2.4 %collective-permute-start.2 = (bf16[96,512]{1,0:T(8,128)(2,1)S(1)}, bf16[96,512]{1,0:T(8,128)(2,1)S(1)}, u32[]{:S(2)}, u32[]{:S(2)}) collective-permute-start(bf16[96,512]{1,0:T(8,128)(2,1)S(1)} %get-tuple-element.65), channel_id=1, source_target_pairs={{0,12},{1,13},{2,14},{3,15},{4,8},{5,9},{6,10},{7,11},{8,4},{9,5},... | collective-permute-start | bytes 294920 | tf_op jit(solution)/shard_map/ppermute | solution.py:59
  14.7 0.7 collective-permute-start.3
  15.4 0.8 collective-permute-done.4.refs_1_
  16.1 0.6 collective-permute-start.5
  16.7 10.9 %collective-permute-done.2.refs_1_ = bf16[96,512]{1,0:T(8,128)(2,1)S(1)} collective-permute-done((bf16[96,512]{1,0:T(8,128)(2,1)S(1)}, bf16[96,512]{1,0:T(8,128)(2,1)S(1)}, u32[]{:S(2)}, u32[]{:S(2)}) %collective-permute-start.2) | collective-permute-done | bytes 98336 | tf_op jit(solution)/shard_map/ppermute | solution.py:59
  27.6 3.1 %collective-permute-done.3.refs_2_ = bf16[96,512]{1,0:T(8,128)(2,1)S(1)} collective-permute-done((bf16[96,512]{1,0:T(8,128)(2,1)S(1)}, bf16[96,512]{1,0:T(8,128)(2,1)S(1)}, u32[]{:S(2)}, u32[]{:S(2)}) %collective-permute-start.3) | collective-permute-done | bytes 98336 | tf_op jit(solution)/shard_map/ppermute | solution.py:59
  30.7 0.0 collective-permute-done.7.refs_2_
  30.7 0.7 collective-permute-done.6.refs_1_
  31.4 0.0 collective-permute-done.5.refs_3_
  31.5 0.0 copy-start.6
  31.5 0.1 shard_map.107
  31.6 0.3 collective-permute-start.10
  31.9 2.5 %collective-permute-start.8 = (bf16[80,512]{1,0:T(8,128)(2,1)S(1)}, bf16[80,512]{1,0:T(8,128)(2,1)S(1)}, u32[]{:S(2)}, u32[]{:S(2)}) collective-permute-start(bf16[80,512]{1,0:T(8,128)(2,1)S(1)} %get-tuple-element.73), channel_id=1, source_target_pairs={{0,12},{1,13},{2,14},{3,15},{4,8},{5,9},{6,10},{7,11},{8,4},{9,5},... | collective-permute-start | bytes 245768 | tf_op jit(solution)/shard_map/ppermute | solution.py:59
  34.3 0.8 collective-permute-start.9
  35.2 0.1 collective-permute-start.11
  35.3 0.1 shard_map.110.refs_5_.refs_2_
  35.4 0.0 copy-start
  35.4 2.2 %shard_map.109 = (f32[512,768]{1,0:T(8,128)S(1)}, bf16[512,256]{1,0:T(8,128)(2,1)S(1)}) custom-call(bf16[512,768]{1,0:T(8,128)(2,1)S(1)} %copy-done.1, bf16[512,768]{1,0:T(8,128)(2,1)S(1)} %collective-permute-done.4.refs_1_, bf16[512,768]{1,0:T(8,128)(2,1)S(1)} %collective-permute-done.7.refs_2_, bf16[512,768]{1,0:T(8,128)(2,1)S(1)} %copy-done.2, ...), custom_call_target="tpu_custom_call" | custom-call | flops 235929600 | bytes 4980736 | tf_op jit(solution)/shard_map/pallas_call | solution.py:333
  37.7 1.6 %collective-permute-done.11.refs_5_ = bf16[48,512]{1,0:T(8,128)(2,1)S(1)} collective-permute-done((bf16[48,512]{1,0:T(8,128)(2,1)S(1)}, bf16[48,512]{1,0:T(8,128)(2,1)S(1)}, u32[]{:S(2)}, u32[]{:S(2)}) %collective-permute-start.11) | collective-permute-done | bytes 49184 | tf_op jit(solution)/shard_map/ppermute | solution.py:59
  39.3 2.7 %collective-permute-done.9.refs_2_ = bf16[80,512]{1,0:T(8,128)(2,1)S(1)} collective-permute-done((bf16[80,512]{1,0:T(8,128)(2,1)S(1)}, bf16[80,512]{1,0:T(8,128)(2,1)S(1)}, u32[]{:S(2)}, u32[]{:S(2)}) %collective-permute-start.9) | collective-permute-done | bytes 81952 | tf_op jit(solution)/shard_map/ppermute | solution.py:59
  42.0 0.1 shard_map.111
  42.1 2.6 %collective-permute-start.12 = (bf16[80,512]{1,0:T(8,128)(2,1)S(1)}, bf16[80,512]{1,0:T(8,128)(2,1)S(1)}, u32[]{:S(2)}, u32[]{:S(2)}) collective-permute-start(bf16[80,512]{1,0:T(8,128)(2,1)S(1)} %get-tuple-element.91.refs_0_), channel_id=1, source_target_pairs={{0,12},{1,13},{2,14},{3,15},{4,8},{5,9},{6,10},{7,11},{8,4},{9,5},... | collective-permute-start | bytes 245768 | tf_op jit(solution)/shard_map/ppermute | solution.py:59
  44.7 1.8 %collective-permute-start.14 = (bf16[80,512]{1,0:T(8,128)(2,1)S(1)}, bf16[80,512]{1,0:T(8,128)(2,1)S(1)}, u32[]{:S(2)}, u32[]{:S(2)}) collective-permute-start(bf16[80,512]{1,0:T(8,128)(2,1)S(1)} %get-tuple-element.91.refs_0_), channel_id=1, source_target_pairs={{0,4},{1,5},{2,6},{3,7},{4,0},{5,1},{6,2},{7,3},{8,12},{9,13},{10,... | collective-permute-start | bytes 245768 | tf_op jit(solution)/shard_map/ppermute | solution.py:59
  46.5 0.4 collective-permute-start.15
  46.9 3.7 %collective-permute-done.15.refs_1_ = bf16[48,512]{1,0:T(8,128)(2,1)S(1)} collective-permute-done((bf16[48,512]{1,0:T(8,128)(2,1)S(1)}, bf16[48,512]{1,0:T(8,128)(2,1)S(1)}, u32[]{:S(2)}, u32[]{:S(2)}) %collective-permute-start.15) | collective-permute-done | bytes 49184 | tf_op jit(solution)/shard_map/ppermute | solution.py:59
  50.6 0.0 collective-permute-done.12.refs_1_
  50.6 0.7 collective-permute-done.13.refs_2_
  51.4 0.0 collective-permute-done.14.refs_3_
  51.4 1.0 %collective-permute-start.17 = (bf16[80,2048]{1,0:T(8,128)(2,1)S(1)}, bf16[80,2048]{1,0:T(8,128)(2,1)S(1)}, u32[]{:S(2)}, u32[]{:S(2)}) collective-permute-start(bf16[80,2048]{1,0:T(8,128)(2,1)S(1)} %shard_map.112.refs_0_), channel_id=1, source_target_pairs={{0,2},{1,3},{2,0},{3,1},{4,6},{5,7},{6,4},{7,5},{8,10},{9,11},{10,... | collective-permute-start | bytes 983048 | tf_op jit(solution)/shard_map/ppermute | solution.py:59
  52.4 1.8 %collective-permute-start.19 = (bf16[96,512]{1,0:T(8,128)(2,1)S(1)}, bf16[96,512]{1,0:T(8,128)(2,1)S(1)}, u32[]{:S(2)}, u32[]{:S(2)}) collective-permute-start(bf16[96,512]{1,0:T(8,128)(2,1)S(1)} %shard_map.113.refs_0_), channel_id=1, source_target_pairs={{0,12},{1,13},{2,14},{3,15},{4,8},{5,9},{6,10},{7,11},{8,4},{9,5},... | collective-permute-start | bytes 294920 | tf_op jit(solution)/shard_map/ppermute | solution.py:59
  54.3 2.6 %collective-permute-start.21 = (bf16[96,512]{1,0:T(8,128)(2,1)S(1)}, bf16[96,512]{1,0:T(8,128)(2,1)S(1)}, u32[]{:S(2)}, u32[]{:S(2)}) collective-permute-start(bf16[96,512]{1,0:T(8,128)(2,1)S(1)} %shard_map.113.refs_0_), channel_id=1, source_target_pairs={{0,4},{1,5},{2,6},{3,7},{4,0},{5,1},{6,2},{7,3},{8,12},{9,13},{10,... | collective-permute-start | bytes 294920 | tf_op jit(solution)/shard_map/ppermute | solution.py:59
  56.9 3.2 %collective-permute-done.19.refs_1_ = bf16[96,512]{1,0:T(8,128)(2,1)S(1)} collective-permute-done((bf16[96,512]{1,0:T(8,128)(2,1)S(1)}, bf16[96,512]{1,0:T(8,128)(2,1)S(1)}, u32[]{:S(2)}, u32[]{:S(2)}) %collective-permute-start.19) | collective-permute-done | bytes 98336 | tf_op jit(solution)/shard_map/ppermute | solution.py:59
  60.1 2.9 %collective-permute-done.20.refs_2_ = bf16[96,512]{1,0:T(8,128)(2,1)S(1)} collective-permute-done((bf16[96,512]{1,0:T(8,128)(2,1)S(1)}, bf16[96,512]{1,0:T(8,128)(2,1)S(1)}, u32[]{:S(2)}, u32[]{:S(2)}) %collective-permute-start.20) | collective-permute-done | bytes 98336 | tf_op jit(solution)/shard_map/ppermute | solution.py:59
  63.0 0.1 collective-permute-start.22
  63.1 0.5 collective-permute-start.16
  63.6 0.1 collective-permute-start.18
  63.7 1.5 %shard_map.115 = (f32[256,768]{1,0:T(8,128)S(1)}, f32[320,128]{1,0:T(8,128)S(1)}) custom-call(bf16[80,2048]{1,0:T(8,128)(2,1)S(1)} %shard_map.112.refs_0_, bf16[80,2048]{1,0:T(8,128)(2,1)S(1)} %collective-permute-done.17.refs_1_, bf16[96,2048]{1,0:T(8,128)(2,1)S(1)} %shard_map.114.refs_2_, bf16[2048,768]{1,0:T(8,128)(2,1)S(1)} %copy-done, ...), custom_call_target="tpu_custom_call" | custom-call | flops 905969664 | bytes 7700480 | tf_op jit(solution)/shard_map/pallas_call | solution.py:91
  65.2 0.1 collective-permute-done.16.refs_0_
  65.3 0.5 collective-permute-done.18.refs_1_
  65.7 1.5 %shard_map.116 = (f32[256,768]{1,0:T(8,128)S(1)}, bf16[320,128]{1,0:T(8,128)(2,1)S(1)}) custom-call(bf16[80,2048]{1,0:T(8,128)(2,1)S(1)} %collective-permute-done.16.refs_0_, bf16[80,2048]{1,0:T(8,128)(2,1)S(1)} %collective-permute-done.18.refs_1_, bf16[96,2048]{1,0:T(8,128)(2,1)S(1)} %collective-permute-done.22.refs_2_, bf16[2048,768]{1,0:T(8,128)(2,1)S(1)} %copy-done, ...), custom_call_target="tpu_custom_call" | custom-call | flops 905969664 | bytes 7618560 | tf_op jit(solution)/shard_map/pallas_call | solution.py:91
  67.2 0.2 collective-permute-start.23
  67.4 1.1 %collective-permute-done.23.refs_0_ = bf16[320,128]{1,0:T(8,128)(2,1)S(1)} collective-permute-done((bf16[320,128]{1,0:T(8,128)(2,1)S(1)}, bf16[320,128]{1,0:T(8,128)(2,1)S(1)}, u32[]{:S(2)}, u32[]{:S(2)}) %collective-permute-start.23) | collective-permute-done | bytes 81952 | tf_op jit(solution)/shard_map/ppermute | solution.py:59
  68.6 1.5 %collective-permute-start.24 = (bf16[320,128]{1,0:T(8,128)(2,1)S(1)}, bf16[320,128]{1,0:T(8,128)(2,1)S(1)}, u32[]{:S(2)}, u32[]{:S(2)}) collective-permute-start(bf16[320,128]{1,0:T(8,128)(2,1)S(1)} %get-tuple-element.106), channel_id=1, source_target_pairs={{0,2},{1,3},{2,0},{3,1},{4,6},{5,7},{6,4},{7,5},{8,10},{9,11},{10,... | collective-permute-start | bytes 245768 | tf_op jit(solution)/shard_map/ppermute | solution.py:59
  70.1 3.0 %collective-permute-done.24.refs_0_ = bf16[320,128]{1,0:T(8,128)(2,1)S(1)} collective-permute-done((bf16[320,128]{1,0:T(8,128)(2,1)S(1)}, bf16[320,128]{1,0:T(8,128)(2,1)S(1)}, u32[]{:S(2)}, u32[]{:S(2)}) %collective-permute-start.24) | collective-permute-done | bytes 81952 | tf_op jit(solution)/shard_map/ppermute | solution.py:59
  73.2 2.1 %collective-permute-start.25 = (bf16[320,128]{1,0:T(8,128)(2,1)S(1)}, bf16[320,128]{1,0:T(8,128)(2,1)S(1)}, u32[]{:S(2)}, u32[]{:S(2)}) collective-permute-start(bf16[320,128]{1,0:T(8,128)(2,1)S(1)} %get-tuple-element.108), channel_id=1, source_target_pairs={{0,12},{1,13},{2,14},{3,15},{4,8},{5,9},{6,10},{7,11},{8,4},{9,5},... | collective-permute-start | bytes 245768 | tf_op jit(solution)/shard_map/ppermute | solution.py:59
  75.3 2.4 %collective-permute-start.27 = (bf16[320,128]{1,0:T(8,128)(2,1)S(1)}, bf16[320,128]{1,0:T(8,128)(2,1)S(1)}, u32[]{:S(2)}, u32[]{:S(2)}) collective-permute-start(bf16[320,128]{1,0:T(8,128)(2,1)S(1)} %get-tuple-element.108), channel_id=1, source_target_pairs={{0,4},{1,5},{2,6},{3,7},{4,0},{5,1},{6,2},{7,3},{8,12},{9,13},{10,... | collective-permute-start | bytes 245768 | tf_op jit(solution)/shard_map/ppermute | solution.py:59
  77.7 2.7 %collective-permute-done.25.refs_0_ = bf16[320,128]{1,0:T(8,128)(2,1)S(1)} collective-permute-done((bf16[320,128]{1,0:T(8,128)(2,1)S(1)}, bf16[320,128]{1,0:T(8,128)(2,1)S(1)}, u32[]{:S(2)}, u32[]{:S(2)}) %collective-permute-start.25) | collective-permute-done | bytes 81952 | tf_op jit(solution)/shard_map/ppermute | solution.py:59
  80.4 2.1 %collective-permute-done.26.refs_1_ = bf16[320,128]{1,0:T(8,128)(2,1)S(1)} collective-permute-done((bf16[320,128]{1,0:T(8,128)(2,1)S(1)}, bf16[320,128]{1,0:T(8,128)(2,1)S(1)}, u32[]{:S(2)}, u32[]{:S(2)}) %collective-permute-start.26) | collective-permute-done | bytes 81952 | tf_op jit(solution)/shard_map/ppermute | solution.py:59
  82.5 0.1 collective-permute-start.28
  82.6 1.2 %shard_map.120 = (bf16[512,768]{1,0:T(8,128)(2,1)}, bf16[512,768]{1,0:T(8,128)(2,1)}) custom-call(bf16[320,128]{1,0:T(8,128)(2,1)S(1)} %shard_map.119.refs_0_, f32[256,768]{1,0:T(8,128)S(1)} %get-tuple-element.111.refs_1_, bf16[640,768]{1,0:T(8,128)(2,1)S(1)} %shard_map.110.refs_5_.refs_2_, bf16[512,768]{1,0:T(8,128)(2,1)S(1)} %copy-done.1, ...), custom_call_target="tpu_custom_call" | custom-call | flops 100663296 | bytes 2555904 | tf_op jit(solution)/shard_map/pallas_call | solution.py:500
  83.8 0.1 collective-permute-done.28.refs_0_
  83.9 1.2 %shard_map.121 = (bf16[512,768]{1,0:T(8,128)(2,1)}, bf16[512,768]{1,0:T(8,128)(2,1)}) custom-call(bf16[320,128]{1,0:T(8,128)(2,1)S(1)} %collective-permute-done.28.refs_0_, f32[256,768]{1,0:T(8,128)S(1)} %get-tuple-element.109.refs_1_, bf16[640,768]{1,0:T(8,128)(2,1)S(1)} %shard_map.110.refs_5_.refs_2_, ...), custom_call_target="tpu_custom_call", output_to_operand_aliasing={{0}: (5, {}), {1}: (6, {})} | custom-call | flops 100663296 | bytes 2555904 | tf_op jit(solution)/shard_map/pallas_call | solution.py:500
  (32 shorter events, 0.3 us)
Async XLA Ops:
  0.6 7.6 %copy-start.1 = (bf16[512,768]{1,0:T(8,128)(2,1)S(1)}, bf16[512,768]{1,0:T(8,128)(2,1)}, u32[]{:S(2)}) copy-start(bf16[512,768]{1,0:T(8,128)(2,1)} %refs_3_.9) | copy-start | bytes 2359300
  0.6 15.5 %collective-permute-start.4 = (bf16[512,768]{1,0:T(8,128)(2,1)}, bf16[512,768]{1,0:T(8,128)(2,1)S(1)}, u32[]{:S(2)}, u32[]{:S(2)}) collective-permute-start(bf16[512,768]{1,0:T(8,128)(2,1)} %refs_3_.9), channel_id=1, source_target_pairs={{0,1},{1,2},{2,3},{3,4},{4,5},{5,6},{6,7},{7,8},{8,9},{9,10},{10,1... | collective-permute-start | bytes 2359304 | tf_op jit(solution)/shard_map/ppermute | solution.py:50
  5.5 5.8 %collective-permute-start = (bf16[256,1024]{1,0:T(8,128)(2,1)S(1)}, bf16[256,1024]{1,0:T(8,128)(2,1)S(1)}, u32[]{:S(2)}, u32[]{:S(2)}) collective-permute-start(bf16[256,1024]{1,0:T(8,128)(2,1)S(1)} %get-tuple-element.60), channel_id=1, source_target_pairs={{0,1},{1,0},{2,3},{3,2},{4,5},{5,4},{6,7},{7,6},{8,9},{9,8},{10,11... | collective-permute-start | bytes 1572872 | tf_op jit(solution)/shard_map/ppermute | solution.py:59
  8.1 3.2 %collective-permute-start.1 = (bf16[256,1024]{1,0:T(8,128)(2,1)S(1)}, bf16[256,1024]{1,0:T(8,128)(2,1)S(1)}, u32[]{:S(2)}, u32[]{:S(2)}) collective-permute-start(bf16[256,1024]{1,0:T(8,128)(2,1)S(1)} %get-tuple-element.61), channel_id=1, source_target_pairs={{0,1},{1,0},{2,3},{3,2},{4,5},{5,4},{6,7},{7,6},{8,9},{9,8},{10,11... | collective-permute-start | bytes 1572872 | tf_op jit(solution)/shard_map/ppermute | solution.py:59
  8.2 22.5 %collective-permute-start.7 = (bf16[512,768]{1,0:T(8,128)(2,1)S(1)}, bf16[512,768]{1,0:T(8,128)(2,1)S(1)}, u32[]{:S(2)}, u32[]{:S(2)}) collective-permute-start(bf16[512,768]{1,0:T(8,128)(2,1)S(1)} %copy-done.1), channel_id=1, source_target_pairs={{0,15},{1,0},{2,1},{3,2},{4,3},{5,4},{6,5},{7,6},{8,7},{9,8},{10,9... | collective-permute-start | bytes 2359304 | tf_op jit(solution)/shard_map/ppermute | solution.py:50
  11.4 23.8 %copy-start.7 = (f32[768]{0:T(1024)S(1)}, f32[768]{0:T(1024)}, u32[]{:S(2)}) copy-start(f32[768]{0:T(1024)} %param.12) | copy-start | bytes 9220
  11.5 23.8 %copy-start.8 = (f32[768]{0:T(1024)S(1)}, f32[768]{0:T(1024)}, u32[]{:S(2)}) copy-start(f32[768]{0:T(1024)} %param.13) | copy-start | bytes 9220
  11.5 23.8 %copy-start.2 = (bf16[512,768]{1,0:T(8,128)(2,1)S(1)}, bf16[512,768]{1,0:T(8,128)(2,1)}, u32[]{:S(2)}) copy-start(bf16[512,768]{1,0:T(8,128)(2,1)} %o_ref.1) | copy-start | bytes 2359300
  11.6 19.8 %collective-permute-start.6 = (bf16[80,2048]{1,0:T(8,128)(2,1)S(1)}, bf16[80,2048]{1,0:T(8,128)(2,1)S(1)}, u32[]{:S(2)}, u32[]{:S(2)}) collective-permute-start(bf16[80,2048]{1,0:T(8,128)(2,1)S(1)} %get-tuple-element.69), channel_id=1, source_target_pairs={{0,2},{1,3},{2,0},{3,1},{4,6},{5,7},{6,4},{7,5},{8,10},{9,11},{10,... | collective-permute-start | bytes 983048 | tf_op jit(solution)/shard_map/ppermute | solution.py:59
  12.3 15.3 %collective-permute-start.2 = (bf16[96,512]{1,0:T(8,128)(2,1)S(1)}, bf16[96,512]{1,0:T(8,128)(2,1)S(1)}, u32[]{:S(2)}, u32[]{:S(2)}) collective-permute-start(bf16[96,512]{1,0:T(8,128)(2,1)S(1)} %get-tuple-element.65), channel_id=1, source_target_pairs={{0,12},{1,13},{2,14},{3,15},{4,8},{5,9},{6,10},{7,11},{8,4},{9,5},... | collective-permute-start | bytes 294920 | tf_op jit(solution)/shard_map/ppermute | solution.py:59
  14.7 16.0 %collective-permute-start.3 = (bf16[96,512]{1,0:T(8,128)(2,1)S(1)}, bf16[96,512]{1,0:T(8,128)(2,1)S(1)}, u32[]{:S(2)}, u32[]{:S(2)}) collective-permute-start(bf16[96,512]{1,0:T(8,128)(2,1)S(1)} %get-tuple-element.66), channel_id=1, source_target_pairs={{0,8},{1,9},{2,10},{3,11},{4,12},{5,13},{6,14},{7,15},{8,0},{9,1},... | collective-permute-start | bytes 294920 | tf_op jit(solution)/shard_map/ppermute | solution.py:59
  16.1 15.3 %collective-permute-start.5 = (bf16[96,512]{1,0:T(8,128)(2,1)S(1)}, bf16[96,512]{1,0:T(8,128)(2,1)S(1)}, u32[]{:S(2)}, u32[]{:S(2)}) collective-permute-start(bf16[96,512]{1,0:T(8,128)(2,1)S(1)} %get-tuple-element.68), channel_id=1, source_target_pairs={{0,4},{1,5},{2,6},{3,7},{4,0},{5,1},{6,2},{7,3},{8,12},{9,13},{10,... | collective-permute-start | bytes 294920 | tf_op jit(solution)/shard_map/ppermute | solution.py:59
  31.5 3.9 %copy-start.3 = (bf16[2,128,128]{2,1,0:T(8,128)(2,1)S(1)}, bf16[2,128,128]{2,1,0:T(8,128)(2,1)}, u32[]{:S(2)}) copy-start(bf16[2,128,128]{2,1,0:T(8,128)(2,1)} %constant.2.clone.refs_4_) | copy-start | bytes 196612
  31.5 3.9 %copy-start.4 = (f32[512]{0:T(512)S(1)}, f32[512]{0:T(512)}, u32[]{:S(2)}) copy-start(f32[512]{0:T(512)} %param.14) | copy-start | bytes 6148
  31.5 3.9 %copy-start.5 = (s32[512]{0:T(512)S(1)}, s32[512]{0:T(512)}, u32[]{:S(2)}) copy-start(s32[512]{0:T(512)} %param.15) | copy-start | bytes 6148
  31.5 3.9 %copy-start.6 = (s32[512]{0:T(512)S(1)}, s32[512]{0:T(512)}, u32[]{:S(2)}) copy-start(s32[512]{0:T(512)} %param.16) | copy-start | bytes 6148
  31.6 7.8 %collective-permute-start.10 = (bf16[80,512]{1,0:T(8,128)(2,1)S(1)}, bf16[80,512]{1,0:T(8,128)(2,1)S(1)}, u32[]{:S(2)}, u32[]{:S(2)}) collective-permute-start(bf16[80,512]{1,0:T(8,128)(2,1)S(1)} %get-tuple-element.75), channel_id=1, source_target_pairs={{0,4},{1,5},{2,6},{3,7},{4,0},{5,1},{6,2},{7,3},{8,12},{9,13},{10,... | collective-permute-start | bytes 245768 | tf_op jit(solution)/shard_map/ppermute | solution.py:59
  31.9 7.5 %collective-permute-start.8 = (bf16[80,512]{1,0:T(8,128)(2,1)S(1)}, bf16[80,512]{1,0:T(8,128)(2,1)S(1)}, u32[]{:S(2)}, u32[]{:S(2)}) collective-permute-start(bf16[80,512]{1,0:T(8,128)(2,1)S(1)} %get-tuple-element.73), channel_id=1, source_target_pairs={{0,12},{1,13},{2,14},{3,15},{4,8},{5,9},{6,10},{7,11},{8,4},{9,5},... | collective-permute-start | bytes 245768 | tf_op jit(solution)/shard_map/ppermute | solution.py:59
  34.3 7.7 %collective-permute-start.9 = (bf16[80,512]{1,0:T(8,128)(2,1)S(1)}, bf16[80,512]{1,0:T(8,128)(2,1)S(1)}, u32[]{:S(2)}, u32[]{:S(2)}) collective-permute-start(bf16[80,512]{1,0:T(8,128)(2,1)S(1)} %get-tuple-element.74), channel_id=1, source_target_pairs={{0,8},{1,9},{2,10},{3,11},{4,12},{5,13},{6,14},{7,15},{8,0},{9,1},... | collective-permute-start | bytes 245768 | tf_op jit(solution)/shard_map/ppermute | solution.py:59
  35.2 4.2 %collective-permute-start.11 = (bf16[48,512]{1,0:T(8,128)(2,1)S(1)}, bf16[48,512]{1,0:T(8,128)(2,1)S(1)}, u32[]{:S(2)}, u32[]{:S(2)}) collective-permute-start(bf16[48,512]{1,0:T(8,128)(2,1)S(1)} %get-tuple-element.80), channel_id=1, source_target_pairs={{0,2},{1,3},{2,0},{3,1},{4,6},{5,7},{6,4},{7,5},{8,10},{9,11},{10,... | collective-permute-start | bytes 147464 | tf_op jit(solution)/shard_map/ppermute | solution.py:59
  35.4 28.2 %copy-start = (bf16[2048,768]{1,0:T(8,128)(2,1)S(1)}, bf16[2048,768]{1,0:T(8,128)(2,1)}, u32[]{:S(2)}) copy-start(bf16[2048,768]{1,0:T(8,128)(2,1)} %refs_3_.7) | copy-start | bytes 9437188
  42.1 8.5 %collective-permute-start.12 = (bf16[80,512]{1,0:T(8,128)(2,1)S(1)}, bf16[80,512]{1,0:T(8,128)(2,1)S(1)}, u32[]{:S(2)}, u32[]{:S(2)}) collective-permute-start(bf16[80,512]{1,0:T(8,128)(2,1)S(1)} %get-tuple-element.91.refs_0_), channel_id=1, source_target_pairs={{0,12},{1,13},{2,14},{3,15},{4,8},{5,9},{6,10},{7,11},{8,4},{9,5},... | collective-permute-start | bytes 245768 | tf_op jit(solution)/shard_map/ppermute | solution.py:59
  44.7 6.7 %collective-permute-start.13 = (bf16[80,512]{1,0:T(8,128)(2,1)S(1)}, bf16[80,512]{1,0:T(8,128)(2,1)S(1)}, u32[]{:S(2)}, u32[]{:S(2)}) collective-permute-start(bf16[80,512]{1,0:T(8,128)(2,1)S(1)} %get-tuple-element.91.refs_0_), channel_id=1, source_target_pairs={{0,8},{1,9},{2,10},{3,11},{4,12},{5,13},{6,14},{7,15},{8,0},{9,1},... | collective-permute-start | bytes 245768 | tf_op jit(solution)/shard_map/ppermute | solution.py:59
  44.7 6.7 %collective-permute-start.14 = (bf16[80,512]{1,0:T(8,128)(2,1)S(1)}, bf16[80,512]{1,0:T(8,128)(2,1)S(1)}, u32[]{:S(2)}, u32[]{:S(2)}) collective-permute-start(bf16[80,512]{1,0:T(8,128)(2,1)S(1)} %get-tuple-element.91.refs_0_), channel_id=1, source_target_pairs={{0,4},{1,5},{2,6},{3,7},{4,0},{5,1},{6,2},{7,3},{8,12},{9,13},{10,... | collective-permute-start | bytes 245768 | tf_op jit(solution)/shard_map/ppermute | solution.py:59
  46.5 4.1 %collective-permute-start.15 = (bf16[48,512]{1,0:T(8,128)(2,1)S(1)}, bf16[48,512]{1,0:T(8,128)(2,1)S(1)}, u32[]{:S(2)}, u32[]{:S(2)}) collective-permute-start(bf16[48,512]{1,0:T(8,128)(2,1)S(1)} %get-tuple-element.95.refs_0_), channel_id=1, source_target_pairs={{0,2},{1,3},{2,0},{3,1},{4,6},{5,7},{6,4},{7,5},{8,10},{9,11},{10,... | collective-permute-start | bytes 147464 | tf_op jit(solution)/shard_map/ppermute | solution.py:59
  51.4 12.2 %collective-permute-start.17 = (bf16[80,2048]{1,0:T(8,128)(2,1)S(1)}, bf16[80,2048]{1,0:T(8,128)(2,1)S(1)}, u32[]{:S(2)}, u32[]{:S(2)}) collective-permute-start(bf16[80,2048]{1,0:T(8,128)(2,1)S(1)} %shard_map.112.refs_0_), channel_id=1, source_target_pairs={{0,2},{1,3},{2,0},{3,1},{4,6},{5,7},{6,4},{7,5},{8,10},{9,11},{10,... | collective-permute-start | bytes 983048 | tf_op jit(solution)/shard_map/ppermute | solution.py:59
  52.4 7.6 %collective-permute-start.19 = (bf16[96,512]{1,0:T(8,128)(2,1)S(1)}, bf16[96,512]{1,0:T(8,128)(2,1)S(1)}, u32[]{:S(2)}, u32[]{:S(2)}) collective-permute-start(bf16[96,512]{1,0:T(8,128)(2,1)S(1)} %shard_map.113.refs_0_), channel_id=1, source_target_pairs={{0,12},{1,13},{2,14},{3,15},{4,8},{5,9},{6,10},{7,11},{8,4},{9,5},... | collective-permute-start | bytes 294920 | tf_op jit(solution)/shard_map/ppermute | solution.py:59
  54.2 8.7 %collective-permute-start.20 = (bf16[96,512]{1,0:T(8,128)(2,1)S(1)}, bf16[96,512]{1,0:T(8,128)(2,1)S(1)}, u32[]{:S(2)}, u32[]{:S(2)}) collective-permute-start(bf16[96,512]{1,0:T(8,128)(2,1)S(1)} %shard_map.113.refs_0_), channel_id=1, source_target_pairs={{0,8},{1,9},{2,10},{3,11},{4,12},{5,13},{6,14},{7,15},{8,0},{9,1},... | collective-permute-start | bytes 294920 | tf_op jit(solution)/shard_map/ppermute | solution.py:59
  54.3 8.7 %collective-permute-start.21 = (bf16[96,512]{1,0:T(8,128)(2,1)S(1)}, bf16[96,512]{1,0:T(8,128)(2,1)S(1)}, u32[]{:S(2)}, u32[]{:S(2)}) collective-permute-start(bf16[96,512]{1,0:T(8,128)(2,1)S(1)} %shard_map.113.refs_0_), channel_id=1, source_target_pairs={{0,4},{1,5},{2,6},{3,7},{4,0},{5,1},{6,2},{7,3},{8,12},{9,13},{10,... | collective-permute-start | bytes 294920 | tf_op jit(solution)/shard_map/ppermute | solution.py:59
  63.0 2.3 %collective-permute-start.22 = (bf16[96,2048]{1,0:T(8,128)(2,1)S(1)}, bf16[96,2048]{1,0:T(8,128)(2,1)S(1)}, u32[]{:S(2)}, u32[]{:S(2)}) collective-permute-start(bf16[96,2048]{1,0:T(8,128)(2,1)S(1)} %shard_map.114.refs_2_), channel_id=1, source_target_pairs={{0,1},{1,0},{2,3},{3,2},{4,5},{5,4},{6,7},{7,6},{8,9},{9,8},{10,11... | collective-permute-start | bytes 1179656 | tf_op jit(solution)/shard_map/ppermute | solution.py:59
  63.1 2.2 %collective-permute-start.16 = (bf16[80,2048]{1,0:T(8,128)(2,1)S(1)}, bf16[80,2048]{1,0:T(8,128)(2,1)S(1)}, u32[]{:S(2)}, u32[]{:S(2)}) collective-permute-start(bf16[80,2048]{1,0:T(8,128)(2,1)S(1)} %shard_map.112.refs_0_), channel_id=1, source_target_pairs={{0,1},{1,0},{2,3},{3,2},{4,5},{5,4},{6,7},{7,6},{8,9},{9,8},{10,11... | collective-permute-start | bytes 983048 | tf_op jit(solution)/shard_map/ppermute | solution.py:59
  63.6 2.1 %collective-permute-start.18 = (bf16[80,2048]{1,0:T(8,128)(2,1)S(1)}, bf16[80,2048]{1,0:T(8,128)(2,1)S(1)}, u32[]{:S(2)}, u32[]{:S(2)}) collective-permute-start(bf16[80,2048]{1,0:T(8,128)(2,1)S(1)} %collective-permute-done.17.refs_1_), channel_id=1, source_target_pairs={{0,1},{1,0},{2,3},{3,2},{4,5},{5,4},{6,7},{7,6},{8,9},{9,8},{10,11... | collective-permute-start | bytes 983048 | tf_op jit(solution)/shard_map/ppermute | solution.py:59
  67.2 1.3 %collective-permute-start.23 = (bf16[320,128]{1,0:T(8,128)(2,1)S(1)}, bf16[320,128]{1,0:T(8,128)(2,1)S(1)}, u32[]{:S(2)}, u32[]{:S(2)}) collective-permute-start(bf16[320,128]{1,0:T(8,128)(2,1)S(1)} %get-tuple-element.104), channel_id=1, source_target_pairs={{0,1},{1,0},{2,3},{3,2},{4,5},{5,4},{6,7},{7,6},{8,9},{9,8},{10,11... | collective-permute-start | bytes 245768 | tf_op jit(solution)/shard_map/ppermute | solution.py:59
  68.6 4.6 %collective-permute-start.24 = (bf16[320,128]{1,0:T(8,128)(2,1)S(1)}, bf16[320,128]{1,0:T(8,128)(2,1)S(1)}, u32[]{:S(2)}, u32[]{:S(2)}) collective-permute-start(bf16[320,128]{1,0:T(8,128)(2,1)S(1)} %get-tuple-element.106), channel_id=1, source_target_pairs={{0,2},{1,3},{2,0},{3,1},{4,6},{5,7},{6,4},{7,5},{8,10},{9,11},{10,... | collective-permute-start | bytes 245768 | tf_op jit(solution)/shard_map/ppermute | solution.py:59
  73.2 7.2 %collective-permute-start.25 = (bf16[320,128]{1,0:T(8,128)(2,1)S(1)}, bf16[320,128]{1,0:T(8,128)(2,1)S(1)}, u32[]{:S(2)}, u32[]{:S(2)}) collective-permute-start(bf16[320,128]{1,0:T(8,128)(2,1)S(1)} %get-tuple-element.108), channel_id=1, source_target_pairs={{0,12},{1,13},{2,14},{3,15},{4,8},{5,9},{6,10},{7,11},{8,4},{9,5},... | collective-permute-start | bytes 245768 | tf_op jit(solution)/shard_map/ppermute | solution.py:59
  75.3 7.2 %collective-permute-start.26 = (bf16[320,128]{1,0:T(8,128)(2,1)S(1)}, bf16[320,128]{1,0:T(8,128)(2,1)S(1)}, u32[]{:S(2)}, u32[]{:S(2)}) collective-permute-start(bf16[320,128]{1,0:T(8,128)(2,1)S(1)} %get-tuple-element.108), channel_id=1, source_target_pairs={{0,8},{1,9},{2,10},{3,11},{4,12},{5,13},{6,14},{7,15},{8,0},{9,1},... | collective-permute-start | bytes 245768 | tf_op jit(solution)/shard_map/ppermute | solution.py:59
  75.3 7.2 %collective-permute-start.27 = (bf16[320,128]{1,0:T(8,128)(2,1)S(1)}, bf16[320,128]{1,0:T(8,128)(2,1)S(1)}, u32[]{:S(2)}, u32[]{:S(2)}) collective-permute-start(bf16[320,128]{1,0:T(8,128)(2,1)S(1)} %get-tuple-element.108), channel_id=1, source_target_pairs={{0,4},{1,5},{2,6},{3,7},{4,0},{5,1},{6,2},{7,3},{8,12},{9,13},{10,... | collective-permute-start | bytes 245768 | tf_op jit(solution)/shard_map/ppermute | solution.py:59
  82.5 1.3 %collective-permute-start.28 = (bf16[320,128]{1,0:T(8,128)(2,1)S(1)}, bf16[320,128]{1,0:T(8,128)(2,1)S(1)}, u32[]{:S(2)}, u32[]{:S(2)}) collective-permute-start(bf16[320,128]{1,0:T(8,128)(2,1)S(1)} %shard_map.119.refs_0_), channel_id=1, source_target_pairs={{0,1},{1,0},{2,3},{3,2},{4,5},{5,4},{6,7},{7,6},{8,9},{9,8},{10,11... | collective-permute-start | bytes 245768 | tf_op jit(solution)/shard_map/ppermute | solution.py:59

commit v21 on v19

--- a/solution.py
+++ b/solution.py
@@ -593,7 +593,8 @@
     other_wide, part = apply(others, projectors, base, padded, *sizes, True)
     total, part = add_up(keep, to(part, core))
     total, part = add_up(total, to(part, across))
-    own = finish(total, to(part, along), window_scale)
+    far_first = [swapped(part, count, along, k) for k in reversed(range(1, along[0]))]
+    own = finish(total, far_first, window_scale)
     (theirs,) = to(own, core)
     outs = project(own, wide, padded, response, mask, core, blk, False, ())
     return project(theirs, other_wide, padded, response, mask, core, blk, True, outs)

time: 85.6 us -> 85.3 us (level)
  no operation moved by 1% of the time
where the time goes in v21:
time: 85.3 us; the launch traced here: 85.1 us
  waiting for transfers between devices  39 us (46%)
  starting transfers between devices  32.5 us (38%)
  Pallas kernels  12.6 us (15%)
  between operations  0.9 us (1%)
    ppermute x27, waiting for transfers between devices, swapped(): return lax.ppermute(array, 'band', pairs)  38.1 us
    ppermute x27, starting transfers between devices, swapped(): return lax.ppermute(array, 'band', pairs)  28.8 us
    pallas_call x1, Pallas kernels, first_sums(): pl.pallas_call(functools.partial(first_body, core, block, tile), out_shap...  4.34 us
    pallas_call x14, Pallas kernels, local_call(): pl.pallas_call(body, out_shape=outs, in_specs=[whole() for _ in args], ou...  3.66 us
    ppermute x2, starting transfers between devices, neighbour(): lax.ppermute(array, 'band', [(i, (i + step) % count) for i in range(count)])  3.62 us
    pallas_call x2, Pallas kernels, project(): pl.pallas_call(functools.partial(project_body, core, blk, other), out_sha...  2.4 us
    pallas_call x1, Pallas kernels, local_part(): pl.pallas_call(functools.partial(local_body, depth, (group_rows, blk)), g...  2.24 us
  transfers between devices with their start and end apart: 29, of which 18 were waited for; matrix products, arithmetic and copies ran while one was open for 0% of the time, Pallas kernels for 11%

profile of v21, /device:TPU:0, one launch (start us, length us, event | category | flops | bytes accessed | tf_op | source)
XLA Modules:
  0.0 85.1 jit_solution(14505683226085731805)
XLA Ops:
  0.6 0.5 collective-permute-start.4
  1.1 4.3 %shard_map.104 = (bf16[256,1024]{1,0:T(8,128)(2,1)S(1)}, bf16[256,1024]{1,0:T(8,128)(2,1)S(1)}, f32[160,2048]{1,0:T(8,128)S(1)}, f32[96,2048]{1,0:T(8,128)S(1)}) custom-call(bf16[512,768]{1,0:T(8,128)(2,1)} %refs_3_.9, bf16[2048,768]{1,0:T(8,128)(2,1)} %refs_3_.7), custom_call_target="tpu_custom_call" | custom-call | flops 1610612736 | bytes 6291456 | tf_op jit(solution)/shard_map/pallas_call | solution.py:153
  5.5 2.6 %collective-permute-start = (bf16[256,1024]{1,0:T(8,128)(2,1)S(1)}, bf16[256,1024]{1,0:T(8,128)(2,1)S(1)}, u32[]{:S(2)}, u32[]{:S(2)}) collective-permute-start(bf16[256,1024]{1,0:T(8,128)(2,1)S(1)} %get-tuple-element.60), channel_id=1, source_target_pairs={{0,1},{1,0},{2,3},{3,2},{4,5},{5,4},{6,7},{7,6},{8,9},{9,8},{10,11... | collective-permute-start | bytes 1572872 | tf_op jit(solution)/shard_map/ppermute | solution.py:59
  8.1 0.1 collective-permute-start.1
  8.2 3.1 %collective-permute-start.7 = (bf16[512,768]{1,0:T(8,128)(2,1)S(1)}, bf16[512,768]{1,0:T(8,128)(2,1)S(1)}, u32[]{:S(2)}, u32[]{:S(2)}) collective-permute-start(bf16[512,768]{1,0:T(8,128)(2,1)S(1)} %copy-done.1), channel_id=1, source_target_pairs={{0,15},{1,0},{2,1},{3,2},{4,3},{5,4},{6,5},{7,6},{8,7},{9,8},{10,9... | collective-permute-start | bytes 2359304 | tf_op jit(solution)/shard_map/ppermute | solution.py:50
  11.3 0.1 shard_map.105
  11.4 0.0 copy-start.7
  11.5 0.0 copy-start.8
  11.5 0.0 copy-start.2
  11.5 0.1 shard_map.106
  11.6 0.7 collective-permute-start.6
  12.3 1.6 %collective-permute-start.2 = (bf16[96,512]{1,0:T(8,128)(2,1)S(1)}, bf16[96,512]{1,0:T(8,128)(2,1)S(1)}, u32[]{:S(2)}, u32[]{:S(2)}) collective-permute-start(bf16[96,512]{1,0:T(8,128)(2,1)S(1)} %get-tuple-element.65), channel_id=1, source_target_pairs={{0,4},{1,5},{2,6},{3,7},{4,0},{5,1},{6,2},{7,3},{8,12},{9,13},{10,... | collective-permute-start | bytes 294920 | tf_op jit(solution)/shard_map/ppermute | solution.py:59
  13.9 1.4 %collective-permute-start.3 = (bf16[96,512]{1,0:T(8,128)(2,1)S(1)}, bf16[96,512]{1,0:T(8,128)(2,1)S(1)}, u32[]{:S(2)}, u32[]{:S(2)}) collective-permute-start(bf16[96,512]{1,0:T(8,128)(2,1)S(1)} %get-tuple-element.66), channel_id=1, source_target_pairs={{0,8},{1,9},{2,10},{3,11},{4,12},{5,13},{6,14},{7,15},{8,0},{9,1},... | collective-permute-start | bytes 294920 | tf_op jit(solution)/shard_map/ppermute | solution.py:59
  15.3 0.9 %collective-permute-done.4.refs_1_ = bf16[512,768]{1,0:T(8,128)(2,1)S(1)} collective-permute-done((bf16[512,768]{1,0:T(8,128)(2,1)}, bf16[512,768]{1,0:T(8,128)(2,1)S(1)}, u32[]{:S(2)}, u32[]{:S(2)}) %collective-permute-start.4) | collective-permute-done | bytes 786464 | tf_op jit(solution)/shard_map/ppermute | solution.py:50
  16.2 2.2 %collective-permute-start.5 = (bf16[96,512]{1,0:T(8,128)(2,1)S(1)}, bf16[96,512]{1,0:T(8,128)(2,1)S(1)}, u32[]{:S(2)}, u32[]{:S(2)}) collective-permute-start(bf16[96,512]{1,0:T(8,128)(2,1)S(1)} %get-tuple-element.68), channel_id=1, source_target_pairs={{0,12},{1,13},{2,14},{3,15},{4,8},{5,9},{6,10},{7,11},{8,4},{9,5},... | collective-permute-start | bytes 294920 | tf_op jit(solution)/shard_map/ppermute | solution.py:59
  18.4 7.1 %collective-permute-done.2.refs_1_ = bf16[96,512]{1,0:T(8,128)(2,1)S(1)} collective-permute-done((bf16[96,512]{1,0:T(8,128)(2,1)S(1)}, bf16[96,512]{1,0:T(8,128)(2,1)S(1)}, u32[]{:S(2)}, u32[]{:S(2)}) %collective-permute-start.2) | collective-permute-done | bytes 98336 | tf_op jit(solution)/shard_map/ppermute | solution.py:59
  25.5 2.1 %collective-permute-done.3.refs_2_ = bf16[96,512]{1,0:T(8,128)(2,1)S(1)} collective-permute-done((bf16[96,512]{1,0:T(8,128)(2,1)S(1)}, bf16[96,512]{1,0:T(8,128)(2,1)S(1)}, u32[]{:S(2)}, u32[]{:S(2)}) %collective-permute-start.3) | collective-permute-done | bytes 98336 | tf_op jit(solution)/shard_map/ppermute | solution.py:59
  27.6 3.9 %collective-permute-done.6.refs_1_ = bf16[80,2048]{1,0:T(8,128)(2,1)S(1)} collective-permute-done((bf16[80,2048]{1,0:T(8,128)(2,1)S(1)}, bf16[80,2048]{1,0:T(8,128)(2,1)S(1)}, u32[]{:S(2)}, u32[]{:S(2)}) %collective-permute-start.6) | collective-permute-done | bytes 327712 | tf_op jit(solution)/shard_map/ppermute | solution.py:59
  31.5 0.0 copy-start.6
  31.5 0.1 shard_map.107
  31.6 2.3 %collective-permute-start.10 = (bf16[80,512]{1,0:T(8,128)(2,1)S(1)}, bf16[80,512]{1,0:T(8,128)(2,1)S(1)}, u32[]{:S(2)}, u32[]{:S(2)}) collective-permute-start(bf16[80,512]{1,0:T(8,128)(2,1)S(1)} %get-tuple-element.75), channel_id=1, source_target_pairs={{0,12},{1,13},{2,14},{3,15},{4,8},{5,9},{6,10},{7,11},{8,4},{9,5},... | collective-permute-start | bytes 245768 | tf_op jit(solution)/shard_map/ppermute | solution.py:59
  33.9 0.1 collective-permute-start.8
  34.0 2.0 %collective-permute-start.9 = (bf16[80,512]{1,0:T(8,128)(2,1)S(1)}, bf16[80,512]{1,0:T(8,128)(2,1)S(1)}, u32[]{:S(2)}, u32[]{:S(2)}) collective-permute-start(bf16[80,512]{1,0:T(8,128)(2,1)S(1)} %get-tuple-element.74), channel_id=1, source_target_pairs={{0,8},{1,9},{2,10},{3,11},{4,12},{5,13},{6,14},{7,15},{8,0},{9,1},... | collective-permute-start | bytes 245768 | tf_op jit(solution)/shard_map/ppermute | solution.py:59
  36.1 0.1 collective-permute-start.11
  36.2 0.1 shard_map.110.refs_5_.refs_2_
  36.3 0.0 copy-start
  36.3 2.2 %shard_map.109 = (f32[512,768]{1,0:T(8,128)S(1)}, bf16[512,256]{1,0:T(8,128)(2,1)S(1)}) custom-call(bf16[512,768]{1,0:T(8,128)(2,1)S(1)} %copy-done.1, bf16[512,768]{1,0:T(8,128)(2,1)S(1)} %collective-permute-done.4.refs_1_, bf16[512,768]{1,0:T(8,128)(2,1)S(1)} %collective-permute-done.7.refs_2_, bf16[512,768]{1,0:T(8,128)(2,1)S(1)} %copy-done.2, ...), custom_call_target="tpu_custom_call" | custom-call | flops 235929600 | bytes 4980736 | tf_op jit(solution)/shard_map/pallas_call | solution.py:333
  38.6 1.6 %collective-permute-done.11.refs_5_ = bf16[48,512]{1,0:T(8,128)(2,1)S(1)} collective-permute-done((bf16[48,512]{1,0:T(8,128)(2,1)S(1)}, bf16[48,512]{1,0:T(8,128)(2,1)S(1)}, u32[]{:S(2)}, u32[]{:S(2)}) %collective-permute-start.11) | collective-permute-done | bytes 49184 | tf_op jit(solution)/shard_map/ppermute | solution.py:59
  40.2 0.3 collective-permute-done.8.refs_1_
  40.5 0.4 collective-permute-done.9.refs_2_
  40.9 0.1 shard_map.111
  41.0 0.5 collective-permute-start.12
  41.5 2.7 %collective-permute-start.13 = (bf16[80,512]{1,0:T(8,128)(2,1)S(1)}, bf16[80,512]{1,0:T(8,128)(2,1)S(1)}, u32[]{:S(2)}, u32[]{:S(2)}) collective-permute-start(bf16[80,512]{1,0:T(8,128)(2,1)S(1)} %get-tuple-element.91.refs_0_), channel_id=1, source_target_pairs={{0,8},{1,9},{2,10},{3,11},{4,12},{5,13},{6,14},{7,15},{8,0},{9,1},... | collective-permute-start | bytes 245768 | tf_op jit(solution)/shard_map/ppermute | solution.py:59
  44.2 1.2 %collective-permute-start.14 = (bf16[80,512]{1,0:T(8,128)(2,1)S(1)}, bf16[80,512]{1,0:T(8,128)(2,1)S(1)}, u32[]{:S(2)}, u32[]{:S(2)}) collective-permute-start(bf16[80,512]{1,0:T(8,128)(2,1)S(1)} %get-tuple-element.91.refs_0_), channel_id=1, source_target_pairs={{0,12},{1,13},{2,14},{3,15},{4,8},{5,9},{6,10},{7,11},{8,4},{9,5},... | collective-permute-start | bytes 245768 | tf_op jit(solution)/shard_map/ppermute | solution.py:59
  45.4 0.4 collective-permute-start.15
  45.9 3.6 %collective-permute-done.15.refs_1_ = bf16[48,512]{1,0:T(8,128)(2,1)S(1)} collective-permute-done((bf16[48,512]{1,0:T(8,128)(2,1)S(1)}, bf16[48,512]{1,0:T(8,128)(2,1)S(1)}, u32[]{:S(2)}, u32[]{:S(2)}) %collective-permute-start.15) | collective-permute-done | bytes 49184 | tf_op jit(solution)/shard_map/ppermute | solution.py:59
  49.5 0.0 collective-permute-done.13.refs_2_
  49.5 1.0 %collective-permute-done.14.refs_3_ = bf16[80,512]{1,0:T(8,128)(2,1)S(1)} collective-permute-done((bf16[80,512]{1,0:T(8,128)(2,1)S(1)}, bf16[80,512]{1,0:T(8,128)(2,1)S(1)}, u32[]{:S(2)}, u32[]{:S(2)}) %collective-permute-start.14) | collective-permute-done | bytes 81952 | tf_op jit(solution)/shard_map/ppermute | solution.py:59
  50.6 0.5 collective-permute-start.17
  51.1 1.5 %collective-permute-start.19 = (bf16[96,512]{1,0:T(8,128)(2,1)S(1)}, bf16[96,512]{1,0:T(8,128)(2,1)S(1)}, u32[]{:S(2)}, u32[]{:S(2)}) collective-permute-start(bf16[96,512]{1,0:T(8,128)(2,1)S(1)} %shard_map.113.refs_0_), channel_id=1, source_target_pairs={{0,4},{1,5},{2,6},{3,7},{4,0},{5,1},{6,2},{7,3},{8,12},{9,13},{10,... | collective-permute-start | bytes 294920 | tf_op jit(solution)/shard_map/ppermute | solution.py:59
  52.6 1.6 %collective-permute-start.20 = (bf16[96,512]{1,0:T(8,128)(2,1)S(1)}, bf16[96,512]{1,0:T(8,128)(2,1)S(1)}, u32[]{:S(2)}, u32[]{:S(2)}) collective-permute-start(bf16[96,512]{1,0:T(8,128)(2,1)S(1)} %shard_map.113.refs_0_), channel_id=1, source_target_pairs={{0,8},{1,9},{2,10},{3,11},{4,12},{5,13},{6,14},{7,15},{8,0},{9,1},... | collective-permute-start | bytes 294920 | tf_op jit(solution)/shard_map/ppermute | solution.py:59
  54.2 1.3 %collective-permute-start.21 = (bf16[96,512]{1,0:T(8,128)(2,1)S(1)}, bf16[96,512]{1,0:T(8,128)(2,1)S(1)}, u32[]{:S(2)}, u32[]{:S(2)}) collective-permute-start(bf16[96,512]{1,0:T(8,128)(2,1)S(1)} %shard_map.113.refs_0_), channel_id=1, source_target_pairs={{0,12},{1,13},{2,14},{3,15},{4,8},{5,9},{6,10},{7,11},{8,4},{9,5},... | collective-permute-start | bytes 294920 | tf_op jit(solution)/shard_map/ppermute | solution.py:59
  55.5 1.3 %collective-permute-done.19.refs_1_ = bf16[96,512]{1,0:T(8,128)(2,1)S(1)} collective-permute-done((bf16[96,512]{1,0:T(8,128)(2,1)S(1)}, bf16[96,512]{1,0:T(8,128)(2,1)S(1)}, u32[]{:S(2)}, u32[]{:S(2)}) %collective-permute-start.19) | collective-permute-done | bytes 98336 | tf_op jit(solution)/shard_map/ppermute | solution.py:59
  56.8 5.4 %collective-permute-done.20.refs_2_ = bf16[96,512]{1,0:T(8,128)(2,1)S(1)} collective-permute-done((bf16[96,512]{1,0:T(8,128)(2,1)S(1)}, bf16[96,512]{1,0:T(8,128)(2,1)S(1)}, u32[]{:S(2)}, u32[]{:S(2)}) %collective-permute-start.20) | collective-permute-done | bytes 98336 | tf_op jit(solution)/shard_map/ppermute | solution.py:59
  62.3 0.1 collective-permute-start.22
  62.3 0.5 collective-permute-start.16
  62.8 0.1 collective-permute-start.18
  62.9 1.5 %shard_map.115 = (f32[256,768]{1,0:T(8,128)S(1)}, f32[320,128]{1,0:T(8,128)S(1)}) custom-call(bf16[80,2048]{1,0:T(8,128)(2,1)S(1)} %shard_map.112.refs_0_, bf16[80,2048]{1,0:T(8,128)(2,1)S(1)} %collective-permute-done.17.refs_1_, bf16[96,2048]{1,0:T(8,128)(2,1)S(1)} %shard_map.114.refs_2_, bf16[2048,768]{1,0:T(8,128)(2,1)S(1)} %copy-done, ...), custom_call_target="tpu_custom_call" | custom-call | flops 905969664 | bytes 7700480 | tf_op jit(solution)/shard_map/pallas_call | solution.py:91
  64.4 0.1 collective-permute-done.16.refs_0_
  64.5 0.5 collective-permute-done.18.refs_1_
  65.0 1.5 %shard_map.116 = (f32[256,768]{1,0:T(8,128)S(1)}, bf16[320,128]{1,0:T(8,128)(2,1)S(1)}) custom-call(bf16[80,2048]{1,0:T(8,128)(2,1)S(1)} %collective-permute-done.16.refs_0_, bf16[80,2048]{1,0:T(8,128)(2,1)S(1)} %collective-permute-done.18.refs_1_, bf16[96,2048]{1,0:T(8,128)(2,1)S(1)} %collective-permute-done.22.refs_2_, bf16[2048,768]{1,0:T(8,128)(2,1)S(1)} %copy-done, ...), custom_call_target="tpu_custom_call" | custom-call | flops 905969664 | bytes 7618560 | tf_op jit(solution)/shard_map/pallas_call | solution.py:91
  66.5 0.2 collective-permute-start.23
  66.7 1.1 %collective-permute-done.23.refs_0_ = bf16[320,128]{1,0:T(8,128)(2,1)S(1)} collective-permute-done((bf16[320,128]{1,0:T(8,128)(2,1)S(1)}, bf16[320,128]{1,0:T(8,128)(2,1)S(1)}, u32[]{:S(2)}, u32[]{:S(2)}) %collective-permute-start.23) | collective-permute-done | bytes 81952 | tf_op jit(solution)/shard_map/ppermute | solution.py:59
  67.9 0.6 collective-permute-start.24
  68.4 4.0 %collective-permute-done.24.refs_0_ = bf16[320,128]{1,0:T(8,128)(2,1)S(1)} collective-permute-done((bf16[320,128]{1,0:T(8,128)(2,1)S(1)}, bf16[320,128]{1,0:T(8,128)(2,1)S(1)}, u32[]{:S(2)}, u32[]{:S(2)}) %collective-permute-start.24) | collective-permute-done | bytes 81952 | tf_op jit(solution)/shard_map/ppermute | solution.py:59
  72.5 2.4 %collective-permute-start.25 = (bf16[320,128]{1,0:T(8,128)(2,1)S(1)}, bf16[320,128]{1,0:T(8,128)(2,1)S(1)}, u32[]{:S(2)}, u32[]{:S(2)}) collective-permute-start(bf16[320,128]{1,0:T(8,128)(2,1)S(1)} %get-tuple-element.108), channel_id=1, source_target_pairs={{0,12},{1,13},{2,14},{3,15},{4,8},{5,9},{6,10},{7,11},{8,4},{9,5},... | collective-permute-start | bytes 245768 | tf_op jit(solution)/shard_map/ppermute | solution.py:59
  74.8 0.8 collective-permute-start.26
  75.6 1.3 %collective-permute-start.27 = (bf16[320,128]{1,0:T(8,128)(2,1)S(1)}, bf16[320,128]{1,0:T(8,128)(2,1)S(1)}, u32[]{:S(2)}, u32[]{:S(2)}) collective-permute-start(bf16[320,128]{1,0:T(8,128)(2,1)S(1)} %get-tuple-element.108), channel_id=1, source_target_pairs={{0,4},{1,5},{2,6},{3,7},{4,0},{5,1},{6,2},{7,3},{8,12},{9,13},{10,... | collective-permute-start | bytes 245768 | tf_op jit(solution)/shard_map/ppermute | solution.py:59
  76.9 2.7 %collective-permute-done.25.refs_0_ = bf16[320,128]{1,0:T(8,128)(2,1)S(1)} collective-permute-done((bf16[320,128]{1,0:T(8,128)(2,1)S(1)}, bf16[320,128]{1,0:T(8,128)(2,1)S(1)}, u32[]{:S(2)}, u32[]{:S(2)}) %collective-permute-start.25) | collective-permute-done | bytes 81952 | tf_op jit(solution)/shard_map/ppermute | solution.py:59
  79.6 2.9 %collective-permute-done.26.refs_1_ = bf16[320,128]{1,0:T(8,128)(2,1)S(1)} collective-permute-done((bf16[320,128]{1,0:T(8,128)(2,1)S(1)}, bf16[320,128]{1,0:T(8,128)(2,1)S(1)}, u32[]{:S(2)}, u32[]{:S(2)}) %collective-permute-start.26) | collective-permute-done | bytes 81952 | tf_op jit(solution)/shard_map/ppermute | solution.py:59
  82.6 0.1 collective-permute-start.28
  82.6 1.2 %shard_map.120 = (bf16[512,768]{1,0:T(8,128)(2,1)}, bf16[512,768]{1,0:T(8,128)(2,1)}) custom-call(bf16[320,128]{1,0:T(8,128)(2,1)S(1)} %shard_map.119.refs_0_, f32[256,768]{1,0:T(8,128)S(1)} %get-tuple-element.111.refs_1_, bf16[640,768]{1,0:T(8,128)(2,1)S(1)} %shard_map.110.refs_5_.refs_2_, bf16[512,768]{1,0:T(8,128)(2,1)S(1)} %copy-done.1, ...), custom_call_target="tpu_custom_call" | custom-call | flops 100663296 | bytes 2555904 | tf_op jit(solution)/shard_map/pallas_call | solution.py:500
  83.9 0.1 collective-permute-done.28.refs_0_
  83.9 1.2 %shard_map.121 = (bf16[512,768]{1,0:T(8,128)(2,1)}, bf16[512,768]{1,0:T(8,128)(2,1)}) custom-call(bf16[320,128]{1,0:T(8,128)(2,1)S(1)} %collective-permute-done.28.refs_0_, f32[256,768]{1,0:T(8,128)S(1)} %get-tuple-element.109.refs_1_, bf16[640,768]{1,0:T(8,128)(2,1)S(1)} %shard_map.110.refs_5_.refs_2_, ...), custom_call_target="tpu_custom_call", output_to_operand_aliasing={{0}: (5, {}), {1}: (6, {})} | custom-call | flops 100663296 | bytes 2555904 | tf_op jit(solution)/shard_map/pallas_call | solution.py:500
  (32 shorter events, 0.3 us)
Async XLA Ops:
  0.6 7.6 %copy-start.1 = (bf16[512,768]{1,0:T(8,128)(2,1)S(1)}, bf16[512,768]{1,0:T(8,128)(2,1)}, u32[]{:S(2)}) copy-start(bf16[512,768]{1,0:T(8,128)(2,1)} %refs_3_.9) | copy-start | bytes 2359300
  0.6 15.6 %collective-permute-start.4 = (bf16[512,768]{1,0:T(8,128)(2,1)}, bf16[512,768]{1,0:T(8,128)(2,1)S(1)}, u32[]{:S(2)}, u32[]{:S(2)}) collective-permute-start(bf16[512,768]{1,0:T(8,128)(2,1)} %refs_3_.9), channel_id=1, source_target_pairs={{0,1},{1,2},{2,3},{3,4},{4,5},{5,6},{6,7},{7,8},{8,9},{9,10},{10,1... | collective-permute-start | bytes 2359304 | tf_op jit(solution)/shard_map/ppermute | solution.py:50
  5.5 5.8 %collective-permute-start = (bf16[256,1024]{1,0:T(8,128)(2,1)S(1)}, bf16[256,1024]{1,0:T(8,128)(2,1)S(1)}, u32[]{:S(2)}, u32[]{:S(2)}) collective-permute-start(bf16[256,1024]{1,0:T(8,128)(2,1)S(1)} %get-tuple-element.60), channel_id=1, source_target_pairs={{0,1},{1,0},{2,3},{3,2},{4,5},{5,4},{6,7},{7,6},{8,9},{9,8},{10,11... | collective-permute-start | bytes 1572872 | tf_op jit(solution)/shard_map/ppermute | solution.py:59
  8.1 3.2 %collective-permute-start.1 = (bf16[256,1024]{1,0:T(8,128)(2,1)S(1)}, bf16[256,1024]{1,0:T(8,128)(2,1)S(1)}, u32[]{:S(2)}, u32[]{:S(2)}) collective-permute-start(bf16[256,1024]{1,0:T(8,128)(2,1)S(1)} %get-tuple-element.61), channel_id=1, source_target_pairs={{0,1},{1,0},{2,3},{3,2},{4,5},{5,4},{6,7},{7,6},{8,9},{9,8},{10,11... | collective-permute-start | bytes 1572872 | tf_op jit(solution)/shard_map/ppermute | solution.py:59
  8.2 19.4 %collective-permute-start.7 = (bf16[512,768]{1,0:T(8,128)(2,1)S(1)}, bf16[512,768]{1,0:T(8,128)(2,1)S(1)}, u32[]{:S(2)}, u32[]{:S(2)}) collective-permute-start(bf16[512,768]{1,0:T(8,128)(2,1)S(1)} %copy-done.1), channel_id=1, source_target_pairs={{0,15},{1,0},{2,1},{3,2},{4,3},{5,4},{6,5},{7,6},{8,7},{9,8},{10,9... | collective-permute-start | bytes 2359304 | tf_op jit(solution)/shard_map/ppermute | solution.py:50
  11.4 24.7 %copy-start.7 = (f32[768]{0:T(1024)S(1)}, f32[768]{0:T(1024)}, u32[]{:S(2)}) copy-start(f32[768]{0:T(1024)} %param.12) | copy-start | bytes 9220
  11.5 24.7 %copy-start.8 = (f32[768]{0:T(1024)S(1)}, f32[768]{0:T(1024)}, u32[]{:S(2)}) copy-start(f32[768]{0:T(1024)} %param.13) | copy-start | bytes 9220
  11.5 24.7 %copy-start.2 = (bf16[512,768]{1,0:T(8,128)(2,1)S(1)}, bf16[512,768]{1,0:T(8,128)(2,1)}, u32[]{:S(2)}) copy-start(bf16[512,768]{1,0:T(8,128)(2,1)} %o_ref.1) | copy-start | bytes 2359300
  11.6 19.8 %collective-permute-start.6 = (bf16[80,2048]{1,0:T(8,128)(2,1)S(1)}, bf16[80,2048]{1,0:T(8,128)(2,1)S(1)}, u32[]{:S(2)}, u32[]{:S(2)}) collective-permute-start(bf16[80,2048]{1,0:T(8,128)(2,1)S(1)} %get-tuple-element.69), channel_id=1, source_target_pairs={{0,2},{1,3},{2,0},{3,1},{4,6},{5,7},{6,4},{7,5},{8,10},{9,11},{10,... | collective-permute-start | bytes 983048 | tf_op jit(solution)/shard_map/ppermute | solution.py:59
  12.3 13.2 %collective-permute-start.2 = (bf16[96,512]{1,0:T(8,128)(2,1)S(1)}, bf16[96,512]{1,0:T(8,128)(2,1)S(1)}, u32[]{:S(2)}, u32[]{:S(2)}) collective-permute-start(bf16[96,512]{1,0:T(8,128)(2,1)S(1)} %get-tuple-element.65), channel_id=1, source_target_pairs={{0,4},{1,5},{2,6},{3,7},{4,0},{5,1},{6,2},{7,3},{8,12},{9,13},{10,... | collective-permute-start | bytes 294920 | tf_op jit(solution)/shard_map/ppermute | solution.py:59
  13.9 13.7 %collective-permute-start.3 = (bf16[96,512]{1,0:T(8,128)(2,1)S(1)}, bf16[96,512]{1,0:T(8,128)(2,1)S(1)}, u32[]{:S(2)}, u32[]{:S(2)}) collective-permute-start(bf16[96,512]{1,0:T(8,128)(2,1)S(1)} %get-tuple-element.66), channel_id=1, source_target_pairs={{0,8},{1,9},{2,10},{3,11},{4,12},{5,13},{6,14},{7,15},{8,0},{9,1},... | collective-permute-start | bytes 294920 | tf_op jit(solution)/shard_map/ppermute | solution.py:59
  16.2 15.3 %collective-permute-start.5 = (bf16[96,512]{1,0:T(8,128)(2,1)S(1)}, bf16[96,512]{1,0:T(8,128)(2,1)S(1)}, u32[]{:S(2)}, u32[]{:S(2)}) collective-permute-start(bf16[96,512]{1,0:T(8,128)(2,1)S(1)} %get-tuple-element.68), channel_id=1, source_target_pairs={{0,12},{1,13},{2,14},{3,15},{4,8},{5,9},{6,10},{7,11},{8,4},{9,5},... | collective-permute-start | bytes 294920 | tf_op jit(solution)/shard_map/ppermute | solution.py:59
  31.5 4.8 %copy-start.3 = (bf16[2,128,128]{2,1,0:T(8,128)(2,1)S(1)}, bf16[2,128,128]{2,1,0:T(8,128)(2,1)}, u32[]{:S(2)}) copy-start(bf16[2,128,128]{2,1,0:T(8,128)(2,1)} %constant.2.clone.refs_4_) | copy-start | bytes 196612
  31.5 4.8 %copy-start.4 = (f32[512]{0:T(512)S(1)}, f32[512]{0:T(512)}, u32[]{:S(2)}) copy-start(f32[512]{0:T(512)} %param.14) | copy-start | bytes 6148
  31.5 4.8 %copy-start.5 = (s32[512]{0:T(512)S(1)}, s32[512]{0:T(512)}, u32[]{:S(2)}) copy-start(s32[512]{0:T(512)} %param.15) | copy-start | bytes 6148
  31.5 4.8 %copy-start.6 = (s32[512]{0:T(512)S(1)}, s32[512]{0:T(512)}, u32[]{:S(2)}) copy-start(s32[512]{0:T(512)} %param.16) | copy-start | bytes 6148
  31.6 8.7 %collective-permute-start.10 = (bf16[80,512]{1,0:T(8,128)(2,1)S(1)}, bf16[80,512]{1,0:T(8,128)(2,1)S(1)}, u32[]{:S(2)}, u32[]{:S(2)}) collective-permute-start(bf16[80,512]{1,0:T(8,128)(2,1)S(1)} %get-tuple-element.75), channel_id=1, source_target_pairs={{0,12},{1,13},{2,14},{3,15},{4,8},{5,9},{6,10},{7,11},{8,4},{9,5},... | collective-permute-start | bytes 245768 | tf_op jit(solution)/shard_map/ppermute | solution.py:59
  33.9 6.6 %collective-permute-start.8 = (bf16[80,512]{1,0:T(8,128)(2,1)S(1)}, bf16[80,512]{1,0:T(8,128)(2,1)S(1)}, u32[]{:S(2)}, u32[]{:S(2)}) collective-permute-start(bf16[80,512]{1,0:T(8,128)(2,1)S(1)} %get-tuple-element.73), channel_id=1, source_target_pairs={{0,4},{1,5},{2,6},{3,7},{4,0},{5,1},{6,2},{7,3},{8,12},{9,13},{10,... | collective-permute-start | bytes 245768 | tf_op jit(solution)/shard_map/ppermute | solution.py:59
  34.0 6.9 %collective-permute-start.9 = (bf16[80,512]{1,0:T(8,128)(2,1)S(1)}, bf16[80,512]{1,0:T(8,128)(2,1)S(1)}, u32[]{:S(2)}, u32[]{:S(2)}) collective-permute-start(bf16[80,512]{1,0:T(8,128)(2,1)S(1)} %get-tuple-element.74), channel_id=1, source_target_pairs={{0,8},{1,9},{2,10},{3,11},{4,12},{5,13},{6,14},{7,15},{8,0},{9,1},... | collective-permute-start | bytes 245768 | tf_op jit(solution)/shard_map/ppermute | solution.py:59
  36.1 4.2 %collective-permute-start.11 = (bf16[48,512]{1,0:T(8,128)(2,1)S(1)}, bf16[48,512]{1,0:T(8,128)(2,1)S(1)}, u32[]{:S(2)}, u32[]{:S(2)}) collective-permute-start(bf16[48,512]{1,0:T(8,128)(2,1)S(1)} %get-tuple-element.80), channel_id=1, source_target_pairs={{0,2},{1,3},{2,0},{3,1},{4,6},{5,7},{6,4},{7,5},{8,10},{9,11},{10,... | collective-permute-start | bytes 147464 | tf_op jit(solution)/shard_map/ppermute | solution.py:59
  36.3 26.6 %copy-start = (bf16[2048,768]{1,0:T(8,128)(2,1)S(1)}, bf16[2048,768]{1,0:T(8,128)(2,1)}, u32[]{:S(2)}) copy-start(bf16[2048,768]{1,0:T(8,128)(2,1)} %refs_3_.7) | copy-start | bytes 9437188
  41.0 8.5 %collective-permute-start.12 = (bf16[80,512]{1,0:T(8,128)(2,1)S(1)}, bf16[80,512]{1,0:T(8,128)(2,1)S(1)}, u32[]{:S(2)}, u32[]{:S(2)}) collective-permute-start(bf16[80,512]{1,0:T(8,128)(2,1)S(1)} %get-tuple-element.91.refs_0_), channel_id=1, source_target_pairs={{0,4},{1,5},{2,6},{3,7},{4,0},{5,1},{6,2},{7,3},{8,12},{9,13},{10,... | collective-permute-start | bytes 245768 | tf_op jit(solution)/shard_map/ppermute | solution.py:59
  41.5 8.0 %collective-permute-start.13 = (bf16[80,512]{1,0:T(8,128)(2,1)S(1)}, bf16[80,512]{1,0:T(8,128)(2,1)S(1)}, u32[]{:S(2)}, u32[]{:S(2)}) collective-permute-start(bf16[80,512]{1,0:T(8,128)(2,1)S(1)} %get-tuple-element.91.refs_0_), channel_id=1, source_target_pairs={{0,8},{1,9},{2,10},{3,11},{4,12},{5,13},{6,14},{7,15},{8,0},{9,1},... | collective-permute-start | bytes 245768 | tf_op jit(solution)/shard_map/ppermute | solution.py:59
  44.2 6.3 %collective-permute-start.14 = (bf16[80,512]{1,0:T(8,128)(2,1)S(1)}, bf16[80,512]{1,0:T(8,128)(2,1)S(1)}, u32[]{:S(2)}, u32[]{:S(2)}) collective-permute-start(bf16[80,512]{1,0:T(8,128)(2,1)S(1)} %get-tuple-element.91.refs_0_), channel_id=1, source_target_pairs={{0,12},{1,13},{2,14},{3,15},{4,8},{5,9},{6,10},{7,11},{8,4},{9,5},... | collective-permute-start | bytes 245768 | tf_op jit(solution)/shard_map/ppermute | solution.py:59
  45.4 4.1 %collective-permute-start.15 = (bf16[48,512]{1,0:T(8,128)(2,1)S(1)}, bf16[48,512]{1,0:T(8,128)(2,1)S(1)}, u32[]{:S(2)}, u32[]{:S(2)}) collective-permute-start(bf16[48,512]{1,0:T(8,128)(2,1)S(1)} %get-tuple-element.95.refs_0_), channel_id=1, source_target_pairs={{0,2},{1,3},{2,0},{3,1},{4,6},{5,7},{6,4},{7,5},{8,10},{9,11},{10,... | collective-permute-start | bytes 147464 | tf_op jit(solution)/shard_map/ppermute | solution.py:59
  50.6 12.3 %collective-permute-start.17 = (bf16[80,2048]{1,0:T(8,128)(2,1)S(1)}, bf16[80,2048]{1,0:T(8,128)(2,1)S(1)}, u32[]{:S(2)}, u32[]{:S(2)}) collective-permute-start(bf16[80,2048]{1,0:T(8,128)(2,1)S(1)} %shard_map.112.refs_0_), channel_id=1, source_target_pairs={{0,2},{1,3},{2,0},{3,1},{4,6},{5,7},{6,4},{7,5},{8,10},{9,11},{10,... | collective-permute-start | bytes 983048 | tf_op jit(solution)/shard_map/ppermute | solution.py:59
  51.1 5.7 %collective-permute-start.19 = (bf16[96,512]{1,0:T(8,128)(2,1)S(1)}, bf16[96,512]{1,0:T(8,128)(2,1)S(1)}, u32[]{:S(2)}, u32[]{:S(2)}) collective-permute-start(bf16[96,512]{1,0:T(8,128)(2,1)S(1)} %shard_map.113.refs_0_), channel_id=1, source_target_pairs={{0,4},{1,5},{2,6},{3,7},{4,0},{5,1},{6,2},{7,3},{8,12},{9,13},{10,... | collective-permute-start | bytes 294920 | tf_op jit(solution)/shard_map/ppermute | solution.py:59
  52.6 9.6 %collective-permute-start.20 = (bf16[96,512]{1,0:T(8,128)(2,1)S(1)}, bf16[96,512]{1,0:T(8,128)(2,1)S(1)}, u32[]{:S(2)}, u32[]{:S(2)}) collective-permute-start(bf16[96,512]{1,0:T(8,128)(2,1)S(1)} %shard_map.113.refs_0_), channel_id=1, source_target_pairs={{0,8},{1,9},{2,10},{3,11},{4,12},{5,13},{6,14},{7,15},{8,0},{9,1},... | collective-permute-start | bytes 294920 | tf_op jit(solution)/shard_map/ppermute | solution.py:59
  54.2 8.0 %collective-permute-start.21 = (bf16[96,512]{1,0:T(8,128)(2,1)S(1)}, bf16[96,512]{1,0:T(8,128)(2,1)S(1)}, u32[]{:S(2)}, u32[]{:S(2)}) collective-permute-start(bf16[96,512]{1,0:T(8,128)(2,1)S(1)} %shard_map.113.refs_0_), channel_id=1, source_target_pairs={{0,12},{1,13},{2,14},{3,15},{4,8},{5,9},{6,10},{7,11},{8,4},{9,5},... | collective-permute-start | bytes 294920 | tf_op jit(solution)/shard_map/ppermute | solution.py:59
  62.3 2.3 %collective-permute-start.22 = (bf16[96,2048]{1,0:T(8,128)(2,1)S(1)}, bf16[96,2048]{1,0:T(8,128)(2,1)S(1)}, u32[]{:S(2)}, u32[]{:S(2)}) collective-permute-start(bf16[96,2048]{1,0:T(8,128)(2,1)S(1)} %shard_map.114.refs_2_), channel_id=1, source_target_pairs={{0,1},{1,0},{2,3},{3,2},{4,5},{5,4},{6,7},{7,6},{8,9},{9,8},{10,11... | collective-permute-start | bytes 1179656 | tf_op jit(solution)/shard_map/ppermute | solution.py:59
  62.3 2.2 %collective-permute-start.16 = (bf16[80,2048]{1,0:T(8,128)(2,1)S(1)}, bf16[80,2048]{1,0:T(8,128)(2,1)S(1)}, u32[]{:S(2)}, u32[]{:S(2)}) collective-permute-start(bf16[80,2048]{1,0:T(8,128)(2,1)S(1)} %shard_map.112.refs_0_), channel_id=1, source_target_pairs={{0,1},{1,0},{2,3},{3,2},{4,5},{5,4},{6,7},{7,6},{8,9},{9,8},{10,11... | collective-permute-start | bytes 983048 | tf_op jit(solution)/shard_map/ppermute | solution.py:59
  62.8 2.1 %collective-permute-start.18 = (bf16[80,2048]{1,0:T(8,128)(2,1)S(1)}, bf16[80,2048]{1,0:T(8,128)(2,1)S(1)}, u32[]{:S(2)}, u32[]{:S(2)}) collective-permute-start(bf16[80,2048]{1,0:T(8,128)(2,1)S(1)} %collective-permute-done.17.refs_1_), channel_id=1, source_target_pairs={{0,1},{1,0},{2,3},{3,2},{4,5},{5,4},{6,7},{7,6},{8,9},{9,8},{10,11... | collective-permute-start | bytes 983048 | tf_op jit(solution)/shard_map/ppermute | solution.py:59
  66.5 1.3 %collective-permute-start.23 = (bf16[320,128]{1,0:T(8,128)(2,1)S(1)}, bf16[320,128]{1,0:T(8,128)(2,1)S(1)}, u32[]{:S(2)}, u32[]{:S(2)}) collective-permute-start(bf16[320,128]{1,0:T(8,128)(2,1)S(1)} %get-tuple-element.104), channel_id=1, source_target_pairs={{0,1},{1,0},{2,3},{3,2},{4,5},{5,4},{6,7},{7,6},{8,9},{9,8},{10,11... | collective-permute-start | bytes 245768 | tf_op jit(solution)/shard_map/ppermute | solution.py:59
  67.9 4.6 %collective-permute-start.24 = (bf16[320,128]{1,0:T(8,128)(2,1)S(1)}, bf16[320,128]{1,0:T(8,128)(2,1)S(1)}, u32[]{:S(2)}, u32[]{:S(2)}) collective-permute-start(bf16[320,128]{1,0:T(8,128)(2,1)S(1)} %get-tuple-element.106), channel_id=1, source_target_pairs={{0,2},{1,3},{2,0},{3,1},{4,6},{5,7},{6,4},{7,5},{8,10},{9,11},{10,... | collective-permute-start | bytes 245768 | tf_op jit(solution)/shard_map/ppermute | solution.py:59
  72.5 7.2 %collective-permute-start.25 = (bf16[320,128]{1,0:T(8,128)(2,1)S(1)}, bf16[320,128]{1,0:T(8,128)(2,1)S(1)}, u32[]{:S(2)}, u32[]{:S(2)}) collective-permute-start(bf16[320,128]{1,0:T(8,128)(2,1)S(1)} %get-tuple-element.108), channel_id=1, source_target_pairs={{0,12},{1,13},{2,14},{3,15},{4,8},{5,9},{6,10},{7,11},{8,4},{9,5},... | collective-permute-start | bytes 245768 | tf_op jit(solution)/shard_map/ppermute | solution.py:59
  74.8 7.7 %collective-permute-start.26 = (bf16[320,128]{1,0:T(8,128)(2,1)S(1)}, bf16[320,128]{1,0:T(8,128)(2,1)S(1)}, u32[]{:S(2)}, u32[]{:S(2)}) collective-permute-start(bf16[320,128]{1,0:T(8,128)(2,1)S(1)} %get-tuple-element.108), channel_id=1, source_target_pairs={{0,8},{1,9},{2,10},{3,11},{4,12},{5,13},{6,14},{7,15},{8,0},{9,1},... | collective-permute-start | bytes 245768 | tf_op jit(solution)/shard_map/ppermute | solution.py:59
  75.6 6.9 %collective-permute-start.27 = (bf16[320,128]{1,0:T(8,128)(2,1)S(1)}, bf16[320,128]{1,0:T(8,128)(2,1)S(1)}, u32[]{:S(2)}, u32[]{:S(2)}) collective-permute-start(bf16[320,128]{1,0:T(8,128)(2,1)S(1)} %get-tuple-element.108), channel_id=1, source_target_pairs={{0,4},{1,5},{2,6},{3,7},{4,0},{5,1},{6,2},{7,3},{8,12},{9,13},{10,... | collective-permute-start | bytes 245768 | tf_op jit(solution)/shard_map/ppermute | solution.py:59
  82.6 1.3 %collective-permute-start.28 = (bf16[320,128]{1,0:T(8,128)(2,1)S(1)}, bf16[320,128]{1,0:T(8,128)(2,1)S(1)}, u32[]{:S(2)}, u32[]{:S(2)}) collective-permute-start(bf16[320,128]{1,0:T(8,128)(2,1)S(1)} %shard_map.119.refs_0_), channel_id=1, source_target_pairs={{0,1},{1,0},{2,3},{3,2},{4,5},{5,4},{6,7},{7,6},{8,9},{9,8},{10,11... | collective-permute-start | bytes 245768 | tf_op jit(solution)/shard_map/ppermute | solution.py:59

commit v22 on v18

--- a/solution.py
+++ b/solution.py
@@ -28,7 +28,7 @@
 STEP_SIZE = 0.3
 MIB = 1024 * 1024
 VMEM_BYTES = 24 * MIB
-REDUCE_SHARE = 0.625
+REDUCE_SHARE = 0.5
 GATHER_SHARE = 0.5
 BF16 = jnp.bfloat16
 F32 = jnp.float32
@@ -113,8 +113,7 @@
 
 
 def first_body(core, block, tile, r_ref, p_ref, *refs):
-    sent_low, sent_high, keep_x, keep_z, r_held, p_held, r_sem, p_sem = refs
-    width = sent_low.shape[1]
+    sent_x, sent_z, keep_x, keep_z, r_held, p_held, r_sem, p_sem = refs
     rows = r_held.shape[0] // 2
     r_copy = pltpu.make_async_copy(r_ref, r_held, r_sem)
     r_copy.start()
@@ -128,28 +127,23 @@
     for t, copy in enumerate(copies):
         copy.wait()
         cols = slice(t * tile, (t + 1) * tile)
-        for side in (1 - c, c):
+        for side, x_ref, z_ref in ((1 - c, sent_x, sent_z), (c, keep_x, keep_z)):
             part = lax.dot_general(
                 r_held[pl.ds(pl.multiple_of(side * rows, rows), rows), :],
                 p_held[cols, :],
                 NT,
                 preferred_element_type=F32,
             )
-            if side is c:
-                cut(part, block, keep_x, keep_z, cols)
-            else:
-                ref, first = (sent_low, 0) if t * tile < width else (sent_high, width)
-                ref[:, t * tile - first : (t + 1) * tile - first] = part.astype(BF16)
+            cut(part, block, x_ref, z_ref, cols)
 
 
 def first_sums(response, projectors, core, block, first):
     bands, cells = response.shape
     count = projectors.shape[0]
     rows = bands // 2
-    tile = min(512, count // 2)
+    tile = min(512, count)
     rows_x = rows // block * first
-    outs = [struct((rows, count // 2), BF16)] * 2
-    outs += [struct((n, count), F32) for n in (rows_x, rows - rows_x)]
+    outs = [struct((n, count), t) for t in (BF16, F32) for n in (rows_x, rows - rows_x)]
     return pl.pallas_call(
         functools.partial(first_body, core, block, tile),
         out_shape=outs,
@@ -182,35 +176,6 @@
     for ref in taken:
         total = total + ref[part].astype(F32)
     return total
-
-
-def first_x_body(level, block, keep_ref, low_ref, high_ref, *outs):
-    me = position(level)
-    rows = outs[0].shape[0]
-    half = low_ref.shape[1]
-    for step, out in enumerate(outs):
-        at = me ^ step
-        mine = rows_at(at, rows)
-        theirs = pl.ds(pl.multiple_of(at * block, 16), rows)
-        for k, ref in enumerate((low_ref, high_ref)):
-            cols = slice(k * half, (k + 1) * half)
-            out[:, cols] = (keep_ref[mine, cols] + ref[theirs, :].astype(F32)).astype(out.dtype)
-
-
-def first_z_body(level, block, first, keep_ref, low_ref, high_ref, *outs):
-    me = position(level)
-    rows = block - first
-    width = outs[0].shape[1]
-    per = low_ref.shape[1] // width
-    for step, out in enumerate(outs):
-        at = me ^ step
-        cols = cols_at(at, width)
-        near = cols_at(lax.rem(at, jnp.int32(per)), width)
-        for i in range(out.shape[0] // rows):
-            mine = slice(i * rows, (i + 1) * rows)
-            theirs = slice(i * block + first, (i + 1) * block)
-            taken = jnp.where(at < per, low_ref[theirs, near], high_ref[theirs, near])
-            out[mine, :] = (keep_ref[mine, cols] + taken.astype(F32)).astype(out.dtype)
 
 
 def split_body(received, level, along, *refs):
@@ -543,29 +508,22 @@
     low = neighbour(response[:, local_cells - halo :], count, 1)
     high = neighbour(response[:, :halo], count, -1)
 
-    *sent, keep_x, keep_z = first_sums(response, projectors, core, block, first)
-    sent = [swapped(part, count, core, 1) for part in sent]
-    keep_z, *parts_z = local_call(
-        functools.partial(first_z_body, along, block, first),
-        shares_of((keep_z.shape[0], projections // along[0]), along[0]),
-        [keep_z, *sent],
-    )
-    keep_x, parts_z[0] = lax.optimization_barrier((keep_x, parts_z[0]))
-    keep_x, *parts_x = local_call(
-        functools.partial(first_x_body, across, block),
-        shares_of((first, projections), across[0]),
-        [keep_x, *sent],
-    )
+    sent_x, sent_z, keep_x, keep_z = first_sums(response, projectors, core, block, first)
+    sent_z = swapped(sent_z, count, core, 1)
+    sent_x = swapped(sent_x, count, core, 1)
+    keep_z, *parts_z = split(keep_z, [sent_z], along, 1)
+    sent_x, parts_z[0] = lax.optimization_barrier((sent_x, parts_z[0]))
+    keep_x, *parts_x = split(keep_x, [sent_x], across, 0)
     parts_z[-1], low = lax.optimization_barrier((parts_z[-1], low))
     taken_z, taken_x, low, high = lax.optimization_barrier(
         (parts_to(parts_z, along), parts_to(parts_x, across), low, high)
     )
+    base, mask = local_part(
+        response, low, high, orbitals, matrix, lines, bounds, group_rows, width, blk
+    )
+    padded = pad_orbitals(orbitals, blk)
     keep_x, *parts_x = split(keep_x, taken_x, along, 1)
     keep_z, *parts_z = split(keep_z, taken_z, across, 0)
-    base, mask = local_part(
-        response, low, high, orbitals, matrix, lines, bounds, group_rows, width, blk
-    )
-    padded = pad_orbitals(orbitals, blk)
     taken_x, taken_z, base, padded = lax.optimization_barrier(
         (parts_to(parts_x, along), parts_to(parts_z, across), base, padded)
     )
@@ -593,7 +551,8 @@
     other_wide, part = apply(others, projectors, base, padded, *sizes, True)
     total, part = add_up(keep, to(part, core))
     total, part = add_up(total, to(part, across))
-    own = finish(total, to(part, along), window_scale)
+    far_first = [swapped(part, count, along, k) for k in reversed(range(1, along[0]))]
+    own = finish(total, far_first, window_scale)
     (theirs,) = to(own, core)
     outs = project(own, wide, padded, response, mask, core, blk, False, ())
     return project(theirs, other_wide, padded, response, mask, core, blk, True, outs)

time: 85.8 us -> 85.6 us (level)
  waiting for transfers between devices: 39.3 us -> 34.3 us
  starting transfers between devices: 32.7 us -> 37.4 us
    ppermute x27, waiting for transfers between devices: 38.4 us -> 33.3 us  [swapped(): return lax.ppermute(array, 'band', pairs)]
    ppermute x27, starting transfers between devices: 29.1 us -> 33.7 us  [swapped(): return lax.ppermute(array, 'band', pairs)]
  transfers between devices with their start and end apart: 29 -> 29, of which waited for: 18 -> 15; matrix products, arithmetic and copies ran while one was open for 0% -> 0% of each run, Pallas kernels for 11% -> 11%
where the time goes in v22:
time: 85.6 us; the launch traced here: 85.4 us
  starting transfers between devices  37.4 us (44%)
  waiting for transfers between devices  34.3 us (40%)
  Pallas kernels  12.7 us (15%)
  between operations  0.94 us (1%)
    ppermute x27, starting transfers between devices, swapped(): return lax.ppermute(array, 'band', pairs)  33.7 us
    ppermute x27, waiting for transfers between devices, swapped(): return lax.ppermute(array, 'band', pairs)  33.3 us
    pallas_call x1, Pallas kernels, first_sums(): pl.pallas_call(functools.partial(first_body, core, block, tile), out_shap...  4.34 us
    pallas_call x14, Pallas kernels, local_call(): pl.pallas_call(body, out_shape=outs, in_specs=[whole() for _ in args], ou...  3.72 us
    ppermute x2, starting transfers between devices, neighbour(): lax.ppermute(array, 'band', [(i, (i + step) % count) for i in range(count)])  3.62 us
    pallas_call x2, Pallas kernels, project(): pl.pallas_call(functools.partial(project_body, core, blk, other), out_sha...  2.4 us
    pallas_call x1, Pallas kernels, local_part(): pl.pallas_call(functools.partial(local_body, depth, (group_rows, blk)), g...  2.27 us
  transfers between devices with their start and end apart: 29, of which 15 were waited for; matrix products, arithmetic and copies ran while one was open for 0% of the time, Pallas kernels for 11%

profile of v22, /device:TPU:0, one launch (start us, length us, event | category | flops | bytes accessed | tf_op | source)
XLA Modules:
  0.0 85.4 jit_solution(4046788064630425490)
XLA Ops:
  0.6 0.5 collective-permute-start.4
  1.1 4.3 %shard_map.104 = (bf16[128,2048]{1,0:T(8,128)(2,1)S(1)}, bf16[128,2048]{1,0:T(8,128)(2,1)S(1)}, f32[128,2048]{1,0:T(8,128)S(1)}, f32[128,2048]{1,0:T(8,128)S(1)}) custom-call(bf16[512,768]{1,0:T(8,128)(2,1)} %refs_3_.9, bf16[2048,768]{1,0:T(8,128)(2,1)} %refs_3_.7), custom_call_target="tpu_custom_call" | custom-call | flops 1610612736 | bytes 6291456 | tf_op jit(solution)/shard_map/pallas_call | solution.py:147
  5.5 0.0 copy-start.7
  5.5 0.0 copy-start.8
  5.5 0.0 copy-start.2
  5.5 2.6 %collective-permute-start.1 = (bf16[128,2048]{1,0:T(8,128)(2,1)S(1)}, bf16[128,2048]{1,0:T(8,128)(2,1)S(1)}, u32[]{:S(2)}, u32[]{:S(2)}) collective-permute-start(bf16[128,2048]{1,0:T(8,128)(2,1)S(1)} %get-tuple-element.61), channel_id=1, source_target_pairs={{0,1},{1,0},{2,3},{3,2},{4,5},{5,4},{6,7},{7,6},{8,9},{9,8},{10,11... | collective-permute-start | bytes 1572872 | tf_op jit(solution)/shard_map/ppermute | solution.py:59
  8.2 0.1 collective-permute-start
  8.2 3.1 %collective-permute-start.7 = (bf16[512,768]{1,0:T(8,128)(2,1)S(1)}, bf16[512,768]{1,0:T(8,128)(2,1)S(1)}, u32[]{:S(2)}, u32[]{:S(2)}) collective-permute-start(bf16[512,768]{1,0:T(8,128)(2,1)S(1)} %copy-done.1), channel_id=1, source_target_pairs={{0,15},{1,0},{2,1},{3,2},{4,3},{5,4},{6,5},{7,6},{8,7},{9,8},{10,9... | collective-permute-start | bytes 2359304 | tf_op jit(solution)/shard_map/ppermute | solution.py:50
  11.4 0.0 copy-start.6
  11.4 0.1 shard_map.105
  11.5 0.0 collective-permute-done.refs_1_
  11.5 0.1 shard_map.106
  11.7 0.5 collective-permute-start.6
  12.2 1.6 %collective-permute-start.2 = (bf16[128,512]{1,0:T(8,128)(2,1)S(1)}, bf16[128,512]{1,0:T(8,128)(2,1)S(1)}, u32[]{:S(2)}, u32[]{:S(2)}) collective-permute-start(bf16[128,512]{1,0:T(8,128)(2,1)S(1)} %get-tuple-element.65), channel_id=1, source_target_pairs={{0,4},{1,5},{2,6},{3,7},{4,0},{5,1},{6,2},{7,3},{8,12},{9,13},{10,... | collective-permute-start | bytes 393224 | tf_op jit(solution)/shard_map/ppermute | solution.py:59
  13.8 1.4 %collective-permute-start.3 = (bf16[128,512]{1,0:T(8,128)(2,1)S(1)}, bf16[128,512]{1,0:T(8,128)(2,1)S(1)}, u32[]{:S(2)}, u32[]{:S(2)}) collective-permute-start(bf16[128,512]{1,0:T(8,128)(2,1)S(1)} %get-tuple-element.66), channel_id=1, source_target_pairs={{0,8},{1,9},{2,10},{3,11},{4,12},{5,13},{6,14},{7,15},{8,0},{9,1},... | collective-permute-start | bytes 393224 | tf_op jit(solution)/shard_map/ppermute | solution.py:59
  15.1 1.1 %collective-permute-done.4.refs_1_ = bf16[512,768]{1,0:T(8,128)(2,1)S(1)} collective-permute-done((bf16[512,768]{1,0:T(8,128)(2,1)}, bf16[512,768]{1,0:T(8,128)(2,1)S(1)}, u32[]{:S(2)}, u32[]{:S(2)}) %collective-permute-start.4) | collective-permute-done | bytes 786464 | tf_op jit(solution)/shard_map/ppermute | solution.py:50
  16.2 2.2 %collective-permute-start.5 = (bf16[128,512]{1,0:T(8,128)(2,1)S(1)}, bf16[128,512]{1,0:T(8,128)(2,1)S(1)}, u32[]{:S(2)}, u32[]{:S(2)}) collective-permute-start(bf16[128,512]{1,0:T(8,128)(2,1)S(1)} %get-tuple-element.68), channel_id=1, source_target_pairs={{0,12},{1,13},{2,14},{3,15},{4,8},{5,9},{6,10},{7,11},{8,4},{9,5},... | collective-permute-start | bytes 393224 | tf_op jit(solution)/shard_map/ppermute | solution.py:59
  18.4 8.6 %collective-permute-done.2.refs_1_ = bf16[128,512]{1,0:T(8,128)(2,1)S(1)} collective-permute-done((bf16[128,512]{1,0:T(8,128)(2,1)S(1)}, bf16[128,512]{1,0:T(8,128)(2,1)S(1)}, u32[]{:S(2)}, u32[]{:S(2)}) %collective-permute-start.2) | collective-permute-done | bytes 131104 | tf_op jit(solution)/shard_map/ppermute | solution.py:59
  26.9 5.2 %collective-permute-done.3.refs_2_ = bf16[128,512]{1,0:T(8,128)(2,1)S(1)} collective-permute-done((bf16[128,512]{1,0:T(8,128)(2,1)S(1)}, bf16[128,512]{1,0:T(8,128)(2,1)S(1)}, u32[]{:S(2)}, u32[]{:S(2)}) %collective-permute-start.3) | collective-permute-done | bytes 131104 | tf_op jit(solution)/shard_map/ppermute | solution.py:59
  32.1 0.0 collective-permute-done.6.refs_1_
  32.1 0.0 collective-permute-done.7.refs_2_
  32.2 0.0 collective-permute-done.5.refs_3_
  32.2 0.1 shard_map.108
  32.2 0.1 collective-permute-start.11
  32.3 0.1 shard_map.107
  32.4 2.7 %collective-permute-start.10 = (bf16[64,512]{1,0:T(8,128)(2,1)S(1)}, bf16[64,512]{1,0:T(8,128)(2,1)S(1)}, u32[]{:S(2)}, u32[]{:S(2)}) collective-permute-start(bf16[64,512]{1,0:T(8,128)(2,1)S(1)} %get-tuple-element.75), channel_id=1, source_target_pairs={{0,12},{1,13},{2,14},{3,15},{4,8},{5,9},{6,10},{7,11},{8,4},{9,5},... | collective-permute-start | bytes 196616 | tf_op jit(solution)/shard_map/ppermute | solution.py:59
  35.1 1.8 %collective-permute-start.8 = (bf16[64,512]{1,0:T(8,128)(2,1)S(1)}, bf16[64,512]{1,0:T(8,128)(2,1)S(1)}, u32[]{:S(2)}, u32[]{:S(2)}) collective-permute-start(bf16[64,512]{1,0:T(8,128)(2,1)S(1)} %get-tuple-element.73), channel_id=1, source_target_pairs={{0,4},{1,5},{2,6},{3,7},{4,0},{5,1},{6,2},{7,3},{8,12},{9,13},{10,... | collective-permute-start | bytes 196616 | tf_op jit(solution)/shard_map/ppermute | solution.py:59
  37.0 0.1 shard_map.110.refs_5_.refs_2_
  37.1 0.0 copy-start
  37.1 2.3 %shard_map.109 = (f32[512,768]{1,0:T(8,128)S(1)}, bf16[512,256]{1,0:T(8,128)(2,1)S(1)}) custom-call(bf16[512,768]{1,0:T(8,128)(2,1)S(1)} %copy-done.1, bf16[512,768]{1,0:T(8,128)(2,1)S(1)} %collective-permute-done.4.refs_1_, bf16[512,768]{1,0:T(8,128)(2,1)S(1)} %collective-permute-done.7.refs_2_, bf16[512,768]{1,0:T(8,128)(2,1)S(1)} %copy-done.2, ...), custom_call_target="tpu_custom_call" | custom-call | flops 235929600 | bytes 4980736 | tf_op jit(solution)/shard_map/pallas_call | solution.py:298
  39.4 0.2 collective-permute-done.8.refs_1_
  39.6 2.8 %collective-permute-done.9.refs_2_ = bf16[64,512]{1,0:T(8,128)(2,1)S(1)} collective-permute-done((bf16[64,512]{1,0:T(8,128)(2,1)S(1)}, bf16[64,512]{1,0:T(8,128)(2,1)S(1)}, u32[]{:S(2)}, u32[]{:S(2)}) %collective-permute-start.9) | collective-permute-done | bytes 65568 | tf_op jit(solution)/shard_map/ppermute | solution.py:59
  42.4 0.1 shard_map.111
  42.5 0.1 collective-permute-start.12
  42.6 2.8 %collective-permute-start.13 = (bf16[64,512]{1,0:T(8,128)(2,1)S(1)}, bf16[64,512]{1,0:T(8,128)(2,1)S(1)}, u32[]{:S(2)}, u32[]{:S(2)}) collective-permute-start(bf16[64,512]{1,0:T(8,128)(2,1)S(1)} %get-tuple-element.91.refs_0_), channel_id=1, source_target_pairs={{0,8},{1,9},{2,10},{3,11},{4,12},{5,13},{6,14},{7,15},{8,0},{9,1},... | collective-permute-start | bytes 196616 | tf_op jit(solution)/shard_map/ppermute | solution.py:59
  45.4 1.5 %collective-permute-start.14 = (bf16[64,512]{1,0:T(8,128)(2,1)S(1)}, bf16[64,512]{1,0:T(8,128)(2,1)S(1)}, u32[]{:S(2)}, u32[]{:S(2)}) collective-permute-start(bf16[64,512]{1,0:T(8,128)(2,1)S(1)} %get-tuple-element.91.refs_0_), channel_id=1, source_target_pairs={{0,12},{1,13},{2,14},{3,15},{4,8},{5,9},{6,10},{7,11},{8,4},{9,5},... | collective-permute-start | bytes 196616 | tf_op jit(solution)/shard_map/ppermute | solution.py:59
  47.0 2.0 %collective-permute-start.15 = (bf16[64,512]{1,0:T(8,128)(2,1)S(1)}, bf16[64,512]{1,0:T(8,128)(2,1)S(1)}, u32[]{:S(2)}, u32[]{:S(2)}) collective-permute-start(bf16[64,512]{1,0:T(8,128)(2,1)S(1)} %get-tuple-element.95.refs_0_), channel_id=1, source_target_pairs={{0,2},{1,3},{2,0},{3,1},{4,6},{5,7},{6,4},{7,5},{8,10},{9,11},{10,... | collective-permute-start | bytes 196616 | tf_op jit(solution)/shard_map/ppermute | solution.py:59
  49.0 0.3 collective-permute-done.13.refs_2_
  49.2 2.7 %collective-permute-done.14.refs_3_ = bf16[64,512]{1,0:T(8,128)(2,1)S(1)} collective-permute-done((bf16[64,512]{1,0:T(8,128)(2,1)S(1)}, bf16[64,512]{1,0:T(8,128)(2,1)S(1)}, u32[]{:S(2)}, u32[]{:S(2)}) %collective-permute-start.14) | collective-permute-done | bytes 65568 | tf_op jit(solution)/shard_map/ppermute | solution.py:59
  51.9 0.1 collective-permute-start.19
  52.0 2.1 %collective-permute-start.20 = (bf16[128,512]{1,0:T(8,128)(2,1)S(1)}, bf16[128,512]{1,0:T(8,128)(2,1)S(1)}, u32[]{:S(2)}, u32[]{:S(2)}) collective-permute-start(bf16[128,512]{1,0:T(8,128)(2,1)S(1)} %shard_map.113.refs_0_), channel_id=1, source_target_pairs={{0,8},{1,9},{2,10},{3,11},{4,12},{5,13},{6,14},{7,15},{8,0},{9,1},... | collective-permute-start | bytes 393224 | tf_op jit(solution)/shard_map/ppermute | solution.py:59
  54.1 2.2 %collective-permute-start.21 = (bf16[128,512]{1,0:T(8,128)(2,1)S(1)}, bf16[128,512]{1,0:T(8,128)(2,1)S(1)}, u32[]{:S(2)}, u32[]{:S(2)}) collective-permute-start(bf16[128,512]{1,0:T(8,128)(2,1)S(1)} %shard_map.113.refs_0_), channel_id=1, source_target_pairs={{0,12},{1,13},{2,14},{3,15},{4,8},{5,9},{6,10},{7,11},{8,4},{9,5},... | collective-permute-start | bytes 393224 | tf_op jit(solution)/shard_map/ppermute | solution.py:59
  56.4 2.2 %collective-permute-start.17 = (bf16[64,2048]{1,0:T(8,128)(2,1)S(1)}, bf16[64,2048]{1,0:T(8,128)(2,1)S(1)}, u32[]{:S(2)}, u32[]{:S(2)}) collective-permute-start(bf16[64,2048]{1,0:T(8,128)(2,1)S(1)} %shard_map.112.refs_0_), channel_id=1, source_target_pairs={{0,2},{1,3},{2,0},{3,1},{4,6},{5,7},{6,4},{7,5},{8,10},{9,11},{10,... | collective-permute-start | bytes 786440 | tf_op jit(solution)/shard_map/ppermute | solution.py:59
  58.6 3.1 %collective-permute-done.20.refs_2_ = bf16[128,512]{1,0:T(8,128)(2,1)S(1)} collective-permute-done((bf16[128,512]{1,0:T(8,128)(2,1)S(1)}, bf16[128,512]{1,0:T(8,128)(2,1)S(1)}, u32[]{:S(2)}, u32[]{:S(2)}) %collective-permute-start.20) | collective-permute-done | bytes 131104 | tf_op jit(solution)/shard_map/ppermute | solution.py:59
  61.7 0.1 shard_map.114.refs_2_
  61.8 0.1 collective-permute-start.22
  61.8 0.5 collective-permute-start.16
  62.3 0.6 collective-permute-done.17.refs_1_
  62.9 1.5 %shard_map.115 = (f32[256,768]{1,0:T(8,128)S(1)}, f32[320,128]{1,0:T(8,128)S(1)}) custom-call(bf16[64,2048]{1,0:T(8,128)(2,1)S(1)} %shard_map.112.refs_0_, bf16[64,2048]{1,0:T(8,128)(2,1)S(1)} %collective-permute-done.17.refs_1_, bf16[128,2048]{1,0:T(8,128)(2,1)S(1)} %shard_map.114.refs_2_, bf16[2048,768]{1,0:T(8,128)(2,1)S(1)} %copy-done, ...), custom_call_target="tpu_custom_call" | custom-call | flops 905969664 | bytes 7700480 | tf_op jit(solution)/shard_map/pallas_call | solution.py:91
  64.4 0.1 collective-permute-done.18.refs_1_
  64.5 1.5 %shard_map.116 = (f32[256,768]{1,0:T(8,128)S(1)}, bf16[320,128]{1,0:T(8,128)(2,1)S(1)}) custom-call(bf16[64,2048]{1,0:T(8,128)(2,1)S(1)} %collective-permute-done.16.refs_0_, bf16[64,2048]{1,0:T(8,128)(2,1)S(1)} %collective-permute-done.18.refs_1_, bf16[128,2048]{1,0:T(8,128)(2,1)S(1)} %collective-permute-done.22.refs_2_, bf16[2048,768]{1,0:T(8,128)(2,1)S(1)} %copy-done, ...), custom_call_target="tpu_custom_call" | custom-call | flops 905969664 | bytes 7618560 | tf_op jit(solution)/shard_map/pallas_call | solution.py:91
  66.0 0.5 collective-permute-start.23
  66.5 0.9 %collective-permute-done.23.refs_0_ = bf16[320,128]{1,0:T(8,128)(2,1)S(1)} collective-permute-done((bf16[320,128]{1,0:T(8,128)(2,1)S(1)}, bf16[320,128]{1,0:T(8,128)(2,1)S(1)}, u32[]{:S(2)}, u32[]{:S(2)}) %collective-permute-start.23) | collective-permute-done | bytes 81952 | tf_op jit(solution)/shard_map/ppermute | solution.py:59
  67.5 2.1 %collective-permute-start.24 = (bf16[320,128]{1,0:T(8,128)(2,1)S(1)}, bf16[320,128]{1,0:T(8,128)(2,1)S(1)}, u32[]{:S(2)}, u32[]{:S(2)}) collective-permute-start(bf16[320,128]{1,0:T(8,128)(2,1)S(1)} %get-tuple-element.106), channel_id=1, source_target_pairs={{0,2},{1,3},{2,0},{3,1},{4,6},{5,7},{6,4},{7,5},{8,10},{9,11},{10,... | collective-permute-start | bytes 245768 | tf_op jit(solution)/shard_map/ppermute | solution.py:59
  69.6 3.0 %collective-permute-done.24.refs_0_ = bf16[320,128]{1,0:T(8,128)(2,1)S(1)} collective-permute-done((bf16[320,128]{1,0:T(8,128)(2,1)S(1)}, bf16[320,128]{1,0:T(8,128)(2,1)S(1)}, u32[]{:S(2)}, u32[]{:S(2)}) %collective-permute-start.24) | collective-permute-done | bytes 81952 | tf_op jit(solution)/shard_map/ppermute | solution.py:59
  72.6 1.5 %collective-permute-start.25 = (bf16[320,128]{1,0:T(8,128)(2,1)S(1)}, bf16[320,128]{1,0:T(8,128)(2,1)S(1)}, u32[]{:S(2)}, u32[]{:S(2)}) collective-permute-start(bf16[320,128]{1,0:T(8,128)(2,1)S(1)} %get-tuple-element.108), channel_id=1, source_target_pairs={{0,12},{1,13},{2,14},{3,15},{4,8},{5,9},{6,10},{7,11},{8,4},{9,5},... | collective-permute-start | bytes 245768 | tf_op jit(solution)/shard_map/ppermute | solution.py:59
  74.0 1.5 %collective-permute-start.26 = (bf16[320,128]{1,0:T(8,128)(2,1)S(1)}, bf16[320,128]{1,0:T(8,128)(2,1)S(1)}, u32[]{:S(2)}, u32[]{:S(2)}) collective-permute-start(bf16[320,128]{1,0:T(8,128)(2,1)S(1)} %get-tuple-element.108), channel_id=1, source_target_pairs={{0,8},{1,9},{2,10},{3,11},{4,12},{5,13},{6,14},{7,15},{8,0},{9,1},... | collective-permute-start | bytes 245768 | tf_op jit(solution)/shard_map/ppermute | solution.py:59
  75.6 1.4 %collective-permute-start.27 = (bf16[320,128]{1,0:T(8,128)(2,1)S(1)}, bf16[320,128]{1,0:T(8,128)(2,1)S(1)}, u32[]{:S(2)}, u32[]{:S(2)}) collective-permute-start(bf16[320,128]{1,0:T(8,128)(2,1)S(1)} %get-tuple-element.108), channel_id=1, source_target_pairs={{0,4},{1,5},{2,6},{3,7},{4,0},{5,1},{6,2},{7,3},{8,12},{9,13},{10,... | collective-permute-start | bytes 245768 | tf_op jit(solution)/shard_map/ppermute | solution.py:59
  77.0 2.8 %collective-permute-done.25.refs_0_ = bf16[320,128]{1,0:T(8,128)(2,1)S(1)} collective-permute-done((bf16[320,128]{1,0:T(8,128)(2,1)S(1)}, bf16[320,128]{1,0:T(8,128)(2,1)S(1)}, u32[]{:S(2)}, u32[]{:S(2)}) %collective-permute-start.25) | collective-permute-done | bytes 81952 | tf_op jit(solution)/shard_map/ppermute | solution.py:59
  79.8 3.0 %collective-permute-done.26.refs_1_ = bf16[320,128]{1,0:T(8,128)(2,1)S(1)} collective-permute-done((bf16[320,128]{1,0:T(8,128)(2,1)S(1)}, bf16[320,128]{1,0:T(8,128)(2,1)S(1)}, u32[]{:S(2)}, u32[]{:S(2)}) %collective-permute-start.26) | collective-permute-done | bytes 81952 | tf_op jit(solution)/shard_map/ppermute | solution.py:59
  82.9 0.1 collective-permute-start.28
  82.9 1.2 %shard_map.120 = (bf16[512,768]{1,0:T(8,128)(2,1)}, bf16[512,768]{1,0:T(8,128)(2,1)}) custom-call(bf16[320,128]{1,0:T(8,128)(2,1)S(1)} %shard_map.119.refs_0_, f32[256,768]{1,0:T(8,128)S(1)} %get-tuple-element.111.refs_1_, bf16[640,768]{1,0:T(8,128)(2,1)S(1)} %shard_map.110.refs_5_.refs_2_, bf16[512,768]{1,0:T(8,128)(2,1)S(1)} %copy-done.1, ...), custom_call_target="tpu_custom_call" | custom-call | flops 100663296 | bytes 2555904 | tf_op jit(solution)/shard_map/pallas_call | solution.py:465
  84.1 0.1 collective-permute-done.28.refs_0_
  84.2 1.2 %shard_map.121 = (bf16[512,768]{1,0:T(8,128)(2,1)}, bf16[512,768]{1,0:T(8,128)(2,1)}) custom-call(bf16[320,128]{1,0:T(8,128)(2,1)S(1)} %collective-permute-done.28.refs_0_, f32[256,768]{1,0:T(8,128)S(1)} %get-tuple-element.109.refs_1_, bf16[640,768]{1,0:T(8,128)(2,1)S(1)} %shard_map.110.refs_5_.refs_2_, ...), custom_call_target="tpu_custom_call", output_to_operand_aliasing={{0}: (5, {}), {1}: (6, {})} | custom-call | flops 100663296 | bytes 2555904 | tf_op jit(solution)/shard_map/pallas_call | solution.py:465
  (32 shorter events, 0.2 us)
Async XLA Ops:
  0.6 7.6 %copy-start.1 = (bf16[512,768]{1,0:T(8,128)(2,1)S(1)}, bf16[512,768]{1,0:T(8,128)(2,1)}, u32[]{:S(2)}) copy-start(bf16[512,768]{1,0:T(8,128)(2,1)} %refs_3_.9) | copy-start | bytes 2359300
  0.6 15.6 %collective-permute-start.4 = (bf16[512,768]{1,0:T(8,128)(2,1)}, bf16[512,768]{1,0:T(8,128)(2,1)S(1)}, u32[]{:S(2)}, u32[]{:S(2)}) collective-permute-start(bf16[512,768]{1,0:T(8,128)(2,1)} %refs_3_.9), channel_id=1, source_target_pairs={{0,1},{1,2},{2,3},{3,4},{4,5},{5,6},{6,7},{7,8},{8,9},{9,10},{10,1... | collective-permute-start | bytes 2359304 | tf_op jit(solution)/shard_map/ppermute | solution.py:50
  5.5 31.5 %copy-start.7 = (f32[768]{0:T(1024)S(1)}, f32[768]{0:T(1024)}, u32[]{:S(2)}) copy-start(f32[768]{0:T(1024)} %param.12) | copy-start | bytes 9220
  5.5 31.5 %copy-start.8 = (f32[768]{0:T(1024)S(1)}, f32[768]{0:T(1024)}, u32[]{:S(2)}) copy-start(f32[768]{0:T(1024)} %param.13) | copy-start | bytes 9220
  5.5 31.5 %copy-start.2 = (bf16[512,768]{1,0:T(8,128)(2,1)S(1)}, bf16[512,768]{1,0:T(8,128)(2,1)}, u32[]{:S(2)}) copy-start(bf16[512,768]{1,0:T(8,128)(2,1)} %o_ref.1) | copy-start | bytes 2359300
  5.5 5.8 %collective-permute-start.1 = (bf16[128,2048]{1,0:T(8,128)(2,1)S(1)}, bf16[128,2048]{1,0:T(8,128)(2,1)S(1)}, u32[]{:S(2)}, u32[]{:S(2)}) collective-permute-start(bf16[128,2048]{1,0:T(8,128)(2,1)S(1)} %get-tuple-element.61), channel_id=1, source_target_pairs={{0,1},{1,0},{2,3},{3,2},{4,5},{5,4},{6,7},{7,6},{8,9},{9,8},{10,11... | collective-permute-start | bytes 1572872 | tf_op jit(solution)/shard_map/ppermute | solution.py:59
  8.2 3.4 %collective-permute-start = (bf16[128,2048]{1,0:T(8,128)(2,1)S(1)}, bf16[128,2048]{1,0:T(8,128)(2,1)S(1)}, u32[]{:S(2)}, u32[]{:S(2)}) collective-permute-start(bf16[128,2048]{1,0:T(8,128)(2,1)S(1)} %get-tuple-element.59), channel_id=1, source_target_pairs={{0,1},{1,0},{2,3},{3,2},{4,5},{5,4},{6,7},{7,6},{8,9},{9,8},{10,11... | collective-permute-start | bytes 1572872 | tf_op jit(solution)/shard_map/ppermute | solution.py:59
  8.2 23.9 %collective-permute-start.7 = (bf16[512,768]{1,0:T(8,128)(2,1)S(1)}, bf16[512,768]{1,0:T(8,128)(2,1)S(1)}, u32[]{:S(2)}, u32[]{:S(2)}) collective-permute-start(bf16[512,768]{1,0:T(8,128)(2,1)S(1)} %copy-done.1), channel_id=1, source_target_pairs={{0,15},{1,0},{2,1},{3,2},{4,3},{5,4},{6,5},{7,6},{8,7},{9,8},{10,9... | collective-permute-start | bytes 2359304 | tf_op jit(solution)/shard_map/ppermute | solution.py:50
  11.4 25.7 %copy-start.3 = (bf16[2,128,128]{2,1,0:T(8,128)(2,1)S(1)}, bf16[2,128,128]{2,1,0:T(8,128)(2,1)}, u32[]{:S(2)}) copy-start(bf16[2,128,128]{2,1,0:T(8,128)(2,1)} %constant.2.clone.refs_4_) | copy-start | bytes 196612
  11.4 25.7 %copy-start.4 = (f32[512]{0:T(512)S(1)}, f32[512]{0:T(512)}, u32[]{:S(2)}) copy-start(f32[512]{0:T(512)} %param.14) | copy-start | bytes 6148
  11.4 25.7 %copy-start.5 = (s32[512]{0:T(512)S(1)}, s32[512]{0:T(512)}, u32[]{:S(2)}) copy-start(s32[512]{0:T(512)} %param.15) | copy-start | bytes 6148
  11.4 25.7 %copy-start.6 = (s32[512]{0:T(512)S(1)}, s32[512]{0:T(512)}, u32[]{:S(2)}) copy-start(s32[512]{0:T(512)} %param.16) | copy-start | bytes 6148
  11.7 20.5 %collective-permute-start.6 = (bf16[64,2048]{1,0:T(8,128)(2,1)S(1)}, bf16[64,2048]{1,0:T(8,128)(2,1)S(1)}, u32[]{:S(2)}, u32[]{:S(2)}) collective-permute-start(bf16[64,2048]{1,0:T(8,128)(2,1)S(1)} %get-tuple-element.69), channel_id=1, source_target_pairs={{0,2},{1,3},{2,0},{3,1},{4,6},{5,7},{6,4},{7,5},{8,10},{9,11},{10,... | collective-permute-start | bytes 786440 | tf_op jit(solution)/shard_map/ppermute | solution.py:59
  12.2 14.7 %collective-permute-start.2 = (bf16[128,512]{1,0:T(8,128)(2,1)S(1)}, bf16[128,512]{1,0:T(8,128)(2,1)S(1)}, u32[]{:S(2)}, u32[]{:S(2)}) collective-permute-start(bf16[128,512]{1,0:T(8,128)(2,1)S(1)} %get-tuple-element.65), channel_id=1, source_target_pairs={{0,4},{1,5},{2,6},{3,7},{4,0},{5,1},{6,2},{7,3},{8,12},{9,13},{10,... | collective-permute-start | bytes 393224 | tf_op jit(solution)/shard_map/ppermute | solution.py:59
  13.8 18.4 %collective-permute-start.3 = (bf16[128,512]{1,0:T(8,128)(2,1)S(1)}, bf16[128,512]{1,0:T(8,128)(2,1)S(1)}, u32[]{:S(2)}, u32[]{:S(2)}) collective-permute-start(bf16[128,512]{1,0:T(8,128)(2,1)S(1)} %get-tuple-element.66), channel_id=1, source_target_pairs={{0,8},{1,9},{2,10},{3,11},{4,12},{5,13},{6,14},{7,15},{8,0},{9,1},... | collective-permute-start | bytes 393224 | tf_op jit(solution)/shard_map/ppermute | solution.py:59
  16.2 16.0 %collective-permute-start.5 = (bf16[128,512]{1,0:T(8,128)(2,1)S(1)}, bf16[128,512]{1,0:T(8,128)(2,1)S(1)}, u32[]{:S(2)}, u32[]{:S(2)}) collective-permute-start(bf16[128,512]{1,0:T(8,128)(2,1)S(1)} %get-tuple-element.68), channel_id=1, source_target_pairs={{0,12},{1,13},{2,14},{3,15},{4,8},{5,9},{6,10},{7,11},{8,4},{9,5},... | collective-permute-start | bytes 393224 | tf_op jit(solution)/shard_map/ppermute | solution.py:59
  32.2 7.2 %collective-permute-start.11 = (bf16[64,512]{1,0:T(8,128)(2,1)S(1)}, bf16[64,512]{1,0:T(8,128)(2,1)S(1)}, u32[]{:S(2)}, u32[]{:S(2)}) collective-permute-start(bf16[64,512]{1,0:T(8,128)(2,1)S(1)} %get-tuple-element.80), channel_id=1, source_target_pairs={{0,2},{1,3},{2,0},{3,1},{4,6},{5,7},{6,4},{7,5},{8,10},{9,11},{10,... | collective-permute-start | bytes 196616 | tf_op jit(solution)/shard_map/ppermute | solution.py:59
  32.4 7.0 %collective-permute-start.10 = (bf16[64,512]{1,0:T(8,128)(2,1)S(1)}, bf16[64,512]{1,0:T(8,128)(2,1)S(1)}, u32[]{:S(2)}, u32[]{:S(2)}) collective-permute-start(bf16[64,512]{1,0:T(8,128)(2,1)S(1)} %get-tuple-element.75), channel_id=1, source_target_pairs={{0,12},{1,13},{2,14},{3,15},{4,8},{5,9},{6,10},{7,11},{8,4},{9,5},... | collective-permute-start | bytes 196616 | tf_op jit(solution)/shard_map/ppermute | solution.py:59
  35.1 4.5 %collective-permute-start.8 = (bf16[64,512]{1,0:T(8,128)(2,1)S(1)}, bf16[64,512]{1,0:T(8,128)(2,1)S(1)}, u32[]{:S(2)}, u32[]{:S(2)}) collective-permute-start(bf16[64,512]{1,0:T(8,128)(2,1)S(1)} %get-tuple-element.73), channel_id=1, source_target_pairs={{0,4},{1,5},{2,6},{3,7},{4,0},{5,1},{6,2},{7,3},{8,12},{9,13},{10,... | collective-permute-start | bytes 196616 | tf_op jit(solution)/shard_map/ppermute | solution.py:59
  37.0 5.5 %collective-permute-start.9 = (bf16[64,512]{1,0:T(8,128)(2,1)S(1)}, bf16[64,512]{1,0:T(8,128)(2,1)S(1)}, u32[]{:S(2)}, u32[]{:S(2)}) collective-permute-start(bf16[64,512]{1,0:T(8,128)(2,1)S(1)} %get-tuple-element.74), channel_id=1, source_target_pairs={{0,8},{1,9},{2,10},{3,11},{4,12},{5,13},{6,14},{7,15},{8,0},{9,1},... | collective-permute-start | bytes 196616 | tf_op jit(solution)/shard_map/ppermute | solution.py:59
  37.1 25.8 %copy-start = (bf16[2048,768]{1,0:T(8,128)(2,1)S(1)}, bf16[2048,768]{1,0:T(8,128)(2,1)}, u32[]{:S(2)}) copy-start(bf16[2048,768]{1,0:T(8,128)(2,1)} %refs_3_.7) | copy-start | bytes 9437188
  42.5 6.5 %collective-permute-start.12 = (bf16[64,512]{1,0:T(8,128)(2,1)S(1)}, bf16[64,512]{1,0:T(8,128)(2,1)S(1)}, u32[]{:S(2)}, u32[]{:S(2)}) collective-permute-start(bf16[64,512]{1,0:T(8,128)(2,1)S(1)} %get-tuple-element.91.refs_0_), channel_id=1, source_target_pairs={{0,4},{1,5},{2,6},{3,7},{4,0},{5,1},{6,2},{7,3},{8,12},{9,13},{10,... | collective-permute-start | bytes 196616 | tf_op jit(solution)/shard_map/ppermute | solution.py:59
  42.6 6.6 %collective-permute-start.13 = (bf16[64,512]{1,0:T(8,128)(2,1)S(1)}, bf16[64,512]{1,0:T(8,128)(2,1)S(1)}, u32[]{:S(2)}, u32[]{:S(2)}) collective-permute-start(bf16[64,512]{1,0:T(8,128)(2,1)S(1)} %get-tuple-element.91.refs_0_), channel_id=1, source_target_pairs={{0,8},{1,9},{2,10},{3,11},{4,12},{5,13},{6,14},{7,15},{8,0},{9,1},... | collective-permute-start | bytes 196616 | tf_op jit(solution)/shard_map/ppermute | solution.py:59
  45.4 6.5 %collective-permute-start.14 = (bf16[64,512]{1,0:T(8,128)(2,1)S(1)}, bf16[64,512]{1,0:T(8,128)(2,1)S(1)}, u32[]{:S(2)}, u32[]{:S(2)}) collective-permute-start(bf16[64,512]{1,0:T(8,128)(2,1)S(1)} %get-tuple-element.91.refs_0_), channel_id=1, source_target_pairs={{0,12},{1,13},{2,14},{3,15},{4,8},{5,9},{6,10},{7,11},{8,4},{9,5},... | collective-permute-start | bytes 196616 | tf_op jit(solution)/shard_map/ppermute | solution.py:59
  47.0 4.9 %collective-permute-start.15 = (bf16[64,512]{1,0:T(8,128)(2,1)S(1)}, bf16[64,512]{1,0:T(8,128)(2,1)S(1)}, u32[]{:S(2)}, u32[]{:S(2)}) collective-permute-start(bf16[64,512]{1,0:T(8,128)(2,1)S(1)} %get-tuple-element.95.refs_0_), channel_id=1, source_target_pairs={{0,2},{1,3},{2,0},{3,1},{4,6},{5,7},{6,4},{7,5},{8,10},{9,11},{10,... | collective-permute-start | bytes 196616 | tf_op jit(solution)/shard_map/ppermute | solution.py:59
  51.9 6.6 %collective-permute-start.19 = (bf16[128,512]{1,0:T(8,128)(2,1)S(1)}, bf16[128,512]{1,0:T(8,128)(2,1)S(1)}, u32[]{:S(2)}, u32[]{:S(2)}) collective-permute-start(bf16[128,512]{1,0:T(8,128)(2,1)S(1)} %shard_map.113.refs_0_), channel_id=1, source_target_pairs={{0,4},{1,5},{2,6},{3,7},{4,0},{5,1},{6,2},{7,3},{8,12},{9,13},{10,... | collective-permute-start | bytes 393224 | tf_op jit(solution)/shard_map/ppermute | solution.py:59
  52.0 9.7 %collective-permute-start.20 = (bf16[128,512]{1,0:T(8,128)(2,1)S(1)}, bf16[128,512]{1,0:T(8,128)(2,1)S(1)}, u32[]{:S(2)}, u32[]{:S(2)}) collective-permute-start(bf16[128,512]{1,0:T(8,128)(2,1)S(1)} %shard_map.113.refs_0_), channel_id=1, source_target_pairs={{0,8},{1,9},{2,10},{3,11},{4,12},{5,13},{6,14},{7,15},{8,0},{9,1},... | collective-permute-start | bytes 393224 | tf_op jit(solution)/shard_map/ppermute | solution.py:59
  54.1 7.6 %collective-permute-start.21 = (bf16[128,512]{1,0:T(8,128)(2,1)S(1)}, bf16[128,512]{1,0:T(8,128)(2,1)S(1)}, u32[]{:S(2)}, u32[]{:S(2)}) collective-permute-start(bf16[128,512]{1,0:T(8,128)(2,1)S(1)} %shard_map.113.refs_0_), channel_id=1, source_target_pairs={{0,12},{1,13},{2,14},{3,15},{4,8},{5,9},{6,10},{7,11},{8,4},{9,5},... | collective-permute-start | bytes 393224 | tf_op jit(solution)/shard_map/ppermute | solution.py:59
  56.4 6.5 %collective-permute-start.17 = (bf16[64,2048]{1,0:T(8,128)(2,1)S(1)}, bf16[64,2048]{1,0:T(8,128)(2,1)S(1)}, u32[]{:S(2)}, u32[]{:S(2)}) collective-permute-start(bf16[64,2048]{1,0:T(8,128)(2,1)S(1)} %shard_map.112.refs_0_), channel_id=1, source_target_pairs={{0,2},{1,3},{2,0},{3,1},{4,6},{5,7},{6,4},{7,5},{8,10},{9,11},{10,... | collective-permute-start | bytes 786440 | tf_op jit(solution)/shard_map/ppermute | solution.py:59
  61.8 2.7 %collective-permute-start.22 = (bf16[128,2048]{1,0:T(8,128)(2,1)S(1)}, bf16[128,2048]{1,0:T(8,128)(2,1)S(1)}, u32[]{:S(2)}, u32[]{:S(2)}) collective-permute-start(bf16[128,2048]{1,0:T(8,128)(2,1)S(1)} %shard_map.114.refs_2_), channel_id=1, source_target_pairs={{0,1},{1,0},{2,3},{3,2},{4,5},{5,4},{6,7},{7,6},{8,9},{9,8},{10,11... | collective-permute-start | bytes 1572872 | tf_op jit(solution)/shard_map/ppermute | solution.py:59
  61.8 2.6 %collective-permute-start.16 = (bf16[64,2048]{1,0:T(8,128)(2,1)S(1)}, bf16[64,2048]{1,0:T(8,128)(2,1)S(1)}, u32[]{:S(2)}, u32[]{:S(2)}) collective-permute-start(bf16[64,2048]{1,0:T(8,128)(2,1)S(1)} %shard_map.112.refs_0_), channel_id=1, source_target_pairs={{0,1},{1,0},{2,3},{3,2},{4,5},{5,4},{6,7},{7,6},{8,9},{9,8},{10,11... | collective-permute-start | bytes 786440 | tf_op jit(solution)/shard_map/ppermute | solution.py:59
  62.9 1.6 %collective-permute-start.18 = (bf16[64,2048]{1,0:T(8,128)(2,1)S(1)}, bf16[64,2048]{1,0:T(8,128)(2,1)S(1)}, u32[]{:S(2)}, u32[]{:S(2)}) collective-permute-start(bf16[64,2048]{1,0:T(8,128)(2,1)S(1)} %collective-permute-done.17.refs_1_), channel_id=1, source_target_pairs={{0,1},{1,0},{2,3},{3,2},{4,5},{5,4},{6,7},{7,6},{8,9},{9,8},{10,11... | collective-permute-start | bytes 786440 | tf_op jit(solution)/shard_map/ppermute | solution.py:59
  66.0 1.5 %collective-permute-start.23 = (bf16[320,128]{1,0:T(8,128)(2,1)S(1)}, bf16[320,128]{1,0:T(8,128)(2,1)S(1)}, u32[]{:S(2)}, u32[]{:S(2)}) collective-permute-start(bf16[320,128]{1,0:T(8,128)(2,1)S(1)} %get-tuple-element.104), channel_id=1, source_target_pairs={{0,1},{1,0},{2,3},{3,2},{4,5},{5,4},{6,7},{7,6},{8,9},{9,8},{10,11... | collective-permute-start | bytes 245768 | tf_op jit(solution)/shard_map/ppermute | solution.py:59
  67.5 5.0 %collective-permute-start.24 = (bf16[320,128]{1,0:T(8,128)(2,1)S(1)}, bf16[320,128]{1,0:T(8,128)(2,1)S(1)}, u32[]{:S(2)}, u32[]{:S(2)}) collective-permute-start(bf16[320,128]{1,0:T(8,128)(2,1)S(1)} %get-tuple-element.106), channel_id=1, source_target_pairs={{0,2},{1,3},{2,0},{3,1},{4,6},{5,7},{6,4},{7,5},{8,10},{9,11},{10,... | collective-permute-start | bytes 245768 | tf_op jit(solution)/shard_map/ppermute | solution.py:59
  72.6 7.2 %collective-permute-start.25 = (bf16[320,128]{1,0:T(8,128)(2,1)S(1)}, bf16[320,128]{1,0:T(8,128)(2,1)S(1)}, u32[]{:S(2)}, u32[]{:S(2)}) collective-permute-start(bf16[320,128]{1,0:T(8,128)(2,1)S(1)} %get-tuple-element.108), channel_id=1, source_target_pairs={{0,12},{1,13},{2,14},{3,15},{4,8},{5,9},{6,10},{7,11},{8,4},{9,5},... | collective-permute-start | bytes 245768 | tf_op jit(solution)/shard_map/ppermute | solution.py:59
  74.0 8.8 %collective-permute-start.26 = (bf16[320,128]{1,0:T(8,128)(2,1)S(1)}, bf16[320,128]{1,0:T(8,128)(2,1)S(1)}, u32[]{:S(2)}, u32[]{:S(2)}) collective-permute-start(bf16[320,128]{1,0:T(8,128)(2,1)S(1)} %get-tuple-element.108), channel_id=1, source_target_pairs={{0,8},{1,9},{2,10},{3,11},{4,12},{5,13},{6,14},{7,15},{8,0},{9,1},... | collective-permute-start | bytes 245768 | tf_op jit(solution)/shard_map/ppermute | solution.py:59
  75.6 7.2 %collective-permute-start.27 = (bf16[320,128]{1,0:T(8,128)(2,1)S(1)}, bf16[320,128]{1,0:T(8,128)(2,1)S(1)}, u32[]{:S(2)}, u32[]{:S(2)}) collective-permute-start(bf16[320,128]{1,0:T(8,128)(2,1)S(1)} %get-tuple-element.108), channel_id=1, source_target_pairs={{0,4},{1,5},{2,6},{3,7},{4,0},{5,1},{6,2},{7,3},{8,12},{9,13},{10,... | collective-permute-start | bytes 245768 | tf_op jit(solution)/shard_map/ppermute | solution.py:59
  82.9 1.3 %collective-permute-start.28 = (bf16[320,128]{1,0:T(8,128)(2,1)S(1)}, bf16[320,128]{1,0:T(8,128)(2,1)S(1)}, u32[]{:S(2)}, u32[]{:S(2)}) collective-permute-start(bf16[320,128]{1,0:T(8,128)(2,1)S(1)} %shard_map.119.refs_0_), channel_id=1, source_target_pairs={{0,1},{1,0},{2,3},{3,2},{4,5},{5,4},{6,7},{7,6},{8,9},{9,8},{10,11... | collective-permute-start | bytes 245768 | tf_op jit(solution)/shard_map/ppermute | solution.py:59

commit v23 on v20

--- a/solution.py
+++ b/solution.py
@@ -568,7 +568,12 @@
     )
     padded = pad_orbitals(orbitals, blk)
     taken_x, taken_z, base, padded = lax.optimization_barrier(
-        (parts_to(parts_x, along), parts_to(parts_z, across), base, padded)
+        (
+            [swapped(part, count, along, k + 1) for k, part in enumerate(parts_x)],
+            parts_to(parts_z, across),
+            base,
+            padded,
+        )
     )
     share_x, share_z = local_call(
         functools.partial(finish_both_body, ace_scale, len(taken_x)),

time: 85.2 us -> 83.8 us (0.984)
  waiting for transfers between devices: 39.9 us -> 38.3 us
    ppermute x27, waiting for transfers between devices: 39.2 us -> 37.6 us  [swapped(): return lax.ppermute(array, 'band', pairs)]
  transfers between devices with their start and end apart: 29 -> 29, of which waited for: 17 -> 17; matrix products, arithmetic and copies ran while one was open for 0% -> 0% of each run, Pallas kernels for 11% -> 12%
where the time goes in v23:
time: 83.8 us; the launch traced here: 83.7 us
  waiting for transfers between devices  38.3 us (46%)
  starting transfers between devices  31.7 us (38%)
  Pallas kernels  12.6 us (15%)
  between operations  0.9 us (1%)
    ppermute x27, waiting for transfers between devices, swapped(): return lax.ppermute(array, 'band', pairs)  37.6 us
    ppermute x27, starting transfers between devices, swapped(): return lax.ppermute(array, 'band', pairs)  28.1 us
    pallas_call x1, Pallas kernels, first_sums(): pl.pallas_call(functools.partial(first_body, core, block, tile), out_shap...  4.34 us
    pallas_call x14, Pallas kernels, local_call(): pl.pallas_call(body, out_shape=outs, in_specs=[whole() for _ in args], ou...  3.66 us
    ppermute x2, starting transfers between devices, neighbour(): lax.ppermute(array, 'band', [(i, (i + step) % count) for i in range(count)])  3.62 us
    pallas_call x2, Pallas kernels, project(): pl.pallas_call(functools.partial(project_body, core, blk, other), out_sha...  2.4 us
    pallas_call x1, Pallas kernels, local_part(): pl.pallas_call(functools.partial(local_body, depth, (group_rows, blk)), g...  2.24 us
  transfers between devices with their start and end apart: 29, of which 17 were waited for; matrix products, arithmetic and copies ran while one was open for 0% of the time, Pallas kernels for 12%

profile of v23, /device:TPU:0, one launch (start us, length us, event | category | flops | bytes accessed | tf_op | source)
XLA Modules:
  0.0 83.7 jit_solution(16277509965720691912)
XLA Ops:
  0.6 0.5 collective-permute-start.4
  1.1 4.3 %shard_map.104 = (bf16[256,1024]{1,0:T(8,128)(2,1)S(1)}, bf16[256,1024]{1,0:T(8,128)(2,1)S(1)}, f32[160,2048]{1,0:T(8,128)S(1)}, f32[96,2048]{1,0:T(8,128)S(1)}) custom-call(bf16[512,768]{1,0:T(8,128)(2,1)} %refs_3_.9, bf16[2048,768]{1,0:T(8,128)(2,1)} %refs_3_.7), custom_call_target="tpu_custom_call" | custom-call | flops 1610612736 | bytes 6291456 | tf_op jit(solution)/shard_map/pallas_call | solution.py:153
  5.5 2.6 %collective-permute-start = (bf16[256,1024]{1,0:T(8,128)(2,1)S(1)}, bf16[256,1024]{1,0:T(8,128)(2,1)S(1)}, u32[]{:S(2)}, u32[]{:S(2)}) collective-permute-start(bf16[256,1024]{1,0:T(8,128)(2,1)S(1)} %get-tuple-element.60), channel_id=1, source_target_pairs={{0,1},{1,0},{2,3},{3,2},{4,5},{5,4},{6,7},{7,6},{8,9},{9,8},{10,11... | collective-permute-start | bytes 1572872 | tf_op jit(solution)/shard_map/ppermute | solution.py:59
  8.1 0.1 collective-permute-start.1
  8.2 3.1 %collective-permute-start.7 = (bf16[512,768]{1,0:T(8,128)(2,1)S(1)}, bf16[512,768]{1,0:T(8,128)(2,1)S(1)}, u32[]{:S(2)}, u32[]{:S(2)}) collective-permute-start(bf16[512,768]{1,0:T(8,128)(2,1)S(1)} %copy-done.1), channel_id=1, source_target_pairs={{0,15},{1,0},{2,1},{3,2},{4,3},{5,4},{6,5},{7,6},{8,7},{9,8},{10,9... | collective-permute-start | bytes 2359304 | tf_op jit(solution)/shard_map/ppermute | solution.py:50
  11.3 0.0 collective-permute-done.low_ref
  11.3 0.0 collective-permute-done.1.high_ref
  11.3 0.1 shard_map.105
  11.4 0.0 copy-start.7
  11.5 0.0 copy-start.8
  11.5 0.0 copy-start.2
  11.5 0.1 shard_map.106
  11.6 0.7 collective-permute-start.6
  12.3 2.4 %collective-permute-start.2 = (bf16[96,512]{1,0:T(8,128)(2,1)S(1)}, bf16[96,512]{1,0:T(8,128)(2,1)S(1)}, u32[]{:S(2)}, u32[]{:S(2)}) collective-permute-start(bf16[96,512]{1,0:T(8,128)(2,1)S(1)} %get-tuple-element.65), channel_id=1, source_target_pairs={{0,12},{1,13},{2,14},{3,15},{4,8},{5,9},{6,10},{7,11},{8,4},{9,5},... | collective-permute-start | bytes 294920 | tf_op jit(solution)/shard_map/ppermute | solution.py:59
  14.7 0.7 collective-permute-start.3
  15.4 0.8 collective-permute-done.4.refs_1_
  16.1 0.6 collective-permute-start.5
  16.7 10.9 %collective-permute-done.2.refs_1_ = bf16[96,512]{1,0:T(8,128)(2,1)S(1)} collective-permute-done((bf16[96,512]{1,0:T(8,128)(2,1)S(1)}, bf16[96,512]{1,0:T(8,128)(2,1)S(1)}, u32[]{:S(2)}, u32[]{:S(2)}) %collective-permute-start.2) | collective-permute-done | bytes 98336 | tf_op jit(solution)/shard_map/ppermute | solution.py:59
  27.6 3.1 %collective-permute-done.3.refs_2_ = bf16[96,512]{1,0:T(8,128)(2,1)S(1)} collective-permute-done((bf16[96,512]{1,0:T(8,128)(2,1)S(1)}, bf16[96,512]{1,0:T(8,128)(2,1)S(1)}, u32[]{:S(2)}, u32[]{:S(2)}) %collective-permute-start.3) | collective-permute-done | bytes 98336 | tf_op jit(solution)/shard_map/ppermute | solution.py:59
  30.7 0.0 collective-permute-done.7.refs_2_
  30.7 0.7 collective-permute-done.6.refs_1_
  31.5 0.0 copy-start.6
  31.5 0.1 shard_map.107
  31.6 2.3 %collective-permute-start.10 = (bf16[80,512]{1,0:T(8,128)(2,1)S(1)}, bf16[80,512]{1,0:T(8,128)(2,1)S(1)}, u32[]{:S(2)}, u32[]{:S(2)}) collective-permute-start(bf16[80,512]{1,0:T(8,128)(2,1)S(1)} %get-tuple-element.75), channel_id=1, source_target_pairs={{0,12},{1,13},{2,14},{3,15},{4,8},{5,9},{6,10},{7,11},{8,4},{9,5},... | collective-permute-start | bytes 245768 | tf_op jit(solution)/shard_map/ppermute | solution.py:59
  33.9 0.0 collective-permute-start.8
  33.9 2.1 %collective-permute-start.9 = (bf16[80,512]{1,0:T(8,128)(2,1)S(1)}, bf16[80,512]{1,0:T(8,128)(2,1)S(1)}, u32[]{:S(2)}, u32[]{:S(2)}) collective-permute-start(bf16[80,512]{1,0:T(8,128)(2,1)S(1)} %get-tuple-element.74), channel_id=1, source_target_pairs={{0,8},{1,9},{2,10},{3,11},{4,12},{5,13},{6,14},{7,15},{8,0},{9,1},... | collective-permute-start | bytes 245768 | tf_op jit(solution)/shard_map/ppermute | solution.py:59
  36.1 0.1 collective-permute-start.11
  36.2 0.1 shard_map.110.refs_5_.refs_2_
  36.3 0.0 copy-start
  36.3 2.2 %shard_map.109 = (f32[512,768]{1,0:T(8,128)S(1)}, bf16[512,256]{1,0:T(8,128)(2,1)S(1)}) custom-call(bf16[512,768]{1,0:T(8,128)(2,1)S(1)} %copy-done.1, bf16[512,768]{1,0:T(8,128)(2,1)S(1)} %collective-permute-done.4.refs_1_, bf16[512,768]{1,0:T(8,128)(2,1)S(1)} %collective-permute-done.7.refs_2_, bf16[512,768]{1,0:T(8,128)(2,1)S(1)} %copy-done.2, ...), custom_call_target="tpu_custom_call" | custom-call | flops 235929600 | bytes 4980736 | tf_op jit(solution)/shard_map/pallas_call | solution.py:333
  38.6 1.6 %collective-permute-done.11.refs_5_ = bf16[48,512]{1,0:T(8,128)(2,1)S(1)} collective-permute-done((bf16[48,512]{1,0:T(8,128)(2,1)S(1)}, bf16[48,512]{1,0:T(8,128)(2,1)S(1)}, u32[]{:S(2)}, u32[]{:S(2)}) %collective-permute-start.11) | collective-permute-done | bytes 49184 | tf_op jit(solution)/shard_map/ppermute | solution.py:59
  40.2 0.0 collective-permute-done.10.refs_3_
  40.2 0.0 collective-permute-done.8.refs_1_
  40.2 1.2 %collective-permute-done.9.refs_2_ = bf16[80,512]{1,0:T(8,128)(2,1)S(1)} collective-permute-done((bf16[80,512]{1,0:T(8,128)(2,1)S(1)}, bf16[80,512]{1,0:T(8,128)(2,1)S(1)}, u32[]{:S(2)}, u32[]{:S(2)}) %collective-permute-start.9) | collective-permute-done | bytes 81952 | tf_op jit(solution)/shard_map/ppermute | solution.py:59
  41.4 0.1 shard_map.111
  41.4 2.2 %collective-permute-start.12 = (bf16[80,512]{1,0:T(8,128)(2,1)S(1)}, bf16[80,512]{1,0:T(8,128)(2,1)S(1)}, u32[]{:S(2)}, u32[]{:S(2)}) collective-permute-start(bf16[80,512]{1,0:T(8,128)(2,1)S(1)} %get-tuple-element.91.refs_0_), channel_id=1, source_target_pairs={{0,12},{1,13},{2,14},{3,15},{4,8},{5,9},{6,10},{7,11},{8,4},{9,5},... | collective-permute-start | bytes 245768 | tf_op jit(solution)/shard_map/ppermute | solution.py:59
  43.6 0.0 collective-permute-start.13
  43.6 2.3 %collective-permute-start.14 = (bf16[80,512]{1,0:T(8,128)(2,1)S(1)}, bf16[80,512]{1,0:T(8,128)(2,1)S(1)}, u32[]{:S(2)}, u32[]{:S(2)}) collective-permute-start(bf16[80,512]{1,0:T(8,128)(2,1)S(1)} %get-tuple-element.91.refs_0_), channel_id=1, source_target_pairs={{0,4},{1,5},{2,6},{3,7},{4,0},{5,1},{6,2},{7,3},{8,12},{9,13},{10,... | collective-permute-start | bytes 245768 | tf_op jit(solution)/shard_map/ppermute | solution.py:59
  45.9 4.1 %collective-permute-done.15.refs_1_ = bf16[48,512]{1,0:T(8,128)(2,1)S(1)} collective-permute-done((bf16[48,512]{1,0:T(8,128)(2,1)S(1)}, bf16[48,512]{1,0:T(8,128)(2,1)S(1)}, u32[]{:S(2)}, u32[]{:S(2)}) %collective-permute-start.15) | collective-permute-done | bytes 49184 | tf_op jit(solution)/shard_map/ppermute | solution.py:59
  50.0 0.5 collective-permute-done.13.refs_2_
  50.6 0.5 collective-permute-start.17
  51.0 2.6 %collective-permute-start.19 = (bf16[96,512]{1,0:T(8,128)(2,1)S(1)}, bf16[96,512]{1,0:T(8,128)(2,1)S(1)}, u32[]{:S(2)}, u32[]{:S(2)}) collective-permute-start(bf16[96,512]{1,0:T(8,128)(2,1)S(1)} %shard_map.113.refs_0_), channel_id=1, source_target_pairs={{0,12},{1,13},{2,14},{3,15},{4,8},{5,9},{6,10},{7,11},{8,4},{9,5},... | collective-permute-start | bytes 294920 | tf_op jit(solution)/shard_map/ppermute | solution.py:59
  53.7 1.8 %collective-permute-start.21 = (bf16[96,512]{1,0:T(8,128)(2,1)S(1)}, bf16[96,512]{1,0:T(8,128)(2,1)S(1)}, u32[]{:S(2)}, u32[]{:S(2)}) collective-permute-start(bf16[96,512]{1,0:T(8,128)(2,1)S(1)} %shard_map.113.refs_0_), channel_id=1, source_target_pairs={{0,4},{1,5},{2,6},{3,7},{4,0},{5,1},{6,2},{7,3},{8,12},{9,13},{10,... | collective-permute-start | bytes 294920 | tf_op jit(solution)/shard_map/ppermute | solution.py:59
  55.5 3.2 %collective-permute-done.19.refs_1_ = bf16[96,512]{1,0:T(8,128)(2,1)S(1)} collective-permute-done((bf16[96,512]{1,0:T(8,128)(2,1)S(1)}, bf16[96,512]{1,0:T(8,128)(2,1)S(1)}, u32[]{:S(2)}, u32[]{:S(2)}) %collective-permute-start.19) | collective-permute-done | bytes 98336 | tf_op jit(solution)/shard_map/ppermute | solution.py:59
  58.7 2.9 %collective-permute-done.20.refs_2_ = bf16[96,512]{1,0:T(8,128)(2,1)S(1)} collective-permute-done((bf16[96,512]{1,0:T(8,128)(2,1)S(1)}, bf16[96,512]{1,0:T(8,128)(2,1)S(1)}, u32[]{:S(2)}, u32[]{:S(2)}) %collective-permute-start.20) | collective-permute-done | bytes 98336 | tf_op jit(solution)/shard_map/ppermute | solution.py:59
  61.6 0.1 collective-permute-start.22
  61.7 0.5 collective-permute-start.16
  62.2 0.1 collective-permute-start.18
  62.3 1.5 %shard_map.115 = (f32[256,768]{1,0:T(8,128)S(1)}, f32[320,128]{1,0:T(8,128)S(1)}) custom-call(bf16[80,2048]{1,0:T(8,128)(2,1)S(1)} %shard_map.112.refs_0_, bf16[80,2048]{1,0:T(8,128)(2,1)S(1)} %collective-permute-done.17.refs_1_, bf16[96,2048]{1,0:T(8,128)(2,1)S(1)} %shard_map.114.refs_2_, bf16[2048,768]{1,0:T(8,128)(2,1)S(1)} %copy-done, ...), custom_call_target="tpu_custom_call" | custom-call | flops 905969664 | bytes 7700480 | tf_op jit(solution)/shard_map/pallas_call | solution.py:91
  63.8 0.1 collective-permute-done.16.refs_0_
  63.9 0.5 collective-permute-done.18.refs_1_
  64.3 1.5 %shard_map.116 = (f32[256,768]{1,0:T(8,128)S(1)}, bf16[320,128]{1,0:T(8,128)(2,1)S(1)}) custom-call(bf16[80,2048]{1,0:T(8,128)(2,1)S(1)} %collective-permute-done.16.refs_0_, bf16[80,2048]{1,0:T(8,128)(2,1)S(1)} %collective-permute-done.18.refs_1_, bf16[96,2048]{1,0:T(8,128)(2,1)S(1)} %collective-permute-done.22.refs_2_, bf16[2048,768]{1,0:T(8,128)(2,1)S(1)} %copy-done, ...), custom_call_target="tpu_custom_call" | custom-call | flops 905969664 | bytes 7618560 | tf_op jit(solution)/shard_map/pallas_call | solution.py:91
  65.9 0.2 collective-permute-start.23
  66.1 1.1 %collective-permute-done.23.refs_0_ = bf16[320,128]{1,0:T(8,128)(2,1)S(1)} collective-permute-done((bf16[320,128]{1,0:T(8,128)(2,1)S(1)}, bf16[320,128]{1,0:T(8,128)(2,1)S(1)}, u32[]{:S(2)}, u32[]{:S(2)}) %collective-permute-start.23) | collective-permute-done | bytes 81952 | tf_op jit(solution)/shard_map/ppermute | solution.py:59
  67.2 1.8 %collective-permute-start.24 = (bf16[320,128]{1,0:T(8,128)(2,1)S(1)}, bf16[320,128]{1,0:T(8,128)(2,1)S(1)}, u32[]{:S(2)}, u32[]{:S(2)}) collective-permute-start(bf16[320,128]{1,0:T(8,128)(2,1)S(1)} %get-tuple-element.106), channel_id=1, source_target_pairs={{0,2},{1,3},{2,0},{3,1},{4,6},{5,7},{6,4},{7,5},{8,10},{9,11},{10,... | collective-permute-start | bytes 245768 | tf_op jit(solution)/shard_map/ppermute | solution.py:59
  69.0 2.8 %collective-permute-done.24.refs_0_ = bf16[320,128]{1,0:T(8,128)(2,1)S(1)} collective-permute-done((bf16[320,128]{1,0:T(8,128)(2,1)S(1)}, bf16[320,128]{1,0:T(8,128)(2,1)S(1)}, u32[]{:S(2)}, u32[]{:S(2)}) %collective-permute-start.24) | collective-permute-done | bytes 81952 | tf_op jit(solution)/shard_map/ppermute | solution.py:59
  71.8 2.2 %collective-permute-start.25 = (bf16[320,128]{1,0:T(8,128)(2,1)S(1)}, bf16[320,128]{1,0:T(8,128)(2,1)S(1)}, u32[]{:S(2)}, u32[]{:S(2)}) collective-permute-start(bf16[320,128]{1,0:T(8,128)(2,1)S(1)} %get-tuple-element.108), channel_id=1, source_target_pairs={{0,12},{1,13},{2,14},{3,15},{4,8},{5,9},{6,10},{7,11},{8,4},{9,5},... | collective-permute-start | bytes 245768 | tf_op jit(solution)/shard_map/ppermute | solution.py:59
  74.1 2.2 %collective-permute-start.27 = (bf16[320,128]{1,0:T(8,128)(2,1)S(1)}, bf16[320,128]{1,0:T(8,128)(2,1)S(1)}, u32[]{:S(2)}, u32[]{:S(2)}) collective-permute-start(bf16[320,128]{1,0:T(8,128)(2,1)S(1)} %get-tuple-element.108), channel_id=1, source_target_pairs={{0,4},{1,5},{2,6},{3,7},{4,0},{5,1},{6,2},{7,3},{8,12},{9,13},{10,... | collective-permute-start | bytes 245768 | tf_op jit(solution)/shard_map/ppermute | solution.py:59
  76.3 2.6 %collective-permute-done.25.refs_0_ = bf16[320,128]{1,0:T(8,128)(2,1)S(1)} collective-permute-done((bf16[320,128]{1,0:T(8,128)(2,1)S(1)}, bf16[320,128]{1,0:T(8,128)(2,1)S(1)}, u32[]{:S(2)}, u32[]{:S(2)}) %collective-permute-start.25) | collective-permute-done | bytes 81952 | tf_op jit(solution)/shard_map/ppermute | solution.py:59
  78.9 2.2 %collective-permute-done.26.refs_1_ = bf16[320,128]{1,0:T(8,128)(2,1)S(1)} collective-permute-done((bf16[320,128]{1,0:T(8,128)(2,1)S(1)}, bf16[320,128]{1,0:T(8,128)(2,1)S(1)}, u32[]{:S(2)}, u32[]{:S(2)}) %collective-permute-start.26) | collective-permute-done | bytes 81952 | tf_op jit(solution)/shard_map/ppermute | solution.py:59
  81.1 0.1 collective-permute-start.28
  81.2 1.2 %shard_map.120 = (bf16[512,768]{1,0:T(8,128)(2,1)}, bf16[512,768]{1,0:T(8,128)(2,1)}) custom-call(bf16[320,128]{1,0:T(8,128)(2,1)S(1)} %shard_map.119.refs_0_, f32[256,768]{1,0:T(8,128)S(1)} %get-tuple-element.111.refs_1_, bf16[640,768]{1,0:T(8,128)(2,1)S(1)} %shard_map.110.refs_5_.refs_2_, bf16[512,768]{1,0:T(8,128)(2,1)S(1)} %copy-done.1, ...), custom_call_target="tpu_custom_call" | custom-call | flops 100663296 | bytes 2555904 | tf_op jit(solution)/shard_map/pallas_call | solution.py:500
  82.4 0.1 collective-permute-done.28.refs_0_
  82.5 1.2 %shard_map.121 = (bf16[512,768]{1,0:T(8,128)(2,1)}, bf16[512,768]{1,0:T(8,128)(2,1)}) custom-call(bf16[320,128]{1,0:T(8,128)(2,1)S(1)} %collective-permute-done.28.refs_0_, f32[256,768]{1,0:T(8,128)S(1)} %get-tuple-element.109.refs_1_, bf16[640,768]{1,0:T(8,128)(2,1)S(1)} %shard_map.110.refs_5_.refs_2_, ...), custom_call_target="tpu_custom_call", output_to_operand_aliasing={{0}: (5, {}), {1}: (6, {})} | custom-call | flops 100663296 | bytes 2555904 | tf_op jit(solution)/shard_map/pallas_call | solution.py:500
  (32 shorter events, 0.3 us)
Async XLA Ops:
  0.6 7.6 %copy-start.1 = (bf16[512,768]{1,0:T(8,128)(2,1)S(1)}, bf16[512,768]{1,0:T(8,128)(2,1)}, u32[]{:S(2)}) copy-start(bf16[512,768]{1,0:T(8,128)(2,1)} %refs_3_.9) | copy-start | bytes 2359300
  0.6 15.5 %collective-permute-start.4 = (bf16[512,768]{1,0:T(8,128)(2,1)}, bf16[512,768]{1,0:T(8,128)(2,1)S(1)}, u32[]{:S(2)}, u32[]{:S(2)}) collective-permute-start(bf16[512,768]{1,0:T(8,128)(2,1)} %refs_3_.9), channel_id=1, source_target_pairs={{0,1},{1,2},{2,3},{3,4},{4,5},{5,6},{6,7},{7,8},{8,9},{9,10},{10,1... | collective-permute-start | bytes 2359304 | tf_op jit(solution)/shard_map/ppermute | solution.py:50
  5.5 5.8 %collective-permute-start = (bf16[256,1024]{1,0:T(8,128)(2,1)S(1)}, bf16[256,1024]{1,0:T(8,128)(2,1)S(1)}, u32[]{:S(2)}, u32[]{:S(2)}) collective-permute-start(bf16[256,1024]{1,0:T(8,128)(2,1)S(1)} %get-tuple-element.60), channel_id=1, source_target_pairs={{0,1},{1,0},{2,3},{3,2},{4,5},{5,4},{6,7},{7,6},{8,9},{9,8},{10,11... | collective-permute-start | bytes 1572872 | tf_op jit(solution)/shard_map/ppermute | solution.py:59
  8.1 3.2 %collective-permute-start.1 = (bf16[256,1024]{1,0:T(8,128)(2,1)S(1)}, bf16[256,1024]{1,0:T(8,128)(2,1)S(1)}, u32[]{:S(2)}, u32[]{:S(2)}) collective-permute-start(bf16[256,1024]{1,0:T(8,128)(2,1)S(1)} %get-tuple-element.61), channel_id=1, source_target_pairs={{0,1},{1,0},{2,3},{3,2},{4,5},{5,4},{6,7},{7,6},{8,9},{9,8},{10,11... | collective-permute-start | bytes 1572872 | tf_op jit(solution)/shard_map/ppermute | solution.py:59
  8.2 22.5 %collective-permute-start.7 = (bf16[512,768]{1,0:T(8,128)(2,1)S(1)}, bf16[512,768]{1,0:T(8,128)(2,1)S(1)}, u32[]{:S(2)}, u32[]{:S(2)}) collective-permute-start(bf16[512,768]{1,0:T(8,128)(2,1)S(1)} %copy-done.1), channel_id=1, source_target_pairs={{0,15},{1,0},{2,1},{3,2},{4,3},{5,4},{6,5},{7,6},{8,7},{9,8},{10,9... | collective-permute-start | bytes 2359304 | tf_op jit(solution)/shard_map/ppermute | solution.py:50
  11.4 24.7 %copy-start.7 = (f32[768]{0:T(1024)S(1)}, f32[768]{0:T(1024)}, u32[]{:S(2)}) copy-start(f32[768]{0:T(1024)} %param.12) | copy-start | bytes 9220
  11.5 24.7 %copy-start.8 = (f32[768]{0:T(1024)S(1)}, f32[768]{0:T(1024)}, u32[]{:S(2)}) copy-start(f32[768]{0:T(1024)} %param.13) | copy-start | bytes 9220
  11.5 24.7 %copy-start.2 = (bf16[512,768]{1,0:T(8,128)(2,1)S(1)}, bf16[512,768]{1,0:T(8,128)(2,1)}, u32[]{:S(2)}) copy-start(bf16[512,768]{1,0:T(8,128)(2,1)} %o_ref.1) | copy-start | bytes 2359300
  11.6 19.8 %collective-permute-start.6 = (bf16[80,2048]{1,0:T(8,128)(2,1)S(1)}, bf16[80,2048]{1,0:T(8,128)(2,1)S(1)}, u32[]{:S(2)}, u32[]{:S(2)}) collective-permute-start(bf16[80,2048]{1,0:T(8,128)(2,1)S(1)} %get-tuple-element.69), channel_id=1, source_target_pairs={{0,2},{1,3},{2,0},{3,1},{4,6},{5,7},{6,4},{7,5},{8,10},{9,11},{10,... | collective-permute-start | bytes 983048 | tf_op jit(solution)/shard_map/ppermute | solution.py:59
  12.3 15.3 %collective-permute-start.2 = (bf16[96,512]{1,0:T(8,128)(2,1)S(1)}, bf16[96,512]{1,0:T(8,128)(2,1)S(1)}, u32[]{:S(2)}, u32[]{:S(2)}) collective-permute-start(bf16[96,512]{1,0:T(8,128)(2,1)S(1)} %get-tuple-element.65), channel_id=1, source_target_pairs={{0,12},{1,13},{2,14},{3,15},{4,8},{5,9},{6,10},{7,11},{8,4},{9,5},... | collective-permute-start | bytes 294920 | tf_op jit(solution)/shard_map/ppermute | solution.py:59
  14.7 16.0 %collective-permute-start.3 = (bf16[96,512]{1,0:T(8,128)(2,1)S(1)}, bf16[96,512]{1,0:T(8,128)(2,1)S(1)}, u32[]{:S(2)}, u32[]{:S(2)}) collective-permute-start(bf16[96,512]{1,0:T(8,128)(2,1)S(1)} %get-tuple-element.66), channel_id=1, source_target_pairs={{0,8},{1,9},{2,10},{3,11},{4,12},{5,13},{6,14},{7,15},{8,0},{9,1},... | collective-permute-start | bytes 294920 | tf_op jit(solution)/shard_map/ppermute | solution.py:59
  16.1 15.3 %collective-permute-start.5 = (bf16[96,512]{1,0:T(8,128)(2,1)S(1)}, bf16[96,512]{1,0:T(8,128)(2,1)S(1)}, u32[]{:S(2)}, u32[]{:S(2)}) collective-permute-start(bf16[96,512]{1,0:T(8,128)(2,1)S(1)} %get-tuple-element.68), channel_id=1, source_target_pairs={{0,4},{1,5},{2,6},{3,7},{4,0},{5,1},{6,2},{7,3},{8,12},{9,13},{10,... | collective-permute-start | bytes 294920 | tf_op jit(solution)/shard_map/ppermute | solution.py:59
  31.5 4.8 %copy-start.3 = (bf16[2,128,128]{2,1,0:T(8,128)(2,1)S(1)}, bf16[2,128,128]{2,1,0:T(8,128)(2,1)}, u32[]{:S(2)}) copy-start(bf16[2,128,128]{2,1,0:T(8,128)(2,1)} %constant.2.clone.refs_4_) | copy-start | bytes 196612
  31.5 4.8 %copy-start.4 = (f32[512]{0:T(512)S(1)}, f32[512]{0:T(512)}, u32[]{:S(2)}) copy-start(f32[512]{0:T(512)} %param.14) | copy-start | bytes 6148
  31.5 4.8 %copy-start.5 = (s32[512]{0:T(512)S(1)}, s32[512]{0:T(512)}, u32[]{:S(2)}) copy-start(s32[512]{0:T(512)} %param.15) | copy-start | bytes 6148
  31.5 4.8 %copy-start.6 = (s32[512]{0:T(512)S(1)}, s32[512]{0:T(512)}, u32[]{:S(2)}) copy-start(s32[512]{0:T(512)} %param.16) | copy-start | bytes 6148
  31.6 8.7 %collective-permute-start.10 = (bf16[80,512]{1,0:T(8,128)(2,1)S(1)}, bf16[80,512]{1,0:T(8,128)(2,1)S(1)}, u32[]{:S(2)}, u32[]{:S(2)}) collective-permute-start(bf16[80,512]{1,0:T(8,128)(2,1)S(1)} %get-tuple-element.75), channel_id=1, source_target_pairs={{0,12},{1,13},{2,14},{3,15},{4,8},{5,9},{6,10},{7,11},{8,4},{9,5},... | collective-permute-start | bytes 245768 | tf_op jit(solution)/shard_map/ppermute | solution.py:59
  33.9 6.3 %collective-permute-start.8 = (bf16[80,512]{1,0:T(8,128)(2,1)S(1)}, bf16[80,512]{1,0:T(8,128)(2,1)S(1)}, u32[]{:S(2)}, u32[]{:S(2)}) collective-permute-start(bf16[80,512]{1,0:T(8,128)(2,1)S(1)} %get-tuple-element.73), channel_id=1, source_target_pairs={{0,4},{1,5},{2,6},{3,7},{4,0},{5,1},{6,2},{7,3},{8,12},{9,13},{10,... | collective-permute-start | bytes 245768 | tf_op jit(solution)/shard_map/ppermute | solution.py:59
  33.9 7.5 %collective-permute-start.9 = (bf16[80,512]{1,0:T(8,128)(2,1)S(1)}, bf16[80,512]{1,0:T(8,128)(2,1)S(1)}, u32[]{:S(2)}, u32[]{:S(2)}) collective-permute-start(bf16[80,512]{1,0:T(8,128)(2,1)S(1)} %get-tuple-element.74), channel_id=1, source_target_pairs={{0,8},{1,9},{2,10},{3,11},{4,12},{5,13},{6,14},{7,15},{8,0},{9,1},... | collective-permute-start | bytes 245768 | tf_op jit(solution)/shard_map/ppermute | solution.py:59
  36.1 4.2 %collective-permute-start.11 = (bf16[48,512]{1,0:T(8,128)(2,1)S(1)}, bf16[48,512]{1,0:T(8,128)(2,1)S(1)}, u32[]{:S(2)}, u32[]{:S(2)}) collective-permute-start(bf16[48,512]{1,0:T(8,128)(2,1)S(1)} %get-tuple-element.80), channel_id=1, source_target_pairs={{0,2},{1,3},{2,0},{3,1},{4,6},{5,7},{6,4},{7,5},{8,10},{9,11},{10,... | collective-permute-start | bytes 147464 | tf_op jit(solution)/shard_map/ppermute | solution.py:59
  36.3 26.0 %copy-start = (bf16[2048,768]{1,0:T(8,128)(2,1)S(1)}, bf16[2048,768]{1,0:T(8,128)(2,1)}, u32[]{:S(2)}) copy-start(bf16[2048,768]{1,0:T(8,128)(2,1)} %refs_3_.7) | copy-start | bytes 9437188
  41.4 8.5 %collective-permute-start.12 = (bf16[80,512]{1,0:T(8,128)(2,1)S(1)}, bf16[80,512]{1,0:T(8,128)(2,1)S(1)}, u32[]{:S(2)}, u32[]{:S(2)}) collective-permute-start(bf16[80,512]{1,0:T(8,128)(2,1)S(1)} %get-tuple-element.91.refs_0_), channel_id=1, source_target_pairs={{0,12},{1,13},{2,14},{3,15},{4,8},{5,9},{6,10},{7,11},{8,4},{9,5},... | collective-permute-start | bytes 245768 | tf_op jit(solution)/shard_map/ppermute | solution.py:59
  43.6 6.9 %collective-permute-start.13 = (bf16[80,512]{1,0:T(8,128)(2,1)S(1)}, bf16[80,512]{1,0:T(8,128)(2,1)S(1)}, u32[]{:S(2)}, u32[]{:S(2)}) collective-permute-start(bf16[80,512]{1,0:T(8,128)(2,1)S(1)} %get-tuple-element.91.refs_0_), channel_id=1, source_target_pairs={{0,8},{1,9},{2,10},{3,11},{4,12},{5,13},{6,14},{7,15},{8,0},{9,1},... | collective-permute-start | bytes 245768 | tf_op jit(solution)/shard_map/ppermute | solution.py:59
  43.6 6.9 %collective-permute-start.14 = (bf16[80,512]{1,0:T(8,128)(2,1)S(1)}, bf16[80,512]{1,0:T(8,128)(2,1)S(1)}, u32[]{:S(2)}, u32[]{:S(2)}) collective-permute-start(bf16[80,512]{1,0:T(8,128)(2,1)S(1)} %get-tuple-element.91.refs_0_), channel_id=1, source_target_pairs={{0,4},{1,5},{2,6},{3,7},{4,0},{5,1},{6,2},{7,3},{8,12},{9,13},{10,... | collective-permute-start | bytes 245768 | tf_op jit(solution)/shard_map/ppermute | solution.py:59
  45.9 4.1 %collective-permute-start.15 = (bf16[48,512]{1,0:T(8,128)(2,1)S(1)}, bf16[48,512]{1,0:T(8,128)(2,1)S(1)}, u32[]{:S(2)}, u32[]{:S(2)}) collective-permute-start(bf16[48,512]{1,0:T(8,128)(2,1)S(1)} %get-tuple-element.95.refs_0_), channel_id=1, source_target_pairs={{0,2},{1,3},{2,0},{3,1},{4,6},{5,7},{6,4},{7,5},{8,10},{9,11},{10,... | collective-permute-start | bytes 147464 | tf_op jit(solution)/shard_map/ppermute | solution.py:59
  50.6 11.6 %collective-permute-start.17 = (bf16[80,2048]{1,0:T(8,128)(2,1)S(1)}, bf16[80,2048]{1,0:T(8,128)(2,1)S(1)}, u32[]{:S(2)}, u32[]{:S(2)}) collective-permute-start(bf16[80,2048]{1,0:T(8,128)(2,1)S(1)} %shard_map.112.refs_0_), channel_id=1, source_target_pairs={{0,2},{1,3},{2,0},{3,1},{4,6},{5,7},{6,4},{7,5},{8,10},{9,11},{10,... | collective-permute-start | bytes 983048 | tf_op jit(solution)/shard_map/ppermute | solution.py:59
  51.0 7.6 %collective-permute-start.19 = (bf16[96,512]{1,0:T(8,128)(2,1)S(1)}, bf16[96,512]{1,0:T(8,128)(2,1)S(1)}, u32[]{:S(2)}, u32[]{:S(2)}) collective-permute-start(bf16[96,512]{1,0:T(8,128)(2,1)S(1)} %shard_map.113.refs_0_), channel_id=1, source_target_pairs={{0,12},{1,13},{2,14},{3,15},{4,8},{5,9},{6,10},{7,11},{8,4},{9,5},... | collective-permute-start | bytes 294920 | tf_op jit(solution)/shard_map/ppermute | solution.py:59
  53.7 7.9 %collective-permute-start.20 = (bf16[96,512]{1,0:T(8,128)(2,1)S(1)}, bf16[96,512]{1,0:T(8,128)(2,1)S(1)}, u32[]{:S(2)}, u32[]{:S(2)}) collective-permute-start(bf16[96,512]{1,0:T(8,128)(2,1)S(1)} %shard_map.113.refs_0_), channel_id=1, source_target_pairs={{0,8},{1,9},{2,10},{3,11},{4,12},{5,13},{6,14},{7,15},{8,0},{9,1},... | collective-permute-start | bytes 294920 | tf_op jit(solution)/shard_map/ppermute | solution.py:59
  53.7 7.9 %collective-permute-start.21 = (bf16[96,512]{1,0:T(8,128)(2,1)S(1)}, bf16[96,512]{1,0:T(8,128)(2,1)S(1)}, u32[]{:S(2)}, u32[]{:S(2)}) collective-permute-start(bf16[96,512]{1,0:T(8,128)(2,1)S(1)} %shard_map.113.refs_0_), channel_id=1, source_target_pairs={{0,4},{1,5},{2,6},{3,7},{4,0},{5,1},{6,2},{7,3},{8,12},{9,13},{10,... | collective-permute-start | bytes 294920 | tf_op jit(solution)/shard_map/ppermute | solution.py:59
  61.6 2.3 %collective-permute-start.22 = (bf16[96,2048]{1,0:T(8,128)(2,1)S(1)}, bf16[96,2048]{1,0:T(8,128)(2,1)S(1)}, u32[]{:S(2)}, u32[]{:S(2)}) collective-permute-start(bf16[96,2048]{1,0:T(8,128)(2,1)S(1)} %shard_map.114.refs_2_), channel_id=1, source_target_pairs={{0,1},{1,0},{2,3},{3,2},{4,5},{5,4},{6,7},{7,6},{8,9},{9,8},{10,11... | collective-permute-start | bytes 1179656 | tf_op jit(solution)/shard_map/ppermute | solution.py:59
  61.7 2.2 %collective-permute-start.16 = (bf16[80,2048]{1,0:T(8,128)(2,1)S(1)}, bf16[80,2048]{1,0:T(8,128)(2,1)S(1)}, u32[]{:S(2)}, u32[]{:S(2)}) collective-permute-start(bf16[80,2048]{1,0:T(8,128)(2,1)S(1)} %shard_map.112.refs_0_), channel_id=1, source_target_pairs={{0,1},{1,0},{2,3},{3,2},{4,5},{5,4},{6,7},{7,6},{8,9},{9,8},{10,11... | collective-permute-start | bytes 983048 | tf_op jit(solution)/shard_map/ppermute | solution.py:59
  62.2 2.1 %collective-permute-start.18 = (bf16[80,2048]{1,0:T(8,128)(2,1)S(1)}, bf16[80,2048]{1,0:T(8,128)(2,1)S(1)}, u32[]{:S(2)}, u32[]{:S(2)}) collective-permute-start(bf16[80,2048]{1,0:T(8,128)(2,1)S(1)} %collective-permute-done.17.refs_1_), channel_id=1, source_target_pairs={{0,1},{1,0},{2,3},{3,2},{4,5},{5,4},{6,7},{7,6},{8,9},{9,8},{10,11... | collective-permute-start | bytes 983048 | tf_op jit(solution)/shard_map/ppermute | solution.py:59
  65.9 1.3 %collective-permute-start.23 = (bf16[320,128]{1,0:T(8,128)(2,1)S(1)}, bf16[320,128]{1,0:T(8,128)(2,1)S(1)}, u32[]{:S(2)}, u32[]{:S(2)}) collective-permute-start(bf16[320,128]{1,0:T(8,128)(2,1)S(1)} %get-tuple-element.104), channel_id=1, source_target_pairs={{0,1},{1,0},{2,3},{3,2},{4,5},{5,4},{6,7},{7,6},{8,9},{9,8},{10,11... | collective-permute-start | bytes 245768 | tf_op jit(solution)/shard_map/ppermute | solution.py:59
  67.2 4.6 %collective-permute-start.24 = (bf16[320,128]{1,0:T(8,128)(2,1)S(1)}, bf16[320,128]{1,0:T(8,128)(2,1)S(1)}, u32[]{:S(2)}, u32[]{:S(2)}) collective-permute-start(bf16[320,128]{1,0:T(8,128)(2,1)S(1)} %get-tuple-element.106), channel_id=1, source_target_pairs={{0,2},{1,3},{2,0},{3,1},{4,6},{5,7},{6,4},{7,5},{8,10},{9,11},{10,... | collective-permute-start | bytes 245768 | tf_op jit(solution)/shard_map/ppermute | solution.py:59
  71.8 7.0 %collective-permute-start.25 = (bf16[320,128]{1,0:T(8,128)(2,1)S(1)}, bf16[320,128]{1,0:T(8,128)(2,1)S(1)}, u32[]{:S(2)}, u32[]{:S(2)}) collective-permute-start(bf16[320,128]{1,0:T(8,128)(2,1)S(1)} %get-tuple-element.108), channel_id=1, source_target_pairs={{0,12},{1,13},{2,14},{3,15},{4,8},{5,9},{6,10},{7,11},{8,4},{9,5},... | collective-permute-start | bytes 245768 | tf_op jit(solution)/shard_map/ppermute | solution.py:59
  74.1 7.0 %collective-permute-start.26 = (bf16[320,128]{1,0:T(8,128)(2,1)S(1)}, bf16[320,128]{1,0:T(8,128)(2,1)S(1)}, u32[]{:S(2)}, u32[]{:S(2)}) collective-permute-start(bf16[320,128]{1,0:T(8,128)(2,1)S(1)} %get-tuple-element.108), channel_id=1, source_target_pairs={{0,8},{1,9},{2,10},{3,11},{4,12},{5,13},{6,14},{7,15},{8,0},{9,1},... | collective-permute-start | bytes 245768 | tf_op jit(solution)/shard_map/ppermute | solution.py:59
  74.1 7.0 %collective-permute-start.27 = (bf16[320,128]{1,0:T(8,128)(2,1)S(1)}, bf16[320,128]{1,0:T(8,128)(2,1)S(1)}, u32[]{:S(2)}, u32[]{:S(2)}) collective-permute-start(bf16[320,128]{1,0:T(8,128)(2,1)S(1)} %get-tuple-element.108), channel_id=1, source_target_pairs={{0,4},{1,5},{2,6},{3,7},{4,0},{5,1},{6,2},{7,3},{8,12},{9,13},{10,... | collective-permute-start | bytes 245768 | tf_op jit(solution)/shard_map/ppermute | solution.py:59
  81.1 1.3 %collective-permute-start.28 = (bf16[320,128]{1,0:T(8,128)(2,1)S(1)}, bf16[320,128]{1,0:T(8,128)(2,1)S(1)}, u32[]{:S(2)}, u32[]{:S(2)}) collective-permute-start(bf16[320,128]{1,0:T(8,128)(2,1)S(1)} %shard_map.119.refs_0_), channel_id=1, source_target_pairs={{0,1},{1,0},{2,3},{3,2},{4,5},{5,4},{6,7},{7,6},{8,9},{9,8},{10,11... | collective-permute-start | bytes 245768 | tf_op jit(solution)/shard_map/ppermute | solution.py:59

commit v24 on v23

--- a/solution.py
+++ b/solution.py
@@ -29,7 +29,7 @@
 MIB = 1024 * 1024
 VMEM_BYTES = 24 * MIB
 REDUCE_SHARE = 0.625
-GATHER_SHARE = 0.625
+GATHER_SHARE = 0.5
 BF16 = jnp.bfloat16
 F32 = jnp.float32
 NT = (((1,), (1,)), ((), ()))

time: 83.8 us -> 84.5 us (level)
  waiting for transfers between devices: 38.3 us -> 40.5 us
  starting transfers between devices: 31.7 us -> 30.3 us
    ppermute x27, waiting for transfers between devices: 37.6 us -> 39.7 us  [swapped(): return lax.ppermute(array, 'band', pairs)]
    ppermute x27, starting transfers between devices: 28.1 us -> 26.7 us  [swapped(): return lax.ppermute(array, 'band', pairs)]
  transfers between devices with their start and end apart: 29 -> 29, of which waited for: 17 -> 18; matrix products, arithmetic and copies ran while one was open for 0% -> 0% of each run, Pallas kernels for 12% -> 12%
where the time goes in v24:
time: 84.5 us; the launch traced here: 84.3 us
  waiting for transfers between devices  40.5 us (48%)
  starting transfers between devices  30.3 us (36%)
  Pallas kernels  12.6 us (15%)
  between operations  0.91 us (1%)
    ppermute x27, waiting for transfers between devices, swapped(): return lax.ppermute(array, 'band', pairs)  39.7 us
    ppermute x27, starting transfers between devices, swapped(): return lax.ppermute(array, 'band', pairs)  26.7 us
    pallas_call x1, Pallas kernels, first_sums(): pl.pallas_call(functools.partial(first_body, core, block, tile), out_shap...  4.34 us
    pallas_call x14, Pallas kernels, local_call(): pl.pallas_call(body, out_shape=outs, in_specs=[whole() for _ in args], ou...  3.66 us
    ppermute x2, starting transfers between devices, neighbour(): lax.ppermute(array, 'band', [(i, (i + step) % count) for i in range(count)])  3.62 us
    pallas_call x2, Pallas kernels, project(): pl.pallas_call(functools.partial(project_body, core, blk, other), out_sha...  2.4 us
    pallas_call x1, Pallas kernels, local_part(): pl.pallas_call(functools.partial(local_body, depth, (group_rows, blk)), g...  2.24 us
  transfers between devices with their start and end apart: 29, of which 18 were waited for; matrix products, arithmetic and copies ran while one was open for 0% of the time, Pallas kernels for 12%

profile of v24, /device:TPU:0, one launch (start us, length us, event | category | flops | bytes accessed | tf_op | source)
XLA Modules:
  0.0 84.3 jit_solution(291079773735679154)
XLA Ops:
  0.6 0.5 collective-permute-start.4
  1.1 4.3 %shard_map.104 = (bf16[256,1024]{1,0:T(8,128)(2,1)S(1)}, bf16[256,1024]{1,0:T(8,128)(2,1)S(1)}, f32[160,2048]{1,0:T(8,128)S(1)}, f32[96,2048]{1,0:T(8,128)S(1)}) custom-call(bf16[512,768]{1,0:T(8,128)(2,1)} %refs_3_.9, bf16[2048,768]{1,0:T(8,128)(2,1)} %refs_3_.7), custom_call_target="tpu_custom_call" | custom-call | flops 1610612736 | bytes 6291456 | tf_op jit(solution)/shard_map/pallas_call | solution.py:153
  5.5 2.6 %collective-permute-start = (bf16[256,1024]{1,0:T(8,128)(2,1)S(1)}, bf16[256,1024]{1,0:T(8,128)(2,1)S(1)}, u32[]{:S(2)}, u32[]{:S(2)}) collective-permute-start(bf16[256,1024]{1,0:T(8,128)(2,1)S(1)} %get-tuple-element.60), channel_id=1, source_target_pairs={{0,1},{1,0},{2,3},{3,2},{4,5},{5,4},{6,7},{7,6},{8,9},{9,8},{10,11... | collective-permute-start | bytes 1572872 | tf_op jit(solution)/shard_map/ppermute | solution.py:59
  8.1 0.1 collective-permute-start.1
  8.2 3.1 %collective-permute-start.7 = (bf16[512,768]{1,0:T(8,128)(2,1)S(1)}, bf16[512,768]{1,0:T(8,128)(2,1)S(1)}, u32[]{:S(2)}, u32[]{:S(2)}) collective-permute-start(bf16[512,768]{1,0:T(8,128)(2,1)S(1)} %copy-done.1), channel_id=1, source_target_pairs={{0,15},{1,0},{2,1},{3,2},{4,3},{5,4},{6,5},{7,6},{8,7},{9,8},{10,9... | collective-permute-start | bytes 2359304 | tf_op jit(solution)/shard_map/ppermute | solution.py:50
  11.3 0.1 shard_map.105
  11.4 0.0 copy-start.7
  11.5 0.0 copy-start.8
  11.5 0.0 copy-start.2
  11.5 0.1 shard_map.106
  11.6 0.7 collective-permute-start.6
  12.3 2.4 %collective-permute-start.2 = (bf16[96,512]{1,0:T(8,128)(2,1)S(1)}, bf16[96,512]{1,0:T(8,128)(2,1)S(1)}, u32[]{:S(2)}, u32[]{:S(2)}) collective-permute-start(bf16[96,512]{1,0:T(8,128)(2,1)S(1)} %get-tuple-element.65), channel_id=1, source_target_pairs={{0,12},{1,13},{2,14},{3,15},{4,8},{5,9},{6,10},{7,11},{8,4},{9,5},... | collective-permute-start | bytes 294920 | tf_op jit(solution)/shard_map/ppermute | solution.py:59
  14.7 0.7 collective-permute-start.3
  15.4 0.8 collective-permute-done.4.refs_1_
  16.1 0.6 collective-permute-start.5
  16.7 10.9 %collective-permute-done.2.refs_1_ = bf16[96,512]{1,0:T(8,128)(2,1)S(1)} collective-permute-done((bf16[96,512]{1,0:T(8,128)(2,1)S(1)}, bf16[96,512]{1,0:T(8,128)(2,1)S(1)}, u32[]{:S(2)}, u32[]{:S(2)}) %collective-permute-start.2) | collective-permute-done | bytes 98336 | tf_op jit(solution)/shard_map/ppermute | solution.py:59
  27.6 3.1 %collective-permute-done.3.refs_2_ = bf16[96,512]{1,0:T(8,128)(2,1)S(1)} collective-permute-done((bf16[96,512]{1,0:T(8,128)(2,1)S(1)}, bf16[96,512]{1,0:T(8,128)(2,1)S(1)}, u32[]{:S(2)}, u32[]{:S(2)}) %collective-permute-start.3) | collective-permute-done | bytes 98336 | tf_op jit(solution)/shard_map/ppermute | solution.py:59
  30.7 0.7 collective-permute-done.6.refs_1_
  31.4 0.0 collective-permute-done.5.refs_3_
  31.5 0.0 copy-start.6
  31.5 0.1 shard_map.107
  31.6 2.3 %collective-permute-start.10 = (bf16[80,512]{1,0:T(8,128)(2,1)S(1)}, bf16[80,512]{1,0:T(8,128)(2,1)S(1)}, u32[]{:S(2)}, u32[]{:S(2)}) collective-permute-start(bf16[80,512]{1,0:T(8,128)(2,1)S(1)} %get-tuple-element.75), channel_id=1, source_target_pairs={{0,12},{1,13},{2,14},{3,15},{4,8},{5,9},{6,10},{7,11},{8,4},{9,5},... | collective-permute-start | bytes 245768 | tf_op jit(solution)/shard_map/ppermute | solution.py:59
  33.9 2.1 %collective-permute-start.9 = (bf16[80,512]{1,0:T(8,128)(2,1)S(1)}, bf16[80,512]{1,0:T(8,128)(2,1)S(1)}, u32[]{:S(2)}, u32[]{:S(2)}) collective-permute-start(bf16[80,512]{1,0:T(8,128)(2,1)S(1)} %get-tuple-element.74), channel_id=1, source_target_pairs={{0,8},{1,9},{2,10},{3,11},{4,12},{5,13},{6,14},{7,15},{8,0},{9,1},... | collective-permute-start | bytes 245768 | tf_op jit(solution)/shard_map/ppermute | solution.py:59
  36.1 0.1 collective-permute-start.11
  36.2 0.1 shard_map.110.refs_5_.refs_2_
  36.3 0.0 copy-start
  36.3 2.2 %shard_map.109 = (f32[512,768]{1,0:T(8,128)S(1)}, bf16[512,256]{1,0:T(8,128)(2,1)S(1)}) custom-call(bf16[512,768]{1,0:T(8,128)(2,1)S(1)} %copy-done.1, bf16[512,768]{1,0:T(8,128)(2,1)S(1)} %collective-permute-done.4.refs_1_, bf16[512,768]{1,0:T(8,128)(2,1)S(1)} %collective-permute-done.7.refs_2_, bf16[512,768]{1,0:T(8,128)(2,1)S(1)} %copy-done.2, ...), custom_call_target="tpu_custom_call" | custom-call | flops 235929600 | bytes 4980736 | tf_op jit(solution)/shard_map/pallas_call | solution.py:333
  38.6 1.6 %collective-permute-done.11.refs_5_ = bf16[48,512]{1,0:T(8,128)(2,1)S(1)} collective-permute-done((bf16[48,512]{1,0:T(8,128)(2,1)S(1)}, bf16[48,512]{1,0:T(8,128)(2,1)S(1)}, u32[]{:S(2)}, u32[]{:S(2)}) %collective-permute-start.11) | collective-permute-done | bytes 49184 | tf_op jit(solution)/shard_map/ppermute | solution.py:59
  40.2 1.2 %collective-permute-done.9.refs_2_ = bf16[80,512]{1,0:T(8,128)(2,1)S(1)} collective-permute-done((bf16[80,512]{1,0:T(8,128)(2,1)S(1)}, bf16[80,512]{1,0:T(8,128)(2,1)S(1)}, u32[]{:S(2)}, u32[]{:S(2)}) %collective-permute-start.9) | collective-permute-done | bytes 81952 | tf_op jit(solution)/shard_map/ppermute | solution.py:59
  41.4 0.1 shard_map.111
  41.4 2.2 %collective-permute-start.12 = (bf16[64,512]{1,0:T(8,128)(2,1)S(1)}, bf16[64,512]{1,0:T(8,128)(2,1)S(1)}, u32[]{:S(2)}, u32[]{:S(2)}) collective-permute-start(bf16[64,512]{1,0:T(8,128)(2,1)S(1)} %get-tuple-element.91.refs_0_), channel_id=1, source_target_pairs={{0,12},{1,13},{2,14},{3,15},{4,8},{5,9},{6,10},{7,11},{8,4},{9,5},... | collective-permute-start | bytes 196616 | tf_op jit(solution)/shard_map/ppermute | solution.py:59
  43.6 2.3 %collective-permute-start.14 = (bf16[64,512]{1,0:T(8,128)(2,1)S(1)}, bf16[64,512]{1,0:T(8,128)(2,1)S(1)}, u32[]{:S(2)}, u32[]{:S(2)}) collective-permute-start(bf16[64,512]{1,0:T(8,128)(2,1)S(1)} %get-tuple-element.91.refs_0_), channel_id=1, source_target_pairs={{0,4},{1,5},{2,6},{3,7},{4,0},{5,1},{6,2},{7,3},{8,12},{9,13},{10,... | collective-permute-start | bytes 196616 | tf_op jit(solution)/shard_map/ppermute | solution.py:59
  45.9 2.4 %collective-permute-done.12.refs_1_ = bf16[64,512]{1,0:T(8,128)(2,1)S(1)} collective-permute-done((bf16[64,512]{1,0:T(8,128)(2,1)S(1)}, bf16[64,512]{1,0:T(8,128)(2,1)S(1)}, u32[]{:S(2)}, u32[]{:S(2)}) %collective-permute-start.12) | collective-permute-done | bytes 65568 | tf_op jit(solution)/shard_map/ppermute | solution.py:59
  48.3 1.3 %collective-permute-done.13.refs_2_ = bf16[64,512]{1,0:T(8,128)(2,1)S(1)} collective-permute-done((bf16[64,512]{1,0:T(8,128)(2,1)S(1)}, bf16[64,512]{1,0:T(8,128)(2,1)S(1)}, u32[]{:S(2)}, u32[]{:S(2)}) %collective-permute-start.13) | collective-permute-done | bytes 65568 | tf_op jit(solution)/shard_map/ppermute | solution.py:59
  49.6 0.0 collective-permute-done.14.refs_3_
  49.6 0.6 collective-permute-done.15.refs_1_
  50.2 2.2 %collective-permute-start.19 = (bf16[128,512]{1,0:T(8,128)(2,1)S(1)}, bf16[128,512]{1,0:T(8,128)(2,1)S(1)}, u32[]{:S(2)}, u32[]{:S(2)}) collective-permute-start(bf16[128,512]{1,0:T(8,128)(2,1)S(1)} %shard_map.113.refs_0_), channel_id=1, source_target_pairs={{0,12},{1,13},{2,14},{3,15},{4,8},{5,9},{6,10},{7,11},{8,4},{9,5},... | collective-permute-start | bytes 393224 | tf_op jit(solution)/shard_map/ppermute | solution.py:59
  52.4 2.3 %collective-permute-start.21 = (bf16[128,512]{1,0:T(8,128)(2,1)S(1)}, bf16[128,512]{1,0:T(8,128)(2,1)S(1)}, u32[]{:S(2)}, u32[]{:S(2)}) collective-permute-start(bf16[128,512]{1,0:T(8,128)(2,1)S(1)} %shard_map.113.refs_0_), channel_id=1, source_target_pairs={{0,4},{1,5},{2,6},{3,7},{4,0},{5,1},{6,2},{7,3},{8,12},{9,13},{10,... | collective-permute-start | bytes 393224 | tf_op jit(solution)/shard_map/ppermute | solution.py:59
  54.7 0.1 collective-permute-start.17
  54.7 3.5 %collective-permute-done.19.refs_1_ = bf16[128,512]{1,0:T(8,128)(2,1)S(1)} collective-permute-done((bf16[128,512]{1,0:T(8,128)(2,1)S(1)}, bf16[128,512]{1,0:T(8,128)(2,1)S(1)}, u32[]{:S(2)}, u32[]{:S(2)}) %collective-permute-start.19) | collective-permute-done | bytes 131104 | tf_op jit(solution)/shard_map/ppermute | solution.py:59
  58.3 4.1 %collective-permute-done.20.refs_2_ = bf16[128,512]{1,0:T(8,128)(2,1)S(1)} collective-permute-done((bf16[128,512]{1,0:T(8,128)(2,1)S(1)}, bf16[128,512]{1,0:T(8,128)(2,1)S(1)}, u32[]{:S(2)}, u32[]{:S(2)}) %collective-permute-start.20) | collective-permute-done | bytes 131104 | tf_op jit(solution)/shard_map/ppermute | solution.py:59
  62.4 0.0 collective-permute-done.21.refs_3_
  62.4 0.1 shard_map.114.refs_2_
  62.5 0.1 collective-permute-start.22
  62.6 0.5 collective-permute-start.16
  63.1 0.0 collective-permute-done.17.refs_1_
  63.1 0.1 collective-permute-start.18
  63.2 1.5 %shard_map.115 = (f32[256,768]{1,0:T(8,128)S(1)}, f32[320,128]{1,0:T(8,128)S(1)}) custom-call(bf16[64,2048]{1,0:T(8,128)(2,1)S(1)} %shard_map.112.refs_0_, bf16[64,2048]{1,0:T(8,128)(2,1)S(1)} %collective-permute-done.17.refs_1_, bf16[128,2048]{1,0:T(8,128)(2,1)S(1)} %shard_map.114.refs_2_, bf16[2048,768]{1,0:T(8,128)(2,1)S(1)} %copy-done, ...), custom_call_target="tpu_custom_call" | custom-call | flops 905969664 | bytes 7700480 | tf_op jit(solution)/shard_map/pallas_call | solution.py:91
  64.7 0.2 collective-permute-done.16.refs_0_
  64.8 0.4 collective-permute-done.18.refs_1_
  65.2 0.0 collective-permute-done.22.refs_2_
  65.2 1.5 %shard_map.116 = (f32[256,768]{1,0:T(8,128)S(1)}, bf16[320,128]{1,0:T(8,128)(2,1)S(1)}) custom-call(bf16[64,2048]{1,0:T(8,128)(2,1)S(1)} %collective-permute-done.16.refs_0_, bf16[64,2048]{1,0:T(8,128)(2,1)S(1)} %collective-permute-done.18.refs_1_, bf16[128,2048]{1,0:T(8,128)(2,1)S(1)} %collective-permute-done.22.refs_2_, bf16[2048,768]{1,0:T(8,128)(2,1)S(1)} %copy-done, ...), custom_call_target="tpu_custom_call" | custom-call | flops 905969664 | bytes 7618560 | tf_op jit(solution)/shard_map/pallas_call | solution.py:91
  66.7 0.2 collective-permute-start.23
  66.9 1.1 %collective-permute-done.23.refs_0_ = bf16[320,128]{1,0:T(8,128)(2,1)S(1)} collective-permute-done((bf16[320,128]{1,0:T(8,128)(2,1)S(1)}, bf16[320,128]{1,0:T(8,128)(2,1)S(1)}, u32[]{:S(2)}, u32[]{:S(2)}) %collective-permute-start.23) | collective-permute-done | bytes 81952 | tf_op jit(solution)/shard_map/ppermute | solution.py:59
  68.1 0.7 collective-permute-start.24
  68.8 3.8 %collective-permute-done.24.refs_0_ = bf16[320,128]{1,0:T(8,128)(2,1)S(1)} collective-permute-done((bf16[320,128]{1,0:T(8,128)(2,1)S(1)}, bf16[320,128]{1,0:T(8,128)(2,1)S(1)}, u32[]{:S(2)}, u32[]{:S(2)}) %collective-permute-start.24) | collective-permute-done | bytes 81952 | tf_op jit(solution)/shard_map/ppermute | solution.py:59
  72.7 1.8 %collective-permute-start.25 = (bf16[320,128]{1,0:T(8,128)(2,1)S(1)}, bf16[320,128]{1,0:T(8,128)(2,1)S(1)}, u32[]{:S(2)}, u32[]{:S(2)}) collective-permute-start(bf16[320,128]{1,0:T(8,128)(2,1)S(1)} %get-tuple-element.108), channel_id=1, source_target_pairs={{0,12},{1,13},{2,14},{3,15},{4,8},{5,9},{6,10},{7,11},{8,4},{9,5},... | collective-permute-start | bytes 245768 | tf_op jit(solution)/shard_map/ppermute | solution.py:59
  74.5 2.6 %collective-permute-start.27 = (bf16[320,128]{1,0:T(8,128)(2,1)S(1)}, bf16[320,128]{1,0:T(8,128)(2,1)S(1)}, u32[]{:S(2)}, u32[]{:S(2)}) collective-permute-start(bf16[320,128]{1,0:T(8,128)(2,1)S(1)} %get-tuple-element.108), channel_id=1, source_target_pairs={{0,4},{1,5},{2,6},{3,7},{4,0},{5,1},{6,2},{7,3},{8,12},{9,13},{10,... | collective-permute-start | bytes 245768 | tf_op jit(solution)/shard_map/ppermute | solution.py:59
  77.1 2.8 %collective-permute-done.25.refs_0_ = bf16[320,128]{1,0:T(8,128)(2,1)S(1)} collective-permute-done((bf16[320,128]{1,0:T(8,128)(2,1)S(1)}, bf16[320,128]{1,0:T(8,128)(2,1)S(1)}, u32[]{:S(2)}, u32[]{:S(2)}) %collective-permute-start.25) | collective-permute-done | bytes 81952 | tf_op jit(solution)/shard_map/ppermute | solution.py:59
  80.0 1.7 %collective-permute-done.26.refs_1_ = bf16[320,128]{1,0:T(8,128)(2,1)S(1)} collective-permute-done((bf16[320,128]{1,0:T(8,128)(2,1)S(1)}, bf16[320,128]{1,0:T(8,128)(2,1)S(1)}, u32[]{:S(2)}, u32[]{:S(2)}) %collective-permute-start.26) | collective-permute-done | bytes 81952 | tf_op jit(solution)/shard_map/ppermute | solution.py:59
  81.8 0.1 collective-permute-start.28
  81.9 1.2 %shard_map.120 = (bf16[512,768]{1,0:T(8,128)(2,1)}, bf16[512,768]{1,0:T(8,128)(2,1)}) custom-call(bf16[320,128]{1,0:T(8,128)(2,1)S(1)} %shard_map.119.refs_0_, f32[256,768]{1,0:T(8,128)S(1)} %get-tuple-element.111.refs_1_, bf16[640,768]{1,0:T(8,128)(2,1)S(1)} %shard_map.110.refs_5_.refs_2_, bf16[512,768]{1,0:T(8,128)(2,1)S(1)} %copy-done.1, ...), custom_call_target="tpu_custom_call" | custom-call | flops 100663296 | bytes 2555904 | tf_op jit(solution)/shard_map/pallas_call | solution.py:500
  83.1 0.1 collective-permute-done.28.refs_0_
  83.1 1.2 %shard_map.121 = (bf16[512,768]{1,0:T(8,128)(2,1)}, bf16[512,768]{1,0:T(8,128)(2,1)}) custom-call(bf16[320,128]{1,0:T(8,128)(2,1)S(1)} %collective-permute-done.28.refs_0_, f32[256,768]{1,0:T(8,128)S(1)} %get-tuple-element.109.refs_1_, bf16[640,768]{1,0:T(8,128)(2,1)S(1)} %shard_map.110.refs_5_.refs_2_, ...), custom_call_target="tpu_custom_call", output_to_operand_aliasing={{0}: (5, {}), {1}: (6, {})} | custom-call | flops 100663296 | bytes 2555904 | tf_op jit(solution)/shard_map/pallas_call | solution.py:500
  (32 shorter events, 0.2 us)
Async XLA Ops:
  0.6 7.6 %copy-start.1 = (bf16[512,768]{1,0:T(8,128)(2,1)S(1)}, bf16[512,768]{1,0:T(8,128)(2,1)}, u32[]{:S(2)}) copy-start(bf16[512,768]{1,0:T(8,128)(2,1)} %refs_3_.9) | copy-start | bytes 2359300
  0.6 15.5 %collective-permute-start.4 = (bf16[512,768]{1,0:T(8,128)(2,1)}, bf16[512,768]{1,0:T(8,128)(2,1)S(1)}, u32[]{:S(2)}, u32[]{:S(2)}) collective-permute-start(bf16[512,768]{1,0:T(8,128)(2,1)} %refs_3_.9), channel_id=1, source_target_pairs={{0,1},{1,2},{2,3},{3,4},{4,5},{5,6},{6,7},{7,8},{8,9},{9,10},{10,1... | collective-permute-start | bytes 2359304 | tf_op jit(solution)/shard_map/ppermute | solution.py:50
  5.5 5.8 %collective-permute-start = (bf16[256,1024]{1,0:T(8,128)(2,1)S(1)}, bf16[256,1024]{1,0:T(8,128)(2,1)S(1)}, u32[]{:S(2)}, u32[]{:S(2)}) collective-permute-start(bf16[256,1024]{1,0:T(8,128)(2,1)S(1)} %get-tuple-element.60), channel_id=1, source_target_pairs={{0,1},{1,0},{2,3},{3,2},{4,5},{5,4},{6,7},{7,6},{8,9},{9,8},{10,11... | collective-permute-start | bytes 1572872 | tf_op jit(solution)/shard_map/ppermute | solution.py:59
  8.1 3.2 %collective-permute-start.1 = (bf16[256,1024]{1,0:T(8,128)(2,1)S(1)}, bf16[256,1024]{1,0:T(8,128)(2,1)S(1)}, u32[]{:S(2)}, u32[]{:S(2)}) collective-permute-start(bf16[256,1024]{1,0:T(8,128)(2,1)S(1)} %get-tuple-element.61), channel_id=1, source_target_pairs={{0,1},{1,0},{2,3},{3,2},{4,5},{5,4},{6,7},{7,6},{8,9},{9,8},{10,11... | collective-permute-start | bytes 1572872 | tf_op jit(solution)/shard_map/ppermute | solution.py:59
  8.2 22.5 %collective-permute-start.7 = (bf16[512,768]{1,0:T(8,128)(2,1)S(1)}, bf16[512,768]{1,0:T(8,128)(2,1)S(1)}, u32[]{:S(2)}, u32[]{:S(2)}) collective-permute-start(bf16[512,768]{1,0:T(8,128)(2,1)S(1)} %copy-done.1), channel_id=1, source_target_pairs={{0,15},{1,0},{2,1},{3,2},{4,3},{5,4},{6,5},{7,6},{8,7},{9,8},{10,9... | collective-permute-start | bytes 2359304 | tf_op jit(solution)/shard_map/ppermute | solution.py:50
  11.4 24.7 %copy-start.7 = (f32[768]{0:T(1024)S(1)}, f32[768]{0:T(1024)}, u32[]{:S(2)}) copy-start(f32[768]{0:T(1024)} %param.12) | copy-start | bytes 9220
  11.5 24.7 %copy-start.8 = (f32[768]{0:T(1024)S(1)}, f32[768]{0:T(1024)}, u32[]{:S(2)}) copy-start(f32[768]{0:T(1024)} %param.13) | copy-start | bytes 9220
  11.5 24.7 %copy-start.2 = (bf16[512,768]{1,0:T(8,128)(2,1)S(1)}, bf16[512,768]{1,0:T(8,128)(2,1)}, u32[]{:S(2)}) copy-start(bf16[512,768]{1,0:T(8,128)(2,1)} %o_ref.1) | copy-start | bytes 2359300
  11.6 19.8 %collective-permute-start.6 = (bf16[80,2048]{1,0:T(8,128)(2,1)S(1)}, bf16[80,2048]{1,0:T(8,128)(2,1)S(1)}, u32[]{:S(2)}, u32[]{:S(2)}) collective-permute-start(bf16[80,2048]{1,0:T(8,128)(2,1)S(1)} %get-tuple-element.69), channel_id=1, source_target_pairs={{0,2},{1,3},{2,0},{3,1},{4,6},{5,7},{6,4},{7,5},{8,10},{9,11},{10,... | collective-permute-start | bytes 983048 | tf_op jit(solution)/shard_map/ppermute | solution.py:59
  12.3 15.3 %collective-permute-start.2 = (bf16[96,512]{1,0:T(8,128)(2,1)S(1)}, bf16[96,512]{1,0:T(8,128)(2,1)S(1)}, u32[]{:S(2)}, u32[]{:S(2)}) collective-permute-start(bf16[96,512]{1,0:T(8,128)(2,1)S(1)} %get-tuple-element.65), channel_id=1, source_target_pairs={{0,12},{1,13},{2,14},{3,15},{4,8},{5,9},{6,10},{7,11},{8,4},{9,5},... | collective-permute-start | bytes 294920 | tf_op jit(solution)/shard_map/ppermute | solution.py:59
  14.7 16.0 %collective-permute-start.3 = (bf16[96,512]{1,0:T(8,128)(2,1)S(1)}, bf16[96,512]{1,0:T(8,128)(2,1)S(1)}, u32[]{:S(2)}, u32[]{:S(2)}) collective-permute-start(bf16[96,512]{1,0:T(8,128)(2,1)S(1)} %get-tuple-element.66), channel_id=1, source_target_pairs={{0,8},{1,9},{2,10},{3,11},{4,12},{5,13},{6,14},{7,15},{8,0},{9,1},... | collective-permute-start | bytes 294920 | tf_op jit(solution)/shard_map/ppermute | solution.py:59
  16.1 15.3 %collective-permute-start.5 = (bf16[96,512]{1,0:T(8,128)(2,1)S(1)}, bf16[96,512]{1,0:T(8,128)(2,1)S(1)}, u32[]{:S(2)}, u32[]{:S(2)}) collective-permute-start(bf16[96,512]{1,0:T(8,128)(2,1)S(1)} %get-tuple-element.68), channel_id=1, source_target_pairs={{0,4},{1,5},{2,6},{3,7},{4,0},{5,1},{6,2},{7,3},{8,12},{9,13},{10,... | collective-permute-start | bytes 294920 | tf_op jit(solution)/shard_map/ppermute | solution.py:59
  31.5 4.8 %copy-start.3 = (bf16[2,128,128]{2,1,0:T(8,128)(2,1)S(1)}, bf16[2,128,128]{2,1,0:T(8,128)(2,1)}, u32[]{:S(2)}) copy-start(bf16[2,128,128]{2,1,0:T(8,128)(2,1)} %constant.2.clone.refs_4_) | copy-start | bytes 196612
  31.5 4.8 %copy-start.4 = (f32[512]{0:T(512)S(1)}, f32[512]{0:T(512)}, u32[]{:S(2)}) copy-start(f32[512]{0:T(512)} %param.14) | copy-start | bytes 6148
  31.5 4.8 %copy-start.5 = (s32[512]{0:T(512)S(1)}, s32[512]{0:T(512)}, u32[]{:S(2)}) copy-start(s32[512]{0:T(512)} %param.15) | copy-start | bytes 6148
  31.5 4.8 %copy-start.6 = (s32[512]{0:T(512)S(1)}, s32[512]{0:T(512)}, u32[]{:S(2)}) copy-start(s32[512]{0:T(512)} %param.16) | copy-start | bytes 6148
  31.6 8.7 %collective-permute-start.10 = (bf16[80,512]{1,0:T(8,128)(2,1)S(1)}, bf16[80,512]{1,0:T(8,128)(2,1)S(1)}, u32[]{:S(2)}, u32[]{:S(2)}) collective-permute-start(bf16[80,512]{1,0:T(8,128)(2,1)S(1)} %get-tuple-element.75), channel_id=1, source_target_pairs={{0,12},{1,13},{2,14},{3,15},{4,8},{5,9},{6,10},{7,11},{8,4},{9,5},... | collective-permute-start | bytes 245768 | tf_op jit(solution)/shard_map/ppermute | solution.py:59
  33.9 6.3 %collective-permute-start.8 = (bf16[80,512]{1,0:T(8,128)(2,1)S(1)}, bf16[80,512]{1,0:T(8,128)(2,1)S(1)}, u32[]{:S(2)}, u32[]{:S(2)}) collective-permute-start(bf16[80,512]{1,0:T(8,128)(2,1)S(1)} %get-tuple-element.73), channel_id=1, source_target_pairs={{0,4},{1,5},{2,6},{3,7},{4,0},{5,1},{6,2},{7,3},{8,12},{9,13},{10,... | collective-permute-start | bytes 245768 | tf_op jit(solution)/shard_map/ppermute | solution.py:59
  33.9 7.5 %collective-permute-start.9 = (bf16[80,512]{1,0:T(8,128)(2,1)S(1)}, bf16[80,512]{1,0:T(8,128)(2,1)S(1)}, u32[]{:S(2)}, u32[]{:S(2)}) collective-permute-start(bf16[80,512]{1,0:T(8,128)(2,1)S(1)} %get-tuple-element.74), channel_id=1, source_target_pairs={{0,8},{1,9},{2,10},{3,11},{4,12},{5,13},{6,14},{7,15},{8,0},{9,1},... | collective-permute-start | bytes 245768 | tf_op jit(solution)/shard_map/ppermute | solution.py:59
  36.1 4.2 %collective-permute-start.11 = (bf16[48,512]{1,0:T(8,128)(2,1)S(1)}, bf16[48,512]{1,0:T(8,128)(2,1)S(1)}, u32[]{:S(2)}, u32[]{:S(2)}) collective-permute-start(bf16[48,512]{1,0:T(8,128)(2,1)S(1)} %get-tuple-element.80), channel_id=1, source_target_pairs={{0,2},{1,3},{2,0},{3,1},{4,6},{5,7},{6,4},{7,5},{8,10},{9,11},{10,... | collective-permute-start | bytes 147464 | tf_op jit(solution)/shard_map/ppermute | solution.py:59
  36.3 26.8 %copy-start = (bf16[2048,768]{1,0:T(8,128)(2,1)S(1)}, bf16[2048,768]{1,0:T(8,128)(2,1)}, u32[]{:S(2)}) copy-start(bf16[2048,768]{1,0:T(8,128)(2,1)} %refs_3_.7) | copy-start | bytes 9437188
  41.4 6.9 %collective-permute-start.12 = (bf16[64,512]{1,0:T(8,128)(2,1)S(1)}, bf16[64,512]{1,0:T(8,128)(2,1)S(1)}, u32[]{:S(2)}, u32[]{:S(2)}) collective-permute-start(bf16[64,512]{1,0:T(8,128)(2,1)S(1)} %get-tuple-element.91.refs_0_), channel_id=1, source_target_pairs={{0,12},{1,13},{2,14},{3,15},{4,8},{5,9},{6,10},{7,11},{8,4},{9,5},... | collective-permute-start | bytes 196616 | tf_op jit(solution)/shard_map/ppermute | solution.py:59
  43.6 6.0 %collective-permute-start.13 = (bf16[64,512]{1,0:T(8,128)(2,1)S(1)}, bf16[64,512]{1,0:T(8,128)(2,1)S(1)}, u32[]{:S(2)}, u32[]{:S(2)}) collective-permute-start(bf16[64,512]{1,0:T(8,128)(2,1)S(1)} %get-tuple-element.91.refs_0_), channel_id=1, source_target_pairs={{0,8},{1,9},{2,10},{3,11},{4,12},{5,13},{6,14},{7,15},{8,0},{9,1},... | collective-permute-start | bytes 196616 | tf_op jit(solution)/shard_map/ppermute | solution.py:59
  43.6 6.0 %collective-permute-start.14 = (bf16[64,512]{1,0:T(8,128)(2,1)S(1)}, bf16[64,512]{1,0:T(8,128)(2,1)S(1)}, u32[]{:S(2)}, u32[]{:S(2)}) collective-permute-start(bf16[64,512]{1,0:T(8,128)(2,1)S(1)} %get-tuple-element.91.refs_0_), channel_id=1, source_target_pairs={{0,4},{1,5},{2,6},{3,7},{4,0},{5,1},{6,2},{7,3},{8,12},{9,13},{10,... | collective-permute-start | bytes 196616 | tf_op jit(solution)/shard_map/ppermute | solution.py:59
  45.9 4.3 %collective-permute-start.15 = (bf16[64,512]{1,0:T(8,128)(2,1)S(1)}, bf16[64,512]{1,0:T(8,128)(2,1)S(1)}, u32[]{:S(2)}, u32[]{:S(2)}) collective-permute-start(bf16[64,512]{1,0:T(8,128)(2,1)S(1)} %get-tuple-element.95.refs_0_), channel_id=1, source_target_pairs={{0,2},{1,3},{2,0},{3,1},{4,6},{5,7},{6,4},{7,5},{8,10},{9,11},{10,... | collective-permute-start | bytes 196616 | tf_op jit(solution)/shard_map/ppermute | solution.py:59
  50.2 8.1 %collective-permute-start.19 = (bf16[128,512]{1,0:T(8,128)(2,1)S(1)}, bf16[128,512]{1,0:T(8,128)(2,1)S(1)}, u32[]{:S(2)}, u32[]{:S(2)}) collective-permute-start(bf16[128,512]{1,0:T(8,128)(2,1)S(1)} %shard_map.113.refs_0_), channel_id=1, source_target_pairs={{0,12},{1,13},{2,14},{3,15},{4,8},{5,9},{6,10},{7,11},{8,4},{9,5},... | collective-permute-start | bytes 393224 | tf_op jit(solution)/shard_map/ppermute | solution.py:59
  52.4 10.1 %collective-permute-start.20 = (bf16[128,512]{1,0:T(8,128)(2,1)S(1)}, bf16[128,512]{1,0:T(8,128)(2,1)S(1)}, u32[]{:S(2)}, u32[]{:S(2)}) collective-permute-start(bf16[128,512]{1,0:T(8,128)(2,1)S(1)} %shard_map.113.refs_0_), channel_id=1, source_target_pairs={{0,8},{1,9},{2,10},{3,11},{4,12},{5,13},{6,14},{7,15},{8,0},{9,1},... | collective-permute-start | bytes 393224 | tf_op jit(solution)/shard_map/ppermute | solution.py:59
  52.4 10.1 %collective-permute-start.21 = (bf16[128,512]{1,0:T(8,128)(2,1)S(1)}, bf16[128,512]{1,0:T(8,128)(2,1)S(1)}, u32[]{:S(2)}, u32[]{:S(2)}) collective-permute-start(bf16[128,512]{1,0:T(8,128)(2,1)S(1)} %shard_map.113.refs_0_), channel_id=1, source_target_pairs={{0,4},{1,5},{2,6},{3,7},{4,0},{5,1},{6,2},{7,3},{8,12},{9,13},{10,... | collective-permute-start | bytes 393224 | tf_op jit(solution)/shard_map/ppermute | solution.py:59
  54.7 8.4 %collective-permute-start.17 = (bf16[64,2048]{1,0:T(8,128)(2,1)S(1)}, bf16[64,2048]{1,0:T(8,128)(2,1)S(1)}, u32[]{:S(2)}, u32[]{:S(2)}) collective-permute-start(bf16[64,2048]{1,0:T(8,128)(2,1)S(1)} %shard_map.112.refs_0_), channel_id=1, source_target_pairs={{0,2},{1,3},{2,0},{3,1},{4,6},{5,7},{6,4},{7,5},{8,10},{9,11},{10,... | collective-permute-start | bytes 786440 | tf_op jit(solution)/shard_map/ppermute | solution.py:59
  62.5 2.7 %collective-permute-start.22 = (bf16[128,2048]{1,0:T(8,128)(2,1)S(1)}, bf16[128,2048]{1,0:T(8,128)(2,1)S(1)}, u32[]{:S(2)}, u32[]{:S(2)}) collective-permute-start(bf16[128,2048]{1,0:T(8,128)(2,1)S(1)} %shard_map.114.refs_2_), channel_id=1, source_target_pairs={{0,1},{1,0},{2,3},{3,2},{4,5},{5,4},{6,7},{7,6},{8,9},{9,8},{10,11... | collective-permute-start | bytes 1572872 | tf_op jit(solution)/shard_map/ppermute | solution.py:59
  62.6 2.3 %collective-permute-start.16 = (bf16[64,2048]{1,0:T(8,128)(2,1)S(1)}, bf16[64,2048]{1,0:T(8,128)(2,1)S(1)}, u32[]{:S(2)}, u32[]{:S(2)}) collective-permute-start(bf16[64,2048]{1,0:T(8,128)(2,1)S(1)} %shard_map.112.refs_0_), channel_id=1, source_target_pairs={{0,1},{1,0},{2,3},{3,2},{4,5},{5,4},{6,7},{7,6},{8,9},{9,8},{10,11... | collective-permute-start | bytes 786440 | tf_op jit(solution)/shard_map/ppermute | solution.py:59
  63.1 2.1 %collective-permute-start.18 = (bf16[64,2048]{1,0:T(8,128)(2,1)S(1)}, bf16[64,2048]{1,0:T(8,128)(2,1)S(1)}, u32[]{:S(2)}, u32[]{:S(2)}) collective-permute-start(bf16[64,2048]{1,0:T(8,128)(2,1)S(1)} %collective-permute-done.17.refs_1_), channel_id=1, source_target_pairs={{0,1},{1,0},{2,3},{3,2},{4,5},{5,4},{6,7},{7,6},{8,9},{9,8},{10,11... | collective-permute-start | bytes 786440 | tf_op jit(solution)/shard_map/ppermute | solution.py:59
  66.7 1.3 %collective-permute-start.23 = (bf16[320,128]{1,0:T(8,128)(2,1)S(1)}, bf16[320,128]{1,0:T(8,128)(2,1)S(1)}, u32[]{:S(2)}, u32[]{:S(2)}) collective-permute-start(bf16[320,128]{1,0:T(8,128)(2,1)S(1)} %get-tuple-element.104), channel_id=1, source_target_pairs={{0,1},{1,0},{2,3},{3,2},{4,5},{5,4},{6,7},{7,6},{8,9},{9,8},{10,11... | collective-permute-start | bytes 245768 | tf_op jit(solution)/shard_map/ppermute | solution.py:59
  68.1 4.6 %collective-permute-start.24 = (bf16[320,128]{1,0:T(8,128)(2,1)S(1)}, bf16[320,128]{1,0:T(8,128)(2,1)S(1)}, u32[]{:S(2)}, u32[]{:S(2)}) collective-permute-start(bf16[320,128]{1,0:T(8,128)(2,1)S(1)} %get-tuple-element.106), channel_id=1, source_target_pairs={{0,2},{1,3},{2,0},{3,1},{4,6},{5,7},{6,4},{7,5},{8,10},{9,11},{10,... | collective-permute-start | bytes 245768 | tf_op jit(solution)/shard_map/ppermute | solution.py:59
  72.7 7.3 %collective-permute-start.25 = (bf16[320,128]{1,0:T(8,128)(2,1)S(1)}, bf16[320,128]{1,0:T(8,128)(2,1)S(1)}, u32[]{:S(2)}, u32[]{:S(2)}) collective-permute-start(bf16[320,128]{1,0:T(8,128)(2,1)S(1)} %get-tuple-element.108), channel_id=1, source_target_pairs={{0,12},{1,13},{2,14},{3,15},{4,8},{5,9},{6,10},{7,11},{8,4},{9,5},... | collective-permute-start | bytes 245768 | tf_op jit(solution)/shard_map/ppermute | solution.py:59
  74.5 7.2 %collective-permute-start.26 = (bf16[320,128]{1,0:T(8,128)(2,1)S(1)}, bf16[320,128]{1,0:T(8,128)(2,1)S(1)}, u32[]{:S(2)}, u32[]{:S(2)}) collective-permute-start(bf16[320,128]{1,0:T(8,128)(2,1)S(1)} %get-tuple-element.108), channel_id=1, source_target_pairs={{0,8},{1,9},{2,10},{3,11},{4,12},{5,13},{6,14},{7,15},{8,0},{9,1},... | collective-permute-start | bytes 245768 | tf_op jit(solution)/shard_map/ppermute | solution.py:59
  74.5 7.2 %collective-permute-start.27 = (bf16[320,128]{1,0:T(8,128)(2,1)S(1)}, bf16[320,128]{1,0:T(8,128)(2,1)S(1)}, u32[]{:S(2)}, u32[]{:S(2)}) collective-permute-start(bf16[320,128]{1,0:T(8,128)(2,1)S(1)} %get-tuple-element.108), channel_id=1, source_target_pairs={{0,4},{1,5},{2,6},{3,7},{4,0},{5,1},{6,2},{7,3},{8,12},{9,13},{10,... | collective-permute-start | bytes 245768 | tf_op jit(solution)/shard_map/ppermute | solution.py:59
  81.8 1.3 %collective-permute-start.28 = (bf16[320,128]{1,0:T(8,128)(2,1)S(1)}, bf16[320,128]{1,0:T(8,128)(2,1)S(1)}, u32[]{:S(2)}, u32[]{:S(2)}) collective-permute-start(bf16[320,128]{1,0:T(8,128)(2,1)S(1)} %shard_map.119.refs_0_), channel_id=1, source_target_pairs={{0,1},{1,0},{2,3},{3,2},{4,5},{5,4},{6,7},{7,6},{8,9},{9,8},{10,11... | collective-permute-start | bytes 245768 | tf_op jit(solution)/shard_map/ppermute | solution.py:59
